TPU v7x, 32 devices: a whole 2x2x4 slice. The times are simulated.
32 devices in a mesh: seq: 16 (over z, y, core), mp: 2 (over x).
Axes of the slice: x: 2, y: 2, z: 4, core: 2. Of those that a mesh axis runs over, the one named last changes fastest.
Arguments:
- queries: bfloat16 [4096, 8, 64], P('seq', 'mp'), may hold values from -6 to 6
- key_value: bfloat16 [4096, 8, 128], P('seq', 'mp'), may hold values from -6 to 6
- tile_fill: int32 [32], P('seq'), may hold values from 0 to 128, as said below
- out_weight: bfloat16 [8, 64, 768], P('mp'), may hold values from -0.75 to 0.75
- grad_output: bfloat16 [4096, 768], P('seq'), may hold values from -6 to 6
Outputs:
- attention_out: bfloat16 [4096, 768], P('seq')
- query_grad: float32 [4096, 8, 64], P('seq', 'mp')
- key_value_grad: float32 [4096, 8, 128], P('seq', 'mp')
- out_weight_grad: float32 [8, 64, 768], P('mp')
Inputs may be any that keep to these rules, and one draw needn't show every extreme that they name: `tile_fill`: tile 0 is full, and the first tile of every block of 256 slots holds at least one active voxel.
All inputs are finite; a program needn't handle non-finite values.
Results may differ from a plain program's by a relative error of at most 0.03.
Values may be sent and summed in bfloat16 or wider, within the bound.
No kernel may reach another device: no remote copies, remote signals or barrier semaphores. Data moves between devices by JAX's collectives and lax.ppermute only.
A program may use at most 64 MiB of HBM per device.

v0:
```python
import jax
import jax.numpy as jnp
from jax import lax
from jax.sharding import PartitionSpec as P

TILE = 128


big_negative = -1e30


def live_slots(tile_fill, tile_rows):
    within = lax.iota(jnp.int32, tile_rows)
    return (within[None, :] < tile_fill[:, None]).reshape(-1)


def over_blocks(advance, carried, pieces):
    total_rows = pieces[0].shape[0]
    block_rows = total_rows
    while block_rows > 2048 and block_rows % 2 == 0:
        block_rows = block_rows // 2
    number = total_rows // block_rows

    def one_turn(turn_index, running):
        sliced = tuple(
            (
                lax.dynamic_slice_in_dim(member, turn_index * block_rows, block_rows, 0)
                for member in pieces
            )
        )
        return advance(running, sliced)

    return lax.fori_loop(0, number, one_turn, carried)


def shards(queries, key_value, tile_fill, out_weight, grad_output):
    head_dim = queries.shape[2]
    heads_here = queries.shape[1]
    local_rows = queries.shape[0]
    score_scale = head_dim ** (-0.5)
    live_mask = live_slots(tile_fill, TILE)
    key_live = live_mask.astype(jnp.bfloat16)
    local_keys = key_value[:, :, :head_dim]
    local_values = key_value[:, :, head_dim:]

    def forward_block(carried, pieces):
        running_max, totals, weighted = carried
        pair_block, live_block = pieces
        usable = (live_block > 0)[None, None, :]
        scores = (
            jnp.einsum(
                "qhd,khd->hqk",
                queries,
                pair_block[:, :, :head_dim],
                preferred_element_type=jnp.float32,
            )
            * score_scale
        )
        block_max = jnp.max(jnp.where(usable, scores, big_negative), axis=2)
        new_max = jnp.maximum(running_max, block_max)
        exp_rows = jnp.where(usable, jnp.exp(scores - new_max[:, :, None]), 0.0)
        factor = jnp.exp(running_max - new_max)
        totals = totals * factor + jnp.sum(exp_rows, axis=2)
        weighted = weighted * factor[:, :, None] + jnp.einsum(
            "hqk,khd->hqd",
            exp_rows.astype(jnp.bfloat16),
            pair_block[:, :, head_dim:],
            preferred_element_type=jnp.float32,
        )
        return (new_max, totals, weighted)

    start_state = (
        jnp.full((heads_here, local_rows), big_negative, jnp.float32),
        jnp.zeros((heads_here, local_rows), jnp.float32),
        jnp.zeros((heads_here, local_rows, head_dim), jnp.float32),
    )
    final_state = over_blocks(
        forward_block,
        start_state,
        (
            lax.all_gather(key_value, "seq", axis=0, tiled=True),
            lax.all_gather(key_live, "seq", axis=0, tiled=True),
        ),
    )
    row_max, totals, weighted = final_state
    attended = (weighted / totals[:, :, None]).astype(jnp.bfloat16)
    log_total = row_max + jnp.log(totals)
    live_float = live_mask.astype(jnp.float32)
    head_terms = jnp.einsum("hqd,hde->qe", attended, out_weight, preferred_element_type=jnp.float32)
    projected = lax.psum(head_terms.astype(jnp.bfloat16), "mp").astype(jnp.float32)
    attention_out = (projected * live_float[:, None]).astype(jnp.bfloat16)
    grad_mixed = grad_output * live_mask[:, None].astype(jnp.bfloat16)
    grad_attn = jnp.einsum(
        "qe,hde->qhd", grad_mixed, out_weight, preferred_element_type=jnp.float32
    ).astype(jnp.bfloat16)
    weight_terms = jnp.einsum(
        "hqd,qe->hde", attended, grad_mixed, preferred_element_type=jnp.float32
    )
    attended_rows = jnp.transpose(attended, (1, 0, 2))
    inner_rows = jnp.sum(grad_attn.astype(jnp.float32) * attended_rows.astype(jnp.float32), axis=2)
    inner_heads = inner_rows.T
    log_rows = log_total.T

    def query_grad_block(carried, pieces):
        pair_block, live_block = pieces
        usable = (live_block > 0)[None, None, :]
        scores = (
            jnp.einsum(
                "qhd,khd->hqk",
                queries,
                pair_block[:, :, :head_dim],
                preferred_element_type=jnp.float32,
            )
            * score_scale
        )
        prob_rows = jnp.where(usable, jnp.exp(scores - log_total[:, :, None]), 0.0)
        grad_probs = jnp.einsum(
            "qhd,khd->hqk",
            grad_attn,
            pair_block[:, :, head_dim:],
            preferred_element_type=jnp.float32,
        )
        grad_scores = (prob_rows * (grad_probs - inner_heads[:, :, None])).astype(jnp.bfloat16)
        return (
            carried
            + jnp.einsum(
                "hqk,khd->qhd",
                grad_scores,
                pair_block[:, :, :head_dim],
                preferred_element_type=jnp.float32,
            )
            * score_scale
        )

    zero_query = jnp.zeros((local_rows, heads_here, head_dim), jnp.float32)
    query_grad = over_blocks(
        query_grad_block,
        zero_query,
        (
            lax.all_gather(key_value, "seq", axis=0, tiled=True),
            lax.all_gather(key_live, "seq", axis=0, tiled=True),
        ),
    )
    whole_log, whole_inner = (
        lax.all_gather(log_rows, "seq", axis=0, tiled=True),
        lax.all_gather(inner_rows, "seq", axis=0, tiled=True),
    )
    key_usable = live_mask[None, :, None]

    def key_grad_block(carried, pieces):
        grad_keys, grad_values = carried
        bundle_block, log_block, inner_block = pieces
        remote_query = bundle_block[:, :, :head_dim]
        remote_grad = bundle_block[:, :, head_dim:]
        scores = (
            jnp.einsum("khd,phd->hkp", local_keys, remote_query, preferred_element_type=jnp.float32)
            * score_scale
        )
        prob_rows = jnp.where(key_usable, jnp.exp(scores - log_block.T[:, None, :]), 0.0)
        grad_values = grad_values + jnp.einsum(
            "hkp,phd->khd",
            prob_rows.astype(jnp.bfloat16),
            remote_grad,
            preferred_element_type=jnp.float32,
        )
        grad_probs = jnp.einsum(
            "khd,phd->hkp", local_values, remote_grad, preferred_element_type=jnp.float32
        )
        grad_scores = (prob_rows * (grad_probs - inner_block.T[:, None, :])).astype(jnp.bfloat16)
        grad_keys = (
            grad_keys
            + jnp.einsum(
                "hkp,phd->khd", grad_scores, remote_query, preferred_element_type=jnp.float32
            )
            * score_scale
        )
        return (grad_keys, grad_values)

    bundle = jnp.concatenate([queries, grad_attn], axis=2)
    zero_keys = jnp.zeros((local_rows, heads_here, head_dim), jnp.float32)
    grad_keys, grad_values = over_blocks(
        key_grad_block,
        (zero_keys, zero_keys),
        (lax.all_gather(bundle, "seq", axis=0, tiled=True), whole_log, whole_inner),
    )
    key_value_grad = jnp.concatenate([grad_keys, grad_values], axis=2)
    out_weight_grad = lax.psum(weight_terms, "seq")
    return (attention_out, query_grad, key_value_grad, out_weight_grad)


def solution(mesh):
    return jax.shard_map(
        shards,
        mesh=mesh,
        in_specs=(
            P("seq", "mp", None),
            P("seq", "mp", None),
            P("seq"),
            P("mp", None, None),
            P("seq", None),
        ),
        out_specs=(P("seq", None), P("seq", "mp", None), P("seq", "mp", None), P("mp", None, None)),
        check_vma=False,
    )
```

profile of v0, /device:TPU:0, one launch (start us, length us, event | category | flops | bytes accessed | tf_op | source)
XLA Modules:
  0.0 267.2 jit_solution(15463160932838811533)
XLA Ops:
  7.2 0.0 copy-start
  7.2 0.0 all-gather.4.cloned.1.call-start
  7.2 1.9 copy.22
  9.1 0.0 all-gather.4.cloned.1.call-update
  9.1 0.0 all-reduce.3.cloned.1.call-start
  9.2 0.7 convert_bitcast_fusion
  9.9 23.1 %all-gather = bf16[16,1,256]{2,1,0:T(2,128)(2,1)S(1)} all-gather(bf16[1,1,256]{2,1,0:T(2,128)(2,1)S(1)} %reshape.71), channel_id=1, replica_groups=mesh['seq'=16,'mp'=2] {'seq'}, dimensions={0}, use_global_device_ids=true | all-gather | bytes 8704 | tf_op jit(solution)/shard_map/all_gather | solution.py:82
  33.1 33.7 %all-gather.4.cloned.1.call-done = bf16[4096,4,128]{0,2,1:T(8,128)(2,1)} async-done(((bf16[256,4,128]{0,2,1:T(8,128)(2,1)}), bf16[4096,4,128]{0,2,1:T(8,128)(2,1)}) %all-gather.4.cloned.1.call-update) | async-done | bytes 4194320 | tf_op jit(solution)/shard_map/all_gather | solution.py:81
  66.8 0.0 copy-start.2
  66.8 0.0 copy-start.1
  66.8 15.6 %while.48 = (s32[]{:T(128)}, f32[4,256]{1,0:T(4,128)S(1)}, f32[4,256]{1,0:T(4,128)S(1)}, f32[4,256,64]{1,2,0:T(8,128)S(1)}, bf16[4096]{0:T(1024)(128)(2,1)S(1)},...) while((s32[]{:T(128)}, f32[4,256]{1,0:T(4,128)S(1)}, ...), condition=%wide.region_3.4_spmd.clone, body=%wide.region_0.3_spmd.clone.sunk | while | flops 560147456 | bytes 27996368 | solution.py:33
  66.8 3.2 %select_reduce_fusion.2 = (f32[4,256]{1,0:T(4,128)S(1)}, f32[4,2048,256]{2,1,0:T(8,128)S(1)}) fusion(pred[2048]{0:T(1024)(128)(4,1)S(1)} %dynamic-slice_compare_fusion.4, bf16[256,4,64]{0,2,1:T(8,128)(2,1)} %get-tuple-element.781, bf16[4096,4,128]{0,2,1:T(8,128)(2,1)} %get-tuple-element.780, s32[]{:T(128)S(6)} %select_n.121), kind=kOutput, calls=%fused_computation.4.clone.1 | convolution fusion | flops 274725888 | bytes 9574404 | tf_op jit(solution)/shard_map/while/body/eval_jaxpr/qhd,khd->hqk/dot_general | solution.py:51
  70.0 1.7 bitcast_reduce_fusion.2
  71.7 2.8 %fusion.100 = f32[4,256,64]{1,2,0:T(8,128)S(1)} fusion(f32[4,2048,256]{2,1,0:T(8,128)S(1)} %get-tuple-element.729, f32[4,256]{1,0:T(4,128)S(1)} %select_maximum_fusion.2, pred[2048]{0:T(1024)(128)(4,1)S(1)} %dynamic-slice_compare_fusion.4, bf16[4096,4,128]{0,2,1:T(8,128)(2,1)} %get-tuple-element.780, s32[]{:T(128)S(6)} %select_n.121, s32[]{:T(128)S(6)} %add.155, ...), kind=kOutput, calls=%fused_computation.7.clone.1 | convolution fusion | flops 277020672 | bytes 9971721 | tf_op jit(solution)/shard_map/while/body/eval_jaxpr/hqk,khd->hqd/dot_general | solution.py:64
  74.6 3.1 %select_reduce_fusion.2 = (f32[4,256]{1,0:T(4,128)S(1)}, f32[4,2048,256]{2,1,0:T(8,128)S(1)}) fusion(pred[2048]{0:T(1024)(128)(4,1)S(1)} %dynamic-slice_compare_fusion.4, bf16[256,4,64]{0,2,1:T(8,128)(2,1)} %get-tuple-element.781, bf16[4096,4,128]{0,2,1:T(8,128)(2,1)} %get-tuple-element.780, s32[]{:T(128)S(6)} %select_n.121), kind=kOutput, calls=%fused_computation.4.clone.1 | convolution fusion | flops 274725888 | bytes 9574404 | tf_op jit(solution)/shard_map/while/body/eval_jaxpr/qhd,khd->hqk/dot_general | solution.py:51
  77.8 1.7 bitcast_reduce_fusion.2
  79.5 2.8 %fusion.100 = f32[4,256,64]{1,2,0:T(8,128)S(1)} fusion(f32[4,2048,256]{2,1,0:T(8,128)S(1)} %get-tuple-element.729, f32[4,256]{1,0:T(4,128)S(1)} %select_maximum_fusion.2, pred[2048]{0:T(1024)(128)(4,1)S(1)} %dynamic-slice_compare_fusion.4, bf16[4096,4,128]{0,2,1:T(8,128)(2,1)} %get-tuple-element.780, s32[]{:T(128)S(6)} %select_n.121, s32[]{:T(128)S(6)} %add.155, ...), kind=kOutput, calls=%fused_computation.7.clone.1 | convolution fusion | flops 277020672 | bytes 9971721 | tf_op jit(solution)/shard_map/while/body/eval_jaxpr/hqk,khd->hqd/dot_general | solution.py:64
  82.3 0.0 copy-done
  82.4 0.0 copy-done.2
  82.4 0.4 fusion.61
  82.8 1.1 fusion.55
  83.8 0.0 all-reduce.3.cloned.1.call-update
  83.8 0.0 all-gather.6.cloned.1.call-start
  83.9 1.6 pad_maximum_fusion.1
  85.5 0.0 all-gather.6.cloned.1.call-update
  85.6 0.0 all-reduce.5.cloned.1.call-start
  85.6 0.0 copy-done.1
  85.7 18.9 %all_gather.21 = f32[4096,4]{0,1:T(4,128)S(1)} all-gather(f32[256,4]{0,1:T(4,128)S(1)} %get-tuple-element.580), channel_id=1, replica_groups=mesh['seq'=16,'mp'=2] {'seq'}, dimensions={0}, use_global_device_ids=true | all-gather | bytes 69632 | tf_op jit(solution)/shard_map/all_gather | solution.py:146
  104.5 17.8 %all_gather.20 = f32[4096,4]{0,1:T(4,128)S(1)} all-gather(f32[256,4]{0,1:T(4,128)S(1)} %bitcast.82), channel_id=1, replica_groups=mesh['seq'=16,'mp'=2] {'seq'}, dimensions={0}, use_global_device_ids=true | all-gather | bytes 69632 | tf_op jit(solution)/shard_map/all_gather | solution.py:145
  122.4 1.2 fusion.56
  123.6 0.0 copy-start.3
  123.6 26.6 %while.49 = (s32[]{:T(128)}, f32[256,4,64]{0,2,1:T(8,128)S(1)}, bf16[4096,4,128]{0,2,1:T(8,128)(2,1)}, bf16[4096]{0:T(1024)(128)(2,1)S(1)}, bf16[256,4,64]{0,2,1...) while((s32[]{:T(128)}, f32[256,4,64]{0,2,1:T(8,128)S(1)}, ...), condition=%wide.region_7.8_spmd.clone, body=%wide.region_6.7_spmd.clone.sunk | while | flops 818092032 | bytes 20728016 | solution.py:33
  123.6 5.8 %fusion.106 = f32[4,2048,256]{2,1,0:T(8,128)} fusion(bf16[256,4,64]{0,2,1:T(8,128)(2,1)} %get-tuple-element.817, bf16[4096,4,128]{0,2,1:T(8,128)(2,1)} %get-tuple-element.815, s32[]{:T(128)S(6)} %select_n.123), kind=kOutput, calls=%fused_computation.28.clone.1 | convolution fusion | flops 268435456 | bytes 9568260 | tf_op jit(solution)/shard_map/while/body/eval_jaxpr/qhd,khd->hqk/dot_general | solution.py:108
  129.4 7.5 %fusion.107 = f32[256,4,64]{0,2,1:T(8,128)S(1)} fusion(f32[4,2048,256]{2,1,0:T(8,128)} %fusion.106, bf16[256,4,64]{0,2,1:T(8,128)(2,1)S(1)} %get-tuple-element.819, f32[4,256]{1,0:T(4,128)S(1)} %get-tuple-element.820, f32[4,256]{1,0:T(4,128)S(1)} %get-tuple-element.818, pred[2048]{0:T(1024)(128)(4,1)S(1)} %dynamic-slice_compare_fusion.5, ...), kind=kOutput, calls=%fused_computation.25.clone.1 | convolution fusion | flops 549650432 | bytes 11153408 | tf_op jit(solution)/shard_map/while/body/eval_jaxpr/hqk,khd->qhd/dot_general | solution.py:126
  136.9 5.8 %fusion.106 = f32[4,2048,256]{2,1,0:T(8,128)} fusion(bf16[256,4,64]{0,2,1:T(8,128)(2,1)} %get-tuple-element.817, bf16[4096,4,128]{0,2,1:T(8,128)(2,1)} %get-tuple-element.815, s32[]{:T(128)S(6)} %select_n.123), kind=kOutput, calls=%fused_computation.28.clone.1 | convolution fusion | flops 268435456 | bytes 9568260 | tf_op jit(solution)/shard_map/while/body/eval_jaxpr/qhd,khd->hqk/dot_general | solution.py:108
  142.7 7.5 %fusion.107 = f32[256,4,64]{0,2,1:T(8,128)S(1)} fusion(f32[4,2048,256]{2,1,0:T(8,128)} %fusion.106, bf16[256,4,64]{0,2,1:T(8,128)(2,1)S(1)} %get-tuple-element.819, f32[4,256]{1,0:T(4,128)S(1)} %get-tuple-element.820, f32[4,256]{1,0:T(4,128)S(1)} %get-tuple-element.818, pred[2048]{0:T(1024)(128)(4,1)S(1)} %dynamic-slice_compare_fusion.5, ...), kind=kOutput, calls=%fused_computation.25.clone.1 | convolution fusion | flops 549650432 | bytes 11153408 | tf_op jit(solution)/shard_map/while/body/eval_jaxpr/hqk,khd->qhd/dot_general | solution.py:126
  150.2 0.0 copy-start.4
  150.2 0.0 all-reduce.5.cloned.1.call-update
  150.2 0.0 all-reduce.3.cloned.1.call-done
  150.2 1.9 multiply_convert_fusion.2
  152.2 11.9 %all-gather.6.cloned.1.call-done = bf16[4096,4,128]{0,2,1:T(8,128)(2,1)} async-done(((bf16[256,4,128]{0,2,1:T(8,128)(2,1)}), bf16[4096,4,128]{0,2,1:T(8,128)(2,1)}) %all-gather.6.cloned.1.call-update) | async-done | bytes 4194320 | tf_op jit(solution)/shard_map/all_gather | solution.py:184
  164.1 0.0 copy-done.3
  164.1 0.0 copy-done.4
  164.1 36.0 %while.50 = (s32[]{:T(128)}, f32[256,4,64]{0,2,1:T(8,128)S(1)}, f32[256,4,64]{0,2,1:T(8,128)S(1)}, bf16[4096,4,128]{0,2,1:T(8,128)(2,1)}, bf16[256,4,64]{0,2,1:T...) while((s32[]{:T(128)}, f32[256,4,64]{0,2,1:T(8,128)S(1)}, ...), condition=%wide.region_9.10_spmd.clone, body=%wide.region_8.9_spmd.clone.sunk | while | flops 1095041280 | bytes 30903272 | solution.py:33
  164.1 0.1 compare_bitcast_fusion.2
  164.2 5.8 %fusion.115 = f32[4,2048,256]{2,1,0:T(8,128)} fusion(bf16[256,4,64]{0,2,1:T(8,128)(2,1)S(1)} %get-tuple-element.858, bf16[4096,4,128]{0,2,1:T(8,128)(2,1)} %get-tuple-element.857, s32[]{:T(128)S(6)} %select_n.126), kind=kOutput, calls=%fused_computation.47.clone.1 | convolution fusion | flops 268435456 | bytes 9568260 | tf_op jit(solution)/shard_map/while/body/eval_jaxpr/khd,phd->hkp/dot_general | solution.py:156
  169.9 7.4 %fusion.116 = f32[256,4,64]{0,2,1:T(8,128)S(1)} fusion(f32[4,2048,256]{2,1,0:T(8,128)} %fusion.115, bf16[256,4,64]{0,2,1:T(8,128)(2,1)S(1)} %get-tuple-element.860, f32[4,2048]{1,0:T(4,128)S(1)} %get-tuple-element.749, f32[4,2048]{1,0:T(4,128)S(1)} %get-tuple-element.750, pred[256]{0:T(512)(128)(4,1)S(1)} %compare_bitcast_fusion.2, ...), kind=kOutput, calls=%fused_computation.45.clone.1 | convolution fusion | flops 549650432 | bytes 11208960 | tf_op jit(solution)/shard_map/while/body/eval_jaxpr/hkp,phd->khd/dot_general | solution.py:172
  177.3 4.8 %fusion.117 = f32[256,4,64]{0,2,1:T(8,128)S(1)} fusion(f32[4,2048,256]{2,1,0:T(8,128)} %fusion.115, f32[4,2048]{1,0:T(4,128)S(1)} %get-tuple-element.750, pred[256]{0:T(512)(128)(4,1)S(1)} %compare_bitcast_fusion.2, bf16[4096,4,128]{0,2,1:T(8,128)(2,1)} %get-tuple-element.857, s32[]{:T(128)S(6)} %select_n.126, s32[]{:T(128)S(6)} %add.164, ...), kind=kOutput, calls=%fused_computation.42.clone.1 | convolution fusion | flops 276955136 | bytes 9994505 | tf_op jit(solution)/shard_map/while/body/eval_jaxpr/hkp,phd->khd/dot_general | solution.py:160
  182.1 0.1 compare_bitcast_fusion.2
  182.2 5.8 %fusion.115 = f32[4,2048,256]{2,1,0:T(8,128)} fusion(bf16[256,4,64]{0,2,1:T(8,128)(2,1)S(1)} %get-tuple-element.858, bf16[4096,4,128]{0,2,1:T(8,128)(2,1)} %get-tuple-element.857, s32[]{:T(128)S(6)} %select_n.126), kind=kOutput, calls=%fused_computation.47.clone.1 | convolution fusion | flops 268435456 | bytes 9568260 | tf_op jit(solution)/shard_map/while/body/eval_jaxpr/khd,phd->hkp/dot_general | solution.py:156
  188.0 7.3 %fusion.116 = f32[256,4,64]{0,2,1:T(8,128)S(1)} fusion(f32[4,2048,256]{2,1,0:T(8,128)} %fusion.115, bf16[256,4,64]{0,2,1:T(8,128)(2,1)S(1)} %get-tuple-element.860, f32[4,2048]{1,0:T(4,128)S(1)} %get-tuple-element.749, f32[4,2048]{1,0:T(4,128)S(1)} %get-tuple-element.750, pred[256]{0:T(512)(128)(4,1)S(1)} %compare_bitcast_fusion.2, ...), kind=kOutput, calls=%fused_computation.45.clone.1 | convolution fusion | flops 549650432 | bytes 11208960 | tf_op jit(solution)/shard_map/while/body/eval_jaxpr/hkp,phd->khd/dot_general | solution.py:172
  195.3 4.8 %fusion.117 = f32[256,4,64]{0,2,1:T(8,128)S(1)} fusion(f32[4,2048,256]{2,1,0:T(8,128)} %fusion.115, f32[4,2048]{1,0:T(4,128)S(1)} %get-tuple-element.750, pred[256]{0:T(512)(128)(4,1)S(1)} %compare_bitcast_fusion.2, bf16[4096,4,128]{0,2,1:T(8,128)(2,1)} %get-tuple-element.857, s32[]{:T(128)S(6)} %select_n.126, s32[]{:T(128)S(6)} %add.164, ...), kind=kOutput, calls=%fused_computation.42.clone.1 | convolution fusion | flops 276955136 | bytes 9994505 | tf_op jit(solution)/shard_map/while/body/eval_jaxpr/hkp,phd->khd/dot_general | solution.py:160
  200.1 0.2 copy.26
  200.3 0.2 copy.25
  200.6 1.1 pad_maximum_fusion
  201.7 56.9 %all-reduce.5.cloned.1.call-done = f32[4,64,768]{2,1,0:T(8,128)} async-done(((f32[4,64,768]{2,1,0:T(8,128)}), f32[4,64,768]{2,1,0:T(8,128)}) %all-reduce.5.cloned.1.call-update) | async-done | bytes 786448 | tf_op jit(solution)/shard_map/psum | solution.py:187
  258.6 2.1 copy.58
  (23 shorter events, 0.2 us)
Async XLA Ops:
  7.2 75.2 %copy-start = (bf16[4,64,768]{2,1,0:T(8,128)(2,1)S(1)}, bf16[4,64,768]{2,1,0:T(8,128)(2,1)}, u32[]{:S(2)}) copy-start(bf16[4,64,768]{2,1,0:T(8,128)(2,1)} %param.14) | copy-start | bytes 1179652
  7.2 59.6 %all-gather.4.cloned.1.call-start = ((), (), s32[]{:S(2)}) async-start(), calls=%async_computation | async-start | bytes 4456448 | tf_op jit(solution)/shard_map/all_gather | solution.py:81
  9.1 141.1 %all-reduce.3.cloned.1.call-start = ((), (), s32[]{:S(2)}) async-start(), calls=%async_computation.1 | async-start | bytes 786432 | tf_op jit(solution)/shard_map/psum | solution.py:90
  66.8 15.6 %copy-start.2 = (bf16[256,768]{1,0:T(8,128)(2,1)S(1)}, bf16[256,768]{1,0:T(8,128)(2,1)}, u32[]{:S(2)}) copy-start(bf16[256,768]{1,0:T(8,128)(2,1)} %param.15) | copy-start | bytes 1179652
  66.8 18.9 %copy-start.1 = (bf16[256,4,128]{0,2,1:T(8,128)(2,1)S(1)}, bf16[256,4,128]{0,2,1:T(8,128)(2,1)}, u32[]{:S(2)}) copy-start(bf16[256,4,128]{0,2,1:T(8,128)(2,1)} %copy.22) | copy-start | bytes 786436
  83.8 80.2 %all-gather.6.cloned.1.call-start = ((), (), s32[]{:S(2)}) async-start(), calls=%async_computation.2 | async-start | bytes 4456448 | tf_op jit(solution)/shard_map/all_gather | solution.py:184
  85.6 173.0 %all-reduce.5.cloned.1.call-start = ((), (), s32[]{:S(2)}) async-start(), calls=%async_computation.3 | async-start | bytes 1572864 | tf_op jit(solution)/shard_map/psum | solution.py:187
  123.6 40.5 %copy-start.3 = (s32[2]{0:T(128)S(1)}, s32[2]{0:T(128)}, u32[]{:S(2)}) copy-start(s32[2]{0:T(128)} %param.13) | copy-start | bytes 28
  150.2 13.9 %copy-start.4 = (f32[256,4,64]{0,2,1:T(8,128)}, f32[256,4,64]{0,2,1:T(8,128)S(1)}, u32[]{:S(2)}) copy-start(f32[256,4,64]{0,2,1:T(8,128)S(1)} %get-tuple-element.869) | copy-start | bytes 786436
Sparse Core Ops, SparseCore 0:
  10.7 55.9 all-gather.3
  84.0 23.8 all-reduce.2
  110.8 53.2 all-gather.5
  168.3 90.2 all-reduce.4
where the time goes:
time: 268 us; the launch traced here: 267 us
  waiting for transfers between devices  103 us (38%)
  matrix products  76.9 us (29%)
  blocking collectives  59.8 us (22%)
  between operations  13.9 us (5%)
  other arithmetic  9.16 us (3%)
  local copies, waits for them, and re-layouts  4.49 us (2%)
    psum x1, waiting for transfers between devices, shards(): out_weight_grad = lax.psum(weight_terms, 'seq')  56.9 us
    all_gather x1, waiting for transfers between devices, shards(): lax.all_gather(key_value, 'seq', axis=0, tiled=True)  33.7 us
    all_gather x1, blocking collectives, shards(): lax.all_gather(key_live, 'seq', axis=0, tiled=True)  23.1 us
    all_gather x1, blocking collectives, shards(): lax.all_gather(inner_rows, 'seq', axis=0, tiled=True)  18.9 us
    all_gather x1, blocking collectives, shards(): lax.all_gather(log_rows, 'seq', axis=0, tiled=True)  17.8 us
    dot_general x2, matrix products, query_grad_block(): jnp.einsum('hqk,khd->qhd', grad_scores, pair_block[:, :, :head_dim], pref...  14.9 us
    dot_general x2, matrix products, key_grad_block(): jnp.einsum('hkp,phd->khd', grad_scores, remote_query, preferred_element_t...  14.7 us
    all_gather x1, waiting for transfers between devices, shards(): lax.all_gather(bundle, 'seq', axis=0, tiled=True)  11.9 us
  transfers between devices with their start and end apart: 4, of which 3 were waited for; matrix products, arithmetic and copies ran while one was open for 26% of the time, Pallas kernels for 0%

commit v1 on v0

v1 whole, which is shorter than its diff:
```python
import functools

import jax
import jax.numpy as jnp
from jax import lax
from jax.experimental import pallas as pl
from jax.experimental.pallas import tpu as pltpu
from jax.sharding import PartitionSpec as P

TILE = 128
DEAD = 1024.0
BIAS = -1e30
F32 = jnp.float32
BF16 = jnp.bfloat16
VMEM = pl.BlockSpec(memory_space=pltpu.VMEM)
SMEM = pl.BlockSpec(memory_space=pltpu.SMEM)
LIMIT = 48 * 1024 * 1024


def dot(a, b):
    return lax.dot_general(a, b, (((1,), (0,)), ((), ())), preferred_element_type=F32)


def dot_nt(a, b):
    return lax.dot_general(a, b, (((1,), (1,)), ((), ())), preferred_element_type=F32)


def call(kernel, outs, scratch=(), n_in=1, smem_first=False, flops=0, moved=0):
    specs = [VMEM] * n_in
    if smem_first:
        specs[0] = SMEM
    return pl.pallas_call(
        kernel,
        out_shape=[jax.ShapeDtypeStruct(shape, kind) for shape, kind in outs],
        in_specs=specs,
        out_specs=[VMEM] * len(outs),
        scratch_shapes=list(scratch),
        compiler_params=pltpu.CompilerParams(vmem_limit_bytes=LIMIT),
        cost_estimate=pl.CostEstimate(flops=flops, bytes_accessed=moved, transcendentals=0),
    )


def live_column(fill_ref, rows):
    parts = []
    within = lax.broadcasted_iota(jnp.int32, (TILE, 1), 0)
    for tile in range(rows // TILE):
        parts.append(jnp.where(within < fill_ref[tile], 1.0, 0.0))
    return jnp.concatenate(parts, axis=0) if len(parts) > 1 else parts[0]


def pack_kernel(heads, rows, dim, a_of, fill_ref, q_ref, kv_ref, w_ref, go_ref, *rest):
    kv_out, qg_out = rest[:heads], rest[heads : 2 * heads]
    kv_all, qg_all = rest[2 * heads :]
    live = live_column(fill_ref, rows)
    mixed = jnp.where(live > 0, go_ref[...].astype(F32), 0.0).astype(BF16)
    lane = lax.broadcasted_iota(jnp.int32, (rows, 2 * dim), 1)
    mark = jnp.where(lane == 0, DEAD, 0.0)
    for head in range(heads):
        grad = dot_nt(w_ref[head], mixed).astype(BF16)
        scaled = (q_ref[head].astype(F32) * dim**-0.5).astype(BF16)
        qg_all[head] = jnp.concatenate([scaled, grad], axis=0)
        pair = kv_ref[:, head, :].astype(F32)
        kv_all[head] = jnp.where(live > 0, pair, mark).astype(BF16)
    me = a_of()
    for slot in range(heads):
        kv_out[slot][...] = kv_all[me ^ slot]
        qg_out[slot][...] = qg_all[me ^ slot]


def forward_kernel(slots, columns, rows, dim, *refs):
    blocks, refs = refs[:columns], refs[columns:]
    qg_in, refs = refs[:slots], refs[slots:]
    att_out, refs = refs[:slots], refs[slots:]
    log_ref, k_ref, v_ref, q_aug, g_aug, vt_ref = refs
    block = slots * rows
    lane = lax.broadcasted_iota(jnp.int32, (block, 2 * dim), 1)
    for column in range(columns):
        pair = blocks[column][...].astype(F32)
        dead = pair[:, 0:1] >= DEAD
        here = pl.ds(column * block, block)
        keys = jnp.where(lane < dim, pair, 0.0)
        k_ref[here, :] = jnp.where(dead, jnp.where(lane == dim, BIAS, 0.0), keys).astype(BF16)
        values = jnp.where(lane >= dim, pair, jnp.where(lane <= 1, 1.0, 0.0))
        values = jnp.where(dead, 0.0, values)
        v_ref[here, :] = values.astype(BF16)
        vt_ref[:, here] = values.T.astype(BF16)
    row = lax.broadcasted_iota(jnp.int32, (2 * dim, rows), 0)
    for slot in range(slots):
        mixed = qg_in[slot][...].astype(F32)
        queries = jnp.where(row < dim, mixed, jnp.where(row == dim, 1.0, 0.0)).astype(BF16)
        q_aug[slot] = queries
        peak = jnp.full((1, rows), BIAS, F32)
        total = jnp.zeros((2 * dim, rows), F32)
        for column in range(columns):
            here = pl.ds(column * block, block)
            scores = dot(k_ref[here, :], queries)
            new_peak = jnp.maximum(peak, jnp.max(scores, axis=0, keepdims=True))
            exps = jnp.exp(scores - new_peak).astype(BF16)
            total = total * jnp.exp(peak - new_peak) + dot(vt_ref[:, here], exps)
            peak = new_peak
        weight = total[0:1, :]
        log_ref[slot] = peak + jnp.log(weight)
        attended = (total / weight).astype(BF16)
        att_out[slot][...] = attended[dim:, :]
        terms = jnp.where(row >= dim, mixed * attended.astype(F32), 0.0)
        inner = jnp.sum(terms, axis=0, keepdims=True)
        high = inner.astype(BF16).astype(F32)
        low = inner - high
        filled = jnp.where(row == 0, -high, jnp.where(row == 1, -low, 0.0))
        g_aug[slot] = jnp.where(row >= dim, mixed, filled).astype(BF16)


def backward_kernel(slots, columns, rows, dim, key_block, log_ref, k_ref, v_ref, q_aug, g_aug, *refs):
    dkv_out, dq_out, (kt_ref, dq_acc) = refs[:columns], refs[columns : columns + slots], refs[columns + slots :]
    block = slots * rows
    for column in range(columns):
        here = pl.ds(column * block, block)
        kt_ref[:, here] = k_ref[here, :].astype(F32).T.astype(BF16)
    lane = lax.broadcasted_iota(jnp.int32, (key_block, 2 * dim), 1)
    dq_acc[...] = jnp.zeros_like(dq_acc)
    for column in range(columns):
        for part in range(block // key_block):
            start = column * block + part * key_block
            here = pl.ds(start, key_block)
            keys, values = k_ref[here, :], v_ref[here, :]
            grad_k = jnp.zeros((key_block, 2 * dim), F32)
            grad_v = jnp.zeros((key_block, 2 * dim), F32)
            for slot in range(slots):
                probs = jnp.exp(dot(keys, q_aug[slot]) - log_ref[slot])
                grads = (probs * dot(values, g_aug[slot])).astype(BF16)
                grad_v = grad_v + dot_nt(probs.astype(BF16), g_aug[slot])
                grad_k = grad_k + dot_nt(grads, q_aug[slot])
                dq_acc[slot] += dot(kt_ref[:, here], grads)
            dkv_out[column][pl.ds(part * key_block, key_block), :] = jnp.where(lane < dim, grad_k, grad_v).astype(BF16)
    for slot in range(slots):
        dq_out[slot][...] = (dq_acc[slot, 0:dim, :] * dim**-0.5).astype(BF16)


def project_kernel(slots, rows, dim, a_of, fill_ref, w_ref, go_ref, *refs):
    att, (terms_ref, wt_ref) = refs[:slots], refs[slots:]
    live = live_column(fill_ref, rows)
    mixed = jnp.where(live > 0, go_ref[...].astype(F32), 0.0).astype(BF16)
    me = a_of()
    total = None
    for slot in range(slots):
        head = me ^ slot
        wt_ref[head] = dot(att[slot][...], mixed).astype(BF16)
        term = dot(att[slot][...].astype(F32).T.astype(BF16), w_ref[head])
        total = term if total is None else total + term
    terms_ref[...] = (total * live).astype(BF16)


def unpack_kernel(slots, rows, dim, a_of, *refs):
    dkv, dq = refs[:slots], refs[slots : 2 * slots]
    kv_out, q_out, kv_all = refs[2 * slots :]
    me = a_of()
    for slot in range(slots):
        q_out[me ^ slot] = dq[slot][...].astype(F32)
        kv_all[me ^ slot] = dkv[slot][...].astype(F32)
    for head in range(slots):
        kv_out[:, head, :] = kv_all[head]


def split_kernel(columns, b_of, wt_ref, *outs):
    me = b_of()
    for column in range(columns):
        outs[column][...] = wt_ref[me ^ column]


def sum_split_kernel(columns, slots, piece, a_of, *refs):
    parts, outs = refs[:columns], refs[columns : columns + slots]
    (held,) = refs[columns + slots :]
    total = parts[0][...].astype(F32)
    for part in parts[1:]:
        total = total + part[...].astype(F32)
    held[...] = total
    me = a_of()
    for slot in range(slots):
        start = pl.multiple_of((me ^ slot) * piece, piece)
        outs[slot][...] = held[pl.ds(start, piece), :].astype(BF16)


def sum_kernel(*refs):
    total = refs[0][...].astype(F32)
    for part in refs[1:-1]:
        total = total + part[...].astype(F32)
    refs[-1][...] = total.astype(refs[-1].dtype)


def place_kernel(columns, slots, piece, a_of, b_of, *refs):
    parts, (out_ref,) = refs[:columns], refs[columns:]
    me_a, me_b = a_of(), b_of()
    for column in range(columns):
        for slot in range(slots):
            start = pl.multiple_of((me_a ^ slot) * piece, piece)
            out_ref[me_b ^ column, pl.ds(start, piece), :] = parts[column][pl.ds(slot * piece, piece), :].astype(F32)


def shards(seq, mp, queries, key_value, tile_fill, out_weight, grad_output):
    rows, heads, dim = queries.shape
    width = grad_output.shape[1]
    slots = heads
    columns = seq // slots
    assert slots * columns == seq and columns & (columns - 1) == 0 and slots & (slots - 1) == 0
    a_of = lambda: lax.axis_index("seq") // columns
    b_of = lambda: lax.axis_index("seq") % columns

    def swap(array, mask, axis="seq", size=seq):
        return lax.ppermute(array, axis, [(i, i ^ mask) for i in range(size)])

    qt = jnp.transpose(queries, (1, 2, 0))
    packed = call(
        functools.partial(pack_kernel, heads, rows, dim, a_of),
        [((rows, 2 * dim), BF16)] * slots + [((2 * dim, rows), BF16)] * slots,
        [pltpu.VMEM((heads, rows, 2 * dim), BF16), pltpu.VMEM((heads, 2 * dim, rows), BF16)],
        n_in=5, smem_first=True,
        flops=2 * rows * heads * dim * width, moved=4 * rows * width,
    )(tile_fill, qt, key_value, out_weight, grad_output)
    kv_send, qg_send = packed[:slots], packed[slots:]
    kv_mine = [kv_send[0]] + [swap(kv_send[s], s * columns) for s in range(1, slots)]
    qg_mine = [qg_send[0]] + [swap(qg_send[s], s * columns) for s in range(1, slots)]
    own = jnp.concatenate(kv_mine, axis=0) if slots > 1 else kv_mine[0]

    blocks = {0: own}
    bit = columns // 2
    while bit:
        for r in sorted(blocks):
            blocks[r ^ bit] = swap(blocks[r], bit)
        bit //= 2

    keys = seq * rows
    block = slots * rows
    mults = slots * rows * keys * 2 * dim
    forward = call(
        functools.partial(forward_kernel, slots, columns, rows, dim),
        [((dim, rows), BF16)] * slots
        + [((slots, 1, rows), F32), ((keys, 2 * dim), BF16), ((keys, 2 * dim), BF16),
           ((slots, 2 * dim, rows), BF16), ((slots, 2 * dim, rows), BF16)],
        [pltpu.VMEM((2 * dim, keys), BF16)],
        n_in=columns + slots, flops=4 * mults, moved=4 * keys * 2 * dim,
    )(*[blocks[r] for r in range(columns)], *qg_mine)
    att_send, saved = forward[:slots], forward[slots:]
    att_mine = [att_send[0]] + [swap(att_send[s], s * columns) for s in range(1, slots)]

    terms, weight_terms = call(
        functools.partial(project_kernel, slots, rows, dim, a_of),
        [((rows, width), BF16), ((heads, dim, width), BF16)],
        n_in=3 + slots, smem_first=True, flops=4 * rows * heads * dim * width, moved=4 * rows * width,
    )(tile_fill, out_weight, grad_output, *att_mine)
    bit = 1
    while bit < mp:
        terms = call(sum_kernel, [((rows, width), BF16)], n_in=2, moved=6 * rows * width)(
            terms, swap(terms, bit, "mp", mp))[0]
        bit *= 2

    if columns == heads:
        piece = dim // slots
        split = call(functools.partial(split_kernel, columns, b_of), [((dim, width), BF16)] * columns)(weight_terms)
        got = [split[0]] + [swap(split[r], r) for r in range(1, columns)]
        split = call(
            functools.partial(sum_split_kernel, columns, slots, piece, a_of),
            [((piece, width), BF16)] * slots, [pltpu.VMEM((dim, width), F32)], n_in=columns)(*got)
        got = [split[0]] + [swap(split[s], s * columns) for s in range(1, slots)]
        summed = call(sum_kernel, [((piece, width), BF16)], n_in=slots)(*got)[0]
        quarter = jnp.concatenate([summed] + [swap(summed, s * columns) for s in range(1, slots)], axis=0)
        whole = [quarter] + [swap(quarter, r) for r in range(1, columns)]
        weight_grad = call(
            functools.partial(place_kernel, columns, slots, piece, a_of, b_of),
            [((heads, dim, width), F32)], n_in=columns)(*whole)[0]
    else:
        weight_grad = lax.psum(weight_terms.astype(F32), "seq")

    key_block = min(block, 512)
    backward = call(
        functools.partial(backward_kernel, slots, columns, rows, dim, key_block),
        [((block, 2 * dim), BF16)] * columns + [((dim, rows), BF16)] * slots,
        [pltpu.VMEM((2 * dim, keys), BF16), pltpu.VMEM((slots, 2 * dim, rows), F32)],
        n_in=5, flops=10 * mults, moved=4 * keys * 2 * dim,
    )(*saved)
    dkv, dq = dict(enumerate(backward[:columns])), backward[columns:]
    dq_mine = [dq[0]] + [swap(dq[s], s * columns) for s in range(1, slots)]
    bit = 1
    while bit < columns:
        kept = sorted(r for r in dkv if not r & bit)
        dkv = {
            r: call(sum_kernel, [((block, 2 * dim), BF16)], n_in=2, moved=12 * block * dim)(
                dkv[r], swap(dkv[r ^ bit], bit))[0]
            for r in kept
        }
        bit *= 2
    parts = [dkv[0][s * rows : (s + 1) * rows] for s in range(slots)]
    dkv_mine = [parts[0]] + [swap(parts[s], s * columns) for s in range(1, slots)]
    key_value_grad, query_grad = call(
        functools.partial(unpack_kernel, slots, rows, dim, a_of),
        [((rows, heads, 2 * dim), F32), ((heads, dim, rows), F32)],
        [pltpu.VMEM((heads, rows, 2 * dim), F32)],
        n_in=2 * slots, moved=8 * rows * heads * dim,
    )(*dkv_mine, *dq_mine)
    return terms, jnp.transpose(query_grad, (2, 0, 1)), key_value_grad, weight_grad


def solution(mesh):
    return jax.shard_map(
        functools.partial(shards, mesh.shape["seq"], mesh.shape["mp"]),
        mesh=mesh,
        in_specs=(
            P("seq", "mp", None),
            P("seq", "mp", None),
            P("seq"),
            P("mp", None, None),
            P("seq", None),
        ),
        out_specs=(P("seq", None), P("seq", "mp", None), P("seq", "mp", None), P("mp", None, None)),
        check_vma=False,
    )
```

time: 268 us -> 106 us (0.40)
  matrix products: 76.9 us -> 0 us
  waiting for transfers between devices: 103 us -> 31.6 us
  blocking collectives: 59.8 us -> 0 us
  starting transfers between devices: 0.16 us -> 40 us
  Pallas kernels: 0 us -> 28.8 us
  between operations: 13.9 us -> 0.83 us
  other arithmetic: 9.16 us -> 0.01 us
    dot_general x17 -> x0, matrix products: 76.9 us -> none  [the longest x2 14.9 us: query_grad_block(): jnp.einsum('hqk,khd->qhd', grad_scores, pair_block[:, :, :head_dim], pref...]
    all_gather x3 -> x0, blocking collectives: 59.8 us -> none  [the longest x1 23.1 us: shards(): lax.all_gather(key_live, 'seq', axis=0, tiled=True)]
    psum x2 -> x0, waiting for transfers between devices: 56.9 us -> none  [the longest x1 56.9 us: shards(): out_weight_grad = lax.psum(weight_terms, 'seq')]
    all_gather x2 -> x0, waiting for transfers between devices: 45.6 us -> none  [the longest x1 33.7 us: shards(): lax.all_gather(key_value, 'seq', axis=0, tiled=True)]
    ppermute x0 -> x34, starting transfers between devices: none -> 40 us  [swap(): return lax.ppermute(array, axis, [(i, i ^ mask) for i in range(size)])]
    ppermute x0 -> x34, waiting for transfers between devices: none -> 31.6 us  [swap(): return lax.ppermute(array, axis, [(i, i ^ mask) for i in range(size)])]
    pallas_call x0 -> x13, Pallas kernels: none -> 28.8 us  [the longest x1 11.4 us: shards(): call(functools.partial(forward_kernel, slots, columns, rows, dim), [((dim...]
    reduce_sum x2 -> x0, other arithmetic: 3.45 us -> none  [forward_block(): totals = totals * factor + jnp.sum(exp_rows, axis=2)]
  transfers between devices with their start and end apart: 4 -> 34, of which waited for: 3 -> 15; matrix products, arithmetic and copies ran while one was open for 26% -> 0% of each run, Pallas kernels for 0% -> 3%
where the time goes in v1:
time: 106 us
  starting transfers between devices  40 us (38%)
  waiting for transfers between devices  31.6 us (30%)
  Pallas kernels  28.8 us (27%)
  local copies, waits for them, and re-layouts  4.57 us (4%)
    ppermute x34, starting transfers between devices, swap(): return lax.ppermute(array, axis, [(i, i ^ mask) for i in range(size)])  40 us
    ppermute x34, waiting for transfers between devices, swap(): return lax.ppermute(array, axis, [(i, i ^ mask) for i in range(size)])  31.6 us
    pallas_call x1, Pallas kernels, shards(): call(functools.partial(forward_kernel, slots, columns, rows, dim), [((dim...  11.4 us
    pallas_call x1, Pallas kernels, shards(): call(functools.partial(backward_kernel, slots, columns, rows, dim, key_bl...  11.1 us
    unnamed x17, local copies, waits for them, and re-layouts  4.54 us
  transfers between devices with their start and end apart: 34, of which 15 were waited for; matrix products, arithmetic and copies ran while one was open for 0% of the time, Pallas kernels for 3%

profile of v1, /device:TPU:0, one launch (start us, length us, event | category | flops | bytes accessed | tf_op | source)
XLA Modules:
  0.0 105.9 jit_solution(15157899572776436758)
XLA Ops:
  0.6 0.6 copy-done.6
  1.3 1.0 copy-done
  2.3 1.0 copy-done.2
  3.3 0.9 copy-done.4
  4.2 0.9 copy-done.5
  5.1 1.6 %shard_map.84 = (bf16[256,128]{1,0:T(8,128)(2,1)S(1)}, bf16[256,128]{1,0:T(8,128)(2,1)S(1)}, bf16[256,128]{1,0:T(8,128)(2,1)S(1)}, bf16[256,128]{1,0:T(8,128)(2,...) custom-call(s32[2]{0:T(128)S(1)} %copy-done.6, ...), custom_call_target="tpu_custom_call" | custom-call | flops 100663296 | bytes 786432 | tf_op jit(solution)/shard_map/pallas_call | solution.py:212
  6.7 3.1 %collective-permute-start = (bf16[256,128]{1,0:T(8,128)(2,1)S(1)}, bf16[256,128]{1,0:T(8,128)(2,1)S(1)}, u32[]{:S(2)}, u32[]{:S(2)}) collective-permute-start(bf16[256,128]{1,0:T(8,128)(2,1)S(1)} %get-tuple-element.42), channel_id=1, source_target_pairs={{0,8},{2,10},{4,12},{6,14},{8,0},{10,2},{12,4},{14,6},{16,24},{18,... | collective-permute-start | bytes 196616 | tf_op jit(solution)/shard_map/ppermute | solution.py:209
  9.8 2.6 %collective-permute-start.1 = (bf16[256,128]{1,0:T(8,128)(2,1)S(1)}, bf16[256,128]{1,0:T(8,128)(2,1)S(1)}, u32[]{:S(2)}, u32[]{:S(2)}) collective-permute-start(bf16[256,128]{1,0:T(8,128)(2,1)S(1)} %get-tuple-element.43), channel_id=1, source_target_pairs={{0,16},{2,18},{4,20},{6,22},{8,24},{10,26},{12,28},{14,30},{16,0},... | collective-permute-start | bytes 196616 | tf_op jit(solution)/shard_map/ppermute | solution.py:209
  12.4 0.0 collective-permute-start.2
  12.4 0.0 collective-permute-done
  12.4 4.6 %collective-permute-done.1 = bf16[256,128]{1,0:T(8,128)(2,1)S(1)} collective-permute-done((bf16[256,128]{1,0:T(8,128)(2,1)S(1)}, bf16[256,128]{1,0:T(8,128)(2,1)S(1)}, u32[]{:S(2)}, u32[]{:S(2)}) %collective-permute-start.1) | collective-permute-done | bytes 65568 | tf_op jit(solution)/shard_map/ppermute | solution.py:209
  17.1 1.4 %collective-permute-done.2 = bf16[256,128]{1,0:T(8,128)(2,1)S(1)} collective-permute-done((bf16[256,128]{1,0:T(8,128)(2,1)S(1)}, bf16[256,128]{1,0:T(8,128)(2,1)S(1)}, u32[]{:S(2)}, u32[]{:S(2)}) %collective-permute-start.2) | collective-permute-done | bytes 65568 | tf_op jit(solution)/shard_map/ppermute | solution.py:209
  18.5 1.6 %collective-permute-start.4 = (bf16[1024,128]{1,0:T(8,128)(2,1)S(1)}, bf16[1024,128]{1,0:T(8,128)(2,1)S(1)}, u32[]{:S(2)}, u32[]{:S(2)}) collective-permute-start(bf16[1024,128]{1,0:T(8,128)(2,1)S(1)} %constant_dynamic-update-slice_fusion.refs_0_), channel_id=1, source_target_pairs={{0,4},{2,6},{4,0},{6,2},{8,12},{10,14},{12,8},{14,10},{16,20},{18,... | collective-permute-start | bytes 786440 | tf_op jit(solution)/shard_map/ppermute | solution.py:209
  20.1 4.9 %collective-permute-done.4.refs_2_ = bf16[1024,128]{1,0:T(8,128)(2,1)S(1)} collective-permute-done((bf16[1024,128]{1,0:T(8,128)(2,1)S(1)}, bf16[1024,128]{1,0:T(8,128)(2,1)S(1)}, u32[]{:S(2)}, u32[]{:S(2)}) %collective-permute-start.4) | collective-permute-done | bytes 262176 | tf_op jit(solution)/shard_map/ppermute | solution.py:209
  25.0 0.7 collective-permute-start.6
  25.6 1.7 %collective-permute-start.7 = (bf16[128,256]{1,0:T(8,128)(2,1)S(1)}, bf16[128,256]{1,0:T(8,128)(2,1)S(1)}, u32[]{:S(2)}, u32[]{:S(2)}) collective-permute-start(bf16[128,256]{1,0:T(8,128)(2,1)S(1)} %get-tuple-element.47), channel_id=1, source_target_pairs={{0,16},{2,18},{4,20},{6,22},{8,24},{10,26},{12,28},{14,30},{16,0},... | collective-permute-start | bytes 196616 | tf_op jit(solution)/shard_map/ppermute | solution.py:209
  27.3 2.1 %collective-permute-start.8 = (bf16[128,256]{1,0:T(8,128)(2,1)S(1)}, bf16[128,256]{1,0:T(8,128)(2,1)S(1)}, u32[]{:S(2)}, u32[]{:S(2)}) collective-permute-start(bf16[128,256]{1,0:T(8,128)(2,1)S(1)} %get-tuple-element.48), channel_id=1, source_target_pairs={{0,24},{2,26},{4,28},{6,30},{8,16},{10,18},{12,20},{14,22},{16,8},... | collective-permute-start | bytes 196616 | tf_op jit(solution)/shard_map/ppermute | solution.py:209
  29.4 1.3 %collective-permute-done.6.refs_5_ = bf16[128,256]{1,0:T(8,128)(2,1)S(1)} collective-permute-done((bf16[128,256]{1,0:T(8,128)(2,1)S(1)}, bf16[128,256]{1,0:T(8,128)(2,1)S(1)}, u32[]{:S(2)}, u32[]{:S(2)}) %collective-permute-start.6) | collective-permute-done | bytes 65568 | tf_op jit(solution)/shard_map/ppermute | solution.py:209
  30.7 0.4 collective-permute-done.7.refs_6_
  31.1 2.7 %collective-permute-done.8.refs_7_ = bf16[128,256]{1,0:T(8,128)(2,1)S(1)} collective-permute-done((bf16[128,256]{1,0:T(8,128)(2,1)S(1)}, bf16[128,256]{1,0:T(8,128)(2,1)S(1)}, u32[]{:S(2)}, u32[]{:S(2)}) %collective-permute-start.8) | collective-permute-done | bytes 65568 | tf_op jit(solution)/shard_map/ppermute | solution.py:209
  33.9 11.4 %shard_map.85 = (bf16[64,256]{1,0:T(8,128)(2,1)S(1)}, bf16[64,256]{1,0:T(8,128)(2,1)S(1)}, bf16[64,256]{1,0:T(8,128)(2,1)S(1)}, bf16[64,256]{1,0:T(8,128)(2,1)S(...) custom-call(bf16[1024,128]{1,0:T(8,128)(2,1)S(1)} %constant_dynamic-, ...), custom_call_target="tpu_custom_call" | custom-call | flops 2147483648 | bytes 2097152 | tf_op jit(solution)/shard_map/pallas_call | solution.py:234
  45.3 0.0 copy-start.1
  45.3 0.0 copy-start.3
  45.3 11.1 %shard_map.88 = (bf16[1024,128]{1,0:T(8,128)(2,1)S(1)}, bf16[1024,128]{1,0:T(8,128)(2,1)S(1)}, bf16[1024,128]{1,0:T(8,128)(2,1)S(1)}, bf16[1024,128]{1,0:T(8,128...) custom-call(f32[4,1,256]{2,1,0:T(1,128)S(1)} %get-tuple-element.54.l, ...), custom_call_target="tpu_custom_call" | custom-call | flops 5368709120 | bytes 2097152 | tf_op jit(solution)/shard_map/pallas_call | solution.py:274
  56.4 0.1 collective-permute-start.14
  56.5 1.8 %collective-permute-start.9 = (bf16[64,256]{1,0:T(8,128)(2,1)S(1)}, bf16[64,256]{1,0:T(8,128)(2,1)S(1)}, u32[]{:S(2)}, u32[]{:S(2)}) collective-permute-start(bf16[64,256]{1,0:T(8,128)(2,1)S(1)} %get-tuple-element.50), channel_id=1, source_target_pairs={{0,8},{2,10},{4,12},{6,14},{8,0},{10,2},{12,4},{14,6},{16,24},{18,... | collective-permute-start | bytes 98312 | tf_op jit(solution)/shard_map/ppermute | solution.py:209
  58.3 1.2 %collective-permute-start.10 = (bf16[64,256]{1,0:T(8,128)(2,1)S(1)}, bf16[64,256]{1,0:T(8,128)(2,1)S(1)}, u32[]{:S(2)}, u32[]{:S(2)}) collective-permute-start(bf16[64,256]{1,0:T(8,128)(2,1)S(1)} %get-tuple-element.51), channel_id=1, source_target_pairs={{0,16},{2,18},{4,20},{6,22},{8,24},{10,26},{12,28},{14,30},{16,0},... | collective-permute-start | bytes 98312 | tf_op jit(solution)/shard_map/ppermute | solution.py:209
  59.5 1.4 %collective-permute-start.11 = (bf16[64,256]{1,0:T(8,128)(2,1)S(1)}, bf16[64,256]{1,0:T(8,128)(2,1)S(1)}, u32[]{:S(2)}, u32[]{:S(2)}) collective-permute-start(bf16[64,256]{1,0:T(8,128)(2,1)S(1)} %get-tuple-element.52), channel_id=1, source_target_pairs={{0,24},{2,26},{4,28},{6,30},{8,16},{10,18},{12,20},{14,22},{16,8},... | collective-permute-start | bytes 98312 | tf_op jit(solution)/shard_map/ppermute | solution.py:209
  61.0 2.7 %collective-permute-done.10.refs_2_ = bf16[64,256]{1,0:T(8,128)(2,1)S(1)} collective-permute-done((bf16[64,256]{1,0:T(8,128)(2,1)S(1)}, bf16[64,256]{1,0:T(8,128)(2,1)S(1)}, u32[]{:S(2)}, u32[]{:S(2)}) %collective-permute-start.10) | collective-permute-done | bytes 32800 | tf_op jit(solution)/shard_map/ppermute | solution.py:209
  63.7 1.6 %collective-permute-done.11.refs_3_ = bf16[64,256]{1,0:T(8,128)(2,1)S(1)} collective-permute-done((bf16[64,256]{1,0:T(8,128)(2,1)S(1)}, bf16[64,256]{1,0:T(8,128)(2,1)S(1)}, u32[]{:S(2)}, u32[]{:S(2)}) %collective-permute-start.11) | collective-permute-done | bytes 32800 | tf_op jit(solution)/shard_map/ppermute | solution.py:209
  65.3 1.4 %shard_map.86 = (bf16[256,768]{1,0:T(8,128)(2,1)S(1)}, bf16[4,64,768]{2,1,0:T(8,128)(2,1)S(1)}) custom-call(s32[2]{0:T(128)S(1)} %copy-done.6, bf16[4,64,768]{2,1,0:T(8,128)(2,1)S(1)} %copy-done.1, bf16[256,768]{1,0:T(8,128)(2,1)S(1)} %copy-done.3, bf16[64,256]{1,0:T(8,128)(2,1)S(1)} %get-tuple-element.49.refs_0_, ...), custom_call_target="tpu_custom_call" | custom-call | flops 201326592 | bytes 786432 | tf_op jit(solution)/shard_map/pallas_call | solution.py:245
  66.7 0.1 collective-permute-start.22
  66.8 1.6 %collective-permute-start.23 = (bf16[64,768]{1,0:T(8,128)(2,1)S(1)}, bf16[64,768]{1,0:T(8,128)(2,1)S(1)}, u32[]{:S(2)}, u32[]{:S(2)}) collective-permute-start(bf16[64,768]{1,0:T(8,128)(2,1)S(1)} %get-tuple-element.72), channel_id=1, source_target_pairs={{0,4},{2,6},{4,0},{6,2},{8,12},{10,14},{12,8},{14,10},{16,20},{18,... | collective-permute-start | bytes 294920 | tf_op jit(solution)/shard_map/ppermute | solution.py:209
  68.4 0.3 collective-permute-start.24
  68.7 0.3 collective-permute-start.13
  69.0 0.1 shard_map.90
  69.1 1.6 %collective-permute-start.15 = (bf16[1024,128]{1,0:T(8,128)(2,1)S(1)}, bf16[1024,128]{1,0:T(8,128)(2,1)S(1)}, u32[]{:S(2)}, u32[]{:S(2)}) collective-permute-start(bf16[1024,128]{1,0:T(8,128)(2,1)S(1)} %shard_map.90), channel_id=1, source_target_pairs={{0,4},{2,6},{4,0},{6,2},{8,12},{10,14},{12,8},{14,10},{16,20},{18,... | collective-permute-start | bytes 786440 | tf_op jit(solution)/shard_map/ppermute | solution.py:209
  70.7 1.8 %collective-permute-done.23.refs_2_ = bf16[64,768]{1,0:T(8,128)(2,1)S(1)} collective-permute-done((bf16[64,768]{1,0:T(8,128)(2,1)S(1)}, bf16[64,768]{1,0:T(8,128)(2,1)S(1)}, u32[]{:S(2)}, u32[]{:S(2)}) %collective-permute-start.23) | collective-permute-done | bytes 98336 | tf_op jit(solution)/shard_map/ppermute | solution.py:209
  72.5 1.2 %collective-permute-done.24.refs_3_ = bf16[64,768]{1,0:T(8,128)(2,1)S(1)} collective-permute-done((bf16[64,768]{1,0:T(8,128)(2,1)S(1)}, bf16[64,768]{1,0:T(8,128)(2,1)S(1)}, u32[]{:S(2)}, u32[]{:S(2)}) %collective-permute-start.24) | collective-permute-done | bytes 98336 | tf_op jit(solution)/shard_map/ppermute | solution.py:209
  73.7 0.1 shard_map.94
  73.7 0.1 collective-permute-start.25
  73.9 2.1 %collective-permute-start.26 = (bf16[16,768]{1,0:T(8,128)(2,1)S(1)}, bf16[16,768]{1,0:T(8,128)(2,1)S(1)}, u32[]{:S(2)}, u32[]{:S(2)}) collective-permute-start(bf16[16,768]{1,0:T(8,128)(2,1)S(1)} %get-tuple-element.76), channel_id=1, source_target_pairs={{0,16},{2,18},{4,20},{6,22},{8,24},{10,26},{12,28},{14,30},{16,0},... | collective-permute-start | bytes 73736 | tf_op jit(solution)/shard_map/ppermute | solution.py:209
  75.9 2.3 %collective-permute-start.27 = (bf16[16,768]{1,0:T(8,128)(2,1)S(1)}, bf16[16,768]{1,0:T(8,128)(2,1)S(1)}, u32[]{:S(2)}, u32[]{:S(2)}) collective-permute-start(bf16[16,768]{1,0:T(8,128)(2,1)S(1)} %get-tuple-element.77), channel_id=1, source_target_pairs={{0,24},{2,26},{4,28},{6,30},{8,16},{10,18},{12,20},{14,22},{16,8},... | collective-permute-start | bytes 73736 | tf_op jit(solution)/shard_map/ppermute | solution.py:209
  78.2 0.4 collective-permute-done.26.refs_2_
  78.6 2.9 %collective-permute-done.27.refs_3_ = bf16[16,768]{1,0:T(8,128)(2,1)S(1)} collective-permute-done((bf16[16,768]{1,0:T(8,128)(2,1)S(1)}, bf16[16,768]{1,0:T(8,128)(2,1)S(1)}, u32[]{:S(2)}, u32[]{:S(2)}) %collective-permute-start.27) | collective-permute-done | bytes 24608 | tf_op jit(solution)/shard_map/ppermute | solution.py:209
  81.6 2.3 %collective-permute-start.30 = (bf16[16,768]{1,0:T(8,128)(2,1)S(1)}, bf16[16,768]{1,0:T(8,128)(2,1)S(1)}, u32[]{:S(2)}, u32[]{:S(2)}) collective-permute-start(bf16[16,768]{1,0:T(8,128)(2,1)S(1)} %shard_map.95), channel_id=1, source_target_pairs={{0,24},{2,26},{4,28},{6,30},{8,16},{10,18},{12,20},{14,22},{16,8},... | collective-permute-start | bytes 73736 | tf_op jit(solution)/shard_map/ppermute | solution.py:209
  83.9 2.1 %collective-permute-start.28 = (bf16[16,768]{1,0:T(8,128)(2,1)S(1)}, bf16[16,768]{1,0:T(8,128)(2,1)S(1)}, u32[]{:S(2)}, u32[]{:S(2)}) collective-permute-start(bf16[16,768]{1,0:T(8,128)(2,1)S(1)} %shard_map.95), channel_id=1, source_target_pairs={{0,8},{2,10},{4,12},{6,14},{8,0},{10,2},{12,4},{14,6},{16,24},{18,... | collective-permute-start | bytes 73736 | tf_op jit(solution)/shard_map/ppermute | solution.py:209
  86.0 1.2 %collective-permute-done.30 = bf16[16,768]{1,0:T(8,128)(2,1)S(1)} collective-permute-done((bf16[16,768]{1,0:T(8,128)(2,1)S(1)}, bf16[16,768]{1,0:T(8,128)(2,1)S(1)}, u32[]{:S(2)}, u32[]{:S(2)}) %collective-permute-start.30) | collective-permute-done | bytes 24608 | tf_op jit(solution)/shard_map/ppermute | solution.py:209
  87.3 1.5 %collective-permute-start.12 = (bf16[256,768]{1,0:T(8,128)(2,1)S(1)}, bf16[256,768]{1,0:T(8,128)(2,1)S(1)}, u32[]{:S(2)}, u32[]{:S(2)}) collective-permute-start(bf16[256,768]{1,0:T(8,128)(2,1)S(1)} %get-tuple-element.53.refs_0_), channel_id=1, source_target_pairs={{0,1},{1,0},{2,3},{3,2},{4,5},{5,4},{6,7},{7,6},{8,9},{9,8},{10,11... | collective-permute-start | bytes 1179656 | tf_op jit(solution)/shard_map/ppermute | solution.py:209
  88.8 0.1 collective-permute-start.31
  88.9 1.6 %collective-permute-start.32 = (bf16[64,768]{1,0:T(8,128)(2,1)S(1)}, bf16[64,768]{1,0:T(8,128)(2,1)S(1)}, u32[]{:S(2)}, u32[]{:S(2)}) collective-permute-start(bf16[64,768]{1,0:T(8,128)(2,1)S(1)} %pad_maximum_fusion.refs_0_), channel_id=1, source_target_pairs={{0,4},{2,6},{4,0},{6,2},{8,12},{10,14},{12,8},{14,10},{16,20},{18,... | collective-permute-start | bytes 294920 | tf_op jit(solution)/shard_map/ppermute | solution.py:209
  90.4 0.1 shard_map.89.refs_0_
  90.5 0.3 collective-permute-start.33
  90.9 0.1 shard_map.91
  91.0 1.7 %collective-permute-done.19.refs_5_ = bf16[64,256]{1,0:T(8,128)(2,1)S(1)} collective-permute-done((bf16[64,256]{1,0:T(8,128)(2,1)S(1)}, bf16[64,256]{1,0:T(8,128)(2,1)S(1)}, u32[]{:S(2)}, u32[]{:S(2)}) %collective-permute-start.19) | collective-permute-done | bytes 32800 | tf_op jit(solution)/shard_map/ppermute | solution.py:209
  92.7 0.4 collective-permute-start.16
  93.0 2.5 %collective-permute-start.17 = (bf16[256,128]{1,0:T(8,128)(2,1)S(1)}, bf16[256,128]{1,0:T(8,128)(2,1)S(1)}, u32[]{:S(2)}, u32[]{:S(2)}) collective-permute-start(bf16[256,128]{1,0:T(8,128)(2,1)S(1)} %get-tuple-element.79), channel_id=1, source_target_pairs={{0,16},{2,18},{4,20},{6,22},{8,24},{10,26},{12,28},{14,30},{16,0},... | collective-permute-start | bytes 196616 | tf_op jit(solution)/shard_map/ppermute | solution.py:209
  95.5 1.5 %collective-permute-start.18 = (bf16[256,128]{1,0:T(8,128)(2,1)S(1)}, bf16[256,128]{1,0:T(8,128)(2,1)S(1)}, u32[]{:S(2)}, u32[]{:S(2)}) collective-permute-start(bf16[256,128]{1,0:T(8,128)(2,1)S(1)} %get-tuple-element.78), channel_id=1, source_target_pairs={{0,24},{2,26},{4,28},{6,30},{8,16},{10,18},{12,20},{14,22},{16,8},... | collective-permute-start | bytes 196616 | tf_op jit(solution)/shard_map/ppermute | solution.py:209
  97.1 1.5 %collective-permute-start.20 = (bf16[64,256]{1,0:T(8,128)(2,1)S(1)}, bf16[64,256]{1,0:T(8,128)(2,1)S(1)}, u32[]{:S(2)}, u32[]{:S(2)}) collective-permute-start(bf16[64,256]{1,0:T(8,128)(2,1)S(1)} %get-tuple-element.65), channel_id=1, source_target_pairs={{0,16},{2,18},{4,20},{6,22},{8,24},{10,26},{12,28},{14,30},{16,0},... | collective-permute-start | bytes 98312 | tf_op jit(solution)/shard_map/ppermute | solution.py:209
  98.5 1.8 %collective-permute-start.21 = (bf16[64,256]{1,0:T(8,128)(2,1)S(1)}, bf16[64,256]{1,0:T(8,128)(2,1)S(1)}, u32[]{:S(2)}, u32[]{:S(2)}) collective-permute-start(bf16[64,256]{1,0:T(8,128)(2,1)S(1)} %get-tuple-element.66), channel_id=1, source_target_pairs={{0,24},{2,26},{4,28},{6,30},{8,16},{10,18},{12,20},{14,22},{16,8},... | collective-permute-start | bytes 98312 | tf_op jit(solution)/shard_map/ppermute | solution.py:209
  100.3 0.9 shard_map.96
  101.2 0.8 shard_map.87
  102.1 2.6 %collective-permute-done.20.refs_6_ = bf16[64,256]{1,0:T(8,128)(2,1)S(1)} collective-permute-done((bf16[64,256]{1,0:T(8,128)(2,1)S(1)}, bf16[64,256]{1,0:T(8,128)(2,1)S(1)}, u32[]{:S(2)}, u32[]{:S(2)}) %collective-permute-start.20) | collective-permute-done | bytes 32800 | tf_op jit(solution)/shard_map/ppermute | solution.py:209
  104.7 1.2 %shard_map.92 = (f32[256,4,128]{2,1,0:T(4,128)}, f32[4,64,256]{2,1,0:T(8,128)}) custom-call(bf16[256,128]{1,0:T(8,128)(2,1)S(1)} %get-tuple-element.81.refs_0_, bf16[256,128]{1,0:T(8,128)(2,1)S(1)} %collective-permute-done.16.refs_1_, bf16[256,128]{1,0:T(8,128)(2,1)S(1)} %collective-permute-done.17.refs_2_, ...), custom_call_target="tpu_custom_call" | custom-call | bytes 524288 | tf_op jit(solution)/shard_map/pallas_call | solution.py:293
  (37 shorter events, 0.2 us)
Async XLA Ops:
  0.6 0.7 copy-start.6
  1.3 1.0 copy-start
  2.3 1.0 copy-start.2
  3.3 0.9 copy-start.4
  4.2 0.9 copy-start.5
  6.7 5.7 %collective-permute-start = (bf16[256,128]{1,0:T(8,128)(2,1)S(1)}, bf16[256,128]{1,0:T(8,128)(2,1)S(1)}, u32[]{:S(2)}, u32[]{:S(2)}) collective-permute-start(bf16[256,128]{1,0:T(8,128)(2,1)S(1)} %get-tuple-element.42), channel_id=1, source_target_pairs={{0,8},{2,10},{4,12},{6,14},{8,0},{10,2},{12,4},{14,6},{16,24},{18,... | collective-permute-start | bytes 196616 | tf_op jit(solution)/shard_map/ppermute | solution.py:209
  9.8 7.3 %collective-permute-start.1 = (bf16[256,128]{1,0:T(8,128)(2,1)S(1)}, bf16[256,128]{1,0:T(8,128)(2,1)S(1)}, u32[]{:S(2)}, u32[]{:S(2)}) collective-permute-start(bf16[256,128]{1,0:T(8,128)(2,1)S(1)} %get-tuple-element.43), channel_id=1, source_target_pairs={{0,16},{2,18},{4,20},{6,22},{8,24},{10,26},{12,28},{14,30},{16,0},... | collective-permute-start | bytes 196616 | tf_op jit(solution)/shard_map/ppermute | solution.py:209
  12.4 6.1 %collective-permute-start.2 = (bf16[256,128]{1,0:T(8,128)(2,1)S(1)}, bf16[256,128]{1,0:T(8,128)(2,1)S(1)}, u32[]{:S(2)}, u32[]{:S(2)}) collective-permute-start(bf16[256,128]{1,0:T(8,128)(2,1)S(1)} %get-tuple-element.44), channel_id=1, source_target_pairs={{0,24},{2,26},{4,28},{6,30},{8,16},{10,18},{12,20},{14,22},{16,8},... | collective-permute-start | bytes 196616 | tf_op jit(solution)/shard_map/ppermute | solution.py:209
  18.5 6.5 %collective-permute-start.4 = (bf16[1024,128]{1,0:T(8,128)(2,1)S(1)}, bf16[1024,128]{1,0:T(8,128)(2,1)S(1)}, u32[]{:S(2)}, u32[]{:S(2)}) collective-permute-start(bf16[1024,128]{1,0:T(8,128)(2,1)S(1)} %constant_dynamic-update-slice_fusion.refs_0_), channel_id=1, source_target_pairs={{0,4},{2,6},{4,0},{6,2},{8,12},{10,14},{12,8},{14,10},{16,20},{18,... | collective-permute-start | bytes 786440 | tf_op jit(solution)/shard_map/ppermute | solution.py:209
  20.1 13.8 %collective-permute-start.3 = (bf16[1024,128]{1,0:T(8,128)(2,1)S(1)}, bf16[1024,128]{1,0:T(8,128)(2,1)S(1)}, u32[]{:S(2)}, u32[]{:S(2)}) collective-permute-start(bf16[1024,128]{1,0:T(8,128)(2,1)S(1)} %constant_dynamic-update-slice_fusion.refs_0_), channel_id=1, source_target_pairs={{0,2},{2,0},{4,6},{6,4},{8,10},{10,8},{12,14},{14,12},{16,18},{18,... | collective-permute-start | bytes 786440 | tf_op jit(solution)/shard_map/ppermute | solution.py:209
  25.0 8.9 %collective-permute-start.5 = (bf16[1024,128]{1,0:T(8,128)(2,1)S(1)}, bf16[1024,128]{1,0:T(8,128)(2,1)S(1)}, u32[]{:S(2)}, u32[]{:S(2)}) collective-permute-start(bf16[1024,128]{1,0:T(8,128)(2,1)S(1)} %collective-permute-done.4.refs_2_), channel_id=1, source_target_pairs={{0,2},{2,0},{4,6},{6,4},{8,10},{10,8},{12,14},{14,12},{16,18},{18,... | collective-permute-start | bytes 786440 | tf_op jit(solution)/shard_map/ppermute | solution.py:209
  25.0 5.7 %collective-permute-start.6 = (bf16[128,256]{1,0:T(8,128)(2,1)S(1)}, bf16[128,256]{1,0:T(8,128)(2,1)S(1)}, u32[]{:S(2)}, u32[]{:S(2)}) collective-permute-start(bf16[128,256]{1,0:T(8,128)(2,1)S(1)} %get-tuple-element.46), channel_id=1, source_target_pairs={{0,8},{2,10},{4,12},{6,14},{8,0},{10,2},{12,4},{14,6},{16,24},{18,... | collective-permute-start | bytes 196616 | tf_op jit(solution)/shard_map/ppermute | solution.py:209
  25.6 5.5 %collective-permute-start.7 = (bf16[128,256]{1,0:T(8,128)(2,1)S(1)}, bf16[128,256]{1,0:T(8,128)(2,1)S(1)}, u32[]{:S(2)}, u32[]{:S(2)}) collective-permute-start(bf16[128,256]{1,0:T(8,128)(2,1)S(1)} %get-tuple-element.47), channel_id=1, source_target_pairs={{0,16},{2,18},{4,20},{6,22},{8,24},{10,26},{12,28},{14,30},{16,0},... | collective-permute-start | bytes 196616 | tf_op jit(solution)/shard_map/ppermute | solution.py:209
  27.3 6.6 %collective-permute-start.8 = (bf16[128,256]{1,0:T(8,128)(2,1)S(1)}, bf16[128,256]{1,0:T(8,128)(2,1)S(1)}, u32[]{:S(2)}, u32[]{:S(2)}) collective-permute-start(bf16[128,256]{1,0:T(8,128)(2,1)S(1)} %get-tuple-element.48), channel_id=1, source_target_pairs={{0,24},{2,26},{4,28},{6,30},{8,16},{10,18},{12,20},{14,22},{16,8},... | collective-permute-start | bytes 196616 | tf_op jit(solution)/shard_map/ppermute | solution.py:209
  45.3 20.0 %copy-start.1 = (bf16[4,64,768]{2,1,0:T(8,128)(2,1)S(1)}, bf16[4,64,768]{2,1,0:T(8,128)(2,1)}, u32[]{:S(2)}) copy-start(bf16[4,64,768]{2,1,0:T(8,128)(2,1)} %w_ref.3) | copy-start | bytes 1179652
  45.3 20.0 %copy-start.3 = (bf16[256,768]{1,0:T(8,128)(2,1)S(1)}, bf16[256,768]{1,0:T(8,128)(2,1)}, u32[]{:S(2)}) copy-start(bf16[256,768]{1,0:T(8,128)(2,1)} %go_ref.3) | copy-start | bytes 1179652
  56.4 12.6 %collective-permute-start.14 = (bf16[1024,128]{1,0:T(8,128)(2,1)S(1)}, bf16[1024,128]{1,0:T(8,128)(2,1)S(1)}, u32[]{:S(2)}, u32[]{:S(2)}) collective-permute-start(bf16[1024,128]{1,0:T(8,128)(2,1)S(1)} %get-tuple-element.62), channel_id=1, source_target_pairs={{0,2},{2,0},{4,6},{6,4},{8,10},{10,8},{12,14},{14,12},{16,18},{18,... | collective-permute-start | bytes 786440 | tf_op jit(solution)/shard_map/ppermute | solution.py:209
  56.5 4.5 %collective-permute-start.9 = (bf16[64,256]{1,0:T(8,128)(2,1)S(1)}, bf16[64,256]{1,0:T(8,128)(2,1)S(1)}, u32[]{:S(2)}, u32[]{:S(2)}) collective-permute-start(bf16[64,256]{1,0:T(8,128)(2,1)S(1)} %get-tuple-element.50), channel_id=1, source_target_pairs={{0,8},{2,10},{4,12},{6,14},{8,0},{10,2},{12,4},{14,6},{16,24},{18,... | collective-permute-start | bytes 98312 | tf_op jit(solution)/shard_map/ppermute | solution.py:209
  58.3 5.3 %collective-permute-start.10 = (bf16[64,256]{1,0:T(8,128)(2,1)S(1)}, bf16[64,256]{1,0:T(8,128)(2,1)S(1)}, u32[]{:S(2)}, u32[]{:S(2)}) collective-permute-start(bf16[64,256]{1,0:T(8,128)(2,1)S(1)} %get-tuple-element.51), channel_id=1, source_target_pairs={{0,16},{2,18},{4,20},{6,22},{8,24},{10,26},{12,28},{14,30},{16,0},... | collective-permute-start | bytes 98312 | tf_op jit(solution)/shard_map/ppermute | solution.py:209
  59.5 5.7 %collective-permute-start.11 = (bf16[64,256]{1,0:T(8,128)(2,1)S(1)}, bf16[64,256]{1,0:T(8,128)(2,1)S(1)}, u32[]{:S(2)}, u32[]{:S(2)}) collective-permute-start(bf16[64,256]{1,0:T(8,128)(2,1)S(1)} %get-tuple-element.52), channel_id=1, source_target_pairs={{0,24},{2,26},{4,28},{6,30},{8,16},{10,18},{12,20},{14,22},{16,8},... | collective-permute-start | bytes 98312 | tf_op jit(solution)/shard_map/ppermute | solution.py:209
  66.7 3.9 %collective-permute-start.22 = (bf16[64,768]{1,0:T(8,128)(2,1)S(1)}, bf16[64,768]{1,0:T(8,128)(2,1)S(1)}, u32[]{:S(2)}, u32[]{:S(2)}) collective-permute-start(bf16[64,768]{1,0:T(8,128)(2,1)S(1)} %get-tuple-element.71), channel_id=1, source_target_pairs={{0,2},{2,0},{4,6},{6,4},{8,10},{10,8},{12,14},{14,12},{16,18},{18,... | collective-permute-start | bytes 294920 | tf_op jit(solution)/shard_map/ppermute | solution.py:209
  66.8 5.7 %collective-permute-start.23 = (bf16[64,768]{1,0:T(8,128)(2,1)S(1)}, bf16[64,768]{1,0:T(8,128)(2,1)S(1)}, u32[]{:S(2)}, u32[]{:S(2)}) collective-permute-start(bf16[64,768]{1,0:T(8,128)(2,1)S(1)} %get-tuple-element.72), channel_id=1, source_target_pairs={{0,4},{2,6},{4,0},{6,2},{8,12},{10,14},{12,8},{14,10},{16,20},{18,... | collective-permute-start | bytes 294920 | tf_op jit(solution)/shard_map/ppermute | solution.py:209
  68.4 5.3 %collective-permute-start.24 = (bf16[64,768]{1,0:T(8,128)(2,1)S(1)}, bf16[64,768]{1,0:T(8,128)(2,1)S(1)}, u32[]{:S(2)}, u32[]{:S(2)}) collective-permute-start(bf16[64,768]{1,0:T(8,128)(2,1)S(1)} %get-tuple-element.73), channel_id=1, source_target_pairs={{0,6},{2,4},{4,2},{6,0},{8,14},{10,12},{12,10},{14,8},{16,22},{18,... | collective-permute-start | bytes 294920 | tf_op jit(solution)/shard_map/ppermute | solution.py:209
  68.7 20.2 %collective-permute-start.13 = (bf16[1024,128]{1,0:T(8,128)(2,1)S(1)}, bf16[1024,128]{1,0:T(8,128)(2,1)S(1)}, u32[]{:S(2)}, u32[]{:S(2)}) collective-permute-start(bf16[1024,128]{1,0:T(8,128)(2,1)S(1)} %get-tuple-element.60), channel_id=1, source_target_pairs={{0,2},{2,0},{4,6},{6,4},{8,10},{10,8},{12,14},{14,12},{16,18},{18,... | collective-permute-start | bytes 786440 | tf_op jit(solution)/shard_map/ppermute | solution.py:209
  69.1 21.4 %collective-permute-start.15 = (bf16[1024,128]{1,0:T(8,128)(2,1)S(1)}, bf16[1024,128]{1,0:T(8,128)(2,1)S(1)}, u32[]{:S(2)}, u32[]{:S(2)}) collective-permute-start(bf16[1024,128]{1,0:T(8,128)(2,1)S(1)} %shard_map.90), channel_id=1, source_target_pairs={{0,4},{2,6},{4,0},{6,2},{8,12},{10,14},{12,8},{14,10},{16,20},{18,... | collective-permute-start | bytes 786440 | tf_op jit(solution)/shard_map/ppermute | solution.py:209
  73.7 4.5 %collective-permute-start.25 = (bf16[16,768]{1,0:T(8,128)(2,1)S(1)}, bf16[16,768]{1,0:T(8,128)(2,1)S(1)}, u32[]{:S(2)}, u32[]{:S(2)}) collective-permute-start(bf16[16,768]{1,0:T(8,128)(2,1)S(1)} %get-tuple-element.75), channel_id=1, source_target_pairs={{0,8},{2,10},{4,12},{6,14},{8,0},{10,2},{12,4},{14,6},{16,24},{18,... | collective-permute-start | bytes 73736 | tf_op jit(solution)/shard_map/ppermute | solution.py:209
  73.9 4.8 %collective-permute-start.26 = (bf16[16,768]{1,0:T(8,128)(2,1)S(1)}, bf16[16,768]{1,0:T(8,128)(2,1)S(1)}, u32[]{:S(2)}, u32[]{:S(2)}) collective-permute-start(bf16[16,768]{1,0:T(8,128)(2,1)S(1)} %get-tuple-element.76), channel_id=1, source_target_pairs={{0,16},{2,18},{4,20},{6,22},{8,24},{10,26},{12,28},{14,30},{16,0},... | collective-permute-start | bytes 73736 | tf_op jit(solution)/shard_map/ppermute | solution.py:209
  75.9 5.6 %collective-permute-start.27 = (bf16[16,768]{1,0:T(8,128)(2,1)S(1)}, bf16[16,768]{1,0:T(8,128)(2,1)S(1)}, u32[]{:S(2)}, u32[]{:S(2)}) collective-permute-start(bf16[16,768]{1,0:T(8,128)(2,1)S(1)} %get-tuple-element.77), channel_id=1, source_target_pairs={{0,24},{2,26},{4,28},{6,30},{8,16},{10,18},{12,20},{14,22},{16,8},... | collective-permute-start | bytes 73736 | tf_op jit(solution)/shard_map/ppermute | solution.py:209
  81.6 5.7 %collective-permute-start.30 = (bf16[16,768]{1,0:T(8,128)(2,1)S(1)}, bf16[16,768]{1,0:T(8,128)(2,1)S(1)}, u32[]{:S(2)}, u32[]{:S(2)}) collective-permute-start(bf16[16,768]{1,0:T(8,128)(2,1)S(1)} %shard_map.95), channel_id=1, source_target_pairs={{0,24},{2,26},{4,28},{6,30},{8,16},{10,18},{12,20},{14,22},{16,8},... | collective-permute-start | bytes 73736 | tf_op jit(solution)/shard_map/ppermute | solution.py:209
  83.9 4.8 %collective-permute-start.29 = (bf16[16,768]{1,0:T(8,128)(2,1)S(1)}, bf16[16,768]{1,0:T(8,128)(2,1)S(1)}, u32[]{:S(2)}, u32[]{:S(2)}) collective-permute-start(bf16[16,768]{1,0:T(8,128)(2,1)S(1)} %shard_map.95), channel_id=1, source_target_pairs={{0,16},{2,18},{4,20},{6,22},{8,24},{10,26},{12,28},{14,30},{16,0},... | collective-permute-start | bytes 73736 | tf_op jit(solution)/shard_map/ppermute | solution.py:209
  83.9 4.8 %collective-permute-start.28 = (bf16[16,768]{1,0:T(8,128)(2,1)S(1)}, bf16[16,768]{1,0:T(8,128)(2,1)S(1)}, u32[]{:S(2)}, u32[]{:S(2)}) collective-permute-start(bf16[16,768]{1,0:T(8,128)(2,1)S(1)} %shard_map.95), channel_id=1, source_target_pairs={{0,8},{2,10},{4,12},{6,14},{8,0},{10,2},{12,4},{14,6},{16,24},{18,... | collective-permute-start | bytes 73736 | tf_op jit(solution)/shard_map/ppermute | solution.py:209
  87.3 11.3 %collective-permute-start.12 = (bf16[256,768]{1,0:T(8,128)(2,1)S(1)}, bf16[256,768]{1,0:T(8,128)(2,1)S(1)}, u32[]{:S(2)}, u32[]{:S(2)}) collective-permute-start(bf16[256,768]{1,0:T(8,128)(2,1)S(1)} %get-tuple-element.53.refs_0_), channel_id=1, source_target_pairs={{0,1},{1,0},{2,3},{3,2},{4,5},{5,4},{6,7},{7,6},{8,9},{9,8},{10,11... | collective-permute-start | bytes 1179656 | tf_op jit(solution)/shard_map/ppermute | solution.py:209
  88.7 3.9 %collective-permute-start.19 = (bf16[64,256]{1,0:T(8,128)(2,1)S(1)}, bf16[64,256]{1,0:T(8,128)(2,1)S(1)}, u32[]{:S(2)}, u32[]{:S(2)}) collective-permute-start(bf16[64,256]{1,0:T(8,128)(2,1)S(1)} %get-tuple-element.64), channel_id=1, source_target_pairs={{0,8},{2,10},{4,12},{6,14},{8,0},{10,2},{12,4},{14,6},{16,24},{18,... | collective-permute-start | bytes 98312 | tf_op jit(solution)/shard_map/ppermute | solution.py:209
  88.8 4.3 %collective-permute-start.31 = (bf16[64,768]{1,0:T(8,128)(2,1)S(1)}, bf16[64,768]{1,0:T(8,128)(2,1)S(1)}, u32[]{:S(2)}, u32[]{:S(2)}) collective-permute-start(bf16[64,768]{1,0:T(8,128)(2,1)S(1)} %pad_maximum_fusion.refs_0_), channel_id=1, source_target_pairs={{0,2},{2,0},{4,6},{6,4},{8,10},{10,8},{12,14},{14,12},{16,18},{18,... | collective-permute-start | bytes 294920 | tf_op jit(solution)/shard_map/ppermute | solution.py:209
  88.9 6.7 %collective-permute-start.32 = (bf16[64,768]{1,0:T(8,128)(2,1)S(1)}, bf16[64,768]{1,0:T(8,128)(2,1)S(1)}, u32[]{:S(2)}, u32[]{:S(2)}) collective-permute-start(bf16[64,768]{1,0:T(8,128)(2,1)S(1)} %pad_maximum_fusion.refs_0_), channel_id=1, source_target_pairs={{0,4},{2,6},{4,0},{6,2},{8,12},{10,14},{12,8},{14,10},{16,20},{18,... | collective-permute-start | bytes 294920 | tf_op jit(solution)/shard_map/ppermute | solution.py:209
  90.5 6.5 %collective-permute-start.33 = (bf16[64,768]{1,0:T(8,128)(2,1)S(1)}, bf16[64,768]{1,0:T(8,128)(2,1)S(1)}, u32[]{:S(2)}, u32[]{:S(2)}) collective-permute-start(bf16[64,768]{1,0:T(8,128)(2,1)S(1)} %pad_maximum_fusion.refs_0_), channel_id=1, source_target_pairs={{0,6},{2,4},{4,2},{6,0},{8,14},{10,12},{12,10},{14,8},{16,22},{18,... | collective-permute-start | bytes 294920 | tf_op jit(solution)/shard_map/ppermute | solution.py:209
  92.7 12.0 %collective-permute-start.16 = (bf16[256,128]{1,0:T(8,128)(2,1)S(1)}, bf16[256,128]{1,0:T(8,128)(2,1)S(1)}, u32[]{:S(2)}, u32[]{:S(2)}) collective-permute-start(bf16[256,128]{1,0:T(8,128)(2,1)S(1)} %get-tuple-element.80), channel_id=1, source_target_pairs={{0,8},{2,10},{4,12},{6,14},{8,0},{10,2},{12,4},{14,6},{16,24},{18,... | collective-permute-start | bytes 196616 | tf_op jit(solution)/shard_map/ppermute | solution.py:209
  93.0 11.6 %collective-permute-start.17 = (bf16[256,128]{1,0:T(8,128)(2,1)S(1)}, bf16[256,128]{1,0:T(8,128)(2,1)S(1)}, u32[]{:S(2)}, u32[]{:S(2)}) collective-permute-start(bf16[256,128]{1,0:T(8,128)(2,1)S(1)} %get-tuple-element.79), channel_id=1, source_target_pairs={{0,16},{2,18},{4,20},{6,22},{8,24},{10,26},{12,28},{14,30},{16,0},... | collective-permute-start | bytes 196616 | tf_op jit(solution)/shard_map/ppermute | solution.py:209
  95.5 9.2 %collective-permute-start.18 = (bf16[256,128]{1,0:T(8,128)(2,1)S(1)}, bf16[256,128]{1,0:T(8,128)(2,1)S(1)}, u32[]{:S(2)}, u32[]{:S(2)}) collective-permute-start(bf16[256,128]{1,0:T(8,128)(2,1)S(1)} %get-tuple-element.78), channel_id=1, source_target_pairs={{0,24},{2,26},{4,28},{6,30},{8,16},{10,18},{12,20},{14,22},{16,8},... | collective-permute-start | bytes 196616 | tf_op jit(solution)/shard_map/ppermute | solution.py:209
  97.1 7.6 %collective-permute-start.20 = (bf16[64,256]{1,0:T(8,128)(2,1)S(1)}, bf16[64,256]{1,0:T(8,128)(2,1)S(1)}, u32[]{:S(2)}, u32[]{:S(2)}) collective-permute-start(bf16[64,256]{1,0:T(8,128)(2,1)S(1)} %get-tuple-element.65), channel_id=1, source_target_pairs={{0,16},{2,18},{4,20},{6,22},{8,24},{10,26},{12,28},{14,30},{16,0},... | collective-permute-start | bytes 98312 | tf_op jit(solution)/shard_map/ppermute | solution.py:209
  98.5 6.1 %collective-permute-start.21 = (bf16[64,256]{1,0:T(8,128)(2,1)S(1)}, bf16[64,256]{1,0:T(8,128)(2,1)S(1)}, u32[]{:S(2)}, u32[]{:S(2)}) collective-permute-start(bf16[64,256]{1,0:T(8,128)(2,1)S(1)} %get-tuple-element.66), channel_id=1, source_target_pairs={{0,24},{2,26},{4,28},{6,30},{8,16},{10,18},{12,20},{14,22},{16,8},... | collective-permute-start | bytes 98312 | tf_op jit(solution)/shard_map/ppermute | solution.py:209

commit v2 on v1

v2 whole, which is shorter than its diff:
```python
import functools

import jax
import jax.numpy as jnp
from jax import lax
from jax.experimental import pallas as pl
from jax.experimental.pallas import tpu as pltpu
from jax.sharding import PartitionSpec as P

TILE = 128
DEAD = 1024.0
BIAS = -1e30
F32 = jnp.float32
BF16 = jnp.bfloat16
VMEM = pl.BlockSpec(memory_space=pltpu.VMEM)
SMEM = pl.BlockSpec(memory_space=pltpu.SMEM)
LIMIT = 48 * 1024 * 1024


def dot(a, b):
    return lax.dot_general(a, b, (((1,), (0,)), ((), ())), preferred_element_type=F32)


def dot_nt(a, b):
    return lax.dot_general(a, b, (((1,), (1,)), ((), ())), preferred_element_type=F32)


def call(kernel, outs, scratch=(), n_in=1, smem_first=False, flops=0, moved=0):
    specs = [VMEM] * n_in
    if smem_first:
        specs[0] = SMEM
    return pl.pallas_call(
        kernel,
        out_shape=[jax.ShapeDtypeStruct(shape, kind) for shape, kind in outs],
        in_specs=specs,
        out_specs=[VMEM] * len(outs),
        scratch_shapes=list(scratch),
        compiler_params=pltpu.CompilerParams(vmem_limit_bytes=LIMIT),
        cost_estimate=pl.CostEstimate(flops=flops, bytes_accessed=moved, transcendentals=0),
    )


def live_column(fill_ref, rows):
    parts = []
    within = lax.broadcasted_iota(jnp.int32, (TILE, 1), 0)
    for tile in range(rows // TILE):
        parts.append(jnp.where(within < fill_ref[tile], 1.0, 0.0))
    return jnp.concatenate(parts, axis=0) if len(parts) > 1 else parts[0]


def pack_kernel(heads, rows, dim, fill_ref, q_ref, kv_ref, w_ref, go_ref, out_ref):
    live = live_column(fill_ref, rows)
    mixed = jnp.where(live > 0, go_ref[...].astype(F32), 0.0).astype(BF16)
    lane = lax.broadcasted_iota(jnp.int32, (rows, 2 * dim), 1)
    mark = jnp.where(lane == 0, DEAD, 0.0)
    for head in range(heads):
        grad = dot_nt(w_ref[head], mixed).astype(BF16)
        scaled = (q_ref[head].astype(F32) * dim**-0.5).astype(BF16)
        pair = kv_ref[:, head, :].astype(F32)
        out_ref[head, 0:rows, :] = jnp.where(live > 0, pair, mark).astype(BF16)
        both = jnp.concatenate([scaled, grad], axis=0)
        for part in range(rows // (2 * dim)):
            across = slice(part * 2 * dim, (part + 1) * 2 * dim)
            out_ref[head, rows + part * 2 * dim : rows + (part + 1) * 2 * dim, :] = both[:, across]


def forward_kernel(slots, columns, rows, dim, *refs):
    blocks, refs = refs[:columns], refs[columns:]
    got_ref, att_out, log_ref, k_ref, v_ref, q_aug, g_aug, vt_ref = refs
    block = slots * rows
    lane = lax.broadcasted_iota(jnp.int32, (block, 2 * dim), 1)
    for column in range(columns):
        pair = blocks[column][...].astype(F32)
        dead = pair[:, 0:1] >= DEAD
        here = pl.ds(column * block, block)
        keys = jnp.where(lane < dim, pair, 0.0)
        k_ref[here, :] = jnp.where(dead, jnp.where(lane == dim, BIAS, 0.0), keys).astype(BF16)
        values = jnp.where(lane >= dim, pair, jnp.where(lane <= 1, 1.0, 0.0))
        values = jnp.where(dead, 0.0, values)
        v_ref[here, :] = values.astype(BF16)
        vt_ref[:, here] = values.T.astype(BF16)
    row = lax.broadcasted_iota(jnp.int32, (2 * dim, rows), 0)
    for slot in range(slots):
        pieces = [
            got_ref[slot, rows + part * 2 * dim : rows + (part + 1) * 2 * dim, :]
            for part in range(rows // (2 * dim))
        ]
        mixed = jnp.concatenate(pieces, axis=1).astype(F32)
        queries = jnp.where(row < dim, mixed, jnp.where(row == dim, 1.0, 0.0)).astype(BF16)
        q_aug[slot] = queries
        peak = jnp.full((1, rows), BIAS, F32)
        total = jnp.zeros((2 * dim, rows), F32)
        for column in range(columns):
            here = pl.ds(column * block, block)
            scores = dot(k_ref[here, :], queries)
            new_peak = jnp.maximum(peak, jnp.max(scores, axis=0, keepdims=True))
            exps = jnp.exp(scores - new_peak).astype(BF16)
            total = total * jnp.exp(peak - new_peak) + dot(vt_ref[:, here], exps)
            peak = new_peak
        weight = total[0:1, :]
        log_ref[slot] = peak + jnp.log(weight)
        attended = (total / weight).astype(BF16)
        att_out[slot] = attended[dim:, :]
        terms = jnp.where(row >= dim, mixed * attended.astype(F32), 0.0)
        inner = jnp.sum(terms, axis=0, keepdims=True)
        high = inner.astype(BF16).astype(F32)
        low = inner - high
        filled = jnp.where(row == 0, -high, jnp.where(row == 1, -low, 0.0))
        g_aug[slot] = jnp.where(row >= dim, mixed, filled).astype(BF16)


def backward_kernel(slots, columns, rows, dim, key_block, log_ref, k_ref, v_ref, q_aug, g_aug, *refs):
    dkv_out, dq_out, kt_ref, dq_acc = refs[:columns], *refs[columns:]
    block = slots * rows
    for column in range(columns):
        here = pl.ds(column * block, block)
        kt_ref[:, here] = k_ref[here, :].astype(F32).T.astype(BF16)
    lane = lax.broadcasted_iota(jnp.int32, (key_block, 2 * dim), 1)
    dq_acc[...] = jnp.zeros_like(dq_acc)
    for column in range(columns):
        for part in range(block // key_block):
            start = column * block + part * key_block
            here = pl.ds(start, key_block)
            keys, values = k_ref[here, :], v_ref[here, :]
            grad_k = jnp.zeros((key_block, 2 * dim), F32)
            grad_v = jnp.zeros((key_block, 2 * dim), F32)
            for slot in range(slots):
                probs = jnp.exp(dot(keys, q_aug[slot]) - log_ref[slot])
                grads = (probs * dot(values, g_aug[slot])).astype(BF16)
                grad_v = grad_v + dot_nt(probs.astype(BF16), g_aug[slot])
                grad_k = grad_k + dot_nt(grads, q_aug[slot])
                dq_acc[slot] += dot(kt_ref[:, here], grads)
            dkv_out[column][pl.ds(part * key_block, key_block), :] = jnp.where(lane < dim, grad_k, grad_v).astype(BF16)
    for slot in range(slots):
        grad = (dq_acc[slot, 0:dim, :] * dim**-0.5).astype(BF16)
        for part in range(rows // (2 * dim)):
            dq_out[slot, part * dim : (part + 1) * dim, :] = grad[:, part * 2 * dim : (part + 1) * 2 * dim]


def project_kernel(heads, rows, dim, fill_ref, w_ref, go_ref, att_ref, terms_ref, wt_ref):
    live = live_column(fill_ref, rows)
    mixed = jnp.where(live > 0, go_ref[...].astype(F32), 0.0).astype(BF16)
    total = None
    for head in range(heads):
        wt_ref[head] = dot(att_ref[head], mixed).astype(BF16)
        term = dot(att_ref[head].astype(F32).T.astype(BF16), w_ref[head])
        total = term if total is None else total + term
    terms_ref[...] = (total * live).astype(BF16)


def unpack_kernel(heads, rows, dim, got_ref, kv_out, q_out):
    for head in range(heads):
        kv_out[:, head, :] = got_ref[head, 0:rows, :].astype(F32)
        for part in range(rows // (2 * dim)):
            start = rows + part * dim
            q_out[head, :, part * 2 * dim : (part + 1) * 2 * dim] = got_ref[head, start : start + dim, :].astype(F32)


def add_send_kernel(slots, rows, kept_ref, came_ref, dq_ref, out_ref):
    for slot in range(slots):
        here = pl.ds(slot * rows, rows)
        total = kept_ref[here, :].astype(F32) + came_ref[here, :].astype(F32)
        out_ref[slot, 0:rows, :] = total.astype(BF16)
        out_ref[slot, rows:, :] = dq_ref[slot]


def halve_kernel(parts, bit, me_of, wt_ref, kept_ref, sent_ref):
    me = me_of()
    for relative in range(parts // 2):
        low = relative % bit + relative // bit * 2 * bit
        kept_ref[relative] = wt_ref[me ^ low]
        sent_ref[relative] = wt_ref[me ^ low ^ bit]


def sum_kernel(*refs):
    total = refs[0][...].astype(F32)
    for part in refs[1:-1]:
        total = total + part[...].astype(F32)
    refs[-1][...] = total.astype(refs[-1].dtype)


def sum_slots_kernel(slots, got_ref, out_ref):
    total = got_ref[0].astype(F32)
    for slot in range(1, slots):
        total = total + got_ref[slot].astype(F32)
    for slot in range(slots):
        out_ref[slot] = total.astype(BF16)


def place_kernel(columns, slots, piece, b_of, *refs):
    parts, (out_ref,) = refs[:columns], refs[columns:]
    me = b_of()
    for column in range(columns):
        for slot in range(slots):
            out_ref[me ^ column, slot * piece : (slot + 1) * piece, :] = parts[column][slot].astype(F32)


def shards(seq, mp, queries, key_value, tile_fill, out_weight, grad_output):
    rows, heads, dim = queries.shape
    width = grad_output.shape[1]
    slots = heads
    columns = seq // slots
    assert slots * columns == seq and columns & (columns - 1) == 0
    b_of = lambda: lax.axis_index("seq") % columns
    groups = [[a * columns + b for a in range(slots)] for b in range(columns)]

    def swap(array, mask, axis="seq", size=seq):
        return lax.ppermute(array, axis, [(i, i ^ mask) for i in range(size)])

    def exchange(array):
        if slots == 1:
            return array
        return lax.all_to_all(array, "seq", 0, 0, axis_index_groups=groups, tiled=True)

    block = slots * rows
    wide = 2 * dim
    qt = jnp.transpose(queries, (1, 2, 0))
    packed = call(
        functools.partial(pack_kernel, heads, rows, dim),
        [((heads, 2 * rows, wide), BF16)],
        n_in=5, smem_first=True,
        flops=2 * rows * heads * dim * width, moved=4 * rows * width,
    )(tile_fill, qt, key_value, out_weight, grad_output)[0]
    got = exchange(packed)
    own = got[:, :rows].reshape(block, wide)

    blocks = {0: own}
    bit = columns // 2
    while bit:
        for r in sorted(blocks):
            blocks[r ^ bit] = swap(blocks[r], bit)
        bit //= 2

    keys = seq * rows
    mults = block * keys * wide
    forward = call(
        functools.partial(forward_kernel, slots, columns, rows, dim),
        [((slots, dim, rows), BF16), ((slots, 1, rows), F32), ((keys, wide), BF16), ((keys, wide), BF16),
         ((slots, wide, rows), BF16), ((slots, wide, rows), BF16)],
        [pltpu.VMEM((wide, keys), BF16)],
        n_in=columns + 1, flops=4 * mults, moved=4 * keys * wide,
    )(*[blocks[r] for r in range(columns)], got)
    attended, saved = exchange(forward[0]), forward[1:]

    terms, weight_terms = call(
        functools.partial(project_kernel, heads, rows, dim),
        [((rows, width), BF16), ((heads, dim, width), BF16)],
        n_in=4, smem_first=True, flops=4 * rows * heads * dim * width, moved=4 * rows * width,
    )(tile_fill, out_weight, grad_output, attended)
    bit = 1
    while bit < mp:
        terms = call(sum_kernel, [((rows, width), BF16)], n_in=2, moved=6 * rows * width)(
            terms, swap(terms, bit, "mp", mp))[0]
        bit *= 2

    if columns == heads == 4:
        piece = dim // slots
        kept, sent = call(
            functools.partial(halve_kernel, columns, 1, b_of), [((columns // 2, dim, width), BF16)] * 2)(weight_terms)
        kept = call(sum_kernel, [((columns // 2, dim, width), BF16)], n_in=2)(kept, swap(sent, 1))[0]
        quarter = call(sum_kernel, [((dim, width), BF16)], n_in=2)(kept[0], swap(kept[1], 2))[0]
        summed = call(functools.partial(sum_slots_kernel, slots), [((slots, piece, width), BF16)])(
            exchange(quarter.reshape(slots, piece, width)))[0]
        mine = exchange(summed)
        across = swap(mine, 2)
        whole = [mine, swap(mine, 1), across, swap(across, 1)]
        weight_grad = call(
            functools.partial(place_kernel, columns, slots, piece, b_of),
            [((heads, dim, width), F32)], n_in=columns)(*whole)[0]
    else:
        weight_grad = lax.psum(weight_terms.astype(F32), "seq")

    key_block = min(block, 512)
    backward = call(
        functools.partial(backward_kernel, slots, columns, rows, dim, key_block),
        [((block, wide), BF16)] * columns + [((slots, rows // 2, wide), BF16)],
        [pltpu.VMEM((wide, keys), BF16), pltpu.VMEM((slots, wide, rows), F32)],
        n_in=5, flops=10 * mults, moved=4 * keys * wide,
    )(*saved)
    dkv, dq = dict(enumerate(backward[:columns])), backward[columns]
    bit = 1
    while 2 * bit < columns:
        kept = sorted(r for r in dkv if not r & bit)
        dkv = {
            r: call(sum_kernel, [((block, wide), BF16)], n_in=2, moved=12 * block * dim)(
                dkv[r], swap(dkv[r ^ bit], bit))[0]
            for r in kept
        }
        bit *= 2
    returned = call(
        functools.partial(add_send_kernel, slots, rows),
        [((slots, rows + rows // 2, wide), BF16)], n_in=3, moved=12 * block * dim,
    )(dkv[0], swap(dkv[bit], bit), dq)[0]
    key_value_grad, query_grad = call(
        functools.partial(unpack_kernel, heads, rows, dim),
        [((rows, heads, wide), F32), ((heads, dim, rows), F32)],
        moved=8 * rows * heads * dim,
    )(exchange(returned))
    return terms, jnp.transpose(query_grad, (2, 0, 1)), key_value_grad, weight_grad


def solution(mesh):
    return jax.shard_map(
        functools.partial(shards, mesh.shape["seq"], mesh.shape["mp"]),
        mesh=mesh,
        in_specs=(
            P("seq", "mp", None),
            P("seq", "mp", None),
            P("seq"),
            P("mp", None, None),
            P("seq", None),
        ),
        out_specs=(P("seq", None), P("seq", "mp", None), P("seq", "mp", None), P("mp", None, None)),
        check_vma=False,
    )
```

time: 106 us -> 109 us (1.028)
  blocking collectives: 0 us -> 30 us
  starting transfers between devices: 40 us -> 18.6 us
  waiting for transfers between devices: 31.6 us -> 24.1 us
  Pallas kernels: 28.8 us -> 30.6 us
    ppermute x34 -> x12, starting transfers between devices: 40 us -> 8.55 us  [swap(): return lax.ppermute(array, axis, [(i, i ^ mask) for i in range(size)])]
    all_to_all x0 -> x2, blocking collectives: none -> 30 us  [exchange(): lax.all_to_all(array, 'seq', 0, 0, axis_index_groups=groups, tiled=True)]
    ppermute x34 -> x12, waiting for transfers between devices: 31.6 us -> 15.1 us  [swap(): return lax.ppermute(array, axis, [(i, i ^ mask) for i in range(size)])]
    all_to_all x0 -> x3, starting transfers between devices: none -> 10.1 us  [exchange(): lax.all_to_all(array, 'seq', 0, 0, axis_index_groups=groups, tiled=True)]
    all_to_all x0 -> x3, waiting for transfers between devices: none -> 8.95 us  [exchange(): lax.all_to_all(array, 'seq', 0, 0, axis_index_groups=groups, tiled=True)]
    pallas_call x11 -> x12, Pallas kernels: 16.8 us -> 18.8 us  [the longest x1 11.4 us: shards(): call(functools.partial(forward_kernel, slots, columns, rows, dim), [((slo...]
    unnamed x17 -> x14, local copies, waits for them, and re-layouts: 4.54 us -> 4.5 us
  transfers between devices with their start and end apart: 34 -> 15, of which waited for: 15 -> 7; matrix products, arithmetic and copies ran while one was open for 0% -> 0% of each run, Pallas kernels for 3% -> 14%
where the time goes in v2:
time: 109 us
  Pallas kernels  30.6 us (28%)
  blocking collectives  30 us (28%)
  waiting for transfers between devices  24.1 us (22%)
  starting transfers between devices  18.6 us (17%)
  local copies, waits for them, and re-layouts  4.53 us (4%)
    all_to_all x2, blocking collectives, exchange(): lax.all_to_all(array, 'seq', 0, 0, axis_index_groups=groups, tiled=True)  30 us
    ppermute x12, waiting for transfers between devices, swap(): return lax.ppermute(array, axis, [(i, i ^ mask) for i in range(size)])  15.1 us
    pallas_call x1, Pallas kernels, shards(): call(functools.partial(forward_kernel, slots, columns, rows, dim), [((slo...  11.4 us
    pallas_call x1, Pallas kernels, shards(): call(functools.partial(backward_kernel, slots, columns, rows, dim, key_bl...  10.9 us
    all_to_all x3, starting transfers between devices, exchange(): lax.all_to_all(array, 'seq', 0, 0, axis_index_groups=groups, tiled=True)  10.1 us
    all_to_all x3, waiting for transfers between devices, exchange(): lax.all_to_all(array, 'seq', 0, 0, axis_index_groups=groups, tiled=True)  8.95 us
    ppermute x12, starting transfers between devices, swap(): return lax.ppermute(array, axis, [(i, i ^ mask) for i in range(size)])  8.55 us
    unnamed x14, local copies, waits for them, and re-layouts  4.5 us
  transfers between devices with their start and end apart: 15, of which 7 were waited for; matrix products, arithmetic and copies ran while one was open for 0% of the time, Pallas kernels for 14%

profile of v2, /device:TPU:0, one launch (start us, length us, event | category | flops | bytes accessed | tf_op | source)
XLA Modules:
  0.0 108.6 jit_solution(13819633537231067472)
XLA Ops:
  0.6 0.0 copy-start.6
  0.6 0.6 copy-done.6
  1.3 0.0 copy-start
  1.3 1.0 copy-done
  2.3 0.0 copy-start.2
  2.3 1.0 copy-done.2
  3.3 0.0 copy-start.4
  3.3 0.9 copy-done.4
  4.2 0.0 copy-start.5
  4.2 0.9 copy-done.5
  5.1 1.5 %shard_map.84 = bf16[4,512,128]{2,1,0:T(8,128)(2,1)S(1)} custom-call(s32[2]{0:T(128)S(1)} %copy-done.6, bf16[4,64,256]{2,1,0:T(8,128)(2,1)S(1)} %bitcast.11, bf16[256,4,128]{2,1,0:T(4,128)(2,1)S(1)} %copy-done.4, bf16[4,64,768]{2,1,0:T(8,128)(2,1)S(1)} %copy-done, bf16[256,768]{1,0:T(8,128)(2,1)S(1)} %copy-done.2), custom_call_target="tpu_custom_call" | custom-call | flops 100663296 | bytes 786432 | tf_op jit(solution)/shard_map/pallas_call | solution.py:218
  6.7 20.6 %all_to_all.25.refs_4_ = bf16[4,512,128]{2,1,0:T(8,128)(2,1)S(1)} all-to-all(bf16[4,512,128]{2,1,0:T(8,128)(2,1)S(1)} %shard_map.84), channel_id=1, replica_groups={{0,8,16,24},{2,10,18,26},{4,12,20,28},{6,14,22,30},{1,9,17,25},{3,11,19..., dimensions={0} | all-to-all | bytes 1048576 | tf_op jit(solution)/shard_map/all_to_all | solution.py:213
  27.3 1.6 %collective-permute-start.1 = (bf16[1024,128]{1,0:T(8,128)(2,1)S(1)}, bf16[1024,128]{1,0:T(8,128)(2,1)S(1)}, u32[]{:S(2)}, u32[]{:S(2)}) collective-permute-start(bf16[1024,128]{1,0:T(8,128)(2,1)S(1)} %bitcast.8), channel_id=1, source_target_pairs={{0,4},{2,6},{4,0},{6,2},{8,12},{10,14},{12,8},{14,10},{16,20},{18,... | collective-permute-start | bytes 786440 | tf_op jit(solution)/shard_map/ppermute | solution.py:208
  28.9 0.0 collective-permute-start
  28.9 5.4 %collective-permute-done.1.refs_2_ = bf16[1024,128]{1,0:T(8,128)(2,1)S(1)} collective-permute-done((bf16[1024,128]{1,0:T(8,128)(2,1)S(1)}, bf16[1024,128]{1,0:T(8,128)(2,1)S(1)}, u32[]{:S(2)}, u32[]{:S(2)}) %collective-permute-start.1) | collective-permute-done | bytes 262176 | tf_op jit(solution)/shard_map/ppermute | solution.py:208
  34.3 0.0 collective-permute-start.2
  34.3 0.0 collective-permute-done.refs_1_
  34.3 1.5 %collective-permute-done.2.refs_3_ = bf16[1024,128]{1,0:T(8,128)(2,1)S(1)} collective-permute-done((bf16[1024,128]{1,0:T(8,128)(2,1)S(1)}, bf16[1024,128]{1,0:T(8,128)(2,1)S(1)}, u32[]{:S(2)}, u32[]{:S(2)}) %collective-permute-start.2) | collective-permute-done | bytes 262176 | tf_op jit(solution)/shard_map/ppermute | solution.py:208
  35.8 0.0 copy-start.1
  35.8 0.0 copy-start.3
  35.8 11.4 %shard_map.85 = (bf16[4,64,256]{2,1,0:T(8,128)(2,1)S(1)}, f32[4,1,256]{2,1,0:T(1,128)S(1)}, bf16[4096,128]{1,0:T(8,128)(2,1)S(1)}, bf16[4096,128]{1,0:T(8,128)(2...) custom-call(bf16[1024,128]{1,0:T(8,128)(2,1)S(1)} %bitcast.10, ...), custom_call_target="tpu_custom_call" | custom-call | flops 2147483648 | bytes 2097152 | tf_op jit(solution)/shard_map/pallas_call | solution.py:236
  47.2 9.4 %all_to_all.26.att_ref = bf16[4,64,256]{2,1,0:T(8,128)(2,1)S(1)} all-to-all(bf16[4,64,256]{2,1,0:T(8,128)(2,1)S(1)} %get-tuple-element.21), channel_id=1, replica_groups={{0,8,16,24},{2,10,18,26},{4,12,20,28},{6,14,22,30},{1,9,17,25},{3,11,19..., dimensions={0} | all-to-all | bytes 262144 | tf_op jit(solution)/shard_map/all_to_all | solution.py:213
  56.6 0.0 copy-done.1
  56.7 0.0 copy-done.3
  56.7 1.4 %shard_map.86 = (bf16[256,768]{1,0:T(8,128)(2,1)S(1)}, bf16[4,64,768]{2,1,0:T(8,128)(2,1)S(1)}) custom-call(s32[2]{0:T(128)S(1)} %copy-done.6, bf16[4,64,768]{2,1,0:T(8,128)(2,1)S(1)} %copy-done.1, bf16[256,768]{1,0:T(8,128)(2,1)S(1)} %copy-done.3, bf16[4,64,256]{2,1,0:T(8,128)(2,1)S(1)} %all_to_all.26.att_ref), custom_call_target="tpu_custom_call" | custom-call | flops 201326592 | bytes 786432 | tf_op jit(solution)/shard_map/pallas_call | solution.py:245
  58.1 0.1 collective-permute-start.7
  58.2 10.9 %shard_map.88 = (bf16[1024,128]{1,0:T(8,128)(2,1)S(1)}, bf16[1024,128]{1,0:T(8,128)(2,1)S(1)}, bf16[1024,128]{1,0:T(8,128)(2,1)S(1)}, bf16[1024,128]{1,0:T(8,128)(2,1)S(1)}, bf16[4,128,128]{2,1,0:T(8,128)(2,1)S(1)}) custom-call(f32[4,1,256]{2,1,0:T(1,128)S(1)} %get-tuple-element.23.log_ref, bf16[4096,128]{1,0:T(8,128)(2,1)S(1)} %get-tuple-element.24.k_ref, ...), custom_call_target="tpu_custom_call" | custom-call | flops 5368709120 | bytes 2097152 | tf_op jit(solution)/shard_map/pallas_call | solution.py:274
  69.1 0.6 collective-permute-start.5
  69.7 0.0 collective-permute-done.7.refs_1_
  69.8 1.6 %collective-permute-start.8 = (bf16[64,768]{1,0:T(8,128)(2,1)S(1)}, bf16[64,768]{1,0:T(8,128)(2,1)S(1)}, u32[]{:S(2)}, u32[]{:S(2)}) collective-permute-start(bf16[64,768]{1,0:T(8,128)(2,1)S(1)} %get-tuple-element.38), channel_id=1, source_target_pairs={{0,4},{2,6},{4,0},{6,2},{8,12},{10,14},{12,8},{14,10},{16,20},{18,... | collective-permute-start | bytes 294920 | tf_op jit(solution)/shard_map/ppermute | solution.py:208
  71.3 3.2 %collective-permute-done.8.refs_1_ = bf16[64,768]{1,0:T(8,128)(2,1)S(1)} collective-permute-done((bf16[64,768]{1,0:T(8,128)(2,1)S(1)}, bf16[64,768]{1,0:T(8,128)(2,1)S(1)}, u32[]{:S(2)}, u32[]{:S(2)}) %collective-permute-start.8) | collective-permute-done | bytes 98336 | tf_op jit(solution)/shard_map/ppermute | solution.py:208
  74.5 0.7 shard_map.95
  75.2 3.3 %all-to-all-start.3 = ((bf16[4,16,768]{2,1,0:T(8,128)(2,1)}), bf16[4,16,768]{2,1,0:T(8,128)(2,1)S(1)}, u32[]{:S(2)}, u32[]{:S(2)}) async-start(bf16[4,16,768]{2,1,0:T(8,128)(2,1)} %bitcast.5), calls=%async_computation.3 | async-start | bytes 196608 | tf_op jit(solution)/shard_map/all_to_all | solution.py:213
  78.5 0.1 collective-permute-start.4
  78.6 0.0 collective-permute-done.5.refs_1_
  78.6 0.1 shard_map.90
  78.7 1.6 %collective-permute-start.6 = (bf16[1024,128]{1,0:T(8,128)(2,1)S(1)}, bf16[1024,128]{1,0:T(8,128)(2,1)S(1)}, u32[]{:S(2)}, u32[]{:S(2)}) collective-permute-start(bf16[1024,128]{1,0:T(8,128)(2,1)S(1)} %shard_map.90), channel_id=1, source_target_pairs={{0,4},{2,6},{4,0},{6,2},{8,12},{10,14},{12,8},{14,10},{16,20},{18,... | collective-permute-start | bytes 786440 | tf_op jit(solution)/shard_map/ppermute | solution.py:208
  80.3 4.1 %all-to-all-done.3.got_ref = bf16[4,16,768]{2,1,0:T(8,128)(2,1)S(1)} async-done(((bf16[4,16,768]{2,1,0:T(8,128)(2,1)}), bf16[4,16,768]{2,1,0:T(8,128)(2,1)S(1)}, u32[]{:S(2)}, u32[]{:S(2)}) %all-to-all-start.3) | async-done | bytes 98336 | tf_op jit(solution)/shard_map/all_to_all | solution.py:213
  84.3 0.7 shard_map.96
  85.0 3.3 %all-to-all-start.4 = ((bf16[4,16,768]{2,1,0:T(8,128)(2,1)}), bf16[4,16,768]{2,1,0:T(8,128)(2,1)S(1)}, u32[]{:S(2)}, u32[]{:S(2)}) async-start(bf16[4,16,768]{2,1,0:T(8,128)(2,1)} %shard_map.96), calls=%async_computation.4 | async-start | bytes 196608 | tf_op jit(solution)/shard_map/all_to_all | solution.py:213
  88.3 0.0 collective-permute-done.4.refs_1_
  88.3 0.1 shard_map.89.kept_ref
  88.4 0.0 collective-permute-done.6.came_ref
  88.4 0.8 shard_map.91
  89.2 4.9 %all-to-all-done.4.refs_0_ = bf16[4,16,768]{2,1,0:T(8,128)(2,1)S(1)} async-done(((bf16[4,16,768]{2,1,0:T(8,128)(2,1)}), bf16[4,16,768]{2,1,0:T(8,128)(2,1)S(1)}, u32[]{:S(2)}, u32[]{:S(2)}) %all-to-all-start.4) | async-done | bytes 98336 | tf_op jit(solution)/shard_map/all_to_all | solution.py:213
  94.1 3.5 %all-to-all-start.2 = ((bf16[4,384,128]{2,1,0:T(8,128)(2,1)}), bf16[4,384,128]{2,1,0:T(8,128)(2,1)S(1)}, u32[]{:S(2)}, u32[]{:S(2)}) async-start(bf16[4,384,128]{2,1,0:T(8,128)(2,1)} %shard_map.91), calls=%async_computation.2 | async-start | bytes 786432 | tf_op jit(solution)/shard_map/all_to_all | solution.py:213
  97.6 1.6 %collective-permute-start.3 = (bf16[256,768]{1,0:T(8,128)(2,1)S(1)}, bf16[256,768]{1,0:T(8,128)(2,1)S(1)}, u32[]{:S(2)}, u32[]{:S(2)}) collective-permute-start(bf16[256,768]{1,0:T(8,128)(2,1)S(1)} %get-tuple-element.22.refs_0_), channel_id=1, source_target_pairs={{0,1},{1,0},{2,3},{3,2},{4,5},{5,4},{6,7},{7,6},{8,9},{9,8},{10,11... | collective-permute-start | bytes 1179656 | tf_op jit(solution)/shard_map/ppermute | solution.py:208
  99.1 1.5 %collective-permute-start.10 = (bf16[4,16,768]{2,1,0:T(8,128)(2,1)S(1)}, bf16[4,16,768]{2,1,0:T(8,128)(2,1)S(1)}, u32[]{:S(2)}, u32[]{:S(2)}) collective-permute-start(bf16[4,16,768]{2,1,0:T(8,128)(2,1)S(1)} %all-to-all-done.4.refs_0_), channel_id=1, source_target_pairs={{0,4},{2,6},{4,0},{6,2},{8,12},{10,14},{12,8},{14,10},{16,20},{18,... | collective-permute-start | bytes 294920 | tf_op jit(solution)/shard_map/ppermute | solution.py:208
  100.7 0.0 collective-permute-start.9
  100.7 3.1 %collective-permute-done.10.refs_2_ = bf16[4,16,768]{2,1,0:T(8,128)(2,1)S(1)} collective-permute-done((bf16[4,16,768]{2,1,0:T(8,128)(2,1)S(1)}, bf16[4,16,768]{2,1,0:T(8,128)(2,1)S(1)}, u32[]{:S(2)}, u32[]{:S(2)}) %collective-permute-start.10) | collective-permute-done | bytes 98336 | tf_op jit(solution)/shard_map/ppermute | solution.py:208
  103.7 0.0 collective-permute-start.11
  103.7 1.9 %collective-permute-done.3.refs_1_ = bf16[256,768]{1,0:T(8,128)(2,1)S(1)} collective-permute-done((bf16[256,768]{1,0:T(8,128)(2,1)S(1)}, bf16[256,768]{1,0:T(8,128)(2,1)S(1)}, u32[]{:S(2)}, u32[]{:S(2)}) %collective-permute-start.3) | collective-permute-done | bytes 393248 | tf_op jit(solution)/shard_map/ppermute | solution.py:208
  105.6 0.8 shard_map.87
  106.5 0.0 collective-permute-done.9.refs_1_
  106.5 0.0 collective-permute-done.11.refs_3_
  106.5 0.9 shard_map.97
  107.4 0.0 all-to-all-done.2.got_ref
  107.4 1.2 %shard_map.92 = (f32[256,4,128]{2,1,0:T(4,128)}, f32[4,64,256]{2,1,0:T(8,128)}) custom-call(bf16[4,384,128]{2,1,0:T(8,128)(2,1)S(1)} %all-to-all-done.2.got_ref), custom_call_target="tpu_custom_call" | custom-call | bytes 524288 | tf_op jit(solution)/shard_map/pallas_call | solution.py:294
  (4 shorter events, 0.1 us)
Async XLA Ops:
  0.6 0.7 copy-start.6
  1.3 1.0 copy-start
  2.3 1.0 copy-start.2
  3.3 0.9 copy-start.4
  4.2 0.9 copy-start.5
  27.3 7.0 %collective-permute-start.1 = (bf16[1024,128]{1,0:T(8,128)(2,1)S(1)}, bf16[1024,128]{1,0:T(8,128)(2,1)S(1)}, u32[]{:S(2)}, u32[]{:S(2)}) collective-permute-start(bf16[1024,128]{1,0:T(8,128)(2,1)S(1)} %bitcast.8), channel_id=1, source_target_pairs={{0,4},{2,6},{4,0},{6,2},{8,12},{10,14},{12,8},{14,10},{16,20},{18,... | collective-permute-start | bytes 786440 | tf_op jit(solution)/shard_map/ppermute | solution.py:208
  28.9 5.4 %collective-permute-start = (bf16[1024,128]{1,0:T(8,128)(2,1)S(1)}, bf16[1024,128]{1,0:T(8,128)(2,1)S(1)}, u32[]{:S(2)}, u32[]{:S(2)}) collective-permute-start(bf16[1024,128]{1,0:T(8,128)(2,1)S(1)} %bitcast.9), channel_id=1, source_target_pairs={{0,2},{2,0},{4,6},{6,4},{8,10},{10,8},{12,14},{14,12},{16,18},{18,... | collective-permute-start | bytes 786440 | tf_op jit(solution)/shard_map/ppermute | solution.py:208
  34.3 1.5 %collective-permute-start.2 = (bf16[1024,128]{1,0:T(8,128)(2,1)S(1)}, bf16[1024,128]{1,0:T(8,128)(2,1)S(1)}, u32[]{:S(2)}, u32[]{:S(2)}) collective-permute-start(bf16[1024,128]{1,0:T(8,128)(2,1)S(1)} %collective-permute-done.1.refs_2_), channel_id=1, source_target_pairs={{0,2},{2,0},{4,6},{6,4},{8,10},{10,8},{12,14},{14,12},{16,18},{18,... | collective-permute-start | bytes 786440 | tf_op jit(solution)/shard_map/ppermute | solution.py:208
  35.8 20.8 %copy-start.1 = (bf16[4,64,768]{2,1,0:T(8,128)(2,1)S(1)}, bf16[4,64,768]{2,1,0:T(8,128)(2,1)}, u32[]{:S(2)}) copy-start(bf16[4,64,768]{2,1,0:T(8,128)(2,1)} %w_ref.3) | copy-start | bytes 1179652
  35.8 20.8 %copy-start.3 = (bf16[256,768]{1,0:T(8,128)(2,1)S(1)}, bf16[256,768]{1,0:T(8,128)(2,1)}, u32[]{:S(2)}) copy-start(bf16[256,768]{1,0:T(8,128)(2,1)} %go_ref.3) | copy-start | bytes 1179652
  58.1 11.6 %collective-permute-start.7 = (bf16[2,64,768]{2,1,0:T(8,128)(2,1)S(1)}, bf16[2,64,768]{2,1,0:T(8,128)(2,1)S(1)}, u32[]{:S(2)}, u32[]{:S(2)}) collective-permute-start(bf16[2,64,768]{2,1,0:T(8,128)(2,1)S(1)} %get-tuple-element.37), channel_id=1, source_target_pairs={{0,2},{2,0},{4,6},{6,4},{8,10},{10,8},{12,14},{14,12},{16,18},{18,... | collective-permute-start | bytes 589832 | tf_op jit(solution)/shard_map/ppermute | solution.py:208
  69.1 9.5 %collective-permute-start.5 = (bf16[1024,128]{1,0:T(8,128)(2,1)S(1)}, bf16[1024,128]{1,0:T(8,128)(2,1)S(1)}, u32[]{:S(2)}, u32[]{:S(2)}) collective-permute-start(bf16[1024,128]{1,0:T(8,128)(2,1)S(1)} %get-tuple-element.31), channel_id=1, source_target_pairs={{0,2},{2,0},{4,6},{6,4},{8,10},{10,8},{12,14},{14,12},{16,18},{18,... | collective-permute-start | bytes 786440 | tf_op jit(solution)/shard_map/ppermute | solution.py:208
  69.8 4.8 %collective-permute-start.8 = (bf16[64,768]{1,0:T(8,128)(2,1)S(1)}, bf16[64,768]{1,0:T(8,128)(2,1)S(1)}, u32[]{:S(2)}, u32[]{:S(2)}) collective-permute-start(bf16[64,768]{1,0:T(8,128)(2,1)S(1)} %get-tuple-element.38), channel_id=1, source_target_pairs={{0,4},{2,6},{4,0},{6,2},{8,12},{10,14},{12,8},{14,10},{16,20},{18,... | collective-permute-start | bytes 294920 | tf_op jit(solution)/shard_map/ppermute | solution.py:208
  75.2 9.1 %all-to-all-start.3 = ((bf16[4,16,768]{2,1,0:T(8,128)(2,1)}), bf16[4,16,768]{2,1,0:T(8,128)(2,1)S(1)}, u32[]{:S(2)}, u32[]{:S(2)}) async-start(bf16[4,16,768]{2,1,0:T(8,128)(2,1)} %bitcast.5), calls=%async_computation.3 | async-start | bytes 196608 | tf_op jit(solution)/shard_map/all_to_all | solution.py:213
  78.5 9.8 %collective-permute-start.4 = (bf16[1024,128]{1,0:T(8,128)(2,1)S(1)}, bf16[1024,128]{1,0:T(8,128)(2,1)S(1)}, u32[]{:S(2)}, u32[]{:S(2)}) collective-permute-start(bf16[1024,128]{1,0:T(8,128)(2,1)S(1)} %get-tuple-element.29), channel_id=1, source_target_pairs={{0,2},{2,0},{4,6},{6,4},{8,10},{10,8},{12,14},{14,12},{16,18},{18,... | collective-permute-start | bytes 786440 | tf_op jit(solution)/shard_map/ppermute | solution.py:208
  78.7 9.7 %collective-permute-start.6 = (bf16[1024,128]{1,0:T(8,128)(2,1)S(1)}, bf16[1024,128]{1,0:T(8,128)(2,1)S(1)}, u32[]{:S(2)}, u32[]{:S(2)}) collective-permute-start(bf16[1024,128]{1,0:T(8,128)(2,1)S(1)} %shard_map.90), channel_id=1, source_target_pairs={{0,4},{2,6},{4,0},{6,2},{8,12},{10,14},{12,8},{14,10},{16,20},{18,... | collective-permute-start | bytes 786440 | tf_op jit(solution)/shard_map/ppermute | solution.py:208
  85.0 9.1 %all-to-all-start.4 = ((bf16[4,16,768]{2,1,0:T(8,128)(2,1)}), bf16[4,16,768]{2,1,0:T(8,128)(2,1)S(1)}, u32[]{:S(2)}, u32[]{:S(2)}) async-start(bf16[4,16,768]{2,1,0:T(8,128)(2,1)} %shard_map.96), calls=%async_computation.4 | async-start | bytes 196608 | tf_op jit(solution)/shard_map/all_to_all | solution.py:213
  94.1 13.3 %all-to-all-start.2 = ((bf16[4,384,128]{2,1,0:T(8,128)(2,1)}), bf16[4,384,128]{2,1,0:T(8,128)(2,1)S(1)}, u32[]{:S(2)}, u32[]{:S(2)}) async-start(bf16[4,384,128]{2,1,0:T(8,128)(2,1)} %shard_map.91), calls=%async_computation.2 | async-start | bytes 786432 | tf_op jit(solution)/shard_map/all_to_all | solution.py:213
  97.6 8.1 %collective-permute-start.3 = (bf16[256,768]{1,0:T(8,128)(2,1)S(1)}, bf16[256,768]{1,0:T(8,128)(2,1)S(1)}, u32[]{:S(2)}, u32[]{:S(2)}) collective-permute-start(bf16[256,768]{1,0:T(8,128)(2,1)S(1)} %get-tuple-element.22.refs_0_), channel_id=1, source_target_pairs={{0,1},{1,0},{2,3},{3,2},{4,5},{5,4},{6,7},{7,6},{8,9},{9,8},{10,11... | collective-permute-start | bytes 1179656 | tf_op jit(solution)/shard_map/ppermute | solution.py:208
  99.1 4.6 %collective-permute-start.10 = (bf16[4,16,768]{2,1,0:T(8,128)(2,1)S(1)}, bf16[4,16,768]{2,1,0:T(8,128)(2,1)S(1)}, u32[]{:S(2)}, u32[]{:S(2)}) collective-permute-start(bf16[4,16,768]{2,1,0:T(8,128)(2,1)S(1)} %all-to-all-done.4.refs_0_), channel_id=1, source_target_pairs={{0,4},{2,6},{4,0},{6,2},{8,12},{10,14},{12,8},{14,10},{16,20},{18,... | collective-permute-start | bytes 294920 | tf_op jit(solution)/shard_map/ppermute | solution.py:208
  100.7 5.8 %collective-permute-start.9 = (bf16[4,16,768]{2,1,0:T(8,128)(2,1)S(1)}, bf16[4,16,768]{2,1,0:T(8,128)(2,1)S(1)}, u32[]{:S(2)}, u32[]{:S(2)}) collective-permute-start(bf16[4,16,768]{2,1,0:T(8,128)(2,1)S(1)} %all-to-all-done.4.refs_0_), channel_id=1, source_target_pairs={{0,2},{2,0},{4,6},{6,4},{8,10},{10,8},{12,14},{14,12},{16,18},{18,... | collective-permute-start | bytes 294920 | tf_op jit(solution)/shard_map/ppermute | solution.py:208
  103.7 2.7 %collective-permute-start.11 = (bf16[4,16,768]{2,1,0:T(8,128)(2,1)S(1)}, bf16[4,16,768]{2,1,0:T(8,128)(2,1)S(1)}, u32[]{:S(2)}, u32[]{:S(2)}) collective-permute-start(bf16[4,16,768]{2,1,0:T(8,128)(2,1)S(1)} %collective-permute-done.10.refs_2_), channel_id=1, source_target_pairs={{0,2},{2,0},{4,6},{6,4},{8,10},{10,8},{12,14},{14,12},{16,18},{18,... | collective-permute-start | bytes 294920 | tf_op jit(solution)/shard_map/ppermute | solution.py:208

commit v3 on v1

v3 whole, which is shorter than its diff:
```python
import functools

import jax
import jax.numpy as jnp
from jax import lax
from jax.experimental import pallas as pl
from jax.experimental.pallas import tpu as pltpu
from jax.sharding import PartitionSpec as P

TILE = 128
DEAD = 1024.0
BIAS = -1e30
F32 = jnp.float32
BF16 = jnp.bfloat16
VMEM = pl.BlockSpec(memory_space=pltpu.VMEM)
SMEM = pl.BlockSpec(memory_space=pltpu.SMEM)
MIB = 1024 * 1024


def dot(a, b):
    return lax.dot_general(a, b, (((1,), (0,)), ((), ())), preferred_element_type=F32)


def dot_nt(a, b):
    return lax.dot_general(a, b, (((1,), (1,)), ((), ())), preferred_element_type=F32)


def call(kernel, outs, scratch=(), n_in=1, smem_first=False, any_last=False, flops=0, moved=0, limit=16):
    specs = [VMEM] * n_in
    if smem_first:
        specs[0] = SMEM
    if any_last:
        specs[-1] = pl.BlockSpec(memory_space=pl.ANY)
    return pl.pallas_call(
        kernel,
        out_shape=[jax.ShapeDtypeStruct(shape, kind) for shape, kind in outs],
        in_specs=specs,
        out_specs=[VMEM] * len(outs),
        scratch_shapes=list(scratch),
        compiler_params=pltpu.CompilerParams(vmem_limit_bytes=limit * MIB),
        cost_estimate=pl.CostEstimate(flops=flops, bytes_accessed=moved, transcendentals=0),
    )


def live_column(fill_ref, rows):
    parts = []
    within = lax.broadcasted_iota(jnp.int32, (TILE, 1), 0)
    for tile in range(rows // TILE):
        parts.append(jnp.where(within < fill_ref[tile], 1.0, 0.0))
    return jnp.concatenate(parts, axis=0) if len(parts) > 1 else parts[0]


def pack_kv_kernel(heads, rows, dim, a_of, fill_ref, kv_ref, *refs):
    outs, (held,) = refs[:heads], refs[heads:]
    live = live_column(fill_ref, rows)
    lane = lax.broadcasted_iota(jnp.int32, (rows, 2 * dim), 1)
    mark = jnp.where(lane == 0, DEAD, 0.0)
    for head in range(heads):
        held[head] = jnp.where(live > 0, kv_ref[:, head, :].astype(F32), mark).astype(BF16)
    me = a_of()
    for slot in range(heads):
        outs[slot][...] = held[me ^ slot]


def pack_qg_kernel(heads, rows, dim, a_of, fill_ref, q_ref, w_ref, go_ref, *refs):
    outs, (held,) = refs[:heads], refs[heads:]
    live = live_column(fill_ref, rows)
    mixed = jnp.where(live > 0, go_ref[...].astype(F32), 0.0).astype(BF16)
    for head in range(heads):
        held[head, 0:dim, :] = (q_ref[head].astype(F32) * dim**-0.5).astype(BF16)
        held[head, dim:, :] = dot_nt(w_ref[head], mixed).astype(BF16)
    me = a_of()
    for slot in range(heads):
        outs[slot][...] = held[me ^ slot]


def forward_kernel(slots, columns, rows, dim, step, *refs):
    blocks, refs = refs[:columns], refs[columns:]
    qg_in, refs = refs[:slots], refs[slots:]
    att_out, refs = refs[:slots], refs[slots:]
    exp_ref, wide_ref, kt_ref, q_ref, g_ref, vt_ref, score_ref, qa_ref = refs
    block, wide = slots * rows, 2 * dim
    keys = block * columns
    lane = lax.broadcasted_iota(jnp.int32, (step, wide), 1)
    ones = jnp.where(lane <= 2, jnp.where(lane == 0, 0.0, 1.0), 0.0)
    for start in range(0, keys, step):
        column, inside = start // block, start % block
        pair = blocks[column][inside : inside + step, :]
        full = pair.astype(F32)
        wide_ref[start : start + step, 0:wide] = pair
        bias = jnp.where(full[:, 0:1] >= DEAD, BIAS, 0.0)
        wide_ref[start : start + step, wide:] = jnp.where(lane == 0, bias, ones).astype(BF16)
        turned = full.T.astype(BF16)
        kt_ref[:, start : start + step] = turned[:dim, :]
        vt_ref[0:dim, start : start + step] = turned[dim:, :]
        vt_ref[dim:, start : start + step] = jnp.ones((16, step), BF16)
    row = lax.broadcasted_iota(jnp.int32, (wide, rows), 0)
    bias_row = jnp.where(row == 0, 1.0, 0.0).astype(BF16)
    for slot in range(slots):
        here = slice(slot * rows, (slot + 1) * rows)
        queries = qg_in[slot][0:dim, :]
        q_ref[:, here] = queries
        qa_ref[0:dim, here] = queries
        qa_ref[dim:wide, here] = jnp.zeros((dim, rows), BF16)
        qa_ref[wide:, here] = bias_row
    peak = None
    for turn in range(slots + 1):
        here = slice(turn * rows, (turn + 1) * rows)
        past = slice((turn - 1) * rows, turn * rows)
        top = jnp.full((8, rows), BIAS, F32)
        total = jnp.zeros((dim + 16, rows), F32)
        for start in range(0, keys, step):
            part = slice(start, start + step)
            if turn < slots:
                scores = dot(wide_ref[part, :], qa_ref[:, here])
                score_ref[turn % 2, part, :] = scores
                top = jnp.maximum(top, jnp.max(scores.reshape(step // 8, 8, rows), axis=0))
            if turn > 0:
                exps = jnp.exp(score_ref[(turn - 1) % 2, part, :] - peak).astype(BF16)
                exp_ref[part, past] = exps
                total = total + dot(vt_ref[:, part], exps)
        if turn > 0:
            inverse = 1.0 / total[dim : dim + 1, :]
            attended = (total[0:dim, :] * inverse).astype(BF16)
            att_out[turn - 1][...] = attended
            grad = qg_in[turn - 1][dim:, :].astype(F32)
            inner = jnp.sum(grad * attended.astype(F32), axis=0, keepdims=True) * inverse
            high = inner.astype(BF16).astype(F32)
            g_ref[0:dim, past] = jnp.zeros((dim, rows), BF16)
            g_ref[dim:wide, past] = (grad * inverse).astype(BF16)
            g_ref[wide:, past] = jnp.where(row == 1, -high, jnp.where(row == 2, high - inner, 0.0)).astype(BF16)
        peak = jnp.max(top, axis=0, keepdims=True)


def backward_kernel(slots, columns, rows, dim, step, exp_ref, wide_ref, kt_ref, q_ref, g_ref, _, *refs):
    dkv_out, dq_out, (dq_acc,) = refs[:columns], refs[columns : columns + slots], refs[columns + slots :]
    block, wide = slots * rows, 2 * dim
    for start in range(0, block * columns, step):
        column, inside = start // block, start % block
        part = slice(start, start + step)
        exps = exp_ref[part, :]
        grads = (exps.astype(F32) * dot(wide_ref[part, :], g_ref[...])).astype(BF16)
        dkv_out[column][dim:, inside : inside + step] = dot_nt(g_ref[dim:wide, :], exps).astype(BF16)
        dkv_out[column][0:dim, inside : inside + step] = dot_nt(q_ref[...], grads).astype(BF16)
        term = dot(kt_ref[:, part], grads)
        dq_acc[...] = term if start == 0 else dq_acc[...] + term
    for slot in range(slots):
        dq_out[slot][...] = (dq_acc[:, slot * rows : (slot + 1) * rows] * dim**-0.5).astype(BF16)


def project_kernel(slots, rows, dim, a_of, b_of, halves, fill_ref, w_ref, go_ref, *refs):
    att, refs = refs[:slots], refs[slots:]
    terms_ref, refs = refs[0], refs[1:]
    live = live_column(fill_ref, rows)
    mixed = jnp.where(live > 0, go_ref[...].astype(F32), 0.0).astype(BF16)
    me = a_of()
    held = refs[-1]
    total = None
    for slot in range(slots):
        head = me ^ slot
        held[head] = dot(att[slot][...], mixed).astype(BF16)
        term = dot(att[slot][...].astype(F32).T.astype(BF16), w_ref[head])
        total = term if total is None else total + term
    terms_ref[...] = (total * live).astype(BF16)
    if not halves:
        refs[0][...] = held[...]
        return
    me = b_of()
    kept_ref, sent_ref = refs[0], refs[1]
    for pair in range(slots // 2):
        kept_ref[pair] = held[me ^ (2 * pair)]
        sent_ref[pair] = held[me ^ (2 * pair) ^ 1]


def add_pairs_kernel(kept_ref, came_ref, first_ref, second_ref):
    for index, out_ref in enumerate((first_ref, second_ref)):
        out_ref[...] = (kept_ref[index].astype(F32) + came_ref[index].astype(F32)).astype(BF16)


def add_pieces_kernel(slots, rows, kept_ref, came_ref, *outs):
    for slot in range(slots):
        here = slice(slot * rows, (slot + 1) * rows)
        outs[slot][...] = (kept_ref[:, here].astype(F32) + came_ref[:, here].astype(F32)).astype(BF16)


def add_kernel(a_ref, b_ref, out_ref):
    out_ref[...] = (a_ref[...].astype(F32) + b_ref[...].astype(F32)).astype(out_ref.dtype)


def unpack_kernel(slots, rows, dim, a_of, *refs):
    dkv, dq = refs[:slots], refs[slots : 2 * slots]
    kv_out, q_out, held = refs[2 * slots :]
    me = a_of()
    for slot in range(slots):
        q_out[me ^ slot] = dq[slot][...].astype(F32)
        held[me ^ slot] = dkv[slot][...].astype(F32).T
    for head in range(slots):
        kv_out[:, head, :] = held[head]


def place_kernel(columns, b_of, *refs):
    parts, (out_ref,) = refs[:columns], refs[columns:]
    me = b_of()
    for column in range(columns):
        out_ref[me ^ column] = parts[column][...].astype(F32)


def shards(seq, mp, queries, key_value, tile_fill, out_weight, grad_output):
    rows, heads, dim = queries.shape
    width = grad_output.shape[1]
    slots = heads
    columns = seq // slots
    assert slots * columns == seq and columns & (columns - 1) == 0 and slots & (slots - 1) == 0
    a_of = lambda: lax.axis_index("seq") // columns
    b_of = lambda: lax.axis_index("seq") % columns

    def swap(array, mask, axis="seq", size=seq):
        return lax.ppermute(array, axis, [(i, i ^ mask) for i in range(size)])

    def exchange(pieces):
        return [pieces[0]] + [swap(pieces[s], s * columns) for s in range(1, slots)]

    block, wide = slots * rows, 2 * dim
    keys = seq * rows
    kv_mine = exchange(call(
        functools.partial(pack_kv_kernel, heads, rows, dim, a_of),
        [((rows, wide), BF16)] * slots, [pltpu.VMEM((heads, rows, wide), BF16)],
        n_in=2, smem_first=True, moved=4 * rows * heads * wide, limit=56,
    )(tile_fill, key_value))
    qg_mine = exchange(call(
        functools.partial(pack_qg_kernel, heads, rows, dim, a_of),
        [((wide, rows), BF16)] * slots, [pltpu.VMEM((heads, wide, rows), BF16)],
        n_in=4, smem_first=True, flops=2 * rows * heads * dim * width, moved=4 * rows * width, limit=56,
    )(tile_fill, jnp.transpose(queries, (1, 2, 0)), out_weight, grad_output))
    own = jnp.concatenate(kv_mine, axis=0) if slots > 1 else kv_mine[0]

    blocks = {0: own}
    bit = columns // 2
    while bit:
        for r in sorted(blocks):
            blocks[r ^ bit] = swap(blocks[r], bit)
        bit //= 2

    step = min(block, 512)
    mults = block * keys * wide
    forward = call(
        functools.partial(forward_kernel, slots, columns, rows, dim, step),
        [((dim, rows), BF16)] * slots
        + [((keys, block), BF16), ((keys, 2 * wide), BF16), ((dim, keys), BF16), ((dim, block), BF16), ((2 * wide, block), BF16)],
        [pltpu.VMEM((dim + 16, keys), BF16), pltpu.VMEM((min(slots, 2), keys, rows), F32), pltpu.VMEM((2 * wide, block), BF16)],
        n_in=columns + slots, flops=4 * mults, moved=4 * keys * wide, limit=24,
    )(*[blocks[r] for r in range(columns)], *qg_mine)
    att_mine, saved = exchange(forward[:slots]), forward[slots:]

    halves = columns == heads == 4
    terms, *weight_terms = call(
        functools.partial(project_kernel, slots, rows, dim, a_of, b_of, halves),
        [((rows, width), BF16)] + ([((2, dim, width), BF16)] * 2 if halves else [((heads, dim, width), BF16)]),
        [pltpu.VMEM((heads, dim, width), BF16)],
        n_in=3 + slots, smem_first=True, flops=4 * rows * heads * dim * width, moved=4 * rows * width,
    )(tile_fill, out_weight, grad_output, *att_mine)

    backward = call(
        functools.partial(backward_kernel, slots, columns, rows, dim, min(step, 256)),
        [((wide, block), BF16)] * columns + [((dim, rows), BF16)] * slots,
        [pltpu.VMEM((dim, block), F32)],
        n_in=6, any_last=True, flops=5 * mults, moved=4 * keys * wide, limit=24,
    )(*saved, terms)

    bit = 1
    while bit < mp:
        terms = call(add_kernel, [((rows, width), BF16)], n_in=2, moved=6 * rows * width)(
            terms, swap(terms, bit, "mp", mp))[0]
        bit *= 2

    if halves:
        kept, sent = weight_terms
        kept, sent = call(add_pairs_kernel, [((dim, width), BF16)] * 2, n_in=2)(kept, swap(sent, 1))
        add = call(add_kernel, [((dim, width), BF16)], n_in=2)
        kept = add(kept, swap(sent, 2))[0]
        bit = columns
        while bit < seq:
            kept = add(kept, swap(kept, bit))[0]
            bit *= 2
        across = swap(kept, 2)
        weight_grad = call(
            functools.partial(place_kernel, columns, b_of), [((heads, dim, width), F32)], n_in=columns,
        )(kept, swap(kept, 1), across, swap(across, 1))[0]
    else:
        weight_grad = lax.psum(weight_terms[0].astype(F32), "seq")

    dkv, dq_mine = dict(enumerate(backward[:columns])), exchange(backward[columns:])
    bit = 1
    while 2 * bit < columns:
        dkv = {
            r: call(add_kernel, [((wide, block), BF16)], n_in=2, moved=12 * block * dim)(
                dkv[r], swap(dkv[r ^ bit], bit))[0]
            for r in sorted(dkv) if not r & bit
        }
        bit *= 2
    dkv_mine = exchange(call(
        functools.partial(add_pieces_kernel, slots, rows), [((wide, rows), BF16)] * slots, n_in=2, moved=12 * block * dim,
    )(dkv[0], swap(dkv[bit], bit)))
    key_value_grad, query_grad = call(
        functools.partial(unpack_kernel, slots, rows, dim, a_of),
        [((rows, heads, wide), F32), ((heads, dim, rows), F32)],
        [pltpu.VMEM((heads, rows, wide), F32)],
        n_in=2 * slots, moved=8 * rows * heads * dim,
    )(*dkv_mine, *dq_mine)
    return terms, jnp.transpose(query_grad, (2, 0, 1)), key_value_grad, weight_grad


def solution(mesh):
    return jax.shard_map(
        functools.partial(shards, mesh.shape["seq"], mesh.shape["mp"]),
        mesh=mesh,
        in_specs=(
            P("seq", "mp", None),
            P("seq", "mp", None),
            P("seq"),
            P("mp", None, None),
            P("seq", None),
        ),
        out_specs=(P("seq", None), P("seq", "mp", None), P("seq", "mp", None), P("mp", None, None)),
        check_vma=False,
    )
```

time: 106 us -> 98.4 us (0.928)
  starting transfers between devices: 40 us -> 29.5 us
  waiting for transfers between devices: 31.6 us -> 40.1 us
  local copies, waits for them, and re-layouts: 4.57 us -> 1.74 us
  Pallas kernels: 28.8 us -> 26.1 us
    ppermute x34 -> x29, starting transfers between devices: 40 us -> 29.5 us  [swap(): return lax.ppermute(array, axis, [(i, i ^ mask) for i in range(size)])]
    ppermute x34 -> x29, waiting for transfers between devices: 31.6 us -> 40.1 us  [swap(): return lax.ppermute(array, axis, [(i, i ^ mask) for i in range(size)])]
    pallas_call x12 -> x14, Pallas kernels: 27.6 us -> 24.8 us  [the longest x1 8.31 us: shards(): call(functools.partial(forward_kernel, slots, columns, rows, dim, step),...]
    unnamed x17 -> x11, local copies, waits for them, and re-layouts: 4.54 us -> 1.73 us
  transfers between devices with their start and end apart: 34 -> 29, of which waited for: 15 -> 16; matrix products, arithmetic and copies ran while one was open for 0% -> 1% of each run, Pallas kernels for 3% -> 13%
where the time goes in v3:
time: 98.4 us; the launch traced here: 98.2 us
  waiting for transfers between devices  40.1 us (41%)
  starting transfers between devices  29.5 us (30%)
  Pallas kernels  26.1 us (27%)
  local copies, waits for them, and re-layouts  1.74 us (2%)
    ppermute x29, waiting for transfers between devices, swap(): return lax.ppermute(array, axis, [(i, i ^ mask) for i in range(size)])  40.1 us
    ppermute x29, starting transfers between devices, swap(): return lax.ppermute(array, axis, [(i, i ^ mask) for i in range(size)])  29.5 us
    pallas_call x1, Pallas kernels, shards(): call(functools.partial(forward_kernel, slots, columns, rows, dim, step),...  8.31 us
    pallas_call x1, Pallas kernels, shards(): call(functools.partial(backward_kernel, slots, columns, rows, dim, min(st...  7.8 us
    pallas_call x1, Pallas kernels, shards(): call(functools.partial(pack_qg_kernel, heads, rows, dim, a_of), [((wide,...  2.58 us
    pallas_call x1, Pallas kernels, shards(): call(functools.partial(pack_kv_kernel, heads, rows, dim, a_of), [((rows,...  2.57 us
  transfers between devices with their start and end apart: 29, of which 16 were waited for; matrix products, arithmetic and copies ran while one was open for 1% of the time, Pallas kernels for 13%

profile of v3, /device:TPU:0, one launch (start us, length us, event | category | flops | bytes accessed | tf_op | source)
XLA Modules:
  0.0 98.2 jit_solution(4634143697981540370)
XLA Ops:
  0.6 0.0 copy-start.2
  0.6 0.0 copy-start.1
  0.7 0.0 copy-start
  0.7 2.6 %shard_map.84 = (bf16[256,128]{1,0:T(8,128)(2,1)}, bf16[256,128]{1,0:T(8,128)(2,1)}, bf16[256,128]{1,0:T(8,128)(2,1)}, bf16[256,128]{1,0:T(8,128)(2,1)}) custom-call(s32[2]{0:T(128)} %fill_ref.5, bf16[256,4,128]{2,1,0:T(4,128)(2,1)} %kv_ref.1), custom_call_target="tpu_custom_call" | custom-call | bytes 524288 | tf_op jit(solution)/shard_map/pallas_call | solution.py:225
  3.2 3.0 %collective-permute-start = (bf16[256,128]{1,0:T(8,128)(2,1)}, bf16[256,128]{1,0:T(8,128)(2,1)S(1)}, u32[]{:S(2)}, u32[]{:S(2)}) collective-permute-start(bf16[256,128]{1,0:T(8,128)(2,1)} %get-tuple-element.41), channel_id=1, source_target_pairs={{0,8},{2,10},{4,12},{6,14},{8,0},{10,2},{12,4},{14,6},{16,24},{18,... | collective-permute-start | bytes 196616 | tf_op jit(solution)/shard_map/ppermute | solution.py:218
  6.3 2.6 %collective-permute-start.1 = (bf16[256,128]{1,0:T(8,128)(2,1)}, bf16[256,128]{1,0:T(8,128)(2,1)S(1)}, u32[]{:S(2)}, u32[]{:S(2)}) collective-permute-start(bf16[256,128]{1,0:T(8,128)(2,1)} %get-tuple-element.42), channel_id=1, source_target_pairs={{0,16},{2,18},{4,20},{6,22},{8,24},{10,26},{12,28},{14,30},{16,0},... | collective-permute-start | bytes 196616 | tf_op jit(solution)/shard_map/ppermute | solution.py:218
  8.9 0.8 constant_dynamic-update-slice_fusion.3
  9.7 0.0 collective-permute-done
  9.7 4.0 %collective-permute-done.1 = bf16[256,128]{1,0:T(8,128)(2,1)S(1)} collective-permute-done((bf16[256,128]{1,0:T(8,128)(2,1)}, bf16[256,128]{1,0:T(8,128)(2,1)S(1)}, u32[]{:S(2)}, u32[]{:S(2)}) %collective-permute-start.1) | collective-permute-done | bytes 65568 | tf_op jit(solution)/shard_map/ppermute | solution.py:218
  13.7 1.4 %collective-permute-done.2 = bf16[256,128]{1,0:T(8,128)(2,1)S(1)} collective-permute-done((bf16[256,128]{1,0:T(8,128)(2,1)}, bf16[256,128]{1,0:T(8,128)(2,1)S(1)}, u32[]{:S(2)}, u32[]{:S(2)}) %collective-permute-start.2) | collective-permute-done | bytes 65568 | tf_op jit(solution)/shard_map/ppermute | solution.py:218
  15.2 1.6 %collective-permute-start.4 = (bf16[1024,128]{1,0:T(8,128)(2,1)S(1)}, bf16[1024,128]{1,0:T(8,128)(2,1)S(1)}, u32[]{:S(2)}, u32[]{:S(2)}) collective-permute-start(bf16[1024,128]{1,0:T(8,128)(2,1)S(1)} %constant_dynamic-update-slice_fusion.refs_0_), channel_id=1, source_target_pairs={{0,4},{2,6},{4,0},{6,2},{8,12},{10,14},{12,8},{14,10},{16,20},{18,... | collective-permute-start | bytes 786440 | tf_op jit(solution)/shard_map/ppermute | solution.py:218
  16.7 0.0 collective-permute-start.3
  16.7 4.9 %collective-permute-done.4.refs_2_ = bf16[1024,128]{1,0:T(8,128)(2,1)S(1)} collective-permute-done((bf16[1024,128]{1,0:T(8,128)(2,1)S(1)}, bf16[1024,128]{1,0:T(8,128)(2,1)S(1)}, u32[]{:S(2)}, u32[]{:S(2)}) %collective-permute-start.4) | collective-permute-done | bytes 262176 | tf_op jit(solution)/shard_map/ppermute | solution.py:218
  21.6 0.0 collective-permute-start.5
  21.6 2.6 %shard_map.85 = (bf16[128,256]{1,0:T(8,128)(2,1)}, bf16[128,256]{1,0:T(8,128)(2,1)}, bf16[128,256]{1,0:T(8,128)(2,1)}, bf16[128,256]{1,0:T(8,128)(2,1)}) custom-call(s32[2]{0:T(128)} %fill_ref.5, bf16[4,64,256]{2,1,0:T(8,128)(2,1)} %bitcast.2, bf16[4,64,768]{2,1,0:T(8,128)(2,1)} %w_ref.3, bf16[256,768]{1,0:T(8,128)(2,1)} %go_ref.3), custom_call_target="tpu_custom_call" | custom-call | flops 100663296 | bytes 786432 | tf_op jit(solution)/shard_map/pallas_call | solution.py:230
  24.2 0.7 collective-permute-start.6
  24.9 1.7 %collective-permute-start.7 = (bf16[128,256]{1,0:T(8,128)(2,1)}, bf16[128,256]{1,0:T(8,128)(2,1)S(1)}, u32[]{:S(2)}, u32[]{:S(2)}) collective-permute-start(bf16[128,256]{1,0:T(8,128)(2,1)} %get-tuple-element.46), channel_id=1, source_target_pairs={{0,16},{2,18},{4,20},{6,22},{8,24},{10,26},{12,28},{14,30},{16,0},... | collective-permute-start | bytes 196616 | tf_op jit(solution)/shard_map/ppermute | solution.py:218
  26.5 2.1 %collective-permute-start.8 = (bf16[128,256]{1,0:T(8,128)(2,1)}, bf16[128,256]{1,0:T(8,128)(2,1)S(1)}, u32[]{:S(2)}, u32[]{:S(2)}) collective-permute-start(bf16[128,256]{1,0:T(8,128)(2,1)} %get-tuple-element.47), channel_id=1, source_target_pairs={{0,24},{2,26},{4,28},{6,30},{8,16},{10,18},{12,20},{14,22},{16,8},... | collective-permute-start | bytes 196616 | tf_op jit(solution)/shard_map/ppermute | solution.py:218
  28.6 1.6 %collective-permute-done.6.refs_5_ = bf16[128,256]{1,0:T(8,128)(2,1)S(1)} collective-permute-done((bf16[128,256]{1,0:T(8,128)(2,1)}, bf16[128,256]{1,0:T(8,128)(2,1)S(1)}, u32[]{:S(2)}, u32[]{:S(2)}) %collective-permute-start.6) | collective-permute-done | bytes 65568 | tf_op jit(solution)/shard_map/ppermute | solution.py:218
  30.2 0.4 collective-permute-done.7.refs_6_
  30.6 2.7 %collective-permute-done.8.refs_7_ = bf16[128,256]{1,0:T(8,128)(2,1)S(1)} collective-permute-done((bf16[128,256]{1,0:T(8,128)(2,1)}, bf16[128,256]{1,0:T(8,128)(2,1)S(1)}, u32[]{:S(2)}, u32[]{:S(2)}) %collective-permute-start.8) | collective-permute-done | bytes 65568 | tf_op jit(solution)/shard_map/ppermute | solution.py:218
  33.3 0.0 collective-permute-done.3.refs_1_
  33.3 0.0 collective-permute-done.5.refs_3_
  33.3 0.8 copy-done.3
  34.2 8.3 %shard_map.86 = (bf16[64,256]{1,0:T(8,128)(2,1)S(1)}, bf16[64,256]{1,0:T(8,128)(2,1)S(1)}, bf16[64,256]{1,0:T(8,128)(2,1)S(1)}, bf16[64,256]{1,0:T(8,128)(2,1)S(...) custom-call(bf16[1024,128]{1,0:T(8,128)(2,1)S(1)} %constant_dynamic-, ...), custom_call_target="tpu_custom_call" | custom-call | flops 2147483648 | bytes 2097152 | tf_op jit(solution)/shard_map/pallas_call | solution.py:246
  42.5 1.8 %collective-permute-start.9 = (bf16[64,256]{1,0:T(8,128)(2,1)S(1)}, bf16[64,256]{1,0:T(8,128)(2,1)S(1)}, u32[]{:S(2)}, u32[]{:S(2)}) collective-permute-start(bf16[64,256]{1,0:T(8,128)(2,1)S(1)} %get-tuple-element.49), channel_id=1, source_target_pairs={{0,8},{2,10},{4,12},{6,14},{8,0},{10,2},{12,4},{14,6},{16,24},{18,... | collective-permute-start | bytes 98312 | tf_op jit(solution)/shard_map/ppermute | solution.py:218
  44.3 1.2 %collective-permute-start.10 = (bf16[64,256]{1,0:T(8,128)(2,1)S(1)}, bf16[64,256]{1,0:T(8,128)(2,1)S(1)}, u32[]{:S(2)}, u32[]{:S(2)}) collective-permute-start(bf16[64,256]{1,0:T(8,128)(2,1)S(1)} %get-tuple-element.50), channel_id=1, source_target_pairs={{0,16},{2,18},{4,20},{6,22},{8,24},{10,26},{12,28},{14,30},{16,0},... | collective-permute-start | bytes 98312 | tf_op jit(solution)/shard_map/ppermute | solution.py:218
  45.5 1.5 %collective-permute-start.11 = (bf16[64,256]{1,0:T(8,128)(2,1)S(1)}, bf16[64,256]{1,0:T(8,128)(2,1)S(1)}, u32[]{:S(2)}, u32[]{:S(2)}) collective-permute-start(bf16[64,256]{1,0:T(8,128)(2,1)S(1)} %get-tuple-element.51), channel_id=1, source_target_pairs={{0,24},{2,26},{4,28},{6,30},{8,16},{10,18},{12,20},{14,22},{16,8},... | collective-permute-start | bytes 98312 | tf_op jit(solution)/shard_map/ppermute | solution.py:218
  46.9 0.0 collective-permute-done.9.refs_1_
  46.9 3.2 %collective-permute-done.10.refs_2_ = bf16[64,256]{1,0:T(8,128)(2,1)S(1)} collective-permute-done((bf16[64,256]{1,0:T(8,128)(2,1)S(1)}, bf16[64,256]{1,0:T(8,128)(2,1)S(1)}, u32[]{:S(2)}, u32[]{:S(2)}) %collective-permute-start.10) | collective-permute-done | bytes 32800 | tf_op jit(solution)/shard_map/ppermute | solution.py:218
  50.1 1.1 %collective-permute-done.11.refs_3_ = bf16[64,256]{1,0:T(8,128)(2,1)S(1)} collective-permute-done((bf16[64,256]{1,0:T(8,128)(2,1)S(1)}, bf16[64,256]{1,0:T(8,128)(2,1)S(1)}, u32[]{:S(2)}, u32[]{:S(2)}) %collective-permute-start.11) | collective-permute-done | bytes 32800 | tf_op jit(solution)/shard_map/ppermute | solution.py:218
  51.2 1.4 %shard_map.87 = (bf16[256,768]{1,0:T(8,128)(2,1)S(1)}, bf16[2,64,768]{2,1,0:T(8,128)(2,1)S(1)}, bf16[2,64,768]{2,1,0:T(8,128)(2,1)S(1)}) custom-call(s32[2]{0:T(128)S(1)} %copy-done.2, bf16[4,64,768]{2,1,0:T(8,128)(2,1)S(1)} %copy-done, bf16[256,768]{1,0:T(8,128)(2,1)S(1)} %copy-done.1, bf16[64,256]{1,0:T(8,128)(2,1)S(1)} %get-tuple-element.48.refs_0_, ...), custom_call_target="tpu_custom_call" | custom-call | flops 201326592 | bytes 786432 | tf_op jit(solution)/shard_map/pallas_call | solution.py:256
  52.6 0.1 collective-permute-start.22
  52.7 7.8 %shard_map.89 = (bf16[128,1024]{1,0:T(8,128)(2,1)S(1)}, bf16[128,1024]{1,0:T(8,128)(2,1)S(1)}, bf16[128,1024]{1,0:T(8,128)(2,1)S(1)}, bf16[128,1024]{1,0:T(8,128...) custom-call(bf16[4096,1024]{1,0:T(8,128)(2,1)S(1)} %get-tuple-elemen, ...), custom_call_target="tpu_custom_call" | custom-call | flops 2684354560 | bytes 2097152 | tf_op jit(solution)/shard_map/pallas_call | solution.py:263
  60.5 0.6 collective-permute-start.14
  61.0 0.0 collective-permute-done.22.came_ref
  61.1 1.6 %collective-permute-start.23 = (bf16[64,768]{1,0:T(8,128)(2,1)S(1)}, bf16[64,768]{1,0:T(8,128)(2,1)S(1)}, u32[]{:S(2)}, u32[]{:S(2)}) collective-permute-start(bf16[64,768]{1,0:T(8,128)(2,1)S(1)} %get-tuple-element.75), channel_id=1, source_target_pairs={{0,4},{2,6},{4,0},{6,2},{8,12},{10,14},{12,8},{14,10},{16,20},{18,... | collective-permute-start | bytes 294920 | tf_op jit(solution)/shard_map/ppermute | solution.py:218
  62.7 1.5 %collective-permute-start.12 = (bf16[256,768]{1,0:T(8,128)(2,1)S(1)}, bf16[256,768]{1,0:T(8,128)(2,1)S(1)}, u32[]{:S(2)}, u32[]{:S(2)}) collective-permute-start(bf16[256,768]{1,0:T(8,128)(2,1)S(1)} %get-tuple-element.52.a_ref._), channel_id=1, source_target_pairs={{0,1},{1,0},{2,3},{3,2},{4,5},{5,4},{6,7},{7,6},{8,9},{9,8},{10,11... | collective-permute-start | bytes 1179656 | tf_op jit(solution)/shard_map/ppermute | solution.py:218
  64.2 1.7 %collective-permute-done.23.b_ref = bf16[64,768]{1,0:T(8,128)(2,1)S(1)} collective-permute-done((bf16[64,768]{1,0:T(8,128)(2,1)S(1)}, bf16[64,768]{1,0:T(8,128)(2,1)S(1)}, u32[]{:S(2)}, u32[]{:S(2)}) %collective-permute-start.23) | collective-permute-done | bytes 98336 | tf_op jit(solution)/shard_map/ppermute | solution.py:218
  65.9 0.2 collective-permute-start.24
  66.1 0.0 collective-permute-start.13
  66.1 0.0 collective-permute-done.14.b_ref
  66.1 0.1 shard_map.91
  66.2 1.6 %collective-permute-start.15 = (bf16[128,1024]{1,0:T(8,128)(2,1)S(1)}, bf16[128,1024]{1,0:T(8,128)(2,1)S(1)}, u32[]{:S(2)}, u32[]{:S(2)}) collective-permute-start(bf16[128,1024]{1,0:T(8,128)(2,1)S(1)} %shard_map.91), channel_id=1, source_target_pairs={{0,4},{2,6},{4,0},{6,2},{8,12},{10,14},{12,8},{14,10},{16,20},{18,... | collective-permute-start | bytes 786440 | tf_op jit(solution)/shard_map/ppermute | solution.py:218
  67.7 2.9 %collective-permute-done.24.b_ref = bf16[64,768]{1,0:T(8,128)(2,1)S(1)} collective-permute-done((bf16[64,768]{1,0:T(8,128)(2,1)S(1)}, bf16[64,768]{1,0:T(8,128)(2,1)S(1)}, u32[]{:S(2)}, u32[]{:S(2)}) %collective-permute-start.24) | collective-permute-done | bytes 98336 | tf_op jit(solution)/shard_map/ppermute | solution.py:218
  70.6 0.7 collective-permute-start.25
  71.4 5.4 %collective-permute-done.25.b_ref = bf16[64,768]{1,0:T(8,128)(2,1)S(1)} collective-permute-done((bf16[64,768]{1,0:T(8,128)(2,1)S(1)}, bf16[64,768]{1,0:T(8,128)(2,1)S(1)}, u32[]{:S(2)}, u32[]{:S(2)}) %collective-permute-start.25) | collective-permute-done | bytes 98336 | tf_op jit(solution)/shard_map/ppermute | solution.py:218
  76.8 1.6 %collective-permute-start.27 = (bf16[64,768]{1,0:T(8,128)(2,1)S(1)}, bf16[64,768]{1,0:T(8,128)(2,1)S(1)}, u32[]{:S(2)}, u32[]{:S(2)}) collective-permute-start(bf16[64,768]{1,0:T(8,128)(2,1)S(1)} %shard_map.97.refs_0_), channel_id=1, source_target_pairs={{0,4},{2,6},{4,0},{6,2},{8,12},{10,14},{12,8},{14,10},{16,20},{18,... | collective-permute-start | bytes 294920 | tf_op jit(solution)/shard_map/ppermute | solution.py:218
  78.4 4.1 %collective-permute-done.19.refs_5_ = bf16[64,256]{1,0:T(8,128)(2,1)S(1)} collective-permute-done((bf16[64,256]{1,0:T(8,128)(2,1)S(1)}, bf16[64,256]{1,0:T(8,128)(2,1)S(1)}, u32[]{:S(2)}, u32[]{:S(2)}) %collective-permute-start.19) | collective-permute-done | bytes 32800 | tf_op jit(solution)/shard_map/ppermute | solution.py:218
  82.5 0.4 collective-permute-start.20
  82.9 0.0 collective-permute-done.13.b_ref
  82.9 1.8 %collective-permute-start.21 = (bf16[64,256]{1,0:T(8,128)(2,1)S(1)}, bf16[64,256]{1,0:T(8,128)(2,1)S(1)}, u32[]{:S(2)}, u32[]{:S(2)}) collective-permute-start(bf16[64,256]{1,0:T(8,128)(2,1)S(1)} %get-tuple-element.69), channel_id=1, source_target_pairs={{0,24},{2,26},{4,28},{6,30},{8,16},{10,18},{12,20},{14,22},{16,8},... | collective-permute-start | bytes 98312 | tf_op jit(solution)/shard_map/ppermute | solution.py:218
  84.7 0.5 collective-permute-start.28
  85.2 0.1 shard_map.90.kept_ref
  85.3 0.1 shard_map.92
  85.4 2.0 %collective-permute-done.20.refs_6_ = bf16[64,256]{1,0:T(8,128)(2,1)S(1)} collective-permute-done((bf16[64,256]{1,0:T(8,128)(2,1)S(1)}, bf16[64,256]{1,0:T(8,128)(2,1)S(1)}, u32[]{:S(2)}, u32[]{:S(2)}) %collective-permute-start.20) | collective-permute-done | bytes 32800 | tf_op jit(solution)/shard_map/ppermute | solution.py:218
  87.3 1.4 %collective-permute-done.21.refs_7_ = bf16[64,256]{1,0:T(8,128)(2,1)S(1)} collective-permute-done((bf16[64,256]{1,0:T(8,128)(2,1)S(1)}, bf16[64,256]{1,0:T(8,128)(2,1)S(1)}, u32[]{:S(2)}, u32[]{:S(2)}) %collective-permute-start.21) | collective-permute-done | bytes 32800 | tf_op jit(solution)/shard_map/ppermute | solution.py:218
  88.7 1.0 %collective-permute-start.17 = (bf16[128,256]{1,0:T(8,128)(2,1)S(1)}, bf16[128,256]{1,0:T(8,128)(2,1)S(1)}, u32[]{:S(2)}, u32[]{:S(2)}) collective-permute-start(bf16[128,256]{1,0:T(8,128)(2,1)S(1)} %get-tuple-element.64), channel_id=1, source_target_pairs={{0,16},{2,18},{4,20},{6,22},{8,24},{10,26},{12,28},{14,30},{16,0},... | collective-permute-start | bytes 196616 | tf_op jit(solution)/shard_map/ppermute | solution.py:218
  89.8 2.0 %collective-permute-start.18 = (bf16[128,256]{1,0:T(8,128)(2,1)S(1)}, bf16[128,256]{1,0:T(8,128)(2,1)S(1)}, u32[]{:S(2)}, u32[]{:S(2)}) collective-permute-start(bf16[128,256]{1,0:T(8,128)(2,1)S(1)} %get-tuple-element.65), channel_id=1, source_target_pairs={{0,24},{2,26},{4,28},{6,30},{8,16},{10,18},{12,20},{14,22},{16,8},... | collective-permute-start | bytes 196616 | tf_op jit(solution)/shard_map/ppermute | solution.py:218
  91.7 0.8 shard_map.88
  92.6 2.0 %collective-permute-done.17.refs_2_ = bf16[128,256]{1,0:T(8,128)(2,1)S(1)} collective-permute-done((bf16[128,256]{1,0:T(8,128)(2,1)S(1)}, bf16[128,256]{1,0:T(8,128)(2,1)S(1)}, u32[]{:S(2)}, u32[]{:S(2)}) %collective-permute-start.17) | collective-permute-done | bytes 65568 | tf_op jit(solution)/shard_map/ppermute | solution.py:218
  94.6 1.3 %collective-permute-done.18.refs_3_ = bf16[128,256]{1,0:T(8,128)(2,1)S(1)} collective-permute-done((bf16[128,256]{1,0:T(8,128)(2,1)S(1)}, bf16[128,256]{1,0:T(8,128)(2,1)S(1)}, u32[]{:S(2)}, u32[]{:S(2)}) %collective-permute-start.18) | collective-permute-done | bytes 65568 | tf_op jit(solution)/shard_map/ppermute | solution.py:218
  95.9 1.3 %shard_map.93 = (f32[256,4,128]{2,1,0:T(4,128)}, f32[4,64,256]{2,1,0:T(8,128)}) custom-call(bf16[128,256]{1,0:T(8,128)(2,1)S(1)} %get-tuple-element.62.refs_0_, bf16[128,256]{1,0:T(8,128)(2,1)S(1)} %collective-permute-done.16.refs_1_, bf16[128,256]{1,0:T(8,128)(2,1)S(1)} %collective-permute-done.17.refs_2_, ...), custom_call_target="tpu_custom_call" | custom-call | bytes 524288 | tf_op jit(solution)/shard_map/pallas_call | solution.py:304
  97.2 0.9 shard_map.98
  (21 shorter events, 0.2 us)
Async XLA Ops:
  0.6 50.5 %copy-start.2 = (s32[2]{0:T(128)S(1)}, s32[2]{0:T(128)}, u32[]{:S(2)}) copy-start(s32[2]{0:T(128)} %fill_ref.5) | copy-start | bytes 28
  0.6 50.5 %copy-start.1 = (bf16[256,768]{1,0:T(8,128)(2,1)S(1)}, bf16[256,768]{1,0:T(8,128)(2,1)}, u32[]{:S(2)}) copy-start(bf16[256,768]{1,0:T(8,128)(2,1)} %go_ref.3) | copy-start | bytes 1179652
  0.7 50.5 %copy-start = (bf16[4,64,768]{2,1,0:T(8,128)(2,1)S(1)}, bf16[4,64,768]{2,1,0:T(8,128)(2,1)}, u32[]{:S(2)}) copy-start(bf16[4,64,768]{2,1,0:T(8,128)(2,1)} %w_ref.3) | copy-start | bytes 1179652
  3.2 6.5 %collective-permute-start = (bf16[256,128]{1,0:T(8,128)(2,1)}, bf16[256,128]{1,0:T(8,128)(2,1)S(1)}, u32[]{:S(2)}, u32[]{:S(2)}) collective-permute-start(bf16[256,128]{1,0:T(8,128)(2,1)} %get-tuple-element.41), channel_id=1, source_target_pairs={{0,8},{2,10},{4,12},{6,14},{8,0},{10,2},{12,4},{14,6},{16,24},{18,... | collective-permute-start | bytes 196616 | tf_op jit(solution)/shard_map/ppermute | solution.py:218
  6.3 7.5 %collective-permute-start.1 = (bf16[256,128]{1,0:T(8,128)(2,1)}, bf16[256,128]{1,0:T(8,128)(2,1)S(1)}, u32[]{:S(2)}, u32[]{:S(2)}) collective-permute-start(bf16[256,128]{1,0:T(8,128)(2,1)} %get-tuple-element.42), channel_id=1, source_target_pairs={{0,16},{2,18},{4,20},{6,22},{8,24},{10,26},{12,28},{14,30},{16,0},... | collective-permute-start | bytes 196616 | tf_op jit(solution)/shard_map/ppermute | solution.py:218
  8.9 6.3 %collective-permute-start.2 = (bf16[256,128]{1,0:T(8,128)(2,1)}, bf16[256,128]{1,0:T(8,128)(2,1)S(1)}, u32[]{:S(2)}, u32[]{:S(2)}) collective-permute-start(bf16[256,128]{1,0:T(8,128)(2,1)} %get-tuple-element.43), channel_id=1, source_target_pairs={{0,24},{2,26},{4,28},{6,30},{8,16},{10,18},{12,20},{14,22},{16,8},... | collective-permute-start | bytes 196616 | tf_op jit(solution)/shard_map/ppermute | solution.py:218
  15.2 6.5 %collective-permute-start.4 = (bf16[1024,128]{1,0:T(8,128)(2,1)S(1)}, bf16[1024,128]{1,0:T(8,128)(2,1)S(1)}, u32[]{:S(2)}, u32[]{:S(2)}) collective-permute-start(bf16[1024,128]{1,0:T(8,128)(2,1)S(1)} %constant_dynamic-update-slice_fusion.refs_0_), channel_id=1, source_target_pairs={{0,4},{2,6},{4,0},{6,2},{8,12},{10,14},{12,8},{14,10},{16,20},{18,... | collective-permute-start | bytes 786440 | tf_op jit(solution)/shard_map/ppermute | solution.py:218
  16.7 16.6 %collective-permute-start.3 = (bf16[1024,128]{1,0:T(8,128)(2,1)S(1)}, bf16[1024,128]{1,0:T(8,128)(2,1)S(1)}, u32[]{:S(2)}, u32[]{:S(2)}) collective-permute-start(bf16[1024,128]{1,0:T(8,128)(2,1)S(1)} %constant_dynamic-update-slice_fusion.refs_0_), channel_id=1, source_target_pairs={{0,2},{2,0},{4,6},{6,4},{8,10},{10,8},{12,14},{14,12},{16,18},{18,... | collective-permute-start | bytes 786440 | tf_op jit(solution)/shard_map/ppermute | solution.py:218
  21.6 11.7 %collective-permute-start.5 = (bf16[1024,128]{1,0:T(8,128)(2,1)S(1)}, bf16[1024,128]{1,0:T(8,128)(2,1)S(1)}, u32[]{:S(2)}, u32[]{:S(2)}) collective-permute-start(bf16[1024,128]{1,0:T(8,128)(2,1)S(1)} %collective-permute-done.4.refs_2_), channel_id=1, source_target_pairs={{0,2},{2,0},{4,6},{6,4},{8,10},{10,8},{12,14},{14,12},{16,18},{18,... | collective-permute-start | bytes 786440 | tf_op jit(solution)/shard_map/ppermute | solution.py:218
  24.2 5.9 %collective-permute-start.6 = (bf16[128,256]{1,0:T(8,128)(2,1)}, bf16[128,256]{1,0:T(8,128)(2,1)S(1)}, u32[]{:S(2)}, u32[]{:S(2)}) collective-permute-start(bf16[128,256]{1,0:T(8,128)(2,1)} %get-tuple-element.45), channel_id=1, source_target_pairs={{0,8},{2,10},{4,12},{6,14},{8,0},{10,2},{12,4},{14,6},{16,24},{18,... | collective-permute-start | bytes 196616 | tf_op jit(solution)/shard_map/ppermute | solution.py:218
  24.9 5.7 %collective-permute-start.7 = (bf16[128,256]{1,0:T(8,128)(2,1)}, bf16[128,256]{1,0:T(8,128)(2,1)S(1)}, u32[]{:S(2)}, u32[]{:S(2)}) collective-permute-start(bf16[128,256]{1,0:T(8,128)(2,1)} %get-tuple-element.46), channel_id=1, source_target_pairs={{0,16},{2,18},{4,20},{6,22},{8,24},{10,26},{12,28},{14,30},{16,0},... | collective-permute-start | bytes 196616 | tf_op jit(solution)/shard_map/ppermute | solution.py:218
  26.5 6.8 %collective-permute-start.8 = (bf16[128,256]{1,0:T(8,128)(2,1)}, bf16[128,256]{1,0:T(8,128)(2,1)S(1)}, u32[]{:S(2)}, u32[]{:S(2)}) collective-permute-start(bf16[128,256]{1,0:T(8,128)(2,1)} %get-tuple-element.47), channel_id=1, source_target_pairs={{0,24},{2,26},{4,28},{6,30},{8,16},{10,18},{12,20},{14,22},{16,8},... | collective-permute-start | bytes 196616 | tf_op jit(solution)/shard_map/ppermute | solution.py:218
  33.3 0.8 copy-start.3
  42.5 4.5 %collective-permute-start.9 = (bf16[64,256]{1,0:T(8,128)(2,1)S(1)}, bf16[64,256]{1,0:T(8,128)(2,1)S(1)}, u32[]{:S(2)}, u32[]{:S(2)}) collective-permute-start(bf16[64,256]{1,0:T(8,128)(2,1)S(1)} %get-tuple-element.49), channel_id=1, source_target_pairs={{0,8},{2,10},{4,12},{6,14},{8,0},{10,2},{12,4},{14,6},{16,24},{18,... | collective-permute-start | bytes 98312 | tf_op jit(solution)/shard_map/ppermute | solution.py:218
  44.3 5.8 %collective-permute-start.10 = (bf16[64,256]{1,0:T(8,128)(2,1)S(1)}, bf16[64,256]{1,0:T(8,128)(2,1)S(1)}, u32[]{:S(2)}, u32[]{:S(2)}) collective-permute-start(bf16[64,256]{1,0:T(8,128)(2,1)S(1)} %get-tuple-element.50), channel_id=1, source_target_pairs={{0,16},{2,18},{4,20},{6,22},{8,24},{10,26},{12,28},{14,30},{16,0},... | collective-permute-start | bytes 98312 | tf_op jit(solution)/shard_map/ppermute | solution.py:218
  45.5 5.7 %collective-permute-start.11 = (bf16[64,256]{1,0:T(8,128)(2,1)S(1)}, bf16[64,256]{1,0:T(8,128)(2,1)S(1)}, u32[]{:S(2)}, u32[]{:S(2)}) collective-permute-start(bf16[64,256]{1,0:T(8,128)(2,1)S(1)} %get-tuple-element.51), channel_id=1, source_target_pairs={{0,24},{2,26},{4,28},{6,30},{8,16},{10,18},{12,20},{14,22},{16,8},... | collective-permute-start | bytes 98312 | tf_op jit(solution)/shard_map/ppermute | solution.py:218
  52.6 8.4 %collective-permute-start.22 = (bf16[2,64,768]{2,1,0:T(8,128)(2,1)S(1)}, bf16[2,64,768]{2,1,0:T(8,128)(2,1)S(1)}, u32[]{:S(2)}, u32[]{:S(2)}) collective-permute-start(bf16[2,64,768]{2,1,0:T(8,128)(2,1)S(1)} %get-tuple-element.73), channel_id=1, source_target_pairs={{0,2},{2,0},{4,6},{6,4},{8,10},{10,8},{12,14},{14,12},{16,18},{18,... | collective-permute-start | bytes 589832 | tf_op jit(solution)/shard_map/ppermute | solution.py:218
  60.5 5.6 %collective-permute-start.14 = (bf16[128,1024]{1,0:T(8,128)(2,1)S(1)}, bf16[128,1024]{1,0:T(8,128)(2,1)S(1)}, u32[]{:S(2)}, u32[]{:S(2)}) collective-permute-start(bf16[128,1024]{1,0:T(8,128)(2,1)S(1)} %get-tuple-element.61), channel_id=1, source_target_pairs={{0,2},{2,0},{4,6},{6,4},{8,10},{10,8},{12,14},{14,12},{16,18},{18,... | collective-permute-start | bytes 786440 | tf_op jit(solution)/shard_map/ppermute | solution.py:218
  61.1 4.8 %collective-permute-start.23 = (bf16[64,768]{1,0:T(8,128)(2,1)S(1)}, bf16[64,768]{1,0:T(8,128)(2,1)S(1)}, u32[]{:S(2)}, u32[]{:S(2)}) collective-permute-start(bf16[64,768]{1,0:T(8,128)(2,1)S(1)} %get-tuple-element.75), channel_id=1, source_target_pairs={{0,4},{2,6},{4,0},{6,2},{8,12},{10,14},{12,8},{14,10},{16,20},{18,... | collective-permute-start | bytes 294920 | tf_op jit(solution)/shard_map/ppermute | solution.py:218
  62.7 27.1 %collective-permute-start.12 = (bf16[256,768]{1,0:T(8,128)(2,1)S(1)}, bf16[256,768]{1,0:T(8,128)(2,1)S(1)}, u32[]{:S(2)}, u32[]{:S(2)}) collective-permute-start(bf16[256,768]{1,0:T(8,128)(2,1)S(1)} %get-tuple-element.52.a_ref._), channel_id=1, source_target_pairs={{0,1},{1,0},{2,3},{3,2},{4,5},{5,4},{6,7},{7,6},{8,9},{9,8},{10,11... | collective-permute-start | bytes 1179656 | tf_op jit(solution)/shard_map/ppermute | solution.py:218
  65.9 4.7 %collective-permute-start.24 = (bf16[64,768]{1,0:T(8,128)(2,1)S(1)}, bf16[64,768]{1,0:T(8,128)(2,1)S(1)}, u32[]{:S(2)}, u32[]{:S(2)}) collective-permute-start(bf16[64,768]{1,0:T(8,128)(2,1)S(1)} %shard_map.95.a_ref), channel_id=1, source_target_pairs={{0,8},{2,10},{4,12},{6,14},{8,0},{10,2},{12,4},{14,6},{16,24},{18,... | collective-permute-start | bytes 294920 | tf_op jit(solution)/shard_map/ppermute | solution.py:218
  66.1 16.8 %collective-permute-start.13 = (bf16[128,1024]{1,0:T(8,128)(2,1)S(1)}, bf16[128,1024]{1,0:T(8,128)(2,1)S(1)}, u32[]{:S(2)}, u32[]{:S(2)}) collective-permute-start(bf16[128,1024]{1,0:T(8,128)(2,1)S(1)} %get-tuple-element.59), channel_id=1, source_target_pairs={{0,2},{2,0},{4,6},{6,4},{8,10},{10,8},{12,14},{14,12},{16,18},{18,... | collective-permute-start | bytes 786440 | tf_op jit(solution)/shard_map/ppermute | solution.py:218
  66.2 18.5 %collective-permute-start.15 = (bf16[128,1024]{1,0:T(8,128)(2,1)S(1)}, bf16[128,1024]{1,0:T(8,128)(2,1)S(1)}, u32[]{:S(2)}, u32[]{:S(2)}) collective-permute-start(bf16[128,1024]{1,0:T(8,128)(2,1)S(1)} %shard_map.91), channel_id=1, source_target_pairs={{0,4},{2,6},{4,0},{6,2},{8,12},{10,14},{12,8},{14,10},{16,20},{18,... | collective-permute-start | bytes 786440 | tf_op jit(solution)/shard_map/ppermute | solution.py:218
  70.6 6.2 %collective-permute-start.25 = (bf16[64,768]{1,0:T(8,128)(2,1)S(1)}, bf16[64,768]{1,0:T(8,128)(2,1)S(1)}, u32[]{:S(2)}, u32[]{:S(2)}) collective-permute-start(bf16[64,768]{1,0:T(8,128)(2,1)S(1)} %shard_map.96.a_ref), channel_id=1, source_target_pairs={{0,16},{2,18},{4,20},{6,22},{8,24},{10,26},{12,28},{14,30},{16,0},... | collective-permute-start | bytes 294920 | tf_op jit(solution)/shard_map/ppermute | solution.py:218
  76.8 7.9 %collective-permute-start.27 = (bf16[64,768]{1,0:T(8,128)(2,1)S(1)}, bf16[64,768]{1,0:T(8,128)(2,1)S(1)}, u32[]{:S(2)}, u32[]{:S(2)}) collective-permute-start(bf16[64,768]{1,0:T(8,128)(2,1)S(1)} %shard_map.97.refs_0_), channel_id=1, source_target_pairs={{0,4},{2,6},{4,0},{6,2},{8,12},{10,14},{12,8},{14,10},{16,20},{18,... | collective-permute-start | bytes 294920 | tf_op jit(solution)/shard_map/ppermute | solution.py:218
  78.4 4.1 %collective-permute-start.19 = (bf16[64,256]{1,0:T(8,128)(2,1)S(1)}, bf16[64,256]{1,0:T(8,128)(2,1)S(1)}, u32[]{:S(2)}, u32[]{:S(2)}) collective-permute-start(bf16[64,256]{1,0:T(8,128)(2,1)S(1)} %get-tuple-element.67), channel_id=1, source_target_pairs={{0,8},{2,10},{4,12},{6,14},{8,0},{10,2},{12,4},{14,6},{16,24},{18,... | collective-permute-start | bytes 98312 | tf_op jit(solution)/shard_map/ppermute | solution.py:218
  82.5 4.8 %collective-permute-start.20 = (bf16[64,256]{1,0:T(8,128)(2,1)S(1)}, bf16[64,256]{1,0:T(8,128)(2,1)S(1)}, u32[]{:S(2)}, u32[]{:S(2)}) collective-permute-start(bf16[64,256]{1,0:T(8,128)(2,1)S(1)} %get-tuple-element.68), channel_id=1, source_target_pairs={{0,16},{2,18},{4,20},{6,22},{8,24},{10,26},{12,28},{14,30},{16,0},... | collective-permute-start | bytes 98312 | tf_op jit(solution)/shard_map/ppermute | solution.py:218
  82.9 5.8 %collective-permute-start.21 = (bf16[64,256]{1,0:T(8,128)(2,1)S(1)}, bf16[64,256]{1,0:T(8,128)(2,1)S(1)}, u32[]{:S(2)}, u32[]{:S(2)}) collective-permute-start(bf16[64,256]{1,0:T(8,128)(2,1)S(1)} %get-tuple-element.69), channel_id=1, source_target_pairs={{0,24},{2,26},{4,28},{6,30},{8,16},{10,18},{12,20},{14,22},{16,8},... | collective-permute-start | bytes 98312 | tf_op jit(solution)/shard_map/ppermute | solution.py:218
  84.7 12.5 %collective-permute-start.26 = (bf16[64,768]{1,0:T(8,128)(2,1)S(1)}, bf16[64,768]{1,0:T(8,128)(2,1)S(1)}, u32[]{:S(2)}, u32[]{:S(2)}) collective-permute-start(bf16[64,768]{1,0:T(8,128)(2,1)S(1)} %shard_map.97.refs_0_), channel_id=1, source_target_pairs={{0,2},{2,0},{4,6},{6,4},{8,10},{10,8},{12,14},{14,12},{16,18},{18,... | collective-permute-start | bytes 294920 | tf_op jit(solution)/shard_map/ppermute | solution.py:218
  84.7 12.5 %collective-permute-start.28 = (bf16[64,768]{1,0:T(8,128)(2,1)S(1)}, bf16[64,768]{1,0:T(8,128)(2,1)S(1)}, u32[]{:S(2)}, u32[]{:S(2)}) collective-permute-start(bf16[64,768]{1,0:T(8,128)(2,1)S(1)} %collective-permute-done.27.refs_2_), channel_id=1, source_target_pairs={{0,2},{2,0},{4,6},{6,4},{8,10},{10,8},{12,14},{14,12},{16,18},{18,... | collective-permute-start | bytes 294920 | tf_op jit(solution)/shard_map/ppermute | solution.py:218
  87.3 5.2 %collective-permute-start.16 = (bf16[128,256]{1,0:T(8,128)(2,1)S(1)}, bf16[128,256]{1,0:T(8,128)(2,1)S(1)}, u32[]{:S(2)}, u32[]{:S(2)}) collective-permute-start(bf16[128,256]{1,0:T(8,128)(2,1)S(1)} %get-tuple-element.63), channel_id=1, source_target_pairs={{0,8},{2,10},{4,12},{6,14},{8,0},{10,2},{12,4},{14,6},{16,24},{18,... | collective-permute-start | bytes 196616 | tf_op jit(solution)/shard_map/ppermute | solution.py:218
  88.7 5.9 %collective-permute-start.17 = (bf16[128,256]{1,0:T(8,128)(2,1)S(1)}, bf16[128,256]{1,0:T(8,128)(2,1)S(1)}, u32[]{:S(2)}, u32[]{:S(2)}) collective-permute-start(bf16[128,256]{1,0:T(8,128)(2,1)S(1)} %get-tuple-element.64), channel_id=1, source_target_pairs={{0,16},{2,18},{4,20},{6,22},{8,24},{10,26},{12,28},{14,30},{16,0},... | collective-permute-start | bytes 196616 | tf_op jit(solution)/shard_map/ppermute | solution.py:218
  89.8 6.2 %collective-permute-start.18 = (bf16[128,256]{1,0:T(8,128)(2,1)S(1)}, bf16[128,256]{1,0:T(8,128)(2,1)S(1)}, u32[]{:S(2)}, u32[]{:S(2)}) collective-permute-start(bf16[128,256]{1,0:T(8,128)(2,1)S(1)} %get-tuple-element.65), channel_id=1, source_target_pairs={{0,24},{2,26},{4,28},{6,30},{8,16},{10,18},{12,20},{14,22},{16,8},... | collective-permute-start | bytes 196616 | tf_op jit(solution)/shard_map/ppermute | solution.py:218

commit v4 on v3

v4 whole, which is shorter than its diff:
```python
import functools

import jax
import jax.numpy as jnp
from jax import lax
from jax.experimental import pallas as pl
from jax.experimental.pallas import tpu as pltpu
from jax.sharding import PartitionSpec as P

TILE = 128
DEAD = 1024.0
BIAS = -1e30
F32 = jnp.float32
BF16 = jnp.bfloat16
VMEM = pl.BlockSpec(memory_space=pltpu.VMEM)
SMEM = pl.BlockSpec(memory_space=pltpu.SMEM)
MIB = 1024 * 1024


def dot(a, b):
    return lax.dot_general(a, b, (((1,), (0,)), ((), ())), preferred_element_type=F32)


def dot_nt(a, b):
    return lax.dot_general(a, b, (((1,), (1,)), ((), ())), preferred_element_type=F32)


def call(kernel, outs, scratch=(), n_in=1, smem_first=False, after=0, micros=0.3, limit=16):
    specs = [SMEM if smem_first else VMEM] + [VMEM] * (n_in - 1) + [pl.BlockSpec(memory_space=pl.ANY)] * after
    return pl.pallas_call(
        kernel,
        out_shape=[jax.ShapeDtypeStruct(shape, kind) for shape, kind in outs],
        in_specs=specs,
        out_specs=[VMEM] * len(outs),
        scratch_shapes=list(scratch),
        compiler_params=pltpu.CompilerParams(vmem_limit_bytes=limit * MIB),
        cost_estimate=pl.CostEstimate(flops=int(micros * 1.15e9), bytes_accessed=0, transcendentals=0),
    )


def live_column(fill_ref, rows):
    parts = []
    within = lax.broadcasted_iota(jnp.int32, (TILE, 1), 0)
    for tile in range(rows // TILE):
        parts.append(jnp.where(within < fill_ref[tile], 1.0, 0.0))
    return jnp.concatenate(parts, axis=0) if len(parts) > 1 else parts[0]


def pack_kv_kernel(heads, rows, dim, a_of, fill_ref, kv_ref, *refs):
    outs, (held,) = refs[:heads], refs[heads:]
    live = live_column(fill_ref, rows)
    lane = lax.broadcasted_iota(jnp.int32, (rows, 2 * dim), 1)
    mark = jnp.where(lane == 0, DEAD, 0.0)
    for head in range(heads):
        held[head] = jnp.where(live > 0, kv_ref[:, head, :].astype(F32), mark).astype(BF16)
    me = a_of()
    for slot in range(heads):
        outs[slot][...] = held[me ^ slot]


def pack_qg_kernel(heads, rows, dim, a_of, fill_ref, q_ref, w_ref, go_ref, *refs):
    outs, (held,) = refs[:heads], refs[heads:]
    live = live_column(fill_ref, rows)
    mixed = jnp.where(live > 0, go_ref[...].astype(F32), 0.0).astype(BF16)
    for head in range(heads):
        held[head, 0:dim, :] = (q_ref[head].astype(F32) * dim**-0.5).astype(BF16)
        held[head, dim:, :] = dot_nt(w_ref[head], mixed).astype(BF16)
    me = a_of()
    for slot in range(heads):
        outs[slot][...] = held[me ^ slot]


def join_kernel(pieces, *refs):
    out_ref = refs[-1]
    rows = refs[0].shape[0]
    for index in range(pieces):
        out_ref[index * rows : (index + 1) * rows, :] = refs[index][...]


def join_q_kernel(slots, rows, dim, *refs):
    pieces, (qa_ref, g_ref) = refs[:slots], refs[slots:]
    wide = 2 * dim
    row = lax.broadcasted_iota(jnp.int32, (wide, slots * rows), 0)
    qa_ref[dim:wide, :] = jnp.zeros((dim, slots * rows), BF16)
    qa_ref[wide:, :] = jnp.where(row == 0, 1.0, 0.0).astype(BF16)
    for slot in range(slots):
        here = slice(slot * rows, (slot + 1) * rows)
        qa_ref[0:dim, here] = pieces[slot][0:dim, :]
        g_ref[:, here] = pieces[slot][dim:, :]


def prep_kernel(dim, pair_ref, wide_ref, kt_ref, vt_ref):
    wide = 2 * dim
    keys = pair_ref.shape[0]
    pair = pair_ref[...]
    full = pair.astype(F32)
    lane = lax.broadcasted_iota(jnp.int32, (keys, wide), 1)
    ones = jnp.where(lane <= 2, 1.0, 0.0)
    bias = jnp.where(full[:, 0:1] >= DEAD, BIAS, 0.0)
    wide_ref[:, 0:wide] = pair
    wide_ref[:, wide:] = jnp.where(lane == 0, bias, ones).astype(BF16)
    turned = full.T.astype(BF16)
    kt_ref[...] = turned[:dim, :]
    vt_ref[0:dim, :] = turned[dim:, :]
    vt_ref[dim:, :] = jnp.ones((16, keys), BF16)


def score_kernel(slots, rows, dim, step, wide_ref, vt_ref, qa_ref, exp_ref, peak_ref, total_ref, score_ref):
    keys = wide_ref.shape[0]
    peak = None
    for turn in range(slots + 1):
        here = slice(turn * rows, (turn + 1) * rows)
        past = slice((turn - 1) * rows, turn * rows)
        top = jnp.full((8, rows), BIAS, F32)
        total = jnp.zeros((dim + 16, rows), F32)
        for start in range(0, keys, step):
            part = slice(start, start + step)
            if turn < slots:
                scores = dot(wide_ref[part, :], qa_ref[:, here])
                score_ref[turn % 2, part, :] = scores
                top = jnp.maximum(top, jnp.max(scores.reshape(step // 8, 8, rows), axis=0))
            if turn > 0:
                exps = jnp.exp(score_ref[(turn - 1) % 2, part, :] - peak).astype(BF16)
                exp_ref[part, past] = exps
                total = total + dot(vt_ref[:, part], exps)
        if turn > 0:
            total_ref[:, past] = total
            peak_ref[:, past] = peak
        peak = jnp.max(top, axis=0, keepdims=True)


def combine_kernel(slots, columns, rows, dim, *refs):
    peaks, totals, (g_ref,), outs = refs[:columns], refs[columns : 2 * columns], refs[2 * columns : 2 * columns + 1], refs[2 * columns + 1 :]
    att_out, factors_out, inner_ref = outs[:slots], outs[slots : slots + columns], outs[-1]
    peak = functools.reduce(jnp.maximum, [ref[...] for ref in peaks])
    factors = [jnp.exp(ref[...] - peak) for ref in peaks]
    total = sum(factor * ref[...] for factor, ref in zip(factors, totals))
    inverse = 1.0 / total[dim : dim + 1, :]
    attended = (total[0:dim, :] * inverse).astype(BF16)
    for slot in range(slots):
        att_out[slot][...] = attended[:, slot * rows : (slot + 1) * rows]
    for factor, ref in zip(factors, factors_out):
        ref[...] = factor * inverse
    inner_ref[...] = jnp.sum(g_ref[...].astype(F32) * attended.astype(F32), axis=0, keepdims=True)


def back_kernel(dim, step, first, exp_ref, wide_ref, kt_ref, qa_ref, g_ref, factor_ref, inner_ref, *refs):
    dkv_ref, dq_ref, ga_ref = refs[-3:]
    wide = 2 * dim
    keys = wide_ref.shape[0]
    factor = factor_ref[...]
    inner = inner_ref[...] * factor
    high = inner.astype(BF16).astype(F32)
    ga_ref[0:dim, :] = jnp.zeros((dim, g_ref.shape[1]), BF16)
    ga_ref[dim:wide, :] = (g_ref[...].astype(F32) * factor).astype(BF16)
    row = lax.broadcasted_iota(jnp.int32, (wide, g_ref.shape[1]), 0)
    ga_ref[wide:, :] = jnp.where(row == 1, -high, jnp.where(row == 2, high - inner, 0.0)).astype(BF16)
    total = None if first else refs[0][...]
    for start in range(0, keys, step):
        part = slice(start, start + step)
        exps = exp_ref[part, :]
        grads = (exps.astype(F32) * dot(wide_ref[part, :], ga_ref[...])).astype(BF16)
        dkv_ref[part, :] = (dot_nt(exps, ga_ref[0:wide, :]) + dot_nt(grads, qa_ref[0:wide, :])).astype(BF16)
        term = dot(kt_ref[:, part], grads)
        total = term if total is None else total + term
    dq_ref[...] = total


def project_kernel(slots, rows, dim, a_of, b_of, halves, fill_ref, w_ref, go_ref, *refs):
    att, refs = refs[:slots], refs[slots + 1 :]
    terms_ref, refs = refs[0], refs[1:]
    live = live_column(fill_ref, rows)
    mixed = jnp.where(live > 0, go_ref[...].astype(F32), 0.0).astype(BF16)
    me = a_of()
    held = refs[-1]
    total = None
    for slot in range(slots):
        head = me ^ slot
        held[head] = dot(att[slot][...], mixed).astype(BF16)
        term = dot(att[slot][...].astype(F32).T.astype(BF16), w_ref[head])
        total = term if total is None else total + term
    terms_ref[...] = (total * live).astype(BF16)
    if not halves:
        refs[0][...] = held[...]
        return
    me = b_of()
    kept_ref, sent_ref = refs[0], refs[1]
    for pair in range(slots // 2):
        kept_ref[pair] = held[me ^ (2 * pair)]
        sent_ref[pair] = held[me ^ (2 * pair) ^ 1]


def add_pairs_kernel(kept_ref, came_ref, first_ref, second_ref):
    for index, out_ref in enumerate((first_ref, second_ref)):
        out_ref[...] = (kept_ref[index].astype(F32) + came_ref[index].astype(F32)).astype(BF16)


def add_pieces_kernel(slots, rows, dim, kept_ref, came_ref, dq_ref, *outs):
    wide = 2 * dim
    for slot in range(slots):
        here = slice(slot * rows, (slot + 1) * rows)
        outs[slot][0:rows, :] = (kept_ref[here, :].astype(F32) + came_ref[here, :].astype(F32)).astype(BF16)
        for part in range(rows // wide):
            start = slot * rows + part * wide
            grad = dq_ref[:, start : start + wide] * dim**-0.5
            outs[slot][rows + part * dim : rows + (part + 1) * dim, :] = grad.astype(BF16)


def add_kernel(a_ref, b_ref, out_ref):
    out_ref[...] = (a_ref[...].astype(F32) + b_ref[...].astype(F32)).astype(out_ref.dtype)


def unpack_kernel(slots, rows, dim, a_of, *refs):
    pieces, (kv_out, q_out, held) = refs[:slots], refs[slots:]
    wide = 2 * dim
    me = a_of()
    for slot in range(slots):
        held[me ^ slot] = pieces[slot][0:rows, :].astype(F32)
        for part in range(rows // wide):
            start = rows + part * dim
            q_out[me ^ slot, :, part * wide : (part + 1) * wide] = pieces[slot][start : start + dim, :].astype(F32)
    for head in range(slots):
        kv_out[:, head, :] = held[head]


def place_kernel(columns, b_of, *refs):
    parts, (out_ref,) = refs[:columns], refs[columns:]
    me = b_of()
    for column in range(columns):
        out_ref[me ^ column] = parts[column][...].astype(F32)


def shards(seq, mp, queries, key_value, tile_fill, out_weight, grad_output):
    rows, heads, dim = queries.shape
    width = grad_output.shape[1]
    slots = heads
    columns = seq // slots
    assert slots * columns == seq and columns & (columns - 1) == 0 and slots & (slots - 1) == 0
    a_of = lambda: lax.axis_index("seq") // columns
    b_of = lambda: lax.axis_index("seq") % columns

    def swap(array, mask, axis="seq", size=seq):
        return lax.ppermute(array, axis, [(i, i ^ mask) for i in range(size)])

    def exchange(pieces):
        came = {s: swap(pieces[s], s * columns) for s in sorted(range(1, slots), key=lambda s: (s < slots // 2, s))}
        return [pieces[0]] + [came[s] for s in range(1, slots)]

    block, wide = slots * rows, 2 * dim
    kv_mine = exchange(call(
        functools.partial(pack_kv_kernel, heads, rows, dim, a_of),
        [((rows, wide), BF16)] * slots, [pltpu.VMEM((heads, rows, wide), BF16)],
        n_in=2, smem_first=True, micros=0.8,
    )(tile_fill, key_value))
    qg_send = call(
        functools.partial(pack_qg_kernel, heads, rows, dim, a_of),
        [((wide, rows), BF16)] * slots, [pltpu.VMEM((heads, wide, rows), BF16)],
        n_in=4, smem_first=True, micros=1,
    )(tile_fill, jnp.transpose(queries, (1, 2, 0)), out_weight, grad_output)
    qg_mine = exchange(qg_send)
    own = call(
        functools.partial(join_kernel, slots), [((block, wide), BF16)], n_in=slots, after=1,
    )(*kv_mine, qg_send[0])[0]

    blocks = {0: own}
    bit = columns // 2
    while bit:
        for r in sorted(blocks):
            blocks[r ^ bit] = swap(blocks[r], bit)
        bit //= 2

    qa, grads = call(
        functools.partial(join_q_kernel, slots, rows, dim), [((2 * wide, block), BF16), ((dim, block), BF16)], n_in=slots,
    )(*qg_mine)
    step = min(block, 512)
    prepared, scored = {}, {}
    for r in range(columns):
        prepared[r] = call(
            functools.partial(prep_kernel, dim),
            [((block, 2 * wide), BF16), ((dim, block), BF16), ((dim + 16, block), BF16)], micros=0.5,
        )(blocks[r])
        wide_keys, _, values = prepared[r]
        scored[r] = call(
            functools.partial(score_kernel, slots, rows, dim, step),
            [((block, block), BF16), ((1, block), F32), ((dim + 16, block), F32)],
            [pltpu.VMEM((min(slots, 2), block, rows), F32)], n_in=3, micros=2,
        )(wide_keys, values, qa)
    combined = call(
        functools.partial(combine_kernel, slots, columns, rows, dim),
        [((dim, rows), BF16)] * slots + [((1, block), F32)] * (columns + 1), n_in=2 * columns + 1, micros=0.5,
    )(*[scored[r][1] for r in range(columns)], *[scored[r][2] for r in range(columns)], grads)
    att_mine, factors, inner = exchange(combined[:slots]), combined[slots:-1], combined[-1]

    halves = columns == heads == 4
    order = sorted(range(columns), key=lambda r: -int(f"{r:032b}"[::-1], 2))
    dkv, dq = {}, None
    for at, r in enumerate(order):
        if at == columns // 2:
            terms, *weight_terms = call(
                functools.partial(project_kernel, slots, rows, dim, a_of, b_of, halves),
                [((rows, width), BF16)] + ([((2, dim, width), BF16)] * 2 if halves else [((heads, dim, width), BF16)]),
                [pltpu.VMEM((heads, dim, width), BF16)],
                n_in=3 + slots, smem_first=True, after=1, micros=1,
            )(tile_fill, out_weight, grad_output, *att_mine, dkv[order[at - 1]])
        operands = [scored[r][0], prepared[r][0], prepared[r][1], qa, grads, factors[r], inner] + ([] if dq is None else [dq])
        later = [terms] if at == columns // 2 else []
        dkv[r], dq = call(
            functools.partial(back_kernel, dim, min(step, 256), dq is None),
            [((block, wide), BF16), ((dim, block), F32)], [pltpu.VMEM((2 * wide, block), BF16)],
            n_in=len(operands), after=len(later), micros=2,
        )(*operands, *later)

    bit = 1
    while bit < mp:
        terms = call(add_kernel, [((rows, width), BF16)], n_in=2)(terms, swap(terms, bit, "mp", mp))[0]
        bit *= 2

    if halves:
        kept, sent = weight_terms
        kept, sent = call(add_pairs_kernel, [((dim, width), BF16)] * 2, n_in=2)(kept, swap(sent, 1))
        add = call(add_kernel, [((dim, width), BF16)], n_in=2)
        kept = add(kept, swap(sent, 2))[0]
        bit = columns
        while bit < seq:
            kept = add(kept, swap(kept, bit))[0]
            bit *= 2
        across = swap(kept, 2)
        weight_grad = call(
            functools.partial(place_kernel, columns, b_of), [((heads, dim, width), F32)], n_in=columns, micros=0.5,
        )(kept, swap(kept, 1), across, swap(across, 1))[0]
    else:
        weight_grad = lax.psum(weight_terms[0].astype(F32), "seq")

    bit = 1
    while 2 * bit < columns:
        dkv = {
            r: call(add_kernel, [((block, wide), BF16)], n_in=2)(dkv[r], swap(dkv[r ^ bit], bit))[0]
            for r in order if r in dkv and not r & bit
        }
        bit *= 2
    returned = exchange(call(
        functools.partial(add_pieces_kernel, slots, rows, dim), [((rows + rows // 2, wide), BF16)] * slots, n_in=3,
    )(dkv[0], swap(dkv[bit], bit), dq))
    key_value_grad, query_grad = call(
        functools.partial(unpack_kernel, slots, rows, dim, a_of),
        [((rows, heads, wide), F32), ((heads, dim, rows), F32)],
        [pltpu.VMEM((heads, rows, wide), F32)], n_in=slots, micros=1,
    )(*returned)
    return terms, jnp.transpose(query_grad, (2, 0, 1)), key_value_grad, weight_grad


def solution(mesh):
    return jax.shard_map(
        functools.partial(shards, mesh.shape["seq"], mesh.shape["mp"]),
        mesh=mesh,
        in_specs=(
            P("seq", "mp", None),
            P("seq", "mp", None),
            P("seq"),
            P("mp", None, None),
            P("seq", None),
        ),
        out_specs=(P("seq", None), P("seq", "mp", None), P("seq", "mp", None), P("mp", None, None)),
        check_vma=False,
    )
```

time: 98.4 us -> 72.9 us (0.74)
  waiting for transfers between devices: 40.1 us -> 12.4 us
  Pallas kernels: 26.1 us -> 27.3 us
    ppermute x29 -> x26, waiting for transfers between devices: 40.1 us -> 12.4 us  [swap(): return lax.ppermute(array, axis, [(i, i ^ mask) for i in range(size)])]
    pallas_call x6 -> x19, Pallas kernels: 17.1 us -> 21 us  [the longest x4 10.9 us: shards(): call(functools.partial(back_kernel, dim, min(step, 256), dq is None), [((...]
    pallas_call x1, Pallas kernels: 2.58 us -> 1.23 us  [shards(): call(functools.partial(pack_qg_kernel, heads, rows, dim, a_of), [((wide,...]
    pallas_call x1, Pallas kernels: 2.57 us -> 1.4 us  [shards(): call(functools.partial(pack_kv_kernel, heads, rows, dim, a_of), [((rows,...]
    ppermute x29 -> x26, starting transfers between devices: 29.5 us -> 30.4 us  [swap(): return lax.ppermute(array, axis, [(i, i ^ mask) for i in range(size)])]
  transfers between devices with their start and end apart: 29 -> 26, of which waited for: 16 -> 8; matrix products, arithmetic and copies ran while one was open for 1% -> 0% of each run, Pallas kernels for 13% -> 29%
where the time goes in v4:
time: 72.9 us; the launch traced here: 72.7 us
  starting transfers between devices  30.4 us (42%)
  Pallas kernels  27.3 us (37%)
  waiting for transfers between devices  12.4 us (17%)
  local copies, waits for them, and re-layouts  1.69 us (2%)
  between operations  0.95 us (1%)
    ppermute x26, starting transfers between devices, swap(): return lax.ppermute(array, axis, [(i, i ^ mask) for i in range(size)])  30.4 us
    ppermute x26, waiting for transfers between devices, swap(): return lax.ppermute(array, axis, [(i, i ^ mask) for i in range(size)])  12.4 us
    pallas_call x4, Pallas kernels, shards(): call(functools.partial(back_kernel, dim, min(step, 256), dq is None), [((...  10.9 us
    pallas_call x4, Pallas kernels, shards(): call(functools.partial(score_kernel, slots, rows, dim, step), [((block, b...  7.89 us
    unnamed x12, local copies, waits for them, and re-layouts  1.69 us
  transfers between devices with their start and end apart: 26, of which 8 were waited for; matrix products, arithmetic and copies ran while one was open for 0% of the time, Pallas kernels for 29%

profile of v4, /device:TPU:0, one launch (start us, length us, event | category | flops | bytes accessed | tf_op | source)
XLA Modules:
  0.0 72.7 jit_solution(2709974299652165068)
XLA Ops:
  0.7 1.0 %copy-done.2 = bf16[256,4,128]{2,1,0:T(4,128)(2,1)S(1)} copy-done((bf16[256,4,128]{2,1,0:T(4,128)(2,1)S(1)}, bf16[256,4,128]{2,1,0:T(4,128)(2,1)}, u32[]{:S(2)}) %copy-start.2) | copy-done | bytes 262168
  1.7 0.7 copy-done.4
  2.3 1.4 %shard_map.84 = (bf16[256,128]{1,0:T(8,128)(2,1)S(1)}, bf16[256,128]{1,0:T(8,128)(2,1)S(1)}, bf16[256,128]{1,0:T(8,128)(2,1)S(1)}, bf16[256,128]{1,0:T(8,128)(2,1)S(1)}) custom-call(s32[2]{0:T(128)S(1)} %copy-done.4, bf16[256,4,128]{2,1,0:T(4,128)(2,1)S(1)} %copy-done.2), custom_call_target="tpu_custom_call" | custom-call | flops 920000000 | tf_op jit(solution)/shard_map/pallas_call | solution.py:250
  3.7 3.1 %collective-permute-start = (bf16[256,128]{1,0:T(8,128)(2,1)S(1)}, bf16[256,128]{1,0:T(8,128)(2,1)S(1)}, u32[]{:S(2)}, u32[]{:S(2)}) collective-permute-start(bf16[256,128]{1,0:T(8,128)(2,1)S(1)} %get-tuple-element.67), channel_id=1, source_target_pairs={{0,8},{2,10},{4,12},{6,14},{8,0},{10,2},{12,4},{14,6},{16,24},{18,... | collective-permute-start | bytes 196616 | tf_op jit(solution)/shard_map/ppermute | solution.py:243
  6.8 2.6 %collective-permute-start.1 = (bf16[256,128]{1,0:T(8,128)(2,1)S(1)}, bf16[256,128]{1,0:T(8,128)(2,1)S(1)}, u32[]{:S(2)}, u32[]{:S(2)}) collective-permute-start(bf16[256,128]{1,0:T(8,128)(2,1)S(1)} %get-tuple-element.68), channel_id=1, source_target_pairs={{0,16},{2,18},{4,20},{6,22},{8,24},{10,26},{12,28},{14,30},{16,0},... | collective-permute-start | bytes 196616 | tf_op jit(solution)/shard_map/ppermute | solution.py:243
  9.4 0.0 collective-permute-start.2
  9.4 1.2 %shard_map.85 = (bf16[128,256]{1,0:T(8,128)(2,1)S(1)}, bf16[128,256]{1,0:T(8,128)(2,1)S(1)}, bf16[128,256]{1,0:T(8,128)(2,1)S(1)}, bf16[128,256]{1,0:T(8,128)(2,1)S(1)}) custom-call(s32[2]{0:T(128)S(1)} %copy-done.4, bf16[4,64,256]{2,1,0:T(8,128)(2,1)S(1)} %bitcast.2, bf16[4,64,768]{2,1,0:T(8,128)(2,1)S(1)} %copy-done, bf16[256,768]{1,0:T(8,128)(2,1)S(1)} %copy-done.1), custom_call_target="tpu_custom_call" | custom-call | flops 1150000000 | tf_op jit(solution)/shard_map/pallas_call | solution.py:255
  10.7 0.9 %collective-permute-start.3 = (bf16[128,256]{1,0:T(8,128)(2,1)S(1)}, bf16[128,256]{1,0:T(8,128)(2,1)S(1)}, u32[]{:S(2)}, u32[]{:S(2)}) collective-permute-start(bf16[128,256]{1,0:T(8,128)(2,1)S(1)} %get-tuple-element.73), channel_id=1, source_target_pairs={{0,8},{2,10},{4,12},{6,14},{8,0},{10,2},{12,4},{14,6},{16,24},{18,... | collective-permute-start | bytes 196616 | tf_op jit(solution)/shard_map/ppermute | solution.py:243
  11.6 3.5 %collective-permute-start.4 = (bf16[128,256]{1,0:T(8,128)(2,1)S(1)}, bf16[128,256]{1,0:T(8,128)(2,1)S(1)}, u32[]{:S(2)}, u32[]{:S(2)}) collective-permute-start(bf16[128,256]{1,0:T(8,128)(2,1)S(1)} %get-tuple-element.74), channel_id=1, source_target_pairs={{0,16},{2,18},{4,20},{6,22},{8,24},{10,26},{12,28},{14,30},{16,0},... | collective-permute-start | bytes 196616 | tf_op jit(solution)/shard_map/ppermute | solution.py:243
  15.1 0.0 collective-permute-done.refs_1_
  15.1 0.0 collective-permute-start.5
  15.1 0.0 collective-permute-done.1.refs_2_
  15.1 1.0 %collective-permute-done.2.refs_3_ = bf16[256,128]{1,0:T(8,128)(2,1)S(1)} collective-permute-done((bf16[256,128]{1,0:T(8,128)(2,1)S(1)}, bf16[256,128]{1,0:T(8,128)(2,1)S(1)}, u32[]{:S(2)}, u32[]{:S(2)}) %collective-permute-start.2) | collective-permute-done | bytes 65568 | tf_op jit(solution)/shard_map/ppermute | solution.py:243
  16.1 1.6 %collective-permute-start.7 = (bf16[1024,128]{1,0:T(8,128)(2,1)S(1)}, bf16[1024,128]{1,0:T(8,128)(2,1)S(1)}, u32[]{:S(2)}, u32[]{:S(2)}) collective-permute-start(bf16[1024,128]{1,0:T(8,128)(2,1)S(1)} %shard_map.86.pair_ref), channel_id=1, source_target_pairs={{0,4},{2,6},{4,0},{6,2},{8,12},{10,14},{12,8},{14,10},{16,20},{18,... | collective-permute-start | bytes 786440 | tf_op jit(solution)/shard_map/ppermute | solution.py:243
  17.7 1.9 %collective-permute-done.4.refs_2_ = bf16[128,256]{1,0:T(8,128)(2,1)S(1)} collective-permute-done((bf16[128,256]{1,0:T(8,128)(2,1)S(1)}, bf16[128,256]{1,0:T(8,128)(2,1)S(1)}, u32[]{:S(2)}, u32[]{:S(2)}) %collective-permute-start.4) | collective-permute-done | bytes 65568 | tf_op jit(solution)/shard_map/ppermute | solution.py:243
  19.6 1.6 %collective-permute-done.5.refs_3_ = bf16[128,256]{1,0:T(8,128)(2,1)S(1)} collective-permute-done((bf16[128,256]{1,0:T(8,128)(2,1)S(1)}, bf16[128,256]{1,0:T(8,128)(2,1)S(1)}, u32[]{:S(2)}, u32[]{:S(2)}) %collective-permute-start.5) | collective-permute-done | bytes 65568 | tf_op jit(solution)/shard_map/ppermute | solution.py:243
  21.2 0.2 shard_map.87
  21.5 2.0 %shard_map.89 = (bf16[1024,1024]{1,0:T(8,128)(2,1)S(1)}, f32[1,1024]{1,0:T(1,128)S(1)}, f32[80,1024]{1,0:T(8,128)S(1)}) custom-call(bf16[1024,256]{1,0:T(8,128)(2,1)S(1)} %get-tuple-element.71.wide_ref, bf16[80,1024]{1,0:T(8,128)(2,1)S(1)} %get-tuple-element.72.vt_ref, bf16[256,1024]{1,0:T(8,128)(2,1)S(1)} %get-tuple-element.76.qa_ref), custom_call_target="tpu_custom_call" | custom-call | flops 2300000000 | tf_op jit(solution)/shard_map/pallas_call | solution.py:283
  23.5 0.0 collective-permute-done.7.pair_ref
  23.5 0.1 collective-permute-start.8
  23.6 0.2 shard_map.92
  23.8 2.0 %shard_map.93 = (bf16[1024,1024]{1,0:T(8,128)(2,1)S(1)}, f32[1,1024]{1,0:T(1,128)S(1)}, f32[80,1024]{1,0:T(8,128)S(1)}) custom-call(bf16[1024,256]{1,0:T(8,128)(2,1)S(1)} %get-tuple-element.81.wide_ref, bf16[80,1024]{1,0:T(8,128)(2,1)S(1)} %get-tuple-element.82.vt_ref, bf16[256,1024]{1,0:T(8,128)(2,1)S(1)} %get-tuple-element.76.qa_ref), custom_call_target="tpu_custom_call" | custom-call | flops 2300000000 | tf_op jit(solution)/shard_map/pallas_call | solution.py:283
  25.8 0.0 collective-permute-done.6.pair_ref
  25.8 0.2 shard_map.90
  26.1 2.0 %shard_map.91 = (bf16[1024,1024]{1,0:T(8,128)(2,1)S(1)}, f32[1,1024]{1,0:T(1,128)S(1)}, f32[80,1024]{1,0:T(8,128)S(1)}) custom-call(bf16[1024,256]{1,0:T(8,128)(2,1)S(1)} %get-tuple-element.78.wide_ref, bf16[80,1024]{1,0:T(8,128)(2,1)S(1)} %get-tuple-element.79.vt_ref, bf16[256,1024]{1,0:T(8,128)(2,1)S(1)} %get-tuple-element.76.qa_ref), custom_call_target="tpu_custom_call" | custom-call | flops 2300000000 | tf_op jit(solution)/shard_map/pallas_call | solution.py:283
  28.0 0.0 collective-permute-done.8.pair_ref
  28.0 0.2 shard_map.94
  28.3 2.0 %shard_map.95 = (bf16[1024,1024]{1,0:T(8,128)(2,1)S(1)}, f32[1,1024]{1,0:T(1,128)S(1)}, f32[80,1024]{1,0:T(8,128)S(1)}) custom-call(bf16[1024,256]{1,0:T(8,128)(2,1)S(1)} %get-tuple-element.84.wide_ref, bf16[80,1024]{1,0:T(8,128)(2,1)S(1)} %get-tuple-element.85.vt_ref, bf16[256,1024]{1,0:T(8,128)(2,1)S(1)} %get-tuple-element.76.qa_ref), custom_call_target="tpu_custom_call" | custom-call | flops 2300000000 | tf_op jit(solution)/shard_map/pallas_call | solution.py:283
  30.3 0.2 shard_map.96
  30.4 0.2 collective-permute-start.9
  30.6 2.3 %collective-permute-start.10 = (bf16[64,256]{1,0:T(8,128)(2,1)S(1)}, bf16[64,256]{1,0:T(8,128)(2,1)S(1)}, u32[]{:S(2)}, u32[]{:S(2)}) collective-permute-start(bf16[64,256]{1,0:T(8,128)(2,1)S(1)} %get-tuple-element.94), channel_id=1, source_target_pairs={{0,16},{2,18},{4,20},{6,22},{8,24},{10,26},{12,28},{14,30},{16,0},... | collective-permute-start | bytes 98312 | tf_op jit(solution)/shard_map/ppermute | solution.py:243
  33.0 1.9 %collective-permute-start.11 = (bf16[64,256]{1,0:T(8,128)(2,1)S(1)}, bf16[64,256]{1,0:T(8,128)(2,1)S(1)}, u32[]{:S(2)}, u32[]{:S(2)}) collective-permute-start(bf16[64,256]{1,0:T(8,128)(2,1)S(1)} %get-tuple-element.95), channel_id=1, source_target_pairs={{0,24},{2,26},{4,28},{6,30},{8,16},{10,18},{12,20},{14,22},{16,8},... | collective-permute-start | bytes 98312 | tf_op jit(solution)/shard_map/ppermute | solution.py:243
  34.9 2.4 %shard_map.97 = (bf16[1024,128]{1,0:T(8,128)(2,1)S(1)}, f32[64,1024]{1,0:T(8,128)S(1)}) custom-call(bf16[1024,1024]{1,0:T(8,128)(2,1)S(1)} %get-tuple-element.100.exp_ref, bf16[1024,256]{1,0:T(8,128)(2,1)S(1)} %get-tuple-element.84.wide_ref, bf16[64,1024]{1,0:T(8,128)(2,1)S(1)} %get-tuple-element.101.kt_ref, bf16[256,1024]{1,0:T(8,128)(2,1)S(1)} %get-tuple-element.76.qa_ref, ...), custom_call_target="tpu_custom_call" | custom-call | flops 2300000000 | tf_op jit(solution)/shard_map/pallas_call | solution.py:307
  37.3 0.0 copy-start.5
  37.3 2.9 %shard_map.98 = (bf16[1024,128]{1,0:T(8,128)(2,1)S(1)}, f32[64,1024]{1,0:T(8,128)S(1)}) custom-call(bf16[1024,1024]{1,0:T(8,128)(2,1)S(1)} %get-tuple-element.96.exp_ref, bf16[1024,256]{1,0:T(8,128)(2,1)S(1)} %get-tuple-element.78.wide_ref, bf16[64,1024]{1,0:T(8,128)(2,1)S(1)} %get-tuple-element.97.kt_ref, bf16[256,1024]{1,0:T(8,128)(2,1)S(1)} %get-tuple-element.76.qa_ref, ...), custom_call_target="tpu_custom_call" | custom-call | flops 2300000000 | tf_op jit(solution)/shard_map/pallas_call | solution.py:307
  40.3 0.0 collective-permute-done.9.refs_1_
  40.3 0.0 collective-permute-done.11.refs_3_
  40.3 1.4 %shard_map.99 = (bf16[256,768]{1,0:T(8,128)(2,1)S(1)}, bf16[2,64,768]{2,1,0:T(8,128)(2,1)S(1)}, bf16[2,64,768]{2,1,0:T(8,128)(2,1)S(1)}) custom-call(s32[2]{0:T(128)S(1)} %copy-done.5, bf16[4,64,768]{2,1,0:T(8,128)(2,1)S(1)} %copy-done, bf16[256,768]{1,0:T(8,128)(2,1)S(1)} %copy-done.1, bf16[64,256]{1,0:T(8,128)(2,1)S(1)} %get-tuple-element.92.refs_0_, ...), custom_call_target="tpu_custom_call" | custom-call | flops 1150000000 | tf_op jit(solution)/shard_map/pallas_call | solution.py:299
  41.7 0.1 collective-permute-start.19
  41.8 1.4 %collective-permute-done.19.came_ref = bf16[2,64,768]{2,1,0:T(8,128)(2,1)S(1)} collective-permute-done((bf16[2,64,768]{2,1,0:T(8,128)(2,1)S(1)}, bf16[2,64,768]{2,1,0:T(8,128)(2,1)S(1)}, u32[]{:S(2)}, u32[]{:S(2)}) %collective-permute-start.19) | collective-permute-done | bytes 196640 | tf_op jit(solution)/shard_map/ppermute | solution.py:243
  43.3 1.6 %collective-permute-start.20 = (bf16[64,768]{1,0:T(8,128)(2,1)S(1)}, bf16[64,768]{1,0:T(8,128)(2,1)S(1)}, u32[]{:S(2)}, u32[]{:S(2)}) collective-permute-start(bf16[64,768]{1,0:T(8,128)(2,1)S(1)} %get-tuple-element.127), channel_id=1, source_target_pairs={{0,4},{2,6},{4,0},{6,2},{8,12},{10,14},{12,8},{14,10},{16,20},{18,... | collective-permute-start | bytes 294920 | tf_op jit(solution)/shard_map/ppermute | solution.py:243
  44.9 0.5 collective-permute-start.13
  45.4 1.5 %collective-permute-start.12 = (bf16[256,768]{1,0:T(8,128)(2,1)S(1)}, bf16[256,768]{1,0:T(8,128)(2,1)S(1)}, u32[]{:S(2)}, u32[]{:S(2)}) collective-permute-start(bf16[256,768]{1,0:T(8,128)(2,1)S(1)} %get-tuple-element.105.a_ref.refs_1_), channel_id=1, source_target_pairs={{0,1},{1,0},{2,3},{3,2},{4,5},{5,4},{6,7},{7,6},{8,9},{9,8},{10,11... | collective-permute-start | bytes 1179656 | tf_op jit(solution)/shard_map/ppermute | solution.py:243
  46.9 1.3 %collective-permute-done.20.b_ref = bf16[64,768]{1,0:T(8,128)(2,1)S(1)} collective-permute-done((bf16[64,768]{1,0:T(8,128)(2,1)S(1)}, bf16[64,768]{1,0:T(8,128)(2,1)S(1)}, u32[]{:S(2)}, u32[]{:S(2)}) %collective-permute-start.20) | collective-permute-done | bytes 98336 | tf_op jit(solution)/shard_map/ppermute | solution.py:243
  48.2 0.1 collective-permute-start.21
  48.3 2.8 %shard_map.101 = (bf16[1024,128]{1,0:T(8,128)(2,1)S(1)}, f32[64,1024]{1,0:T(8,128)S(1)}) custom-call(bf16[1024,1024]{1,0:T(8,128)(2,1)S(1)} %get-tuple-element.109.exp_ref, bf16[1024,256]{1,0:T(8,128)(2,1)S(1)} %get-tuple-element.81.wide_ref, bf16[64,1024]{1,0:T(8,128)(2,1)S(1)} %get-tuple-element.110.kt_ref, ...), custom_call_target="tpu_custom_call" | custom-call | flops 2300000000 | tf_op jit(solution)/shard_map/pallas_call | solution.py:307
  51.1 0.1 shard_map.104
  51.1 1.6 %collective-permute-start.15 = (bf16[1024,128]{1,0:T(8,128)(2,1)S(1)}, bf16[1024,128]{1,0:T(8,128)(2,1)S(1)}, u32[]{:S(2)}, u32[]{:S(2)}) collective-permute-start(bf16[1024,128]{1,0:T(8,128)(2,1)S(1)} %shard_map.104), channel_id=1, source_target_pairs={{0,4},{2,6},{4,0},{6,2},{8,12},{10,14},{12,8},{14,10},{16,20},{18,... | collective-permute-start | bytes 786440 | tf_op jit(solution)/shard_map/ppermute | solution.py:243
  52.7 0.2 collective-permute-done.21.b_ref
  52.9 2.3 %collective-permute-start.22 = (bf16[64,768]{1,0:T(8,128)(2,1)S(1)}, bf16[64,768]{1,0:T(8,128)(2,1)S(1)}, u32[]{:S(2)}, u32[]{:S(2)}) collective-permute-start(bf16[64,768]{1,0:T(8,128)(2,1)S(1)} %shard_map.109.a_ref), channel_id=1, source_target_pairs={{0,16},{2,18},{4,20},{6,22},{8,24},{10,26},{12,28},{14,30},{16,0},... | collective-permute-start | bytes 294920 | tf_op jit(solution)/shard_map/ppermute | solution.py:243
  55.2 2.8 %shard_map.102 = (bf16[1024,128]{1,0:T(8,128)(2,1)S(1)}, f32[64,1024]{1,0:T(8,128)S(1)}) custom-call(bf16[1024,1024]{1,0:T(8,128)(2,1)S(1)} %get-tuple-element.106.exp_ref, bf16[1024,256]{1,0:T(8,128)(2,1)S(1)} %get-tuple-element.71.wide_ref, bf16[64,1024]{1,0:T(8,128)(2,1)S(1)} %get-tuple-element.107.kt_ref, ...), custom_call_target="tpu_custom_call" | custom-call | flops 2300000000 | tf_op jit(solution)/shard_map/pallas_call | solution.py:307
  58.0 0.0 collective-permute-done.13.b_ref
  58.0 0.1 shard_map.103.kept_ref
  58.1 0.6 collective-permute-done.15.came_ref
  58.7 0.1 shard_map.105
  58.8 1.8 %collective-permute-start.16 = (bf16[384,128]{1,0:T(8,128)(2,1)S(1)}, bf16[384,128]{1,0:T(8,128)(2,1)S(1)}, u32[]{:S(2)}, u32[]{:S(2)}) collective-permute-start(bf16[384,128]{1,0:T(8,128)(2,1)S(1)} %get-tuple-element.119), channel_id=1, source_target_pairs={{0,8},{2,10},{4,12},{6,14},{8,0},{10,2},{12,4},{14,6},{16,24},{18,... | collective-permute-start | bytes 294920 | tf_op jit(solution)/shard_map/ppermute | solution.py:243
  60.6 1.6 %collective-permute-start.24 = (bf16[64,768]{1,0:T(8,128)(2,1)S(1)}, bf16[64,768]{1,0:T(8,128)(2,1)S(1)}, u32[]{:S(2)}, u32[]{:S(2)}) collective-permute-start(bf16[64,768]{1,0:T(8,128)(2,1)S(1)} %shard_map.110.refs_0_), channel_id=1, source_target_pairs={{0,4},{2,6},{4,0},{6,2},{8,12},{10,14},{12,8},{14,10},{16,20},{18,... | collective-permute-start | bytes 294920 | tf_op jit(solution)/shard_map/ppermute | solution.py:243
  62.2 1.3 %collective-permute-start.17 = (bf16[384,128]{1,0:T(8,128)(2,1)S(1)}, bf16[384,128]{1,0:T(8,128)(2,1)S(1)}, u32[]{:S(2)}, u32[]{:S(2)}) collective-permute-start(bf16[384,128]{1,0:T(8,128)(2,1)S(1)} %get-tuple-element.120), channel_id=1, source_target_pairs={{0,16},{2,18},{4,20},{6,22},{8,24},{10,26},{12,28},{14,30},{16,0},... | collective-permute-start | bytes 294920 | tf_op jit(solution)/shard_map/ppermute | solution.py:243
  63.5 1.3 %collective-permute-start.18 = (bf16[384,128]{1,0:T(8,128)(2,1)S(1)}, bf16[384,128]{1,0:T(8,128)(2,1)S(1)}, u32[]{:S(2)}, u32[]{:S(2)}) collective-permute-start(bf16[384,128]{1,0:T(8,128)(2,1)S(1)} %get-tuple-element.121), channel_id=1, source_target_pairs={{0,24},{2,26},{4,28},{6,30},{8,16},{10,18},{12,20},{14,22},{16,8},... | collective-permute-start | bytes 294920 | tf_op jit(solution)/shard_map/ppermute | solution.py:243
  64.9 0.8 %shard_map.100 = bf16[256,768]{1,0:T(8,128)(2,1)} custom-call(bf16[256,768]{1,0:T(8,128)(2,1)S(1)} %get-tuple-element.105.a_ref.refs_1_, bf16[256,768]{1,0:T(8,128)(2,1)S(1)} %collective-permute-done.12.b_ref), custom_call_target="tpu_custom_call" | custom-call | flops 345000000 | tf_op jit(solution)/shard_map/pallas_call | solution.py:315
  65.7 0.5 collective-permute-start.25
  66.2 4.4 %collective-permute-done.17.refs_2_ = bf16[384,128]{1,0:T(8,128)(2,1)S(1)} collective-permute-done((bf16[384,128]{1,0:T(8,128)(2,1)S(1)}, bf16[384,128]{1,0:T(8,128)(2,1)S(1)}, u32[]{:S(2)}, u32[]{:S(2)}) %collective-permute-start.17) | collective-permute-done | bytes 98336 | tf_op jit(solution)/shard_map/ppermute | solution.py:243
  70.6 1.1 %shard_map.106 = (f32[256,4,128]{2,1,0:T(4,128)}, f32[4,64,256]{2,1,0:T(8,128)}) custom-call(bf16[384,128]{1,0:T(8,128)(2,1)S(1)} %get-tuple-element.118.refs_0_, bf16[384,128]{1,0:T(8,128)(2,1)S(1)} %collective-permute-done.16.refs_1_, bf16[384,128]{1,0:T(8,128)(2,1)S(1)} %collective-permute-done.17.refs_2_, ...), custom_call_target="tpu_custom_call" | custom-call | flops 1150000000 | tf_op jit(solution)/shard_map/pallas_call | solution.py:344
  71.8 0.9 %shard_map.111 = f32[4,64,768]{2,1,0:T(8,128)} custom-call(bf16[64,768]{1,0:T(8,128)(2,1)S(1)} %shard_map.110.refs_0_, bf16[64,768]{1,0:T(8,128)(2,1)S(1)} %collective-permute-done.23.refs_1_, bf16[64,768]{1,0:T(8,128)(2,1)S(1)} %collective-permute-done.24.refs_2_, bf16[64,768]{1,0:T(8,128)(2,1)S(1)} %collective-permute-done.25.refs_3_), custom_call_target="tpu_custom_call" | custom-call | flops 575000000 | tf_op jit(solution)/shard_map/pallas_call | solution.py:328
  (28 shorter events, 0.2 us)
Async XLA Ops:
  0.6 8.8 %copy-start.1 = (bf16[256,768]{1,0:T(8,128)(2,1)S(1)}, bf16[256,768]{1,0:T(8,128)(2,1)}, u32[]{:S(2)}) copy-start(bf16[256,768]{1,0:T(8,128)(2,1)} %go_ref.3) | copy-start | bytes 1179652
  0.6 8.8 %copy-start = (bf16[4,64,768]{2,1,0:T(8,128)(2,1)S(1)}, bf16[4,64,768]{2,1,0:T(8,128)(2,1)}, u32[]{:S(2)}) copy-start(bf16[4,64,768]{2,1,0:T(8,128)(2,1)} %w_ref.3) | copy-start | bytes 1179652
  0.7 1.0 %copy-start.2 = (bf16[256,4,128]{2,1,0:T(4,128)(2,1)S(1)}, bf16[256,4,128]{2,1,0:T(4,128)(2,1)}, u32[]{:S(2)}) copy-start(bf16[256,4,128]{2,1,0:T(4,128)(2,1)} %kv_ref.1) | copy-start | bytes 786436
  1.7 0.7 copy-start.4
  2.3 7.1 %copy-start.3 = (bf16[256,4,64]{0,2,1:T(8,128)(2,1)S(1)}, bf16[256,4,64]{0,2,1:T(8,128)(2,1)}, u32[]{:S(2)}) copy-start(bf16[256,4,64]{0,2,1:T(8,128)(2,1)} %param.5) | copy-start | bytes 393220
  3.7 11.4 %collective-permute-start = (bf16[256,128]{1,0:T(8,128)(2,1)S(1)}, bf16[256,128]{1,0:T(8,128)(2,1)S(1)}, u32[]{:S(2)}, u32[]{:S(2)}) collective-permute-start(bf16[256,128]{1,0:T(8,128)(2,1)S(1)} %get-tuple-element.67), channel_id=1, source_target_pairs={{0,8},{2,10},{4,12},{6,14},{8,0},{10,2},{12,4},{14,6},{16,24},{18,... | collective-permute-start | bytes 196616 | tf_op jit(solution)/shard_map/ppermute | solution.py:243
  6.8 8.3 %collective-permute-start.1 = (bf16[256,128]{1,0:T(8,128)(2,1)S(1)}, bf16[256,128]{1,0:T(8,128)(2,1)S(1)}, u32[]{:S(2)}, u32[]{:S(2)}) collective-permute-start(bf16[256,128]{1,0:T(8,128)(2,1)S(1)} %get-tuple-element.68), channel_id=1, source_target_pairs={{0,16},{2,18},{4,20},{6,22},{8,24},{10,26},{12,28},{14,30},{16,0},... | collective-permute-start | bytes 196616 | tf_op jit(solution)/shard_map/ppermute | solution.py:243
  9.4 6.7 %collective-permute-start.2 = (bf16[256,128]{1,0:T(8,128)(2,1)S(1)}, bf16[256,128]{1,0:T(8,128)(2,1)S(1)}, u32[]{:S(2)}, u32[]{:S(2)}) collective-permute-start(bf16[256,128]{1,0:T(8,128)(2,1)S(1)} %get-tuple-element.69), channel_id=1, source_target_pairs={{0,24},{2,26},{4,28},{6,30},{8,16},{10,18},{12,20},{14,22},{16,8},... | collective-permute-start | bytes 196616 | tf_op jit(solution)/shard_map/ppermute | solution.py:243
  10.7 7.0 %collective-permute-start.3 = (bf16[128,256]{1,0:T(8,128)(2,1)S(1)}, bf16[128,256]{1,0:T(8,128)(2,1)S(1)}, u32[]{:S(2)}, u32[]{:S(2)}) collective-permute-start(bf16[128,256]{1,0:T(8,128)(2,1)S(1)} %get-tuple-element.73), channel_id=1, source_target_pairs={{0,8},{2,10},{4,12},{6,14},{8,0},{10,2},{12,4},{14,6},{16,24},{18,... | collective-permute-start | bytes 196616 | tf_op jit(solution)/shard_map/ppermute | solution.py:243
  11.6 8.0 %collective-permute-start.4 = (bf16[128,256]{1,0:T(8,128)(2,1)S(1)}, bf16[128,256]{1,0:T(8,128)(2,1)S(1)}, u32[]{:S(2)}, u32[]{:S(2)}) collective-permute-start(bf16[128,256]{1,0:T(8,128)(2,1)S(1)} %get-tuple-element.74), channel_id=1, source_target_pairs={{0,16},{2,18},{4,20},{6,22},{8,24},{10,26},{12,28},{14,30},{16,0},... | collective-permute-start | bytes 196616 | tf_op jit(solution)/shard_map/ppermute | solution.py:243
  15.1 6.1 %collective-permute-start.5 = (bf16[128,256]{1,0:T(8,128)(2,1)S(1)}, bf16[128,256]{1,0:T(8,128)(2,1)S(1)}, u32[]{:S(2)}, u32[]{:S(2)}) collective-permute-start(bf16[128,256]{1,0:T(8,128)(2,1)S(1)} %get-tuple-element.75), channel_id=1, source_target_pairs={{0,24},{2,26},{4,28},{6,30},{8,16},{10,18},{12,20},{14,22},{16,8},... | collective-permute-start | bytes 196616 | tf_op jit(solution)/shard_map/ppermute | solution.py:243
  16.1 7.4 %collective-permute-start.7 = (bf16[1024,128]{1,0:T(8,128)(2,1)S(1)}, bf16[1024,128]{1,0:T(8,128)(2,1)S(1)}, u32[]{:S(2)}, u32[]{:S(2)}) collective-permute-start(bf16[1024,128]{1,0:T(8,128)(2,1)S(1)} %shard_map.86.pair_ref), channel_id=1, source_target_pairs={{0,4},{2,6},{4,0},{6,2},{8,12},{10,14},{12,8},{14,10},{16,20},{18,... | collective-permute-start | bytes 786440 | tf_op jit(solution)/shard_map/ppermute | solution.py:243
  17.7 8.1 %collective-permute-start.6 = (bf16[1024,128]{1,0:T(8,128)(2,1)S(1)}, bf16[1024,128]{1,0:T(8,128)(2,1)S(1)}, u32[]{:S(2)}, u32[]{:S(2)}) collective-permute-start(bf16[1024,128]{1,0:T(8,128)(2,1)S(1)} %shard_map.86.pair_ref), channel_id=1, source_target_pairs={{0,2},{2,0},{4,6},{6,4},{8,10},{10,8},{12,14},{14,12},{16,18},{18,... | collective-permute-start | bytes 786440 | tf_op jit(solution)/shard_map/ppermute | solution.py:243
  23.5 4.5 %collective-permute-start.8 = (bf16[1024,128]{1,0:T(8,128)(2,1)S(1)}, bf16[1024,128]{1,0:T(8,128)(2,1)S(1)}, u32[]{:S(2)}, u32[]{:S(2)}) collective-permute-start(bf16[1024,128]{1,0:T(8,128)(2,1)S(1)} %collective-permute-done.7.pair_ref), channel_id=1, source_target_pairs={{0,2},{2,0},{4,6},{6,4},{8,10},{10,8},{12,14},{14,12},{16,18},{18,... | collective-permute-start | bytes 786440 | tf_op jit(solution)/shard_map/ppermute | solution.py:243
  30.4 9.8 %collective-permute-start.9 = (bf16[64,256]{1,0:T(8,128)(2,1)S(1)}, bf16[64,256]{1,0:T(8,128)(2,1)S(1)}, u32[]{:S(2)}, u32[]{:S(2)}) collective-permute-start(bf16[64,256]{1,0:T(8,128)(2,1)S(1)} %get-tuple-element.93), channel_id=1, source_target_pairs={{0,8},{2,10},{4,12},{6,14},{8,0},{10,2},{12,4},{14,6},{16,24},{18,... | collective-permute-start | bytes 98312 | tf_op jit(solution)/shard_map/ppermute | solution.py:243
  30.6 9.6 %collective-permute-start.10 = (bf16[64,256]{1,0:T(8,128)(2,1)S(1)}, bf16[64,256]{1,0:T(8,128)(2,1)S(1)}, u32[]{:S(2)}, u32[]{:S(2)}) collective-permute-start(bf16[64,256]{1,0:T(8,128)(2,1)S(1)} %get-tuple-element.94), channel_id=1, source_target_pairs={{0,16},{2,18},{4,20},{6,22},{8,24},{10,26},{12,28},{14,30},{16,0},... | collective-permute-start | bytes 98312 | tf_op jit(solution)/shard_map/ppermute | solution.py:243
  33.0 7.3 %collective-permute-start.11 = (bf16[64,256]{1,0:T(8,128)(2,1)S(1)}, bf16[64,256]{1,0:T(8,128)(2,1)S(1)}, u32[]{:S(2)}, u32[]{:S(2)}) collective-permute-start(bf16[64,256]{1,0:T(8,128)(2,1)S(1)} %get-tuple-element.95), channel_id=1, source_target_pairs={{0,24},{2,26},{4,28},{6,30},{8,16},{10,18},{12,20},{14,22},{16,8},... | collective-permute-start | bytes 98312 | tf_op jit(solution)/shard_map/ppermute | solution.py:243
  37.3 3.0 %copy-start.5 = (s32[2]{0:T(128)S(1)}, s32[2]{0:T(128)}, u32[]{:S(2)}) copy-start(s32[2]{0:T(128)} %fill_ref.5) | copy-start | bytes 28
  41.7 1.5 %collective-permute-start.19 = (bf16[2,64,768]{2,1,0:T(8,128)(2,1)S(1)}, bf16[2,64,768]{2,1,0:T(8,128)(2,1)S(1)}, u32[]{:S(2)}, u32[]{:S(2)}) collective-permute-start(bf16[2,64,768]{2,1,0:T(8,128)(2,1)S(1)} %get-tuple-element.125), channel_id=1, source_target_pairs={{0,2},{2,0},{4,6},{6,4},{8,10},{10,8},{12,14},{14,12},{16,18},{18,... | collective-permute-start | bytes 589832 | tf_op jit(solution)/shard_map/ppermute | solution.py:243
  43.3 4.9 %collective-permute-start.20 = (bf16[64,768]{1,0:T(8,128)(2,1)S(1)}, bf16[64,768]{1,0:T(8,128)(2,1)S(1)}, u32[]{:S(2)}, u32[]{:S(2)}) collective-permute-start(bf16[64,768]{1,0:T(8,128)(2,1)S(1)} %get-tuple-element.127), channel_id=1, source_target_pairs={{0,4},{2,6},{4,0},{6,2},{8,12},{10,14},{12,8},{14,10},{16,20},{18,... | collective-permute-start | bytes 294920 | tf_op jit(solution)/shard_map/ppermute | solution.py:243
  44.9 6.2 %collective-permute-start.14 = (bf16[1024,128]{1,0:T(8,128)(2,1)S(1)}, bf16[1024,128]{1,0:T(8,128)(2,1)S(1)}, u32[]{:S(2)}, u32[]{:S(2)}) collective-permute-start(bf16[1024,128]{1,0:T(8,128)(2,1)S(1)} %get-tuple-element.116), channel_id=1, source_target_pairs={{0,2},{2,0},{4,6},{6,4},{8,10},{10,8},{12,14},{14,12},{16,18},{18,... | collective-permute-start | bytes 786440 | tf_op jit(solution)/shard_map/ppermute | solution.py:243
  44.9 13.2 %collective-permute-start.13 = (bf16[1024,128]{1,0:T(8,128)(2,1)S(1)}, bf16[1024,128]{1,0:T(8,128)(2,1)S(1)}, u32[]{:S(2)}, u32[]{:S(2)}) collective-permute-start(bf16[1024,128]{1,0:T(8,128)(2,1)S(1)} %get-tuple-element.104.refs_4_), channel_id=1, source_target_pairs={{0,2},{2,0},{4,6},{6,4},{8,10},{10,8},{12,14},{14,12},{16,18},{18,... | collective-permute-start | bytes 786440 | tf_op jit(solution)/shard_map/ppermute | solution.py:243
  45.4 19.5 %collective-permute-start.12 = (bf16[256,768]{1,0:T(8,128)(2,1)S(1)}, bf16[256,768]{1,0:T(8,128)(2,1)S(1)}, u32[]{:S(2)}, u32[]{:S(2)}) collective-permute-start(bf16[256,768]{1,0:T(8,128)(2,1)S(1)} %get-tuple-element.105.a_ref.refs_1_), channel_id=1, source_target_pairs={{0,1},{1,0},{2,3},{3,2},{4,5},{5,4},{6,7},{7,6},{8,9},{9,8},{10,11... | collective-permute-start | bytes 1179656 | tf_op jit(solution)/shard_map/ppermute | solution.py:243
  48.2 4.7 %collective-permute-start.21 = (bf16[64,768]{1,0:T(8,128)(2,1)S(1)}, bf16[64,768]{1,0:T(8,128)(2,1)S(1)}, u32[]{:S(2)}, u32[]{:S(2)}) collective-permute-start(bf16[64,768]{1,0:T(8,128)(2,1)S(1)} %shard_map.108.a_ref), channel_id=1, source_target_pairs={{0,8},{2,10},{4,12},{6,14},{8,0},{10,2},{12,4},{14,6},{16,24},{18,... | collective-permute-start | bytes 294920 | tf_op jit(solution)/shard_map/ppermute | solution.py:243
  51.1 7.6 %collective-permute-start.15 = (bf16[1024,128]{1,0:T(8,128)(2,1)S(1)}, bf16[1024,128]{1,0:T(8,128)(2,1)S(1)}, u32[]{:S(2)}, u32[]{:S(2)}) collective-permute-start(bf16[1024,128]{1,0:T(8,128)(2,1)S(1)} %shard_map.104), channel_id=1, source_target_pairs={{0,4},{2,6},{4,0},{6,2},{8,12},{10,14},{12,8},{14,10},{16,20},{18,... | collective-permute-start | bytes 786440 | tf_op jit(solution)/shard_map/ppermute | solution.py:243
  52.9 7.7 %collective-permute-start.22 = (bf16[64,768]{1,0:T(8,128)(2,1)S(1)}, bf16[64,768]{1,0:T(8,128)(2,1)S(1)}, u32[]{:S(2)}, u32[]{:S(2)}) collective-permute-start(bf16[64,768]{1,0:T(8,128)(2,1)S(1)} %shard_map.109.a_ref), channel_id=1, source_target_pairs={{0,16},{2,18},{4,20},{6,22},{8,24},{10,26},{12,28},{14,30},{16,0},... | collective-permute-start | bytes 294920 | tf_op jit(solution)/shard_map/ppermute | solution.py:243
  58.8 7.4 %collective-permute-start.16 = (bf16[384,128]{1,0:T(8,128)(2,1)S(1)}, bf16[384,128]{1,0:T(8,128)(2,1)S(1)}, u32[]{:S(2)}, u32[]{:S(2)}) collective-permute-start(bf16[384,128]{1,0:T(8,128)(2,1)S(1)} %get-tuple-element.119), channel_id=1, source_target_pairs={{0,8},{2,10},{4,12},{6,14},{8,0},{10,2},{12,4},{14,6},{16,24},{18,... | collective-permute-start | bytes 294920 | tf_op jit(solution)/shard_map/ppermute | solution.py:243
  60.6 5.1 %collective-permute-start.24 = (bf16[64,768]{1,0:T(8,128)(2,1)S(1)}, bf16[64,768]{1,0:T(8,128)(2,1)S(1)}, u32[]{:S(2)}, u32[]{:S(2)}) collective-permute-start(bf16[64,768]{1,0:T(8,128)(2,1)S(1)} %shard_map.110.refs_0_), channel_id=1, source_target_pairs={{0,4},{2,6},{4,0},{6,2},{8,12},{10,14},{12,8},{14,10},{16,20},{18,... | collective-permute-start | bytes 294920 | tf_op jit(solution)/shard_map/ppermute | solution.py:243
  62.2 8.4 %collective-permute-start.17 = (bf16[384,128]{1,0:T(8,128)(2,1)S(1)}, bf16[384,128]{1,0:T(8,128)(2,1)S(1)}, u32[]{:S(2)}, u32[]{:S(2)}) collective-permute-start(bf16[384,128]{1,0:T(8,128)(2,1)S(1)} %get-tuple-element.120), channel_id=1, source_target_pairs={{0,16},{2,18},{4,20},{6,22},{8,24},{10,26},{12,28},{14,30},{16,0},... | collective-permute-start | bytes 294920 | tf_op jit(solution)/shard_map/ppermute | solution.py:243
  63.5 7.1 %collective-permute-start.18 = (bf16[384,128]{1,0:T(8,128)(2,1)S(1)}, bf16[384,128]{1,0:T(8,128)(2,1)S(1)}, u32[]{:S(2)}, u32[]{:S(2)}) collective-permute-start(bf16[384,128]{1,0:T(8,128)(2,1)S(1)} %get-tuple-element.121), channel_id=1, source_target_pairs={{0,24},{2,26},{4,28},{6,30},{8,16},{10,18},{12,20},{14,22},{16,8},... | collective-permute-start | bytes 294920 | tf_op jit(solution)/shard_map/ppermute | solution.py:243
  65.7 6.1 %collective-permute-start.23 = (bf16[64,768]{1,0:T(8,128)(2,1)S(1)}, bf16[64,768]{1,0:T(8,128)(2,1)S(1)}, u32[]{:S(2)}, u32[]{:S(2)}) collective-permute-start(bf16[64,768]{1,0:T(8,128)(2,1)S(1)} %shard_map.110.refs_0_), channel_id=1, source_target_pairs={{0,2},{2,0},{4,6},{6,4},{8,10},{10,8},{12,14},{14,12},{16,18},{18,... | collective-permute-start | bytes 294920 | tf_op jit(solution)/shard_map/ppermute | solution.py:243
  65.7 6.1 %collective-permute-start.25 = (bf16[64,768]{1,0:T(8,128)(2,1)S(1)}, bf16[64,768]{1,0:T(8,128)(2,1)S(1)}, u32[]{:S(2)}, u32[]{:S(2)}) collective-permute-start(bf16[64,768]{1,0:T(8,128)(2,1)S(1)} %collective-permute-done.24.refs_2_), channel_id=1, source_target_pairs={{0,2},{2,0},{4,6},{6,4},{8,10},{10,8},{12,14},{14,12},{16,18},{18,... | collective-permute-start | bytes 294920 | tf_op jit(solution)/shard_map/ppermute | solution.py:243

commit v5 on v4

--- a/solution.py
+++ b/solution.py
@@ -13,6 +13,7 @@
 F32 = jnp.float32
 BF16 = jnp.bfloat16
 VMEM = pl.BlockSpec(memory_space=pltpu.VMEM)
+HBM = pl.BlockSpec(memory_space=pltpu.HBM)
 SMEM = pl.BlockSpec(memory_space=pltpu.SMEM)
 MIB = 1024 * 1024
 
@@ -25,8 +26,9 @@
     return lax.dot_general(a, b, (((1,), (1,)), ((), ())), preferred_element_type=F32)
 
 
-def call(kernel, outs, scratch=(), n_in=1, smem_first=False, after=0, micros=0.3, limit=16):
-    specs = [SMEM if smem_first else VMEM] + [VMEM] * (n_in - 1) + [pl.BlockSpec(memory_space=pl.ANY)] * after
+def call(kernel, outs, scratch=(), n_in=1, smem_first=False, far=False, after=0, micros=0.3, limit=16):
+    specs = [SMEM if smem_first else VMEM] + [HBM if far else VMEM] * (n_in - 1)
+    specs += [pl.BlockSpec(memory_space=pl.ANY)] * after
     return pl.pallas_call(
         kernel,
         out_shape=[jax.ShapeDtypeStruct(shape, kind) for shape, kind in outs],
@@ -46,47 +48,57 @@
     return jnp.concatenate(parts, axis=0) if len(parts) > 1 else parts[0]
 
 
-def pack_kv_kernel(heads, rows, dim, a_of, fill_ref, kv_ref, *refs):
-    outs, (held,) = refs[:heads], refs[heads:]
+def pack_kernel(heads, rows, dim, a_of, fill_ref, q_hbm, kv_hbm, *refs):
+    outs, (held, q_ref, kv_ref, q_sem, kv_sem) = refs[:heads], refs[heads:]
+    q_copy = pltpu.make_async_copy(q_hbm, q_ref, q_sem)
+    kv_copy = pltpu.make_async_copy(kv_hbm, kv_ref, kv_sem)
+    kv_copy.start()
+    q_copy.start()
+    wide = 2 * dim
     live = live_column(fill_ref, rows)
-    lane = lax.broadcasted_iota(jnp.int32, (rows, 2 * dim), 1)
+    lane = lax.broadcasted_iota(jnp.int32, (rows, wide), 1)
     mark = jnp.where(lane == 0, DEAD, 0.0)
+    kv_copy.wait()
     for head in range(heads):
-        held[head] = jnp.where(live > 0, kv_ref[:, head, :].astype(F32), mark).astype(BF16)
+        held[head, 0:rows, :] = jnp.where(live > 0, kv_ref[:, head, :].astype(F32), mark).astype(BF16)
+    q_copy.wait()
+    for head in range(heads):
+        scaled = (q_ref[head].astype(F32) * dim**-0.5).astype(BF16)
+        for part in range(rows // wide):
+            start = rows + part * dim
+            held[head, start : start + dim, :] = scaled[:, part * wide : (part + 1) * wide]
     me = a_of()
     for slot in range(heads):
         outs[slot][...] = held[me ^ slot]
 
 
-def pack_qg_kernel(heads, rows, dim, a_of, fill_ref, q_ref, w_ref, go_ref, *refs):
+def pack_grad_kernel(heads, rows, dim, a_of, fill_ref, w_ref, go_ref, *refs):
     outs, (held,) = refs[:heads], refs[heads:]
     live = live_column(fill_ref, rows)
     mixed = jnp.where(live > 0, go_ref[...].astype(F32), 0.0).astype(BF16)
     for head in range(heads):
-        held[head, 0:dim, :] = (q_ref[head].astype(F32) * dim**-0.5).astype(BF16)
-        held[head, dim:, :] = dot_nt(w_ref[head], mixed).astype(BF16)
+        held[head] = dot_nt(w_ref[head], mixed).astype(BF16)
     me = a_of()
     for slot in range(heads):
         outs[slot][...] = held[me ^ slot]
 
 
-def join_kernel(pieces, *refs):
+def join_kernel(pieces, rows, *refs):
     out_ref = refs[-1]
-    rows = refs[0].shape[0]
     for index in range(pieces):
-        out_ref[index * rows : (index + 1) * rows, :] = refs[index][...]
+        out_ref[index * rows : (index + 1) * rows, :] = refs[index][0:rows, :]
 
 
 def join_q_kernel(slots, rows, dim, *refs):
-    pieces, (qa_ref, g_ref) = refs[:slots], refs[slots:]
+    pieces, (qa_ref,) = refs[:slots], refs[slots:]
     wide = 2 * dim
     row = lax.broadcasted_iota(jnp.int32, (wide, slots * rows), 0)
     qa_ref[dim:wide, :] = jnp.zeros((dim, slots * rows), BF16)
     qa_ref[wide:, :] = jnp.where(row == 0, 1.0, 0.0).astype(BF16)
     for slot in range(slots):
-        here = slice(slot * rows, (slot + 1) * rows)
-        qa_ref[0:dim, here] = pieces[slot][0:dim, :]
-        g_ref[:, here] = pieces[slot][dim:, :]
+        for part in range(rows // wide):
+            start, across = rows + part * dim, slot * rows + part * wide
+            qa_ref[0:dim, across : across + wide] = pieces[slot][start : start + dim, :]
 
 
 def prep_kernel(dim, pair_ref, wide_ref, kt_ref, vt_ref):
@@ -130,8 +142,9 @@
 
 
 def combine_kernel(slots, columns, rows, dim, *refs):
-    peaks, totals, (g_ref,), outs = refs[:columns], refs[columns : 2 * columns], refs[2 * columns : 2 * columns + 1], refs[2 * columns + 1 :]
-    att_out, factors_out, inner_ref = outs[:slots], outs[slots : slots + columns], outs[-1]
+    peaks, totals, refs = refs[:columns], refs[columns : 2 * columns], refs[2 * columns :]
+    grads, outs = refs[:slots], refs[slots:]
+    att_out, factors_out, (inner_ref, g_ref) = outs[:slots], outs[slots : slots + columns], outs[slots + columns :]
     peak = functools.reduce(jnp.maximum, [ref[...] for ref in peaks])
     factors = [jnp.exp(ref[...] - peak) for ref in peaks]
     total = sum(factor * ref[...] for factor, ref in zip(factors, totals))
@@ -139,6 +152,7 @@
     attended = (total[0:dim, :] * inverse).astype(BF16)
     for slot in range(slots):
         att_out[slot][...] = attended[:, slot * rows : (slot + 1) * rows]
+        g_ref[:, slot * rows : (slot + 1) * rows] = grads[slot][...]
     for factor, ref in zip(factors, factors_out):
         ref[...] = factor * inverse
     inner_ref[...] = jnp.sum(g_ref[...].astype(F32) * attended.astype(F32), axis=0, keepdims=True)
@@ -156,11 +170,16 @@
     row = lax.broadcasted_iota(jnp.int32, (wide, g_ref.shape[1]), 0)
     ga_ref[wide:, :] = jnp.where(row == 1, -high, jnp.where(row == 2, high - inner, 0.0)).astype(BF16)
     total = None if first else refs[0][...]
+    ahead = dot(wide_ref[0:step, :], ga_ref[...])
     for start in range(0, keys, step):
         part = slice(start, start + step)
+        products = ahead
+        if start + step < keys:
+            ahead = dot(wide_ref[start + step : start + 2 * step, :], ga_ref[...])
         exps = exp_ref[part, :]
-        grads = (exps.astype(F32) * dot(wide_ref[part, :], ga_ref[...])).astype(BF16)
-        dkv_ref[part, :] = (dot_nt(exps, ga_ref[0:wide, :]) + dot_nt(grads, qa_ref[0:wide, :])).astype(BF16)
+        grads = (exps.astype(F32) * products).astype(BF16)
+        dkv_ref[dim:, part] = dot_nt(ga_ref[dim:wide, :], exps).astype(BF16)
+        dkv_ref[0:dim, part] = dot_nt(qa_ref[0:dim, :], grads).astype(BF16)
         term = dot(kt_ref[:, part], grads)
         total = term if total is None else total + term
     dq_ref[...] = total
@@ -190,7 +209,7 @@
         sent_ref[pair] = held[me ^ (2 * pair) ^ 1]
 
 
-def add_pairs_kernel(kept_ref, came_ref, first_ref, second_ref):
+def add_pairs_kernel(kept_ref, came_ref, _, first_ref, second_ref):
     for index, out_ref in enumerate((first_ref, second_ref)):
         out_ref[...] = (kept_ref[index].astype(F32) + came_ref[index].astype(F32)).astype(BF16)
 
@@ -199,11 +218,8 @@
     wide = 2 * dim
     for slot in range(slots):
         here = slice(slot * rows, (slot + 1) * rows)
-        outs[slot][0:rows, :] = (kept_ref[here, :].astype(F32) + came_ref[here, :].astype(F32)).astype(BF16)
-        for part in range(rows // wide):
-            start = slot * rows + part * wide
-            grad = dq_ref[:, start : start + wide] * dim**-0.5
-            outs[slot][rows + part * dim : rows + (part + 1) * dim, :] = grad.astype(BF16)
+        outs[slot][0:wide, :] = (kept_ref[:, here].astype(F32) + came_ref[:, here].astype(F32)).astype(BF16)
+        outs[slot][wide:, :] = (dq_ref[:, here] * dim**-0.5).astype(BF16)
 
 
 def add_kernel(a_ref, b_ref, out_ref):
@@ -215,10 +231,8 @@
     wide = 2 * dim
     me = a_of()
     for slot in range(slots):
-        held[me ^ slot] = pieces[slot][0:rows, :].astype(F32)
-        for part in range(rows // wide):
-            start = rows + part * dim
-            q_out[me ^ slot, :, part * wide : (part + 1) * wide] = pieces[slot][start : start + dim, :].astype(F32)
+        held[me ^ slot] = pieces[slot][0:wide, :].astype(F32).T
+        q_out[me ^ slot] = pieces[slot][wide:, :].astype(F32)
     for head in range(slots):
         kv_out[:, head, :] = held[head]
 
@@ -247,20 +261,23 @@
         return [pieces[0]] + [came[s] for s in range(1, slots)]
 
     block, wide = slots * rows, 2 * dim
-    kv_mine = exchange(call(
-        functools.partial(pack_kv_kernel, heads, rows, dim, a_of),
-        [((rows, wide), BF16)] * slots, [pltpu.VMEM((heads, rows, wide), BF16)],
-        n_in=2, smem_first=True, micros=0.8,
-    )(tile_fill, key_value))
-    qg_send = call(
-        functools.partial(pack_qg_kernel, heads, rows, dim, a_of),
-        [((wide, rows), BF16)] * slots, [pltpu.VMEM((heads, wide, rows), BF16)],
-        n_in=4, smem_first=True, micros=1,
-    )(tile_fill, jnp.transpose(queries, (1, 2, 0)), out_weight, grad_output)
-    qg_mine = exchange(qg_send)
+    sent = call(
+        functools.partial(pack_kernel, heads, rows, dim, a_of),
+        [((rows + rows // 2, wide), BF16)] * slots,
+        [pltpu.VMEM((heads, rows + rows // 2, wide), BF16), pltpu.VMEM((heads, dim, rows), BF16),
+         pltpu.VMEM((rows, heads, wide), BF16), pltpu.SemaphoreType.DMA, pltpu.SemaphoreType.DMA],
+        n_in=3, smem_first=True, far=True, micros=1.5, limit=56,
+    )(tile_fill, jnp.transpose(queries, (1, 2, 0)), key_value)
+    mine = exchange(sent)
+    grad_sent = call(
+        functools.partial(pack_grad_kernel, heads, rows, dim, a_of),
+        [((dim, rows), BF16)] * slots, [pltpu.VMEM((heads, dim, rows), BF16)],
+        n_in=3, smem_first=True, micros=1,
+    )(tile_fill, out_weight, grad_output)
+    grads = exchange(grad_sent)
     own = call(
-        functools.partial(join_kernel, slots), [((block, wide), BF16)], n_in=slots, after=1,
-    )(*kv_mine, qg_send[0])[0]
+        functools.partial(join_kernel, slots, rows), [((block, wide), BF16)], n_in=slots, after=1,
+    )(*mine, grad_sent[0])[0]
 
     blocks = {0: own}
     bit = columns // 2
@@ -269,9 +286,9 @@
             blocks[r ^ bit] = swap(blocks[r], bit)
         bit //= 2
 
-    qa, grads = call(
-        functools.partial(join_q_kernel, slots, rows, dim), [((2 * wide, block), BF16), ((dim, block), BF16)], n_in=slots,
-    )(*qg_mine)
+    qa = call(
+        functools.partial(join_q_kernel, slots, rows, dim), [((2 * wide, block), BF16)], n_in=slots,
+    )(*mine)[0]
     step = min(block, 512)
     prepared, scored = {}, {}
     for r in range(columns):
@@ -287,26 +304,33 @@
         )(wide_keys, values, qa)
     combined = call(
         functools.partial(combine_kernel, slots, columns, rows, dim),
-        [((dim, rows), BF16)] * slots + [((1, block), F32)] * (columns + 1), n_in=2 * columns + 1, micros=0.5,
-    )(*[scored[r][1] for r in range(columns)], *[scored[r][2] for r in range(columns)], grads)
-    att_mine, factors, inner = exchange(combined[:slots]), combined[slots:-1], combined[-1]
+        [((dim, rows), BF16)] * slots + [((1, block), F32)] * (columns + 1) + [((dim, block), BF16)],
+        n_in=2 * columns + slots, micros=0.5,
+    )(*[scored[r][1] for r in range(columns)], *[scored[r][2] for r in range(columns)], *grads)
+    att_mine, factors, (inner, grads) = exchange(combined[:slots]), combined[slots : slots + columns], combined[slots + columns :]
 
     halves = columns == heads == 4
     order = sorted(range(columns), key=lambda r: -int(f"{r:032b}"[::-1], 2))
     dkv, dq = {}, None
     for at, r in enumerate(order):
-        if at == columns // 2:
+        later = []
+        if at == min(1, columns - 1):
             terms, *weight_terms = call(
                 functools.partial(project_kernel, slots, rows, dim, a_of, b_of, halves),
                 [((rows, width), BF16)] + ([((2, dim, width), BF16)] * 2 if halves else [((heads, dim, width), BF16)]),
                 [pltpu.VMEM((heads, dim, width), BF16)],
                 n_in=3 + slots, smem_first=True, after=1, micros=1,
             )(tile_fill, out_weight, grad_output, *att_mine, dkv[order[at - 1]])
+            later = [terms]
+        if at == 2 and halves:
+            kept, sent = weight_terms
+            kept, sent = call(add_pairs_kernel, [((dim, width), BF16)] * 2, n_in=2, after=1)(
+                kept, swap(sent, 1), dkv[order[at - 1]])
+            later = [kept]
         operands = [scored[r][0], prepared[r][0], prepared[r][1], qa, grads, factors[r], inner] + ([] if dq is None else [dq])
-        later = [terms] if at == columns // 2 else []
         dkv[r], dq = call(
             functools.partial(back_kernel, dim, min(step, 256), dq is None),
-            [((block, wide), BF16), ((dim, block), F32)], [pltpu.VMEM((2 * wide, block), BF16)],
+            [((wide, block), BF16), ((dim, block), F32)], [pltpu.VMEM((2 * wide, block), BF16)],
             n_in=len(operands), after=len(later), micros=2,
         )(*operands, *later)
 
@@ -316,8 +340,6 @@
         bit *= 2
 
     if halves:
-        kept, sent = weight_terms
-        kept, sent = call(add_pairs_kernel, [((dim, width), BF16)] * 2, n_in=2)(kept, swap(sent, 1))
         add = call(add_kernel, [((dim, width), BF16)], n_in=2)
         kept = add(kept, swap(sent, 2))[0]
         bit = columns
@@ -334,12 +356,12 @@
     bit = 1
     while 2 * bit < columns:
         dkv = {
-            r: call(add_kernel, [((block, wide), BF16)], n_in=2)(dkv[r], swap(dkv[r ^ bit], bit))[0]
+            r: call(add_kernel, [((wide, block), BF16)], n_in=2)(dkv[r], swap(dkv[r ^ bit], bit))[0]
             for r in order if r in dkv and not r & bit
         }
         bit *= 2
     returned = exchange(call(
-        functools.partial(add_pieces_kernel, slots, rows, dim), [((rows + rows // 2, wide), BF16)] * slots, n_in=3,
+        functools.partial(add_pieces_kernel, slots, rows, dim), [((wide + dim, rows), BF16)] * slots, n_in=3,
     )(dkv[0], swap(dkv[bit], bit), dq))
     key_value_grad, query_grad = call(
         functools.partial(unpack_kernel, slots, rows, dim, a_of),

time: 72.9 us -> 76 us (1.043)
  waiting for transfers between devices: 12.4 us -> 17.1 us
  local copies, waits for them, and re-layouts: 1.69 us -> 0.02 us
    ppermute x26, waiting for transfers between devices: 12.4 us -> 17.1 us  [swap(): return lax.ppermute(array, axis, [(i, i ^ mask) for i in range(size)])]
    pallas_call x4, Pallas kernels: 10.9 us -> 8.75 us  [shards(): call(functools.partial(back_kernel, dim, min(step, 256), dq is None), [((...]
    pallas_call x7, Pallas kernels: 2.91 us -> 4.89 us  [the longest x1 3.39 us: shards(): call(functools.partial(pack_kernel, heads, rows, dim, a_of), [((rows + ro...]
    unnamed x12 -> x8, local copies, waits for them, and re-layouts: 1.69 us -> 0.02 us
  transfers between devices with their start and end apart: 26 -> 26, of which waited for: 8 -> 7; matrix products, arithmetic and copies ran while one was open for 0% -> 0% of each run, Pallas kernels for 29% -> 28%
where the time goes in v5:
time: 76 us; the launch traced here: 75.9 us
  starting transfers between devices  30.3 us (40%)
  Pallas kernels  27.6 us (36%)
  waiting for transfers between devices  17.1 us (23%)
  between operations  0.89 us (1%)
    ppermute x26, starting transfers between devices, swap(): return lax.ppermute(array, axis, [(i, i ^ mask) for i in range(size)])  30.3 us
    ppermute x26, waiting for transfers between devices, swap(): return lax.ppermute(array, axis, [(i, i ^ mask) for i in range(size)])  17.1 us
    pallas_call x4, Pallas kernels, shards(): call(functools.partial(back_kernel, dim, min(step, 256), dq is None), [((...  8.75 us
    pallas_call x4, Pallas kernels, shards(): call(functools.partial(score_kernel, slots, rows, dim, step), [((block, b...  7.91 us
    pallas_call x1, Pallas kernels, shards(): call(functools.partial(pack_kernel, heads, rows, dim, a_of), [((rows + ro...  3.39 us
    pallas_call x1, Pallas kernels, shards(): call(functools.partial(project_kernel, slots, rows, dim, a_of, b_of, halv...  1.59 us
  transfers between devices with their start and end apart: 26, of which 7 were waited for; matrix products, arithmetic and copies ran while one was open for 0% of the time, Pallas kernels for 28%

profile of v5, /device:TPU:0, one launch (start us, length us, event | category | flops | bytes accessed | tf_op | source)
XLA Modules:
  0.0 75.9 jit_solution(1525027893838418761)
XLA Ops:
  0.7 3.4 %shard_map.84 = (bf16[384,128]{1,0:T(8,128)(2,1)}, bf16[384,128]{1,0:T(8,128)(2,1)}, bf16[384,128]{1,0:T(8,128)(2,1)}, bf16[384,128]{1,0:T(8,128)(2,1)}) custom-call(s32[2]{0:T(128)} %fill_ref.5, bf16[4,64,256]{2,1,0:T(8,128)(2,1)} %bitcast.2, bf16[256,4,128]{2,1,0:T(4,128)(2,1)} %kv_hbm.1), custom_call_target="tpu_custom_call" | custom-call | flops 1724999936 | tf_op jit(solution)/shard_map/pallas_call | solution.py:264
  4.1 3.1 %collective-permute-start = (bf16[384,128]{1,0:T(8,128)(2,1)}, bf16[384,128]{1,0:T(8,128)(2,1)S(1)}, u32[]{:S(2)}, u32[]{:S(2)}) collective-permute-start(bf16[384,128]{1,0:T(8,128)(2,1)} %get-tuple-element.66), channel_id=1, source_target_pairs={{0,8},{2,10},{4,12},{6,14},{8,0},{10,2},{12,4},{14,6},{16,24},{18,... | collective-permute-start | bytes 294920 | tf_op jit(solution)/shard_map/ppermute | solution.py:257
  7.1 2.6 %collective-permute-start.1 = (bf16[384,128]{1,0:T(8,128)(2,1)}, bf16[384,128]{1,0:T(8,128)(2,1)S(1)}, u32[]{:S(2)}, u32[]{:S(2)}) collective-permute-start(bf16[384,128]{1,0:T(8,128)(2,1)} %get-tuple-element.67), channel_id=1, source_target_pairs={{0,16},{2,18},{4,20},{6,22},{8,24},{10,26},{12,28},{14,30},{16,0},... | collective-permute-start | bytes 294920 | tf_op jit(solution)/shard_map/ppermute | solution.py:257
  9.8 1.2 %shard_map.85 = (bf16[64,256]{1,0:T(8,128)(2,1)S(1)}, bf16[64,256]{1,0:T(8,128)(2,1)S(1)}, bf16[64,256]{1,0:T(8,128)(2,1)S(1)}, bf16[64,256]{1,0:T(8,128)(2,1)S(1)}) custom-call(s32[2]{0:T(128)S(1)} %copy-done.2, bf16[4,64,768]{2,1,0:T(8,128)(2,1)S(1)} %copy-done, bf16[256,768]{1,0:T(8,128)(2,1)S(1)} %copy-done.1), custom_call_target="tpu_custom_call" | custom-call | flops 1150000000 | tf_op jit(solution)/shard_map/pallas_call | solution.py:272
  11.0 1.0 %collective-permute-start.6 = (bf16[64,256]{1,0:T(8,128)(2,1)S(1)}, bf16[64,256]{1,0:T(8,128)(2,1)S(1)}, u32[]{:S(2)}, u32[]{:S(2)}) collective-permute-start(bf16[64,256]{1,0:T(8,128)(2,1)S(1)} %get-tuple-element.86), channel_id=1, source_target_pairs={{0,8},{2,10},{4,12},{6,14},{8,0},{10,2},{12,4},{14,6},{16,24},{18,... | collective-permute-start | bytes 98312 | tf_op jit(solution)/shard_map/ppermute | solution.py:257
  11.9 3.5 %collective-permute-start.7 = (bf16[64,256]{1,0:T(8,128)(2,1)S(1)}, bf16[64,256]{1,0:T(8,128)(2,1)S(1)}, u32[]{:S(2)}, u32[]{:S(2)}) collective-permute-start(bf16[64,256]{1,0:T(8,128)(2,1)S(1)} %get-tuple-element.87), channel_id=1, source_target_pairs={{0,16},{2,18},{4,20},{6,22},{8,24},{10,26},{12,28},{14,30},{16,0},... | collective-permute-start | bytes 98312 | tf_op jit(solution)/shard_map/ppermute | solution.py:257
  15.4 0.0 collective-permute-start.8
  15.4 3.5 %collective-permute-done.1.refs_2_ = bf16[384,128]{1,0:T(8,128)(2,1)S(1)} collective-permute-done((bf16[384,128]{1,0:T(8,128)(2,1)}, bf16[384,128]{1,0:T(8,128)(2,1)S(1)}, u32[]{:S(2)}, u32[]{:S(2)}) %collective-permute-start.1) | collective-permute-done | bytes 98336 | tf_op jit(solution)/shard_map/ppermute | solution.py:257
  18.9 0.0 collective-permute-done.2.refs_3_
  19.0 1.6 %collective-permute-start.4 = (bf16[1024,128]{1,0:T(8,128)(2,1)S(1)}, bf16[1024,128]{1,0:T(8,128)(2,1)S(1)}, u32[]{:S(2)}, u32[]{:S(2)}) collective-permute-start(bf16[1024,128]{1,0:T(8,128)(2,1)S(1)} %shard_map.86.pair_ref), channel_id=1, source_target_pairs={{0,4},{2,6},{4,0},{6,2},{8,12},{10,14},{12,8},{14,10},{16,20},{18,... | collective-permute-start | bytes 786440 | tf_op jit(solution)/shard_map/ppermute | solution.py:257
  20.6 0.2 shard_map.87
  20.8 2.0 %shard_map.89 = (bf16[1024,1024]{1,0:T(8,128)(2,1)S(1)}, f32[1,1024]{1,0:T(1,128)S(1)}, f32[80,1024]{1,0:T(8,128)S(1)}) custom-call(bf16[1024,256]{1,0:T(8,128)(2,1)S(1)} %get-tuple-element.70.wide_ref, bf16[80,1024]{1,0:T(8,128)(2,1)S(1)} %get-tuple-element.71.vt_ref, bf16[256,1024]{1,0:T(8,128)(2,1)S(1)} %shard_map.88.qa_ref), custom_call_target="tpu_custom_call" | custom-call | flops 2300000000 | tf_op jit(solution)/shard_map/pallas_call | solution.py:300
  22.8 2.6 %collective-permute-done.4.pair_ref = bf16[1024,128]{1,0:T(8,128)(2,1)S(1)} collective-permute-done((bf16[1024,128]{1,0:T(8,128)(2,1)S(1)}, bf16[1024,128]{1,0:T(8,128)(2,1)S(1)}, u32[]{:S(2)}, u32[]{:S(2)}) %collective-permute-start.4) | collective-permute-done | bytes 262176 | tf_op jit(solution)/shard_map/ppermute | solution.py:257
  25.4 0.0 collective-permute-start.5
  25.4 0.2 shard_map.92
  25.6 2.0 %shard_map.93 = (bf16[1024,1024]{1,0:T(8,128)(2,1)S(1)}, f32[1,1024]{1,0:T(1,128)S(1)}, f32[80,1024]{1,0:T(8,128)S(1)}) custom-call(bf16[1024,256]{1,0:T(8,128)(2,1)S(1)} %get-tuple-element.76.wide_ref, bf16[80,1024]{1,0:T(8,128)(2,1)S(1)} %get-tuple-element.77.vt_ref, bf16[256,1024]{1,0:T(8,128)(2,1)S(1)} %shard_map.88.qa_ref), custom_call_target="tpu_custom_call" | custom-call | flops 2300000000 | tf_op jit(solution)/shard_map/pallas_call | solution.py:300
  27.6 0.0 collective-permute-done.3.pair_ref
  27.6 0.2 shard_map.90
  27.9 2.0 %shard_map.91 = (bf16[1024,1024]{1,0:T(8,128)(2,1)S(1)}, f32[1,1024]{1,0:T(1,128)S(1)}, f32[80,1024]{1,0:T(8,128)S(1)}) custom-call(bf16[1024,256]{1,0:T(8,128)(2,1)S(1)} %get-tuple-element.73.wide_ref, bf16[80,1024]{1,0:T(8,128)(2,1)S(1)} %get-tuple-element.74.vt_ref, bf16[256,1024]{1,0:T(8,128)(2,1)S(1)} %shard_map.88.qa_ref), custom_call_target="tpu_custom_call" | custom-call | flops 2300000000 | tf_op jit(solution)/shard_map/pallas_call | solution.py:300
  29.9 0.2 shard_map.94
  30.1 2.0 %shard_map.95 = (bf16[1024,1024]{1,0:T(8,128)(2,1)S(1)}, f32[1,1024]{1,0:T(1,128)S(1)}, f32[80,1024]{1,0:T(8,128)S(1)}) custom-call(bf16[1024,256]{1,0:T(8,128)(2,1)S(1)} %get-tuple-element.79.wide_ref, bf16[80,1024]{1,0:T(8,128)(2,1)S(1)} %get-tuple-element.80.vt_ref, bf16[256,1024]{1,0:T(8,128)(2,1)S(1)} %shard_map.88.qa_ref), custom_call_target="tpu_custom_call" | custom-call | flops 2300000000 | tf_op jit(solution)/shard_map/pallas_call | solution.py:300
  32.1 0.0 collective-permute-done.6.refs_9_
  32.1 0.0 collective-permute-done.7.refs_10_
  32.2 0.2 shard_map.96
  32.4 2.3 %collective-permute-start.9 = (bf16[64,256]{1,0:T(8,128)(2,1)S(1)}, bf16[64,256]{1,0:T(8,128)(2,1)S(1)}, u32[]{:S(2)}, u32[]{:S(2)}) collective-permute-start(bf16[64,256]{1,0:T(8,128)(2,1)S(1)} %get-tuple-element.90), channel_id=1, source_target_pairs={{0,8},{2,10},{4,12},{6,14},{8,0},{10,2},{12,4},{14,6},{16,24},{18,... | collective-permute-start | bytes 98312 | tf_op jit(solution)/shard_map/ppermute | solution.py:257
  34.7 1.4 %collective-permute-start.10 = (bf16[64,256]{1,0:T(8,128)(2,1)S(1)}, bf16[64,256]{1,0:T(8,128)(2,1)S(1)}, u32[]{:S(2)}, u32[]{:S(2)}) collective-permute-start(bf16[64,256]{1,0:T(8,128)(2,1)S(1)} %get-tuple-element.91), channel_id=1, source_target_pairs={{0,16},{2,18},{4,20},{6,22},{8,24},{10,26},{12,28},{14,30},{16,0},... | collective-permute-start | bytes 98312 | tf_op jit(solution)/shard_map/ppermute | solution.py:257
  36.1 1.4 %collective-permute-start.11 = (bf16[64,256]{1,0:T(8,128)(2,1)S(1)}, bf16[64,256]{1,0:T(8,128)(2,1)S(1)}, u32[]{:S(2)}, u32[]{:S(2)}) collective-permute-start(bf16[64,256]{1,0:T(8,128)(2,1)S(1)} %get-tuple-element.92), channel_id=1, source_target_pairs={{0,24},{2,26},{4,28},{6,30},{8,16},{10,18},{12,20},{14,22},{16,8},... | collective-permute-start | bytes 98312 | tf_op jit(solution)/shard_map/ppermute | solution.py:257
  37.5 2.2 %shard_map.97 = (bf16[128,1024]{1,0:T(8,128)(2,1)S(1)}, f32[64,1024]{1,0:T(8,128)S(1)}) custom-call(bf16[1024,1024]{1,0:T(8,128)(2,1)S(1)} %get-tuple-element.93.exp_ref, bf16[1024,256]{1,0:T(8,128)(2,1)S(1)} %get-tuple-element.79.wide_ref, bf16[64,1024]{1,0:T(8,128)(2,1)S(1)} %get-tuple-element.94.kt_ref, bf16[256,1024]{1,0:T(8,128)(2,1)S(1)} %shard_map.88.qa_ref, ...), custom_call_target="tpu_custom_call" | custom-call | flops 2300000000 | tf_op jit(solution)/shard_map/pallas_call | solution.py:331
  39.7 0.0 collective-permute-done.9.refs_1_
  39.7 0.0 collective-permute-done.10.refs_2_
  39.7 2.1 %collective-permute-done.11.refs_3_ = bf16[64,256]{1,0:T(8,128)(2,1)S(1)} collective-permute-done((bf16[64,256]{1,0:T(8,128)(2,1)S(1)}, bf16[64,256]{1,0:T(8,128)(2,1)S(1)}, u32[]{:S(2)}, u32[]{:S(2)}) %collective-permute-start.11) | collective-permute-done | bytes 32800 | tf_op jit(solution)/shard_map/ppermute | solution.py:257
  41.8 1.6 %shard_map.98 = (bf16[256,768]{1,0:T(8,128)(2,1)S(1)}, bf16[2,64,768]{2,1,0:T(8,128)(2,1)S(1)}, bf16[2,64,768]{2,1,0:T(8,128)(2,1)S(1)}) custom-call(s32[2]{0:T(128)S(1)} %copy-done.2, bf16[4,64,768]{2,1,0:T(8,128)(2,1)S(1)} %copy-done, bf16[256,768]{1,0:T(8,128)(2,1)S(1)} %copy-done.1, bf16[64,256]{1,0:T(8,128)(2,1)S(1)} %get-tuple-element.89.refs_0_, ...), custom_call_target="tpu_custom_call" | custom-call | flops 1150000000 | tf_op jit(solution)/shard_map/pallas_call | solution.py:318
  43.4 0.1 collective-permute-start.13
  43.5 2.2 %shard_map.100 = (bf16[128,1024]{1,0:T(8,128)(2,1)S(1)}, f32[64,1024]{1,0:T(8,128)S(1)}) custom-call(bf16[1024,1024]{1,0:T(8,128)(2,1)S(1)} %get-tuple-element.106.exp_ref, bf16[1024,256]{1,0:T(8,128)(2,1)S(1)} %get-tuple-element.73.wide_ref, bf16[64,1024]{1,0:T(8,128)(2,1)S(1)} %get-tuple-element.107.kt_ref, bf16[256,1024]{1,0:T(8,128)(2,1)S(1)} %shard_map.88.qa_ref, ...), custom_call_target="tpu_custom_call" | custom-call | flops 2300000000 | tf_op jit(solution)/shard_map/pallas_call | solution.py:331
  45.7 0.0 collective-permute-done.13.came_ref
  45.7 0.1 shard_map.101
  45.8 1.6 %collective-permute-start.20 = (bf16[64,768]{1,0:T(8,128)(2,1)S(1)}, bf16[64,768]{1,0:T(8,128)(2,1)S(1)}, u32[]{:S(2)}, u32[]{:S(2)}) collective-permute-start(bf16[64,768]{1,0:T(8,128)(2,1)S(1)} %get-tuple-element.125), channel_id=1, source_target_pairs={{0,4},{2,6},{4,0},{6,2},{8,12},{10,14},{12,8},{14,10},{16,20},{18,... | collective-permute-start | bytes 294920 | tf_op jit(solution)/shard_map/ppermute | solution.py:257
  47.4 0.2 collective-permute-start.15
  47.6 0.3 collective-permute-start.14
  47.9 1.5 %collective-permute-start.12 = (bf16[256,768]{1,0:T(8,128)(2,1)S(1)}, bf16[256,768]{1,0:T(8,128)(2,1)S(1)}, u32[]{:S(2)}, u32[]{:S(2)}) collective-permute-start(bf16[256,768]{1,0:T(8,128)(2,1)S(1)} %get-tuple-element.99.a_ref.refs_1_), channel_id=1, source_target_pairs={{0,1},{1,0},{2,3},{3,2},{4,5},{5,4},{6,7},{7,6},{8,9},{9,8},{10,11... | collective-permute-start | bytes 1179656 | tf_op jit(solution)/shard_map/ppermute | solution.py:257
  49.4 1.7 %collective-permute-done.20.b_ref = bf16[64,768]{1,0:T(8,128)(2,1)S(1)} collective-permute-done((bf16[64,768]{1,0:T(8,128)(2,1)S(1)}, bf16[64,768]{1,0:T(8,128)(2,1)S(1)}, u32[]{:S(2)}, u32[]{:S(2)}) %collective-permute-start.20) | collective-permute-done | bytes 98336 | tf_op jit(solution)/shard_map/ppermute | solution.py:257
  51.1 0.2 collective-permute-start.21
  51.3 2.2 %shard_map.102 = (bf16[128,1024]{1,0:T(8,128)(2,1)S(1)}, f32[64,1024]{1,0:T(8,128)S(1)}) custom-call(bf16[1024,1024]{1,0:T(8,128)(2,1)S(1)} %get-tuple-element.103.exp_ref, bf16[1024,256]{1,0:T(8,128)(2,1)S(1)} %get-tuple-element.76.wide_ref, bf16[64,1024]{1,0:T(8,128)(2,1)S(1)} %get-tuple-element.104.kt_ref, bf16[256,1024]{1,0:T(8,128)(2,1)S(1)} %shard_map.88.qa_ref, ...), custom_call_target="tpu_custom_call" | custom-call | flops 2300000000 | tf_op jit(solution)/shard_map/pallas_call | solution.py:331
  53.5 0.0 collective-permute-done.15.b_ref
  53.5 0.1 shard_map.105
  53.6 1.6 %collective-permute-start.16 = (bf16[128,1024]{1,0:T(8,128)(2,1)S(1)}, bf16[128,1024]{1,0:T(8,128)(2,1)S(1)}, u32[]{:S(2)}, u32[]{:S(2)}) collective-permute-start(bf16[128,1024]{1,0:T(8,128)(2,1)S(1)} %shard_map.105), channel_id=1, source_target_pairs={{0,4},{2,6},{4,0},{6,2},{8,12},{10,14},{12,8},{14,10},{16,20},{18,... | collective-permute-start | bytes 786440 | tf_op jit(solution)/shard_map/ppermute | solution.py:257
  55.2 0.6 collective-permute-done.21.b_ref
  55.8 1.4 %collective-permute-start.22 = (bf16[64,768]{1,0:T(8,128)(2,1)S(1)}, bf16[64,768]{1,0:T(8,128)(2,1)S(1)}, u32[]{:S(2)}, u32[]{:S(2)}) collective-permute-start(bf16[64,768]{1,0:T(8,128)(2,1)S(1)} %shard_map.109.a_ref), channel_id=1, source_target_pairs={{0,16},{2,18},{4,20},{6,22},{8,24},{10,26},{12,28},{14,30},{16,0},... | collective-permute-start | bytes 294920 | tf_op jit(solution)/shard_map/ppermute | solution.py:257
  57.2 2.2 %shard_map.103 = (bf16[128,1024]{1,0:T(8,128)(2,1)S(1)}, f32[64,1024]{1,0:T(8,128)S(1)}) custom-call(bf16[1024,1024]{1,0:T(8,128)(2,1)S(1)} %get-tuple-element.100.exp_ref, bf16[1024,256]{1,0:T(8,128)(2,1)S(1)} %get-tuple-element.70.wide_ref, bf16[64,1024]{1,0:T(8,128)(2,1)S(1)} %get-tuple-element.101.kt_ref, bf16[256,1024]{1,0:T(8,128)(2,1)S(1)} %shard_map.88.qa_ref, ...), custom_call_target="tpu_custom_call" | custom-call | flops 2300000000 | tf_op jit(solution)/shard_map/pallas_call | solution.py:331
  59.4 0.0 collective-permute-done.14.b_ref
  59.4 0.1 shard_map.104.kept_ref
  59.5 2.0 %collective-permute-done.16.came_ref = bf16[128,1024]{1,0:T(8,128)(2,1)S(1)} collective-permute-done((bf16[128,1024]{1,0:T(8,128)(2,1)S(1)}, bf16[128,1024]{1,0:T(8,128)(2,1)S(1)}, u32[]{:S(2)}, u32[]{:S(2)}) %collective-permute-start.16) | collective-permute-done | bytes 262176 | tf_op jit(solution)/shard_map/ppermute | solution.py:257
  61.4 0.1 shard_map.106
  61.5 1.8 %collective-permute-start.17 = (bf16[192,256]{1,0:T(8,128)(2,1)S(1)}, bf16[192,256]{1,0:T(8,128)(2,1)S(1)}, u32[]{:S(2)}, u32[]{:S(2)}) collective-permute-start(bf16[192,256]{1,0:T(8,128)(2,1)S(1)} %get-tuple-element.120), channel_id=1, source_target_pairs={{0,8},{2,10},{4,12},{6,14},{8,0},{10,2},{12,4},{14,6},{16,24},{18,... | collective-permute-start | bytes 294920 | tf_op jit(solution)/shard_map/ppermute | solution.py:257
  63.3 1.6 %collective-permute-start.24 = (bf16[64,768]{1,0:T(8,128)(2,1)S(1)}, bf16[64,768]{1,0:T(8,128)(2,1)S(1)}, u32[]{:S(2)}, u32[]{:S(2)}) collective-permute-start(bf16[64,768]{1,0:T(8,128)(2,1)S(1)} %shard_map.110.refs_0_), channel_id=1, source_target_pairs={{0,4},{2,6},{4,0},{6,2},{8,12},{10,14},{12,8},{14,10},{16,20},{18,... | collective-permute-start | bytes 294920 | tf_op jit(solution)/shard_map/ppermute | solution.py:257
  64.9 1.1 %collective-permute-start.18 = (bf16[192,256]{1,0:T(8,128)(2,1)S(1)}, bf16[192,256]{1,0:T(8,128)(2,1)S(1)}, u32[]{:S(2)}, u32[]{:S(2)}) collective-permute-start(bf16[192,256]{1,0:T(8,128)(2,1)S(1)} %get-tuple-element.121), channel_id=1, source_target_pairs={{0,16},{2,18},{4,20},{6,22},{8,24},{10,26},{12,28},{14,30},{16,0},... | collective-permute-start | bytes 294920 | tf_op jit(solution)/shard_map/ppermute | solution.py:257
  66.0 1.5 %collective-permute-start.19 = (bf16[192,256]{1,0:T(8,128)(2,1)S(1)}, bf16[192,256]{1,0:T(8,128)(2,1)S(1)}, u32[]{:S(2)}, u32[]{:S(2)}) collective-permute-start(bf16[192,256]{1,0:T(8,128)(2,1)S(1)} %get-tuple-element.122), channel_id=1, source_target_pairs={{0,24},{2,26},{4,28},{6,30},{8,16},{10,18},{12,20},{14,22},{16,8},... | collective-permute-start | bytes 294920 | tf_op jit(solution)/shard_map/ppermute | solution.py:257
  67.6 0.8 %shard_map.99 = bf16[256,768]{1,0:T(8,128)(2,1)} custom-call(bf16[256,768]{1,0:T(8,128)(2,1)S(1)} %get-tuple-element.99.a_ref.refs_1_, bf16[256,768]{1,0:T(8,128)(2,1)S(1)} %collective-permute-done.12.b_ref), custom_call_target="tpu_custom_call" | custom-call | flops 345000000 | tf_op jit(solution)/shard_map/pallas_call | solution.py:339
  68.4 0.0 collective-permute-start.23
  68.4 0.0 collective-permute-done.24.refs_2_
  68.4 0.5 collective-permute-start.25
  68.9 4.7 %collective-permute-done.18.refs_2_ = bf16[192,256]{1,0:T(8,128)(2,1)S(1)} collective-permute-done((bf16[192,256]{1,0:T(8,128)(2,1)S(1)}, bf16[192,256]{1,0:T(8,128)(2,1)S(1)}, u32[]{:S(2)}, u32[]{:S(2)}) %collective-permute-start.18) | collective-permute-done | bytes 98336 | tf_op jit(solution)/shard_map/ppermute | solution.py:257
  73.6 1.3 %shard_map.107 = (f32[256,4,128]{2,1,0:T(4,128)}, f32[4,64,256]{2,1,0:T(8,128)}) custom-call(bf16[192,256]{1,0:T(8,128)(2,1)S(1)} %get-tuple-element.119.refs_0_, bf16[192,256]{1,0:T(8,128)(2,1)S(1)} %collective-permute-done.17.refs_1_, bf16[192,256]{1,0:T(8,128)(2,1)S(1)} %collective-permute-done.18.refs_2_, ...), custom_call_target="tpu_custom_call" | custom-call | flops 1150000000 | tf_op jit(solution)/shard_map/pallas_call | solution.py:366
  74.9 0.9 %shard_map.111 = f32[4,64,768]{2,1,0:T(8,128)} custom-call(bf16[64,768]{1,0:T(8,128)(2,1)S(1)} %shard_map.110.refs_0_, bf16[64,768]{1,0:T(8,128)(2,1)S(1)} %collective-permute-done.23.refs_1_, bf16[64,768]{1,0:T(8,128)(2,1)S(1)} %collective-permute-done.24.refs_2_, bf16[64,768]{1,0:T(8,128)(2,1)S(1)} %collective-permute-done.25.refs_3_), custom_call_target="tpu_custom_call" | custom-call | flops 575000000 | tf_op jit(solution)/shard_map/pallas_call | solution.py:350
  (24 shorter events, 0.2 us)
Async XLA Ops:
  0.6 9.1 %copy-start = (bf16[4,64,768]{2,1,0:T(8,128)(2,1)S(1)}, bf16[4,64,768]{2,1,0:T(8,128)(2,1)}, u32[]{:S(2)}) copy-start(bf16[4,64,768]{2,1,0:T(8,128)(2,1)} %w_ref.3) | copy-start | bytes 1179652
  0.6 9.1 %copy-start.1 = (bf16[256,768]{1,0:T(8,128)(2,1)S(1)}, bf16[256,768]{1,0:T(8,128)(2,1)}, u32[]{:S(2)}) copy-start(bf16[256,768]{1,0:T(8,128)(2,1)} %go_ref.3) | copy-start | bytes 1179652
  0.7 9.1 %copy-start.2 = (s32[2]{0:T(128)S(1)}, s32[2]{0:T(128)}, u32[]{:S(2)}) copy-start(s32[2]{0:T(128)} %fill_ref.5) | copy-start | bytes 28
  4.1 11.4 %collective-permute-start = (bf16[384,128]{1,0:T(8,128)(2,1)}, bf16[384,128]{1,0:T(8,128)(2,1)S(1)}, u32[]{:S(2)}, u32[]{:S(2)}) collective-permute-start(bf16[384,128]{1,0:T(8,128)(2,1)} %get-tuple-element.66), channel_id=1, source_target_pairs={{0,8},{2,10},{4,12},{6,14},{8,0},{10,2},{12,4},{14,6},{16,24},{18,... | collective-permute-start | bytes 294920 | tf_op jit(solution)/shard_map/ppermute | solution.py:257
  7.1 11.8 %collective-permute-start.1 = (bf16[384,128]{1,0:T(8,128)(2,1)}, bf16[384,128]{1,0:T(8,128)(2,1)S(1)}, u32[]{:S(2)}, u32[]{:S(2)}) collective-permute-start(bf16[384,128]{1,0:T(8,128)(2,1)} %get-tuple-element.67), channel_id=1, source_target_pairs={{0,16},{2,18},{4,20},{6,22},{8,24},{10,26},{12,28},{14,30},{16,0},... | collective-permute-start | bytes 294920 | tf_op jit(solution)/shard_map/ppermute | solution.py:257
  9.7 9.2 %copy-start.3 = (bf16[384,128]{1,0:T(8,128)(2,1)S(1)}, bf16[384,128]{1,0:T(8,128)(2,1)}, u32[]{:S(2)}) copy-start(bf16[384,128]{1,0:T(8,128)(2,1)} %get-tuple-element.65.refs_0_) | copy-start | bytes 294916
  9.7 9.2 %collective-permute-start.2 = (bf16[384,128]{1,0:T(8,128)(2,1)}, bf16[384,128]{1,0:T(8,128)(2,1)S(1)}, u32[]{:S(2)}, u32[]{:S(2)}) collective-permute-start(bf16[384,128]{1,0:T(8,128)(2,1)} %get-tuple-element.68), channel_id=1, source_target_pairs={{0,24},{2,26},{4,28},{6,30},{8,16},{10,18},{12,20},{14,22},{16,8},... | collective-permute-start | bytes 294920 | tf_op jit(solution)/shard_map/ppermute | solution.py:257
  11.0 21.1 %collective-permute-start.6 = (bf16[64,256]{1,0:T(8,128)(2,1)S(1)}, bf16[64,256]{1,0:T(8,128)(2,1)S(1)}, u32[]{:S(2)}, u32[]{:S(2)}) collective-permute-start(bf16[64,256]{1,0:T(8,128)(2,1)S(1)} %get-tuple-element.86), channel_id=1, source_target_pairs={{0,8},{2,10},{4,12},{6,14},{8,0},{10,2},{12,4},{14,6},{16,24},{18,... | collective-permute-start | bytes 98312 | tf_op jit(solution)/shard_map/ppermute | solution.py:257
  11.9 20.2 %collective-permute-start.7 = (bf16[64,256]{1,0:T(8,128)(2,1)S(1)}, bf16[64,256]{1,0:T(8,128)(2,1)S(1)}, u32[]{:S(2)}, u32[]{:S(2)}) collective-permute-start(bf16[64,256]{1,0:T(8,128)(2,1)S(1)} %get-tuple-element.87), channel_id=1, source_target_pairs={{0,16},{2,18},{4,20},{6,22},{8,24},{10,26},{12,28},{14,30},{16,0},... | collective-permute-start | bytes 98312 | tf_op jit(solution)/shard_map/ppermute | solution.py:257
  15.4 16.7 %collective-permute-start.8 = (bf16[64,256]{1,0:T(8,128)(2,1)S(1)}, bf16[64,256]{1,0:T(8,128)(2,1)S(1)}, u32[]{:S(2)}, u32[]{:S(2)}) collective-permute-start(bf16[64,256]{1,0:T(8,128)(2,1)S(1)} %get-tuple-element.88), channel_id=1, source_target_pairs={{0,24},{2,26},{4,28},{6,30},{8,16},{10,18},{12,20},{14,22},{16,8},... | collective-permute-start | bytes 98312 | tf_op jit(solution)/shard_map/ppermute | solution.py:257
  19.0 6.4 %collective-permute-start.4 = (bf16[1024,128]{1,0:T(8,128)(2,1)S(1)}, bf16[1024,128]{1,0:T(8,128)(2,1)S(1)}, u32[]{:S(2)}, u32[]{:S(2)}) collective-permute-start(bf16[1024,128]{1,0:T(8,128)(2,1)S(1)} %shard_map.86.pair_ref), channel_id=1, source_target_pairs={{0,4},{2,6},{4,0},{6,2},{8,12},{10,14},{12,8},{14,10},{16,20},{18,... | collective-permute-start | bytes 786440 | tf_op jit(solution)/shard_map/ppermute | solution.py:257
  20.5 7.1 %collective-permute-start.3 = (bf16[1024,128]{1,0:T(8,128)(2,1)S(1)}, bf16[1024,128]{1,0:T(8,128)(2,1)S(1)}, u32[]{:S(2)}, u32[]{:S(2)}) collective-permute-start(bf16[1024,128]{1,0:T(8,128)(2,1)S(1)} %shard_map.86.pair_ref), channel_id=1, source_target_pairs={{0,2},{2,0},{4,6},{6,4},{8,10},{10,8},{12,14},{14,12},{16,18},{18,... | collective-permute-start | bytes 786440 | tf_op jit(solution)/shard_map/ppermute | solution.py:257
  25.4 4.5 %collective-permute-start.5 = (bf16[1024,128]{1,0:T(8,128)(2,1)S(1)}, bf16[1024,128]{1,0:T(8,128)(2,1)S(1)}, u32[]{:S(2)}, u32[]{:S(2)}) collective-permute-start(bf16[1024,128]{1,0:T(8,128)(2,1)S(1)} %collective-permute-done.4.pair_ref), channel_id=1, source_target_pairs={{0,2},{2,0},{4,6},{6,4},{8,10},{10,8},{12,14},{14,12},{16,18},{18,... | collective-permute-start | bytes 786440 | tf_op jit(solution)/shard_map/ppermute | solution.py:257
  32.4 7.3 %collective-permute-start.9 = (bf16[64,256]{1,0:T(8,128)(2,1)S(1)}, bf16[64,256]{1,0:T(8,128)(2,1)S(1)}, u32[]{:S(2)}, u32[]{:S(2)}) collective-permute-start(bf16[64,256]{1,0:T(8,128)(2,1)S(1)} %get-tuple-element.90), channel_id=1, source_target_pairs={{0,8},{2,10},{4,12},{6,14},{8,0},{10,2},{12,4},{14,6},{16,24},{18,... | collective-permute-start | bytes 98312 | tf_op jit(solution)/shard_map/ppermute | solution.py:257
  34.7 5.0 %collective-permute-start.10 = (bf16[64,256]{1,0:T(8,128)(2,1)S(1)}, bf16[64,256]{1,0:T(8,128)(2,1)S(1)}, u32[]{:S(2)}, u32[]{:S(2)}) collective-permute-start(bf16[64,256]{1,0:T(8,128)(2,1)S(1)} %get-tuple-element.91), channel_id=1, source_target_pairs={{0,16},{2,18},{4,20},{6,22},{8,24},{10,26},{12,28},{14,30},{16,0},... | collective-permute-start | bytes 98312 | tf_op jit(solution)/shard_map/ppermute | solution.py:257
  36.1 5.7 %collective-permute-start.11 = (bf16[64,256]{1,0:T(8,128)(2,1)S(1)}, bf16[64,256]{1,0:T(8,128)(2,1)S(1)}, u32[]{:S(2)}, u32[]{:S(2)}) collective-permute-start(bf16[64,256]{1,0:T(8,128)(2,1)S(1)} %get-tuple-element.92), channel_id=1, source_target_pairs={{0,24},{2,26},{4,28},{6,30},{8,16},{10,18},{12,20},{14,22},{16,8},... | collective-permute-start | bytes 98312 | tf_op jit(solution)/shard_map/ppermute | solution.py:257
  43.4 2.3 %collective-permute-start.13 = (bf16[2,64,768]{2,1,0:T(8,128)(2,1)S(1)}, bf16[2,64,768]{2,1,0:T(8,128)(2,1)S(1)}, u32[]{:S(2)}, u32[]{:S(2)}) collective-permute-start(bf16[2,64,768]{2,1,0:T(8,128)(2,1)S(1)} %get-tuple-element.112), channel_id=1, source_target_pairs={{0,2},{2,0},{4,6},{6,4},{8,10},{10,8},{12,14},{14,12},{16,18},{18,... | collective-permute-start | bytes 589832 | tf_op jit(solution)/shard_map/ppermute | solution.py:257
  45.8 5.3 %collective-permute-start.20 = (bf16[64,768]{1,0:T(8,128)(2,1)S(1)}, bf16[64,768]{1,0:T(8,128)(2,1)S(1)}, u32[]{:S(2)}, u32[]{:S(2)}) collective-permute-start(bf16[64,768]{1,0:T(8,128)(2,1)S(1)} %get-tuple-element.125), channel_id=1, source_target_pairs={{0,4},{2,6},{4,0},{6,2},{8,12},{10,14},{12,8},{14,10},{16,20},{18,... | collective-permute-start | bytes 294920 | tf_op jit(solution)/shard_map/ppermute | solution.py:257
  47.4 6.1 %collective-permute-start.15 = (bf16[128,1024]{1,0:T(8,128)(2,1)S(1)}, bf16[128,1024]{1,0:T(8,128)(2,1)S(1)}, u32[]{:S(2)}, u32[]{:S(2)}) collective-permute-start(bf16[128,1024]{1,0:T(8,128)(2,1)S(1)} %get-tuple-element.98.refs_4_), channel_id=1, source_target_pairs={{0,2},{2,0},{4,6},{6,4},{8,10},{10,8},{12,14},{14,12},{16,18},{18,... | collective-permute-start | bytes 786440 | tf_op jit(solution)/shard_map/ppermute | solution.py:257
  47.6 11.8 %collective-permute-start.14 = (bf16[128,1024]{1,0:T(8,128)(2,1)S(1)}, bf16[128,1024]{1,0:T(8,128)(2,1)S(1)}, u32[]{:S(2)}, u32[]{:S(2)}) collective-permute-start(bf16[128,1024]{1,0:T(8,128)(2,1)S(1)} %get-tuple-element.113._), channel_id=1, source_target_pairs={{0,2},{2,0},{4,6},{6,4},{8,10},{10,8},{12,14},{14,12},{16,18},{18,... | collective-permute-start | bytes 786440 | tf_op jit(solution)/shard_map/ppermute | solution.py:257
  47.9 19.7 %collective-permute-start.12 = (bf16[256,768]{1,0:T(8,128)(2,1)S(1)}, bf16[256,768]{1,0:T(8,128)(2,1)S(1)}, u32[]{:S(2)}, u32[]{:S(2)}) collective-permute-start(bf16[256,768]{1,0:T(8,128)(2,1)S(1)} %get-tuple-element.99.a_ref.refs_1_), channel_id=1, source_target_pairs={{0,1},{1,0},{2,3},{3,2},{4,5},{5,4},{6,7},{7,6},{8,9},{9,8},{10,11... | collective-permute-start | bytes 1179656 | tf_op jit(solution)/shard_map/ppermute | solution.py:257
  51.1 4.7 %collective-permute-start.21 = (bf16[64,768]{1,0:T(8,128)(2,1)S(1)}, bf16[64,768]{1,0:T(8,128)(2,1)S(1)}, u32[]{:S(2)}, u32[]{:S(2)}) collective-permute-start(bf16[64,768]{1,0:T(8,128)(2,1)S(1)} %shard_map.108.a_ref), channel_id=1, source_target_pairs={{0,8},{2,10},{4,12},{6,14},{8,0},{10,2},{12,4},{14,6},{16,24},{18,... | collective-permute-start | bytes 294920 | tf_op jit(solution)/shard_map/ppermute | solution.py:257
  53.6 7.8 %collective-permute-start.16 = (bf16[128,1024]{1,0:T(8,128)(2,1)S(1)}, bf16[128,1024]{1,0:T(8,128)(2,1)S(1)}, u32[]{:S(2)}, u32[]{:S(2)}) collective-permute-start(bf16[128,1024]{1,0:T(8,128)(2,1)S(1)} %shard_map.105), channel_id=1, source_target_pairs={{0,4},{2,6},{4,0},{6,2},{8,12},{10,14},{12,8},{14,10},{16,20},{18,... | collective-permute-start | bytes 786440 | tf_op jit(solution)/shard_map/ppermute | solution.py:257
  55.8 7.5 %collective-permute-start.22 = (bf16[64,768]{1,0:T(8,128)(2,1)S(1)}, bf16[64,768]{1,0:T(8,128)(2,1)S(1)}, u32[]{:S(2)}, u32[]{:S(2)}) collective-permute-start(bf16[64,768]{1,0:T(8,128)(2,1)S(1)} %shard_map.109.a_ref), channel_id=1, source_target_pairs={{0,16},{2,18},{4,20},{6,22},{8,24},{10,26},{12,28},{14,30},{16,0},... | collective-permute-start | bytes 294920 | tf_op jit(solution)/shard_map/ppermute | solution.py:257
  61.5 7.4 %collective-permute-start.17 = (bf16[192,256]{1,0:T(8,128)(2,1)S(1)}, bf16[192,256]{1,0:T(8,128)(2,1)S(1)}, u32[]{:S(2)}, u32[]{:S(2)}) collective-permute-start(bf16[192,256]{1,0:T(8,128)(2,1)S(1)} %get-tuple-element.120), channel_id=1, source_target_pairs={{0,8},{2,10},{4,12},{6,14},{8,0},{10,2},{12,4},{14,6},{16,24},{18,... | collective-permute-start | bytes 294920 | tf_op jit(solution)/shard_map/ppermute | solution.py:257
  63.3 5.1 %collective-permute-start.24 = (bf16[64,768]{1,0:T(8,128)(2,1)S(1)}, bf16[64,768]{1,0:T(8,128)(2,1)S(1)}, u32[]{:S(2)}, u32[]{:S(2)}) collective-permute-start(bf16[64,768]{1,0:T(8,128)(2,1)S(1)} %shard_map.110.refs_0_), channel_id=1, source_target_pairs={{0,4},{2,6},{4,0},{6,2},{8,12},{10,14},{12,8},{14,10},{16,20},{18,... | collective-permute-start | bytes 294920 | tf_op jit(solution)/shard_map/ppermute | solution.py:257
  64.9 8.7 %collective-permute-start.18 = (bf16[192,256]{1,0:T(8,128)(2,1)S(1)}, bf16[192,256]{1,0:T(8,128)(2,1)S(1)}, u32[]{:S(2)}, u32[]{:S(2)}) collective-permute-start(bf16[192,256]{1,0:T(8,128)(2,1)S(1)} %get-tuple-element.121), channel_id=1, source_target_pairs={{0,16},{2,18},{4,20},{6,22},{8,24},{10,26},{12,28},{14,30},{16,0},... | collective-permute-start | bytes 294920 | tf_op jit(solution)/shard_map/ppermute | solution.py:257
  66.0 7.6 %collective-permute-start.19 = (bf16[192,256]{1,0:T(8,128)(2,1)S(1)}, bf16[192,256]{1,0:T(8,128)(2,1)S(1)}, u32[]{:S(2)}, u32[]{:S(2)}) collective-permute-start(bf16[192,256]{1,0:T(8,128)(2,1)S(1)} %get-tuple-element.122), channel_id=1, source_target_pairs={{0,24},{2,26},{4,28},{6,30},{8,16},{10,18},{12,20},{14,22},{16,8},... | collective-permute-start | bytes 294920 | tf_op jit(solution)/shard_map/ppermute | solution.py:257
  68.4 6.5 %collective-permute-start.23 = (bf16[64,768]{1,0:T(8,128)(2,1)S(1)}, bf16[64,768]{1,0:T(8,128)(2,1)S(1)}, u32[]{:S(2)}, u32[]{:S(2)}) collective-permute-start(bf16[64,768]{1,0:T(8,128)(2,1)S(1)} %shard_map.110.refs_0_), channel_id=1, source_target_pairs={{0,2},{2,0},{4,6},{6,4},{8,10},{10,8},{12,14},{14,12},{16,18},{18,... | collective-permute-start | bytes 294920 | tf_op jit(solution)/shard_map/ppermute | solution.py:257
  68.4 6.5 %collective-permute-start.25 = (bf16[64,768]{1,0:T(8,128)(2,1)S(1)}, bf16[64,768]{1,0:T(8,128)(2,1)S(1)}, u32[]{:S(2)}, u32[]{:S(2)}) collective-permute-start(bf16[64,768]{1,0:T(8,128)(2,1)S(1)} %collective-permute-done.24.refs_2_), channel_id=1, source_target_pairs={{0,2},{2,0},{4,6},{6,4},{8,10},{10,8},{12,14},{14,12},{16,18},{18,... | collective-permute-start | bytes 294920 | tf_op jit(solution)/shard_map/ppermute | solution.py:257

commit v6 on v4

v6 whole, which is shorter than its diff:
```python
import functools

import jax
import jax.numpy as jnp
from jax import lax
from jax.experimental import pallas as pl
from jax.experimental.pallas import tpu as pltpu
from jax.sharding import PartitionSpec as P

TILE = 128
DEAD = 1024.0
BIAS = -1e30
LOG2_E = 1.4426950408889634
SAFE = 64.0
F32 = jnp.float32
BF16 = jnp.bfloat16
VMEM = pl.BlockSpec(memory_space=pltpu.VMEM)
SMEM = pl.BlockSpec(memory_space=pltpu.SMEM)
MIB = 1024 * 1024


def dot(a, b):
    return lax.dot_general(a, b, (((1,), (0,)), ((), ())), preferred_element_type=F32)


def dot_nt(a, b):
    return lax.dot_general(a, b, (((1,), (1,)), ((), ())), preferred_element_type=F32)


def call(kernel, outs, scratch=(), n_in=1, smem_first=False, after=0, micros=0.01, limit=16):
    specs = [SMEM if smem_first else VMEM] + [VMEM] * (n_in - 1) + [pl.BlockSpec(memory_space=pl.ANY)] * after
    return pl.pallas_call(
        kernel,
        out_shape=[jax.ShapeDtypeStruct(shape, kind) for shape, kind in outs],
        in_specs=specs,
        out_specs=[VMEM] * len(outs),
        scratch_shapes=list(scratch),
        compiler_params=pltpu.CompilerParams(vmem_limit_bytes=limit * MIB),
        cost_estimate=pl.CostEstimate(flops=int(micros * 1.15e9), bytes_accessed=0, transcendentals=0),
    )


def live_column(fill_ref, rows):
    parts = []
    within = lax.broadcasted_iota(jnp.int32, (TILE, 1), 0)
    for tile in range(rows // TILE):
        parts.append(jnp.where(within < fill_ref[tile], 1.0, 0.0))
    return jnp.concatenate(parts, axis=0) if len(parts) > 1 else parts[0]


def pack_kv_kernel(heads, rows, dim, a_of, fill_ref, kv_ref, *refs):
    outs, (held,) = refs[:heads], refs[heads:]
    live = live_column(fill_ref, rows)
    lane = lax.broadcasted_iota(jnp.int32, (rows, 2 * dim), 1)
    mark = jnp.where(lane == 0, DEAD, 0.0)
    for head in range(heads):
        held[head] = jnp.where(live > 0, kv_ref[:, head, :].astype(F32), mark).astype(BF16)
    me = a_of()
    for slot in range(heads):
        outs[slot][...] = held[me ^ slot]


def pack_qg_kernel(heads, rows, dim, a_of, fill_ref, q_ref, w_ref, go_ref, *refs):
    outs, (held,) = refs[:heads], refs[heads:]
    live = live_column(fill_ref, rows)
    mixed = jnp.where(live > 0, go_ref[...].astype(F32), 0.0).astype(BF16)
    for head in range(heads):
        held[head, 0:dim, :] = (q_ref[head].astype(F32) * dim**-0.5).astype(BF16)
        held[head, dim:, :] = dot_nt(w_ref[head], mixed).astype(BF16)
    me = a_of()
    for slot in range(heads):
        outs[slot][...] = held[me ^ slot]


def join_kernel(pieces, *refs):
    out_ref = refs[-1]
    rows = refs[0].shape[0]
    for index in range(pieces):
        out_ref[index * rows : (index + 1) * rows, :] = refs[index][...]


def join_q_kernel(slots, rows, dim, *refs):
    pieces, (qa_ref, q_ref, g_ref, norm_ref) = refs[:slots], refs[slots:]
    wide = 2 * dim
    row = lax.broadcasted_iota(jnp.int32, (dim, slots * rows), 0)
    qa_ref[dim:wide, :] = jnp.zeros((dim, slots * rows), BF16)
    qa_ref[wide : wide + dim, :] = jnp.where(row == 0, 1.0, 0.0).astype(BF16)
    for slot in range(slots):
        here = slice(slot * rows, (slot + 1) * rows)
        queries = pieces[slot][0:dim, :]
        q_ref[:, here] = queries
        g_ref[:, here] = pieces[slot][dim:, :]
        scaled = queries.astype(F32) * LOG2_E
        high = scaled.astype(BF16)
        qa_ref[0:dim, here] = high
        qa_ref[wide + dim :, here] = (scaled - high.astype(F32)).astype(BF16)
        norm_ref[:, here] = jnp.sum(scaled * scaled, axis=0, keepdims=True)


def prep_kernel(dim, pair_ref, wide_ref, kt_ref, vt_ref, norm_ref):
    wide = 2 * dim
    keys = pair_ref.shape[0]
    pair = pair_ref[...]
    full = pair.astype(F32)
    lane = lax.broadcasted_iota(jnp.int32, (keys, wide), 1)
    ones = jnp.where(lane <= 2, 1.0, 0.0)
    bias = jnp.where(full[:, 0:1] >= DEAD, BIAS, 0.0)
    extra = jnp.where(lane == 0, bias, ones)
    wide_ref[:, 0:wide] = pair
    wide_ref[:, wide:] = jnp.where(lane < dim, extra, pltpu.roll(full, dim, 1)).astype(BF16)
    turned = full.T
    kt_ref[...] = turned[:dim, :].astype(BF16)
    vt_ref[0:dim, :] = turned[dim:, :].astype(BF16)
    vt_ref[dim:, :] = jnp.ones((16, keys), BF16)
    norm = jnp.sum(turned[:dim, :] * turned[:dim, :], axis=0, keepdims=True)
    norm_ref[...] = jnp.where(turned[0:1, :] >= DEAD, 0.0, norm)


def score_kernel(slots, rows, dim, step, wide_ref, vt_ref, norm_ref, qa_ref, q_norm_ref, exp_ref, peak_ref, total_ref, score_ref):
    keys = wide_ref.shape[0]
    small = jnp.max(norm_ref[...]) * jnp.max(q_norm_ref[...]) <= SAFE * SAFE

    @pl.when(small)
    def _():
        peak_ref[...] = jnp.zeros_like(peak_ref)
        ahead = dot(wide_ref[...], qa_ref[:, 0:rows])
        for slot in range(slots):
            here = slice(slot * rows, (slot + 1) * rows)
            scores = ahead
            if slot + 1 < slots:
                ahead = dot(wide_ref[...], qa_ref[:, (slot + 1) * rows : (slot + 2) * rows])
            exps = jnp.exp2(scores).astype(BF16)
            exp_ref[:, here] = exps
            total_ref[:, here] = dot(vt_ref[...], exps)

    @pl.when(jnp.logical_not(small))
    def _():
        for slot in range(slots):
            here = slice(slot * rows, (slot + 1) * rows)
            top = jnp.full((8, rows), BIAS, F32)
            for start in range(0, keys, step):
                part = slice(start, start + step)
                scores = dot(wide_ref[part, :], qa_ref[:, here])
                score_ref[part, :] = scores
                top = jnp.maximum(top, jnp.max(scores.reshape(step // 8, 8, rows), axis=0))
            peak = jnp.max(top, axis=0, keepdims=True)
            peak_ref[:, here] = peak
            total = jnp.zeros((dim + 16, rows), F32)
            for start in range(0, keys, step):
                part = slice(start, start + step)
                exps = jnp.exp2(score_ref[part, :] - peak).astype(BF16)
                exp_ref[part, here] = exps
                total = total + dot(vt_ref[:, part], exps)
            total_ref[:, here] = total


def combine_kernel(slots, columns, rows, dim, *refs):
    peaks, totals, (g_ref,), outs = refs[:columns], refs[columns : 2 * columns], refs[2 * columns : 2 * columns + 1], refs[2 * columns + 1 :]
    att_out, factors_out, inner_ref = outs[:slots], outs[slots : slots + columns], outs[-1]
    peak = functools.reduce(jnp.maximum, [ref[...] for ref in peaks])
    factors = [jnp.exp2(ref[...] - peak) for ref in peaks]
    total = sum(factor * ref[...] for factor, ref in zip(factors, totals))
    inverse = 1.0 / total[dim : dim + 1, :]
    attended = (total[0:dim, :] * inverse).astype(BF16)
    for slot in range(slots):
        att_out[slot][...] = attended[:, slot * rows : (slot + 1) * rows]
    for factor, ref in zip(factors, factors_out):
        ref[...] = factor * inverse
    inner_ref[...] = jnp.sum(g_ref[...].astype(F32) * attended.astype(F32), axis=0, keepdims=True)


def back_kernel(slots, rows, dim, first, exp_ref, wide_ref, kt_ref, q_ref, g_ref, factor_ref, inner_ref, *refs):
    dkv_ref, dq_ref, ga_ref = refs[-3:]
    wide = 2 * dim
    block = g_ref.shape[1]
    factor = factor_ref[...]
    inner = inner_ref[...] * factor
    high = inner.astype(BF16).astype(F32)
    row = lax.broadcasted_iota(jnp.int32, (dim, block), 0)
    ga_ref[0:dim, :] = jnp.zeros((dim, block), BF16)
    ga_ref[dim:wide, :] = (g_ref[...].astype(F32) * factor).astype(BF16)
    ga_ref[wide : wide + dim, :] = jnp.where(row == 1, -high, jnp.where(row == 2, high - inner, 0.0)).astype(BF16)
    ga_ref[wide + dim :, :] = jnp.zeros((dim, block), BF16)
    grad_k = grad_v = None
    ahead = dot(wide_ref[...], ga_ref[:, 0:rows])
    for slot in range(slots):
        here = slice(slot * rows, (slot + 1) * rows)
        products = ahead
        if slot + 1 < slots:
            ahead = dot(wide_ref[...], ga_ref[:, (slot + 1) * rows : (slot + 2) * rows])
        exps = exp_ref[:, here]
        grads = exps * products.astype(BF16)
        term_v = dot_nt(ga_ref[dim:wide, here], exps)
        term_k = dot_nt(q_ref[:, here], grads)
        grad_v = term_v if grad_v is None else grad_v + term_v
        grad_k = term_k if grad_k is None else grad_k + term_k
        term = dot(kt_ref[...], grads)
        dq_ref[:, here] = term if first else refs[0][:, here] + term
    dkv_ref[dim:, :] = grad_v.astype(BF16)
    dkv_ref[0:dim, :] = grad_k.astype(BF16)


def project_grad_kernel(slots, rows, a_of, b_of, halves, fill_ref, go_ref, *refs):
    att, refs = refs[:slots], refs[slots + 1 :]
    live = live_column(fill_ref, rows)
    mixed = jnp.where(live > 0, go_ref[...].astype(F32), 0.0).astype(BF16)
    me = a_of()
    held = refs[-1]
    for slot in range(slots):
        held[me ^ slot] = dot(att[slot][...], mixed).astype(BF16)
    if not halves:
        refs[0][...] = held[...]
        return
    me = b_of()
    kept_ref, sent_ref = refs[0], refs[1]
    for pair in range(slots // 2):
        kept_ref[pair] = held[me ^ (2 * pair)]
        sent_ref[pair] = held[me ^ (2 * pair) ^ 1]


def project_kernel(slots, rows, a_of, fill_ref, w_ref, *refs):
    att, terms_ref = refs[:slots], refs[-1]
    me = a_of()
    total = None
    for slot in range(slots):
        term = dot(att[slot][...].astype(F32).T.astype(BF16), w_ref[me ^ slot])
        total = term if total is None else total + term
    terms_ref[...] = (total * live_column(fill_ref, rows)).astype(BF16)


def add_pairs_kernel(kept_ref, came_ref, _, first_ref, second_ref):
    for index, out_ref in enumerate((first_ref, second_ref)):
        out_ref[...] = (kept_ref[index].astype(F32) + came_ref[index].astype(F32)).astype(BF16)


def add_pieces_kernel(slots, rows, dim, kept_ref, came_ref, dq_ref, _, *outs):
    wide = 2 * dim
    for slot in range(slots):
        here = slice(slot * rows, (slot + 1) * rows)
        outs[slot][0:wide, :] = (kept_ref[:, here].astype(F32) + came_ref[:, here].astype(F32)).astype(BF16)
        outs[slot][wide:, :] = (dq_ref[:, here] * dim**-0.5).astype(BF16)


def add_out_kernel(a_ref, b_ref, out_ref, done_ref):
    out_ref[...] = (a_ref[...].astype(F32) + b_ref[...].astype(F32)).astype(out_ref.dtype)
    done_ref[...] = jnp.zeros_like(done_ref)


def add_kernel(a_ref, b_ref, *refs):
    refs[-1][...] = (a_ref[...].astype(F32) + b_ref[...].astype(F32)).astype(refs[-1].dtype)


def unpack_kernel(slots, rows, dim, a_of, *refs):
    pieces, (kv_out, q_out, held) = refs[:slots], refs[slots:]
    wide = 2 * dim
    me = a_of()
    for slot in range(slots):
        held[me ^ slot] = pieces[slot][0:wide, :].astype(F32).T
        q_out[me ^ slot] = pieces[slot][wide:, :].astype(F32)
    for head in range(slots):
        kv_out[:, head, :] = held[head]


def place_kernel(columns, b_of, *refs):
    parts, (out_ref,) = refs[:columns], refs[columns:]
    me = b_of()
    for column in range(columns):
        out_ref[me ^ column] = parts[column][...].astype(F32)


def shards(seq, mp, queries, key_value, tile_fill, out_weight, grad_output):
    rows, heads, dim = queries.shape
    width = grad_output.shape[1]
    slots = heads
    columns = seq // slots
    assert slots * columns == seq and columns & (columns - 1) == 0 and slots & (slots - 1) == 0
    a_of = lambda: lax.axis_index("seq") // columns
    b_of = lambda: lax.axis_index("seq") % columns

    def swap(array, mask, axis="seq", size=seq):
        return lax.ppermute(array, axis, [(i, i ^ mask) for i in range(size)])

    def exchange(pieces):
        came = {s: swap(pieces[s], s * columns) for s in sorted(range(1, slots), key=lambda s: (s < slots // 2, s))}
        return [pieces[0]] + [came[s] for s in range(1, slots)]

    block, wide = slots * rows, 2 * dim
    kv_mine = exchange(call(
        functools.partial(pack_kv_kernel, heads, rows, dim, a_of),
        [((rows, wide), BF16)] * slots, [pltpu.VMEM((heads, rows, wide), BF16)],
        n_in=2, smem_first=True, micros=1.5, limit=56,
    )(tile_fill, key_value))
    qg_send = call(
        functools.partial(pack_qg_kernel, heads, rows, dim, a_of),
        [((wide, rows), BF16)] * slots, [pltpu.VMEM((heads, wide, rows), BF16)],
        n_in=4, smem_first=True, micros=1,
    )(tile_fill, jnp.transpose(queries, (1, 2, 0)), out_weight, grad_output)
    qg_mine = exchange(qg_send)
    own = call(
        functools.partial(join_kernel, slots), [((block, wide), BF16)], n_in=slots, after=1,
    )(*kv_mine, qg_send[0])[0]

    blocks = {0: own}
    bit = columns // 2
    while bit:
        for r in sorted(blocks):
            blocks[r ^ bit] = swap(blocks[r], bit)
        bit //= 2

    qa, q_all, grads, q_norm = call(
        functools.partial(join_q_kernel, slots, rows, dim),
        [((2 * wide, block), BF16), ((dim, block), BF16), ((dim, block), BF16), ((1, block), F32)], n_in=slots,
    )(*qg_mine)
    step = min(block, 512)
    prepared, scored = {}, {}
    for r in range(columns):
        *prepared[r], values, norm = call(
            functools.partial(prep_kernel, dim),
            [((block, 2 * wide), BF16), ((dim, block), BF16), ((dim + 16, block), BF16), ((1, block), F32)],
        )(blocks[r])
        scored[r] = call(
            functools.partial(score_kernel, slots, rows, dim, step),
            [((block, block), BF16), ((1, block), F32), ((dim + 16, block), F32)],
            [pltpu.VMEM((block, rows), F32)], n_in=5, micros=1.5,
        )(prepared[r][0], values, norm, qa, q_norm)
    combined = call(
        functools.partial(combine_kernel, slots, columns, rows, dim),
        [((dim, rows), BF16)] * slots + [((1, block), F32)] * (columns + 1), n_in=2 * columns + 1,
    )(*[scored[r][1] for r in range(columns)], *[scored[r][2] for r in range(columns)], grads)
    att_mine, factors, inner = exchange(combined[:slots]), combined[slots:-1], combined[-1]

    halves = columns == heads == 4
    order = sorted(range(columns), key=lambda r: -int(f"{r:032b}"[::-1], 2))
    dkv, dq, terms, kept = {}, None, None, None
    for at, r in enumerate(order):
        later = []
        if at == columns // 2:
            weight_terms = call(
                functools.partial(project_grad_kernel, slots, rows, a_of, b_of, halves),
                [((2, dim, width), BF16)] * 2 if halves else [((heads, dim, width), BF16)],
                [pltpu.VMEM((heads, dim, width), BF16)],
                n_in=2 + slots, smem_first=True, after=1, micros=0.7,
            )(tile_fill, grad_output, *att_mine, dkv[order[at - 1]])
            terms = call(
                functools.partial(project_kernel, slots, rows, a_of), [((rows, width), BF16)],
                n_in=2 + slots, smem_first=True, after=1, micros=0.7,
            )(tile_fill, out_weight, *att_mine, weight_terms[-1])[0]
            later = [terms]
            if halves:
                kept, sent = call(add_pairs_kernel, [((dim, width), BF16)] * 2, n_in=2, after=1)(
                    weight_terms[0], swap(weight_terms[1], 1), terms)
                later = [kept]
        if at == columns - 1 and halves:
            kept = call(add_kernel, [((dim, width), BF16)], n_in=2, after=1)(kept, swap(sent, 2), dkv[order[at - 1]])[0]
            later = [kept]
        operands = [scored[r][0], *prepared[r], q_all, grads, factors[r], inner] + ([] if dq is None else [dq])
        dkv[r], dq = call(
            functools.partial(back_kernel, slots, rows, dim, dq is None),
            [((wide, block), BF16), ((dim, block), F32)], [pltpu.VMEM((2 * wide, block), BF16)],
            n_in=len(operands), after=len(later), micros=2,
        )(*operands, *later)

    bit, done = 1, terms
    while bit < mp:
        terms, done = call(add_out_kernel, [((rows, width), BF16), ((8, 128), F32)], n_in=2)(
            terms, swap(terms, bit, "mp", mp))
        bit *= 2

    dkv_last = dkv[order[-1]]
    bit = 1
    while 2 * bit < columns:
        dkv = {
            r: call(add_kernel, [((wide, block), BF16)], n_in=2)(dkv[r], swap(dkv[r ^ bit], bit))[0]
            for r in order if r in dkv and not r & bit
        }
        bit *= 2
    returned = exchange(call(
        functools.partial(add_pieces_kernel, slots, rows, dim), [((wide + dim, rows), BF16)] * slots, n_in=3, after=1,
    )(dkv[0], swap(dkv[bit], bit), dq, done))
    if halves:
        bit, last = columns, dkv_last
        while bit < seq:
            kept = call(add_kernel, [((dim, width), BF16)], n_in=2, after=1)(kept, swap(kept, bit), last)[0]
            bit *= 2
        across = swap(kept, 2)
        weight_grad = call(
            functools.partial(place_kernel, columns, b_of), [((heads, dim, width), F32)], n_in=columns, micros=0.5,
        )(kept, swap(kept, 1), across, swap(across, 1))[0]
    else:
        weight_grad = lax.psum(weight_terms[0].astype(F32), "seq")

    key_value_grad, query_grad = call(
        functools.partial(unpack_kernel, slots, rows, dim, a_of),
        [((rows, heads, wide), F32), ((heads, dim, rows), F32)],
        [pltpu.VMEM((heads, rows, wide), F32)], n_in=slots, micros=1,
    )(*returned)
    return terms, jnp.transpose(query_grad, (2, 0, 1)), key_value_grad, weight_grad


def solution(mesh):
    return jax.shard_map(
        functools.partial(shards, mesh.shape["seq"], mesh.shape["mp"]),
        mesh=mesh,
        in_specs=(
            P("seq", "mp", None),
            P("seq", "mp", None),
            P("seq"),
            P("mp", None, None),
            P("seq", None),
        ),
        out_specs=(P("seq", None), P("seq", "mp", None), P("seq", "mp", None), P("mp", None, None)),
        check_vma=False,
    )
```

time: 72.9 us -> 78.5 us (1.077)
  waiting for transfers between devices: 12.4 us -> 18.3 us
  Pallas kernels: 27.3 us -> 31 us
  starting transfers between devices: 30.4 us -> 28.1 us
  local copies, waits for them, and re-layouts: 1.69 us -> 0.02 us
    ppermute x26, waiting for transfers between devices: 12.4 us -> 18.3 us  [swap(): return lax.ppermute(array, axis, [(i, i ^ mask) for i in range(size)])]
    pallas_call x4, Pallas kernels: 7.89 us -> 10.9 us  [shards(): call(functools.partial(score_kernel, slots, rows, dim, step), [((block, b...]
    ppermute x26, starting transfers between devices: 30.4 us -> 28.1 us  [swap(): return lax.ppermute(array, axis, [(i, i ^ mask) for i in range(size)])]
    unnamed x12 -> x10, local copies, waits for them, and re-layouts: 1.69 us -> 0.02 us
    pallas_call x1, Pallas kernels: 1.4 us -> 2.58 us  [shards(): call(functools.partial(pack_kv_kernel, heads, rows, dim, a_of), [((rows,...]
    pallas_call x13 -> x14, Pallas kernels: 13.4 us -> 12.4 us  [the longest x4 9.07 us: shards(): call(functools.partial(back_kernel, slots, rows, dim, dq is None), [((wid...]
  transfers between devices with their start and end apart: 26 -> 26, of which waited for: 8 -> 11; matrix products, arithmetic and copies ran while one was open for 0% -> 0% of each run, Pallas kernels for 29% -> 30%
where the time goes in v6:
time: 78.5 us; the launch traced here: 78.4 us
  Pallas kernels  31 us (39%)
  starting transfers between devices  28.1 us (36%)
  waiting for transfers between devices  18.3 us (23%)
  between operations  0.95 us (1%)
    ppermute x26, starting transfers between devices, swap(): return lax.ppermute(array, axis, [(i, i ^ mask) for i in range(size)])  28.1 us
    ppermute x26, waiting for transfers between devices, swap(): return lax.ppermute(array, axis, [(i, i ^ mask) for i in range(size)])  18.3 us
    pallas_call x4, Pallas kernels, shards(): call(functools.partial(score_kernel, slots, rows, dim, step), [((block, b...  10.9 us
    pallas_call x4, Pallas kernels, shards(): call(functools.partial(back_kernel, slots, rows, dim, dq is None), [((wid...  9.07 us
    pallas_call x1, Pallas kernels, shards(): call(functools.partial(pack_kv_kernel, heads, rows, dim, a_of), [((rows,...  2.58 us
  transfers between devices with their start and end apart: 26, of which 11 were waited for; matrix products, arithmetic and copies ran while one was open for 0% of the time, Pallas kernels for 30%

profile of v6, /device:TPU:0, one launch (start us, length us, event | category | flops | bytes accessed | tf_op | source)
XLA Modules:
  0.0 78.4 jit_solution(14250158520011387502)
XLA Ops:
  0.7 2.6 %shard_map.84 = (bf16[256,128]{1,0:T(8,128)(2,1)}, bf16[256,128]{1,0:T(8,128)(2,1)}, bf16[256,128]{1,0:T(8,128)(2,1)}, bf16[256,128]{1,0:T(8,128)(2,1)}) custom-call(s32[2]{0:T(128)} %fill_ref.7, bf16[256,4,128]{2,1,0:T(4,128)(2,1)} %kv_ref.1), custom_call_target="tpu_custom_call" | custom-call | flops 1724999936 | tf_op jit(solution)/shard_map/pallas_call | solution.py:288
  3.2 3.0 %collective-permute-start = (bf16[256,128]{1,0:T(8,128)(2,1)}, bf16[256,128]{1,0:T(8,128)(2,1)S(1)}, u32[]{:S(2)}, u32[]{:S(2)}) collective-permute-start(bf16[256,128]{1,0:T(8,128)(2,1)} %get-tuple-element.74), channel_id=1, source_target_pairs={{0,8},{2,10},{4,12},{6,14},{8,0},{10,2},{12,4},{14,6},{16,24},{18,... | collective-permute-start | bytes 196616 | tf_op jit(solution)/shard_map/ppermute | solution.py:281
  6.3 2.6 %collective-permute-start.1 = (bf16[256,128]{1,0:T(8,128)(2,1)}, bf16[256,128]{1,0:T(8,128)(2,1)S(1)}, u32[]{:S(2)}, u32[]{:S(2)}) collective-permute-start(bf16[256,128]{1,0:T(8,128)(2,1)} %get-tuple-element.75), channel_id=1, source_target_pairs={{0,16},{2,18},{4,20},{6,22},{8,24},{10,26},{12,28},{14,30},{16,0},... | collective-permute-start | bytes 196616 | tf_op jit(solution)/shard_map/ppermute | solution.py:281
  8.9 0.0 copy-start
  8.9 1.2 %shard_map.85 = (bf16[128,256]{1,0:T(8,128)(2,1)S(1)}, bf16[128,256]{1,0:T(8,128)(2,1)S(1)}, bf16[128,256]{1,0:T(8,128)(2,1)S(1)}, bf16[128,256]{1,0:T(8,128)(2,1)S(1)}) custom-call(s32[2]{0:T(128)S(1)} %copy-done.4, bf16[4,64,256]{2,1,0:T(8,128)(2,1)S(1)} %bitcast.2, bf16[4,64,768]{2,1,0:T(8,128)(2,1)S(1)} %copy-done.2, bf16[256,768]{1,0:T(8,128)(2,1)S(1)} %copy-done.1), custom_call_target="tpu_custom_call" | custom-call | flops 1150000000 | tf_op jit(solution)/shard_map/pallas_call | solution.py:293
  10.2 3.6 %collective-permute-done.1.refs_2_ = bf16[256,128]{1,0:T(8,128)(2,1)S(1)} collective-permute-done((bf16[256,128]{1,0:T(8,128)(2,1)}, bf16[256,128]{1,0:T(8,128)(2,1)S(1)}, u32[]{:S(2)}, u32[]{:S(2)}) %collective-permute-start.1) | collective-permute-done | bytes 65568 | tf_op jit(solution)/shard_map/ppermute | solution.py:281
  13.7 1.4 %collective-permute-done.2.refs_3_ = bf16[256,128]{1,0:T(8,128)(2,1)S(1)} collective-permute-done((bf16[256,128]{1,0:T(8,128)(2,1)}, bf16[256,128]{1,0:T(8,128)(2,1)S(1)}, u32[]{:S(2)}, u32[]{:S(2)}) %collective-permute-start.2) | collective-permute-done | bytes 65568 | tf_op jit(solution)/shard_map/ppermute | solution.py:281
  15.2 1.6 %collective-permute-start.7 = (bf16[1024,128]{1,0:T(8,128)(2,1)S(1)}, bf16[1024,128]{1,0:T(8,128)(2,1)S(1)}, u32[]{:S(2)}, u32[]{:S(2)}) collective-permute-start(bf16[1024,128]{1,0:T(8,128)(2,1)S(1)} %shard_map.86.pair_ref), channel_id=1, source_target_pairs={{0,4},{2,6},{4,0},{6,2},{8,12},{10,14},{12,8},{14,10},{16,20},{18,... | collective-permute-start | bytes 786440 | tf_op jit(solution)/shard_map/ppermute | solution.py:281
  16.8 2.3 %collective-permute-start.4 = (bf16[128,256]{1,0:T(8,128)(2,1)S(1)}, bf16[128,256]{1,0:T(8,128)(2,1)S(1)}, u32[]{:S(2)}, u32[]{:S(2)}) collective-permute-start(bf16[128,256]{1,0:T(8,128)(2,1)S(1)} %get-tuple-element.82), channel_id=1, source_target_pairs={{0,16},{2,18},{4,20},{6,22},{8,24},{10,26},{12,28},{14,30},{16,0},... | collective-permute-start | bytes 196616 | tf_op jit(solution)/shard_map/ppermute | solution.py:281
  19.1 2.0 %collective-permute-start.5 = (bf16[128,256]{1,0:T(8,128)(2,1)S(1)}, bf16[128,256]{1,0:T(8,128)(2,1)S(1)}, u32[]{:S(2)}, u32[]{:S(2)}) collective-permute-start(bf16[128,256]{1,0:T(8,128)(2,1)S(1)} %get-tuple-element.83), channel_id=1, source_target_pairs={{0,24},{2,26},{4,28},{6,30},{8,16},{10,18},{12,20},{14,22},{16,8},... | collective-permute-start | bytes 196616 | tf_op jit(solution)/shard_map/ppermute | solution.py:281
  21.1 0.3 shard_map.87
  21.5 1.2 %collective-permute-done.3.refs_1_ = bf16[128,256]{1,0:T(8,128)(2,1)S(1)} collective-permute-done((bf16[128,256]{1,0:T(8,128)(2,1)S(1)}, bf16[128,256]{1,0:T(8,128)(2,1)S(1)}, u32[]{:S(2)}, u32[]{:S(2)}) %collective-permute-start.3) | collective-permute-done | bytes 65568 | tf_op jit(solution)/shard_map/ppermute | solution.py:281
  22.7 1.7 %collective-permute-done.4.refs_2_ = bf16[128,256]{1,0:T(8,128)(2,1)S(1)} collective-permute-done((bf16[128,256]{1,0:T(8,128)(2,1)S(1)}, bf16[128,256]{1,0:T(8,128)(2,1)S(1)}, u32[]{:S(2)}, u32[]{:S(2)}) %collective-permute-start.4) | collective-permute-done | bytes 65568 | tf_op jit(solution)/shard_map/ppermute | solution.py:281
  24.4 0.8 %collective-permute-done.5.refs_3_ = bf16[128,256]{1,0:T(8,128)(2,1)S(1)} collective-permute-done((bf16[128,256]{1,0:T(8,128)(2,1)S(1)}, bf16[128,256]{1,0:T(8,128)(2,1)S(1)}, u32[]{:S(2)}, u32[]{:S(2)}) %collective-permute-start.5) | collective-permute-done | bytes 65568 | tf_op jit(solution)/shard_map/ppermute | solution.py:281
  25.2 0.1 shard_map.88
  25.3 2.7 %shard_map.89 = (bf16[1024,1024]{1,0:T(8,128)(2,1)S(1)}, f32[1,1024]{1,0:T(1,128)S(1)}, f32[80,1024]{1,0:T(8,128)S(1)}) custom-call(bf16[1024,256]{1,0:T(8,128)(2,1)S(1)} %get-tuple-element.78.wide_ref, bf16[80,1024]{1,0:T(8,128)(2,1)S(1)} %get-tuple-element.79.vt_ref, f32[1,1024]{1,0:T(1,128)S(1)} %get-tuple-element.80.norm_ref, ...), custom_call_target="tpu_custom_call" | custom-call | flops 1724999936 | tf_op jit(solution)/shard_map/pallas_call | solution.py:321
  28.0 0.0 collective-permute-done.7.pair_ref
  28.0 0.1 collective-permute-start.8
  28.1 0.3 shard_map.92
  28.5 0.3 shard_map.90
  28.8 2.7 %shard_map.93 = (bf16[1024,1024]{1,0:T(8,128)(2,1)S(1)}, f32[1,1024]{1,0:T(1,128)S(1)}, f32[80,1024]{1,0:T(8,128)S(1)}) custom-call(bf16[1024,256]{1,0:T(8,128)(2,1)S(1)} %get-tuple-element.91.wide_ref, bf16[80,1024]{1,0:T(8,128)(2,1)S(1)} %get-tuple-element.92.vt_ref, f32[1,1024]{1,0:T(1,128)S(1)} %get-tuple-element.93.norm_ref, ...), custom_call_target="tpu_custom_call" | custom-call | flops 1724999936 | tf_op jit(solution)/shard_map/pallas_call | solution.py:321
  31.5 2.9 %shard_map.91 = (bf16[1024,1024]{1,0:T(8,128)(2,1)S(1)}, f32[1,1024]{1,0:T(1,128)S(1)}, f32[80,1024]{1,0:T(8,128)S(1)}) custom-call(bf16[1024,256]{1,0:T(8,128)(2,1)S(1)} %get-tuple-element.87.wide_ref, bf16[80,1024]{1,0:T(8,128)(2,1)S(1)} %get-tuple-element.88.vt_ref, f32[1,1024]{1,0:T(1,128)S(1)} %get-tuple-element.89.norm_ref, ...), custom_call_target="tpu_custom_call" | custom-call | flops 1724999936 | tf_op jit(solution)/shard_map/pallas_call | solution.py:321
  34.3 0.0 collective-permute-done.8.pair_ref
  34.3 0.3 shard_map.94
  34.7 2.7 %shard_map.95 = (bf16[1024,1024]{1,0:T(8,128)(2,1)S(1)}, f32[1,1024]{1,0:T(1,128)S(1)}, f32[80,1024]{1,0:T(8,128)S(1)}) custom-call(bf16[1024,256]{1,0:T(8,128)(2,1)S(1)} %get-tuple-element.95.wide_ref, bf16[80,1024]{1,0:T(8,128)(2,1)S(1)} %get-tuple-element.96.vt_ref, f32[1,1024]{1,0:T(1,128)S(1)} %get-tuple-element.97.norm_ref, ...), custom_call_target="tpu_custom_call" | custom-call | flops 1724999936 | tf_op jit(solution)/shard_map/pallas_call | solution.py:321
  37.3 0.2 shard_map.96
  37.5 1.9 %collective-permute-start.9 = (bf16[64,256]{1,0:T(8,128)(2,1)S(1)}, bf16[64,256]{1,0:T(8,128)(2,1)S(1)}, u32[]{:S(2)}, u32[]{:S(2)}) collective-permute-start(bf16[64,256]{1,0:T(8,128)(2,1)S(1)} %get-tuple-element.105), channel_id=1, source_target_pairs={{0,8},{2,10},{4,12},{6,14},{8,0},{10,2},{12,4},{14,6},{16,24},{18,... | collective-permute-start | bytes 98312 | tf_op jit(solution)/shard_map/ppermute | solution.py:281
  39.4 1.6 %collective-permute-start.10 = (bf16[64,256]{1,0:T(8,128)(2,1)S(1)}, bf16[64,256]{1,0:T(8,128)(2,1)S(1)}, u32[]{:S(2)}, u32[]{:S(2)}) collective-permute-start(bf16[64,256]{1,0:T(8,128)(2,1)S(1)} %get-tuple-element.106), channel_id=1, source_target_pairs={{0,16},{2,18},{4,20},{6,22},{8,24},{10,26},{12,28},{14,30},{16,0},... | collective-permute-start | bytes 98312 | tf_op jit(solution)/shard_map/ppermute | solution.py:281
  41.0 1.1 %collective-permute-start.11 = (bf16[64,256]{1,0:T(8,128)(2,1)S(1)}, bf16[64,256]{1,0:T(8,128)(2,1)S(1)}, u32[]{:S(2)}, u32[]{:S(2)}) collective-permute-start(bf16[64,256]{1,0:T(8,128)(2,1)S(1)} %get-tuple-element.107), channel_id=1, source_target_pairs={{0,24},{2,26},{4,28},{6,30},{8,16},{10,18},{12,20},{14,22},{16,8},... | collective-permute-start | bytes 98312 | tf_op jit(solution)/shard_map/ppermute | solution.py:281
  42.1 2.3 %shard_map.97 = (bf16[128,1024]{1,0:T(8,128)(2,1)S(1)}, f32[64,1024]{1,0:T(8,128)S(1)}) custom-call(bf16[1024,1024]{1,0:T(8,128)(2,1)S(1)} %get-tuple-element.113.exp_ref, bf16[1024,256]{1,0:T(8,128)(2,1)S(1)} %get-tuple-element.95.wide_ref, bf16[64,1024]{1,0:T(8,128)(2,1)S(1)} %get-tuple-element.114.kt_ref, bf16[64,1024]{1,0:T(8,128)(2,1)S(1)} %get-tuple-element.110.q_ref, ...), custom_call_target="tpu_custom_call" | custom-call | flops 2300000000 | tf_op jit(solution)/shard_map/pallas_call | solution.py:357
  44.3 2.3 %shard_map.98 = (bf16[128,1024]{1,0:T(8,128)(2,1)S(1)}, f32[64,1024]{1,0:T(8,128)S(1)}) custom-call(bf16[1024,1024]{1,0:T(8,128)(2,1)S(1)} %get-tuple-element.108.exp_ref, bf16[1024,256]{1,0:T(8,128)(2,1)S(1)} %get-tuple-element.87.wide_ref, bf16[64,1024]{1,0:T(8,128)(2,1)S(1)} %get-tuple-element.109.kt_ref, bf16[64,1024]{1,0:T(8,128)(2,1)S(1)} %get-tuple-element.110.q_ref, ...), custom_call_target="tpu_custom_call" | custom-call | flops 2300000000 | tf_op jit(solution)/shard_map/pallas_call | solution.py:357
  46.6 0.0 collective-permute-done.9.refs_1_
  46.6 0.0 collective-permute-done.11.refs_3_
  46.7 1.0 %shard_map.99 = (bf16[2,64,768]{2,1,0:T(8,128)(2,1)S(1)}, bf16[2,64,768]{2,1,0:T(8,128)(2,1)S(1)}) custom-call(s32[2]{0:T(128)S(1)} %copy-done.4, bf16[256,768]{1,0:T(8,128)(2,1)S(1)} %copy-done.1, bf16[64,256]{1,0:T(8,128)(2,1)S(1)} %get-tuple-element.104.refs_0_, bf16[64,256]{1,0:T(8,128)(2,1)S(1)} %collective-permute-done.9.refs_1_, ...), custom_call_target="tpu_custom_call" | custom-call | flops 805000000 | tf_op jit(solution)/shard_map/pallas_call | solution.py:338
  47.7 0.1 collective-permute-start.13
  47.8 0.5 collective-permute-start.15
  48.3 0.1 collective-permute-start.16
  48.4 1.2 %shard_map.100.a_ref._ = bf16[256,768]{1,0:T(8,128)(2,1)S(1)} custom-call(s32[2]{0:T(128)S(1)} %copy-done.4, bf16[4,64,768]{2,1,0:T(8,128)(2,1)S(1)} %copy-done.2, bf16[64,256]{1,0:T(8,128)(2,1)S(1)} %get-tuple-element.104.refs_0_, bf16[64,256]{1,0:T(8,128)(2,1)S(1)} %collective-permute-done.9.refs_1_, bf16[64,256]{1,0:T(8,128)(2,1)S(1)} %collective-permute-done.10.refs_2_, ...), custom_call_target="tpu_custom_call" | custom-call | flops 805000000 | tf_op jit(solution)/shard_map/pallas_call | solution.py:344
  49.5 1.5 %collective-permute-start.12 = (bf16[256,768]{1,0:T(8,128)(2,1)S(1)}, bf16[256,768]{1,0:T(8,128)(2,1)S(1)}, u32[]{:S(2)}, u32[]{:S(2)}) collective-permute-start(bf16[256,768]{1,0:T(8,128)(2,1)S(1)} %shard_map.100.a_ref._), channel_id=1, source_target_pairs={{0,1},{1,0},{2,3},{3,2},{4,5},{5,4},{6,7},{7,6},{8,9},{9,8},{10,11... | collective-permute-start | bytes 1179656 | tf_op jit(solution)/shard_map/ppermute | solution.py:281
  51.1 0.0 collective-permute-done.13.came_ref
  51.1 0.6 collective-permute-start.14
  51.7 2.3 %shard_map.103 = (bf16[128,1024]{1,0:T(8,128)(2,1)S(1)}, f32[64,1024]{1,0:T(8,128)S(1)}) custom-call(bf16[1024,1024]{1,0:T(8,128)(2,1)S(1)} %get-tuple-element.123.exp_ref, bf16[1024,256]{1,0:T(8,128)(2,1)S(1)} %get-tuple-element.91.wide_ref, bf16[64,1024]{1,0:T(8,128)(2,1)S(1)} %get-tuple-element.124.kt_ref, bf16[64,1024]{1,0:T(8,128)(2,1)S(1)} %get-tuple-element.110.q_ref, ...), custom_call_target="tpu_custom_call" | custom-call | flops 2300000000 | tf_op jit(solution)/shard_map/pallas_call | solution.py:357
  54.0 0.0 collective-permute-done.16.b_ref
  54.0 0.1 shard_map.107
  54.1 1.6 %collective-permute-start.17 = (bf16[128,1024]{1,0:T(8,128)(2,1)S(1)}, bf16[128,1024]{1,0:T(8,128)(2,1)S(1)}, u32[]{:S(2)}, u32[]{:S(2)}) collective-permute-start(bf16[128,1024]{1,0:T(8,128)(2,1)S(1)} %shard_map.107), channel_id=1, source_target_pairs={{0,4},{2,6},{4,0},{6,2},{8,12},{10,14},{12,8},{14,10},{16,20},{18,... | collective-permute-start | bytes 786440 | tf_op jit(solution)/shard_map/ppermute | solution.py:281
  55.7 0.4 collective-permute-done.14.b_ref
  56.1 0.8 %collective-permute-start.21 = (bf16[64,768]{1,0:T(8,128)(2,1)S(1)}, bf16[64,768]{1,0:T(8,128)(2,1)S(1)}, u32[]{:S(2)}, u32[]{:S(2)}) collective-permute-start(bf16[64,768]{1,0:T(8,128)(2,1)S(1)} %shard_map.104.refs_1_.a_ref), channel_id=1, source_target_pairs={{0,8},{2,10},{4,12},{6,14},{8,0},{10,2},{12,4},{14,6},{16,24},{18,... | collective-permute-start | bytes 294920 | tf_op jit(solution)/shard_map/ppermute | solution.py:281
  57.0 2.3 %shard_map.105 = (bf16[128,1024]{1,0:T(8,128)(2,1)S(1)}, f32[64,1024]{1,0:T(8,128)S(1)}) custom-call(bf16[1024,1024]{1,0:T(8,128)(2,1)S(1)} %get-tuple-element.120.exp_ref, bf16[1024,256]{1,0:T(8,128)(2,1)S(1)} %get-tuple-element.78.wide_ref, bf16[64,1024]{1,0:T(8,128)(2,1)S(1)} %get-tuple-element.121.kt_ref, bf16[64,1024]{1,0:T(8,128)(2,1)S(1)} %get-tuple-element.110.q_ref, ...), custom_call_target="tpu_custom_call" | custom-call | flops 2300000000 | tf_op jit(solution)/shard_map/pallas_call | solution.py:357
  59.2 1.6 %collective-permute-done.21.b_ref = bf16[64,768]{1,0:T(8,128)(2,1)S(1)} collective-permute-done((bf16[64,768]{1,0:T(8,128)(2,1)S(1)}, bf16[64,768]{1,0:T(8,128)(2,1)S(1)}, u32[]{:S(2)}, u32[]{:S(2)}) %collective-permute-start.21) | collective-permute-done | bytes 98336 | tf_op jit(solution)/shard_map/ppermute | solution.py:281
  60.8 2.1 %collective-permute-start.22 = (bf16[64,768]{1,0:T(8,128)(2,1)S(1)}, bf16[64,768]{1,0:T(8,128)(2,1)S(1)}, u32[]{:S(2)}, u32[]{:S(2)}) collective-permute-start(bf16[64,768]{1,0:T(8,128)(2,1)S(1)} %shard_map.110.a_ref), channel_id=1, source_target_pairs={{0,16},{2,18},{4,20},{6,22},{8,24},{10,26},{12,28},{14,30},{16,0},... | collective-permute-start | bytes 294920 | tf_op jit(solution)/shard_map/ppermute | solution.py:281
  62.9 0.1 shard_map.106.kept_ref
  63.0 0.0 collective-permute-done.12.b_ref
  63.0 0.8 %shard_map.101 = (bf16[256,768]{1,0:T(8,128)(2,1)}, f32[8,128]{1,0:T(8,128)S(1)}) custom-call(bf16[256,768]{1,0:T(8,128)(2,1)S(1)} %shard_map.100.a_ref._, bf16[256,768]{1,0:T(8,128)(2,1)S(1)} %collective-permute-done.12.b_ref), custom_call_target="tpu_custom_call" | custom-call | flops 11500000 | tf_op jit(solution)/shard_map/pallas_call | solution.py:365
  63.8 0.1 shard_map.108
  63.9 1.3 %collective-permute-start.18 = (bf16[192,256]{1,0:T(8,128)(2,1)S(1)}, bf16[192,256]{1,0:T(8,128)(2,1)S(1)}, u32[]{:S(2)}, u32[]{:S(2)}) collective-permute-start(bf16[192,256]{1,0:T(8,128)(2,1)S(1)} %get-tuple-element.137), channel_id=1, source_target_pairs={{0,8},{2,10},{4,12},{6,14},{8,0},{10,2},{12,4},{14,6},{16,24},{18,... | collective-permute-start | bytes 294920 | tf_op jit(solution)/shard_map/ppermute | solution.py:281
  65.2 2.2 %collective-permute-done.22.b_ref = bf16[64,768]{1,0:T(8,128)(2,1)S(1)} collective-permute-done((bf16[64,768]{1,0:T(8,128)(2,1)S(1)}, bf16[64,768]{1,0:T(8,128)(2,1)S(1)}, u32[]{:S(2)}, u32[]{:S(2)}) %collective-permute-start.22) | collective-permute-done | bytes 98336 | tf_op jit(solution)/shard_map/ppermute | solution.py:281
  67.4 0.6 collective-permute-start.24
  68.1 1.5 %collective-permute-start.19 = (bf16[192,256]{1,0:T(8,128)(2,1)S(1)}, bf16[192,256]{1,0:T(8,128)(2,1)S(1)}, u32[]{:S(2)}, u32[]{:S(2)}) collective-permute-start(bf16[192,256]{1,0:T(8,128)(2,1)S(1)} %get-tuple-element.138), channel_id=1, source_target_pairs={{0,16},{2,18},{4,20},{6,22},{8,24},{10,26},{12,28},{14,30},{16,0},... | collective-permute-start | bytes 294920 | tf_op jit(solution)/shard_map/ppermute | solution.py:281
  69.6 1.2 %collective-permute-start.20 = (bf16[192,256]{1,0:T(8,128)(2,1)S(1)}, bf16[192,256]{1,0:T(8,128)(2,1)S(1)}, u32[]{:S(2)}, u32[]{:S(2)}) collective-permute-start(bf16[192,256]{1,0:T(8,128)(2,1)S(1)} %get-tuple-element.139), channel_id=1, source_target_pairs={{0,24},{2,26},{4,28},{6,30},{8,16},{10,18},{12,20},{14,22},{16,8},... | collective-permute-start | bytes 294920 | tf_op jit(solution)/shard_map/ppermute | solution.py:281
  70.8 1.3 %collective-permute-done.24.refs_2_ = bf16[64,768]{1,0:T(8,128)(2,1)S(1)} collective-permute-done((bf16[64,768]{1,0:T(8,128)(2,1)S(1)}, bf16[64,768]{1,0:T(8,128)(2,1)S(1)}, u32[]{:S(2)}, u32[]{:S(2)}) %collective-permute-start.24) | collective-permute-done | bytes 98336 | tf_op jit(solution)/shard_map/ppermute | solution.py:281
  72.1 2.8 %collective-permute-done.19.refs_2_ = bf16[192,256]{1,0:T(8,128)(2,1)S(1)} collective-permute-done((bf16[192,256]{1,0:T(8,128)(2,1)S(1)}, bf16[192,256]{1,0:T(8,128)(2,1)S(1)}, u32[]{:S(2)}, u32[]{:S(2)}) %collective-permute-start.19) | collective-permute-done | bytes 98336 | tf_op jit(solution)/shard_map/ppermute | solution.py:281
  74.9 1.2 %collective-permute-done.20.refs_3_ = bf16[192,256]{1,0:T(8,128)(2,1)S(1)} collective-permute-done((bf16[192,256]{1,0:T(8,128)(2,1)S(1)}, bf16[192,256]{1,0:T(8,128)(2,1)S(1)}, u32[]{:S(2)}, u32[]{:S(2)}) %collective-permute-start.20) | collective-permute-done | bytes 98336 | tf_op jit(solution)/shard_map/ppermute | solution.py:281
  76.1 1.3 %shard_map.109 = (f32[256,4,128]{2,1,0:T(4,128)}, f32[4,64,256]{2,1,0:T(8,128)}) custom-call(bf16[192,256]{1,0:T(8,128)(2,1)S(1)} %get-tuple-element.136.refs_0_, bf16[192,256]{1,0:T(8,128)(2,1)S(1)} %collective-permute-done.18.refs_1_, bf16[192,256]{1,0:T(8,128)(2,1)S(1)} %collective-permute-done.19.refs_2_, ...), custom_call_target="tpu_custom_call" | custom-call | flops 1150000000 | tf_op jit(solution)/shard_map/pallas_call | solution.py:392
  77.4 0.9 %shard_map.112 = f32[4,64,768]{2,1,0:T(8,128)} custom-call(bf16[64,768]{1,0:T(8,128)(2,1)S(1)} %shard_map.111.refs_0_, bf16[64,768]{1,0:T(8,128)(2,1)S(1)} %collective-permute-done.23.refs_1_, bf16[64,768]{1,0:T(8,128)(2,1)S(1)} %collective-permute-done.24.refs_2_, bf16[64,768]{1,0:T(8,128)(2,1)S(1)} %collective-permute-done.25.refs_3_), custom_call_target="tpu_custom_call" | custom-call | flops 575000000 | tf_op jit(solution)/shard_map/pallas_call | solution.py:386
  (27 shorter events, 0.2 us)
Async XLA Ops:
  0.6 8.2 %copy-start.4 = (s32[2]{0:T(128)S(1)}, s32[2]{0:T(128)}, u32[]{:S(2)}) copy-start(s32[2]{0:T(128)} %fill_ref.7) | copy-start | bytes 28
  0.6 8.2 %copy-start.1 = (bf16[256,768]{1,0:T(8,128)(2,1)S(1)}, bf16[256,768]{1,0:T(8,128)(2,1)}, u32[]{:S(2)}) copy-start(bf16[256,768]{1,0:T(8,128)(2,1)} %go_ref.3) | copy-start | bytes 1179652
  0.7 8.2 %copy-start.2 = (bf16[4,64,768]{2,1,0:T(8,128)(2,1)S(1)}, bf16[4,64,768]{2,1,0:T(8,128)(2,1)}, u32[]{:S(2)}) copy-start(bf16[4,64,768]{2,1,0:T(8,128)(2,1)} %w_ref.3) | copy-start | bytes 1179652
  0.7 8.2 %copy-start.3 = (bf16[256,4,64]{0,2,1:T(8,128)(2,1)S(1)}, bf16[256,4,64]{0,2,1:T(8,128)(2,1)}, u32[]{:S(2)}) copy-start(bf16[256,4,64]{0,2,1:T(8,128)(2,1)} %param.5) | copy-start | bytes 393220
  3.2 6.9 %collective-permute-start = (bf16[256,128]{1,0:T(8,128)(2,1)}, bf16[256,128]{1,0:T(8,128)(2,1)S(1)}, u32[]{:S(2)}, u32[]{:S(2)}) collective-permute-start(bf16[256,128]{1,0:T(8,128)(2,1)} %get-tuple-element.74), channel_id=1, source_target_pairs={{0,8},{2,10},{4,12},{6,14},{8,0},{10,2},{12,4},{14,6},{16,24},{18,... | collective-permute-start | bytes 196616 | tf_op jit(solution)/shard_map/ppermute | solution.py:281
  6.3 7.5 %collective-permute-start.1 = (bf16[256,128]{1,0:T(8,128)(2,1)}, bf16[256,128]{1,0:T(8,128)(2,1)S(1)}, u32[]{:S(2)}, u32[]{:S(2)}) collective-permute-start(bf16[256,128]{1,0:T(8,128)(2,1)} %get-tuple-element.75), channel_id=1, source_target_pairs={{0,16},{2,18},{4,20},{6,22},{8,24},{10,26},{12,28},{14,30},{16,0},... | collective-permute-start | bytes 196616 | tf_op jit(solution)/shard_map/ppermute | solution.py:281
  8.9 6.3 %collective-permute-start.2 = (bf16[256,128]{1,0:T(8,128)(2,1)}, bf16[256,128]{1,0:T(8,128)(2,1)S(1)}, u32[]{:S(2)}, u32[]{:S(2)}) collective-permute-start(bf16[256,128]{1,0:T(8,128)(2,1)} %get-tuple-element.76), channel_id=1, source_target_pairs={{0,24},{2,26},{4,28},{6,30},{8,16},{10,18},{12,20},{14,22},{16,8},... | collective-permute-start | bytes 196616 | tf_op jit(solution)/shard_map/ppermute | solution.py:281
  8.9 6.3 %copy-start = (bf16[256,128]{1,0:T(8,128)(2,1)S(1)}, bf16[256,128]{1,0:T(8,128)(2,1)}, u32[]{:S(2)}) copy-start(bf16[256,128]{1,0:T(8,128)(2,1)} %get-tuple-element.73.refs_0_) | copy-start | bytes 196612
  15.2 12.9 %collective-permute-start.7 = (bf16[1024,128]{1,0:T(8,128)(2,1)S(1)}, bf16[1024,128]{1,0:T(8,128)(2,1)S(1)}, u32[]{:S(2)}, u32[]{:S(2)}) collective-permute-start(bf16[1024,128]{1,0:T(8,128)(2,1)S(1)} %shard_map.86.pair_ref), channel_id=1, source_target_pairs={{0,4},{2,6},{4,0},{6,2},{8,12},{10,14},{12,8},{14,10},{16,20},{18,... | collective-permute-start | bytes 786440 | tf_op jit(solution)/shard_map/ppermute | solution.py:281
  16.8 11.7 %collective-permute-start.6 = (bf16[1024,128]{1,0:T(8,128)(2,1)S(1)}, bf16[1024,128]{1,0:T(8,128)(2,1)S(1)}, u32[]{:S(2)}, u32[]{:S(2)}) collective-permute-start(bf16[1024,128]{1,0:T(8,128)(2,1)S(1)} %shard_map.86.pair_ref), channel_id=1, source_target_pairs={{0,2},{2,0},{4,6},{6,4},{8,10},{10,8},{12,14},{14,12},{16,18},{18,... | collective-permute-start | bytes 786440 | tf_op jit(solution)/shard_map/ppermute | solution.py:281
  16.8 5.9 %collective-permute-start.3 = (bf16[128,256]{1,0:T(8,128)(2,1)S(1)}, bf16[128,256]{1,0:T(8,128)(2,1)S(1)}, u32[]{:S(2)}, u32[]{:S(2)}) collective-permute-start(bf16[128,256]{1,0:T(8,128)(2,1)S(1)} %get-tuple-element.81), channel_id=1, source_target_pairs={{0,8},{2,10},{4,12},{6,14},{8,0},{10,2},{12,4},{14,6},{16,24},{18,... | collective-permute-start | bytes 196616 | tf_op jit(solution)/shard_map/ppermute | solution.py:281
  16.8 7.6 %collective-permute-start.4 = (bf16[128,256]{1,0:T(8,128)(2,1)S(1)}, bf16[128,256]{1,0:T(8,128)(2,1)S(1)}, u32[]{:S(2)}, u32[]{:S(2)}) collective-permute-start(bf16[128,256]{1,0:T(8,128)(2,1)S(1)} %get-tuple-element.82), channel_id=1, source_target_pairs={{0,16},{2,18},{4,20},{6,22},{8,24},{10,26},{12,28},{14,30},{16,0},... | collective-permute-start | bytes 196616 | tf_op jit(solution)/shard_map/ppermute | solution.py:281
  19.1 6.1 %collective-permute-start.5 = (bf16[128,256]{1,0:T(8,128)(2,1)S(1)}, bf16[128,256]{1,0:T(8,128)(2,1)S(1)}, u32[]{:S(2)}, u32[]{:S(2)}) collective-permute-start(bf16[128,256]{1,0:T(8,128)(2,1)S(1)} %get-tuple-element.83), channel_id=1, source_target_pairs={{0,24},{2,26},{4,28},{6,30},{8,16},{10,18},{12,20},{14,22},{16,8},... | collective-permute-start | bytes 196616 | tf_op jit(solution)/shard_map/ppermute | solution.py:281
  28.0 6.3 %collective-permute-start.8 = (bf16[1024,128]{1,0:T(8,128)(2,1)S(1)}, bf16[1024,128]{1,0:T(8,128)(2,1)S(1)}, u32[]{:S(2)}, u32[]{:S(2)}) collective-permute-start(bf16[1024,128]{1,0:T(8,128)(2,1)S(1)} %collective-permute-done.7.pair_ref), channel_id=1, source_target_pairs={{0,2},{2,0},{4,6},{6,4},{8,10},{10,8},{12,14},{14,12},{16,18},{18,... | collective-permute-start | bytes 786440 | tf_op jit(solution)/shard_map/ppermute | solution.py:281
  37.5 9.1 %collective-permute-start.9 = (bf16[64,256]{1,0:T(8,128)(2,1)S(1)}, bf16[64,256]{1,0:T(8,128)(2,1)S(1)}, u32[]{:S(2)}, u32[]{:S(2)}) collective-permute-start(bf16[64,256]{1,0:T(8,128)(2,1)S(1)} %get-tuple-element.105), channel_id=1, source_target_pairs={{0,8},{2,10},{4,12},{6,14},{8,0},{10,2},{12,4},{14,6},{16,24},{18,... | collective-permute-start | bytes 98312 | tf_op jit(solution)/shard_map/ppermute | solution.py:281
  39.4 7.3 %collective-permute-start.10 = (bf16[64,256]{1,0:T(8,128)(2,1)S(1)}, bf16[64,256]{1,0:T(8,128)(2,1)S(1)}, u32[]{:S(2)}, u32[]{:S(2)}) collective-permute-start(bf16[64,256]{1,0:T(8,128)(2,1)S(1)} %get-tuple-element.106), channel_id=1, source_target_pairs={{0,16},{2,18},{4,20},{6,22},{8,24},{10,26},{12,28},{14,30},{16,0},... | collective-permute-start | bytes 98312 | tf_op jit(solution)/shard_map/ppermute | solution.py:281
  41.0 5.7 %collective-permute-start.11 = (bf16[64,256]{1,0:T(8,128)(2,1)S(1)}, bf16[64,256]{1,0:T(8,128)(2,1)S(1)}, u32[]{:S(2)}, u32[]{:S(2)}) collective-permute-start(bf16[64,256]{1,0:T(8,128)(2,1)S(1)} %get-tuple-element.107), channel_id=1, source_target_pairs={{0,24},{2,26},{4,28},{6,30},{8,16},{10,18},{12,20},{14,22},{16,8},... | collective-permute-start | bytes 98312 | tf_op jit(solution)/shard_map/ppermute | solution.py:281
  47.7 3.4 %collective-permute-start.13 = (bf16[2,64,768]{2,1,0:T(8,128)(2,1)S(1)}, bf16[2,64,768]{2,1,0:T(8,128)(2,1)S(1)}, u32[]{:S(2)}, u32[]{:S(2)}) collective-permute-start(bf16[2,64,768]{2,1,0:T(8,128)(2,1)S(1)} %get-tuple-element.118.refs_4_), channel_id=1, source_target_pairs={{0,2},{2,0},{4,6},{6,4},{8,10},{10,8},{12,14},{14,12},{16,18},{18,... | collective-permute-start | bytes 589832 | tf_op jit(solution)/shard_map/ppermute | solution.py:281
  47.8 15.1 %collective-permute-start.15 = (bf16[128,1024]{1,0:T(8,128)(2,1)S(1)}, bf16[128,1024]{1,0:T(8,128)(2,1)S(1)}, u32[]{:S(2)}, u32[]{:S(2)}) collective-permute-start(bf16[128,1024]{1,0:T(8,128)(2,1)S(1)} %get-tuple-element.117.refs_4_), channel_id=1, source_target_pairs={{0,2},{2,0},{4,6},{6,4},{8,10},{10,8},{12,14},{14,12},{16,18},{18,... | collective-permute-start | bytes 786440 | tf_op jit(solution)/shard_map/ppermute | solution.py:281
  48.3 5.7 %collective-permute-start.16 = (bf16[128,1024]{1,0:T(8,128)(2,1)S(1)}, bf16[128,1024]{1,0:T(8,128)(2,1)S(1)}, u32[]{:S(2)}, u32[]{:S(2)}) collective-permute-start(bf16[128,1024]{1,0:T(8,128)(2,1)S(1)} %get-tuple-element.133), channel_id=1, source_target_pairs={{0,2},{2,0},{4,6},{6,4},{8,10},{10,8},{12,14},{14,12},{16,18},{18,... | collective-permute-start | bytes 786440 | tf_op jit(solution)/shard_map/ppermute | solution.py:281
  49.5 13.4 %collective-permute-start.12 = (bf16[256,768]{1,0:T(8,128)(2,1)S(1)}, bf16[256,768]{1,0:T(8,128)(2,1)S(1)}, u32[]{:S(2)}, u32[]{:S(2)}) collective-permute-start(bf16[256,768]{1,0:T(8,128)(2,1)S(1)} %shard_map.100.a_ref._), channel_id=1, source_target_pairs={{0,1},{1,0},{2,3},{3,2},{4,5},{5,4},{6,7},{7,6},{8,9},{9,8},{10,11... | collective-permute-start | bytes 1179656 | tf_op jit(solution)/shard_map/ppermute | solution.py:281
  51.1 4.9 %collective-permute-start.14 = (bf16[64,768]{1,0:T(8,128)(2,1)S(1)}, bf16[64,768]{1,0:T(8,128)(2,1)S(1)}, u32[]{:S(2)}, u32[]{:S(2)}) collective-permute-start(bf16[64,768]{1,0:T(8,128)(2,1)S(1)} %get-tuple-element.130), channel_id=1, source_target_pairs={{0,4},{2,6},{4,0},{6,2},{8,12},{10,14},{12,8},{14,10},{16,20},{18,... | collective-permute-start | bytes 294920 | tf_op jit(solution)/shard_map/ppermute | solution.py:281
  54.1 9.7 %collective-permute-start.17 = (bf16[128,1024]{1,0:T(8,128)(2,1)S(1)}, bf16[128,1024]{1,0:T(8,128)(2,1)S(1)}, u32[]{:S(2)}, u32[]{:S(2)}) collective-permute-start(bf16[128,1024]{1,0:T(8,128)(2,1)S(1)} %shard_map.107), channel_id=1, source_target_pairs={{0,4},{2,6},{4,0},{6,2},{8,12},{10,14},{12,8},{14,10},{16,20},{18,... | collective-permute-start | bytes 786440 | tf_op jit(solution)/shard_map/ppermute | solution.py:281
  56.1 4.7 %collective-permute-start.21 = (bf16[64,768]{1,0:T(8,128)(2,1)S(1)}, bf16[64,768]{1,0:T(8,128)(2,1)S(1)}, u32[]{:S(2)}, u32[]{:S(2)}) collective-permute-start(bf16[64,768]{1,0:T(8,128)(2,1)S(1)} %shard_map.104.refs_1_.a_ref), channel_id=1, source_target_pairs={{0,8},{2,10},{4,12},{6,14},{8,0},{10,2},{12,4},{14,6},{16,24},{18,... | collective-permute-start | bytes 294920 | tf_op jit(solution)/shard_map/ppermute | solution.py:281
  60.8 6.6 %collective-permute-start.22 = (bf16[64,768]{1,0:T(8,128)(2,1)S(1)}, bf16[64,768]{1,0:T(8,128)(2,1)S(1)}, u32[]{:S(2)}, u32[]{:S(2)}) collective-permute-start(bf16[64,768]{1,0:T(8,128)(2,1)S(1)} %shard_map.110.a_ref), channel_id=1, source_target_pairs={{0,16},{2,18},{4,20},{6,22},{8,24},{10,26},{12,28},{14,30},{16,0},... | collective-permute-start | bytes 294920 | tf_op jit(solution)/shard_map/ppermute | solution.py:281
  63.9 8.2 %collective-permute-start.18 = (bf16[192,256]{1,0:T(8,128)(2,1)S(1)}, bf16[192,256]{1,0:T(8,128)(2,1)S(1)}, u32[]{:S(2)}, u32[]{:S(2)}) collective-permute-start(bf16[192,256]{1,0:T(8,128)(2,1)S(1)} %get-tuple-element.137), channel_id=1, source_target_pairs={{0,8},{2,10},{4,12},{6,14},{8,0},{10,2},{12,4},{14,6},{16,24},{18,... | collective-permute-start | bytes 294920 | tf_op jit(solution)/shard_map/ppermute | solution.py:281
  67.4 4.7 %collective-permute-start.24 = (bf16[64,768]{1,0:T(8,128)(2,1)S(1)}, bf16[64,768]{1,0:T(8,128)(2,1)S(1)}, u32[]{:S(2)}, u32[]{:S(2)}) collective-permute-start(bf16[64,768]{1,0:T(8,128)(2,1)S(1)} %shard_map.111.refs_0_), channel_id=1, source_target_pairs={{0,4},{2,6},{4,0},{6,2},{8,12},{10,14},{12,8},{14,10},{16,20},{18,... | collective-permute-start | bytes 294920 | tf_op jit(solution)/shard_map/ppermute | solution.py:281
  68.1 6.9 %collective-permute-start.19 = (bf16[192,256]{1,0:T(8,128)(2,1)S(1)}, bf16[192,256]{1,0:T(8,128)(2,1)S(1)}, u32[]{:S(2)}, u32[]{:S(2)}) collective-permute-start(bf16[192,256]{1,0:T(8,128)(2,1)S(1)} %get-tuple-element.138), channel_id=1, source_target_pairs={{0,16},{2,18},{4,20},{6,22},{8,24},{10,26},{12,28},{14,30},{16,0},... | collective-permute-start | bytes 294920 | tf_op jit(solution)/shard_map/ppermute | solution.py:281
  69.6 6.5 %collective-permute-start.20 = (bf16[192,256]{1,0:T(8,128)(2,1)S(1)}, bf16[192,256]{1,0:T(8,128)(2,1)S(1)}, u32[]{:S(2)}, u32[]{:S(2)}) collective-permute-start(bf16[192,256]{1,0:T(8,128)(2,1)S(1)} %get-tuple-element.139), channel_id=1, source_target_pairs={{0,24},{2,26},{4,28},{6,30},{8,16},{10,18},{12,20},{14,22},{16,8},... | collective-permute-start | bytes 294920 | tf_op jit(solution)/shard_map/ppermute | solution.py:281
  70.8 6.7 %collective-permute-start.23 = (bf16[64,768]{1,0:T(8,128)(2,1)S(1)}, bf16[64,768]{1,0:T(8,128)(2,1)S(1)}, u32[]{:S(2)}, u32[]{:S(2)}) collective-permute-start(bf16[64,768]{1,0:T(8,128)(2,1)S(1)} %shard_map.111.refs_0_), channel_id=1, source_target_pairs={{0,2},{2,0},{4,6},{6,4},{8,10},{10,8},{12,14},{14,12},{16,18},{18,... | collective-permute-start | bytes 294920 | tf_op jit(solution)/shard_map/ppermute | solution.py:281
  72.1 5.3 %collective-permute-start.25 = (bf16[64,768]{1,0:T(8,128)(2,1)S(1)}, bf16[64,768]{1,0:T(8,128)(2,1)S(1)}, u32[]{:S(2)}, u32[]{:S(2)}) collective-permute-start(bf16[64,768]{1,0:T(8,128)(2,1)S(1)} %collective-permute-done.24.refs_2_), channel_id=1, source_target_pairs={{0,2},{2,0},{4,6},{6,4},{8,10},{10,8},{12,14},{14,12},{16,18},{18,... | collective-permute-start | bytes 294920 | tf_op jit(solution)/shard_map/ppermute | solution.py:281

commit v7 on v6

--- a/solution.py
+++ b/solution.py
@@ -48,28 +48,33 @@
     return jnp.concatenate(parts, axis=0) if len(parts) > 1 else parts[0]
 
 
+def spread(slots):
+    return [0] + sorted(range(1, slots), key=lambda mask: (mask < slots // 2, mask))
+
+
 def pack_kv_kernel(heads, rows, dim, a_of, fill_ref, kv_ref, *refs):
     outs, (held,) = refs[:heads], refs[heads:]
     live = live_column(fill_ref, rows)
     lane = lax.broadcasted_iota(jnp.int32, (rows, 2 * dim), 1)
-    mark = jnp.where(lane == 0, DEAD, 0.0)
+    mark = jnp.where(lane == 0, DEAD * (1.0 - live), 0.0).astype(BF16)
+    live = live.astype(BF16)
     for head in range(heads):
-        held[head] = jnp.where(live > 0, kv_ref[:, head, :].astype(F32), mark).astype(BF16)
+        held[head] = kv_ref[:, head, :] * live + mark
     me = a_of()
-    for slot in range(heads):
-        outs[slot][...] = held[me ^ slot]
+    for slot, mask in enumerate(spread(heads)):
+        outs[slot][...] = held[me ^ mask]
 
 
 def pack_qg_kernel(heads, rows, dim, a_of, fill_ref, q_ref, w_ref, go_ref, *refs):
     outs, (held,) = refs[:heads], refs[heads:]
-    live = live_column(fill_ref, rows)
-    mixed = jnp.where(live > 0, go_ref[...].astype(F32), 0.0).astype(BF16)
+    mixed = go_ref[...] * live_column(fill_ref, rows).astype(BF16)
+    grads = dot_nt(w_ref[...].reshape(heads * dim, mixed.shape[1]), mixed).astype(BF16)
     for head in range(heads):
         held[head, 0:dim, :] = (q_ref[head].astype(F32) * dim**-0.5).astype(BF16)
-        held[head, dim:, :] = dot_nt(w_ref[head], mixed).astype(BF16)
+        held[head, dim:, :] = grads[head * dim : (head + 1) * dim, :]
     me = a_of()
-    for slot in range(heads):
-        outs[slot][...] = held[me ^ slot]
+    for slot, mask in enumerate(spread(heads)):
+        outs[slot][...] = held[me ^ mask]
 
 
 def join_kernel(pieces, *refs):
@@ -202,12 +207,13 @@
 
 def project_grad_kernel(slots, rows, a_of, b_of, halves, fill_ref, go_ref, *refs):
     att, refs = refs[:slots], refs[slots + 1 :]
-    live = live_column(fill_ref, rows)
-    mixed = jnp.where(live > 0, go_ref[...].astype(F32), 0.0).astype(BF16)
+    mixed = go_ref[...] * live_column(fill_ref, rows).astype(BF16)
     me = a_of()
     held = refs[-1]
-    for slot in range(slots):
-        held[me ^ slot] = dot(att[slot][...], mixed).astype(BF16)
+    dim = held.shape[1]
+    grads = dot(jnp.concatenate([ref[...] for ref in att], axis=0), mixed).astype(BF16)
+    for slot, mask in enumerate(spread(slots)):
+        held[me ^ mask] = grads[slot * dim : (slot + 1) * dim, :]
     if not halves:
         refs[0][...] = held[...]
         return
@@ -221,11 +227,9 @@
 def project_kernel(slots, rows, a_of, fill_ref, w_ref, *refs):
     att, terms_ref = refs[:slots], refs[-1]
     me = a_of()
-    total = None
-    for slot in range(slots):
-        term = dot(att[slot][...].astype(F32).T.astype(BF16), w_ref[me ^ slot])
-        total = term if total is None else total + term
-    terms_ref[...] = (total * live_column(fill_ref, rows)).astype(BF16)
+    rows_in = jnp.concatenate([ref[...] for ref in att], axis=0).astype(F32).T.astype(BF16)
+    weights = jnp.concatenate([w_ref[me ^ mask] for mask in spread(slots)], axis=0)
+    terms_ref[...] = (dot(rows_in, weights) * live_column(fill_ref, rows)).astype(BF16)
 
 
 def add_pairs_kernel(kept_ref, came_ref, _, first_ref, second_ref):
@@ -254,9 +258,9 @@
     pieces, (kv_out, q_out, held) = refs[:slots], refs[slots:]
     wide = 2 * dim
     me = a_of()
-    for slot in range(slots):
-        held[me ^ slot] = pieces[slot][0:wide, :].astype(F32).T
-        q_out[me ^ slot] = pieces[slot][wide:, :].astype(F32)
+    for slot, mask in enumerate(spread(slots)):
+        held[me ^ mask] = pieces[slot][0:wide, :].astype(F32).T
+        q_out[me ^ mask] = pieces[slot][wide:, :].astype(F32)
     for head in range(slots):
         kv_out[:, head, :] = held[head]
 
@@ -281,8 +285,7 @@
         return lax.ppermute(array, axis, [(i, i ^ mask) for i in range(size)])
 
     def exchange(pieces):
-        came = {s: swap(pieces[s], s * columns) for s in sorted(range(1, slots), key=lambda s: (s < slots // 2, s))}
-        return [pieces[0]] + [came[s] for s in range(1, slots)]
+        return [pieces[0]] + [swap(piece, mask * columns) for piece, mask in zip(pieces[1:], spread(slots)[1:])]
 
     block, wide = slots * rows, 2 * dim
     kv_mine = exchange(call(
@@ -298,7 +301,7 @@
     qg_mine = exchange(qg_send)
     own = call(
         functools.partial(join_kernel, slots), [((block, wide), BF16)], n_in=slots, after=1,
-    )(*kv_mine, qg_send[0])[0]
+    )(*kv_mine, qg_mine[-1])[0]
 
     blocks = {0: own}
     bit = columns // 2
@@ -378,10 +381,8 @@
         functools.partial(add_pieces_kernel, slots, rows, dim), [((wide + dim, rows), BF16)] * slots, n_in=3, after=1,
     )(dkv[0], swap(dkv[bit], bit), dq, done))
     if halves:
-        bit, last = columns, dkv_last
-        while bit < seq:
-            kept = call(add_kernel, [((dim, width), BF16)], n_in=2, after=1)(kept, swap(kept, bit), last)[0]
-            bit *= 2
+        for mask in [seq >> step for step in range(1, slots.bit_length())]:
+            kept = call(add_kernel, [((dim, width), BF16)], n_in=2, after=1)(kept, swap(kept, mask), dkv_last)[0]
         across = swap(kept, 2)
         weight_grad = call(
             functools.partial(place_kernel, columns, b_of), [((heads, dim, width), F32)], n_in=columns, micros=0.5,

time: 78.5 us -> 83.6 us (1.065)
  local copies, waits for them, and re-layouts: 0.02 us -> 4.4 us
  Pallas kernels: 31 us -> 30.1 us
  waiting for transfers between devices: 18.3 us -> 19.2 us
    unnamed x10 -> x16, local copies, waits for them, and re-layouts: 0.02 us -> 4.4 us
    ppermute x26, waiting for transfers between devices: 18.3 us -> 19.2 us  [swap(): return lax.ppermute(array, axis, [(i, i ^ mask) for i in range(size)])]
  transfers between devices with their start and end apart: 26 -> 26, of which waited for: 11 -> 9; matrix products, arithmetic and copies ran while one was open for 0% -> 0% of each run, Pallas kernels for 30% -> 29%
where the time goes in v7:
time: 83.6 us; the launch traced here: 83.3 us
  Pallas kernels  30.1 us (36%)
  starting transfers between devices  28.7 us (34%)
  waiting for transfers between devices  19.2 us (23%)
  local copies, waits for them, and re-layouts  4.4 us (5%)
  between operations  0.94 us (1%)
    ppermute x26, starting transfers between devices, swap(): return lax.ppermute(array, axis, [(i, i ^ mask) for i in range(size)])  28.7 us
    ppermute x26, waiting for transfers between devices, swap(): return lax.ppermute(array, axis, [(i, i ^ mask) for i in range(size)])  19.2 us
    pallas_call x4, Pallas kernels, shards(): call(functools.partial(score_kernel, slots, rows, dim, step), [((block, b...  10.9 us
    pallas_call x4, Pallas kernels, shards(): call(functools.partial(back_kernel, slots, rows, dim, dq is None), [((wid...  9.07 us
    unnamed x16, local copies, waits for them, and re-layouts  4.4 us
    pallas_call x1, Pallas kernels, shards(): call(functools.partial(pack_kv_kernel, heads, rows, dim, a_of), [((rows,...  2.46 us
  transfers between devices with their start and end apart: 26, of which 9 were waited for; matrix products, arithmetic and copies ran while one was open for 0% of the time, Pallas kernels for 29%

profile of v7, /device:TPU:0, one launch (start us, length us, event | category | flops | bytes accessed | tf_op | source)
XLA Modules:
  0.0 83.3 jit_solution(1569580260122385346)
XLA Ops:
  0.6 0.0 copy-start.1
  0.6 1.0 %copy-done.1 = bf16[256,768]{1,0:T(8,128)(2,1)S(1)} copy-done((bf16[256,768]{1,0:T(8,128)(2,1)S(1)}, bf16[256,768]{1,0:T(8,128)(2,1)}, u32[]{:S(2)}) %copy-start.1) | copy-done | bytes 393240
  1.6 1.0 %copy-done.3 = bf16[4,64,768]{2,1,0:T(8,128)(2,1)S(1)} copy-done((bf16[4,64,768]{2,1,0:T(8,128)(2,1)S(1)}, bf16[4,64,768]{2,1,0:T(8,128)(2,1)}, u32[]{:S(2)}) %copy-start.3) | copy-done | bytes 393240
  2.6 0.9 %copy-done.5 = bf16[256,4,64]{0,2,1:T(8,128)(2,1)S(1)} copy-done((bf16[256,4,64]{0,2,1:T(8,128)(2,1)S(1)}, bf16[256,4,64]{0,2,1:T(8,128)(2,1)}, u32[]{:S(2)}) %copy-start.5) | copy-done | bytes 131096
  3.5 0.7 copy-done.6
  4.2 0.9 %shard_map.85 = (bf16[128,256]{1,0:T(8,128)(2,1)S(1)}, bf16[128,256]{1,0:T(8,128)(2,1)S(1)}, bf16[128,256]{1,0:T(8,128)(2,1)S(1)}, bf16[128,256]{1,0:T(8,128)(2,1)S(1)}) custom-call(s32[2]{0:T(128)S(1)} %copy-done.6, bf16[4,64,256]{2,1,0:T(8,128)(2,1)S(1)} %bitcast.2, bf16[4,64,768]{2,1,0:T(8,128)(2,1)S(1)} %copy-done.3, bf16[256,768]{1,0:T(8,128)(2,1)S(1)} %copy-done.1), custom_call_target="tpu_custom_call" | custom-call | flops 1150000000 | tf_op jit(solution)/shard_map/pallas_call | solution.py:296
  5.1 3.1 %collective-permute-start.3 = (bf16[128,256]{1,0:T(8,128)(2,1)S(1)}, bf16[128,256]{1,0:T(8,128)(2,1)S(1)}, u32[]{:S(2)}, u32[]{:S(2)}) collective-permute-start(bf16[128,256]{1,0:T(8,128)(2,1)S(1)} %get-tuple-element.77), channel_id=1, source_target_pairs={{0,8},{2,10},{4,12},{6,14},{8,0},{10,2},{12,4},{14,6},{16,24},{18,... | collective-permute-start | bytes 196616 | tf_op jit(solution)/shard_map/ppermute | solution.py:285
  8.2 2.5 %shard_map.84 = (bf16[256,128]{1,0:T(8,128)(2,1)}, bf16[256,128]{1,0:T(8,128)(2,1)}, bf16[256,128]{1,0:T(8,128)(2,1)}, bf16[256,128]{1,0:T(8,128)(2,1)}) custom-call(s32[2]{0:T(128)} %fill_ref.7, bf16[256,4,128]{2,1,0:T(4,128)(2,1)} %kv_ref.1), custom_call_target="tpu_custom_call" | custom-call | flops 1724999936 | tf_op jit(solution)/shard_map/pallas_call | solution.py:291
  10.7 2.6 %collective-permute-start = (bf16[256,128]{1,0:T(8,128)(2,1)}, bf16[256,128]{1,0:T(8,128)(2,1)S(1)}, u32[]{:S(2)}, u32[]{:S(2)}) collective-permute-start(bf16[256,128]{1,0:T(8,128)(2,1)} %get-tuple-element.74), channel_id=1, source_target_pairs={{0,16},{2,18},{4,20},{6,22},{8,24},{10,26},{12,28},{14,30},{16,0},... | collective-permute-start | bytes 196616 | tf_op jit(solution)/shard_map/ppermute | solution.py:285
  13.3 0.0 collective-permute-start.1
  13.3 0.9 %collective-permute-start.2 = (bf16[256,128]{1,0:T(8,128)(2,1)}, bf16[256,128]{1,0:T(8,128)(2,1)S(1)}, u32[]{:S(2)}, u32[]{:S(2)}) collective-permute-start(bf16[256,128]{1,0:T(8,128)(2,1)} %get-tuple-element.76), channel_id=1, source_target_pairs={{0,8},{2,10},{4,12},{6,14},{8,0},{10,2},{12,4},{14,6},{16,24},{18,... | collective-permute-start | bytes 196616 | tf_op jit(solution)/shard_map/ppermute | solution.py:285
  14.2 0.0 collective-permute-done.3.refs_4_.refs_3_
  14.2 2.9 %collective-permute-done.refs_1_ = bf16[256,128]{1,0:T(8,128)(2,1)S(1)} collective-permute-done((bf16[256,128]{1,0:T(8,128)(2,1)}, bf16[256,128]{1,0:T(8,128)(2,1)S(1)}, u32[]{:S(2)}, u32[]{:S(2)}) %collective-permute-start) | collective-permute-done | bytes 65568 | tf_op jit(solution)/shard_map/ppermute | solution.py:285
  17.1 2.5 %collective-permute-done.1.refs_2_ = bf16[256,128]{1,0:T(8,128)(2,1)S(1)} collective-permute-done((bf16[256,128]{1,0:T(8,128)(2,1)}, bf16[256,128]{1,0:T(8,128)(2,1)S(1)}, u32[]{:S(2)}, u32[]{:S(2)}) %collective-permute-start.1) | collective-permute-done | bytes 65568 | tf_op jit(solution)/shard_map/ppermute | solution.py:285
  19.6 0.8 %copy-done = bf16[256,128]{1,0:T(8,128)(2,1)S(1)} copy-done((bf16[256,128]{1,0:T(8,128)(2,1)S(1)}, bf16[256,128]{1,0:T(8,128)(2,1)}, u32[]{:S(2)}) %copy-start) | copy-done | bytes 65560
  20.4 1.6 %collective-permute-start.7 = (bf16[1024,128]{1,0:T(8,128)(2,1)S(1)}, bf16[1024,128]{1,0:T(8,128)(2,1)S(1)}, u32[]{:S(2)}, u32[]{:S(2)}) collective-permute-start(bf16[1024,128]{1,0:T(8,128)(2,1)S(1)} %shard_map.86.pair_ref), channel_id=1, source_target_pairs={{0,4},{2,6},{4,0},{6,2},{8,12},{10,14},{12,8},{14,10},{16,20},{18,... | collective-permute-start | bytes 786440 | tf_op jit(solution)/shard_map/ppermute | solution.py:285
  22.0 1.6 %collective-permute-start.4 = (bf16[128,256]{1,0:T(8,128)(2,1)S(1)}, bf16[128,256]{1,0:T(8,128)(2,1)S(1)}, u32[]{:S(2)}, u32[]{:S(2)}) collective-permute-start(bf16[128,256]{1,0:T(8,128)(2,1)S(1)} %get-tuple-element.82), channel_id=1, source_target_pairs={{0,16},{2,18},{4,20},{6,22},{8,24},{10,26},{12,28},{14,30},{16,0},... | collective-permute-start | bytes 196616 | tf_op jit(solution)/shard_map/ppermute | solution.py:285
  23.6 1.1 %collective-permute-start.5 = (bf16[128,256]{1,0:T(8,128)(2,1)S(1)}, bf16[128,256]{1,0:T(8,128)(2,1)S(1)}, u32[]{:S(2)}, u32[]{:S(2)}) collective-permute-start(bf16[128,256]{1,0:T(8,128)(2,1)S(1)} %get-tuple-element.83), channel_id=1, source_target_pairs={{0,24},{2,26},{4,28},{6,30},{8,16},{10,18},{12,20},{14,22},{16,8},... | collective-permute-start | bytes 196616 | tf_op jit(solution)/shard_map/ppermute | solution.py:285
  24.7 0.3 shard_map.87
  25.0 5.1 %collective-permute-done.4.refs_1_ = bf16[128,256]{1,0:T(8,128)(2,1)S(1)} collective-permute-done((bf16[128,256]{1,0:T(8,128)(2,1)S(1)}, bf16[128,256]{1,0:T(8,128)(2,1)S(1)}, u32[]{:S(2)}, u32[]{:S(2)}) %collective-permute-start.4) | collective-permute-done | bytes 65568 | tf_op jit(solution)/shard_map/ppermute | solution.py:285
  30.1 0.1 shard_map.88
  30.2 2.7 %shard_map.89 = (bf16[1024,1024]{1,0:T(8,128)(2,1)S(1)}, f32[1,1024]{1,0:T(1,128)S(1)}, f32[80,1024]{1,0:T(8,128)S(1)}) custom-call(bf16[1024,256]{1,0:T(8,128)(2,1)S(1)} %get-tuple-element.78.wide_ref, bf16[80,1024]{1,0:T(8,128)(2,1)S(1)} %get-tuple-element.79.vt_ref, f32[1,1024]{1,0:T(1,128)S(1)} %get-tuple-element.80.norm_ref, ...), custom_call_target="tpu_custom_call" | custom-call | flops 1724999936 | tf_op jit(solution)/shard_map/pallas_call | solution.py:324
  32.9 0.1 collective-permute-start.8
  33.0 0.3 shard_map.92
  33.3 0.3 shard_map.90
  33.7 2.7 %shard_map.93 = (bf16[1024,1024]{1,0:T(8,128)(2,1)S(1)}, f32[1,1024]{1,0:T(1,128)S(1)}, f32[80,1024]{1,0:T(8,128)S(1)}) custom-call(bf16[1024,256]{1,0:T(8,128)(2,1)S(1)} %get-tuple-element.91.wide_ref, bf16[80,1024]{1,0:T(8,128)(2,1)S(1)} %get-tuple-element.92.vt_ref, f32[1,1024]{1,0:T(1,128)S(1)} %get-tuple-element.93.norm_ref, ...), custom_call_target="tpu_custom_call" | custom-call | flops 1724999936 | tf_op jit(solution)/shard_map/pallas_call | solution.py:324
  36.4 2.9 %shard_map.91 = (bf16[1024,1024]{1,0:T(8,128)(2,1)S(1)}, f32[1,1024]{1,0:T(1,128)S(1)}, f32[80,1024]{1,0:T(8,128)S(1)}) custom-call(bf16[1024,256]{1,0:T(8,128)(2,1)S(1)} %get-tuple-element.87.wide_ref, bf16[80,1024]{1,0:T(8,128)(2,1)S(1)} %get-tuple-element.88.vt_ref, f32[1,1024]{1,0:T(1,128)S(1)} %get-tuple-element.89.norm_ref, ...), custom_call_target="tpu_custom_call" | custom-call | flops 1724999936 | tf_op jit(solution)/shard_map/pallas_call | solution.py:324
  39.2 0.3 shard_map.94
  39.6 2.7 %shard_map.95 = (bf16[1024,1024]{1,0:T(8,128)(2,1)S(1)}, f32[1,1024]{1,0:T(1,128)S(1)}, f32[80,1024]{1,0:T(8,128)S(1)}) custom-call(bf16[1024,256]{1,0:T(8,128)(2,1)S(1)} %get-tuple-element.95.wide_ref, bf16[80,1024]{1,0:T(8,128)(2,1)S(1)} %get-tuple-element.96.vt_ref, f32[1,1024]{1,0:T(1,128)S(1)} %get-tuple-element.97.norm_ref, ...), custom_call_target="tpu_custom_call" | custom-call | flops 1724999936 | tf_op jit(solution)/shard_map/pallas_call | solution.py:324
  42.2 0.2 shard_map.96
  42.4 3.1 %collective-permute-start.9 = (bf16[64,256]{1,0:T(8,128)(2,1)S(1)}, bf16[64,256]{1,0:T(8,128)(2,1)S(1)}, u32[]{:S(2)}, u32[]{:S(2)}) collective-permute-start(bf16[64,256]{1,0:T(8,128)(2,1)S(1)} %get-tuple-element.105), channel_id=1, source_target_pairs={{0,16},{2,18},{4,20},{6,22},{8,24},{10,26},{12,28},{14,30},{16,0},... | collective-permute-start | bytes 98312 | tf_op jit(solution)/shard_map/ppermute | solution.py:285
  45.5 1.2 %collective-permute-start.10 = (bf16[64,256]{1,0:T(8,128)(2,1)S(1)}, bf16[64,256]{1,0:T(8,128)(2,1)S(1)}, u32[]{:S(2)}, u32[]{:S(2)}) collective-permute-start(bf16[64,256]{1,0:T(8,128)(2,1)S(1)} %get-tuple-element.106), channel_id=1, source_target_pairs={{0,24},{2,26},{4,28},{6,30},{8,16},{10,18},{12,20},{14,22},{16,8},... | collective-permute-start | bytes 98312 | tf_op jit(solution)/shard_map/ppermute | solution.py:285
  46.8 2.3 %shard_map.97 = (bf16[128,1024]{1,0:T(8,128)(2,1)S(1)}, f32[64,1024]{1,0:T(8,128)S(1)}) custom-call(bf16[1024,1024]{1,0:T(8,128)(2,1)S(1)} %get-tuple-element.113.exp_ref, bf16[1024,256]{1,0:T(8,128)(2,1)S(1)} %get-tuple-element.95.wide_ref, bf16[64,1024]{1,0:T(8,128)(2,1)S(1)} %get-tuple-element.114.kt_ref, bf16[64,1024]{1,0:T(8,128)(2,1)S(1)} %get-tuple-element.110.q_ref, ...), custom_call_target="tpu_custom_call" | custom-call | flops 2300000000 | tf_op jit(solution)/shard_map/pallas_call | solution.py:360
  49.1 0.0 copy-start.2
  49.1 0.0 copy-start.7
  49.1 2.3 %shard_map.98 = (bf16[128,1024]{1,0:T(8,128)(2,1)S(1)}, f32[64,1024]{1,0:T(8,128)S(1)}) custom-call(bf16[1024,1024]{1,0:T(8,128)(2,1)S(1)} %get-tuple-element.108.exp_ref, bf16[1024,256]{1,0:T(8,128)(2,1)S(1)} %get-tuple-element.87.wide_ref, bf16[64,1024]{1,0:T(8,128)(2,1)S(1)} %get-tuple-element.109.kt_ref, bf16[64,1024]{1,0:T(8,128)(2,1)S(1)} %get-tuple-element.110.q_ref, ...), custom_call_target="tpu_custom_call" | custom-call | flops 2300000000 | tf_op jit(solution)/shard_map/pallas_call | solution.py:360
  51.4 0.0 copy-start.4
  51.4 0.9 %shard_map.99 = (bf16[2,64,768]{2,1,0:T(8,128)(2,1)S(1)}, bf16[2,64,768]{2,1,0:T(8,128)(2,1)S(1)}) custom-call(s32[2]{0:T(128)S(1)} %copy-done.7, bf16[256,768]{1,0:T(8,128)(2,1)S(1)} %copy-done.2, bf16[64,256]{1,0:T(8,128)(2,1)S(1)} %get-tuple-element.104.refs_0_, bf16[64,256]{1,0:T(8,128)(2,1)S(1)} %collective-permute-done.9.refs_1_, ...), custom_call_target="tpu_custom_call" | custom-call | flops 805000000 | tf_op jit(solution)/shard_map/pallas_call | solution.py:341
  52.4 0.1 collective-permute-start.13
  52.4 0.5 collective-permute-start.15
  52.9 0.1 collective-permute-start.16
  53.0 0.8 %shard_map.100.a_ref._ = bf16[256,768]{1,0:T(8,128)(2,1)S(1)} custom-call(s32[2]{0:T(128)S(1)} %copy-done.7, bf16[4,64,768]{2,1,0:T(8,128)(2,1)S(1)} %copy-done.4, bf16[64,256]{1,0:T(8,128)(2,1)S(1)} %get-tuple-element.104.refs_0_, bf16[64,256]{1,0:T(8,128)(2,1)S(1)} %collective-permute-done.9.refs_1_, bf16[64,256]{1,0:T(8,128)(2,1)S(1)} %collective-permute-done.10.refs_2_, ...), custom_call_target="tpu_custom_call" | custom-call | flops 805000000 | tf_op jit(solution)/shard_map/pallas_call | solution.py:347
  53.9 1.6 %collective-permute-start.12 = (bf16[256,768]{1,0:T(8,128)(2,1)S(1)}, bf16[256,768]{1,0:T(8,128)(2,1)S(1)}, u32[]{:S(2)}, u32[]{:S(2)}) collective-permute-start(bf16[256,768]{1,0:T(8,128)(2,1)S(1)} %shard_map.100.a_ref._), channel_id=1, source_target_pairs={{0,1},{1,0},{2,3},{3,2},{4,5},{5,4},{6,7},{7,6},{8,9},{9,8},{10,11... | collective-permute-start | bytes 1179656 | tf_op jit(solution)/shard_map/ppermute | solution.py:285
  55.5 0.6 collective-permute-start.14
  56.1 2.3 %shard_map.103 = (bf16[128,1024]{1,0:T(8,128)(2,1)S(1)}, f32[64,1024]{1,0:T(8,128)S(1)}) custom-call(bf16[1024,1024]{1,0:T(8,128)(2,1)S(1)} %get-tuple-element.123.exp_ref, bf16[1024,256]{1,0:T(8,128)(2,1)S(1)} %get-tuple-element.91.wide_ref, bf16[64,1024]{1,0:T(8,128)(2,1)S(1)} %get-tuple-element.124.kt_ref, bf16[64,1024]{1,0:T(8,128)(2,1)S(1)} %get-tuple-element.110.q_ref, ...), custom_call_target="tpu_custom_call" | custom-call | flops 2300000000 | tf_op jit(solution)/shard_map/pallas_call | solution.py:360
  58.3 0.1 shard_map.107
  58.4 1.6 %collective-permute-start.17 = (bf16[128,1024]{1,0:T(8,128)(2,1)S(1)}, bf16[128,1024]{1,0:T(8,128)(2,1)S(1)}, u32[]{:S(2)}, u32[]{:S(2)}) collective-permute-start(bf16[128,1024]{1,0:T(8,128)(2,1)S(1)} %shard_map.107), channel_id=1, source_target_pairs={{0,4},{2,6},{4,0},{6,2},{8,12},{10,14},{12,8},{14,10},{16,20},{18,... | collective-permute-start | bytes 786440 | tf_op jit(solution)/shard_map/ppermute | solution.py:285
  60.0 0.4 collective-permute-done.14.b_ref
  60.4 3.2 %collective-permute-start.21 = (bf16[64,768]{1,0:T(8,128)(2,1)S(1)}, bf16[64,768]{1,0:T(8,128)(2,1)S(1)}, u32[]{:S(2)}, u32[]{:S(2)}) collective-permute-start(bf16[64,768]{1,0:T(8,128)(2,1)S(1)} %shard_map.104.refs_1_.a_ref), channel_id=1, source_target_pairs={{0,16},{2,18},{4,20},{6,22},{8,24},{10,26},{12,28},{14,30},{16,0},... | collective-permute-start | bytes 294920 | tf_op jit(solution)/shard_map/ppermute | solution.py:285
  63.6 2.3 %shard_map.105 = (bf16[128,1024]{1,0:T(8,128)(2,1)S(1)}, f32[64,1024]{1,0:T(8,128)S(1)}) custom-call(bf16[1024,1024]{1,0:T(8,128)(2,1)S(1)} %get-tuple-element.120.exp_ref, bf16[1024,256]{1,0:T(8,128)(2,1)S(1)} %get-tuple-element.78.wide_ref, bf16[64,1024]{1,0:T(8,128)(2,1)S(1)} %get-tuple-element.121.kt_ref, bf16[64,1024]{1,0:T(8,128)(2,1)S(1)} %get-tuple-element.110.q_ref, ...), custom_call_target="tpu_custom_call" | custom-call | flops 2300000000 | tf_op jit(solution)/shard_map/pallas_call | solution.py:360
  65.9 2.2 %collective-permute-done.21.b_ref = bf16[64,768]{1,0:T(8,128)(2,1)S(1)} collective-permute-done((bf16[64,768]{1,0:T(8,128)(2,1)S(1)}, bf16[64,768]{1,0:T(8,128)(2,1)S(1)}, u32[]{:S(2)}, u32[]{:S(2)}) %collective-permute-start.21) | collective-permute-done | bytes 98336 | tf_op jit(solution)/shard_map/ppermute | solution.py:285
  68.1 0.1 collective-permute-start.22
  68.2 0.1 shard_map.106.kept_ref
  68.3 0.8 %shard_map.101 = (bf16[256,768]{1,0:T(8,128)(2,1)}, f32[8,128]{1,0:T(8,128)S(1)}) custom-call(bf16[256,768]{1,0:T(8,128)(2,1)S(1)} %shard_map.100.a_ref._, bf16[256,768]{1,0:T(8,128)(2,1)S(1)} %collective-permute-done.12.b_ref), custom_call_target="tpu_custom_call" | custom-call | flops 11500000 | tf_op jit(solution)/shard_map/pallas_call | solution.py:368
  69.2 0.1 shard_map.108
  69.2 3.1 %collective-permute-start.18 = (bf16[192,256]{1,0:T(8,128)(2,1)S(1)}, bf16[192,256]{1,0:T(8,128)(2,1)S(1)}, u32[]{:S(2)}, u32[]{:S(2)}) collective-permute-start(bf16[192,256]{1,0:T(8,128)(2,1)S(1)} %get-tuple-element.137), channel_id=1, source_target_pairs={{0,16},{2,18},{4,20},{6,22},{8,24},{10,26},{12,28},{14,30},{16,0},... | collective-permute-start | bytes 294920 | tf_op jit(solution)/shard_map/ppermute | solution.py:285
  72.4 1.1 %collective-permute-done.22.b_ref = bf16[64,768]{1,0:T(8,128)(2,1)S(1)} collective-permute-done((bf16[64,768]{1,0:T(8,128)(2,1)S(1)}, bf16[64,768]{1,0:T(8,128)(2,1)S(1)}, u32[]{:S(2)}, u32[]{:S(2)}) %collective-permute-start.22) | collective-permute-done | bytes 98336 | tf_op jit(solution)/shard_map/ppermute | solution.py:285
  73.5 0.1 collective-permute-start.24
  73.6 2.4 %collective-permute-start.19 = (bf16[192,256]{1,0:T(8,128)(2,1)S(1)}, bf16[192,256]{1,0:T(8,128)(2,1)S(1)}, u32[]{:S(2)}, u32[]{:S(2)}) collective-permute-start(bf16[192,256]{1,0:T(8,128)(2,1)S(1)} %get-tuple-element.138), channel_id=1, source_target_pairs={{0,24},{2,26},{4,28},{6,30},{8,16},{10,18},{12,20},{14,22},{16,8},... | collective-permute-start | bytes 294920 | tf_op jit(solution)/shard_map/ppermute | solution.py:285
  76.0 2.2 %collective-permute-done.24.refs_2_ = bf16[64,768]{1,0:T(8,128)(2,1)S(1)} collective-permute-done((bf16[64,768]{1,0:T(8,128)(2,1)S(1)}, bf16[64,768]{1,0:T(8,128)(2,1)S(1)}, u32[]{:S(2)}, u32[]{:S(2)}) %collective-permute-start.24) | collective-permute-done | bytes 98336 | tf_op jit(solution)/shard_map/ppermute | solution.py:285
  78.2 1.9 %collective-permute-done.19.refs_2_ = bf16[192,256]{1,0:T(8,128)(2,1)S(1)} collective-permute-done((bf16[192,256]{1,0:T(8,128)(2,1)S(1)}, bf16[192,256]{1,0:T(8,128)(2,1)S(1)}, u32[]{:S(2)}, u32[]{:S(2)}) %collective-permute-start.19) | collective-permute-done | bytes 98336 | tf_op jit(solution)/shard_map/ppermute | solution.py:285
  80.1 1.0 %collective-permute-done.20.refs_3_ = bf16[192,256]{1,0:T(8,128)(2,1)S(1)} collective-permute-done((bf16[192,256]{1,0:T(8,128)(2,1)S(1)}, bf16[192,256]{1,0:T(8,128)(2,1)S(1)}, u32[]{:S(2)}, u32[]{:S(2)}) %collective-permute-start.20) | collective-permute-done | bytes 98336 | tf_op jit(solution)/shard_map/ppermute | solution.py:285
  81.1 1.3 %shard_map.109 = (f32[256,4,128]{2,1,0:T(4,128)}, f32[4,64,256]{2,1,0:T(8,128)}) custom-call(bf16[192,256]{1,0:T(8,128)(2,1)S(1)} %get-tuple-element.136.refs_0_, bf16[192,256]{1,0:T(8,128)(2,1)S(1)} %collective-permute-done.18.refs_1_, bf16[192,256]{1,0:T(8,128)(2,1)S(1)} %collective-permute-done.19.refs_2_, ...), custom_call_target="tpu_custom_call" | custom-call | flops 1150000000 | tf_op jit(solution)/shard_map/pallas_call | solution.py:393
  82.4 0.9 %shard_map.112 = f32[4,64,768]{2,1,0:T(8,128)} custom-call(bf16[64,768]{1,0:T(8,128)(2,1)S(1)} %shard_map.111.refs_0_, bf16[64,768]{1,0:T(8,128)(2,1)S(1)} %collective-permute-done.23.refs_1_, bf16[64,768]{1,0:T(8,128)(2,1)S(1)} %collective-permute-done.24.refs_2_, bf16[64,768]{1,0:T(8,128)(2,1)S(1)} %collective-permute-done.25.refs_3_), custom_call_target="tpu_custom_call" | custom-call | flops 575000000 | tf_op jit(solution)/shard_map/pallas_call | solution.py:387
  (33 shorter events, 0.2 us)
Async XLA Ops:
  0.6 1.0 %copy-start.1 = (bf16[256,768]{1,0:T(8,128)(2,1)S(1)}, bf16[256,768]{1,0:T(8,128)(2,1)}, u32[]{:S(2)}) copy-start(bf16[256,768]{1,0:T(8,128)(2,1)} %go_ref.3) | copy-start | bytes 1179652
  1.6 1.0 %copy-start.3 = (bf16[4,64,768]{2,1,0:T(8,128)(2,1)S(1)}, bf16[4,64,768]{2,1,0:T(8,128)(2,1)}, u32[]{:S(2)}) copy-start(bf16[4,64,768]{2,1,0:T(8,128)(2,1)} %w_ref.3) | copy-start | bytes 1179652
  2.6 0.9 %copy-start.5 = (bf16[256,4,64]{0,2,1:T(8,128)(2,1)S(1)}, bf16[256,4,64]{0,2,1:T(8,128)(2,1)}, u32[]{:S(2)}) copy-start(bf16[256,4,64]{0,2,1:T(8,128)(2,1)} %param.5) | copy-start | bytes 393220
  3.5 0.7 copy-start.6
  5.1 9.0 %collective-permute-start.3 = (bf16[128,256]{1,0:T(8,128)(2,1)S(1)}, bf16[128,256]{1,0:T(8,128)(2,1)S(1)}, u32[]{:S(2)}, u32[]{:S(2)}) collective-permute-start(bf16[128,256]{1,0:T(8,128)(2,1)S(1)} %get-tuple-element.77), channel_id=1, source_target_pairs={{0,8},{2,10},{4,12},{6,14},{8,0},{10,2},{12,4},{14,6},{16,24},{18,... | collective-permute-start | bytes 196616 | tf_op jit(solution)/shard_map/ppermute | solution.py:285
  10.7 6.4 %collective-permute-start = (bf16[256,128]{1,0:T(8,128)(2,1)}, bf16[256,128]{1,0:T(8,128)(2,1)S(1)}, u32[]{:S(2)}, u32[]{:S(2)}) collective-permute-start(bf16[256,128]{1,0:T(8,128)(2,1)} %get-tuple-element.74), channel_id=1, source_target_pairs={{0,16},{2,18},{4,20},{6,22},{8,24},{10,26},{12,28},{14,30},{16,0},... | collective-permute-start | bytes 196616 | tf_op jit(solution)/shard_map/ppermute | solution.py:285
  13.3 6.3 %collective-permute-start.1 = (bf16[256,128]{1,0:T(8,128)(2,1)}, bf16[256,128]{1,0:T(8,128)(2,1)S(1)}, u32[]{:S(2)}, u32[]{:S(2)}) collective-permute-start(bf16[256,128]{1,0:T(8,128)(2,1)} %get-tuple-element.75), channel_id=1, source_target_pairs={{0,24},{2,26},{4,28},{6,30},{8,16},{10,18},{12,20},{14,22},{16,8},... | collective-permute-start | bytes 196616 | tf_op jit(solution)/shard_map/ppermute | solution.py:285
  13.3 6.3 %collective-permute-start.2 = (bf16[256,128]{1,0:T(8,128)(2,1)}, bf16[256,128]{1,0:T(8,128)(2,1)S(1)}, u32[]{:S(2)}, u32[]{:S(2)}) collective-permute-start(bf16[256,128]{1,0:T(8,128)(2,1)} %get-tuple-element.76), channel_id=1, source_target_pairs={{0,8},{2,10},{4,12},{6,14},{8,0},{10,2},{12,4},{14,6},{16,24},{18,... | collective-permute-start | bytes 196616 | tf_op jit(solution)/shard_map/ppermute | solution.py:285
  19.5 0.8 %copy-start = (bf16[256,128]{1,0:T(8,128)(2,1)S(1)}, bf16[256,128]{1,0:T(8,128)(2,1)}, u32[]{:S(2)}) copy-start(bf16[256,128]{1,0:T(8,128)(2,1)} %get-tuple-element.73.refs_0_) | copy-start | bytes 196612
  20.4 12.5 %collective-permute-start.7 = (bf16[1024,128]{1,0:T(8,128)(2,1)S(1)}, bf16[1024,128]{1,0:T(8,128)(2,1)S(1)}, u32[]{:S(2)}, u32[]{:S(2)}) collective-permute-start(bf16[1024,128]{1,0:T(8,128)(2,1)S(1)} %shard_map.86.pair_ref), channel_id=1, source_target_pairs={{0,4},{2,6},{4,0},{6,2},{8,12},{10,14},{12,8},{14,10},{16,20},{18,... | collective-permute-start | bytes 786440 | tf_op jit(solution)/shard_map/ppermute | solution.py:285
  22.0 11.3 %collective-permute-start.6 = (bf16[1024,128]{1,0:T(8,128)(2,1)S(1)}, bf16[1024,128]{1,0:T(8,128)(2,1)S(1)}, u32[]{:S(2)}, u32[]{:S(2)}) collective-permute-start(bf16[1024,128]{1,0:T(8,128)(2,1)S(1)} %shard_map.86.pair_ref), channel_id=1, source_target_pairs={{0,2},{2,0},{4,6},{6,4},{8,10},{10,8},{12,14},{14,12},{16,18},{18,... | collective-permute-start | bytes 786440 | tf_op jit(solution)/shard_map/ppermute | solution.py:285
  22.0 8.1 %collective-permute-start.4 = (bf16[128,256]{1,0:T(8,128)(2,1)S(1)}, bf16[128,256]{1,0:T(8,128)(2,1)S(1)}, u32[]{:S(2)}, u32[]{:S(2)}) collective-permute-start(bf16[128,256]{1,0:T(8,128)(2,1)S(1)} %get-tuple-element.82), channel_id=1, source_target_pairs={{0,16},{2,18},{4,20},{6,22},{8,24},{10,26},{12,28},{14,30},{16,0},... | collective-permute-start | bytes 196616 | tf_op jit(solution)/shard_map/ppermute | solution.py:285
  23.6 6.5 %collective-permute-start.5 = (bf16[128,256]{1,0:T(8,128)(2,1)S(1)}, bf16[128,256]{1,0:T(8,128)(2,1)S(1)}, u32[]{:S(2)}, u32[]{:S(2)}) collective-permute-start(bf16[128,256]{1,0:T(8,128)(2,1)S(1)} %get-tuple-element.83), channel_id=1, source_target_pairs={{0,24},{2,26},{4,28},{6,30},{8,16},{10,18},{12,20},{14,22},{16,8},... | collective-permute-start | bytes 196616 | tf_op jit(solution)/shard_map/ppermute | solution.py:285
  32.9 6.3 %collective-permute-start.8 = (bf16[1024,128]{1,0:T(8,128)(2,1)S(1)}, bf16[1024,128]{1,0:T(8,128)(2,1)S(1)}, u32[]{:S(2)}, u32[]{:S(2)}) collective-permute-start(bf16[1024,128]{1,0:T(8,128)(2,1)S(1)} %collective-permute-done.7.pair_ref), channel_id=1, source_target_pairs={{0,2},{2,0},{4,6},{6,4},{8,10},{10,8},{12,14},{14,12},{16,18},{18,... | collective-permute-start | bytes 786440 | tf_op jit(solution)/shard_map/ppermute | solution.py:285
  42.4 9.0 %collective-permute-start.9 = (bf16[64,256]{1,0:T(8,128)(2,1)S(1)}, bf16[64,256]{1,0:T(8,128)(2,1)S(1)}, u32[]{:S(2)}, u32[]{:S(2)}) collective-permute-start(bf16[64,256]{1,0:T(8,128)(2,1)S(1)} %get-tuple-element.105), channel_id=1, source_target_pairs={{0,16},{2,18},{4,20},{6,22},{8,24},{10,26},{12,28},{14,30},{16,0},... | collective-permute-start | bytes 98312 | tf_op jit(solution)/shard_map/ppermute | solution.py:285
  45.5 5.9 %collective-permute-start.10 = (bf16[64,256]{1,0:T(8,128)(2,1)S(1)}, bf16[64,256]{1,0:T(8,128)(2,1)S(1)}, u32[]{:S(2)}, u32[]{:S(2)}) collective-permute-start(bf16[64,256]{1,0:T(8,128)(2,1)S(1)} %get-tuple-element.106), channel_id=1, source_target_pairs={{0,24},{2,26},{4,28},{6,30},{8,16},{10,18},{12,20},{14,22},{16,8},... | collective-permute-start | bytes 98312 | tf_op jit(solution)/shard_map/ppermute | solution.py:285
  46.8 4.6 %collective-permute-start.11 = (bf16[64,256]{1,0:T(8,128)(2,1)S(1)}, bf16[64,256]{1,0:T(8,128)(2,1)S(1)}, u32[]{:S(2)}, u32[]{:S(2)}) collective-permute-start(bf16[64,256]{1,0:T(8,128)(2,1)S(1)} %get-tuple-element.107), channel_id=1, source_target_pairs={{0,8},{2,10},{4,12},{6,14},{8,0},{10,2},{12,4},{14,6},{16,24},{18,... | collective-permute-start | bytes 98312 | tf_op jit(solution)/shard_map/ppermute | solution.py:285
  49.1 2.3 %copy-start.2 = (bf16[256,768]{1,0:T(8,128)(2,1)S(1)}, bf16[256,768]{1,0:T(8,128)(2,1)}, u32[]{:S(2)}) copy-start(bf16[256,768]{1,0:T(8,128)(2,1)} %go_ref.3) | copy-start | bytes 1179652
  49.1 2.3 %copy-start.7 = (s32[2]{0:T(128)S(1)}, s32[2]{0:T(128)}, u32[]{:S(2)}) copy-start(s32[2]{0:T(128)} %fill_ref.7) | copy-start | bytes 28
  51.4 1.6 %copy-start.4 = (bf16[4,64,768]{2,1,0:T(8,128)(2,1)S(1)}, bf16[4,64,768]{2,1,0:T(8,128)(2,1)}, u32[]{:S(2)}) copy-start(bf16[4,64,768]{2,1,0:T(8,128)(2,1)} %w_ref.3) | copy-start | bytes 1179652
  52.4 3.1 %collective-permute-start.13 = (bf16[2,64,768]{2,1,0:T(8,128)(2,1)S(1)}, bf16[2,64,768]{2,1,0:T(8,128)(2,1)S(1)}, u32[]{:S(2)}, u32[]{:S(2)}) collective-permute-start(bf16[2,64,768]{2,1,0:T(8,128)(2,1)S(1)} %get-tuple-element.118.refs_4_), channel_id=1, source_target_pairs={{0,2},{2,0},{4,6},{6,4},{8,10},{10,8},{12,14},{14,12},{16,18},{18,... | collective-permute-start | bytes 589832 | tf_op jit(solution)/shard_map/ppermute | solution.py:285
  52.4 15.8 %collective-permute-start.15 = (bf16[128,1024]{1,0:T(8,128)(2,1)S(1)}, bf16[128,1024]{1,0:T(8,128)(2,1)S(1)}, u32[]{:S(2)}, u32[]{:S(2)}) collective-permute-start(bf16[128,1024]{1,0:T(8,128)(2,1)S(1)} %get-tuple-element.117.refs_4_), channel_id=1, source_target_pairs={{0,2},{2,0},{4,6},{6,4},{8,10},{10,8},{12,14},{14,12},{16,18},{18,... | collective-permute-start | bytes 786440 | tf_op jit(solution)/shard_map/ppermute | solution.py:285
  52.9 5.4 %collective-permute-start.16 = (bf16[128,1024]{1,0:T(8,128)(2,1)S(1)}, bf16[128,1024]{1,0:T(8,128)(2,1)S(1)}, u32[]{:S(2)}, u32[]{:S(2)}) collective-permute-start(bf16[128,1024]{1,0:T(8,128)(2,1)S(1)} %get-tuple-element.133), channel_id=1, source_target_pairs={{0,2},{2,0},{4,6},{6,4},{8,10},{10,8},{12,14},{14,12},{16,18},{18,... | collective-permute-start | bytes 786440 | tf_op jit(solution)/shard_map/ppermute | solution.py:285
  53.9 14.4 %collective-permute-start.12 = (bf16[256,768]{1,0:T(8,128)(2,1)S(1)}, bf16[256,768]{1,0:T(8,128)(2,1)S(1)}, u32[]{:S(2)}, u32[]{:S(2)}) collective-permute-start(bf16[256,768]{1,0:T(8,128)(2,1)S(1)} %shard_map.100.a_ref._), channel_id=1, source_target_pairs={{0,1},{1,0},{2,3},{3,2},{4,5},{5,4},{6,7},{7,6},{8,9},{9,8},{10,11... | collective-permute-start | bytes 1179656 | tf_op jit(solution)/shard_map/ppermute | solution.py:285
  55.5 4.9 %collective-permute-start.14 = (bf16[64,768]{1,0:T(8,128)(2,1)S(1)}, bf16[64,768]{1,0:T(8,128)(2,1)S(1)}, u32[]{:S(2)}, u32[]{:S(2)}) collective-permute-start(bf16[64,768]{1,0:T(8,128)(2,1)S(1)} %get-tuple-element.130), channel_id=1, source_target_pairs={{0,4},{2,6},{4,0},{6,2},{8,12},{10,14},{12,8},{14,10},{16,20},{18,... | collective-permute-start | bytes 294920 | tf_op jit(solution)/shard_map/ppermute | solution.py:285
  58.4 10.7 %collective-permute-start.17 = (bf16[128,1024]{1,0:T(8,128)(2,1)S(1)}, bf16[128,1024]{1,0:T(8,128)(2,1)S(1)}, u32[]{:S(2)}, u32[]{:S(2)}) collective-permute-start(bf16[128,1024]{1,0:T(8,128)(2,1)S(1)} %shard_map.107), channel_id=1, source_target_pairs={{0,4},{2,6},{4,0},{6,2},{8,12},{10,14},{12,8},{14,10},{16,20},{18,... | collective-permute-start | bytes 786440 | tf_op jit(solution)/shard_map/ppermute | solution.py:285
  60.4 7.6 %collective-permute-start.21 = (bf16[64,768]{1,0:T(8,128)(2,1)S(1)}, bf16[64,768]{1,0:T(8,128)(2,1)S(1)}, u32[]{:S(2)}, u32[]{:S(2)}) collective-permute-start(bf16[64,768]{1,0:T(8,128)(2,1)S(1)} %shard_map.104.refs_1_.a_ref), channel_id=1, source_target_pairs={{0,16},{2,18},{4,20},{6,22},{8,24},{10,26},{12,28},{14,30},{16,0},... | collective-permute-start | bytes 294920 | tf_op jit(solution)/shard_map/ppermute | solution.py:285
  68.1 5.3 %collective-permute-start.22 = (bf16[64,768]{1,0:T(8,128)(2,1)S(1)}, bf16[64,768]{1,0:T(8,128)(2,1)S(1)}, u32[]{:S(2)}, u32[]{:S(2)}) collective-permute-start(bf16[64,768]{1,0:T(8,128)(2,1)S(1)} %shard_map.110.a_ref), channel_id=1, source_target_pairs={{0,8},{2,10},{4,12},{6,14},{8,0},{10,2},{12,4},{14,6},{16,24},{18,... | collective-permute-start | bytes 294920 | tf_op jit(solution)/shard_map/ppermute | solution.py:285
  69.2 8.9 %collective-permute-start.18 = (bf16[192,256]{1,0:T(8,128)(2,1)S(1)}, bf16[192,256]{1,0:T(8,128)(2,1)S(1)}, u32[]{:S(2)}, u32[]{:S(2)}) collective-permute-start(bf16[192,256]{1,0:T(8,128)(2,1)S(1)} %get-tuple-element.137), channel_id=1, source_target_pairs={{0,16},{2,18},{4,20},{6,22},{8,24},{10,26},{12,28},{14,30},{16,0},... | collective-permute-start | bytes 294920 | tf_op jit(solution)/shard_map/ppermute | solution.py:285
  73.5 4.7 %collective-permute-start.24 = (bf16[64,768]{1,0:T(8,128)(2,1)S(1)}, bf16[64,768]{1,0:T(8,128)(2,1)S(1)}, u32[]{:S(2)}, u32[]{:S(2)}) collective-permute-start(bf16[64,768]{1,0:T(8,128)(2,1)S(1)} %shard_map.111.refs_0_), channel_id=1, source_target_pairs={{0,4},{2,6},{4,0},{6,2},{8,12},{10,14},{12,8},{14,10},{16,20},{18,... | collective-permute-start | bytes 294920 | tf_op jit(solution)/shard_map/ppermute | solution.py:285
  73.6 6.5 %collective-permute-start.19 = (bf16[192,256]{1,0:T(8,128)(2,1)S(1)}, bf16[192,256]{1,0:T(8,128)(2,1)S(1)}, u32[]{:S(2)}, u32[]{:S(2)}) collective-permute-start(bf16[192,256]{1,0:T(8,128)(2,1)S(1)} %get-tuple-element.138), channel_id=1, source_target_pairs={{0,24},{2,26},{4,28},{6,30},{8,16},{10,18},{12,20},{14,22},{16,8},... | collective-permute-start | bytes 294920 | tf_op jit(solution)/shard_map/ppermute | solution.py:285
  76.0 5.1 %collective-permute-start.20 = (bf16[192,256]{1,0:T(8,128)(2,1)S(1)}, bf16[192,256]{1,0:T(8,128)(2,1)S(1)}, u32[]{:S(2)}, u32[]{:S(2)}) collective-permute-start(bf16[192,256]{1,0:T(8,128)(2,1)S(1)} %get-tuple-element.139), channel_id=1, source_target_pairs={{0,8},{2,10},{4,12},{6,14},{8,0},{10,2},{12,4},{14,6},{16,24},{18,... | collective-permute-start | bytes 294920 | tf_op jit(solution)/shard_map/ppermute | solution.py:285
  76.0 6.4 %collective-permute-start.23 = (bf16[64,768]{1,0:T(8,128)(2,1)S(1)}, bf16[64,768]{1,0:T(8,128)(2,1)S(1)}, u32[]{:S(2)}, u32[]{:S(2)}) collective-permute-start(bf16[64,768]{1,0:T(8,128)(2,1)S(1)} %shard_map.111.refs_0_), channel_id=1, source_target_pairs={{0,2},{2,0},{4,6},{6,4},{8,10},{10,8},{12,14},{14,12},{16,18},{18,... | collective-permute-start | bytes 294920 | tf_op jit(solution)/shard_map/ppermute | solution.py:285
  78.2 4.2 %collective-permute-start.25 = (bf16[64,768]{1,0:T(8,128)(2,1)S(1)}, bf16[64,768]{1,0:T(8,128)(2,1)S(1)}, u32[]{:S(2)}, u32[]{:S(2)}) collective-permute-start(bf16[64,768]{1,0:T(8,128)(2,1)S(1)} %collective-permute-done.24.refs_2_), channel_id=1, source_target_pairs={{0,2},{2,0},{4,6},{6,4},{8,10},{10,8},{12,14},{14,12},{16,18},{18,... | collective-permute-start | bytes 294920 | tf_op jit(solution)/shard_map/ppermute | solution.py:285

commit v8 on v7

--- a/solution.py
+++ b/solution.py
@@ -301,7 +301,7 @@
     qg_mine = exchange(qg_send)
     own = call(
         functools.partial(join_kernel, slots), [((block, wide), BF16)], n_in=slots, after=1,
-    )(*kv_mine, qg_mine[-1])[0]
+    )(*kv_mine, qg_send[0])[0]
 
     blocks = {0: own}
     bit = columns // 2
@@ -319,12 +319,12 @@
     for r in range(columns):
         *prepared[r], values, norm = call(
             functools.partial(prep_kernel, dim),
-            [((block, 2 * wide), BF16), ((dim, block), BF16), ((dim + 16, block), BF16), ((1, block), F32)],
+            [((block, 2 * wide), BF16), ((dim, block), BF16), ((dim + 16, block), BF16), ((1, block), F32)], micros=2,
         )(blocks[r])
         scored[r] = call(
             functools.partial(score_kernel, slots, rows, dim, step),
             [((block, block), BF16), ((1, block), F32), ((dim + 16, block), F32)],
-            [pltpu.VMEM((block, rows), F32)], n_in=5, micros=1.5,
+            [pltpu.VMEM((block, rows), F32)], n_in=5, micros=4,
         )(prepared[r][0], values, norm, qa, q_norm)
     combined = call(
         functools.partial(combine_kernel, slots, columns, rows, dim),

time: 83.6 us -> 75.4 us (0.902)
  waiting for transfers between devices: 19.2 us -> 12.7 us
  local copies, waits for them, and re-layouts: 4.4 us -> 0.02 us
  starting transfers between devices: 28.7 us -> 31.4 us
    ppermute x26, waiting for transfers between devices: 19.2 us -> 12.7 us  [swap(): return lax.ppermute(array, axis, [(i, i ^ mask) for i in range(size)])]
    unnamed x16 -> x10, local copies, waits for them, and re-layouts: 4.4 us -> 0.02 us
    ppermute x26, starting transfers between devices: 28.7 us -> 31.4 us  [swap(): return lax.ppermute(array, axis, [(i, i ^ mask) for i in range(size)])]
  transfers between devices with their start and end apart: 26 -> 26, of which waited for: 9 -> 10; matrix products, arithmetic and copies ran while one was open for 0% -> 0% of each run, Pallas kernels for 29% -> 30%
where the time goes in v8:
time: 75.4 us; the launch traced here: 75.2 us
  starting transfers between devices  31.4 us (42%)
  Pallas kernels  30.2 us (40%)
  waiting for transfers between devices  12.7 us (17%)
  between operations  0.96 us (1%)
    ppermute x26, starting transfers between devices, swap(): return lax.ppermute(array, axis, [(i, i ^ mask) for i in range(size)])  31.4 us
    ppermute x26, waiting for transfers between devices, swap(): return lax.ppermute(array, axis, [(i, i ^ mask) for i in range(size)])  12.7 us
    pallas_call x4, Pallas kernels, shards(): call(functools.partial(score_kernel, slots, rows, dim, step), [((block, b...  10.9 us
    pallas_call x4, Pallas kernels, shards(): call(functools.partial(back_kernel, slots, rows, dim, dq is None), [((wid...  9.07 us
    pallas_call x1, Pallas kernels, shards(): call(functools.partial(pack_kv_kernel, heads, rows, dim, a_of), [((rows,...  2.53 us
  transfers between devices with their start and end apart: 26, of which 10 were waited for; matrix products, arithmetic and copies ran while one was open for 0% of the time, Pallas kernels for 30%

profile of v8, /device:TPU:0, one launch (start us, length us, event | category | flops | bytes accessed | tf_op | source)
XLA Modules:
  0.0 75.2 jit_solution(8481518070988437599)
XLA Ops:
  0.7 2.5 %shard_map.84 = (bf16[256,128]{1,0:T(8,128)(2,1)}, bf16[256,128]{1,0:T(8,128)(2,1)}, bf16[256,128]{1,0:T(8,128)(2,1)}, bf16[256,128]{1,0:T(8,128)(2,1)}) custom-call(s32[2]{0:T(128)} %fill_ref.7, bf16[256,4,128]{2,1,0:T(4,128)(2,1)} %kv_ref.1), custom_call_target="tpu_custom_call" | custom-call | flops 1724999936 | tf_op jit(solution)/shard_map/pallas_call | solution.py:291
  3.2 4.0 %collective-permute-start = (bf16[256,128]{1,0:T(8,128)(2,1)}, bf16[256,128]{1,0:T(8,128)(2,1)S(1)}, u32[]{:S(2)}, u32[]{:S(2)}) collective-permute-start(bf16[256,128]{1,0:T(8,128)(2,1)} %get-tuple-element.74), channel_id=1, source_target_pairs={{0,16},{2,18},{4,20},{6,22},{8,24},{10,26},{12,28},{14,30},{16,0},... | collective-permute-start | bytes 196616 | tf_op jit(solution)/shard_map/ppermute | solution.py:285
  7.2 1.3 %collective-permute-start.1 = (bf16[256,128]{1,0:T(8,128)(2,1)}, bf16[256,128]{1,0:T(8,128)(2,1)S(1)}, u32[]{:S(2)}, u32[]{:S(2)}) collective-permute-start(bf16[256,128]{1,0:T(8,128)(2,1)} %get-tuple-element.75), channel_id=1, source_target_pairs={{0,24},{2,26},{4,28},{6,30},{8,16},{10,18},{12,20},{14,22},{16,8},... | collective-permute-start | bytes 196616 | tf_op jit(solution)/shard_map/ppermute | solution.py:285
  8.6 0.2 collective-permute-start.2
  8.8 0.0 copy-start
  8.8 0.9 %shard_map.85 = (bf16[128,256]{1,0:T(8,128)(2,1)S(1)}, bf16[128,256]{1,0:T(8,128)(2,1)S(1)}, bf16[128,256]{1,0:T(8,128)(2,1)S(1)}, bf16[128,256]{1,0:T(8,128)(2,1)S(1)}) custom-call(s32[2]{0:T(128)S(1)} %copy-done.4, bf16[4,64,256]{2,1,0:T(8,128)(2,1)S(1)} %bitcast.2, bf16[4,64,768]{2,1,0:T(8,128)(2,1)S(1)} %copy-done.2, bf16[256,768]{1,0:T(8,128)(2,1)S(1)} %copy-done.1), custom_call_target="tpu_custom_call" | custom-call | flops 1150000000 | tf_op jit(solution)/shard_map/pallas_call | solution.py:296
  9.8 2.9 %collective-permute-start.3 = (bf16[128,256]{1,0:T(8,128)(2,1)S(1)}, bf16[128,256]{1,0:T(8,128)(2,1)S(1)}, u32[]{:S(2)}, u32[]{:S(2)}) collective-permute-start(bf16[128,256]{1,0:T(8,128)(2,1)S(1)} %get-tuple-element.81), channel_id=1, source_target_pairs={{0,16},{2,18},{4,20},{6,22},{8,24},{10,26},{12,28},{14,30},{16,0},... | collective-permute-start | bytes 196616 | tf_op jit(solution)/shard_map/ppermute | solution.py:285
  12.7 1.3 %collective-permute-start.4 = (bf16[128,256]{1,0:T(8,128)(2,1)S(1)}, bf16[128,256]{1,0:T(8,128)(2,1)S(1)}, u32[]{:S(2)}, u32[]{:S(2)}) collective-permute-start(bf16[128,256]{1,0:T(8,128)(2,1)S(1)} %get-tuple-element.82), channel_id=1, source_target_pairs={{0,24},{2,26},{4,28},{6,30},{8,16},{10,18},{12,20},{14,22},{16,8},... | collective-permute-start | bytes 196616 | tf_op jit(solution)/shard_map/ppermute | solution.py:285
  14.0 0.0 collective-permute-done.refs_1_
  14.0 0.0 collective-permute-start.5
  14.0 0.0 collective-permute-done.1.refs_2_
  14.1 1.6 %collective-permute-start.7 = (bf16[1024,128]{1,0:T(8,128)(2,1)S(1)}, bf16[1024,128]{1,0:T(8,128)(2,1)S(1)}, u32[]{:S(2)}, u32[]{:S(2)}) collective-permute-start(bf16[1024,128]{1,0:T(8,128)(2,1)S(1)} %shard_map.86.pair_ref), channel_id=1, source_target_pairs={{0,4},{2,6},{4,0},{6,2},{8,12},{10,14},{12,8},{14,10},{16,20},{18,... | collective-permute-start | bytes 786440 | tf_op jit(solution)/shard_map/ppermute | solution.py:285
  15.7 0.3 shard_map.87
  16.0 1.8 %collective-permute-done.3.refs_1_ = bf16[128,256]{1,0:T(8,128)(2,1)S(1)} collective-permute-done((bf16[128,256]{1,0:T(8,128)(2,1)S(1)}, bf16[128,256]{1,0:T(8,128)(2,1)S(1)}, u32[]{:S(2)}, u32[]{:S(2)}) %collective-permute-start.3) | collective-permute-done | bytes 65568 | tf_op jit(solution)/shard_map/ppermute | solution.py:285
  17.8 1.1 %collective-permute-done.4.refs_2_ = bf16[128,256]{1,0:T(8,128)(2,1)S(1)} collective-permute-done((bf16[128,256]{1,0:T(8,128)(2,1)S(1)}, bf16[128,256]{1,0:T(8,128)(2,1)S(1)}, u32[]{:S(2)}, u32[]{:S(2)}) %collective-permute-start.4) | collective-permute-done | bytes 65568 | tf_op jit(solution)/shard_map/ppermute | solution.py:285
  18.9 0.2 collective-permute-done.5.refs_3_
  19.1 0.1 shard_map.88
  19.2 2.7 %shard_map.89 = (bf16[1024,1024]{1,0:T(8,128)(2,1)S(1)}, f32[1,1024]{1,0:T(1,128)S(1)}, f32[80,1024]{1,0:T(8,128)S(1)}) custom-call(bf16[1024,256]{1,0:T(8,128)(2,1)S(1)} %get-tuple-element.78.wide_ref, bf16[80,1024]{1,0:T(8,128)(2,1)S(1)} %get-tuple-element.79.vt_ref, f32[1,1024]{1,0:T(1,128)S(1)} %get-tuple-element.80.norm_ref, ...), custom_call_target="tpu_custom_call" | custom-call | flops 4600000000 | tf_op jit(solution)/shard_map/pallas_call | solution.py:324
  21.9 0.0 collective-permute-done.7.pair_ref
  21.9 0.1 collective-permute-start.8
  22.0 0.3 shard_map.92
  22.3 2.7 %shard_map.93 = (bf16[1024,1024]{1,0:T(8,128)(2,1)S(1)}, f32[1,1024]{1,0:T(1,128)S(1)}, f32[80,1024]{1,0:T(8,128)S(1)}) custom-call(bf16[1024,256]{1,0:T(8,128)(2,1)S(1)} %get-tuple-element.91.wide_ref, bf16[80,1024]{1,0:T(8,128)(2,1)S(1)} %get-tuple-element.92.vt_ref, f32[1,1024]{1,0:T(1,128)S(1)} %get-tuple-element.93.norm_ref, ...), custom_call_target="tpu_custom_call" | custom-call | flops 4600000000 | tf_op jit(solution)/shard_map/pallas_call | solution.py:324
  25.0 0.0 collective-permute-done.6.pair_ref
  25.0 0.3 shard_map.90
  25.3 2.9 %shard_map.91 = (bf16[1024,1024]{1,0:T(8,128)(2,1)S(1)}, f32[1,1024]{1,0:T(1,128)S(1)}, f32[80,1024]{1,0:T(8,128)S(1)}) custom-call(bf16[1024,256]{1,0:T(8,128)(2,1)S(1)} %get-tuple-element.87.wide_ref, bf16[80,1024]{1,0:T(8,128)(2,1)S(1)} %get-tuple-element.88.vt_ref, f32[1,1024]{1,0:T(1,128)S(1)} %get-tuple-element.89.norm_ref, ...), custom_call_target="tpu_custom_call" | custom-call | flops 4600000000 | tf_op jit(solution)/shard_map/pallas_call | solution.py:324
  28.2 0.3 shard_map.94
  28.5 2.7 %shard_map.95 = (bf16[1024,1024]{1,0:T(8,128)(2,1)S(1)}, f32[1,1024]{1,0:T(1,128)S(1)}, f32[80,1024]{1,0:T(8,128)S(1)}) custom-call(bf16[1024,256]{1,0:T(8,128)(2,1)S(1)} %get-tuple-element.95.wide_ref, bf16[80,1024]{1,0:T(8,128)(2,1)S(1)} %get-tuple-element.96.vt_ref, f32[1,1024]{1,0:T(1,128)S(1)} %get-tuple-element.97.norm_ref, ...), custom_call_target="tpu_custom_call" | custom-call | flops 4600000000 | tf_op jit(solution)/shard_map/pallas_call | solution.py:324
  31.2 0.2 shard_map.96
  31.4 4.3 %collective-permute-start.9 = (bf16[64,256]{1,0:T(8,128)(2,1)S(1)}, bf16[64,256]{1,0:T(8,128)(2,1)S(1)}, u32[]{:S(2)}, u32[]{:S(2)}) collective-permute-start(bf16[64,256]{1,0:T(8,128)(2,1)S(1)} %get-tuple-element.105), channel_id=1, source_target_pairs={{0,16},{2,18},{4,20},{6,22},{8,24},{10,26},{12,28},{14,30},{16,0},... | collective-permute-start | bytes 98312 | tf_op jit(solution)/shard_map/ppermute | solution.py:285
  35.7 0.3 collective-permute-start.10
  36.0 0.4 collective-permute-start.11
  36.3 2.3 %shard_map.97 = (bf16[128,1024]{1,0:T(8,128)(2,1)S(1)}, f32[64,1024]{1,0:T(8,128)S(1)}) custom-call(bf16[1024,1024]{1,0:T(8,128)(2,1)S(1)} %get-tuple-element.113.exp_ref, bf16[1024,256]{1,0:T(8,128)(2,1)S(1)} %get-tuple-element.95.wide_ref, bf16[64,1024]{1,0:T(8,128)(2,1)S(1)} %get-tuple-element.114.kt_ref, bf16[64,1024]{1,0:T(8,128)(2,1)S(1)} %get-tuple-element.110.q_ref, ...), custom_call_target="tpu_custom_call" | custom-call | flops 2300000000 | tf_op jit(solution)/shard_map/pallas_call | solution.py:360
  38.6 2.3 %shard_map.98 = (bf16[128,1024]{1,0:T(8,128)(2,1)S(1)}, f32[64,1024]{1,0:T(8,128)S(1)}) custom-call(bf16[1024,1024]{1,0:T(8,128)(2,1)S(1)} %get-tuple-element.108.exp_ref, bf16[1024,256]{1,0:T(8,128)(2,1)S(1)} %get-tuple-element.87.wide_ref, bf16[64,1024]{1,0:T(8,128)(2,1)S(1)} %get-tuple-element.109.kt_ref, bf16[64,1024]{1,0:T(8,128)(2,1)S(1)} %get-tuple-element.110.q_ref, ...), custom_call_target="tpu_custom_call" | custom-call | flops 2300000000 | tf_op jit(solution)/shard_map/pallas_call | solution.py:360
  40.9 0.5 collective-permute-done.10.refs_2_
  41.4 0.0 collective-permute-done.11.refs_3_
  41.4 0.9 %shard_map.99 = (bf16[2,64,768]{2,1,0:T(8,128)(2,1)S(1)}, bf16[2,64,768]{2,1,0:T(8,128)(2,1)S(1)}) custom-call(s32[2]{0:T(128)S(1)} %copy-done.4, bf16[256,768]{1,0:T(8,128)(2,1)S(1)} %copy-done.1, bf16[64,256]{1,0:T(8,128)(2,1)S(1)} %get-tuple-element.104.refs_0_, bf16[64,256]{1,0:T(8,128)(2,1)S(1)} %collective-permute-done.9.refs_1_, ...), custom_call_target="tpu_custom_call" | custom-call | flops 805000000 | tf_op jit(solution)/shard_map/pallas_call | solution.py:341
  42.3 0.1 collective-permute-start.13
  42.4 0.5 collective-permute-start.15
  42.9 0.1 collective-permute-start.16
  43.0 0.8 %shard_map.100.a_ref._ = bf16[256,768]{1,0:T(8,128)(2,1)S(1)} custom-call(s32[2]{0:T(128)S(1)} %copy-done.4, bf16[4,64,768]{2,1,0:T(8,128)(2,1)S(1)} %copy-done.2, bf16[64,256]{1,0:T(8,128)(2,1)S(1)} %get-tuple-element.104.refs_0_, bf16[64,256]{1,0:T(8,128)(2,1)S(1)} %collective-permute-done.9.refs_1_, bf16[64,256]{1,0:T(8,128)(2,1)S(1)} %collective-permute-done.10.refs_2_, ...), custom_call_target="tpu_custom_call" | custom-call | flops 805000000 | tf_op jit(solution)/shard_map/pallas_call | solution.py:347
  43.9 1.5 %collective-permute-start.12 = (bf16[256,768]{1,0:T(8,128)(2,1)S(1)}, bf16[256,768]{1,0:T(8,128)(2,1)S(1)}, u32[]{:S(2)}, u32[]{:S(2)}) collective-permute-start(bf16[256,768]{1,0:T(8,128)(2,1)S(1)} %shard_map.100.a_ref._), channel_id=1, source_target_pairs={{0,1},{1,0},{2,3},{3,2},{4,5},{5,4},{6,7},{7,6},{8,9},{9,8},{10,11... | collective-permute-start | bytes 1179656 | tf_op jit(solution)/shard_map/ppermute | solution.py:285
  45.4 0.0 collective-permute-done.13.came_ref
  45.5 1.6 %collective-permute-start.14 = (bf16[64,768]{1,0:T(8,128)(2,1)S(1)}, bf16[64,768]{1,0:T(8,128)(2,1)S(1)}, u32[]{:S(2)}, u32[]{:S(2)}) collective-permute-start(bf16[64,768]{1,0:T(8,128)(2,1)S(1)} %get-tuple-element.130), channel_id=1, source_target_pairs={{0,4},{2,6},{4,0},{6,2},{8,12},{10,14},{12,8},{14,10},{16,20},{18,... | collective-permute-start | bytes 294920 | tf_op jit(solution)/shard_map/ppermute | solution.py:285
  47.1 2.3 %shard_map.103 = (bf16[128,1024]{1,0:T(8,128)(2,1)S(1)}, f32[64,1024]{1,0:T(8,128)S(1)}) custom-call(bf16[1024,1024]{1,0:T(8,128)(2,1)S(1)} %get-tuple-element.123.exp_ref, bf16[1024,256]{1,0:T(8,128)(2,1)S(1)} %get-tuple-element.91.wide_ref, bf16[64,1024]{1,0:T(8,128)(2,1)S(1)} %get-tuple-element.124.kt_ref, bf16[64,1024]{1,0:T(8,128)(2,1)S(1)} %get-tuple-element.110.q_ref, ...), custom_call_target="tpu_custom_call" | custom-call | flops 2300000000 | tf_op jit(solution)/shard_map/pallas_call | solution.py:360
  49.3 0.0 collective-permute-done.16.b_ref
  49.3 0.1 shard_map.107
  49.4 0.6 collective-permute-start.17
  50.0 0.4 collective-permute-done.14.b_ref
  50.4 3.3 %collective-permute-start.21 = (bf16[64,768]{1,0:T(8,128)(2,1)S(1)}, bf16[64,768]{1,0:T(8,128)(2,1)S(1)}, u32[]{:S(2)}, u32[]{:S(2)}) collective-permute-start(bf16[64,768]{1,0:T(8,128)(2,1)S(1)} %shard_map.104.refs_1_.a_ref), channel_id=1, source_target_pairs={{0,16},{2,18},{4,20},{6,22},{8,24},{10,26},{12,28},{14,30},{16,0},... | collective-permute-start | bytes 294920 | tf_op jit(solution)/shard_map/ppermute | solution.py:285
  53.7 2.3 %shard_map.105 = (bf16[128,1024]{1,0:T(8,128)(2,1)S(1)}, f32[64,1024]{1,0:T(8,128)S(1)}) custom-call(bf16[1024,1024]{1,0:T(8,128)(2,1)S(1)} %get-tuple-element.120.exp_ref, bf16[1024,256]{1,0:T(8,128)(2,1)S(1)} %get-tuple-element.78.wide_ref, bf16[64,1024]{1,0:T(8,128)(2,1)S(1)} %get-tuple-element.121.kt_ref, bf16[64,1024]{1,0:T(8,128)(2,1)S(1)} %get-tuple-element.110.q_ref, ...), custom_call_target="tpu_custom_call" | custom-call | flops 2300000000 | tf_op jit(solution)/shard_map/pallas_call | solution.py:360
  56.0 2.1 %collective-permute-done.21.b_ref = bf16[64,768]{1,0:T(8,128)(2,1)S(1)} collective-permute-done((bf16[64,768]{1,0:T(8,128)(2,1)S(1)}, bf16[64,768]{1,0:T(8,128)(2,1)S(1)}, u32[]{:S(2)}, u32[]{:S(2)}) %collective-permute-start.21) | collective-permute-done | bytes 98336 | tf_op jit(solution)/shard_map/ppermute | solution.py:285
  58.2 0.1 collective-permute-start.22
  58.2 0.1 shard_map.106.kept_ref
  58.3 0.8 %shard_map.101 = (bf16[256,768]{1,0:T(8,128)(2,1)}, f32[8,128]{1,0:T(8,128)S(1)}) custom-call(bf16[256,768]{1,0:T(8,128)(2,1)S(1)} %shard_map.100.a_ref._, bf16[256,768]{1,0:T(8,128)(2,1)S(1)} %collective-permute-done.12.b_ref), custom_call_target="tpu_custom_call" | custom-call | flops 11500000 | tf_op jit(solution)/shard_map/pallas_call | solution.py:368
  59.2 0.1 shard_map.108
  59.3 3.2 %collective-permute-start.18 = (bf16[192,256]{1,0:T(8,128)(2,1)S(1)}, bf16[192,256]{1,0:T(8,128)(2,1)S(1)}, u32[]{:S(2)}, u32[]{:S(2)}) collective-permute-start(bf16[192,256]{1,0:T(8,128)(2,1)S(1)} %get-tuple-element.137), channel_id=1, source_target_pairs={{0,16},{2,18},{4,20},{6,22},{8,24},{10,26},{12,28},{14,30},{16,0},... | collective-permute-start | bytes 294920 | tf_op jit(solution)/shard_map/ppermute | solution.py:285
  62.4 1.4 %collective-permute-done.22.b_ref = bf16[64,768]{1,0:T(8,128)(2,1)S(1)} collective-permute-done((bf16[64,768]{1,0:T(8,128)(2,1)S(1)}, bf16[64,768]{1,0:T(8,128)(2,1)S(1)}, u32[]{:S(2)}, u32[]{:S(2)}) %collective-permute-start.22) | collective-permute-done | bytes 98336 | tf_op jit(solution)/shard_map/ppermute | solution.py:285
  63.9 1.6 %collective-permute-start.24 = (bf16[64,768]{1,0:T(8,128)(2,1)S(1)}, bf16[64,768]{1,0:T(8,128)(2,1)S(1)}, u32[]{:S(2)}, u32[]{:S(2)}) collective-permute-start(bf16[64,768]{1,0:T(8,128)(2,1)S(1)} %shard_map.111.refs_0_), channel_id=1, source_target_pairs={{0,4},{2,6},{4,0},{6,2},{8,12},{10,14},{12,8},{14,10},{16,20},{18,... | collective-permute-start | bytes 294920 | tf_op jit(solution)/shard_map/ppermute | solution.py:285
  65.5 2.4 %collective-permute-start.19 = (bf16[192,256]{1,0:T(8,128)(2,1)S(1)}, bf16[192,256]{1,0:T(8,128)(2,1)S(1)}, u32[]{:S(2)}, u32[]{:S(2)}) collective-permute-start(bf16[192,256]{1,0:T(8,128)(2,1)S(1)} %get-tuple-element.138), channel_id=1, source_target_pairs={{0,24},{2,26},{4,28},{6,30},{8,16},{10,18},{12,20},{14,22},{16,8},... | collective-permute-start | bytes 294920 | tf_op jit(solution)/shard_map/ppermute | solution.py:285
  67.9 0.7 collective-permute-done.24.refs_2_
  68.6 3.3 %collective-permute-done.19.refs_2_ = bf16[192,256]{1,0:T(8,128)(2,1)S(1)} collective-permute-done((bf16[192,256]{1,0:T(8,128)(2,1)S(1)}, bf16[192,256]{1,0:T(8,128)(2,1)S(1)}, u32[]{:S(2)}, u32[]{:S(2)}) %collective-permute-start.19) | collective-permute-done | bytes 98336 | tf_op jit(solution)/shard_map/ppermute | solution.py:285
  72.0 1.0 %collective-permute-done.20.refs_3_ = bf16[192,256]{1,0:T(8,128)(2,1)S(1)} collective-permute-done((bf16[192,256]{1,0:T(8,128)(2,1)S(1)}, bf16[192,256]{1,0:T(8,128)(2,1)S(1)}, u32[]{:S(2)}, u32[]{:S(2)}) %collective-permute-start.20) | collective-permute-done | bytes 98336 | tf_op jit(solution)/shard_map/ppermute | solution.py:285
  73.0 1.3 %shard_map.109 = (f32[256,4,128]{2,1,0:T(4,128)}, f32[4,64,256]{2,1,0:T(8,128)}) custom-call(bf16[192,256]{1,0:T(8,128)(2,1)S(1)} %get-tuple-element.136.refs_0_, bf16[192,256]{1,0:T(8,128)(2,1)S(1)} %collective-permute-done.18.refs_1_, bf16[192,256]{1,0:T(8,128)(2,1)S(1)} %collective-permute-done.19.refs_2_, ...), custom_call_target="tpu_custom_call" | custom-call | flops 1150000000 | tf_op jit(solution)/shard_map/pallas_call | solution.py:393
  74.3 0.9 %shard_map.112 = f32[4,64,768]{2,1,0:T(8,128)} custom-call(bf16[64,768]{1,0:T(8,128)(2,1)S(1)} %shard_map.111.refs_0_, bf16[64,768]{1,0:T(8,128)(2,1)S(1)} %collective-permute-done.23.refs_1_, bf16[64,768]{1,0:T(8,128)(2,1)S(1)} %collective-permute-done.24.refs_2_, bf16[64,768]{1,0:T(8,128)(2,1)S(1)} %collective-permute-done.25.refs_3_), custom_call_target="tpu_custom_call" | custom-call | flops 575000000 | tf_op jit(solution)/shard_map/pallas_call | solution.py:387
  (27 shorter events, 0.2 us)
Async XLA Ops:
  0.6 8.2 %copy-start.4 = (s32[2]{0:T(128)S(1)}, s32[2]{0:T(128)}, u32[]{:S(2)}) copy-start(s32[2]{0:T(128)} %fill_ref.7) | copy-start | bytes 28
  0.6 8.2 %copy-start.1 = (bf16[256,768]{1,0:T(8,128)(2,1)S(1)}, bf16[256,768]{1,0:T(8,128)(2,1)}, u32[]{:S(2)}) copy-start(bf16[256,768]{1,0:T(8,128)(2,1)} %go_ref.3) | copy-start | bytes 1179652
  0.7 8.2 %copy-start.2 = (bf16[4,64,768]{2,1,0:T(8,128)(2,1)S(1)}, bf16[4,64,768]{2,1,0:T(8,128)(2,1)}, u32[]{:S(2)}) copy-start(bf16[4,64,768]{2,1,0:T(8,128)(2,1)} %w_ref.3) | copy-start | bytes 1179652
  0.7 8.2 %copy-start.3 = (bf16[256,4,64]{0,2,1:T(8,128)(2,1)S(1)}, bf16[256,4,64]{0,2,1:T(8,128)(2,1)}, u32[]{:S(2)}) copy-start(bf16[256,4,64]{0,2,1:T(8,128)(2,1)} %param.5) | copy-start | bytes 393220
  3.2 10.8 %collective-permute-start = (bf16[256,128]{1,0:T(8,128)(2,1)}, bf16[256,128]{1,0:T(8,128)(2,1)S(1)}, u32[]{:S(2)}, u32[]{:S(2)}) collective-permute-start(bf16[256,128]{1,0:T(8,128)(2,1)} %get-tuple-element.74), channel_id=1, source_target_pairs={{0,16},{2,18},{4,20},{6,22},{8,24},{10,26},{12,28},{14,30},{16,0},... | collective-permute-start | bytes 196616 | tf_op jit(solution)/shard_map/ppermute | solution.py:285
  7.2 6.8 %collective-permute-start.1 = (bf16[256,128]{1,0:T(8,128)(2,1)}, bf16[256,128]{1,0:T(8,128)(2,1)S(1)}, u32[]{:S(2)}, u32[]{:S(2)}) collective-permute-start(bf16[256,128]{1,0:T(8,128)(2,1)} %get-tuple-element.75), channel_id=1, source_target_pairs={{0,24},{2,26},{4,28},{6,30},{8,16},{10,18},{12,20},{14,22},{16,8},... | collective-permute-start | bytes 196616 | tf_op jit(solution)/shard_map/ppermute | solution.py:285
  8.6 5.4 %collective-permute-start.2 = (bf16[256,128]{1,0:T(8,128)(2,1)}, bf16[256,128]{1,0:T(8,128)(2,1)S(1)}, u32[]{:S(2)}, u32[]{:S(2)}) collective-permute-start(bf16[256,128]{1,0:T(8,128)(2,1)} %get-tuple-element.76), channel_id=1, source_target_pairs={{0,8},{2,10},{4,12},{6,14},{8,0},{10,2},{12,4},{14,6},{16,24},{18,... | collective-permute-start | bytes 196616 | tf_op jit(solution)/shard_map/ppermute | solution.py:285
  8.8 5.2 %copy-start = (bf16[256,128]{1,0:T(8,128)(2,1)S(1)}, bf16[256,128]{1,0:T(8,128)(2,1)}, u32[]{:S(2)}) copy-start(bf16[256,128]{1,0:T(8,128)(2,1)} %get-tuple-element.73.refs_0_) | copy-start | bytes 196612
  9.8 8.0 %collective-permute-start.3 = (bf16[128,256]{1,0:T(8,128)(2,1)S(1)}, bf16[128,256]{1,0:T(8,128)(2,1)S(1)}, u32[]{:S(2)}, u32[]{:S(2)}) collective-permute-start(bf16[128,256]{1,0:T(8,128)(2,1)S(1)} %get-tuple-element.81), channel_id=1, source_target_pairs={{0,16},{2,18},{4,20},{6,22},{8,24},{10,26},{12,28},{14,30},{16,0},... | collective-permute-start | bytes 196616 | tf_op jit(solution)/shard_map/ppermute | solution.py:285
  12.7 6.2 %collective-permute-start.4 = (bf16[128,256]{1,0:T(8,128)(2,1)S(1)}, bf16[128,256]{1,0:T(8,128)(2,1)S(1)}, u32[]{:S(2)}, u32[]{:S(2)}) collective-permute-start(bf16[128,256]{1,0:T(8,128)(2,1)S(1)} %get-tuple-element.82), channel_id=1, source_target_pairs={{0,24},{2,26},{4,28},{6,30},{8,16},{10,18},{12,20},{14,22},{16,8},... | collective-permute-start | bytes 196616 | tf_op jit(solution)/shard_map/ppermute | solution.py:285
  14.0 5.1 %collective-permute-start.5 = (bf16[128,256]{1,0:T(8,128)(2,1)S(1)}, bf16[128,256]{1,0:T(8,128)(2,1)S(1)}, u32[]{:S(2)}, u32[]{:S(2)}) collective-permute-start(bf16[128,256]{1,0:T(8,128)(2,1)S(1)} %get-tuple-element.83), channel_id=1, source_target_pairs={{0,8},{2,10},{4,12},{6,14},{8,0},{10,2},{12,4},{14,6},{16,24},{18,... | collective-permute-start | bytes 196616 | tf_op jit(solution)/shard_map/ppermute | solution.py:285
  14.1 7.8 %collective-permute-start.7 = (bf16[1024,128]{1,0:T(8,128)(2,1)S(1)}, bf16[1024,128]{1,0:T(8,128)(2,1)S(1)}, u32[]{:S(2)}, u32[]{:S(2)}) collective-permute-start(bf16[1024,128]{1,0:T(8,128)(2,1)S(1)} %shard_map.86.pair_ref), channel_id=1, source_target_pairs={{0,4},{2,6},{4,0},{6,2},{8,12},{10,14},{12,8},{14,10},{16,20},{18,... | collective-permute-start | bytes 786440 | tf_op jit(solution)/shard_map/ppermute | solution.py:285
  15.7 9.3 %collective-permute-start.6 = (bf16[1024,128]{1,0:T(8,128)(2,1)S(1)}, bf16[1024,128]{1,0:T(8,128)(2,1)S(1)}, u32[]{:S(2)}, u32[]{:S(2)}) collective-permute-start(bf16[1024,128]{1,0:T(8,128)(2,1)S(1)} %shard_map.86.pair_ref), channel_id=1, source_target_pairs={{0,2},{2,0},{4,6},{6,4},{8,10},{10,8},{12,14},{14,12},{16,18},{18,... | collective-permute-start | bytes 786440 | tf_op jit(solution)/shard_map/ppermute | solution.py:285
  21.9 6.3 %collective-permute-start.8 = (bf16[1024,128]{1,0:T(8,128)(2,1)S(1)}, bf16[1024,128]{1,0:T(8,128)(2,1)S(1)}, u32[]{:S(2)}, u32[]{:S(2)}) collective-permute-start(bf16[1024,128]{1,0:T(8,128)(2,1)S(1)} %collective-permute-done.7.pair_ref), channel_id=1, source_target_pairs={{0,2},{2,0},{4,6},{6,4},{8,10},{10,8},{12,14},{14,12},{16,18},{18,... | collective-permute-start | bytes 786440 | tf_op jit(solution)/shard_map/ppermute | solution.py:285
  31.4 9.5 %collective-permute-start.9 = (bf16[64,256]{1,0:T(8,128)(2,1)S(1)}, bf16[64,256]{1,0:T(8,128)(2,1)S(1)}, u32[]{:S(2)}, u32[]{:S(2)}) collective-permute-start(bf16[64,256]{1,0:T(8,128)(2,1)S(1)} %get-tuple-element.105), channel_id=1, source_target_pairs={{0,16},{2,18},{4,20},{6,22},{8,24},{10,26},{12,28},{14,30},{16,0},... | collective-permute-start | bytes 98312 | tf_op jit(solution)/shard_map/ppermute | solution.py:285
  35.7 5.7 %collective-permute-start.10 = (bf16[64,256]{1,0:T(8,128)(2,1)S(1)}, bf16[64,256]{1,0:T(8,128)(2,1)S(1)}, u32[]{:S(2)}, u32[]{:S(2)}) collective-permute-start(bf16[64,256]{1,0:T(8,128)(2,1)S(1)} %get-tuple-element.106), channel_id=1, source_target_pairs={{0,24},{2,26},{4,28},{6,30},{8,16},{10,18},{12,20},{14,22},{16,8},... | collective-permute-start | bytes 98312 | tf_op jit(solution)/shard_map/ppermute | solution.py:285
  36.0 5.4 %collective-permute-start.11 = (bf16[64,256]{1,0:T(8,128)(2,1)S(1)}, bf16[64,256]{1,0:T(8,128)(2,1)S(1)}, u32[]{:S(2)}, u32[]{:S(2)}) collective-permute-start(bf16[64,256]{1,0:T(8,128)(2,1)S(1)} %get-tuple-element.107), channel_id=1, source_target_pairs={{0,8},{2,10},{4,12},{6,14},{8,0},{10,2},{12,4},{14,6},{16,24},{18,... | collective-permute-start | bytes 98312 | tf_op jit(solution)/shard_map/ppermute | solution.py:285
  42.3 3.1 %collective-permute-start.13 = (bf16[2,64,768]{2,1,0:T(8,128)(2,1)S(1)}, bf16[2,64,768]{2,1,0:T(8,128)(2,1)S(1)}, u32[]{:S(2)}, u32[]{:S(2)}) collective-permute-start(bf16[2,64,768]{2,1,0:T(8,128)(2,1)S(1)} %get-tuple-element.118.refs_4_), channel_id=1, source_target_pairs={{0,2},{2,0},{4,6},{6,4},{8,10},{10,8},{12,14},{14,12},{16,18},{18,... | collective-permute-start | bytes 589832 | tf_op jit(solution)/shard_map/ppermute | solution.py:285
  42.4 15.8 %collective-permute-start.15 = (bf16[128,1024]{1,0:T(8,128)(2,1)S(1)}, bf16[128,1024]{1,0:T(8,128)(2,1)S(1)}, u32[]{:S(2)}, u32[]{:S(2)}) collective-permute-start(bf16[128,1024]{1,0:T(8,128)(2,1)S(1)} %get-tuple-element.117.refs_4_), channel_id=1, source_target_pairs={{0,2},{2,0},{4,6},{6,4},{8,10},{10,8},{12,14},{14,12},{16,18},{18,... | collective-permute-start | bytes 786440 | tf_op jit(solution)/shard_map/ppermute | solution.py:285
  42.9 6.4 %collective-permute-start.16 = (bf16[128,1024]{1,0:T(8,128)(2,1)S(1)}, bf16[128,1024]{1,0:T(8,128)(2,1)S(1)}, u32[]{:S(2)}, u32[]{:S(2)}) collective-permute-start(bf16[128,1024]{1,0:T(8,128)(2,1)S(1)} %get-tuple-element.133), channel_id=1, source_target_pairs={{0,2},{2,0},{4,6},{6,4},{8,10},{10,8},{12,14},{14,12},{16,18},{18,... | collective-permute-start | bytes 786440 | tf_op jit(solution)/shard_map/ppermute | solution.py:285
  43.9 14.5 %collective-permute-start.12 = (bf16[256,768]{1,0:T(8,128)(2,1)S(1)}, bf16[256,768]{1,0:T(8,128)(2,1)S(1)}, u32[]{:S(2)}, u32[]{:S(2)}) collective-permute-start(bf16[256,768]{1,0:T(8,128)(2,1)S(1)} %shard_map.100.a_ref._), channel_id=1, source_target_pairs={{0,1},{1,0},{2,3},{3,2},{4,5},{5,4},{6,7},{7,6},{8,9},{9,8},{10,11... | collective-permute-start | bytes 1179656 | tf_op jit(solution)/shard_map/ppermute | solution.py:285
  45.5 4.9 %collective-permute-start.14 = (bf16[64,768]{1,0:T(8,128)(2,1)S(1)}, bf16[64,768]{1,0:T(8,128)(2,1)S(1)}, u32[]{:S(2)}, u32[]{:S(2)}) collective-permute-start(bf16[64,768]{1,0:T(8,128)(2,1)S(1)} %get-tuple-element.130), channel_id=1, source_target_pairs={{0,4},{2,6},{4,0},{6,2},{8,12},{10,14},{12,8},{14,10},{16,20},{18,... | collective-permute-start | bytes 294920 | tf_op jit(solution)/shard_map/ppermute | solution.py:285
  49.4 9.8 %collective-permute-start.17 = (bf16[128,1024]{1,0:T(8,128)(2,1)S(1)}, bf16[128,1024]{1,0:T(8,128)(2,1)S(1)}, u32[]{:S(2)}, u32[]{:S(2)}) collective-permute-start(bf16[128,1024]{1,0:T(8,128)(2,1)S(1)} %shard_map.107), channel_id=1, source_target_pairs={{0,4},{2,6},{4,0},{6,2},{8,12},{10,14},{12,8},{14,10},{16,20},{18,... | collective-permute-start | bytes 786440 | tf_op jit(solution)/shard_map/ppermute | solution.py:285
  50.4 7.7 %collective-permute-start.21 = (bf16[64,768]{1,0:T(8,128)(2,1)S(1)}, bf16[64,768]{1,0:T(8,128)(2,1)S(1)}, u32[]{:S(2)}, u32[]{:S(2)}) collective-permute-start(bf16[64,768]{1,0:T(8,128)(2,1)S(1)} %shard_map.104.refs_1_.a_ref), channel_id=1, source_target_pairs={{0,16},{2,18},{4,20},{6,22},{8,24},{10,26},{12,28},{14,30},{16,0},... | collective-permute-start | bytes 294920 | tf_op jit(solution)/shard_map/ppermute | solution.py:285
  58.2 5.7 %collective-permute-start.22 = (bf16[64,768]{1,0:T(8,128)(2,1)S(1)}, bf16[64,768]{1,0:T(8,128)(2,1)S(1)}, u32[]{:S(2)}, u32[]{:S(2)}) collective-permute-start(bf16[64,768]{1,0:T(8,128)(2,1)S(1)} %shard_map.110.a_ref), channel_id=1, source_target_pairs={{0,8},{2,10},{4,12},{6,14},{8,0},{10,2},{12,4},{14,6},{16,24},{18,... | collective-permute-start | bytes 294920 | tf_op jit(solution)/shard_map/ppermute | solution.py:285
  59.3 9.4 %collective-permute-start.18 = (bf16[192,256]{1,0:T(8,128)(2,1)S(1)}, bf16[192,256]{1,0:T(8,128)(2,1)S(1)}, u32[]{:S(2)}, u32[]{:S(2)}) collective-permute-start(bf16[192,256]{1,0:T(8,128)(2,1)S(1)} %get-tuple-element.137), channel_id=1, source_target_pairs={{0,16},{2,18},{4,20},{6,22},{8,24},{10,26},{12,28},{14,30},{16,0},... | collective-permute-start | bytes 294920 | tf_op jit(solution)/shard_map/ppermute | solution.py:285
  63.9 4.7 %collective-permute-start.24 = (bf16[64,768]{1,0:T(8,128)(2,1)S(1)}, bf16[64,768]{1,0:T(8,128)(2,1)S(1)}, u32[]{:S(2)}, u32[]{:S(2)}) collective-permute-start(bf16[64,768]{1,0:T(8,128)(2,1)S(1)} %shard_map.111.refs_0_), channel_id=1, source_target_pairs={{0,4},{2,6},{4,0},{6,2},{8,12},{10,14},{12,8},{14,10},{16,20},{18,... | collective-permute-start | bytes 294920 | tf_op jit(solution)/shard_map/ppermute | solution.py:285
  65.5 6.5 %collective-permute-start.19 = (bf16[192,256]{1,0:T(8,128)(2,1)S(1)}, bf16[192,256]{1,0:T(8,128)(2,1)S(1)}, u32[]{:S(2)}, u32[]{:S(2)}) collective-permute-start(bf16[192,256]{1,0:T(8,128)(2,1)S(1)} %get-tuple-element.138), channel_id=1, source_target_pairs={{0,24},{2,26},{4,28},{6,30},{8,16},{10,18},{12,20},{14,22},{16,8},... | collective-permute-start | bytes 294920 | tf_op jit(solution)/shard_map/ppermute | solution.py:285
  67.9 5.0 %collective-permute-start.20 = (bf16[192,256]{1,0:T(8,128)(2,1)S(1)}, bf16[192,256]{1,0:T(8,128)(2,1)S(1)}, u32[]{:S(2)}, u32[]{:S(2)}) collective-permute-start(bf16[192,256]{1,0:T(8,128)(2,1)S(1)} %get-tuple-element.139), channel_id=1, source_target_pairs={{0,8},{2,10},{4,12},{6,14},{8,0},{10,2},{12,4},{14,6},{16,24},{18,... | collective-permute-start | bytes 294920 | tf_op jit(solution)/shard_map/ppermute | solution.py:285
  67.9 6.3 %collective-permute-start.23 = (bf16[64,768]{1,0:T(8,128)(2,1)S(1)}, bf16[64,768]{1,0:T(8,128)(2,1)S(1)}, u32[]{:S(2)}, u32[]{:S(2)}) collective-permute-start(bf16[64,768]{1,0:T(8,128)(2,1)S(1)} %shard_map.111.refs_0_), channel_id=1, source_target_pairs={{0,2},{2,0},{4,6},{6,4},{8,10},{10,8},{12,14},{14,12},{16,18},{18,... | collective-permute-start | bytes 294920 | tf_op jit(solution)/shard_map/ppermute | solution.py:285
  68.6 5.7 %collective-permute-start.25 = (bf16[64,768]{1,0:T(8,128)(2,1)S(1)}, bf16[64,768]{1,0:T(8,128)(2,1)S(1)}, u32[]{:S(2)}, u32[]{:S(2)}) collective-permute-start(bf16[64,768]{1,0:T(8,128)(2,1)S(1)} %collective-permute-done.24.refs_2_), channel_id=1, source_target_pairs={{0,2},{2,0},{4,6},{6,4},{8,10},{10,8},{12,14},{14,12},{16,18},{18,... | collective-permute-start | bytes 294920 | tf_op jit(solution)/shard_map/ppermute | solution.py:285

commit v9 on v8

--- a/solution.py
+++ b/solution.py
@@ -237,17 +237,12 @@
         out_ref[...] = (kept_ref[index].astype(F32) + came_ref[index].astype(F32)).astype(BF16)
 
 
-def add_pieces_kernel(slots, rows, dim, kept_ref, came_ref, dq_ref, _, *outs):
+def add_pieces_kernel(slots, rows, dim, kept_ref, came_ref, dq_ref, *outs):
     wide = 2 * dim
     for slot in range(slots):
         here = slice(slot * rows, (slot + 1) * rows)
         outs[slot][0:wide, :] = (kept_ref[:, here].astype(F32) + came_ref[:, here].astype(F32)).astype(BF16)
         outs[slot][wide:, :] = (dq_ref[:, here] * dim**-0.5).astype(BF16)
-
-
-def add_out_kernel(a_ref, b_ref, out_ref, done_ref):
-    out_ref[...] = (a_ref[...].astype(F32) + b_ref[...].astype(F32)).astype(out_ref.dtype)
-    done_ref[...] = jnp.zeros_like(done_ref)
 
 
 def add_kernel(a_ref, b_ref, *refs):
@@ -333,11 +328,13 @@
     att_mine, factors, inner = exchange(combined[:slots]), combined[slots:-1], combined[-1]
 
     halves = columns == heads == 4
-    order = sorted(range(columns), key=lambda r: -int(f"{r:032b}"[::-1], 2))
-    dkv, dq, terms, kept = {}, None, None, None
+    order = sorted(range(columns), reverse=True)
+    add = call(add_kernel, [((dim, width), BF16)], n_in=2, after=1)
+    add_halves = call(add_kernel, [((wide, block), BF16)], n_in=2)
+    far_masks = [seq >> level for level in range(1, slots.bit_length())]
+    dkv, dq, kept, summed, later = {}, None, None, {}, []
     for at, r in enumerate(order):
-        later = []
-        if at == columns // 2:
+        if at and not halves and at == columns - 1 or halves and at == 1:
             weight_terms = call(
                 functools.partial(project_grad_kernel, slots, rows, a_of, b_of, halves),
                 [((2, dim, width), BF16)] * 2 if halves else [((heads, dim, width), BF16)],
@@ -353,36 +350,40 @@
                 kept, sent = call(add_pairs_kernel, [((dim, width), BF16)] * 2, n_in=2, after=1)(
                     weight_terms[0], swap(weight_terms[1], 1), terms)
                 later = [kept]
-        if at == columns - 1 and halves:
-            kept = call(add_kernel, [((dim, width), BF16)], n_in=2, after=1)(kept, swap(sent, 2), dkv[order[at - 1]])[0]
+        if at == 2 and halves:
+            kept = add(kept, swap(sent, 2), dkv[order[at - 1]])[0]
             later = [kept]
+        if at == 3 and halves:
+            kept = add(kept, swap(kept, far_masks[0]), dkv[order[at - 1]])[0]
+            later = [kept, summed[2]]
         operands = [scored[r][0], *prepared[r], q_all, grads, factors[r], inner] + ([] if dq is None else [dq])
         dkv[r], dq = call(
             functools.partial(back_kernel, slots, rows, dim, dq is None),
             [((wide, block), BF16), ((dim, block), F32)], [pltpu.VMEM((2 * wide, block), BF16)],
             n_in=len(operands), after=len(later), micros=2,
         )(*operands, *later)
-
-    bit, done = 1, terms
-    while bit < mp:
-        terms, done = call(add_out_kernel, [((rows, width), BF16), ((8, 128), F32)], n_in=2)(
-            terms, swap(terms, bit, "mp", mp))
-        bit *= 2
-
-    dkv_last = dkv[order[-1]]
-    bit = 1
-    while 2 * bit < columns:
-        dkv = {
-            r: call(add_kernel, [((wide, block), BF16)], n_in=2)(dkv[r], swap(dkv[r ^ bit], bit))[0]
-            for r in order if r in dkv and not r & bit
-        }
-        bit *= 2
-    returned = exchange(call(
-        functools.partial(add_pieces_kernel, slots, rows, dim), [((wide + dim, rows), BF16)] * slots, n_in=3, after=1,
-    )(dkv[0], swap(dkv[bit], bit), dq, done))
+        later = []
+        if columns == 4 and r == 2:
+            summed[2] = swap(add_halves(dkv[2], swap(dkv[3], 1))[0], 2)
+
+    attention_out = lax.psum(terms, "mp") if mp > 1 else terms
+
+    if columns == 4:
+        halved = add_halves(dkv[0], swap(dkv[1], 1))[0], summed[2]
+    else:
+        bit = 1
+        while 2 * bit < columns:
+            dkv = {r: add_halves(dkv[r], swap(dkv[r ^ bit], bit))[0] for r in order if r in dkv and not r & bit}
+            bit *= 2
+        halved = dkv[0], swap(dkv[bit], bit)
+    pieces = call(
+        functools.partial(add_pieces_kernel, slots, rows, dim), [((wide + dim, rows), BF16)] * slots, n_in=3,
+    )(*halved, dq)
+    returned = exchange(pieces)
+
     if halves:
-        for mask in [seq >> step for step in range(1, slots.bit_length())]:
-            kept = call(add_kernel, [((dim, width), BF16)], n_in=2, after=1)(kept, swap(kept, mask), dkv_last)[0]
+        for mask in far_masks[1:]:
+            kept = add(kept, swap(kept, mask), dkv[0])[0]
         across = swap(kept, 2)
         weight_grad = call(
             functools.partial(place_kernel, columns, b_of), [((heads, dim, width), F32)], n_in=columns, micros=0.5,
@@ -395,7 +396,7 @@
         [((rows, heads, wide), F32), ((heads, dim, rows), F32)],
         [pltpu.VMEM((heads, rows, wide), F32)], n_in=slots, micros=1,
     )(*returned)
-    return terms, jnp.transpose(query_grad, (2, 0, 1)), key_value_grad, weight_grad
+    return attention_out, jnp.transpose(query_grad, (2, 0, 1)), key_value_grad, weight_grad
 
 
 def solution(mesh):

time: 75.4 us -> 98.2 us (1.30)
  between operations: 0.96 us -> 14.4 us
  local copies, waits for them, and re-layouts: 0.02 us -> 9.17 us
  waiting for transfers between devices: 12.7 us -> 19.3 us
  starting transfers between devices: 31.4 us -> 25 us
    unnamed x10 -> x35, local copies, waits for them, and re-layouts: 0.02 us -> 9.17 us
    ppermute x26 -> x25, starting transfers between devices: 31.4 us -> 24.8 us  [swap(): return lax.ppermute(array, axis, [(i, i ^ mask) for i in range(size)])]
    ppermute x26 -> x25, waiting for transfers between devices: 12.7 us -> 16 us  [swap(): return lax.ppermute(array, axis, [(i, i ^ mask) for i in range(size)])]
    psum x0 -> x1, waiting for transfers between devices: none -> 3.27 us  [shards(): attention_out = lax.psum(terms, 'mp') if mp > 1 else terms]
  transfers between devices with their start and end apart: 26 -> 26, of which waited for: 10 -> 10; matrix products, arithmetic and copies ran while one was open for 0% -> 0% of each run, Pallas kernels for 30% -> 24%
where the time goes in v9:
time: 98.2 us; the launch traced here: 98 us
  Pallas kernels  30.1 us (31%)
  starting transfers between devices  25 us (25%)
  waiting for transfers between devices  19.3 us (20%)
  between operations  14.4 us (15%)
  local copies, waits for them, and re-layouts  9.17 us (9%)
    ppermute x25, starting transfers between devices, swap(): return lax.ppermute(array, axis, [(i, i ^ mask) for i in range(size)])  24.8 us
    ppermute x25, waiting for transfers between devices, swap(): return lax.ppermute(array, axis, [(i, i ^ mask) for i in range(size)])  16 us
    pallas_call x4, Pallas kernels, shards(): call(functools.partial(score_kernel, slots, rows, dim, step), [((block, b...  10.9 us
    unnamed x35, local copies, waits for them, and re-layouts  9.17 us
    pallas_call x4, Pallas kernels, shards(): call(functools.partial(back_kernel, slots, rows, dim, dq is None), [((wid...  9.06 us
    psum x1, waiting for transfers between devices, shards(): attention_out = lax.psum(terms, 'mp') if mp > 1 else terms  3.27 us
    pallas_call x1, Pallas kernels, shards(): call(functools.partial(pack_kv_kernel, heads, rows, dim, a_of), [((rows,...  2.53 us
  transfers between devices with their start and end apart: 26, of which 10 were waited for; matrix products, arithmetic and copies ran while one was open for 0% of the time, Pallas kernels for 24%

profile of v9, /device:TPU:0, one launch (start us, length us, event | category | flops | bytes accessed | tf_op | source)
XLA Modules:
  0.0 98.0 jit_solution(13369987692836437417)
XLA Ops:
  7.2 2.5 %shard_map.84 = (bf16[256,128]{1,0:T(8,128)(2,1)}, bf16[256,128]{1,0:T(8,128)(2,1)}, bf16[256,128]{1,0:T(8,128)(2,1)}, bf16[256,128]{1,0:T(8,128)(2,1)}) custom-call(s32[2]{0:T(128)} %fill_ref.7, bf16[256,4,128]{2,1,0:T(4,128)(2,1)} %kv_ref.1), custom_call_target="tpu_custom_call" | custom-call | flops 1724999936 | tf_op jit(solution)/shard_map/pallas_call | solution.py:286
  9.7 4.0 %collective-permute-start = (bf16[256,128]{1,0:T(8,128)(2,1)}, bf16[256,128]{1,0:T(8,128)(2,1)S(1)}, u32[]{:S(2)}, u32[]{:S(2)}) collective-permute-start(bf16[256,128]{1,0:T(8,128)(2,1)} %get-tuple-element.72), channel_id=1, source_target_pairs={{0,16},{2,18},{4,20},{6,22},{8,24},{10,26},{12,28},{14,30},{16,0},... | collective-permute-start | bytes 196616 | tf_op jit(solution)/shard_map/ppermute | solution.py:280
  13.8 1.3 %collective-permute-start.1 = (bf16[256,128]{1,0:T(8,128)(2,1)}, bf16[256,128]{1,0:T(8,128)(2,1)S(1)}, u32[]{:S(2)}, u32[]{:S(2)}) collective-permute-start(bf16[256,128]{1,0:T(8,128)(2,1)} %get-tuple-element.73), channel_id=1, source_target_pairs={{0,24},{2,26},{4,28},{6,30},{8,16},{10,18},{12,20},{14,22},{16,8},... | collective-permute-start | bytes 196616 | tf_op jit(solution)/shard_map/ppermute | solution.py:280
  15.1 0.2 collective-permute-start.2
  15.4 0.9 shard_map.85
  16.3 2.9 %collective-permute-start.3 = (bf16[128,256]{1,0:T(8,128)(2,1)S(1)}, bf16[128,256]{1,0:T(8,128)(2,1)S(1)}, u32[]{:S(2)}, u32[]{:S(2)}) collective-permute-start(bf16[128,256]{1,0:T(8,128)(2,1)S(1)} %get-tuple-element.79), channel_id=1, source_target_pairs={{0,16},{2,18},{4,20},{6,22},{8,24},{10,26},{12,28},{14,30},{16,0},... | collective-permute-start | bytes 196616 | tf_op jit(solution)/shard_map/ppermute | solution.py:280
  19.2 1.3 %collective-permute-start.4 = (bf16[128,256]{1,0:T(8,128)(2,1)S(1)}, bf16[128,256]{1,0:T(8,128)(2,1)S(1)}, u32[]{:S(2)}, u32[]{:S(2)}) collective-permute-start(bf16[128,256]{1,0:T(8,128)(2,1)S(1)} %get-tuple-element.80), channel_id=1, source_target_pairs={{0,24},{2,26},{4,28},{6,30},{8,16},{10,18},{12,20},{14,22},{16,8},... | collective-permute-start | bytes 196616 | tf_op jit(solution)/shard_map/ppermute | solution.py:280
  20.6 1.6 %collective-permute-start.7 = (bf16[1024,128]{1,0:T(8,128)(2,1)S(1)}, bf16[1024,128]{1,0:T(8,128)(2,1)S(1)}, u32[]{:S(2)}, u32[]{:S(2)}) collective-permute-start(bf16[1024,128]{1,0:T(8,128)(2,1)S(1)} %shard_map.86.pair_ref), channel_id=1, source_target_pairs={{0,4},{2,6},{4,0},{6,2},{8,12},{10,14},{12,8},{14,10},{16,20},{18,... | collective-permute-start | bytes 786440 | tf_op jit(solution)/shard_map/ppermute | solution.py:280
  22.2 0.3 shard_map.87
  22.5 0.0 copy-start.11
  22.5 1.8 %collective-permute-done.3.refs_1_ = bf16[128,256]{1,0:T(8,128)(2,1)S(1)} collective-permute-done((bf16[128,256]{1,0:T(8,128)(2,1)S(1)}, bf16[128,256]{1,0:T(8,128)(2,1)S(1)}, u32[]{:S(2)}, u32[]{:S(2)}) %collective-permute-start.3) | collective-permute-done | bytes 65568 | tf_op jit(solution)/shard_map/ppermute | solution.py:280
  24.4 1.1 %collective-permute-done.4.refs_2_ = bf16[128,256]{1,0:T(8,128)(2,1)S(1)} collective-permute-done((bf16[128,256]{1,0:T(8,128)(2,1)S(1)}, bf16[128,256]{1,0:T(8,128)(2,1)S(1)}, u32[]{:S(2)}, u32[]{:S(2)}) %collective-permute-start.4) | collective-permute-done | bytes 65568 | tf_op jit(solution)/shard_map/ppermute | solution.py:280
  25.4 0.2 collective-permute-done.5.refs_3_
  25.6 0.1 shard_map.88
  25.8 2.7 %shard_map.89 = (bf16[1024,1024]{1,0:T(8,128)(2,1)S(1)}, f32[1,1024]{1,0:T(1,128)S(1)}, f32[80,1024]{1,0:T(8,128)S(1)}) custom-call(bf16[1024,256]{1,0:T(8,128)(2,1)S(1)} %get-tuple-element.76.wide_ref, bf16[80,1024]{1,0:T(8,128)(2,1)S(1)} %get-tuple-element.77.vt_ref, f32[1,1024]{1,0:T(1,128)S(1)} %get-tuple-element.78.norm_ref, ...), custom_call_target="tpu_custom_call" | custom-call | flops 4600000000 | tf_op jit(solution)/shard_map/pallas_call | solution.py:319
  28.5 1.3 %copy-done.5 = bf16[1024,1024]{1,0:T(8,128)(2,1)} copy-done((bf16[1024,1024]{1,0:T(8,128)(2,1)}, bf16[1024,1024]{1,0:T(8,128)(2,1)S(1)}, u32[]{:S(2)}) %copy-start.5) | copy-done | bytes 2097176
  29.8 0.3 shard_map.92
  30.1 0.0 copy-start.15
  30.2 2.7 %shard_map.93 = (bf16[1024,1024]{1,0:T(8,128)(2,1)S(1)}, f32[1,1024]{1,0:T(1,128)S(1)}, f32[80,1024]{1,0:T(8,128)S(1)}) custom-call(bf16[1024,256]{1,0:T(8,128)(2,1)S(1)} %get-tuple-element.89.wide_ref, bf16[80,1024]{1,0:T(8,128)(2,1)S(1)} %get-tuple-element.90.vt_ref, f32[1,1024]{1,0:T(1,128)S(1)} %get-tuple-element.91.norm_ref, ...), custom_call_target="tpu_custom_call" | custom-call | flops 4600000000 | tf_op jit(solution)/shard_map/pallas_call | solution.py:319
  32.9 0.3 shard_map.90
  33.2 1.0 %copy-done.9 = bf16[1024,1024]{1,0:T(8,128)(2,1)} copy-done((bf16[1024,1024]{1,0:T(8,128)(2,1)}, bf16[1024,1024]{1,0:T(8,128)(2,1)S(1)}, u32[]{:S(2)}) %copy-start.9) | copy-done | bytes 2097176
  34.2 0.7 copy-done.13
  34.9 2.9 %shard_map.91 = (bf16[1024,1024]{1,0:T(8,128)(2,1)S(1)}, f32[1,1024]{1,0:T(1,128)S(1)}, f32[80,1024]{1,0:T(8,128)S(1)}) custom-call(bf16[1024,256]{1,0:T(8,128)(2,1)S(1)} %get-tuple-element.85.wide_ref, bf16[80,1024]{1,0:T(8,128)(2,1)S(1)} %get-tuple-element.86.vt_ref, f32[1,1024]{1,0:T(1,128)S(1)} %get-tuple-element.87.norm_ref, ...), custom_call_target="tpu_custom_call" | custom-call | flops 4600000000 | tf_op jit(solution)/shard_map/pallas_call | solution.py:319
  37.8 0.3 shard_map.94
  38.1 1.0 %copy-done.7 = bf16[1024,1024]{1,0:T(8,128)(2,1)} copy-done((bf16[1024,1024]{1,0:T(8,128)(2,1)}, bf16[1024,1024]{1,0:T(8,128)(2,1)S(1)}, u32[]{:S(2)}) %copy-start.7) | copy-done | bytes 2097176
  39.1 2.7 %shard_map.95 = (bf16[1024,1024]{1,0:T(8,128)(2,1)S(1)}, f32[1,1024]{1,0:T(1,128)S(1)}, f32[80,1024]{1,0:T(8,128)S(1)}) custom-call(bf16[1024,256]{1,0:T(8,128)(2,1)S(1)} %get-tuple-element.93.wide_ref, bf16[80,1024]{1,0:T(8,128)(2,1)S(1)} %get-tuple-element.94.vt_ref, f32[1,1024]{1,0:T(1,128)S(1)} %get-tuple-element.95.norm_ref, ...), custom_call_target="tpu_custom_call" | custom-call | flops 4600000000 | tf_op jit(solution)/shard_map/pallas_call | solution.py:319
  41.8 0.2 shard_map.96
  42.0 3.1 %collective-permute-start.9 = (bf16[64,256]{1,0:T(8,128)(2,1)S(1)}, bf16[64,256]{1,0:T(8,128)(2,1)S(1)}, u32[]{:S(2)}, u32[]{:S(2)}) collective-permute-start(bf16[64,256]{1,0:T(8,128)(2,1)S(1)} %get-tuple-element.103), channel_id=1, source_target_pairs={{0,16},{2,18},{4,20},{6,22},{8,24},{10,26},{12,28},{14,30},{16,0},... | collective-permute-start | bytes 98312 | tf_op jit(solution)/shard_map/ppermute | solution.py:280
  45.1 0.4 collective-permute-start.10
  45.5 0.2 collective-permute-start.11
  45.7 2.3 %shard_map.97 = (bf16[128,1024]{1,0:T(8,128)(2,1)S(1)}, f32[64,1024]{1,0:T(8,128)S(1)}) custom-call(bf16[1024,1024]{1,0:T(8,128)(2,1)S(1)} %get-tuple-element.106.exp_ref, bf16[1024,256]{1,0:T(8,128)(2,1)S(1)} %get-tuple-element.93.wide_ref, bf16[64,1024]{1,0:T(8,128)(2,1)S(1)} %get-tuple-element.107.kt_ref, bf16[64,1024]{1,0:T(8,128)(2,1)S(1)} %get-tuple-element.108.q_ref, ...), custom_call_target="tpu_custom_call" | custom-call | flops 2300000000 | tf_op jit(solution)/shard_map/pallas_call | solution.py:360
  48.0 2.8 %collective-permute-done.10.refs_2_ = bf16[64,256]{1,0:T(8,128)(2,1)S(1)} collective-permute-done((bf16[64,256]{1,0:T(8,128)(2,1)S(1)}, bf16[64,256]{1,0:T(8,128)(2,1)S(1)}, u32[]{:S(2)}, u32[]{:S(2)}) %collective-permute-start.10) | collective-permute-done | bytes 32800 | tf_op jit(solution)/shard_map/ppermute | solution.py:280
  50.8 0.9 shard_map.98
  51.7 0.1 collective-permute-start.12
  51.8 0.5 collective-permute-start.15
  52.3 1.6 %shard_map.99._ = bf16[256,768]{1,0:T(8,128)(2,1)} custom-call(s32[2]{0:T(128)S(1)} %copy-done.4, bf16[4,64,768]{2,1,0:T(8,128)(2,1)S(1)} %copy-done.2, bf16[64,256]{1,0:T(8,128)(2,1)S(1)} %get-tuple-element.102.refs_0_, bf16[64,256]{1,0:T(8,128)(2,1)S(1)} %collective-permute-done.9.refs_1_, bf16[64,256]{1,0:T(8,128)(2,1)S(1)} %collective-permute-done.10.refs_2_, ...), custom_call_target="tpu_custom_call" | custom-call | flops 805000000 | tf_op jit(solution)/shard_map/pallas_call | solution.py:344
  54.0 0.3 all-reduce.2.cloned.1.call-start
  54.2 1.5 %collective-permute-start.13 = (bf16[64,768]{1,0:T(8,128)(2,1)S(1)}, bf16[64,768]{1,0:T(8,128)(2,1)S(1)}, u32[]{:S(2)}, u32[]{:S(2)}) collective-permute-start(bf16[64,768]{1,0:T(8,128)(2,1)S(1)} %get-tuple-element.126), channel_id=1, source_target_pairs={{0,4},{2,6},{4,0},{6,2},{8,12},{10,14},{12,8},{14,10},{16,20},{18,... | collective-permute-start | bytes 294920 | tf_op jit(solution)/shard_map/ppermute | solution.py:280
  55.8 1.6 %copy-done.10 = bf16[1024,1024]{1,0:T(8,128)(2,1)S(1)} copy-done((bf16[1024,1024]{1,0:T(8,128)(2,1)S(1)}, bf16[1024,1024]{1,0:T(8,128)(2,1)}, u32[]{:S(2)}) %copy-start.10) | copy-done | bytes 2097176
  57.4 2.2 %shard_map.101 = (bf16[128,1024]{1,0:T(8,128)(2,1)S(1)}, f32[64,1024]{1,0:T(8,128)S(1)}) custom-call(bf16[1024,1024]{1,0:T(8,128)(2,1)S(1)} %copy-done.10, bf16[1024,256]{1,0:T(8,128)(2,1)S(1)} %get-tuple-element.89.wide_ref, bf16[64,1024]{1,0:T(8,128)(2,1)S(1)} %copy-done.16, bf16[64,1024]{1,0:T(8,128)(2,1)S(1)} %get-tuple-element.108.q_ref, ...), custom_call_target="tpu_custom_call" | custom-call | flops 2300000000 | tf_op jit(solution)/shard_map/pallas_call | solution.py:360
  59.6 0.1 shard_map.105
  59.7 0.6 collective-permute-start.16
  60.4 1.0 %collective-permute-start.14 = (bf16[64,768]{1,0:T(8,128)(2,1)S(1)}, bf16[64,768]{1,0:T(8,128)(2,1)S(1)}, u32[]{:S(2)}, u32[]{:S(2)}) collective-permute-start(bf16[64,768]{1,0:T(8,128)(2,1)S(1)} %shard_map.102.refs_1_.a_ref), channel_id=1, source_target_pairs={{0,16},{2,18},{4,20},{6,22},{8,24},{10,26},{12,28},{14,30},{16,0},... | collective-permute-start | bytes 294920 | tf_op jit(solution)/shard_map/ppermute | solution.py:280
  61.4 2.3 %shard_map.103 = (bf16[128,1024]{1,0:T(8,128)(2,1)S(1)}, f32[64,1024]{1,0:T(8,128)S(1)}) custom-call(bf16[1024,1024]{1,0:T(8,128)(2,1)S(1)} %copy-done.8, bf16[1024,256]{1,0:T(8,128)(2,1)S(1)} %get-tuple-element.85.wide_ref, bf16[64,1024]{1,0:T(8,128)(2,1)S(1)} %copy-done.14, bf16[64,1024]{1,0:T(8,128)(2,1)S(1)} %get-tuple-element.108.q_ref, ...), custom_call_target="tpu_custom_call" | custom-call | flops 2300000000 | tf_op jit(solution)/shard_map/pallas_call | solution.py:360
  63.7 0.1 collective-permute-start.17
  63.8 0.0 all-reduce.2.cloned.1.call-update
  63.8 3.2 %collective-permute-done.14.b_ref = bf16[64,768]{1,0:T(8,128)(2,1)S(1)} collective-permute-done((bf16[64,768]{1,0:T(8,128)(2,1)S(1)}, bf16[64,768]{1,0:T(8,128)(2,1)S(1)}, u32[]{:S(2)}, u32[]{:S(2)}) %collective-permute-start.14) | collective-permute-done | bytes 98336 | tf_op jit(solution)/shard_map/ppermute | solution.py:280
  67.1 0.1 collective-permute-start.21
  67.1 0.6 collective-permute-done.16.refs_2_.came_ref
  67.8 1.7 %copy-done.6 = bf16[1024,1024]{1,0:T(8,128)(2,1)S(1)} copy-done((bf16[1024,1024]{1,0:T(8,128)(2,1)S(1)}, bf16[1024,1024]{1,0:T(8,128)(2,1)}, u32[]{:S(2)}) %copy-start.6) | copy-done | bytes 2097176
  69.5 2.3 %shard_map.106 = (bf16[128,1024]{1,0:T(8,128)(2,1)S(1)}, f32[64,1024]{1,0:T(8,128)S(1)}) custom-call(bf16[1024,1024]{1,0:T(8,128)(2,1)S(1)} %copy-done.6, bf16[1024,256]{1,0:T(8,128)(2,1)S(1)} %get-tuple-element.76.wide_ref, bf16[64,1024]{1,0:T(8,128)(2,1)S(1)} %copy-done.12, bf16[64,1024]{1,0:T(8,128)(2,1)S(1)} %get-tuple-element.108.q_ref, ...), custom_call_target="tpu_custom_call" | custom-call | flops 2300000000 | tf_op jit(solution)/shard_map/pallas_call | solution.py:360
  71.7 0.1 collective-permute-done.21.b_ref
  71.8 1.5 %collective-permute-start.23 = (bf16[64,768]{1,0:T(8,128)(2,1)S(1)}, bf16[64,768]{1,0:T(8,128)(2,1)S(1)}, u32[]{:S(2)}, u32[]{:S(2)}) collective-permute-start(bf16[64,768]{1,0:T(8,128)(2,1)S(1)} %shard_map.110.refs_0_), channel_id=1, source_target_pairs={{0,4},{2,6},{4,0},{6,2},{8,12},{10,14},{12,8},{14,10},{16,20},{18,... | collective-permute-start | bytes 294920 | tf_op jit(solution)/shard_map/ppermute | solution.py:280
  73.4 0.1 shard_map.107.kept_ref
  73.5 0.1 shard_map.108
  73.5 2.3 %collective-permute-start.18 = (bf16[192,256]{1,0:T(8,128)(2,1)S(1)}, bf16[192,256]{1,0:T(8,128)(2,1)S(1)}, u32[]{:S(2)}, u32[]{:S(2)}) collective-permute-start(bf16[192,256]{1,0:T(8,128)(2,1)S(1)} %get-tuple-element.133), channel_id=1, source_target_pairs={{0,16},{2,18},{4,20},{6,22},{8,24},{10,26},{12,28},{14,30},{16,0},... | collective-permute-start | bytes 294920 | tf_op jit(solution)/shard_map/ppermute | solution.py:280
  75.8 1.3 %collective-permute-start.19 = (bf16[192,256]{1,0:T(8,128)(2,1)S(1)}, bf16[192,256]{1,0:T(8,128)(2,1)S(1)}, u32[]{:S(2)}, u32[]{:S(2)}) collective-permute-start(bf16[192,256]{1,0:T(8,128)(2,1)S(1)} %get-tuple-element.134), channel_id=1, source_target_pairs={{0,24},{2,26},{4,28},{6,30},{8,16},{10,18},{12,20},{14,22},{16,8},... | collective-permute-start | bytes 294920 | tf_op jit(solution)/shard_map/ppermute | solution.py:280
  77.2 0.5 collective-permute-start.24
  77.7 5.7 %collective-permute-done.18.refs_1_ = bf16[192,256]{1,0:T(8,128)(2,1)S(1)} collective-permute-done((bf16[192,256]{1,0:T(8,128)(2,1)S(1)}, bf16[192,256]{1,0:T(8,128)(2,1)S(1)}, u32[]{:S(2)}, u32[]{:S(2)}) %collective-permute-start.18) | collective-permute-done | bytes 98336 | tf_op jit(solution)/shard_map/ppermute | solution.py:280
  83.4 0.4 collective-permute-done.20.refs_3_
  83.8 1.3 %shard_map.109 = (f32[256,4,128]{2,1,0:T(4,128)}, f32[4,64,256]{2,1,0:T(8,128)}) custom-call(bf16[192,256]{1,0:T(8,128)(2,1)S(1)} %get-tuple-element.132.refs_0_, bf16[192,256]{1,0:T(8,128)(2,1)S(1)} %collective-permute-done.18.refs_1_, bf16[192,256]{1,0:T(8,128)(2,1)S(1)} %collective-permute-done.19.refs_2_, ...), custom_call_target="tpu_custom_call" | custom-call | flops 1150000000 | tf_op jit(solution)/shard_map/pallas_call | solution.py:394
  85.1 0.9 shard_map.111
  86.1 3.3 %all-reduce.2.cloned.1.call-done = bf16[256,768]{1,0:T(8,128)(2,1)} async-done(((bf16[256,768]{1,0:T(8,128)(2,1)}), bf16[256,768]{1,0:T(8,128)(2,1)}) %all-reduce.2.cloned.1.call-update) | async-done | bytes 393232 | tf_op jit(solution)/shard_map/psum | solution.py:369
  89.3 1.8 %copy.10 = bf16[256,768]{1,0:T(8,128)(2,1)} copy(bf16[256,768]{1,0:T(8,128)(2,1)} %all-reduce.2.cloned.1.call-done) | data formatting | bytes 786432
  (52 shorter events, 0.3 us)
Async XLA Ops:
  7.2 8.2 %copy-start.4 = (s32[2]{0:T(128)S(1)}, s32[2]{0:T(128)}, u32[]{:S(2)}) copy-start(s32[2]{0:T(128)} %fill_ref.7) | copy-start | bytes 28
  7.2 8.2 %copy-start.1 = (bf16[256,768]{1,0:T(8,128)(2,1)S(1)}, bf16[256,768]{1,0:T(8,128)(2,1)}, u32[]{:S(2)}) copy-start(bf16[256,768]{1,0:T(8,128)(2,1)} %go_ref.3) | copy-start | bytes 1179652
  7.2 8.2 %copy-start.2 = (bf16[4,64,768]{2,1,0:T(8,128)(2,1)S(1)}, bf16[4,64,768]{2,1,0:T(8,128)(2,1)}, u32[]{:S(2)}) copy-start(bf16[4,64,768]{2,1,0:T(8,128)(2,1)} %w_ref.3) | copy-start | bytes 1179652
  7.2 8.2 %copy-start.3 = (bf16[256,4,64]{0,2,1:T(8,128)(2,1)S(1)}, bf16[256,4,64]{0,2,1:T(8,128)(2,1)}, u32[]{:S(2)}) copy-start(bf16[256,4,64]{0,2,1:T(8,128)(2,1)} %param.5) | copy-start | bytes 393220
  9.7 10.8 %collective-permute-start = (bf16[256,128]{1,0:T(8,128)(2,1)}, bf16[256,128]{1,0:T(8,128)(2,1)S(1)}, u32[]{:S(2)}, u32[]{:S(2)}) collective-permute-start(bf16[256,128]{1,0:T(8,128)(2,1)} %get-tuple-element.72), channel_id=1, source_target_pairs={{0,16},{2,18},{4,20},{6,22},{8,24},{10,26},{12,28},{14,30},{16,0},... | collective-permute-start | bytes 196616 | tf_op jit(solution)/shard_map/ppermute | solution.py:280
  13.8 6.8 %collective-permute-start.1 = (bf16[256,128]{1,0:T(8,128)(2,1)}, bf16[256,128]{1,0:T(8,128)(2,1)S(1)}, u32[]{:S(2)}, u32[]{:S(2)}) collective-permute-start(bf16[256,128]{1,0:T(8,128)(2,1)} %get-tuple-element.73), channel_id=1, source_target_pairs={{0,24},{2,26},{4,28},{6,30},{8,16},{10,18},{12,20},{14,22},{16,8},... | collective-permute-start | bytes 196616 | tf_op jit(solution)/shard_map/ppermute | solution.py:280
  15.1 5.4 %collective-permute-start.2 = (bf16[256,128]{1,0:T(8,128)(2,1)}, bf16[256,128]{1,0:T(8,128)(2,1)S(1)}, u32[]{:S(2)}, u32[]{:S(2)}) collective-permute-start(bf16[256,128]{1,0:T(8,128)(2,1)} %get-tuple-element.74), channel_id=1, source_target_pairs={{0,8},{2,10},{4,12},{6,14},{8,0},{10,2},{12,4},{14,6},{16,24},{18,... | collective-permute-start | bytes 196616 | tf_op jit(solution)/shard_map/ppermute | solution.py:280
  15.4 5.2 %copy-start = (bf16[256,128]{1,0:T(8,128)(2,1)S(1)}, bf16[256,128]{1,0:T(8,128)(2,1)}, u32[]{:S(2)}) copy-start(bf16[256,128]{1,0:T(8,128)(2,1)} %get-tuple-element.71.refs_0_) | copy-start | bytes 196612
  16.3 8.0 %collective-permute-start.3 = (bf16[128,256]{1,0:T(8,128)(2,1)S(1)}, bf16[128,256]{1,0:T(8,128)(2,1)S(1)}, u32[]{:S(2)}, u32[]{:S(2)}) collective-permute-start(bf16[128,256]{1,0:T(8,128)(2,1)S(1)} %get-tuple-element.79), channel_id=1, source_target_pairs={{0,16},{2,18},{4,20},{6,22},{8,24},{10,26},{12,28},{14,30},{16,0},... | collective-permute-start | bytes 196616 | tf_op jit(solution)/shard_map/ppermute | solution.py:280
  19.2 6.2 %collective-permute-start.4 = (bf16[128,256]{1,0:T(8,128)(2,1)S(1)}, bf16[128,256]{1,0:T(8,128)(2,1)S(1)}, u32[]{:S(2)}, u32[]{:S(2)}) collective-permute-start(bf16[128,256]{1,0:T(8,128)(2,1)S(1)} %get-tuple-element.80), channel_id=1, source_target_pairs={{0,24},{2,26},{4,28},{6,30},{8,16},{10,18},{12,20},{14,22},{16,8},... | collective-permute-start | bytes 196616 | tf_op jit(solution)/shard_map/ppermute | solution.py:280
  20.6 5.1 %collective-permute-start.5 = (bf16[128,256]{1,0:T(8,128)(2,1)S(1)}, bf16[128,256]{1,0:T(8,128)(2,1)S(1)}, u32[]{:S(2)}, u32[]{:S(2)}) collective-permute-start(bf16[128,256]{1,0:T(8,128)(2,1)S(1)} %get-tuple-element.81), channel_id=1, source_target_pairs={{0,8},{2,10},{4,12},{6,14},{8,0},{10,2},{12,4},{14,6},{16,24},{18,... | collective-permute-start | bytes 196616 | tf_op jit(solution)/shard_map/ppermute | solution.py:280
  20.6 9.2 %collective-permute-start.7 = (bf16[1024,128]{1,0:T(8,128)(2,1)S(1)}, bf16[1024,128]{1,0:T(8,128)(2,1)S(1)}, u32[]{:S(2)}, u32[]{:S(2)}) collective-permute-start(bf16[1024,128]{1,0:T(8,128)(2,1)S(1)} %shard_map.86.pair_ref), channel_id=1, source_target_pairs={{0,4},{2,6},{4,0},{6,2},{8,12},{10,14},{12,8},{14,10},{16,20},{18,... | collective-permute-start | bytes 786440 | tf_op jit(solution)/shard_map/ppermute | solution.py:280
  22.2 10.7 %collective-permute-start.6 = (bf16[1024,128]{1,0:T(8,128)(2,1)S(1)}, bf16[1024,128]{1,0:T(8,128)(2,1)S(1)}, u32[]{:S(2)}, u32[]{:S(2)}) collective-permute-start(bf16[1024,128]{1,0:T(8,128)(2,1)S(1)} %shard_map.86.pair_ref), channel_id=1, source_target_pairs={{0,2},{2,0},{4,6},{6,4},{8,10},{10,8},{12,14},{14,12},{16,18},{18,... | collective-permute-start | bytes 786440 | tf_op jit(solution)/shard_map/ppermute | solution.py:280
  22.5 5.9 %copy-start.11 = (bf16[64,1024]{1,0:T(8,128)(2,1)}, bf16[64,1024]{1,0:T(8,128)(2,1)S(1)}, u32[]{:S(2)}) copy-start(bf16[64,1024]{1,0:T(8,128)(2,1)S(1)} %get-tuple-element.114.kt_ref) | copy-start | bytes 393220
  28.5 1.4 %copy-start.5 = (bf16[1024,1024]{1,0:T(8,128)(2,1)}, bf16[1024,1024]{1,0:T(8,128)(2,1)S(1)}, u32[]{:S(2)}) copy-start(bf16[1024,1024]{1,0:T(8,128)(2,1)S(1)} %get-tuple-element.113.exp_ref) | copy-start | bytes 6291460
  29.8 7.9 %collective-permute-start.8 = (bf16[1024,128]{1,0:T(8,128)(2,1)S(1)}, bf16[1024,128]{1,0:T(8,128)(2,1)S(1)}, u32[]{:S(2)}, u32[]{:S(2)}) collective-permute-start(bf16[1024,128]{1,0:T(8,128)(2,1)S(1)} %collective-permute-done.7.pair_ref), channel_id=1, source_target_pairs={{0,2},{2,0},{4,6},{6,4},{8,10},{10,8},{12,14},{14,12},{16,18},{18,... | collective-permute-start | bytes 786440 | tf_op jit(solution)/shard_map/ppermute | solution.py:280
  30.1 2.7 %copy-start.15 = (bf16[64,1024]{1,0:T(8,128)(2,1)}, bf16[64,1024]{1,0:T(8,128)(2,1)S(1)}, u32[]{:S(2)}) copy-start(bf16[64,1024]{1,0:T(8,128)(2,1)S(1)} %get-tuple-element.120.kt_ref) | copy-start | bytes 393220
  32.9 1.4 %copy-start.9 = (bf16[1024,1024]{1,0:T(8,128)(2,1)}, bf16[1024,1024]{1,0:T(8,128)(2,1)S(1)}, u32[]{:S(2)}) copy-start(bf16[1024,1024]{1,0:T(8,128)(2,1)S(1)} %get-tuple-element.119.exp_ref) | copy-start | bytes 6291460
  34.2 0.7 copy-start.13
  37.7 1.4 %copy-start.7 = (bf16[1024,1024]{1,0:T(8,128)(2,1)}, bf16[1024,1024]{1,0:T(8,128)(2,1)S(1)}, u32[]{:S(2)}) copy-start(bf16[1024,1024]{1,0:T(8,128)(2,1)S(1)} %get-tuple-element.116.exp_ref) | copy-start | bytes 6291460
  42.0 6.0 %collective-permute-start.9 = (bf16[64,256]{1,0:T(8,128)(2,1)S(1)}, bf16[64,256]{1,0:T(8,128)(2,1)S(1)}, u32[]{:S(2)}, u32[]{:S(2)}) collective-permute-start(bf16[64,256]{1,0:T(8,128)(2,1)S(1)} %get-tuple-element.103), channel_id=1, source_target_pairs={{0,16},{2,18},{4,20},{6,22},{8,24},{10,26},{12,28},{14,30},{16,0},... | collective-permute-start | bytes 98312 | tf_op jit(solution)/shard_map/ppermute | solution.py:280
  45.1 5.7 %collective-permute-start.10 = (bf16[64,256]{1,0:T(8,128)(2,1)S(1)}, bf16[64,256]{1,0:T(8,128)(2,1)S(1)}, u32[]{:S(2)}, u32[]{:S(2)}) collective-permute-start(bf16[64,256]{1,0:T(8,128)(2,1)S(1)} %get-tuple-element.104), channel_id=1, source_target_pairs={{0,24},{2,26},{4,28},{6,30},{8,16},{10,18},{12,20},{14,22},{16,8},... | collective-permute-start | bytes 98312 | tf_op jit(solution)/shard_map/ppermute | solution.py:280
  45.5 5.3 %collective-permute-start.11 = (bf16[64,256]{1,0:T(8,128)(2,1)S(1)}, bf16[64,256]{1,0:T(8,128)(2,1)S(1)}, u32[]{:S(2)}, u32[]{:S(2)}) collective-permute-start(bf16[64,256]{1,0:T(8,128)(2,1)S(1)} %get-tuple-element.105), channel_id=1, source_target_pairs={{0,8},{2,10},{4,12},{6,14},{8,0},{10,2},{12,4},{14,6},{16,24},{18,... | collective-permute-start | bytes 98312 | tf_op jit(solution)/shard_map/ppermute | solution.py:280
  51.7 4.0 %copy-start.16 = (bf16[64,1024]{1,0:T(8,128)(2,1)S(1)}, bf16[64,1024]{1,0:T(8,128)(2,1)}, u32[]{:S(2)}) copy-start(bf16[64,1024]{1,0:T(8,128)(2,1)} %copy-done.15) | copy-start | bytes 393220
  51.7 2.2 %collective-permute-start.12 = (bf16[2,64,768]{2,1,0:T(8,128)(2,1)S(1)}, bf16[2,64,768]{2,1,0:T(8,128)(2,1)S(1)}, u32[]{:S(2)}, u32[]{:S(2)}) collective-permute-start(bf16[2,64,768]{2,1,0:T(8,128)(2,1)S(1)} %get-tuple-element.112.refs_4_), channel_id=1, source_target_pairs={{0,2},{2,0},{4,6},{6,4},{8,10},{10,8},{12,14},{14,12},{16,18},{18,... | collective-permute-start | bytes 589832 | tf_op jit(solution)/shard_map/ppermute | solution.py:280
  51.8 7.8 %collective-permute-start.15 = (bf16[128,1024]{1,0:T(8,128)(2,1)S(1)}, bf16[128,1024]{1,0:T(8,128)(2,1)S(1)}, u32[]{:S(2)}, u32[]{:S(2)}) collective-permute-start(bf16[128,1024]{1,0:T(8,128)(2,1)S(1)} %get-tuple-element.111.refs_4_), channel_id=1, source_target_pairs={{0,2},{2,0},{4,6},{6,4},{8,10},{10,8},{12,14},{14,12},{16,18},{18,... | collective-permute-start | bytes 786440 | tf_op jit(solution)/shard_map/ppermute | solution.py:280
  54.0 35.4 %all-reduce.2.cloned.1.call-start = ((), (), s32[]{:S(2)}) async-start(), calls=%async_computation | async-start | bytes 786432 | tf_op jit(solution)/shard_map/psum | solution.py:369
  54.2 6.1 %collective-permute-start.13 = (bf16[64,768]{1,0:T(8,128)(2,1)S(1)}, bf16[64,768]{1,0:T(8,128)(2,1)S(1)}, u32[]{:S(2)}, u32[]{:S(2)}) collective-permute-start(bf16[64,768]{1,0:T(8,128)(2,1)S(1)} %get-tuple-element.126), channel_id=1, source_target_pairs={{0,4},{2,6},{4,0},{6,2},{8,12},{10,14},{12,8},{14,10},{16,20},{18,... | collective-permute-start | bytes 294920 | tf_op jit(solution)/shard_map/ppermute | solution.py:280
  55.8 1.6 %copy-start.10 = (bf16[1024,1024]{1,0:T(8,128)(2,1)S(1)}, bf16[1024,1024]{1,0:T(8,128)(2,1)}, u32[]{:S(2)}) copy-start(bf16[1024,1024]{1,0:T(8,128)(2,1)} %copy-done.9) | copy-start | bytes 6291460
  57.4 4.0 %copy-start.8 = (bf16[1024,1024]{1,0:T(8,128)(2,1)S(1)}, bf16[1024,1024]{1,0:T(8,128)(2,1)}, u32[]{:S(2)}) copy-start(bf16[1024,1024]{1,0:T(8,128)(2,1)} %copy-done.7) | copy-start | bytes 6291460
  57.4 4.0 %copy-start.14 = (bf16[64,1024]{1,0:T(8,128)(2,1)S(1)}, bf16[64,1024]{1,0:T(8,128)(2,1)}, u32[]{:S(2)}) copy-start(bf16[64,1024]{1,0:T(8,128)(2,1)} %copy-done.13) | copy-start | bytes 393220
  59.7 8.1 %collective-permute-start.16 = (bf16[128,1024]{1,0:T(8,128)(2,1)S(1)}, bf16[128,1024]{1,0:T(8,128)(2,1)S(1)}, u32[]{:S(2)}, u32[]{:S(2)}) collective-permute-start(bf16[128,1024]{1,0:T(8,128)(2,1)S(1)} %shard_map.105), channel_id=1, source_target_pairs={{0,4},{2,6},{4,0},{6,2},{8,12},{10,14},{12,8},{14,10},{16,20},{18,... | collective-permute-start | bytes 786440 | tf_op jit(solution)/shard_map/ppermute | solution.py:280
  60.4 6.7 %collective-permute-start.14 = (bf16[64,768]{1,0:T(8,128)(2,1)S(1)}, bf16[64,768]{1,0:T(8,128)(2,1)S(1)}, u32[]{:S(2)}, u32[]{:S(2)}) collective-permute-start(bf16[64,768]{1,0:T(8,128)(2,1)S(1)} %shard_map.102.refs_1_.a_ref), channel_id=1, source_target_pairs={{0,16},{2,18},{4,20},{6,22},{8,24},{10,26},{12,28},{14,30},{16,0},... | collective-permute-start | bytes 294920 | tf_op jit(solution)/shard_map/ppermute | solution.py:280
  61.4 6.4 %copy-start.12 = (bf16[64,1024]{1,0:T(8,128)(2,1)S(1)}, bf16[64,1024]{1,0:T(8,128)(2,1)}, u32[]{:S(2)}) copy-start(bf16[64,1024]{1,0:T(8,128)(2,1)} %copy-done.11) | copy-start | bytes 393220
  63.7 9.7 %collective-permute-start.17 = (bf16[128,1024]{1,0:T(8,128)(2,1)S(1)}, bf16[128,1024]{1,0:T(8,128)(2,1)S(1)}, u32[]{:S(2)}, u32[]{:S(2)}) collective-permute-start(bf16[128,1024]{1,0:T(8,128)(2,1)S(1)} %get-tuple-element.129.refs_0_), channel_id=1, source_target_pairs={{0,2},{2,0},{4,6},{6,4},{8,10},{10,8},{12,14},{14,12},{16,18},{18,... | collective-permute-start | bytes 786440 | tf_op jit(solution)/shard_map/ppermute | solution.py:280
  67.1 4.8 %collective-permute-start.21 = (bf16[64,768]{1,0:T(8,128)(2,1)S(1)}, bf16[64,768]{1,0:T(8,128)(2,1)S(1)}, u32[]{:S(2)}, u32[]{:S(2)}) collective-permute-start(bf16[64,768]{1,0:T(8,128)(2,1)S(1)} %shard_map.104.refs_1_.a_ref), channel_id=1, source_target_pairs={{0,8},{2,10},{4,12},{6,14},{8,0},{10,2},{12,4},{14,6},{16,24},{18,... | collective-permute-start | bytes 294920 | tf_op jit(solution)/shard_map/ppermute | solution.py:280
  67.8 1.7 %copy-start.6 = (bf16[1024,1024]{1,0:T(8,128)(2,1)S(1)}, bf16[1024,1024]{1,0:T(8,128)(2,1)}, u32[]{:S(2)}) copy-start(bf16[1024,1024]{1,0:T(8,128)(2,1)} %copy-done.5) | copy-start | bytes 6291460
  71.8 5.3 %collective-permute-start.23 = (bf16[64,768]{1,0:T(8,128)(2,1)S(1)}, bf16[64,768]{1,0:T(8,128)(2,1)S(1)}, u32[]{:S(2)}, u32[]{:S(2)}) collective-permute-start(bf16[64,768]{1,0:T(8,128)(2,1)S(1)} %shard_map.110.refs_0_), channel_id=1, source_target_pairs={{0,4},{2,6},{4,0},{6,2},{8,12},{10,14},{12,8},{14,10},{16,20},{18,... | collective-permute-start | bytes 294920 | tf_op jit(solution)/shard_map/ppermute | solution.py:280
  73.5 9.9 %collective-permute-start.18 = (bf16[192,256]{1,0:T(8,128)(2,1)S(1)}, bf16[192,256]{1,0:T(8,128)(2,1)S(1)}, u32[]{:S(2)}, u32[]{:S(2)}) collective-permute-start(bf16[192,256]{1,0:T(8,128)(2,1)S(1)} %get-tuple-element.133), channel_id=1, source_target_pairs={{0,16},{2,18},{4,20},{6,22},{8,24},{10,26},{12,28},{14,30},{16,0},... | collective-permute-start | bytes 294920 | tf_op jit(solution)/shard_map/ppermute | solution.py:280
  75.8 7.6 %collective-permute-start.19 = (bf16[192,256]{1,0:T(8,128)(2,1)S(1)}, bf16[192,256]{1,0:T(8,128)(2,1)S(1)}, u32[]{:S(2)}, u32[]{:S(2)}) collective-permute-start(bf16[192,256]{1,0:T(8,128)(2,1)S(1)} %get-tuple-element.134), channel_id=1, source_target_pairs={{0,24},{2,26},{4,28},{6,30},{8,16},{10,18},{12,20},{14,22},{16,8},... | collective-permute-start | bytes 294920 | tf_op jit(solution)/shard_map/ppermute | solution.py:280
  77.2 6.6 %collective-permute-start.20 = (bf16[192,256]{1,0:T(8,128)(2,1)S(1)}, bf16[192,256]{1,0:T(8,128)(2,1)S(1)}, u32[]{:S(2)}, u32[]{:S(2)}) collective-permute-start(bf16[192,256]{1,0:T(8,128)(2,1)S(1)} %get-tuple-element.135), channel_id=1, source_target_pairs={{0,8},{2,10},{4,12},{6,14},{8,0},{10,2},{12,4},{14,6},{16,24},{18,... | collective-permute-start | bytes 294920 | tf_op jit(solution)/shard_map/ppermute | solution.py:280
  77.2 8.0 %collective-permute-start.22 = (bf16[64,768]{1,0:T(8,128)(2,1)S(1)}, bf16[64,768]{1,0:T(8,128)(2,1)S(1)}, u32[]{:S(2)}, u32[]{:S(2)}) collective-permute-start(bf16[64,768]{1,0:T(8,128)(2,1)S(1)} %shard_map.110.refs_0_), channel_id=1, source_target_pairs={{0,2},{2,0},{4,6},{6,4},{8,10},{10,8},{12,14},{14,12},{16,18},{18,... | collective-permute-start | bytes 294920 | tf_op jit(solution)/shard_map/ppermute | solution.py:280
  77.2 8.0 %collective-permute-start.24 = (bf16[64,768]{1,0:T(8,128)(2,1)S(1)}, bf16[64,768]{1,0:T(8,128)(2,1)S(1)}, u32[]{:S(2)}, u32[]{:S(2)}) collective-permute-start(bf16[64,768]{1,0:T(8,128)(2,1)S(1)} %collective-permute-done.23.refs_2_), channel_id=1, source_target_pairs={{0,2},{2,0},{4,6},{6,4},{8,10},{10,8},{12,14},{14,12},{16,18},{18,... | collective-permute-start | bytes 294920 | tf_op jit(solution)/shard_map/ppermute | solution.py:280
Sparse Core Ops, SparseCore 0:
  63.9 25.3 all-reduce.1

commit v10 on v9

--- a/solution.py
+++ b/solution.py
@@ -56,13 +56,11 @@
     outs, (held,) = refs[:heads], refs[heads:]
     live = live_column(fill_ref, rows)
     lane = lax.broadcasted_iota(jnp.int32, (rows, 2 * dim), 1)
-    mark = jnp.where(lane == 0, DEAD * (1.0 - live), 0.0).astype(BF16)
-    live = live.astype(BF16)
-    for head in range(heads):
-        held[head] = kv_ref[:, head, :] * live + mark
+    mark = jnp.where(lane == 0, DEAD * (1.0 - live), 0.0)
+    held[...] = kv_ref[...].astype(F32)
     me = a_of()
     for slot, mask in enumerate(spread(heads)):
-        outs[slot][...] = held[me ^ mask]
+        outs[slot][...] = (held[pl.ds(me ^ mask, rows, stride=heads), :] * live + mark).astype(BF16)
 
 
 def pack_qg_kernel(heads, rows, dim, a_of, fill_ref, q_ref, w_ref, go_ref, *refs):
@@ -102,7 +100,8 @@
         norm_ref[:, here] = jnp.sum(scaled * scaled, axis=0, keepdims=True)
 
 
-def prep_kernel(dim, pair_ref, wide_ref, kt_ref, vt_ref, norm_ref):
+def prep_kernel(dim, pair_ref, *refs):
+    wide_ref, kt_ref, vt_ref, norm_ref = refs[-4:]
     wide = 2 * dim
     keys = pair_ref.shape[0]
     pair = pair_ref[...]
@@ -245,19 +244,22 @@
         outs[slot][wide:, :] = (dq_ref[:, here] * dim**-0.5).astype(BF16)
 
 
+def add_out_kernel(a_ref, b_ref, out_ref, done_ref):
+    out_ref[...] = (a_ref[...].astype(F32) + b_ref[...].astype(F32)).astype(out_ref.dtype)
+    done_ref[...] = jnp.zeros_like(done_ref)
+
+
 def add_kernel(a_ref, b_ref, *refs):
     refs[-1][...] = (a_ref[...].astype(F32) + b_ref[...].astype(F32)).astype(refs[-1].dtype)
 
 
 def unpack_kernel(slots, rows, dim, a_of, *refs):
-    pieces, (kv_out, q_out, held) = refs[:slots], refs[slots:]
+    pieces, (kv_out, q_out) = refs[:slots], refs[-2:]
     wide = 2 * dim
     me = a_of()
     for slot, mask in enumerate(spread(slots)):
-        held[me ^ mask] = pieces[slot][0:wide, :].astype(F32).T
+        kv_out[pl.ds(me ^ mask, rows, stride=slots), :] = pieces[slot][0:wide, :].astype(F32).T
         q_out[me ^ mask] = pieces[slot][wide:, :].astype(F32)
-    for head in range(slots):
-        kv_out[:, head, :] = held[head]
 
 
 def place_kernel(columns, b_of, *refs):
@@ -285,9 +287,9 @@
     block, wide = slots * rows, 2 * dim
     kv_mine = exchange(call(
         functools.partial(pack_kv_kernel, heads, rows, dim, a_of),
-        [((rows, wide), BF16)] * slots, [pltpu.VMEM((heads, rows, wide), BF16)],
+        [((rows, wide), BF16)] * slots, [pltpu.VMEM((rows * heads, wide), F32)],
         n_in=2, smem_first=True, micros=1.5, limit=56,
-    )(tile_fill, key_value))
+    )(tile_fill, key_value.reshape(rows * heads, wide)))
     qg_send = call(
         functools.partial(pack_qg_kernel, heads, rows, dim, a_of),
         [((wide, rows), BF16)] * slots, [pltpu.VMEM((heads, wide, rows), BF16)],
@@ -314,8 +316,9 @@
     for r in range(columns):
         *prepared[r], values, norm = call(
             functools.partial(prep_kernel, dim),
-            [((block, 2 * wide), BF16), ((dim, block), BF16), ((dim + 16, block), BF16), ((1, block), F32)], micros=2,
-        )(blocks[r])
+            [((block, 2 * wide), BF16), ((dim, block), BF16), ((dim + 16, block), BF16), ((1, block), F32)],
+            after=min(r, 1), micros=2,
+        )(blocks[r], *([scored[r - 1][1]] if r else []))
         scored[r] = call(
             functools.partial(score_kernel, slots, rows, dim, step),
             [((block, block), BF16), ((1, block), F32), ((dim + 16, block), F32)],
@@ -345,17 +348,22 @@
                 functools.partial(project_kernel, slots, rows, a_of), [((rows, width), BF16)],
                 n_in=2 + slots, smem_first=True, after=1, micros=0.7,
             )(tile_fill, out_weight, *att_mine, weight_terms[-1])[0]
-            later = [terms]
+            later, bit, done = [terms], 1, terms
+            first_terms = terms
+            while bit < mp:
+                terms, done = call(add_out_kernel, [((rows, width), BF16), ((8, 128), F32)], n_in=2)(
+                    terms, swap(terms, bit, "mp", mp))
+                bit *= 2
             if halves:
                 kept, sent = call(add_pairs_kernel, [((dim, width), BF16)] * 2, n_in=2, after=1)(
-                    weight_terms[0], swap(weight_terms[1], 1), terms)
+                    weight_terms[0], swap(weight_terms[1], 1), first_terms)
                 later = [kept]
         if at == 2 and halves:
             kept = add(kept, swap(sent, 2), dkv[order[at - 1]])[0]
             later = [kept]
         if at == 3 and halves:
             kept = add(kept, swap(kept, far_masks[0]), dkv[order[at - 1]])[0]
-            later = [kept, summed[2]]
+            later = [kept, summed[2], done]
         operands = [scored[r][0], *prepared[r], q_all, grads, factors[r], inner] + ([] if dq is None else [dq])
         dkv[r], dq = call(
             functools.partial(back_kernel, slots, rows, dim, dq is None),
@@ -365,8 +373,6 @@
         later = []
         if columns == 4 and r == 2:
             summed[2] = swap(add_halves(dkv[2], swap(dkv[3], 1))[0], 2)
-
-    attention_out = lax.psum(terms, "mp") if mp > 1 else terms
 
     if columns == 4:
         halved = add_halves(dkv[0], swap(dkv[1], 1))[0], summed[2]
@@ -383,7 +389,7 @@
 
     if halves:
         for mask in far_masks[1:]:
-            kept = add(kept, swap(kept, mask), dkv[0])[0]
+            kept = add(kept, swap(kept, mask), pieces[0])[0]
         across = swap(kept, 2)
         weight_grad = call(
             functools.partial(place_kernel, columns, b_of), [((heads, dim, width), F32)], n_in=columns, micros=0.5,
@@ -393,10 +399,10 @@
 
     key_value_grad, query_grad = call(
         functools.partial(unpack_kernel, slots, rows, dim, a_of),
-        [((rows, heads, wide), F32), ((heads, dim, rows), F32)],
-        [pltpu.VMEM((heads, rows, wide), F32)], n_in=slots, micros=1,
+        [((rows * heads, wide), F32), ((heads, dim, rows), F32)],
+        n_in=slots, micros=1,
     )(*returned)
-    return attention_out, jnp.transpose(query_grad, (2, 0, 1)), key_value_grad, weight_grad
+    return terms, jnp.transpose(query_grad, (2, 0, 1)), key_value_grad.reshape(rows, heads, wide), weight_grad
 
 
 def solution(mesh):

time: 98.2 us -> 71 us (0.72)
  between operations: 14.4 us -> 0.96 us
  local copies, waits for them, and re-layouts: 9.17 us -> 0.02 us
  waiting for transfers between devices: 19.3 us -> 14.4 us
  starting transfers between devices: 25 us -> 26.2 us
    unnamed x35 -> x10, local copies, waits for them, and re-layouts: 9.17 us -> 0.02 us
    psum x1 -> x0, waiting for transfers between devices: 3.27 us -> none  [shards(): attention_out = lax.psum(terms, 'mp') if mp > 1 else terms]
    ppermute x25 -> x26, waiting for transfers between devices: 16 us -> 14.4 us  [swap(): return lax.ppermute(array, axis, [(i, i ^ mask) for i in range(size)])]
    ppermute x25 -> x26, starting transfers between devices: 24.8 us -> 26.2 us  [swap(): return lax.ppermute(array, axis, [(i, i ^ mask) for i in range(size)])]
  transfers between devices with their start and end apart: 26 -> 26, of which waited for: 10 -> 12; matrix products, arithmetic and copies ran while one was open for 0% -> 0% of each run, Pallas kernels for 24% -> 31%
where the time goes in v10:
time: 71 us; the launch traced here: 70.8 us
  Pallas kernels  29.2 us (41%)
  starting transfers between devices  26.2 us (37%)
  waiting for transfers between devices  14.4 us (20%)
  between operations  0.96 us (1%)
    ppermute x26, starting transfers between devices, swap(): return lax.ppermute(array, axis, [(i, i ^ mask) for i in range(size)])  26.2 us
    ppermute x26, waiting for transfers between devices, swap(): return lax.ppermute(array, axis, [(i, i ^ mask) for i in range(size)])  14.4 us
    pallas_call x4, Pallas kernels, shards(): call(functools.partial(score_kernel, slots, rows, dim, step), [((block, b...  10.9 us
    pallas_call x4, Pallas kernels, shards(): call(functools.partial(back_kernel, slots, rows, dim, dq is None), [((wid...  9.06 us
    pallas_call x1, Pallas kernels, shards(): call(functools.partial(pack_kv_kernel, heads, rows, dim, a_of), [((rows,...  1.9 us
  transfers between devices with their start and end apart: 26, of which 12 were waited for; matrix products, arithmetic and copies ran while one was open for 0% of the time, Pallas kernels for 31%

profile of v10, /device:TPU:0, one launch (start us, length us, event | category | flops | bytes accessed | tf_op | source)
XLA Modules:
  0.0 70.8 jit_solution(17097710210872192028)
XLA Ops:
  0.7 1.9 %shard_map.84 = (bf16[256,128]{1,0:T(8,128)(2,1)}, bf16[256,128]{1,0:T(8,128)(2,1)}, bf16[256,128]{1,0:T(8,128)(2,1)}, bf16[256,128]{1,0:T(8,128)(2,1)}) custom-call(s32[2]{0:T(128)} %fill_ref.7, bf16[1024,128]{1,0:T(8,128)(2,1)} %bitcast.5), custom_call_target="tpu_custom_call" | custom-call | flops 1724999936 | tf_op jit(solution)/shard_map/pallas_call | solution.py:288
  2.6 4.0 %collective-permute-start = (bf16[256,128]{1,0:T(8,128)(2,1)}, bf16[256,128]{1,0:T(8,128)(2,1)S(1)}, u32[]{:S(2)}, u32[]{:S(2)}) collective-permute-start(bf16[256,128]{1,0:T(8,128)(2,1)} %get-tuple-element.74), channel_id=1, source_target_pairs={{0,16},{2,18},{4,20},{6,22},{8,24},{10,26},{12,28},{14,30},{16,0},... | collective-permute-start | bytes 196616 | tf_op jit(solution)/shard_map/ppermute | solution.py:282
  6.6 1.3 %collective-permute-start.1 = (bf16[256,128]{1,0:T(8,128)(2,1)}, bf16[256,128]{1,0:T(8,128)(2,1)S(1)}, u32[]{:S(2)}, u32[]{:S(2)}) collective-permute-start(bf16[256,128]{1,0:T(8,128)(2,1)} %get-tuple-element.75), channel_id=1, source_target_pairs={{0,24},{2,26},{4,28},{6,30},{8,16},{10,18},{12,20},{14,22},{16,8},... | collective-permute-start | bytes 196616 | tf_op jit(solution)/shard_map/ppermute | solution.py:282
  8.0 0.2 collective-permute-start.2
  8.2 0.0 copy-start
  8.2 0.9 %shard_map.85 = (bf16[128,256]{1,0:T(8,128)(2,1)S(1)}, bf16[128,256]{1,0:T(8,128)(2,1)S(1)}, bf16[128,256]{1,0:T(8,128)(2,1)S(1)}, bf16[128,256]{1,0:T(8,128)(2,1)S(1)}) custom-call(s32[2]{0:T(128)S(1)} %copy-done.4, bf16[4,64,256]{2,1,0:T(8,128)(2,1)S(1)} %bitcast.4, bf16[4,64,768]{2,1,0:T(8,128)(2,1)S(1)} %copy-done.2, bf16[256,768]{1,0:T(8,128)(2,1)S(1)} %copy-done.1), custom_call_target="tpu_custom_call" | custom-call | flops 1150000000 | tf_op jit(solution)/shard_map/pallas_call | solution.py:293
  9.2 2.9 %collective-permute-start.3 = (bf16[128,256]{1,0:T(8,128)(2,1)S(1)}, bf16[128,256]{1,0:T(8,128)(2,1)S(1)}, u32[]{:S(2)}, u32[]{:S(2)}) collective-permute-start(bf16[128,256]{1,0:T(8,128)(2,1)S(1)} %get-tuple-element.81), channel_id=1, source_target_pairs={{0,16},{2,18},{4,20},{6,22},{8,24},{10,26},{12,28},{14,30},{16,0},... | collective-permute-start | bytes 196616 | tf_op jit(solution)/shard_map/ppermute | solution.py:282
  12.0 1.3 %collective-permute-start.4 = (bf16[128,256]{1,0:T(8,128)(2,1)S(1)}, bf16[128,256]{1,0:T(8,128)(2,1)S(1)}, u32[]{:S(2)}, u32[]{:S(2)}) collective-permute-start(bf16[128,256]{1,0:T(8,128)(2,1)S(1)} %get-tuple-element.82), channel_id=1, source_target_pairs={{0,24},{2,26},{4,28},{6,30},{8,16},{10,18},{12,20},{14,22},{16,8},... | collective-permute-start | bytes 196616 | tf_op jit(solution)/shard_map/ppermute | solution.py:282
  13.4 0.0 collective-permute-done.2.refs_3_
  13.4 1.6 %collective-permute-start.7 = (bf16[1024,128]{1,0:T(8,128)(2,1)S(1)}, bf16[1024,128]{1,0:T(8,128)(2,1)S(1)}, u32[]{:S(2)}, u32[]{:S(2)}) collective-permute-start(bf16[1024,128]{1,0:T(8,128)(2,1)S(1)} %shard_map.86.pair_ref), channel_id=1, source_target_pairs={{0,4},{2,6},{4,0},{6,2},{8,12},{10,14},{12,8},{14,10},{16,20},{18,... | collective-permute-start | bytes 786440 | tf_op jit(solution)/shard_map/ppermute | solution.py:282
  15.0 0.0 collective-permute-start.6
  15.0 0.3 shard_map.87
  15.4 1.8 %collective-permute-done.3.refs_1_ = bf16[128,256]{1,0:T(8,128)(2,1)S(1)} collective-permute-done((bf16[128,256]{1,0:T(8,128)(2,1)S(1)}, bf16[128,256]{1,0:T(8,128)(2,1)S(1)}, u32[]{:S(2)}, u32[]{:S(2)}) %collective-permute-start.3) | collective-permute-done | bytes 65568 | tf_op jit(solution)/shard_map/ppermute | solution.py:282
  17.2 1.1 %collective-permute-done.4.refs_2_ = bf16[128,256]{1,0:T(8,128)(2,1)S(1)} collective-permute-done((bf16[128,256]{1,0:T(8,128)(2,1)S(1)}, bf16[128,256]{1,0:T(8,128)(2,1)S(1)}, u32[]{:S(2)}, u32[]{:S(2)}) %collective-permute-start.4) | collective-permute-done | bytes 65568 | tf_op jit(solution)/shard_map/ppermute | solution.py:282
  18.3 0.2 collective-permute-done.5.refs_3_
  18.5 0.1 shard_map.88
  18.6 2.7 %shard_map.89 = (bf16[1024,1024]{1,0:T(8,128)(2,1)S(1)}, f32[1,1024]{1,0:T(1,128)S(1)}, f32[80,1024]{1,0:T(8,128)S(1)}) custom-call(bf16[1024,256]{1,0:T(8,128)(2,1)S(1)} %get-tuple-element.78.wide_ref, bf16[80,1024]{1,0:T(8,128)(2,1)S(1)} %get-tuple-element.79.vt_ref, f32[1,1024]{1,0:T(1,128)S(1)} %get-tuple-element.80.norm_ref, ...), custom_call_target="tpu_custom_call" | custom-call | flops 4600000000 | tf_op jit(solution)/shard_map/pallas_call | solution.py:322
  21.3 0.0 collective-permute-done.6.pair_ref
  21.3 0.3 shard_map.90
  21.6 2.7 %shard_map.91 = (bf16[1024,1024]{1,0:T(8,128)(2,1)S(1)}, f32[1,1024]{1,0:T(1,128)S(1)}, f32[80,1024]{1,0:T(8,128)S(1)}) custom-call(bf16[1024,256]{1,0:T(8,128)(2,1)S(1)} %get-tuple-element.87.wide_ref, bf16[80,1024]{1,0:T(8,128)(2,1)S(1)} %get-tuple-element.88.vt_ref, f32[1,1024]{1,0:T(1,128)S(1)} %get-tuple-element.89.norm_ref, ...), custom_call_target="tpu_custom_call" | custom-call | flops 4600000000 | tf_op jit(solution)/shard_map/pallas_call | solution.py:322
  24.3 0.0 collective-permute-done.7.pair_ref
  24.3 0.1 collective-permute-start.8
  24.4 0.3 shard_map.92
  24.7 2.7 %shard_map.93 = (bf16[1024,1024]{1,0:T(8,128)(2,1)S(1)}, f32[1,1024]{1,0:T(1,128)S(1)}, f32[80,1024]{1,0:T(8,128)S(1)}) custom-call(bf16[1024,256]{1,0:T(8,128)(2,1)S(1)} %get-tuple-element.91.wide_ref, bf16[80,1024]{1,0:T(8,128)(2,1)S(1)} %get-tuple-element.92.vt_ref, f32[1,1024]{1,0:T(1,128)S(1)} %get-tuple-element.93.norm_ref, ...), custom_call_target="tpu_custom_call" | custom-call | flops 4600000000 | tf_op jit(solution)/shard_map/pallas_call | solution.py:322
  27.4 0.3 shard_map.94
  27.7 2.9 %shard_map.95 = (bf16[1024,1024]{1,0:T(8,128)(2,1)S(1)}, f32[1,1024]{1,0:T(1,128)S(1)}, f32[80,1024]{1,0:T(8,128)S(1)}) custom-call(bf16[1024,256]{1,0:T(8,128)(2,1)S(1)} %get-tuple-element.95.wide_ref, bf16[80,1024]{1,0:T(8,128)(2,1)S(1)} %get-tuple-element.96.vt_ref, f32[1,1024]{1,0:T(1,128)S(1)} %get-tuple-element.97.norm_ref, ...), custom_call_target="tpu_custom_call" | custom-call | flops 4600000000 | tf_op jit(solution)/shard_map/pallas_call | solution.py:322
  30.6 0.2 shard_map.96
  30.8 3.1 %collective-permute-start.9 = (bf16[64,256]{1,0:T(8,128)(2,1)S(1)}, bf16[64,256]{1,0:T(8,128)(2,1)S(1)}, u32[]{:S(2)}, u32[]{:S(2)}) collective-permute-start(bf16[64,256]{1,0:T(8,128)(2,1)S(1)} %get-tuple-element.105), channel_id=1, source_target_pairs={{0,16},{2,18},{4,20},{6,22},{8,24},{10,26},{12,28},{14,30},{16,0},... | collective-permute-start | bytes 98312 | tf_op jit(solution)/shard_map/ppermute | solution.py:282
  33.8 0.4 collective-permute-start.10
  34.2 0.2 collective-permute-start.11
  34.5 2.3 %shard_map.97 = (bf16[128,1024]{1,0:T(8,128)(2,1)S(1)}, f32[64,1024]{1,0:T(8,128)S(1)}) custom-call(bf16[1024,1024]{1,0:T(8,128)(2,1)S(1)} %get-tuple-element.108.exp_ref, bf16[1024,256]{1,0:T(8,128)(2,1)S(1)} %get-tuple-element.95.wide_ref, bf16[64,1024]{1,0:T(8,128)(2,1)S(1)} %get-tuple-element.109.kt_ref, bf16[64,1024]{1,0:T(8,128)(2,1)S(1)} %get-tuple-element.110.q_ref, ...), custom_call_target="tpu_custom_call" | custom-call | flops 2300000000 | tf_op jit(solution)/shard_map/pallas_call | solution.py:368
  36.8 0.0 collective-permute-done.9.refs_1_
  36.8 2.8 %collective-permute-done.10.refs_2_ = bf16[64,256]{1,0:T(8,128)(2,1)S(1)} collective-permute-done((bf16[64,256]{1,0:T(8,128)(2,1)S(1)}, bf16[64,256]{1,0:T(8,128)(2,1)S(1)}, u32[]{:S(2)}, u32[]{:S(2)}) %collective-permute-start.10) | collective-permute-done | bytes 32800 | tf_op jit(solution)/shard_map/ppermute | solution.py:282
  39.6 0.9 %shard_map.98 = (bf16[2,64,768]{2,1,0:T(8,128)(2,1)S(1)}, bf16[2,64,768]{2,1,0:T(8,128)(2,1)S(1)}) custom-call(s32[2]{0:T(128)S(1)} %copy-done.4, bf16[256,768]{1,0:T(8,128)(2,1)S(1)} %copy-done.1, bf16[64,256]{1,0:T(8,128)(2,1)S(1)} %get-tuple-element.104.refs_0_, bf16[64,256]{1,0:T(8,128)(2,1)S(1)} %collective-permute-done.9.refs_1_, ...), custom_call_target="tpu_custom_call" | custom-call | flops 805000000 | tf_op jit(solution)/shard_map/pallas_call | solution.py:341
  40.5 0.1 collective-permute-start.13
  40.6 0.5 collective-permute-start.16
  41.1 0.8 %shard_map.99.a_ref._ = bf16[256,768]{1,0:T(8,128)(2,1)S(1)} custom-call(s32[2]{0:T(128)S(1)} %copy-done.4, bf16[4,64,768]{2,1,0:T(8,128)(2,1)S(1)} %copy-done.2, bf16[64,256]{1,0:T(8,128)(2,1)S(1)} %get-tuple-element.104.refs_0_, bf16[64,256]{1,0:T(8,128)(2,1)S(1)} %collective-permute-done.9.refs_1_, bf16[64,256]{1,0:T(8,128)(2,1)S(1)} %collective-permute-done.10.refs_2_, ...), custom_call_target="tpu_custom_call" | custom-call | flops 805000000 | tf_op jit(solution)/shard_map/pallas_call | solution.py:347
  41.9 1.5 %collective-permute-start.12 = (bf16[256,768]{1,0:T(8,128)(2,1)S(1)}, bf16[256,768]{1,0:T(8,128)(2,1)S(1)}, u32[]{:S(2)}, u32[]{:S(2)}) collective-permute-start(bf16[256,768]{1,0:T(8,128)(2,1)S(1)} %shard_map.99.a_ref._), channel_id=1, source_target_pairs={{0,1},{1,0},{2,3},{3,2},{4,5},{5,4},{6,7},{7,6},{8,9},{9,8},{10,11... | collective-permute-start | bytes 1179656 | tf_op jit(solution)/shard_map/ppermute | solution.py:282
  43.5 1.5 %collective-permute-start.14 = (bf16[64,768]{1,0:T(8,128)(2,1)S(1)}, bf16[64,768]{1,0:T(8,128)(2,1)S(1)}, u32[]{:S(2)}, u32[]{:S(2)}) collective-permute-start(bf16[64,768]{1,0:T(8,128)(2,1)S(1)} %get-tuple-element.129), channel_id=1, source_target_pairs={{0,4},{2,6},{4,0},{6,2},{8,12},{10,14},{12,8},{14,10},{16,20},{18,... | collective-permute-start | bytes 294920 | tf_op jit(solution)/shard_map/ppermute | solution.py:282
  45.1 2.3 %shard_map.102 = (bf16[128,1024]{1,0:T(8,128)(2,1)S(1)}, f32[64,1024]{1,0:T(8,128)S(1)}) custom-call(bf16[1024,1024]{1,0:T(8,128)(2,1)S(1)} %get-tuple-element.122.exp_ref, bf16[1024,256]{1,0:T(8,128)(2,1)S(1)} %get-tuple-element.91.wide_ref, bf16[64,1024]{1,0:T(8,128)(2,1)S(1)} %get-tuple-element.123.kt_ref, bf16[64,1024]{1,0:T(8,128)(2,1)S(1)} %get-tuple-element.110.q_ref, ...), custom_call_target="tpu_custom_call" | custom-call | flops 2300000000 | tf_op jit(solution)/shard_map/pallas_call | solution.py:368
  47.3 0.1 shard_map.106
  47.4 0.6 collective-permute-start.17
  48.0 0.2 collective-permute-done.14.b_ref
  48.2 1.0 %collective-permute-start.15 = (bf16[64,768]{1,0:T(8,128)(2,1)S(1)}, bf16[64,768]{1,0:T(8,128)(2,1)S(1)}, u32[]{:S(2)}, u32[]{:S(2)}) collective-permute-start(bf16[64,768]{1,0:T(8,128)(2,1)S(1)} %shard_map.103.refs_1_.a_ref), channel_id=1, source_target_pairs={{0,16},{2,18},{4,20},{6,22},{8,24},{10,26},{12,28},{14,30},{16,0},... | collective-permute-start | bytes 294920 | tf_op jit(solution)/shard_map/ppermute | solution.py:282
  49.3 2.3 %shard_map.104 = (bf16[128,1024]{1,0:T(8,128)(2,1)S(1)}, f32[64,1024]{1,0:T(8,128)S(1)}) custom-call(bf16[1024,1024]{1,0:T(8,128)(2,1)S(1)} %get-tuple-element.119.exp_ref, bf16[1024,256]{1,0:T(8,128)(2,1)S(1)} %get-tuple-element.87.wide_ref, bf16[64,1024]{1,0:T(8,128)(2,1)S(1)} %get-tuple-element.120.kt_ref, bf16[64,1024]{1,0:T(8,128)(2,1)S(1)} %get-tuple-element.110.q_ref, ...), custom_call_target="tpu_custom_call" | custom-call | flops 2300000000 | tf_op jit(solution)/shard_map/pallas_call | solution.py:368
  51.5 0.1 collective-permute-start.18
  51.6 1.5 %collective-permute-done.12.b_ref = bf16[256,768]{1,0:T(8,128)(2,1)S(1)} collective-permute-done((bf16[256,768]{1,0:T(8,128)(2,1)S(1)}, bf16[256,768]{1,0:T(8,128)(2,1)S(1)}, u32[]{:S(2)}, u32[]{:S(2)}) %collective-permute-start.12) | collective-permute-done | bytes 393248 | tf_op jit(solution)/shard_map/ppermute | solution.py:282
  53.1 0.8 %shard_map.100 = (bf16[256,768]{1,0:T(8,128)(2,1)}, f32[8,128]{1,0:T(8,128)S(1)}) custom-call(bf16[256,768]{1,0:T(8,128)(2,1)S(1)} %shard_map.99.a_ref._, bf16[256,768]{1,0:T(8,128)(2,1)S(1)} %collective-permute-done.12.b_ref), custom_call_target="tpu_custom_call" | custom-call | flops 11500000 | tf_op jit(solution)/shard_map/pallas_call | solution.py:354
  53.9 0.5 collective-permute-done.15.b_ref
  54.5 0.1 collective-permute-start.22
  54.6 0.6 collective-permute-done.17.refs_2_.came_ref
  55.2 2.3 %shard_map.107 = (bf16[128,1024]{1,0:T(8,128)(2,1)S(1)}, f32[64,1024]{1,0:T(8,128)S(1)}) custom-call(bf16[1024,1024]{1,0:T(8,128)(2,1)S(1)} %get-tuple-element.116.exp_ref, bf16[1024,256]{1,0:T(8,128)(2,1)S(1)} %get-tuple-element.78.wide_ref, bf16[64,1024]{1,0:T(8,128)(2,1)S(1)} %get-tuple-element.117.kt_ref, bf16[64,1024]{1,0:T(8,128)(2,1)S(1)} %get-tuple-element.110.q_ref, ...), custom_call_target="tpu_custom_call" | custom-call | flops 2300000000 | tf_op jit(solution)/shard_map/pallas_call | solution.py:368
  57.5 0.0 collective-permute-done.18.b_ref
  57.5 0.1 shard_map.108.kept_ref
  57.6 0.1 shard_map.109
  57.7 2.5 %collective-permute-start.19 = (bf16[192,256]{1,0:T(8,128)(2,1)S(1)}, bf16[192,256]{1,0:T(8,128)(2,1)S(1)}, u32[]{:S(2)}, u32[]{:S(2)}) collective-permute-start(bf16[192,256]{1,0:T(8,128)(2,1)S(1)} %get-tuple-element.137), channel_id=1, source_target_pairs={{0,16},{2,18},{4,20},{6,22},{8,24},{10,26},{12,28},{14,30},{16,0},... | collective-permute-start | bytes 294920 | tf_op jit(solution)/shard_map/ppermute | solution.py:282
  60.1 1.5 %collective-permute-start.24 = (bf16[64,768]{1,0:T(8,128)(2,1)S(1)}, bf16[64,768]{1,0:T(8,128)(2,1)S(1)}, u32[]{:S(2)}, u32[]{:S(2)}) collective-permute-start(bf16[64,768]{1,0:T(8,128)(2,1)S(1)} %shard_map.111.refs_0_), channel_id=1, source_target_pairs={{0,4},{2,6},{4,0},{6,2},{8,12},{10,14},{12,8},{14,10},{16,20},{18,... | collective-permute-start | bytes 294920 | tf_op jit(solution)/shard_map/ppermute | solution.py:282
  61.7 1.5 %collective-permute-start.20 = (bf16[192,256]{1,0:T(8,128)(2,1)S(1)}, bf16[192,256]{1,0:T(8,128)(2,1)S(1)}, u32[]{:S(2)}, u32[]{:S(2)}) collective-permute-start(bf16[192,256]{1,0:T(8,128)(2,1)S(1)} %get-tuple-element.138), channel_id=1, source_target_pairs={{0,24},{2,26},{4,28},{6,30},{8,16},{10,18},{12,20},{14,22},{16,8},... | collective-permute-start | bytes 294920 | tf_op jit(solution)/shard_map/ppermute | solution.py:282
  63.2 1.6 %collective-permute-done.24.refs_2_ = bf16[64,768]{1,0:T(8,128)(2,1)S(1)} collective-permute-done((bf16[64,768]{1,0:T(8,128)(2,1)S(1)}, bf16[64,768]{1,0:T(8,128)(2,1)S(1)}, u32[]{:S(2)}, u32[]{:S(2)}) %collective-permute-start.24) | collective-permute-done | bytes 98336 | tf_op jit(solution)/shard_map/ppermute | solution.py:282
  64.8 1.8 %collective-permute-done.19.refs_1_ = bf16[192,256]{1,0:T(8,128)(2,1)S(1)} collective-permute-done((bf16[192,256]{1,0:T(8,128)(2,1)S(1)}, bf16[192,256]{1,0:T(8,128)(2,1)S(1)}, u32[]{:S(2)}, u32[]{:S(2)}) %collective-permute-start.19) | collective-permute-done | bytes 98336 | tf_op jit(solution)/shard_map/ppermute | solution.py:282
  66.6 1.7 %collective-permute-done.20.refs_2_ = bf16[192,256]{1,0:T(8,128)(2,1)S(1)} collective-permute-done((bf16[192,256]{1,0:T(8,128)(2,1)S(1)}, bf16[192,256]{1,0:T(8,128)(2,1)S(1)}, u32[]{:S(2)}, u32[]{:S(2)}) %collective-permute-start.20) | collective-permute-done | bytes 98336 | tf_op jit(solution)/shard_map/ppermute | solution.py:282
  68.3 0.6 collective-permute-done.21.refs_3_
  68.9 1.0 %shard_map.110 = (f32[1024,128]{1,0:T(8,128)}, f32[4,64,256]{2,1,0:T(8,128)}) custom-call(bf16[192,256]{1,0:T(8,128)(2,1)S(1)} %get-tuple-element.136.refs_0_, bf16[192,256]{1,0:T(8,128)(2,1)S(1)} %collective-permute-done.19.refs_1_, bf16[192,256]{1,0:T(8,128)(2,1)S(1)} %collective-permute-done.20.refs_2_, bf16[192,256]{1,0:T(8,128)(2,1)S(1)} %collective-permute-done.21.refs_3_), custom_call_target="tpu_custom_call" | custom-call | flops 1150000000 | tf_op jit(solution)/shard_map/pallas_call | solution.py:400
  69.9 0.9 %shard_map.112 = f32[4,64,768]{2,1,0:T(8,128)} custom-call(bf16[64,768]{1,0:T(8,128)(2,1)S(1)} %shard_map.111.refs_0_, bf16[64,768]{1,0:T(8,128)(2,1)S(1)} %collective-permute-done.23.refs_1_, bf16[64,768]{1,0:T(8,128)(2,1)S(1)} %collective-permute-done.24.refs_2_, bf16[64,768]{1,0:T(8,128)(2,1)S(1)} %collective-permute-done.25.refs_3_), custom_call_target="tpu_custom_call" | custom-call | flops 575000000 | tf_op jit(solution)/shard_map/pallas_call | solution.py:394
  (27 shorter events, 0.2 us)
Async XLA Ops:
  0.6 7.6 %copy-start.1 = (bf16[256,768]{1,0:T(8,128)(2,1)S(1)}, bf16[256,768]{1,0:T(8,128)(2,1)}, u32[]{:S(2)}) copy-start(bf16[256,768]{1,0:T(8,128)(2,1)} %go_ref.3) | copy-start | bytes 1179652
  0.6 7.6 %copy-start.2 = (bf16[4,64,768]{2,1,0:T(8,128)(2,1)S(1)}, bf16[4,64,768]{2,1,0:T(8,128)(2,1)}, u32[]{:S(2)}) copy-start(bf16[4,64,768]{2,1,0:T(8,128)(2,1)} %w_ref.3) | copy-start | bytes 1179652
  0.7 7.5 %copy-start.3 = (bf16[256,4,64]{0,2,1:T(8,128)(2,1)S(1)}, bf16[256,4,64]{0,2,1:T(8,128)(2,1)}, u32[]{:S(2)}) copy-start(bf16[256,4,64]{0,2,1:T(8,128)(2,1)} %param.5) | copy-start | bytes 393220
  0.7 7.5 %copy-start.4 = (s32[2]{0:T(128)S(1)}, s32[2]{0:T(128)}, u32[]{:S(2)}) copy-start(s32[2]{0:T(128)} %fill_ref.7) | copy-start | bytes 28
  2.6 10.8 %collective-permute-start = (bf16[256,128]{1,0:T(8,128)(2,1)}, bf16[256,128]{1,0:T(8,128)(2,1)S(1)}, u32[]{:S(2)}, u32[]{:S(2)}) collective-permute-start(bf16[256,128]{1,0:T(8,128)(2,1)} %get-tuple-element.74), channel_id=1, source_target_pairs={{0,16},{2,18},{4,20},{6,22},{8,24},{10,26},{12,28},{14,30},{16,0},... | collective-permute-start | bytes 196616 | tf_op jit(solution)/shard_map/ppermute | solution.py:282
  6.6 6.8 %collective-permute-start.1 = (bf16[256,128]{1,0:T(8,128)(2,1)}, bf16[256,128]{1,0:T(8,128)(2,1)S(1)}, u32[]{:S(2)}, u32[]{:S(2)}) collective-permute-start(bf16[256,128]{1,0:T(8,128)(2,1)} %get-tuple-element.75), channel_id=1, source_target_pairs={{0,24},{2,26},{4,28},{6,30},{8,16},{10,18},{12,20},{14,22},{16,8},... | collective-permute-start | bytes 196616 | tf_op jit(solution)/shard_map/ppermute | solution.py:282
  8.0 5.4 %collective-permute-start.2 = (bf16[256,128]{1,0:T(8,128)(2,1)}, bf16[256,128]{1,0:T(8,128)(2,1)S(1)}, u32[]{:S(2)}, u32[]{:S(2)}) collective-permute-start(bf16[256,128]{1,0:T(8,128)(2,1)} %get-tuple-element.76), channel_id=1, source_target_pairs={{0,8},{2,10},{4,12},{6,14},{8,0},{10,2},{12,4},{14,6},{16,24},{18,... | collective-permute-start | bytes 196616 | tf_op jit(solution)/shard_map/ppermute | solution.py:282
  8.2 5.2 %copy-start = (bf16[256,128]{1,0:T(8,128)(2,1)S(1)}, bf16[256,128]{1,0:T(8,128)(2,1)}, u32[]{:S(2)}) copy-start(bf16[256,128]{1,0:T(8,128)(2,1)} %get-tuple-element.73.refs_0_) | copy-start | bytes 196612
  9.2 8.0 %collective-permute-start.3 = (bf16[128,256]{1,0:T(8,128)(2,1)S(1)}, bf16[128,256]{1,0:T(8,128)(2,1)S(1)}, u32[]{:S(2)}, u32[]{:S(2)}) collective-permute-start(bf16[128,256]{1,0:T(8,128)(2,1)S(1)} %get-tuple-element.81), channel_id=1, source_target_pairs={{0,16},{2,18},{4,20},{6,22},{8,24},{10,26},{12,28},{14,30},{16,0},... | collective-permute-start | bytes 196616 | tf_op jit(solution)/shard_map/ppermute | solution.py:282
  12.0 6.2 %collective-permute-start.4 = (bf16[128,256]{1,0:T(8,128)(2,1)S(1)}, bf16[128,256]{1,0:T(8,128)(2,1)S(1)}, u32[]{:S(2)}, u32[]{:S(2)}) collective-permute-start(bf16[128,256]{1,0:T(8,128)(2,1)S(1)} %get-tuple-element.82), channel_id=1, source_target_pairs={{0,24},{2,26},{4,28},{6,30},{8,16},{10,18},{12,20},{14,22},{16,8},... | collective-permute-start | bytes 196616 | tf_op jit(solution)/shard_map/ppermute | solution.py:282
  13.4 5.1 %collective-permute-start.5 = (bf16[128,256]{1,0:T(8,128)(2,1)S(1)}, bf16[128,256]{1,0:T(8,128)(2,1)S(1)}, u32[]{:S(2)}, u32[]{:S(2)}) collective-permute-start(bf16[128,256]{1,0:T(8,128)(2,1)S(1)} %get-tuple-element.83), channel_id=1, source_target_pairs={{0,8},{2,10},{4,12},{6,14},{8,0},{10,2},{12,4},{14,6},{16,24},{18,... | collective-permute-start | bytes 196616 | tf_op jit(solution)/shard_map/ppermute | solution.py:282
  13.4 10.9 %collective-permute-start.7 = (bf16[1024,128]{1,0:T(8,128)(2,1)S(1)}, bf16[1024,128]{1,0:T(8,128)(2,1)S(1)}, u32[]{:S(2)}, u32[]{:S(2)}) collective-permute-start(bf16[1024,128]{1,0:T(8,128)(2,1)S(1)} %shard_map.86.pair_ref), channel_id=1, source_target_pairs={{0,4},{2,6},{4,0},{6,2},{8,12},{10,14},{12,8},{14,10},{16,20},{18,... | collective-permute-start | bytes 786440 | tf_op jit(solution)/shard_map/ppermute | solution.py:282
  15.0 6.2 %collective-permute-start.6 = (bf16[1024,128]{1,0:T(8,128)(2,1)S(1)}, bf16[1024,128]{1,0:T(8,128)(2,1)S(1)}, u32[]{:S(2)}, u32[]{:S(2)}) collective-permute-start(bf16[1024,128]{1,0:T(8,128)(2,1)S(1)} %shard_map.86.pair_ref), channel_id=1, source_target_pairs={{0,2},{2,0},{4,6},{6,4},{8,10},{10,8},{12,14},{14,12},{16,18},{18,... | collective-permute-start | bytes 786440 | tf_op jit(solution)/shard_map/ppermute | solution.py:282
  24.3 3.1 %collective-permute-start.8 = (bf16[1024,128]{1,0:T(8,128)(2,1)S(1)}, bf16[1024,128]{1,0:T(8,128)(2,1)S(1)}, u32[]{:S(2)}, u32[]{:S(2)}) collective-permute-start(bf16[1024,128]{1,0:T(8,128)(2,1)S(1)} %collective-permute-done.7.pair_ref), channel_id=1, source_target_pairs={{0,2},{2,0},{4,6},{6,4},{8,10},{10,8},{12,14},{14,12},{16,18},{18,... | collective-permute-start | bytes 786440 | tf_op jit(solution)/shard_map/ppermute | solution.py:282
  30.8 6.0 %collective-permute-start.9 = (bf16[64,256]{1,0:T(8,128)(2,1)S(1)}, bf16[64,256]{1,0:T(8,128)(2,1)S(1)}, u32[]{:S(2)}, u32[]{:S(2)}) collective-permute-start(bf16[64,256]{1,0:T(8,128)(2,1)S(1)} %get-tuple-element.105), channel_id=1, source_target_pairs={{0,16},{2,18},{4,20},{6,22},{8,24},{10,26},{12,28},{14,30},{16,0},... | collective-permute-start | bytes 98312 | tf_op jit(solution)/shard_map/ppermute | solution.py:282
  33.8 5.7 %collective-permute-start.10 = (bf16[64,256]{1,0:T(8,128)(2,1)S(1)}, bf16[64,256]{1,0:T(8,128)(2,1)S(1)}, u32[]{:S(2)}, u32[]{:S(2)}) collective-permute-start(bf16[64,256]{1,0:T(8,128)(2,1)S(1)} %get-tuple-element.106), channel_id=1, source_target_pairs={{0,24},{2,26},{4,28},{6,30},{8,16},{10,18},{12,20},{14,22},{16,8},... | collective-permute-start | bytes 98312 | tf_op jit(solution)/shard_map/ppermute | solution.py:282
  34.2 5.3 %collective-permute-start.11 = (bf16[64,256]{1,0:T(8,128)(2,1)S(1)}, bf16[64,256]{1,0:T(8,128)(2,1)S(1)}, u32[]{:S(2)}, u32[]{:S(2)}) collective-permute-start(bf16[64,256]{1,0:T(8,128)(2,1)S(1)} %get-tuple-element.107), channel_id=1, source_target_pairs={{0,8},{2,10},{4,12},{6,14},{8,0},{10,2},{12,4},{14,6},{16,24},{18,... | collective-permute-start | bytes 98312 | tf_op jit(solution)/shard_map/ppermute | solution.py:282
  40.5 3.0 %collective-permute-start.13 = (bf16[2,64,768]{2,1,0:T(8,128)(2,1)S(1)}, bf16[2,64,768]{2,1,0:T(8,128)(2,1)S(1)}, u32[]{:S(2)}, u32[]{:S(2)}) collective-permute-start(bf16[2,64,768]{2,1,0:T(8,128)(2,1)S(1)} %get-tuple-element.114.refs_4_), channel_id=1, source_target_pairs={{0,2},{2,0},{4,6},{6,4},{8,10},{10,8},{12,14},{14,12},{16,18},{18,... | collective-permute-start | bytes 589832 | tf_op jit(solution)/shard_map/ppermute | solution.py:282
  40.6 6.8 %collective-permute-start.16 = (bf16[128,1024]{1,0:T(8,128)(2,1)S(1)}, bf16[128,1024]{1,0:T(8,128)(2,1)S(1)}, u32[]{:S(2)}, u32[]{:S(2)}) collective-permute-start(bf16[128,1024]{1,0:T(8,128)(2,1)S(1)} %get-tuple-element.113.refs_4_), channel_id=1, source_target_pairs={{0,2},{2,0},{4,6},{6,4},{8,10},{10,8},{12,14},{14,12},{16,18},{18,... | collective-permute-start | bytes 786440 | tf_op jit(solution)/shard_map/ppermute | solution.py:282
  41.9 11.2 %collective-permute-start.12 = (bf16[256,768]{1,0:T(8,128)(2,1)S(1)}, bf16[256,768]{1,0:T(8,128)(2,1)S(1)}, u32[]{:S(2)}, u32[]{:S(2)}) collective-permute-start(bf16[256,768]{1,0:T(8,128)(2,1)S(1)} %shard_map.99.a_ref._), channel_id=1, source_target_pairs={{0,1},{1,0},{2,3},{3,2},{4,5},{5,4},{6,7},{7,6},{8,9},{9,8},{10,11... | collective-permute-start | bytes 1179656 | tf_op jit(solution)/shard_map/ppermute | solution.py:282
  43.5 4.7 %collective-permute-start.14 = (bf16[64,768]{1,0:T(8,128)(2,1)S(1)}, bf16[64,768]{1,0:T(8,128)(2,1)S(1)}, u32[]{:S(2)}, u32[]{:S(2)}) collective-permute-start(bf16[64,768]{1,0:T(8,128)(2,1)S(1)} %get-tuple-element.129), channel_id=1, source_target_pairs={{0,4},{2,6},{4,0},{6,2},{8,12},{10,14},{12,8},{14,10},{16,20},{18,... | collective-permute-start | bytes 294920 | tf_op jit(solution)/shard_map/ppermute | solution.py:282
  47.4 7.8 %collective-permute-start.17 = (bf16[128,1024]{1,0:T(8,128)(2,1)S(1)}, bf16[128,1024]{1,0:T(8,128)(2,1)S(1)}, u32[]{:S(2)}, u32[]{:S(2)}) collective-permute-start(bf16[128,1024]{1,0:T(8,128)(2,1)S(1)} %shard_map.106), channel_id=1, source_target_pairs={{0,4},{2,6},{4,0},{6,2},{8,12},{10,14},{12,8},{14,10},{16,20},{18,... | collective-permute-start | bytes 786440 | tf_op jit(solution)/shard_map/ppermute | solution.py:282
  48.2 6.2 %collective-permute-start.15 = (bf16[64,768]{1,0:T(8,128)(2,1)S(1)}, bf16[64,768]{1,0:T(8,128)(2,1)S(1)}, u32[]{:S(2)}, u32[]{:S(2)}) collective-permute-start(bf16[64,768]{1,0:T(8,128)(2,1)S(1)} %shard_map.103.refs_1_.a_ref), channel_id=1, source_target_pairs={{0,16},{2,18},{4,20},{6,22},{8,24},{10,26},{12,28},{14,30},{16,0},... | collective-permute-start | bytes 294920 | tf_op jit(solution)/shard_map/ppermute | solution.py:282
  51.5 6.0 %collective-permute-start.18 = (bf16[128,1024]{1,0:T(8,128)(2,1)S(1)}, bf16[128,1024]{1,0:T(8,128)(2,1)S(1)}, u32[]{:S(2)}, u32[]{:S(2)}) collective-permute-start(bf16[128,1024]{1,0:T(8,128)(2,1)S(1)} %get-tuple-element.132.refs_0_), channel_id=1, source_target_pairs={{0,2},{2,0},{4,6},{6,4},{8,10},{10,8},{12,14},{14,12},{16,18},{18,... | collective-permute-start | bytes 786440 | tf_op jit(solution)/shard_map/ppermute | solution.py:282
  54.5 5.6 %collective-permute-start.22 = (bf16[64,768]{1,0:T(8,128)(2,1)S(1)}, bf16[64,768]{1,0:T(8,128)(2,1)S(1)}, u32[]{:S(2)}, u32[]{:S(2)}) collective-permute-start(bf16[64,768]{1,0:T(8,128)(2,1)S(1)} %shard_map.105.refs_1_.a_ref), channel_id=1, source_target_pairs={{0,8},{2,10},{4,12},{6,14},{8,0},{10,2},{12,4},{14,6},{16,24},{18,... | collective-permute-start | bytes 294920 | tf_op jit(solution)/shard_map/ppermute | solution.py:282
  57.7 8.9 %collective-permute-start.19 = (bf16[192,256]{1,0:T(8,128)(2,1)S(1)}, bf16[192,256]{1,0:T(8,128)(2,1)S(1)}, u32[]{:S(2)}, u32[]{:S(2)}) collective-permute-start(bf16[192,256]{1,0:T(8,128)(2,1)S(1)} %get-tuple-element.137), channel_id=1, source_target_pairs={{0,16},{2,18},{4,20},{6,22},{8,24},{10,26},{12,28},{14,30},{16,0},... | collective-permute-start | bytes 294920 | tf_op jit(solution)/shard_map/ppermute | solution.py:282
  60.1 4.7 %collective-permute-start.24 = (bf16[64,768]{1,0:T(8,128)(2,1)S(1)}, bf16[64,768]{1,0:T(8,128)(2,1)S(1)}, u32[]{:S(2)}, u32[]{:S(2)}) collective-permute-start(bf16[64,768]{1,0:T(8,128)(2,1)S(1)} %shard_map.111.refs_0_), channel_id=1, source_target_pairs={{0,4},{2,6},{4,0},{6,2},{8,12},{10,14},{12,8},{14,10},{16,20},{18,... | collective-permute-start | bytes 294920 | tf_op jit(solution)/shard_map/ppermute | solution.py:282
  61.7 6.6 %collective-permute-start.20 = (bf16[192,256]{1,0:T(8,128)(2,1)S(1)}, bf16[192,256]{1,0:T(8,128)(2,1)S(1)}, u32[]{:S(2)}, u32[]{:S(2)}) collective-permute-start(bf16[192,256]{1,0:T(8,128)(2,1)S(1)} %get-tuple-element.138), channel_id=1, source_target_pairs={{0,24},{2,26},{4,28},{6,30},{8,16},{10,18},{12,20},{14,22},{16,8},... | collective-permute-start | bytes 294920 | tf_op jit(solution)/shard_map/ppermute | solution.py:282
  63.2 5.7 %collective-permute-start.21 = (bf16[192,256]{1,0:T(8,128)(2,1)S(1)}, bf16[192,256]{1,0:T(8,128)(2,1)S(1)}, u32[]{:S(2)}, u32[]{:S(2)}) collective-permute-start(bf16[192,256]{1,0:T(8,128)(2,1)S(1)} %get-tuple-element.139), channel_id=1, source_target_pairs={{0,8},{2,10},{4,12},{6,14},{8,0},{10,2},{12,4},{14,6},{16,24},{18,... | collective-permute-start | bytes 294920 | tf_op jit(solution)/shard_map/ppermute | solution.py:282
  63.2 6.6 %collective-permute-start.23 = (bf16[64,768]{1,0:T(8,128)(2,1)S(1)}, bf16[64,768]{1,0:T(8,128)(2,1)S(1)}, u32[]{:S(2)}, u32[]{:S(2)}) collective-permute-start(bf16[64,768]{1,0:T(8,128)(2,1)S(1)} %shard_map.111.refs_0_), channel_id=1, source_target_pairs={{0,2},{2,0},{4,6},{6,4},{8,10},{10,8},{12,14},{14,12},{16,18},{18,... | collective-permute-start | bytes 294920 | tf_op jit(solution)/shard_map/ppermute | solution.py:282
  64.8 5.0 %collective-permute-start.25 = (bf16[64,768]{1,0:T(8,128)(2,1)S(1)}, bf16[64,768]{1,0:T(8,128)(2,1)S(1)}, u32[]{:S(2)}, u32[]{:S(2)}) collective-permute-start(bf16[64,768]{1,0:T(8,128)(2,1)S(1)} %collective-permute-done.24.refs_2_), channel_id=1, source_target_pairs={{0,2},{2,0},{4,6},{6,4},{8,10},{10,8},{12,14},{14,12},{16,18},{18,... | collective-permute-start | bytes 294920 | tf_op jit(solution)/shard_map/ppermute | solution.py:282

commit v11 on v10

--- a/solution.py
+++ b/solution.py
@@ -236,12 +236,13 @@
         out_ref[...] = (kept_ref[index].astype(F32) + came_ref[index].astype(F32)).astype(BF16)
 
 
-def add_pieces_kernel(slots, rows, dim, kept_ref, came_ref, dq_ref, *outs):
+def add_pieces_kernel(slots, rows, dim, a_of, kept_ref, came_ref, dq_ref, out_ref):
     wide = 2 * dim
-    for slot in range(slots):
+    me = a_of()
+    for slot, mask in enumerate(spread(slots)):
         here = slice(slot * rows, (slot + 1) * rows)
-        outs[slot][0:wide, :] = (kept_ref[:, here].astype(F32) + came_ref[:, here].astype(F32)).astype(BF16)
-        outs[slot][wide:, :] = (dq_ref[:, here] * dim**-0.5).astype(BF16)
+        out_ref[me ^ mask, 0:wide, :] = (kept_ref[:, here].astype(F32) + came_ref[:, here].astype(F32)).astype(BF16)
+        out_ref[me ^ mask, wide:, :] = (dq_ref[:, here] * dim**-0.5).astype(BF16)
 
 
 def add_out_kernel(a_ref, b_ref, out_ref, done_ref):
@@ -253,20 +254,16 @@
     refs[-1][...] = (a_ref[...].astype(F32) + b_ref[...].astype(F32)).astype(refs[-1].dtype)
 
 
-def unpack_kernel(slots, rows, dim, a_of, *refs):
-    pieces, (kv_out, q_out) = refs[:slots], refs[-2:]
+def finish_kernel(slots, rows, dim, columns, b_of, got_ref, *refs):
+    parts, (kv_out, q_out, *outs) = refs[:columns], refs[columns:]
     wide = 2 * dim
-    me = a_of()
-    for slot, mask in enumerate(spread(slots)):
-        kv_out[pl.ds(me ^ mask, rows, stride=slots), :] = pieces[slot][0:wide, :].astype(F32).T
-        q_out[me ^ mask] = pieces[slot][wide:, :].astype(F32)
-
-
-def place_kernel(columns, b_of, *refs):
-    parts, (out_ref,) = refs[:columns], refs[columns:]
-    me = b_of()
-    for column in range(columns):
-        out_ref[me ^ column] = parts[column][...].astype(F32)
+    if columns:
+        me = b_of()
+        for column in range(columns):
+            outs[-1][me ^ column] = parts[column][...].astype(F32)
+    for head in range(slots):
+        kv_out[pl.ds(head, rows, stride=slots), :] = got_ref[head, 0:wide, :].astype(F32).T
+        q_out[head] = got_ref[head, wide:, :].astype(F32)
 
 
 def shards(seq, mp, queries, key_value, tile_fill, out_weight, grad_output):
@@ -383,25 +380,27 @@
             bit *= 2
         halved = dkv[0], swap(dkv[bit], bit)
     pieces = call(
-        functools.partial(add_pieces_kernel, slots, rows, dim), [((wide + dim, rows), BF16)] * slots, n_in=3,
-    )(*halved, dq)
-    returned = exchange(pieces)
+        functools.partial(add_pieces_kernel, slots, rows, dim, a_of), [((slots, wide + dim, rows), BF16)], n_in=3,
+    )(*halved, dq)[0]
+    got = pieces
+    if slots > 1:
+        groups = [[a * columns + b for a in range(slots)] for b in range(columns)]
+        got = lax.all_to_all(pieces, "seq", 0, 0, axis_index_groups=groups, tiled=True)
 
     if halves:
         for mask in far_masks[1:]:
-            kept = add(kept, swap(kept, mask), pieces[0])[0]
+            kept = add(kept, swap(kept, mask), pieces)[0]
         across = swap(kept, 2)
-        weight_grad = call(
-            functools.partial(place_kernel, columns, b_of), [((heads, dim, width), F32)], n_in=columns, micros=0.5,
-        )(kept, swap(kept, 1), across, swap(across, 1))[0]
+        parts = [kept, swap(kept, 1), across, swap(across, 1)]
     else:
-        weight_grad = lax.psum(weight_terms[0].astype(F32), "seq")
-
-    key_value_grad, query_grad = call(
-        functools.partial(unpack_kernel, slots, rows, dim, a_of),
-        [((rows * heads, wide), F32), ((heads, dim, rows), F32)],
-        n_in=slots, micros=1,
-    )(*returned)
+        parts, weight_grad = [], lax.psum(weight_terms[0].astype(F32), "seq")
+    outs = [((rows * heads, wide), F32), ((heads, dim, rows), F32)]
+    outs += [((heads, dim, width), F32)] if parts else []
+    key_value_grad, query_grad, *outs = call(
+        functools.partial(finish_kernel, slots, rows, dim, len(parts), b_of), outs,
+        n_in=1 + len(parts), micros=1,
+    )(got, *parts)
+    weight_grad = outs[0] if parts else weight_grad
     return terms, jnp.transpose(query_grad, (2, 0, 1)), key_value_grad.reshape(rows, heads, wide), weight_grad
 
 

time: 71 us -> 79.2 us (1.12)
  waiting for transfers between devices: 14.4 us -> 21.2 us
  starting transfers between devices: 26.2 us -> 27.5 us
    ppermute x26 -> x23, waiting for transfers between devices: 14.4 us -> 21.2 us  [swap(): return lax.ppermute(array, axis, [(i, i ^ mask) for i in range(size)])]
    all_to_all x0 -> x1, starting transfers between devices: none -> 3.46 us  [shards(): lax.all_to_all(pieces, 'seq', 0, 0, axis_index_groups=groups, tiled=True)]
    ppermute x26 -> x23, starting transfers between devices: 26.2 us -> 24.1 us  [swap(): return lax.ppermute(array, axis, [(i, i ^ mask) for i in range(size)])]
    pallas_call x4 -> x3, Pallas kernels: 2.02 us -> 2.08 us  [the longest x1 1.22 us: shards(): call(functools.partial(finish_kernel, slots, rows, dim, len(parts), b_of)...]
  transfers between devices with their start and end apart: 26 -> 24, of which waited for: 12 -> 11; matrix products, arithmetic and copies ran while one was open for 0% -> 0% of each run, Pallas kernels for 31% -> 27%
where the time goes in v11:
time: 79.2 us; the launch traced here: 79 us
  Pallas kernels  29.3 us (37%)
  starting transfers between devices  27.5 us (35%)
  waiting for transfers between devices  21.2 us (27%)
  between operations  0.95 us (1%)
    ppermute x23, starting transfers between devices, swap(): return lax.ppermute(array, axis, [(i, i ^ mask) for i in range(size)])  24.1 us
    ppermute x23, waiting for transfers between devices, swap(): return lax.ppermute(array, axis, [(i, i ^ mask) for i in range(size)])  21.2 us
    pallas_call x4, Pallas kernels, shards(): call(functools.partial(score_kernel, slots, rows, dim, step), [((block, b...  10.9 us
    pallas_call x4, Pallas kernels, shards(): call(functools.partial(back_kernel, slots, rows, dim, dq is None), [((wid...  9.13 us
    all_to_all x1, starting transfers between devices, shards(): lax.all_to_all(pieces, 'seq', 0, 0, axis_index_groups=groups, tiled=True)  3.46 us
    pallas_call x1, Pallas kernels, shards(): call(functools.partial(pack_kv_kernel, heads, rows, dim, a_of), [((rows,...  1.9 us
  transfers between devices with their start and end apart: 24, of which 11 were waited for; matrix products, arithmetic and copies ran while one was open for 0% of the time, Pallas kernels for 27%

profile of v11, /device:TPU:0, one launch (start us, length us, event | category | flops | bytes accessed | tf_op | source)
XLA Modules:
  0.0 79.0 jit_solution(3071314125338964983)
XLA Ops:
  0.7 1.9 %shard_map.84 = (bf16[256,128]{1,0:T(8,128)(2,1)}, bf16[256,128]{1,0:T(8,128)(2,1)}, bf16[256,128]{1,0:T(8,128)(2,1)}, bf16[256,128]{1,0:T(8,128)(2,1)}) custom-call(s32[2]{0:T(128)} %fill_ref.7, bf16[1024,128]{1,0:T(8,128)(2,1)} %bitcast.5), custom_call_target="tpu_custom_call" | custom-call | flops 1724999936 | tf_op jit(solution)/shard_map/pallas_call | solution.py:285
  2.6 4.0 %collective-permute-start = (bf16[256,128]{1,0:T(8,128)(2,1)}, bf16[256,128]{1,0:T(8,128)(2,1)S(1)}, u32[]{:S(2)}, u32[]{:S(2)}) collective-permute-start(bf16[256,128]{1,0:T(8,128)(2,1)} %get-tuple-element.71), channel_id=1, source_target_pairs={{0,16},{2,18},{4,20},{6,22},{8,24},{10,26},{12,28},{14,30},{16,0},... | collective-permute-start | bytes 196616 | tf_op jit(solution)/shard_map/ppermute | solution.py:279
  6.6 1.3 %collective-permute-start.1 = (bf16[256,128]{1,0:T(8,128)(2,1)}, bf16[256,128]{1,0:T(8,128)(2,1)S(1)}, u32[]{:S(2)}, u32[]{:S(2)}) collective-permute-start(bf16[256,128]{1,0:T(8,128)(2,1)} %get-tuple-element.72), channel_id=1, source_target_pairs={{0,24},{2,26},{4,28},{6,30},{8,16},{10,18},{12,20},{14,22},{16,8},... | collective-permute-start | bytes 196616 | tf_op jit(solution)/shard_map/ppermute | solution.py:279
  8.0 0.2 collective-permute-start.2
  8.2 0.0 copy-start
  8.2 0.9 %shard_map.85 = (bf16[128,256]{1,0:T(8,128)(2,1)S(1)}, bf16[128,256]{1,0:T(8,128)(2,1)S(1)}, bf16[128,256]{1,0:T(8,128)(2,1)S(1)}, bf16[128,256]{1,0:T(8,128)(2,1)S(1)}) custom-call(s32[2]{0:T(128)S(1)} %copy-done.4, bf16[4,64,256]{2,1,0:T(8,128)(2,1)S(1)} %bitcast.4, bf16[4,64,768]{2,1,0:T(8,128)(2,1)S(1)} %copy-done.2, bf16[256,768]{1,0:T(8,128)(2,1)S(1)} %copy-done.1), custom_call_target="tpu_custom_call" | custom-call | flops 1150000000 | tf_op jit(solution)/shard_map/pallas_call | solution.py:290
  9.2 2.9 %collective-permute-start.3 = (bf16[128,256]{1,0:T(8,128)(2,1)S(1)}, bf16[128,256]{1,0:T(8,128)(2,1)S(1)}, u32[]{:S(2)}, u32[]{:S(2)}) collective-permute-start(bf16[128,256]{1,0:T(8,128)(2,1)S(1)} %get-tuple-element.78), channel_id=1, source_target_pairs={{0,16},{2,18},{4,20},{6,22},{8,24},{10,26},{12,28},{14,30},{16,0},... | collective-permute-start | bytes 196616 | tf_op jit(solution)/shard_map/ppermute | solution.py:279
  12.0 1.3 %collective-permute-start.4 = (bf16[128,256]{1,0:T(8,128)(2,1)S(1)}, bf16[128,256]{1,0:T(8,128)(2,1)S(1)}, u32[]{:S(2)}, u32[]{:S(2)}) collective-permute-start(bf16[128,256]{1,0:T(8,128)(2,1)S(1)} %get-tuple-element.79), channel_id=1, source_target_pairs={{0,24},{2,26},{4,28},{6,30},{8,16},{10,18},{12,20},{14,22},{16,8},... | collective-permute-start | bytes 196616 | tf_op jit(solution)/shard_map/ppermute | solution.py:279
  13.4 0.0 collective-permute-done.refs_1_
  13.4 0.0 collective-permute-start.5
  13.4 0.0 collective-permute-done.1.refs_2_
  13.4 1.6 %collective-permute-start.7 = (bf16[1024,128]{1,0:T(8,128)(2,1)S(1)}, bf16[1024,128]{1,0:T(8,128)(2,1)S(1)}, u32[]{:S(2)}, u32[]{:S(2)}) collective-permute-start(bf16[1024,128]{1,0:T(8,128)(2,1)S(1)} %shard_map.86.pair_ref), channel_id=1, source_target_pairs={{0,4},{2,6},{4,0},{6,2},{8,12},{10,14},{12,8},{14,10},{16,20},{18,... | collective-permute-start | bytes 786440 | tf_op jit(solution)/shard_map/ppermute | solution.py:279
  15.0 0.3 shard_map.87
  15.4 1.8 %collective-permute-done.3.refs_1_ = bf16[128,256]{1,0:T(8,128)(2,1)S(1)} collective-permute-done((bf16[128,256]{1,0:T(8,128)(2,1)S(1)}, bf16[128,256]{1,0:T(8,128)(2,1)S(1)}, u32[]{:S(2)}, u32[]{:S(2)}) %collective-permute-start.3) | collective-permute-done | bytes 65568 | tf_op jit(solution)/shard_map/ppermute | solution.py:279
  17.2 1.1 %collective-permute-done.4.refs_2_ = bf16[128,256]{1,0:T(8,128)(2,1)S(1)} collective-permute-done((bf16[128,256]{1,0:T(8,128)(2,1)S(1)}, bf16[128,256]{1,0:T(8,128)(2,1)S(1)}, u32[]{:S(2)}, u32[]{:S(2)}) %collective-permute-start.4) | collective-permute-done | bytes 65568 | tf_op jit(solution)/shard_map/ppermute | solution.py:279
  18.3 0.2 collective-permute-done.5.refs_3_
  18.5 0.1 shard_map.88
  18.6 2.7 %shard_map.89 = (bf16[1024,1024]{1,0:T(8,128)(2,1)S(1)}, f32[1,1024]{1,0:T(1,128)S(1)}, f32[80,1024]{1,0:T(8,128)S(1)}) custom-call(bf16[1024,256]{1,0:T(8,128)(2,1)S(1)} %get-tuple-element.75.wide_ref, bf16[80,1024]{1,0:T(8,128)(2,1)S(1)} %get-tuple-element.76.vt_ref, f32[1,1024]{1,0:T(1,128)S(1)} %get-tuple-element.77.norm_ref, ...), custom_call_target="tpu_custom_call" | custom-call | flops 4600000000 | tf_op jit(solution)/shard_map/pallas_call | solution.py:319
  21.3 0.3 shard_map.90
  21.6 2.7 %shard_map.91 = (bf16[1024,1024]{1,0:T(8,128)(2,1)S(1)}, f32[1,1024]{1,0:T(1,128)S(1)}, f32[80,1024]{1,0:T(8,128)S(1)}) custom-call(bf16[1024,256]{1,0:T(8,128)(2,1)S(1)} %get-tuple-element.84.wide_ref, bf16[80,1024]{1,0:T(8,128)(2,1)S(1)} %get-tuple-element.85.vt_ref, f32[1,1024]{1,0:T(1,128)S(1)} %get-tuple-element.86.norm_ref, ...), custom_call_target="tpu_custom_call" | custom-call | flops 4600000000 | tf_op jit(solution)/shard_map/pallas_call | solution.py:319
  24.3 0.1 collective-permute-start.8
  24.4 0.3 shard_map.92
  24.7 2.7 %shard_map.93 = (bf16[1024,1024]{1,0:T(8,128)(2,1)S(1)}, f32[1,1024]{1,0:T(1,128)S(1)}, f32[80,1024]{1,0:T(8,128)S(1)}) custom-call(bf16[1024,256]{1,0:T(8,128)(2,1)S(1)} %get-tuple-element.88.wide_ref, bf16[80,1024]{1,0:T(8,128)(2,1)S(1)} %get-tuple-element.89.vt_ref, f32[1,1024]{1,0:T(1,128)S(1)} %get-tuple-element.90.norm_ref, ...), custom_call_target="tpu_custom_call" | custom-call | flops 4600000000 | tf_op jit(solution)/shard_map/pallas_call | solution.py:319
  27.4 0.0 collective-permute-done.8.pair_ref
  27.4 0.3 shard_map.94
  27.7 2.9 %shard_map.95 = (bf16[1024,1024]{1,0:T(8,128)(2,1)S(1)}, f32[1,1024]{1,0:T(1,128)S(1)}, f32[80,1024]{1,0:T(8,128)S(1)}) custom-call(bf16[1024,256]{1,0:T(8,128)(2,1)S(1)} %get-tuple-element.92.wide_ref, bf16[80,1024]{1,0:T(8,128)(2,1)S(1)} %get-tuple-element.93.vt_ref, f32[1,1024]{1,0:T(1,128)S(1)} %get-tuple-element.94.norm_ref, ...), custom_call_target="tpu_custom_call" | custom-call | flops 4600000000 | tf_op jit(solution)/shard_map/pallas_call | solution.py:319
  30.6 0.2 shard_map.96
  30.7 3.1 %collective-permute-start.9 = (bf16[64,256]{1,0:T(8,128)(2,1)S(1)}, bf16[64,256]{1,0:T(8,128)(2,1)S(1)}, u32[]{:S(2)}, u32[]{:S(2)}) collective-permute-start(bf16[64,256]{1,0:T(8,128)(2,1)S(1)} %get-tuple-element.102), channel_id=1, source_target_pairs={{0,16},{2,18},{4,20},{6,22},{8,24},{10,26},{12,28},{14,30},{16,0},... | collective-permute-start | bytes 98312 | tf_op jit(solution)/shard_map/ppermute | solution.py:279
  33.8 0.4 collective-permute-start.10
  34.2 0.2 collective-permute-start.11
  34.5 2.3 %shard_map.97 = (bf16[128,1024]{1,0:T(8,128)(2,1)S(1)}, f32[64,1024]{1,0:T(8,128)S(1)}) custom-call(bf16[1024,1024]{1,0:T(8,128)(2,1)S(1)} %get-tuple-element.105.exp_ref, bf16[1024,256]{1,0:T(8,128)(2,1)S(1)} %get-tuple-element.92.wide_ref, bf16[64,1024]{1,0:T(8,128)(2,1)S(1)} %get-tuple-element.106.kt_ref, bf16[64,1024]{1,0:T(8,128)(2,1)S(1)} %get-tuple-element.107.q_ref, ...), custom_call_target="tpu_custom_call" | custom-call | flops 2300000000 | tf_op jit(solution)/shard_map/pallas_call | solution.py:365
  36.7 2.8 %collective-permute-done.10.refs_2_ = bf16[64,256]{1,0:T(8,128)(2,1)S(1)} collective-permute-done((bf16[64,256]{1,0:T(8,128)(2,1)S(1)}, bf16[64,256]{1,0:T(8,128)(2,1)S(1)}, u32[]{:S(2)}, u32[]{:S(2)}) %collective-permute-start.10) | collective-permute-done | bytes 32800 | tf_op jit(solution)/shard_map/ppermute | solution.py:279
  39.5 0.0 collective-permute-done.11.refs_3_
  39.5 0.9 %shard_map.98 = (bf16[2,64,768]{2,1,0:T(8,128)(2,1)S(1)}, bf16[2,64,768]{2,1,0:T(8,128)(2,1)S(1)}) custom-call(s32[2]{0:T(128)S(1)} %copy-done.4, bf16[256,768]{1,0:T(8,128)(2,1)S(1)} %copy-done.1, bf16[64,256]{1,0:T(8,128)(2,1)S(1)} %get-tuple-element.101.refs_0_, bf16[64,256]{1,0:T(8,128)(2,1)S(1)} %collective-permute-done.9.refs_1_, ...), custom_call_target="tpu_custom_call" | custom-call | flops 805000000 | tf_op jit(solution)/shard_map/pallas_call | solution.py:338
  40.5 0.1 collective-permute-start.13
  40.5 0.5 collective-permute-start.16
  41.0 0.8 %shard_map.99.a_ref._ = bf16[256,768]{1,0:T(8,128)(2,1)S(1)} custom-call(s32[2]{0:T(128)S(1)} %copy-done.4, bf16[4,64,768]{2,1,0:T(8,128)(2,1)S(1)} %copy-done.2, bf16[64,256]{1,0:T(8,128)(2,1)S(1)} %get-tuple-element.101.refs_0_, bf16[64,256]{1,0:T(8,128)(2,1)S(1)} %collective-permute-done.9.refs_1_, bf16[64,256]{1,0:T(8,128)(2,1)S(1)} %collective-permute-done.10.refs_2_, ...), custom_call_target="tpu_custom_call" | custom-call | flops 805000000 | tf_op jit(solution)/shard_map/pallas_call | solution.py:344
  41.9 1.6 %collective-permute-start.12 = (bf16[256,768]{1,0:T(8,128)(2,1)S(1)}, bf16[256,768]{1,0:T(8,128)(2,1)S(1)}, u32[]{:S(2)}, u32[]{:S(2)}) collective-permute-start(bf16[256,768]{1,0:T(8,128)(2,1)S(1)} %shard_map.99.a_ref._), channel_id=1, source_target_pairs={{0,1},{1,0},{2,3},{3,2},{4,5},{5,4},{6,7},{7,6},{8,9},{9,8},{10,11... | collective-permute-start | bytes 1179656 | tf_op jit(solution)/shard_map/ppermute | solution.py:279
  43.5 1.6 %collective-permute-start.14 = (bf16[64,768]{1,0:T(8,128)(2,1)S(1)}, bf16[64,768]{1,0:T(8,128)(2,1)S(1)}, u32[]{:S(2)}, u32[]{:S(2)}) collective-permute-start(bf16[64,768]{1,0:T(8,128)(2,1)S(1)} %get-tuple-element.126), channel_id=1, source_target_pairs={{0,4},{2,6},{4,0},{6,2},{8,12},{10,14},{12,8},{14,10},{16,20},{18,... | collective-permute-start | bytes 294920 | tf_op jit(solution)/shard_map/ppermute | solution.py:279
  45.0 2.3 %shard_map.102 = (bf16[128,1024]{1,0:T(8,128)(2,1)S(1)}, f32[64,1024]{1,0:T(8,128)S(1)}) custom-call(bf16[1024,1024]{1,0:T(8,128)(2,1)S(1)} %get-tuple-element.119.exp_ref, bf16[1024,256]{1,0:T(8,128)(2,1)S(1)} %get-tuple-element.88.wide_ref, bf16[64,1024]{1,0:T(8,128)(2,1)S(1)} %get-tuple-element.120.kt_ref, bf16[64,1024]{1,0:T(8,128)(2,1)S(1)} %get-tuple-element.107.q_ref, ...), custom_call_target="tpu_custom_call" | custom-call | flops 2300000000 | tf_op jit(solution)/shard_map/pallas_call | solution.py:365
  47.3 0.1 shard_map.106
  47.4 0.6 collective-permute-start.17
  48.0 0.2 collective-permute-done.14.b_ref
  48.2 1.0 %collective-permute-start.15 = (bf16[64,768]{1,0:T(8,128)(2,1)S(1)}, bf16[64,768]{1,0:T(8,128)(2,1)S(1)}, u32[]{:S(2)}, u32[]{:S(2)}) collective-permute-start(bf16[64,768]{1,0:T(8,128)(2,1)S(1)} %shard_map.103.refs_1_.a_ref), channel_id=1, source_target_pairs={{0,16},{2,18},{4,20},{6,22},{8,24},{10,26},{12,28},{14,30},{16,0},... | collective-permute-start | bytes 294920 | tf_op jit(solution)/shard_map/ppermute | solution.py:279
  49.2 2.3 %shard_map.104 = (bf16[128,1024]{1,0:T(8,128)(2,1)S(1)}, f32[64,1024]{1,0:T(8,128)S(1)}) custom-call(bf16[1024,1024]{1,0:T(8,128)(2,1)S(1)} %get-tuple-element.116.exp_ref, bf16[1024,256]{1,0:T(8,128)(2,1)S(1)} %get-tuple-element.84.wide_ref, bf16[64,1024]{1,0:T(8,128)(2,1)S(1)} %get-tuple-element.117.kt_ref, bf16[64,1024]{1,0:T(8,128)(2,1)S(1)} %get-tuple-element.107.q_ref, ...), custom_call_target="tpu_custom_call" | custom-call | flops 2300000000 | tf_op jit(solution)/shard_map/pallas_call | solution.py:365
  51.5 0.1 collective-permute-start.18
  51.6 1.4 %collective-permute-done.12.b_ref = bf16[256,768]{1,0:T(8,128)(2,1)S(1)} collective-permute-done((bf16[256,768]{1,0:T(8,128)(2,1)S(1)}, bf16[256,768]{1,0:T(8,128)(2,1)S(1)}, u32[]{:S(2)}, u32[]{:S(2)}) %collective-permute-start.12) | collective-permute-done | bytes 393248 | tf_op jit(solution)/shard_map/ppermute | solution.py:279
  53.0 0.8 %shard_map.100 = (bf16[256,768]{1,0:T(8,128)(2,1)}, f32[8,128]{1,0:T(8,128)S(1)}) custom-call(bf16[256,768]{1,0:T(8,128)(2,1)S(1)} %shard_map.99.a_ref._, bf16[256,768]{1,0:T(8,128)(2,1)S(1)} %collective-permute-done.12.b_ref), custom_call_target="tpu_custom_call" | custom-call | flops 11500000 | tf_op jit(solution)/shard_map/pallas_call | solution.py:351
  53.9 0.6 collective-permute-done.15.b_ref
  54.5 0.7 collective-permute-done.17.refs_2_.came_ref
  55.2 2.3 %shard_map.107 = (bf16[128,1024]{1,0:T(8,128)(2,1)S(1)}, f32[64,1024]{1,0:T(8,128)S(1)}) custom-call(bf16[1024,1024]{1,0:T(8,128)(2,1)S(1)} %get-tuple-element.113.exp_ref, bf16[1024,256]{1,0:T(8,128)(2,1)S(1)} %get-tuple-element.75.wide_ref, bf16[64,1024]{1,0:T(8,128)(2,1)S(1)} %get-tuple-element.114.kt_ref, bf16[64,1024]{1,0:T(8,128)(2,1)S(1)} %get-tuple-element.107.q_ref, ...), custom_call_target="tpu_custom_call" | custom-call | flops 2300000000 | tf_op jit(solution)/shard_map/pallas_call | solution.py:365
  57.5 0.1 shard_map.108.kept_ref
  57.6 0.8 %shard_map.109.refs_0_ = bf16[4,192,256]{2,1,0:T(8,128)(2,1)} custom-call(bf16[128,1024]{1,0:T(8,128)(2,1)S(1)} %shard_map.108.kept_ref, bf16[128,1024]{1,0:T(8,128)(2,1)S(1)} %collective-permute-done.17.refs_2_.came_ref, f32[64,1024]{1,0:T(8,128)S(1)} %get-tuple-element.132.dq_ref), custom_call_target="tpu_custom_call" | custom-call | flops 11500000 | tf_op jit(solution)/shard_map/pallas_call | solution.py:382
  58.4 3.5 %all-to-all-start = ((bf16[4,192,256]{2,1,0:T(8,128)(2,1)}), bf16[4,192,256]{2,1,0:T(8,128)(2,1)S(1)}, u32[]{:S(2)}, u32[]{:S(2)}) async-start(bf16[4,192,256]{2,1,0:T(8,128)(2,1)} %shard_map.109.refs_0_), calls=%async_computation | async-start | bytes 786432 | tf_op jit(solution)/shard_map/all_to_all | solution.py:388
  61.9 2.0 %collective-permute-start.19 = (bf16[64,768]{1,0:T(8,128)(2,1)S(1)}, bf16[64,768]{1,0:T(8,128)(2,1)S(1)}, u32[]{:S(2)}, u32[]{:S(2)}) collective-permute-start(bf16[64,768]{1,0:T(8,128)(2,1)S(1)} %shard_map.105.refs_1_.a_ref), channel_id=1, source_target_pairs={{0,8},{2,10},{4,12},{6,14},{8,0},{10,2},{12,4},{14,6},{16,24},{18,... | collective-permute-start | bytes 294920 | tf_op jit(solution)/shard_map/ppermute | solution.py:279
  63.9 7.9 %collective-permute-done.19.b_ref = bf16[64,768]{1,0:T(8,128)(2,1)S(1)} collective-permute-done((bf16[64,768]{1,0:T(8,128)(2,1)S(1)}, bf16[64,768]{1,0:T(8,128)(2,1)S(1)}, u32[]{:S(2)}, u32[]{:S(2)}) %collective-permute-start.19) | collective-permute-done | bytes 98336 | tf_op jit(solution)/shard_map/ppermute | solution.py:279
  71.8 1.5 %collective-permute-start.21 = (bf16[64,768]{1,0:T(8,128)(2,1)S(1)}, bf16[64,768]{1,0:T(8,128)(2,1)S(1)}, u32[]{:S(2)}, u32[]{:S(2)}) collective-permute-start(bf16[64,768]{1,0:T(8,128)(2,1)S(1)} %shard_map.110.refs_0_), channel_id=1, source_target_pairs={{0,4},{2,6},{4,0},{6,2},{8,12},{10,14},{12,8},{14,10},{16,20},{18,... | collective-permute-start | bytes 294920 | tf_op jit(solution)/shard_map/ppermute | solution.py:279
  73.2 0.0 collective-permute-start.20
  73.3 3.2 %collective-permute-done.21.refs_2_ = bf16[64,768]{1,0:T(8,128)(2,1)S(1)} collective-permute-done((bf16[64,768]{1,0:T(8,128)(2,1)S(1)}, bf16[64,768]{1,0:T(8,128)(2,1)S(1)}, u32[]{:S(2)}, u32[]{:S(2)}) %collective-permute-start.21) | collective-permute-done | bytes 98336 | tf_op jit(solution)/shard_map/ppermute | solution.py:279
  76.5 0.0 collective-permute-start.22
  76.5 0.0 collective-permute-done.20.refs_1_
  76.5 1.3 %collective-permute-done.22.refs_3_ = bf16[64,768]{1,0:T(8,128)(2,1)S(1)} collective-permute-done((bf16[64,768]{1,0:T(8,128)(2,1)S(1)}, bf16[64,768]{1,0:T(8,128)(2,1)S(1)}, u32[]{:S(2)}, u32[]{:S(2)}) %collective-permute-start.22) | collective-permute-done | bytes 98336 | tf_op jit(solution)/shard_map/ppermute | solution.py:279
  77.8 0.0 all-to-all-done.got_ref
  77.8 1.2 %shard_map.111 = (f32[1024,128]{1,0:T(8,128)}, f32[4,64,256]{2,1,0:T(8,128)}, f32[4,64,768]{2,1,0:T(8,128)}) custom-call(bf16[4,192,256]{2,1,0:T(8,128)(2,1)S(1)} %all-to-all-done.got_ref, bf16[64,768]{1,0:T(8,128)(2,1)S(1)} %shard_map.110.refs_0_, bf16[64,768]{1,0:T(8,128)(2,1)S(1)} %collective-permute-done.20.refs_1_, ...), custom_call_target="tpu_custom_call" | custom-call | flops 1150000000 | tf_op jit(solution)/shard_map/pallas_call | solution.py:399
  (22 shorter events, 0.2 us)
Async XLA Ops:
  0.6 7.6 %copy-start.1 = (bf16[256,768]{1,0:T(8,128)(2,1)S(1)}, bf16[256,768]{1,0:T(8,128)(2,1)}, u32[]{:S(2)}) copy-start(bf16[256,768]{1,0:T(8,128)(2,1)} %go_ref.3) | copy-start | bytes 1179652
  0.6 7.6 %copy-start.2 = (bf16[4,64,768]{2,1,0:T(8,128)(2,1)S(1)}, bf16[4,64,768]{2,1,0:T(8,128)(2,1)}, u32[]{:S(2)}) copy-start(bf16[4,64,768]{2,1,0:T(8,128)(2,1)} %w_ref.3) | copy-start | bytes 1179652
  0.7 7.5 %copy-start.3 = (bf16[256,4,64]{0,2,1:T(8,128)(2,1)S(1)}, bf16[256,4,64]{0,2,1:T(8,128)(2,1)}, u32[]{:S(2)}) copy-start(bf16[256,4,64]{0,2,1:T(8,128)(2,1)} %param.5) | copy-start | bytes 393220
  0.7 7.5 %copy-start.4 = (s32[2]{0:T(128)S(1)}, s32[2]{0:T(128)}, u32[]{:S(2)}) copy-start(s32[2]{0:T(128)} %fill_ref.7) | copy-start | bytes 28
  2.6 10.8 %collective-permute-start = (bf16[256,128]{1,0:T(8,128)(2,1)}, bf16[256,128]{1,0:T(8,128)(2,1)S(1)}, u32[]{:S(2)}, u32[]{:S(2)}) collective-permute-start(bf16[256,128]{1,0:T(8,128)(2,1)} %get-tuple-element.71), channel_id=1, source_target_pairs={{0,16},{2,18},{4,20},{6,22},{8,24},{10,26},{12,28},{14,30},{16,0},... | collective-permute-start | bytes 196616 | tf_op jit(solution)/shard_map/ppermute | solution.py:279
  6.6 6.8 %collective-permute-start.1 = (bf16[256,128]{1,0:T(8,128)(2,1)}, bf16[256,128]{1,0:T(8,128)(2,1)S(1)}, u32[]{:S(2)}, u32[]{:S(2)}) collective-permute-start(bf16[256,128]{1,0:T(8,128)(2,1)} %get-tuple-element.72), channel_id=1, source_target_pairs={{0,24},{2,26},{4,28},{6,30},{8,16},{10,18},{12,20},{14,22},{16,8},... | collective-permute-start | bytes 196616 | tf_op jit(solution)/shard_map/ppermute | solution.py:279
  8.0 5.4 %collective-permute-start.2 = (bf16[256,128]{1,0:T(8,128)(2,1)}, bf16[256,128]{1,0:T(8,128)(2,1)S(1)}, u32[]{:S(2)}, u32[]{:S(2)}) collective-permute-start(bf16[256,128]{1,0:T(8,128)(2,1)} %get-tuple-element.73), channel_id=1, source_target_pairs={{0,8},{2,10},{4,12},{6,14},{8,0},{10,2},{12,4},{14,6},{16,24},{18,... | collective-permute-start | bytes 196616 | tf_op jit(solution)/shard_map/ppermute | solution.py:279
  8.2 5.2 %copy-start = (bf16[256,128]{1,0:T(8,128)(2,1)S(1)}, bf16[256,128]{1,0:T(8,128)(2,1)}, u32[]{:S(2)}) copy-start(bf16[256,128]{1,0:T(8,128)(2,1)} %get-tuple-element.70.refs_0_) | copy-start | bytes 196612
  9.2 8.0 %collective-permute-start.3 = (bf16[128,256]{1,0:T(8,128)(2,1)S(1)}, bf16[128,256]{1,0:T(8,128)(2,1)S(1)}, u32[]{:S(2)}, u32[]{:S(2)}) collective-permute-start(bf16[128,256]{1,0:T(8,128)(2,1)S(1)} %get-tuple-element.78), channel_id=1, source_target_pairs={{0,16},{2,18},{4,20},{6,22},{8,24},{10,26},{12,28},{14,30},{16,0},... | collective-permute-start | bytes 196616 | tf_op jit(solution)/shard_map/ppermute | solution.py:279
  12.0 6.2 %collective-permute-start.4 = (bf16[128,256]{1,0:T(8,128)(2,1)S(1)}, bf16[128,256]{1,0:T(8,128)(2,1)S(1)}, u32[]{:S(2)}, u32[]{:S(2)}) collective-permute-start(bf16[128,256]{1,0:T(8,128)(2,1)S(1)} %get-tuple-element.79), channel_id=1, source_target_pairs={{0,24},{2,26},{4,28},{6,30},{8,16},{10,18},{12,20},{14,22},{16,8},... | collective-permute-start | bytes 196616 | tf_op jit(solution)/shard_map/ppermute | solution.py:279
  13.4 5.1 %collective-permute-start.5 = (bf16[128,256]{1,0:T(8,128)(2,1)S(1)}, bf16[128,256]{1,0:T(8,128)(2,1)S(1)}, u32[]{:S(2)}, u32[]{:S(2)}) collective-permute-start(bf16[128,256]{1,0:T(8,128)(2,1)S(1)} %get-tuple-element.80), channel_id=1, source_target_pairs={{0,8},{2,10},{4,12},{6,14},{8,0},{10,2},{12,4},{14,6},{16,24},{18,... | collective-permute-start | bytes 196616 | tf_op jit(solution)/shard_map/ppermute | solution.py:279
  13.4 10.8 %collective-permute-start.7 = (bf16[1024,128]{1,0:T(8,128)(2,1)S(1)}, bf16[1024,128]{1,0:T(8,128)(2,1)S(1)}, u32[]{:S(2)}, u32[]{:S(2)}) collective-permute-start(bf16[1024,128]{1,0:T(8,128)(2,1)S(1)} %shard_map.86.pair_ref), channel_id=1, source_target_pairs={{0,4},{2,6},{4,0},{6,2},{8,12},{10,14},{12,8},{14,10},{16,20},{18,... | collective-permute-start | bytes 786440 | tf_op jit(solution)/shard_map/ppermute | solution.py:279
  15.0 6.2 %collective-permute-start.6 = (bf16[1024,128]{1,0:T(8,128)(2,1)S(1)}, bf16[1024,128]{1,0:T(8,128)(2,1)S(1)}, u32[]{:S(2)}, u32[]{:S(2)}) collective-permute-start(bf16[1024,128]{1,0:T(8,128)(2,1)S(1)} %shard_map.86.pair_ref), channel_id=1, source_target_pairs={{0,2},{2,0},{4,6},{6,4},{8,10},{10,8},{12,14},{14,12},{16,18},{18,... | collective-permute-start | bytes 786440 | tf_op jit(solution)/shard_map/ppermute | solution.py:279
  24.3 3.1 %collective-permute-start.8 = (bf16[1024,128]{1,0:T(8,128)(2,1)S(1)}, bf16[1024,128]{1,0:T(8,128)(2,1)S(1)}, u32[]{:S(2)}, u32[]{:S(2)}) collective-permute-start(bf16[1024,128]{1,0:T(8,128)(2,1)S(1)} %collective-permute-done.7.pair_ref), channel_id=1, source_target_pairs={{0,2},{2,0},{4,6},{6,4},{8,10},{10,8},{12,14},{14,12},{16,18},{18,... | collective-permute-start | bytes 786440 | tf_op jit(solution)/shard_map/ppermute | solution.py:279
  30.7 6.0 %collective-permute-start.9 = (bf16[64,256]{1,0:T(8,128)(2,1)S(1)}, bf16[64,256]{1,0:T(8,128)(2,1)S(1)}, u32[]{:S(2)}, u32[]{:S(2)}) collective-permute-start(bf16[64,256]{1,0:T(8,128)(2,1)S(1)} %get-tuple-element.102), channel_id=1, source_target_pairs={{0,16},{2,18},{4,20},{6,22},{8,24},{10,26},{12,28},{14,30},{16,0},... | collective-permute-start | bytes 98312 | tf_op jit(solution)/shard_map/ppermute | solution.py:279
  33.8 5.7 %collective-permute-start.10 = (bf16[64,256]{1,0:T(8,128)(2,1)S(1)}, bf16[64,256]{1,0:T(8,128)(2,1)S(1)}, u32[]{:S(2)}, u32[]{:S(2)}) collective-permute-start(bf16[64,256]{1,0:T(8,128)(2,1)S(1)} %get-tuple-element.103), channel_id=1, source_target_pairs={{0,24},{2,26},{4,28},{6,30},{8,16},{10,18},{12,20},{14,22},{16,8},... | collective-permute-start | bytes 98312 | tf_op jit(solution)/shard_map/ppermute | solution.py:279
  34.2 5.3 %collective-permute-start.11 = (bf16[64,256]{1,0:T(8,128)(2,1)S(1)}, bf16[64,256]{1,0:T(8,128)(2,1)S(1)}, u32[]{:S(2)}, u32[]{:S(2)}) collective-permute-start(bf16[64,256]{1,0:T(8,128)(2,1)S(1)} %get-tuple-element.104), channel_id=1, source_target_pairs={{0,8},{2,10},{4,12},{6,14},{8,0},{10,2},{12,4},{14,6},{16,24},{18,... | collective-permute-start | bytes 98312 | tf_op jit(solution)/shard_map/ppermute | solution.py:279
  40.5 3.0 %collective-permute-start.13 = (bf16[2,64,768]{2,1,0:T(8,128)(2,1)S(1)}, bf16[2,64,768]{2,1,0:T(8,128)(2,1)S(1)}, u32[]{:S(2)}, u32[]{:S(2)}) collective-permute-start(bf16[2,64,768]{2,1,0:T(8,128)(2,1)S(1)} %get-tuple-element.111.refs_4_), channel_id=1, source_target_pairs={{0,2},{2,0},{4,6},{6,4},{8,10},{10,8},{12,14},{14,12},{16,18},{18,... | collective-permute-start | bytes 589832 | tf_op jit(solution)/shard_map/ppermute | solution.py:279
  40.5 6.8 %collective-permute-start.16 = (bf16[128,1024]{1,0:T(8,128)(2,1)S(1)}, bf16[128,1024]{1,0:T(8,128)(2,1)S(1)}, u32[]{:S(2)}, u32[]{:S(2)}) collective-permute-start(bf16[128,1024]{1,0:T(8,128)(2,1)S(1)} %get-tuple-element.110.refs_4_), channel_id=1, source_target_pairs={{0,2},{2,0},{4,6},{6,4},{8,10},{10,8},{12,14},{14,12},{16,18},{18,... | collective-permute-start | bytes 786440 | tf_op jit(solution)/shard_map/ppermute | solution.py:279
  41.9 11.2 %collective-permute-start.12 = (bf16[256,768]{1,0:T(8,128)(2,1)S(1)}, bf16[256,768]{1,0:T(8,128)(2,1)S(1)}, u32[]{:S(2)}, u32[]{:S(2)}) collective-permute-start(bf16[256,768]{1,0:T(8,128)(2,1)S(1)} %shard_map.99.a_ref._), channel_id=1, source_target_pairs={{0,1},{1,0},{2,3},{3,2},{4,5},{5,4},{6,7},{7,6},{8,9},{9,8},{10,11... | collective-permute-start | bytes 1179656 | tf_op jit(solution)/shard_map/ppermute | solution.py:279
  43.5 4.7 %collective-permute-start.14 = (bf16[64,768]{1,0:T(8,128)(2,1)S(1)}, bf16[64,768]{1,0:T(8,128)(2,1)S(1)}, u32[]{:S(2)}, u32[]{:S(2)}) collective-permute-start(bf16[64,768]{1,0:T(8,128)(2,1)S(1)} %get-tuple-element.126), channel_id=1, source_target_pairs={{0,4},{2,6},{4,0},{6,2},{8,12},{10,14},{12,8},{14,10},{16,20},{18,... | collective-permute-start | bytes 294920 | tf_op jit(solution)/shard_map/ppermute | solution.py:279
  47.4 7.8 %collective-permute-start.17 = (bf16[128,1024]{1,0:T(8,128)(2,1)S(1)}, bf16[128,1024]{1,0:T(8,128)(2,1)S(1)}, u32[]{:S(2)}, u32[]{:S(2)}) collective-permute-start(bf16[128,1024]{1,0:T(8,128)(2,1)S(1)} %shard_map.106), channel_id=1, source_target_pairs={{0,4},{2,6},{4,0},{6,2},{8,12},{10,14},{12,8},{14,10},{16,20},{18,... | collective-permute-start | bytes 786440 | tf_op jit(solution)/shard_map/ppermute | solution.py:279
  48.2 6.2 %collective-permute-start.15 = (bf16[64,768]{1,0:T(8,128)(2,1)S(1)}, bf16[64,768]{1,0:T(8,128)(2,1)S(1)}, u32[]{:S(2)}, u32[]{:S(2)}) collective-permute-start(bf16[64,768]{1,0:T(8,128)(2,1)S(1)} %shard_map.103.refs_1_.a_ref), channel_id=1, source_target_pairs={{0,16},{2,18},{4,20},{6,22},{8,24},{10,26},{12,28},{14,30},{16,0},... | collective-permute-start | bytes 294920 | tf_op jit(solution)/shard_map/ppermute | solution.py:279
  51.5 6.0 %collective-permute-start.18 = (bf16[128,1024]{1,0:T(8,128)(2,1)S(1)}, bf16[128,1024]{1,0:T(8,128)(2,1)S(1)}, u32[]{:S(2)}, u32[]{:S(2)}) collective-permute-start(bf16[128,1024]{1,0:T(8,128)(2,1)S(1)} %get-tuple-element.129.refs_0_), channel_id=1, source_target_pairs={{0,2},{2,0},{4,6},{6,4},{8,10},{10,8},{12,14},{14,12},{16,18},{18,... | collective-permute-start | bytes 786440 | tf_op jit(solution)/shard_map/ppermute | solution.py:279
  58.4 19.3 %all-to-all-start = ((bf16[4,192,256]{2,1,0:T(8,128)(2,1)}), bf16[4,192,256]{2,1,0:T(8,128)(2,1)S(1)}, u32[]{:S(2)}, u32[]{:S(2)}) async-start(bf16[4,192,256]{2,1,0:T(8,128)(2,1)} %shard_map.109.refs_0_), calls=%async_computation | async-start | bytes 786432 | tf_op jit(solution)/shard_map/all_to_all | solution.py:388
  61.9 9.9 %collective-permute-start.19 = (bf16[64,768]{1,0:T(8,128)(2,1)S(1)}, bf16[64,768]{1,0:T(8,128)(2,1)S(1)}, u32[]{:S(2)}, u32[]{:S(2)}) collective-permute-start(bf16[64,768]{1,0:T(8,128)(2,1)S(1)} %shard_map.105.refs_1_.a_ref), channel_id=1, source_target_pairs={{0,8},{2,10},{4,12},{6,14},{8,0},{10,2},{12,4},{14,6},{16,24},{18,... | collective-permute-start | bytes 294920 | tf_op jit(solution)/shard_map/ppermute | solution.py:279
  71.8 4.7 %collective-permute-start.21 = (bf16[64,768]{1,0:T(8,128)(2,1)S(1)}, bf16[64,768]{1,0:T(8,128)(2,1)S(1)}, u32[]{:S(2)}, u32[]{:S(2)}) collective-permute-start(bf16[64,768]{1,0:T(8,128)(2,1)S(1)} %shard_map.110.refs_0_), channel_id=1, source_target_pairs={{0,4},{2,6},{4,0},{6,2},{8,12},{10,14},{12,8},{14,10},{16,20},{18,... | collective-permute-start | bytes 294920 | tf_op jit(solution)/shard_map/ppermute | solution.py:279
  73.2 3.2 %collective-permute-start.20 = (bf16[64,768]{1,0:T(8,128)(2,1)S(1)}, bf16[64,768]{1,0:T(8,128)(2,1)S(1)}, u32[]{:S(2)}, u32[]{:S(2)}) collective-permute-start(bf16[64,768]{1,0:T(8,128)(2,1)S(1)} %shard_map.110.refs_0_), channel_id=1, source_target_pairs={{0,2},{2,0},{4,6},{6,4},{8,10},{10,8},{12,14},{14,12},{16,18},{18,... | collective-permute-start | bytes 294920 | tf_op jit(solution)/shard_map/ppermute | solution.py:279
  76.5 1.3 %collective-permute-start.22 = (bf16[64,768]{1,0:T(8,128)(2,1)S(1)}, bf16[64,768]{1,0:T(8,128)(2,1)S(1)}, u32[]{:S(2)}, u32[]{:S(2)}) collective-permute-start(bf16[64,768]{1,0:T(8,128)(2,1)S(1)} %collective-permute-done.21.refs_2_), channel_id=1, source_target_pairs={{0,2},{2,0},{4,6},{6,4},{8,10},{10,8},{12,14},{14,12},{16,18},{18,... | collective-permute-start | bytes 294920 | tf_op jit(solution)/shard_map/ppermute | solution.py:279

commit v12 on v10

--- a/solution.py
+++ b/solution.py
@@ -48,6 +48,12 @@
     return jnp.concatenate(parts, axis=0) if len(parts) > 1 else parts[0]
 
 
+def live_row(fill_ref, rows):
+    within = lax.broadcasted_iota(jnp.int32, (1, TILE), 1)
+    parts = [jnp.where(within < fill_ref[tile], 1.0, 0.0) for tile in range(rows // TILE)]
+    return jnp.concatenate(parts, axis=1) if len(parts) > 1 else parts[0]
+
+
 def spread(slots):
     return [0] + sorted(range(1, slots), key=lambda mask: (mask < slots // 2, mask))
 
@@ -65,8 +71,8 @@
 
 def pack_qg_kernel(heads, rows, dim, a_of, fill_ref, q_ref, w_ref, go_ref, *refs):
     outs, (held,) = refs[:heads], refs[heads:]
-    mixed = go_ref[...] * live_column(fill_ref, rows).astype(BF16)
-    grads = dot_nt(w_ref[...].reshape(heads * dim, mixed.shape[1]), mixed).astype(BF16)
+    grads = dot_nt(w_ref[...].reshape(heads * dim, go_ref.shape[1]), go_ref[...])
+    grads = (grads * live_row(fill_ref, rows)).astype(BF16)
     for head in range(heads):
         held[head, 0:dim, :] = (q_ref[head].astype(F32) * dim**-0.5).astype(BF16)
         held[head, dim:, :] = grads[head * dim : (head + 1) * dim, :]
@@ -86,8 +92,8 @@
     pieces, (qa_ref, q_ref, g_ref, norm_ref) = refs[:slots], refs[slots:]
     wide = 2 * dim
     row = lax.broadcasted_iota(jnp.int32, (dim, slots * rows), 0)
-    qa_ref[dim:wide, :] = jnp.zeros((dim, slots * rows), BF16)
-    qa_ref[wide : wide + dim, :] = jnp.where(row == 0, 1.0, 0.0).astype(BF16)
+    qa_ref[wide : wide + dim, :] = jnp.zeros((dim, slots * rows), BF16)
+    qa_ref[wide + dim :, :] = jnp.where(row == 0, 1.0, 0.0).astype(BF16)
     for slot in range(slots):
         here = slice(slot * rows, (slot + 1) * rows)
         queries = pieces[slot][0:dim, :]
@@ -96,33 +102,30 @@
         scaled = queries.astype(F32) * LOG2_E
         high = scaled.astype(BF16)
         qa_ref[0:dim, here] = high
-        qa_ref[wide + dim :, here] = (scaled - high.astype(F32)).astype(BF16)
+        qa_ref[dim:wide, here] = (scaled - high.astype(F32)).astype(BF16)
         norm_ref[:, here] = jnp.sum(scaled * scaled, axis=0, keepdims=True)
 
 
-def prep_kernel(dim, pair_ref, *refs):
-    wide_ref, kt_ref, vt_ref, norm_ref = refs[-4:]
+def score_kernel(slots, rows, dim, step, pair_ref, qa_ref, q_norm_ref, *refs):
+    exp_ref, peak_ref, total_ref, v_ref, kt_ref, wide_ref, vt_ref, score_ref = refs[-8:]
     wide = 2 * dim
     keys = pair_ref.shape[0]
-    pair = pair_ref[...]
-    full = pair.astype(F32)
+    full = pair_ref[...].astype(F32)
+    turned = full.T
+    norm = jnp.sum(turned[:dim, :] * turned[:dim, :], axis=0, keepdims=True)
+    norm = jnp.where(turned[0:1, :] >= DEAD, 0.0, norm)
+    small = jnp.max(norm) * jnp.max(q_norm_ref[...]) <= SAFE * SAFE
     lane = lax.broadcasted_iota(jnp.int32, (keys, wide), 1)
-    ones = jnp.where(lane <= 2, 1.0, 0.0)
     bias = jnp.where(full[:, 0:1] >= DEAD, BIAS, 0.0)
-    extra = jnp.where(lane == 0, bias, ones)
-    wide_ref[:, 0:wide] = pair
-    wide_ref[:, wide:] = jnp.where(lane < dim, extra, pltpu.roll(full, dim, 1)).astype(BF16)
-    turned = full.T
+    extra = jnp.where(lane == dim, bias, jnp.where(lane <= dim + 2, 1.0, 0.0))
+    rolled = pltpu.roll(full, dim, 1)
+    values = jnp.where(lane < dim, rolled, extra).astype(BF16)
+    wide_ref[:, 0:wide] = jnp.where(lane < dim, full, rolled).astype(BF16)
+    wide_ref[:, wide:] = values
+    v_ref[...] = values
     kt_ref[...] = turned[:dim, :].astype(BF16)
     vt_ref[0:dim, :] = turned[dim:, :].astype(BF16)
     vt_ref[dim:, :] = jnp.ones((16, keys), BF16)
-    norm = jnp.sum(turned[:dim, :] * turned[:dim, :], axis=0, keepdims=True)
-    norm_ref[...] = jnp.where(turned[0:1, :] >= DEAD, 0.0, norm)
-
-
-def score_kernel(slots, rows, dim, step, wide_ref, vt_ref, norm_ref, qa_ref, q_norm_ref, exp_ref, peak_ref, total_ref, score_ref):
-    keys = wide_ref.shape[0]
-    small = jnp.max(norm_ref[...]) * jnp.max(q_norm_ref[...]) <= SAFE * SAFE
 
     @pl.when(small)
     def _():
@@ -173,28 +176,25 @@
     inner_ref[...] = jnp.sum(g_ref[...].astype(F32) * attended.astype(F32), axis=0, keepdims=True)
 
 
-def back_kernel(slots, rows, dim, first, exp_ref, wide_ref, kt_ref, q_ref, g_ref, factor_ref, inner_ref, *refs):
+def back_kernel(slots, rows, dim, first, exp_ref, v_ref, kt_ref, q_ref, g_ref, factor_ref, inner_ref, *refs):
     dkv_ref, dq_ref, ga_ref = refs[-3:]
-    wide = 2 * dim
     block = g_ref.shape[1]
     factor = factor_ref[...]
     inner = inner_ref[...] * factor
     high = inner.astype(BF16).astype(F32)
     row = lax.broadcasted_iota(jnp.int32, (dim, block), 0)
-    ga_ref[0:dim, :] = jnp.zeros((dim, block), BF16)
-    ga_ref[dim:wide, :] = (g_ref[...].astype(F32) * factor).astype(BF16)
-    ga_ref[wide : wide + dim, :] = jnp.where(row == 1, -high, jnp.where(row == 2, high - inner, 0.0)).astype(BF16)
-    ga_ref[wide + dim :, :] = jnp.zeros((dim, block), BF16)
+    ga_ref[0:dim, :] = (g_ref[...].astype(F32) * factor).astype(BF16)
+    ga_ref[dim:, :] = jnp.where(row == 1, -high, jnp.where(row == 2, high - inner, 0.0)).astype(BF16)
     grad_k = grad_v = None
-    ahead = dot(wide_ref[...], ga_ref[:, 0:rows])
+    ahead = dot(v_ref[...], ga_ref[:, 0:rows])
     for slot in range(slots):
         here = slice(slot * rows, (slot + 1) * rows)
         products = ahead
         if slot + 1 < slots:
-            ahead = dot(wide_ref[...], ga_ref[:, (slot + 1) * rows : (slot + 2) * rows])
+            ahead = dot(v_ref[...], ga_ref[:, (slot + 1) * rows : (slot + 2) * rows])
         exps = exp_ref[:, here]
         grads = exps * products.astype(BF16)
-        term_v = dot_nt(ga_ref[dim:wide, here], exps)
+        term_v = dot_nt(ga_ref[0:dim, here], exps)
         term_k = dot_nt(q_ref[:, here], grads)
         grad_v = term_v if grad_v is None else grad_v + term_v
         grad_k = term_k if grad_k is None else grad_k + term_k
@@ -206,11 +206,11 @@
 
 def project_grad_kernel(slots, rows, a_of, b_of, halves, fill_ref, go_ref, *refs):
     att, refs = refs[:slots], refs[slots + 1 :]
-    mixed = go_ref[...] * live_column(fill_ref, rows).astype(BF16)
     me = a_of()
     held = refs[-1]
     dim = held.shape[1]
-    grads = dot(jnp.concatenate([ref[...] for ref in att], axis=0), mixed).astype(BF16)
+    live = live_row(fill_ref, rows).astype(BF16)
+    grads = dot(jnp.concatenate([ref[...] * live for ref in att], axis=0), go_ref[...]).astype(BF16)
     for slot, mask in enumerate(spread(slots)):
         held[me ^ mask] = grads[slot * dim : (slot + 1) * dim, :]
     if not halves:
@@ -226,9 +226,10 @@
 def project_kernel(slots, rows, a_of, fill_ref, w_ref, *refs):
     att, terms_ref = refs[:slots], refs[-1]
     me = a_of()
-    rows_in = jnp.concatenate([ref[...] for ref in att], axis=0).astype(F32).T.astype(BF16)
+    live = live_row(fill_ref, rows)
+    rows_in = jnp.concatenate([ref[...].astype(F32) * live for ref in att], axis=0).T.astype(BF16)
     weights = jnp.concatenate([w_ref[me ^ mask] for mask in spread(slots)], axis=0)
-    terms_ref[...] = (dot(rows_in, weights) * live_column(fill_ref, rows)).astype(BF16)
+    terms_ref[...] = dot(rows_in, weights).astype(BF16)
 
 
 def add_pairs_kernel(kept_ref, came_ref, _, first_ref, second_ref):
@@ -253,20 +254,17 @@
     refs[-1][...] = (a_ref[...].astype(F32) + b_ref[...].astype(F32)).astype(refs[-1].dtype)
 
 
-def unpack_kernel(slots, rows, dim, a_of, *refs):
-    pieces, (kv_out, q_out) = refs[:slots], refs[-2:]
+def finish_kernel(slots, rows, dim, a_of, b_of, columns, *refs):
+    pieces, parts, (kv_out, q_out, *outs) = refs[:slots], refs[slots : slots + columns], refs[slots + columns :]
     wide = 2 * dim
+    if columns:
+        me = b_of()
+        for column in range(columns):
+            outs[0][me ^ column] = parts[column][...].astype(F32)
     me = a_of()
     for slot, mask in enumerate(spread(slots)):
         kv_out[pl.ds(me ^ mask, rows, stride=slots), :] = pieces[slot][0:wide, :].astype(F32).T
         q_out[me ^ mask] = pieces[slot][wide:, :].astype(F32)
-
-
-def place_kernel(columns, b_of, *refs):
-    parts, (out_ref,) = refs[:columns], refs[columns:]
-    me = b_of()
-    for column in range(columns):
-        out_ref[me ^ column] = parts[column][...].astype(F32)
 
 
 def shards(seq, mp, queries, key_value, tile_fill, out_weight, grad_output):
@@ -312,18 +310,14 @@
         [((2 * wide, block), BF16), ((dim, block), BF16), ((dim, block), BF16), ((1, block), F32)], n_in=slots,
     )(*qg_mine)
     step = min(block, 512)
-    prepared, scored = {}, {}
+    scored = {}
     for r in range(columns):
-        *prepared[r], values, norm = call(
-            functools.partial(prep_kernel, dim),
-            [((block, 2 * wide), BF16), ((dim, block), BF16), ((dim + 16, block), BF16), ((1, block), F32)],
-            after=min(r, 1), micros=2,
-        )(blocks[r], *([scored[r - 1][1]] if r else []))
         scored[r] = call(
             functools.partial(score_kernel, slots, rows, dim, step),
-            [((block, block), BF16), ((1, block), F32), ((dim + 16, block), F32)],
-            [pltpu.VMEM((block, rows), F32)], n_in=5, micros=4,
-        )(prepared[r][0], values, norm, qa, q_norm)
+            [((block, block), BF16), ((1, block), F32), ((dim + 16, block), F32), ((block, wide), BF16), ((dim, block), BF16)],
+            [pltpu.VMEM((block, 2 * wide), BF16), pltpu.VMEM((dim + 16, block), BF16), pltpu.VMEM((block, rows), F32)],
+            n_in=3, after=min(r, 1), micros=5,
+        )(blocks[r], qa, q_norm, *([scored[r - 1][1]] if r else []))
     combined = call(
         functools.partial(combine_kernel, slots, columns, rows, dim),
         [((dim, rows), BF16)] * slots + [((1, block), F32)] * (columns + 1), n_in=2 * columns + 1,
@@ -364,10 +358,10 @@
         if at == 3 and halves:
             kept = add(kept, swap(kept, far_masks[0]), dkv[order[at - 1]])[0]
             later = [kept, summed[2], done]
-        operands = [scored[r][0], *prepared[r], q_all, grads, factors[r], inner] + ([] if dq is None else [dq])
+        operands = [scored[r][0], *scored[r][3:], q_all, grads, factors[r], inner] + ([] if dq is None else [dq])
         dkv[r], dq = call(
             functools.partial(back_kernel, slots, rows, dim, dq is None),
-            [((wide, block), BF16), ((dim, block), F32)], [pltpu.VMEM((2 * wide, block), BF16)],
+            [((wide, block), BF16), ((dim, block), F32)], [pltpu.VMEM((wide, block), BF16)],
             n_in=len(operands), after=len(later), micros=2,
         )(*operands, *later)
         later = []
@@ -391,17 +385,15 @@
         for mask in far_masks[1:]:
             kept = add(kept, swap(kept, mask), pieces[0])[0]
         across = swap(kept, 2)
-        weight_grad = call(
-            functools.partial(place_kernel, columns, b_of), [((heads, dim, width), F32)], n_in=columns, micros=0.5,
-        )(kept, swap(kept, 1), across, swap(across, 1))[0]
+        parts = [kept, swap(kept, 1), across, swap(across, 1)]
     else:
-        weight_grad = lax.psum(weight_terms[0].astype(F32), "seq")
-
-    key_value_grad, query_grad = call(
-        functools.partial(unpack_kernel, slots, rows, dim, a_of),
-        [((rows * heads, wide), F32), ((heads, dim, rows), F32)],
-        n_in=slots, micros=1,
-    )(*returned)
+        parts, weight_grad = [], lax.psum(weight_terms[0].astype(F32), "seq")
+    key_value_grad, query_grad, *outs = call(
+        functools.partial(finish_kernel, slots, rows, dim, a_of, b_of, len(parts)),
+        [((rows * heads, wide), F32), ((heads, dim, rows), F32)] + ([((heads, dim, width), F32)] if parts else []),
+        n_in=slots + len(parts), micros=1,
+    )(*returned, *parts)
+    weight_grad = outs[0] if parts else weight_grad
     return terms, jnp.transpose(query_grad, (2, 0, 1)), key_value_grad.reshape(rows, heads, wide), weight_grad
 
 

time: 71 us -> 74.6 us (1.051)
  waiting for transfers between devices: 14.4 us -> 18.9 us
  Pallas kernels: 29.2 us -> 27.7 us
    ppermute x26, waiting for transfers between devices: 14.4 us -> 18.9 us  [swap(): return lax.ppermute(array, axis, [(i, i ^ mask) for i in range(size)])]
    pallas_call x6 -> x1, Pallas kernels: 3.18 us -> 1.22 us  [shards(): call(functools.partial(finish_kernel, slots, rows, dim, a_of, b_of, len(p...]
    pallas_call x4, Pallas kernels: 10.9 us -> 11.9 us  [shards(): call(functools.partial(score_kernel, slots, rows, dim, step), [((block, b...]
  transfers between devices with their start and end apart: 26 -> 26, of which waited for: 12 -> 11; matrix products, arithmetic and copies ran while one was open for 0% -> 0% of each run, Pallas kernels for 31% -> 28%
where the time goes in v12:
time: 74.6 us; the launch traced here: 74.4 us
  Pallas kernels  27.7 us (37%)
  starting transfers between devices  26.8 us (36%)
  waiting for transfers between devices  18.9 us (25%)
  between operations  0.93 us (1%)
    ppermute x26, starting transfers between devices, swap(): return lax.ppermute(array, axis, [(i, i ^ mask) for i in range(size)])  26.8 us
    ppermute x26, waiting for transfers between devices, swap(): return lax.ppermute(array, axis, [(i, i ^ mask) for i in range(size)])  18.9 us
    pallas_call x4, Pallas kernels, shards(): call(functools.partial(score_kernel, slots, rows, dim, step), [((block, b...  11.9 us
    pallas_call x4, Pallas kernels, shards(): call(functools.partial(back_kernel, slots, rows, dim, dq is None), [((wid...  8.68 us
    pallas_call x1, Pallas kernels, shards(): call(functools.partial(pack_kv_kernel, heads, rows, dim, a_of), [((rows,...  1.9 us
  transfers between devices with their start and end apart: 26, of which 11 were waited for; matrix products, arithmetic and copies ran while one was open for 0% of the time, Pallas kernels for 28%

profile of v12, /device:TPU:0, one launch (start us, length us, event | category | flops | bytes accessed | tf_op | source)
XLA Modules:
  0.0 74.4 jit_solution(5486747562912071948)
XLA Ops:
  0.7 1.9 %shard_map.84 = (bf16[256,128]{1,0:T(8,128)(2,1)}, bf16[256,128]{1,0:T(8,128)(2,1)}, bf16[256,128]{1,0:T(8,128)(2,1)}, bf16[256,128]{1,0:T(8,128)(2,1)}) custom-call(s32[2]{0:T(128)} %fill_ref.7, bf16[1024,128]{1,0:T(8,128)(2,1)} %bitcast.5), custom_call_target="tpu_custom_call" | custom-call | flops 1724999936 | tf_op jit(solution)/shard_map/pallas_call | solution.py:286
  2.6 4.0 %collective-permute-start = (bf16[256,128]{1,0:T(8,128)(2,1)}, bf16[256,128]{1,0:T(8,128)(2,1)S(1)}, u32[]{:S(2)}, u32[]{:S(2)}) collective-permute-start(bf16[256,128]{1,0:T(8,128)(2,1)} %get-tuple-element.67), channel_id=1, source_target_pairs={{0,16},{2,18},{4,20},{6,22},{8,24},{10,26},{12,28},{14,30},{16,0},... | collective-permute-start | bytes 196616 | tf_op jit(solution)/shard_map/ppermute | solution.py:280
  6.6 1.3 %collective-permute-start.1 = (bf16[256,128]{1,0:T(8,128)(2,1)}, bf16[256,128]{1,0:T(8,128)(2,1)S(1)}, u32[]{:S(2)}, u32[]{:S(2)}) collective-permute-start(bf16[256,128]{1,0:T(8,128)(2,1)} %get-tuple-element.68), channel_id=1, source_target_pairs={{0,24},{2,26},{4,28},{6,30},{8,16},{10,18},{12,20},{14,22},{16,8},... | collective-permute-start | bytes 196616 | tf_op jit(solution)/shard_map/ppermute | solution.py:280
  8.0 0.2 collective-permute-start.2
  8.2 0.0 copy-start
  8.2 0.9 %shard_map.85 = (bf16[128,256]{1,0:T(8,128)(2,1)S(1)}, bf16[128,256]{1,0:T(8,128)(2,1)S(1)}, bf16[128,256]{1,0:T(8,128)(2,1)S(1)}, bf16[128,256]{1,0:T(8,128)(2,1)S(1)}) custom-call(s32[2]{0:T(128)S(1)} %copy-done.4, bf16[4,64,256]{2,1,0:T(8,128)(2,1)S(1)} %bitcast.4, bf16[4,64,768]{2,1,0:T(8,128)(2,1)S(1)} %copy-done.2, bf16[256,768]{1,0:T(8,128)(2,1)S(1)} %copy-done.1), custom_call_target="tpu_custom_call" | custom-call | flops 1150000000 | tf_op jit(solution)/shard_map/pallas_call | solution.py:291
  9.1 2.9 %collective-permute-start.3 = (bf16[128,256]{1,0:T(8,128)(2,1)S(1)}, bf16[128,256]{1,0:T(8,128)(2,1)S(1)}, u32[]{:S(2)}, u32[]{:S(2)}) collective-permute-start(bf16[128,256]{1,0:T(8,128)(2,1)S(1)} %get-tuple-element.71), channel_id=1, source_target_pairs={{0,16},{2,18},{4,20},{6,22},{8,24},{10,26},{12,28},{14,30},{16,0},... | collective-permute-start | bytes 196616 | tf_op jit(solution)/shard_map/ppermute | solution.py:280
  12.0 1.3 %collective-permute-start.4 = (bf16[128,256]{1,0:T(8,128)(2,1)S(1)}, bf16[128,256]{1,0:T(8,128)(2,1)S(1)}, u32[]{:S(2)}, u32[]{:S(2)}) collective-permute-start(bf16[128,256]{1,0:T(8,128)(2,1)S(1)} %get-tuple-element.72), channel_id=1, source_target_pairs={{0,24},{2,26},{4,28},{6,30},{8,16},{10,18},{12,20},{14,22},{16,8},... | collective-permute-start | bytes 196616 | tf_op jit(solution)/shard_map/ppermute | solution.py:280
  13.3 0.0 collective-permute-done.refs_1_
  13.3 0.0 collective-permute-start.5
  13.3 0.0 collective-permute-done.2.refs_3_
  13.4 1.6 %collective-permute-start.7 = (bf16[1024,128]{1,0:T(8,128)(2,1)S(1)}, bf16[1024,128]{1,0:T(8,128)(2,1)S(1)}, u32[]{:S(2)}, u32[]{:S(2)}) collective-permute-start(bf16[1024,128]{1,0:T(8,128)(2,1)S(1)} %shard_map.86.pair_ref), channel_id=1, source_target_pairs={{0,4},{2,6},{4,0},{6,2},{8,12},{10,14},{12,8},{14,10},{16,20},{18,... | collective-permute-start | bytes 786440 | tf_op jit(solution)/shard_map/ppermute | solution.py:280
  15.0 2.2 %collective-permute-done.3.refs_1_ = bf16[128,256]{1,0:T(8,128)(2,1)S(1)} collective-permute-done((bf16[128,256]{1,0:T(8,128)(2,1)S(1)}, bf16[128,256]{1,0:T(8,128)(2,1)S(1)}, u32[]{:S(2)}, u32[]{:S(2)}) %collective-permute-start.3) | collective-permute-done | bytes 65568 | tf_op jit(solution)/shard_map/ppermute | solution.py:280
  17.2 1.0 %collective-permute-done.4.refs_2_ = bf16[128,256]{1,0:T(8,128)(2,1)S(1)} collective-permute-done((bf16[128,256]{1,0:T(8,128)(2,1)S(1)}, bf16[128,256]{1,0:T(8,128)(2,1)S(1)}, u32[]{:S(2)}, u32[]{:S(2)}) %collective-permute-start.4) | collective-permute-done | bytes 65568 | tf_op jit(solution)/shard_map/ppermute | solution.py:280
  18.2 0.3 collective-permute-done.5.refs_3_
  18.4 0.1 shard_map.87
  18.6 2.9 %shard_map.88 = (bf16[1024,1024]{1,0:T(8,128)(2,1)S(1)}, f32[1,1024]{1,0:T(1,128)S(1)}, f32[80,1024]{1,0:T(8,128)S(1)}, bf16[1024,128]{1,0:T(8,128)(2,1)S(1)}, bf16[64,1024]{1,0:T(8,128)(2,1)S(1)}) custom-call(bf16[1024,128]{1,0:T(8,128)(2,1)S(1)} %shard_map.86.pair_ref, bf16[256,1024]{1,0:T(8,128)(2,1)S(1)} %get-tuple-element.74.qa_ref, ...), custom_call_target="tpu_custom_call" | custom-call | flops 5750000128 | tf_op jit(solution)/shard_map/pallas_call | solution.py:315
  21.5 0.0 collective-permute-done.7.pair_ref
  21.5 0.1 collective-permute-start.8
  21.6 0.0 collective-permute-done.6.pair_ref
  21.6 2.9 %shard_map.89 = (bf16[1024,1024]{1,0:T(8,128)(2,1)S(1)}, f32[1,1024]{1,0:T(1,128)S(1)}, f32[80,1024]{1,0:T(8,128)S(1)}, bf16[1024,128]{1,0:T(8,128)(2,1)S(1)}, bf16[64,1024]{1,0:T(8,128)(2,1)S(1)}) custom-call(bf16[1024,128]{1,0:T(8,128)(2,1)S(1)} %collective-permute-done.6.pair_ref, bf16[256,1024]{1,0:T(8,128)(2,1)S(1)} %get-tuple-element.74.qa_ref, ...), custom_call_target="tpu_custom_call" | custom-call | flops 5750000128 | tf_op jit(solution)/shard_map/pallas_call | solution.py:315
  24.5 2.9 %shard_map.90 = (bf16[1024,1024]{1,0:T(8,128)(2,1)S(1)}, f32[1,1024]{1,0:T(1,128)S(1)}, f32[80,1024]{1,0:T(8,128)S(1)}, bf16[1024,128]{1,0:T(8,128)(2,1)S(1)}, bf16[64,1024]{1,0:T(8,128)(2,1)S(1)}) custom-call(bf16[1024,128]{1,0:T(8,128)(2,1)S(1)} %collective-permute-done.7.pair_ref, bf16[256,1024]{1,0:T(8,128)(2,1)S(1)} %get-tuple-element.74.qa_ref, ...), custom_call_target="tpu_custom_call" | custom-call | flops 5750000128 | tf_op jit(solution)/shard_map/pallas_call | solution.py:315
  27.5 0.0 collective-permute-done.8.pair_ref
  27.5 3.1 %shard_map.91 = (bf16[1024,1024]{1,0:T(8,128)(2,1)S(1)}, f32[1,1024]{1,0:T(1,128)S(1)}, f32[80,1024]{1,0:T(8,128)S(1)}, bf16[1024,128]{1,0:T(8,128)(2,1)S(1)}, bf16[64,1024]{1,0:T(8,128)(2,1)S(1)}) custom-call(bf16[1024,128]{1,0:T(8,128)(2,1)S(1)} %collective-permute-done.8.pair_ref, bf16[256,1024]{1,0:T(8,128)(2,1)S(1)} %get-tuple-element.74.qa_ref, ...), custom_call_target="tpu_custom_call" | custom-call | flops 5750000128 | tf_op jit(solution)/shard_map/pallas_call | solution.py:315
  30.6 0.2 shard_map.92
  30.8 4.1 %collective-permute-start.9 = (bf16[64,256]{1,0:T(8,128)(2,1)S(1)}, bf16[64,256]{1,0:T(8,128)(2,1)S(1)}, u32[]{:S(2)}, u32[]{:S(2)}) collective-permute-start(bf16[64,256]{1,0:T(8,128)(2,1)S(1)} %get-tuple-element.86), channel_id=1, source_target_pairs={{0,16},{2,18},{4,20},{6,22},{8,24},{10,26},{12,28},{14,30},{16,0},... | collective-permute-start | bytes 98312 | tf_op jit(solution)/shard_map/ppermute | solution.py:280
  34.9 0.2 collective-permute-start.10
  35.1 0.4 collective-permute-start.11
  35.6 2.2 %shard_map.93 = (bf16[128,1024]{1,0:T(8,128)(2,1)S(1)}, f32[64,1024]{1,0:T(8,128)S(1)}) custom-call(bf16[1024,1024]{1,0:T(8,128)(2,1)S(1)} %get-tuple-element.89.exp_ref, bf16[1024,128]{1,0:T(8,128)(2,1)S(1)} %get-tuple-element.90.v_ref, bf16[64,1024]{1,0:T(8,128)(2,1)S(1)} %get-tuple-element.91.kt_ref, bf16[64,1024]{1,0:T(8,128)(2,1)S(1)} %get-tuple-element.92.q_ref, ...), custom_call_target="tpu_custom_call" | custom-call | flops 2300000000 | tf_op jit(solution)/shard_map/pallas_call | solution.py:362
  37.8 0.0 collective-permute-done.9.refs_1_
  37.8 2.9 %collective-permute-done.10.refs_2_ = bf16[64,256]{1,0:T(8,128)(2,1)S(1)} collective-permute-done((bf16[64,256]{1,0:T(8,128)(2,1)S(1)}, bf16[64,256]{1,0:T(8,128)(2,1)S(1)}, u32[]{:S(2)}, u32[]{:S(2)}) %collective-permute-start.10) | collective-permute-done | bytes 32800 | tf_op jit(solution)/shard_map/ppermute | solution.py:280
  40.6 0.0 collective-permute-done.11.refs_3_
  40.6 0.8 %shard_map.94 = (bf16[2,64,768]{2,1,0:T(8,128)(2,1)S(1)}, bf16[2,64,768]{2,1,0:T(8,128)(2,1)S(1)}) custom-call(s32[2]{0:T(128)S(1)} %copy-done.4, bf16[256,768]{1,0:T(8,128)(2,1)S(1)} %copy-done.1, bf16[64,256]{1,0:T(8,128)(2,1)S(1)} %get-tuple-element.85.refs_0_, bf16[64,256]{1,0:T(8,128)(2,1)S(1)} %collective-permute-done.9.refs_1_, ...), custom_call_target="tpu_custom_call" | custom-call | flops 805000000 | tf_op jit(solution)/shard_map/pallas_call | solution.py:335
  41.5 0.1 collective-permute-start.13
  41.6 0.5 collective-permute-start.16
  42.1 0.8 %shard_map.95.a_ref._ = bf16[256,768]{1,0:T(8,128)(2,1)S(1)} custom-call(s32[2]{0:T(128)S(1)} %copy-done.4, bf16[4,64,768]{2,1,0:T(8,128)(2,1)S(1)} %copy-done.2, bf16[64,256]{1,0:T(8,128)(2,1)S(1)} %get-tuple-element.85.refs_0_, bf16[64,256]{1,0:T(8,128)(2,1)S(1)} %collective-permute-done.9.refs_1_, bf16[64,256]{1,0:T(8,128)(2,1)S(1)} %collective-permute-done.10.refs_2_, ...), custom_call_target="tpu_custom_call" | custom-call | flops 805000000 | tf_op jit(solution)/shard_map/pallas_call | solution.py:341
  42.9 1.6 %collective-permute-start.12 = (bf16[256,768]{1,0:T(8,128)(2,1)S(1)}, bf16[256,768]{1,0:T(8,128)(2,1)S(1)}, u32[]{:S(2)}, u32[]{:S(2)}) collective-permute-start(bf16[256,768]{1,0:T(8,128)(2,1)S(1)} %shard_map.95.a_ref._), channel_id=1, source_target_pairs={{0,1},{1,0},{2,3},{3,2},{4,5},{5,4},{6,7},{7,6},{8,9},{9,8},{10,11... | collective-permute-start | bytes 1179656 | tf_op jit(solution)/shard_map/ppermute | solution.py:280
  44.5 1.6 %collective-permute-start.14 = (bf16[64,768]{1,0:T(8,128)(2,1)S(1)}, bf16[64,768]{1,0:T(8,128)(2,1)S(1)}, u32[]{:S(2)}, u32[]{:S(2)}) collective-permute-start(bf16[64,768]{1,0:T(8,128)(2,1)S(1)} %get-tuple-element.114), channel_id=1, source_target_pairs={{0,4},{2,6},{4,0},{6,2},{8,12},{10,14},{12,8},{14,10},{16,20},{18,... | collective-permute-start | bytes 294920 | tf_op jit(solution)/shard_map/ppermute | solution.py:280
  46.1 2.2 %shard_map.98 = (bf16[128,1024]{1,0:T(8,128)(2,1)S(1)}, f32[64,1024]{1,0:T(8,128)S(1)}) custom-call(bf16[1024,1024]{1,0:T(8,128)(2,1)S(1)} %get-tuple-element.106.exp_ref, bf16[1024,128]{1,0:T(8,128)(2,1)S(1)} %get-tuple-element.107.v_ref, bf16[64,1024]{1,0:T(8,128)(2,1)S(1)} %get-tuple-element.108.kt_ref, bf16[64,1024]{1,0:T(8,128)(2,1)S(1)} %get-tuple-element.92.q_ref, ...), custom_call_target="tpu_custom_call" | custom-call | flops 2300000000 | tf_op jit(solution)/shard_map/pallas_call | solution.py:362
  48.3 0.1 shard_map.102
  48.4 0.6 collective-permute-start.17
  49.0 0.3 collective-permute-done.14.b_ref
  49.2 1.0 %collective-permute-start.15 = (bf16[64,768]{1,0:T(8,128)(2,1)S(1)}, bf16[64,768]{1,0:T(8,128)(2,1)S(1)}, u32[]{:S(2)}, u32[]{:S(2)}) collective-permute-start(bf16[64,768]{1,0:T(8,128)(2,1)S(1)} %shard_map.99.refs_1_.a_ref), channel_id=1, source_target_pairs={{0,16},{2,18},{4,20},{6,22},{8,24},{10,26},{12,28},{14,30},{16,0},... | collective-permute-start | bytes 294920 | tf_op jit(solution)/shard_map/ppermute | solution.py:280
  50.2 2.2 %shard_map.100 = (bf16[128,1024]{1,0:T(8,128)(2,1)S(1)}, f32[64,1024]{1,0:T(8,128)S(1)}) custom-call(bf16[1024,1024]{1,0:T(8,128)(2,1)S(1)} %get-tuple-element.102.exp_ref, bf16[1024,128]{1,0:T(8,128)(2,1)S(1)} %get-tuple-element.103.v_ref, bf16[64,1024]{1,0:T(8,128)(2,1)S(1)} %get-tuple-element.104.kt_ref, bf16[64,1024]{1,0:T(8,128)(2,1)S(1)} %get-tuple-element.92.q_ref, ...), custom_call_target="tpu_custom_call" | custom-call | flops 2300000000 | tf_op jit(solution)/shard_map/pallas_call | solution.py:362
  52.4 0.1 collective-permute-start.18
  52.5 1.6 %collective-permute-done.12.b_ref = bf16[256,768]{1,0:T(8,128)(2,1)S(1)} collective-permute-done((bf16[256,768]{1,0:T(8,128)(2,1)S(1)}, bf16[256,768]{1,0:T(8,128)(2,1)S(1)}, u32[]{:S(2)}, u32[]{:S(2)}) %collective-permute-start.12) | collective-permute-done | bytes 393248 | tf_op jit(solution)/shard_map/ppermute | solution.py:280
  54.1 0.8 %shard_map.96 = (bf16[256,768]{1,0:T(8,128)(2,1)}, f32[8,128]{1,0:T(8,128)S(1)}) custom-call(bf16[256,768]{1,0:T(8,128)(2,1)S(1)} %shard_map.95.a_ref._, bf16[256,768]{1,0:T(8,128)(2,1)S(1)} %collective-permute-done.12.b_ref), custom_call_target="tpu_custom_call" | custom-call | flops 11500000 | tf_op jit(solution)/shard_map/pallas_call | solution.py:348
  54.9 0.5 collective-permute-done.15.b_ref
  55.4 0.1 collective-permute-start.22
  55.5 0.7 collective-permute-done.17.refs_2_.came_ref
  56.2 2.2 %shard_map.103 = (bf16[128,1024]{1,0:T(8,128)(2,1)S(1)}, f32[64,1024]{1,0:T(8,128)S(1)}) custom-call(bf16[1024,1024]{1,0:T(8,128)(2,1)S(1)} %get-tuple-element.98.exp_ref, bf16[1024,128]{1,0:T(8,128)(2,1)S(1)} %get-tuple-element.99.v_ref, bf16[64,1024]{1,0:T(8,128)(2,1)S(1)} %get-tuple-element.100.kt_ref, bf16[64,1024]{1,0:T(8,128)(2,1)S(1)} %get-tuple-element.92.q_ref, ...), custom_call_target="tpu_custom_call" | custom-call | flops 2300000000 | tf_op jit(solution)/shard_map/pallas_call | solution.py:362
  58.3 0.0 collective-permute-done.18.b_ref
  58.4 0.1 shard_map.104.kept_ref
  58.4 0.1 shard_map.105
  58.5 1.6 %collective-permute-done.22.b_ref = bf16[64,768]{1,0:T(8,128)(2,1)S(1)} collective-permute-done((bf16[64,768]{1,0:T(8,128)(2,1)S(1)}, bf16[64,768]{1,0:T(8,128)(2,1)S(1)}, u32[]{:S(2)}, u32[]{:S(2)}) %collective-permute-start.22) | collective-permute-done | bytes 98336 | tf_op jit(solution)/shard_map/ppermute | solution.py:280
  60.1 1.6 %collective-permute-start.24 = (bf16[64,768]{1,0:T(8,128)(2,1)S(1)}, bf16[64,768]{1,0:T(8,128)(2,1)S(1)}, u32[]{:S(2)}, u32[]{:S(2)}) collective-permute-start(bf16[64,768]{1,0:T(8,128)(2,1)S(1)} %shard_map.106.refs_4_), channel_id=1, source_target_pairs={{0,4},{2,6},{4,0},{6,2},{8,12},{10,14},{12,8},{14,10},{16,20},{18,... | collective-permute-start | bytes 294920 | tf_op jit(solution)/shard_map/ppermute | solution.py:280
  61.7 1.0 %collective-permute-start.19 = (bf16[192,256]{1,0:T(8,128)(2,1)S(1)}, bf16[192,256]{1,0:T(8,128)(2,1)S(1)}, u32[]{:S(2)}, u32[]{:S(2)}) collective-permute-start(bf16[192,256]{1,0:T(8,128)(2,1)S(1)} %get-tuple-element.122), channel_id=1, source_target_pairs={{0,16},{2,18},{4,20},{6,22},{8,24},{10,26},{12,28},{14,30},{16,0},... | collective-permute-start | bytes 294920 | tf_op jit(solution)/shard_map/ppermute | solution.py:280
  62.7 1.6 %collective-permute-start.20 = (bf16[192,256]{1,0:T(8,128)(2,1)S(1)}, bf16[192,256]{1,0:T(8,128)(2,1)S(1)}, u32[]{:S(2)}, u32[]{:S(2)}) collective-permute-start(bf16[192,256]{1,0:T(8,128)(2,1)S(1)} %get-tuple-element.123), channel_id=1, source_target_pairs={{0,24},{2,26},{4,28},{6,30},{8,16},{10,18},{12,20},{14,22},{16,8},... | collective-permute-start | bytes 294920 | tf_op jit(solution)/shard_map/ppermute | solution.py:280
  64.3 0.9 %collective-permute-start.21 = (bf16[192,256]{1,0:T(8,128)(2,1)S(1)}, bf16[192,256]{1,0:T(8,128)(2,1)S(1)}, u32[]{:S(2)}, u32[]{:S(2)}) collective-permute-start(bf16[192,256]{1,0:T(8,128)(2,1)S(1)} %get-tuple-element.124), channel_id=1, source_target_pairs={{0,8},{2,10},{4,12},{6,14},{8,0},{10,2},{12,4},{14,6},{16,24},{18,... | collective-permute-start | bytes 294920 | tf_op jit(solution)/shard_map/ppermute | solution.py:280
  65.2 0.0 collective-permute-done.24.refs_6_
  65.2 0.0 collective-permute-start.25
  65.2 6.7 %collective-permute-done.19.refs_1_ = bf16[192,256]{1,0:T(8,128)(2,1)S(1)} collective-permute-done((bf16[192,256]{1,0:T(8,128)(2,1)S(1)}, bf16[192,256]{1,0:T(8,128)(2,1)S(1)}, u32[]{:S(2)}, u32[]{:S(2)}) %collective-permute-start.19) | collective-permute-done | bytes 98336 | tf_op jit(solution)/shard_map/ppermute | solution.py:280
  71.9 1.3 %collective-permute-done.21.refs_3_ = bf16[192,256]{1,0:T(8,128)(2,1)S(1)} collective-permute-done((bf16[192,256]{1,0:T(8,128)(2,1)S(1)}, bf16[192,256]{1,0:T(8,128)(2,1)S(1)}, u32[]{:S(2)}, u32[]{:S(2)}) %collective-permute-start.21) | collective-permute-done | bytes 98336 | tf_op jit(solution)/shard_map/ppermute | solution.py:280
  73.2 1.2 %shard_map.107 = (f32[1024,128]{1,0:T(8,128)}, f32[4,64,256]{2,1,0:T(8,128)}, f32[4,64,768]{2,1,0:T(8,128)}) custom-call(bf16[192,256]{1,0:T(8,128)(2,1)S(1)} %get-tuple-element.121.refs_0_, bf16[192,256]{1,0:T(8,128)(2,1)S(1)} %collective-permute-done.19.refs_1_, bf16[192,256]{1,0:T(8,128)(2,1)S(1)} %collective-permute-done.20.refs_2_, ...), custom_call_target="tpu_custom_call" | custom-call | flops 1150000000 | tf_op jit(solution)/shard_map/pallas_call | solution.py:391
  (22 shorter events, 0.2 us)
Async XLA Ops:
  0.6 7.6 %copy-start.1 = (bf16[256,768]{1,0:T(8,128)(2,1)S(1)}, bf16[256,768]{1,0:T(8,128)(2,1)}, u32[]{:S(2)}) copy-start(bf16[256,768]{1,0:T(8,128)(2,1)} %go_ref.3) | copy-start | bytes 1179652
  0.6 7.6 %copy-start.2 = (bf16[4,64,768]{2,1,0:T(8,128)(2,1)S(1)}, bf16[4,64,768]{2,1,0:T(8,128)(2,1)}, u32[]{:S(2)}) copy-start(bf16[4,64,768]{2,1,0:T(8,128)(2,1)} %w_ref.3) | copy-start | bytes 1179652
  0.7 7.5 %copy-start.3 = (bf16[256,4,64]{0,2,1:T(8,128)(2,1)S(1)}, bf16[256,4,64]{0,2,1:T(8,128)(2,1)}, u32[]{:S(2)}) copy-start(bf16[256,4,64]{0,2,1:T(8,128)(2,1)} %param.5) | copy-start | bytes 393220
  0.7 7.5 %copy-start.4 = (s32[2]{0:T(128)S(1)}, s32[2]{0:T(128)}, u32[]{:S(2)}) copy-start(s32[2]{0:T(128)} %fill_ref.7) | copy-start | bytes 28
  2.6 10.7 %collective-permute-start = (bf16[256,128]{1,0:T(8,128)(2,1)}, bf16[256,128]{1,0:T(8,128)(2,1)S(1)}, u32[]{:S(2)}, u32[]{:S(2)}) collective-permute-start(bf16[256,128]{1,0:T(8,128)(2,1)} %get-tuple-element.67), channel_id=1, source_target_pairs={{0,16},{2,18},{4,20},{6,22},{8,24},{10,26},{12,28},{14,30},{16,0},... | collective-permute-start | bytes 196616 | tf_op jit(solution)/shard_map/ppermute | solution.py:280
  6.6 6.7 %collective-permute-start.1 = (bf16[256,128]{1,0:T(8,128)(2,1)}, bf16[256,128]{1,0:T(8,128)(2,1)S(1)}, u32[]{:S(2)}, u32[]{:S(2)}) collective-permute-start(bf16[256,128]{1,0:T(8,128)(2,1)} %get-tuple-element.68), channel_id=1, source_target_pairs={{0,24},{2,26},{4,28},{6,30},{8,16},{10,18},{12,20},{14,22},{16,8},... | collective-permute-start | bytes 196616 | tf_op jit(solution)/shard_map/ppermute | solution.py:280
  8.0 5.4 %collective-permute-start.2 = (bf16[256,128]{1,0:T(8,128)(2,1)}, bf16[256,128]{1,0:T(8,128)(2,1)S(1)}, u32[]{:S(2)}, u32[]{:S(2)}) collective-permute-start(bf16[256,128]{1,0:T(8,128)(2,1)} %get-tuple-element.69), channel_id=1, source_target_pairs={{0,8},{2,10},{4,12},{6,14},{8,0},{10,2},{12,4},{14,6},{16,24},{18,... | collective-permute-start | bytes 196616 | tf_op jit(solution)/shard_map/ppermute | solution.py:280
  8.2 5.1 %copy-start = (bf16[256,128]{1,0:T(8,128)(2,1)S(1)}, bf16[256,128]{1,0:T(8,128)(2,1)}, u32[]{:S(2)}) copy-start(bf16[256,128]{1,0:T(8,128)(2,1)} %get-tuple-element.66.refs_0_) | copy-start | bytes 196612
  9.1 8.1 %collective-permute-start.3 = (bf16[128,256]{1,0:T(8,128)(2,1)S(1)}, bf16[128,256]{1,0:T(8,128)(2,1)S(1)}, u32[]{:S(2)}, u32[]{:S(2)}) collective-permute-start(bf16[128,256]{1,0:T(8,128)(2,1)S(1)} %get-tuple-element.71), channel_id=1, source_target_pairs={{0,16},{2,18},{4,20},{6,22},{8,24},{10,26},{12,28},{14,30},{16,0},... | collective-permute-start | bytes 196616 | tf_op jit(solution)/shard_map/ppermute | solution.py:280
  12.0 6.2 %collective-permute-start.4 = (bf16[128,256]{1,0:T(8,128)(2,1)S(1)}, bf16[128,256]{1,0:T(8,128)(2,1)S(1)}, u32[]{:S(2)}, u32[]{:S(2)}) collective-permute-start(bf16[128,256]{1,0:T(8,128)(2,1)S(1)} %get-tuple-element.72), channel_id=1, source_target_pairs={{0,24},{2,26},{4,28},{6,30},{8,16},{10,18},{12,20},{14,22},{16,8},... | collective-permute-start | bytes 196616 | tf_op jit(solution)/shard_map/ppermute | solution.py:280
  13.3 5.1 %collective-permute-start.5 = (bf16[128,256]{1,0:T(8,128)(2,1)S(1)}, bf16[128,256]{1,0:T(8,128)(2,1)S(1)}, u32[]{:S(2)}, u32[]{:S(2)}) collective-permute-start(bf16[128,256]{1,0:T(8,128)(2,1)S(1)} %get-tuple-element.73), channel_id=1, source_target_pairs={{0,8},{2,10},{4,12},{6,14},{8,0},{10,2},{12,4},{14,6},{16,24},{18,... | collective-permute-start | bytes 196616 | tf_op jit(solution)/shard_map/ppermute | solution.py:280
  13.4 8.1 %collective-permute-start.7 = (bf16[1024,128]{1,0:T(8,128)(2,1)S(1)}, bf16[1024,128]{1,0:T(8,128)(2,1)S(1)}, u32[]{:S(2)}, u32[]{:S(2)}) collective-permute-start(bf16[1024,128]{1,0:T(8,128)(2,1)S(1)} %shard_map.86.pair_ref), channel_id=1, source_target_pairs={{0,4},{2,6},{4,0},{6,2},{8,12},{10,14},{12,8},{14,10},{16,20},{18,... | collective-permute-start | bytes 786440 | tf_op jit(solution)/shard_map/ppermute | solution.py:280
  14.9 6.6 %collective-permute-start.6 = (bf16[1024,128]{1,0:T(8,128)(2,1)S(1)}, bf16[1024,128]{1,0:T(8,128)(2,1)S(1)}, u32[]{:S(2)}, u32[]{:S(2)}) collective-permute-start(bf16[1024,128]{1,0:T(8,128)(2,1)S(1)} %shard_map.86.pair_ref), channel_id=1, source_target_pairs={{0,2},{2,0},{4,6},{6,4},{8,10},{10,8},{12,14},{14,12},{16,18},{18,... | collective-permute-start | bytes 786440 | tf_op jit(solution)/shard_map/ppermute | solution.py:280
  21.5 6.0 %collective-permute-start.8 = (bf16[1024,128]{1,0:T(8,128)(2,1)S(1)}, bf16[1024,128]{1,0:T(8,128)(2,1)S(1)}, u32[]{:S(2)}, u32[]{:S(2)}) collective-permute-start(bf16[1024,128]{1,0:T(8,128)(2,1)S(1)} %collective-permute-done.7.pair_ref), channel_id=1, source_target_pairs={{0,2},{2,0},{4,6},{6,4},{8,10},{10,8},{12,14},{14,12},{16,18},{18,... | collective-permute-start | bytes 786440 | tf_op jit(solution)/shard_map/ppermute | solution.py:280
  30.8 7.0 %collective-permute-start.9 = (bf16[64,256]{1,0:T(8,128)(2,1)S(1)}, bf16[64,256]{1,0:T(8,128)(2,1)S(1)}, u32[]{:S(2)}, u32[]{:S(2)}) collective-permute-start(bf16[64,256]{1,0:T(8,128)(2,1)S(1)} %get-tuple-element.86), channel_id=1, source_target_pairs={{0,16},{2,18},{4,20},{6,22},{8,24},{10,26},{12,28},{14,30},{16,0},... | collective-permute-start | bytes 98312 | tf_op jit(solution)/shard_map/ppermute | solution.py:280
  34.9 5.7 %collective-permute-start.10 = (bf16[64,256]{1,0:T(8,128)(2,1)S(1)}, bf16[64,256]{1,0:T(8,128)(2,1)S(1)}, u32[]{:S(2)}, u32[]{:S(2)}) collective-permute-start(bf16[64,256]{1,0:T(8,128)(2,1)S(1)} %get-tuple-element.87), channel_id=1, source_target_pairs={{0,24},{2,26},{4,28},{6,30},{8,16},{10,18},{12,20},{14,22},{16,8},... | collective-permute-start | bytes 98312 | tf_op jit(solution)/shard_map/ppermute | solution.py:280
  35.1 5.5 %collective-permute-start.11 = (bf16[64,256]{1,0:T(8,128)(2,1)S(1)}, bf16[64,256]{1,0:T(8,128)(2,1)S(1)}, u32[]{:S(2)}, u32[]{:S(2)}) collective-permute-start(bf16[64,256]{1,0:T(8,128)(2,1)S(1)} %get-tuple-element.88), channel_id=1, source_target_pairs={{0,8},{2,10},{4,12},{6,14},{8,0},{10,2},{12,4},{14,6},{16,24},{18,... | collective-permute-start | bytes 98312 | tf_op jit(solution)/shard_map/ppermute | solution.py:280
  41.5 3.0 %collective-permute-start.13 = (bf16[2,64,768]{2,1,0:T(8,128)(2,1)S(1)}, bf16[2,64,768]{2,1,0:T(8,128)(2,1)S(1)}, u32[]{:S(2)}, u32[]{:S(2)}) collective-permute-start(bf16[2,64,768]{2,1,0:T(8,128)(2,1)S(1)} %get-tuple-element.96.refs_4_), channel_id=1, source_target_pairs={{0,2},{2,0},{4,6},{6,4},{8,10},{10,8},{12,14},{14,12},{16,18},{18,... | collective-permute-start | bytes 589832 | tf_op jit(solution)/shard_map/ppermute | solution.py:280
  41.6 6.7 %collective-permute-start.16 = (bf16[128,1024]{1,0:T(8,128)(2,1)S(1)}, bf16[128,1024]{1,0:T(8,128)(2,1)S(1)}, u32[]{:S(2)}, u32[]{:S(2)}) collective-permute-start(bf16[128,1024]{1,0:T(8,128)(2,1)S(1)} %get-tuple-element.95.refs_4_), channel_id=1, source_target_pairs={{0,2},{2,0},{4,6},{6,4},{8,10},{10,8},{12,14},{14,12},{16,18},{18,... | collective-permute-start | bytes 786440 | tf_op jit(solution)/shard_map/ppermute | solution.py:280
  42.9 11.2 %collective-permute-start.12 = (bf16[256,768]{1,0:T(8,128)(2,1)S(1)}, bf16[256,768]{1,0:T(8,128)(2,1)S(1)}, u32[]{:S(2)}, u32[]{:S(2)}) collective-permute-start(bf16[256,768]{1,0:T(8,128)(2,1)S(1)} %shard_map.95.a_ref._), channel_id=1, source_target_pairs={{0,1},{1,0},{2,3},{3,2},{4,5},{5,4},{6,7},{7,6},{8,9},{9,8},{10,11... | collective-permute-start | bytes 1179656 | tf_op jit(solution)/shard_map/ppermute | solution.py:280
  44.5 4.7 %collective-permute-start.14 = (bf16[64,768]{1,0:T(8,128)(2,1)S(1)}, bf16[64,768]{1,0:T(8,128)(2,1)S(1)}, u32[]{:S(2)}, u32[]{:S(2)}) collective-permute-start(bf16[64,768]{1,0:T(8,128)(2,1)S(1)} %get-tuple-element.114), channel_id=1, source_target_pairs={{0,4},{2,6},{4,0},{6,2},{8,12},{10,14},{12,8},{14,10},{16,20},{18,... | collective-permute-start | bytes 294920 | tf_op jit(solution)/shard_map/ppermute | solution.py:280
  48.4 7.8 %collective-permute-start.17 = (bf16[128,1024]{1,0:T(8,128)(2,1)S(1)}, bf16[128,1024]{1,0:T(8,128)(2,1)S(1)}, u32[]{:S(2)}, u32[]{:S(2)}) collective-permute-start(bf16[128,1024]{1,0:T(8,128)(2,1)S(1)} %shard_map.102), channel_id=1, source_target_pairs={{0,4},{2,6},{4,0},{6,2},{8,12},{10,14},{12,8},{14,10},{16,20},{18,... | collective-permute-start | bytes 786440 | tf_op jit(solution)/shard_map/ppermute | solution.py:280
  49.2 6.1 %collective-permute-start.15 = (bf16[64,768]{1,0:T(8,128)(2,1)S(1)}, bf16[64,768]{1,0:T(8,128)(2,1)S(1)}, u32[]{:S(2)}, u32[]{:S(2)}) collective-permute-start(bf16[64,768]{1,0:T(8,128)(2,1)S(1)} %shard_map.99.refs_1_.a_ref), channel_id=1, source_target_pairs={{0,16},{2,18},{4,20},{6,22},{8,24},{10,26},{12,28},{14,30},{16,0},... | collective-permute-start | bytes 294920 | tf_op jit(solution)/shard_map/ppermute | solution.py:280
  52.4 5.9 %collective-permute-start.18 = (bf16[128,1024]{1,0:T(8,128)(2,1)S(1)}, bf16[128,1024]{1,0:T(8,128)(2,1)S(1)}, u32[]{:S(2)}, u32[]{:S(2)}) collective-permute-start(bf16[128,1024]{1,0:T(8,128)(2,1)S(1)} %get-tuple-element.117.refs_0_), channel_id=1, source_target_pairs={{0,2},{2,0},{4,6},{6,4},{8,10},{10,8},{12,14},{14,12},{16,18},{18,... | collective-permute-start | bytes 786440 | tf_op jit(solution)/shard_map/ppermute | solution.py:280
  55.4 4.7 %collective-permute-start.22 = (bf16[64,768]{1,0:T(8,128)(2,1)S(1)}, bf16[64,768]{1,0:T(8,128)(2,1)S(1)}, u32[]{:S(2)}, u32[]{:S(2)}) collective-permute-start(bf16[64,768]{1,0:T(8,128)(2,1)S(1)} %shard_map.101.refs_1_.a_ref), channel_id=1, source_target_pairs={{0,8},{2,10},{4,12},{6,14},{8,0},{10,2},{12,4},{14,6},{16,24},{18,... | collective-permute-start | bytes 294920 | tf_op jit(solution)/shard_map/ppermute | solution.py:280
  60.1 5.1 %collective-permute-start.24 = (bf16[64,768]{1,0:T(8,128)(2,1)S(1)}, bf16[64,768]{1,0:T(8,128)(2,1)S(1)}, u32[]{:S(2)}, u32[]{:S(2)}) collective-permute-start(bf16[64,768]{1,0:T(8,128)(2,1)S(1)} %shard_map.106.refs_4_), channel_id=1, source_target_pairs={{0,4},{2,6},{4,0},{6,2},{8,12},{10,14},{12,8},{14,10},{16,20},{18,... | collective-permute-start | bytes 294920 | tf_op jit(solution)/shard_map/ppermute | solution.py:280
  61.7 11.5 %collective-permute-start.23 = (bf16[64,768]{1,0:T(8,128)(2,1)S(1)}, bf16[64,768]{1,0:T(8,128)(2,1)S(1)}, u32[]{:S(2)}, u32[]{:S(2)}) collective-permute-start(bf16[64,768]{1,0:T(8,128)(2,1)S(1)} %shard_map.106.refs_4_), channel_id=1, source_target_pairs={{0,2},{2,0},{4,6},{6,4},{8,10},{10,8},{12,14},{14,12},{16,18},{18,... | collective-permute-start | bytes 294920 | tf_op jit(solution)/shard_map/ppermute | solution.py:280
  61.7 10.2 %collective-permute-start.19 = (bf16[192,256]{1,0:T(8,128)(2,1)S(1)}, bf16[192,256]{1,0:T(8,128)(2,1)S(1)}, u32[]{:S(2)}, u32[]{:S(2)}) collective-permute-start(bf16[192,256]{1,0:T(8,128)(2,1)S(1)} %get-tuple-element.122), channel_id=1, source_target_pairs={{0,16},{2,18},{4,20},{6,22},{8,24},{10,26},{12,28},{14,30},{16,0},... | collective-permute-start | bytes 294920 | tf_op jit(solution)/shard_map/ppermute | solution.py:280
  62.7 9.2 %collective-permute-start.20 = (bf16[192,256]{1,0:T(8,128)(2,1)S(1)}, bf16[192,256]{1,0:T(8,128)(2,1)S(1)}, u32[]{:S(2)}, u32[]{:S(2)}) collective-permute-start(bf16[192,256]{1,0:T(8,128)(2,1)S(1)} %get-tuple-element.123), channel_id=1, source_target_pairs={{0,24},{2,26},{4,28},{6,30},{8,16},{10,18},{12,20},{14,22},{16,8},... | collective-permute-start | bytes 294920 | tf_op jit(solution)/shard_map/ppermute | solution.py:280
  64.3 8.9 %collective-permute-start.21 = (bf16[192,256]{1,0:T(8,128)(2,1)S(1)}, bf16[192,256]{1,0:T(8,128)(2,1)S(1)}, u32[]{:S(2)}, u32[]{:S(2)}) collective-permute-start(bf16[192,256]{1,0:T(8,128)(2,1)S(1)} %get-tuple-element.124), channel_id=1, source_target_pairs={{0,8},{2,10},{4,12},{6,14},{8,0},{10,2},{12,4},{14,6},{16,24},{18,... | collective-permute-start | bytes 294920 | tf_op jit(solution)/shard_map/ppermute | solution.py:280
  65.2 8.0 %collective-permute-start.25 = (bf16[64,768]{1,0:T(8,128)(2,1)S(1)}, bf16[64,768]{1,0:T(8,128)(2,1)S(1)}, u32[]{:S(2)}, u32[]{:S(2)}) collective-permute-start(bf16[64,768]{1,0:T(8,128)(2,1)S(1)} %collective-permute-done.24.refs_6_), channel_id=1, source_target_pairs={{0,2},{2,0},{4,6},{6,4},{8,10},{10,8},{12,14},{14,12},{16,18},{18,... | collective-permute-start | bytes 294920 | tf_op jit(solution)/shard_map/ppermute | solution.py:280

commit v13 on v12

--- a/solution.py
+++ b/solution.py
@@ -245,26 +245,25 @@
         outs[slot][wide:, :] = (dq_ref[:, here] * dim**-0.5).astype(BF16)
 
 
-def add_out_kernel(a_ref, b_ref, out_ref, done_ref):
-    out_ref[...] = (a_ref[...].astype(F32) + b_ref[...].astype(F32)).astype(out_ref.dtype)
-    done_ref[...] = jnp.zeros_like(done_ref)
-
-
 def add_kernel(a_ref, b_ref, *refs):
     refs[-1][...] = (a_ref[...].astype(F32) + b_ref[...].astype(F32)).astype(refs[-1].dtype)
 
 
-def finish_kernel(slots, rows, dim, a_of, b_of, columns, *refs):
-    pieces, parts, (kv_out, q_out, *outs) = refs[:slots], refs[slots : slots + columns], refs[slots + columns :]
+def unpack_kernel(slots, rows, dim, a_of, *refs):
+    pieces, (kv_out, q_out) = refs[:slots], refs[slots:]
     wide = 2 * dim
-    if columns:
-        me = b_of()
-        for column in range(columns):
-            outs[0][me ^ column] = parts[column][...].astype(F32)
     me = a_of()
     for slot, mask in enumerate(spread(slots)):
         kv_out[pl.ds(me ^ mask, rows, stride=slots), :] = pieces[slot][0:wide, :].astype(F32).T
         q_out[me ^ mask] = pieces[slot][wide:, :].astype(F32)
+
+
+def place_kernel(columns, b_of, *refs):
+    parts, (a_ref, b_ref), (sum_out, grad_out) = refs[:columns], refs[columns : columns + 2], refs[columns + 2 :]
+    sum_out[...] = (a_ref[...].astype(F32) + b_ref[...].astype(F32)).astype(BF16)
+    me = b_of()
+    for column in range(columns):
+        grad_out[me ^ column] = parts[column][...].astype(F32)
 
 
 def shards(seq, mp, queries, key_value, tile_fill, out_weight, grad_output):
@@ -298,20 +297,22 @@
         functools.partial(join_kernel, slots), [((block, wide), BF16)], n_in=slots, after=1,
     )(*kv_mine, qg_send[0])[0]
 
-    blocks = {0: own}
+    qa, q_all, grads, q_norm = call(
+        functools.partial(join_q_kernel, slots, rows, dim),
+        [((2 * wide, block), BF16), ((dim, block), BF16), ((dim, block), BF16), ((1, block), F32)], n_in=slots,
+    )(*qg_mine)
+    step = min(block, 512)
+    scored, blocks = {}, {0: own}
     bit = columns // 2
     while bit:
         for r in sorted(blocks):
             blocks[r ^ bit] = swap(blocks[r], bit)
         bit //= 2
-
-    qa, q_all, grads, q_norm = call(
-        functools.partial(join_q_kernel, slots, rows, dim),
-        [((2 * wide, block), BF16), ((dim, block), BF16), ((dim, block), BF16), ((1, block), F32)], n_in=slots,
-    )(*qg_mine)
-    step = min(block, 512)
-    scored = {}
     for r in range(columns):
+        if r == 2 and columns == 4:
+            blocks[2] = call(functools.partial(join_kernel, 1), [((block, wide), BF16)], after=1)(
+                blocks[2], scored[1][1])[0]
+            blocks[3] = swap(blocks[2], 1)
         scored[r] = call(
             functools.partial(score_kernel, slots, rows, dim, step),
             [((block, block), BF16), ((1, block), F32), ((dim + 16, block), F32), ((block, wide), BF16), ((dim, block), BF16)],
@@ -342,12 +343,11 @@
                 functools.partial(project_kernel, slots, rows, a_of), [((rows, width), BF16)],
                 n_in=2 + slots, smem_first=True, after=1, micros=0.7,
             )(tile_fill, out_weight, *att_mine, weight_terms[-1])[0]
-            later, bit, done = [terms], 1, terms
-            first_terms = terms
-            while bit < mp:
-                terms, done = call(add_out_kernel, [((rows, width), BF16), ((8, 128), F32)], n_in=2)(
-                    terms, swap(terms, bit, "mp", mp))
+            later, bit, first_terms = [terms], 1, terms
+            while bit < mp // 2:
+                terms = call(add_kernel, [((rows, width), BF16)], n_in=2)(terms, swap(terms, bit, "mp", mp))[0]
                 bit *= 2
+            terms_came = swap(terms, bit, "mp", mp)
             if halves:
                 kept, sent = call(add_pairs_kernel, [((dim, width), BF16)] * 2, n_in=2, after=1)(
                     weight_terms[0], swap(weight_terms[1], 1), first_terms)
@@ -357,7 +357,7 @@
             later = [kept]
         if at == 3 and halves:
             kept = add(kept, swap(kept, far_masks[0]), dkv[order[at - 1]])[0]
-            later = [kept, summed[2], done]
+            later = [kept, summed[2], terms_came]
         operands = [scored[r][0], *scored[r][3:], q_all, grads, factors[r], inner] + ([] if dq is None else [dq])
         dkv[r], dq = call(
             functools.partial(back_kernel, slots, rows, dim, dq is None),
@@ -385,16 +385,18 @@
         for mask in far_masks[1:]:
             kept = add(kept, swap(kept, mask), pieces[0])[0]
         across = swap(kept, 2)
-        parts = [kept, swap(kept, 1), across, swap(across, 1)]
+        attention_out, weight_grad = call(
+            functools.partial(place_kernel, columns, b_of),
+            [((rows, width), BF16), ((heads, dim, width), F32)], n_in=columns + 2, micros=0.5,
+        )(kept, swap(kept, 1), across, swap(across, 1), terms, terms_came)
     else:
-        parts, weight_grad = [], lax.psum(weight_terms[0].astype(F32), "seq")
-    key_value_grad, query_grad, *outs = call(
-        functools.partial(finish_kernel, slots, rows, dim, a_of, b_of, len(parts)),
-        [((rows * heads, wide), F32), ((heads, dim, rows), F32)] + ([((heads, dim, width), F32)] if parts else []),
-        n_in=slots + len(parts), micros=1,
-    )(*returned, *parts)
-    weight_grad = outs[0] if parts else weight_grad
-    return terms, jnp.transpose(query_grad, (2, 0, 1)), key_value_grad.reshape(rows, heads, wide), weight_grad
+        attention_out = call(add_kernel, [((rows, width), BF16)], n_in=2)(terms, terms_came)[0]
+        weight_grad = lax.psum(weight_terms[0].astype(F32), "seq")
+    key_value_grad, query_grad = call(
+        functools.partial(unpack_kernel, slots, rows, dim, a_of),
+        [((rows * heads, wide), F32), ((heads, dim, rows), F32)], n_in=slots, micros=1,
+    )(*returned)
+    return attention_out, jnp.transpose(query_grad, (2, 0, 1)), key_value_grad.reshape(rows, heads, wide), weight_grad
 
 
 def solution(mesh):

time: 74.6 us -> 71 us (0.952)
  waiting for transfers between devices: 18.9 us -> 15.9 us
    ppermute x26, waiting for transfers between devices: 18.9 us -> 15.9 us  [swap(): return lax.ppermute(array, axis, [(i, i ^ mask) for i in range(size)])]
    pallas_call x2 -> x3, Pallas kernels: 2.06 us -> 2.13 us  [the longest x1 1.15 us: shards(): call(functools.partial(place_kernel, columns, b_of), [((rows, width), BF1...]
  transfers between devices with their start and end apart: 26 -> 26, of which waited for: 11 -> 11; matrix products, arithmetic and copies ran while one was open for 0% -> 0% of each run, Pallas kernels for 28% -> 29%
where the time goes in v13:
time: 71 us; the launch traced here: 70.9 us
  Pallas kernels  27.8 us (39%)
  starting transfers between devices  26.2 us (37%)
  waiting for transfers between devices  15.9 us (22%)
  between operations  0.95 us (1%)
    ppermute x26, starting transfers between devices, swap(): return lax.ppermute(array, axis, [(i, i ^ mask) for i in range(size)])  26.2 us
    ppermute x26, waiting for transfers between devices, swap(): return lax.ppermute(array, axis, [(i, i ^ mask) for i in range(size)])  15.9 us
    pallas_call x4, Pallas kernels, shards(): call(functools.partial(score_kernel, slots, rows, dim, step), [((block, b...  11.9 us
    pallas_call x4, Pallas kernels, shards(): call(functools.partial(back_kernel, slots, rows, dim, dq is None), [((wid...  8.66 us
    pallas_call x1, Pallas kernels, shards(): call(functools.partial(pack_kv_kernel, heads, rows, dim, a_of), [((rows,...  1.9 us
  transfers between devices with their start and end apart: 26, of which 11 were waited for; matrix products, arithmetic and copies ran while one was open for 0% of the time, Pallas kernels for 29%

profile of v13, /device:TPU:0, one launch (start us, length us, event | category | flops | bytes accessed | tf_op | source)
XLA Modules:
  0.0 70.9 jit_solution(2938560758542226264)
XLA Ops:
  0.7 1.9 %shard_map.84 = (bf16[256,128]{1,0:T(8,128)(2,1)}, bf16[256,128]{1,0:T(8,128)(2,1)}, bf16[256,128]{1,0:T(8,128)(2,1)}, bf16[256,128]{1,0:T(8,128)(2,1)}) custom-call(s32[2]{0:T(128)} %fill_ref.7, bf16[1024,128]{1,0:T(8,128)(2,1)} %bitcast.5), custom_call_target="tpu_custom_call" | custom-call | flops 1724999936 | tf_op jit(solution)/shard_map/pallas_call | solution.py:285
  2.6 4.0 %collective-permute-start = (bf16[256,128]{1,0:T(8,128)(2,1)}, bf16[256,128]{1,0:T(8,128)(2,1)S(1)}, u32[]{:S(2)}, u32[]{:S(2)}) collective-permute-start(bf16[256,128]{1,0:T(8,128)(2,1)} %get-tuple-element.66), channel_id=1, source_target_pairs={{0,16},{2,18},{4,20},{6,22},{8,24},{10,26},{12,28},{14,30},{16,0},... | collective-permute-start | bytes 196616 | tf_op jit(solution)/shard_map/ppermute | solution.py:279
  6.6 1.3 %collective-permute-start.1 = (bf16[256,128]{1,0:T(8,128)(2,1)}, bf16[256,128]{1,0:T(8,128)(2,1)S(1)}, u32[]{:S(2)}, u32[]{:S(2)}) collective-permute-start(bf16[256,128]{1,0:T(8,128)(2,1)} %get-tuple-element.67), channel_id=1, source_target_pairs={{0,24},{2,26},{4,28},{6,30},{8,16},{10,18},{12,20},{14,22},{16,8},... | collective-permute-start | bytes 196616 | tf_op jit(solution)/shard_map/ppermute | solution.py:279
  8.0 0.2 collective-permute-start.2
  8.2 0.0 copy-start
  8.2 0.9 %shard_map.85 = (bf16[128,256]{1,0:T(8,128)(2,1)S(1)}, bf16[128,256]{1,0:T(8,128)(2,1)S(1)}, bf16[128,256]{1,0:T(8,128)(2,1)S(1)}, bf16[128,256]{1,0:T(8,128)(2,1)S(1)}) custom-call(s32[2]{0:T(128)S(1)} %copy-done.4, bf16[4,64,256]{2,1,0:T(8,128)(2,1)S(1)} %bitcast.4, bf16[4,64,768]{2,1,0:T(8,128)(2,1)S(1)} %copy-done.2, bf16[256,768]{1,0:T(8,128)(2,1)S(1)} %copy-done.1), custom_call_target="tpu_custom_call" | custom-call | flops 1150000000 | tf_op jit(solution)/shard_map/pallas_call | solution.py:290
  9.1 2.9 %collective-permute-start.3 = (bf16[128,256]{1,0:T(8,128)(2,1)S(1)}, bf16[128,256]{1,0:T(8,128)(2,1)S(1)}, u32[]{:S(2)}, u32[]{:S(2)}) collective-permute-start(bf16[128,256]{1,0:T(8,128)(2,1)S(1)} %get-tuple-element.70), channel_id=1, source_target_pairs={{0,16},{2,18},{4,20},{6,22},{8,24},{10,26},{12,28},{14,30},{16,0},... | collective-permute-start | bytes 196616 | tf_op jit(solution)/shard_map/ppermute | solution.py:279
  12.0 1.3 %collective-permute-start.4 = (bf16[128,256]{1,0:T(8,128)(2,1)S(1)}, bf16[128,256]{1,0:T(8,128)(2,1)S(1)}, u32[]{:S(2)}, u32[]{:S(2)}) collective-permute-start(bf16[128,256]{1,0:T(8,128)(2,1)S(1)} %get-tuple-element.71), channel_id=1, source_target_pairs={{0,24},{2,26},{4,28},{6,30},{8,16},{10,18},{12,20},{14,22},{16,8},... | collective-permute-start | bytes 196616 | tf_op jit(solution)/shard_map/ppermute | solution.py:279
  13.3 0.0 collective-permute-done.refs_1_
  13.3 0.0 collective-permute-start.5
  13.3 0.0 collective-permute-done.2.refs_3_
  13.4 1.6 %collective-permute-start.7 = (bf16[1024,128]{1,0:T(8,128)(2,1)S(1)}, bf16[1024,128]{1,0:T(8,128)(2,1)S(1)}, u32[]{:S(2)}, u32[]{:S(2)}) collective-permute-start(bf16[1024,128]{1,0:T(8,128)(2,1)S(1)} %shard_map.86.pair_ref), channel_id=1, source_target_pairs={{0,4},{2,6},{4,0},{6,2},{8,12},{10,14},{12,8},{14,10},{16,20},{18,... | collective-permute-start | bytes 786440 | tf_op jit(solution)/shard_map/ppermute | solution.py:279
  15.0 2.2 %collective-permute-done.3.refs_1_ = bf16[128,256]{1,0:T(8,128)(2,1)S(1)} collective-permute-done((bf16[128,256]{1,0:T(8,128)(2,1)S(1)}, bf16[128,256]{1,0:T(8,128)(2,1)S(1)}, u32[]{:S(2)}, u32[]{:S(2)}) %collective-permute-start.3) | collective-permute-done | bytes 65568 | tf_op jit(solution)/shard_map/ppermute | solution.py:279
  17.2 1.0 %collective-permute-done.4.refs_2_ = bf16[128,256]{1,0:T(8,128)(2,1)S(1)} collective-permute-done((bf16[128,256]{1,0:T(8,128)(2,1)S(1)}, bf16[128,256]{1,0:T(8,128)(2,1)S(1)}, u32[]{:S(2)}, u32[]{:S(2)}) %collective-permute-start.4) | collective-permute-done | bytes 65568 | tf_op jit(solution)/shard_map/ppermute | solution.py:279
  18.2 0.3 collective-permute-done.5.refs_3_
  18.4 0.1 shard_map.87
  18.6 2.9 %shard_map.88 = (bf16[1024,1024]{1,0:T(8,128)(2,1)S(1)}, f32[1,1024]{1,0:T(1,128)S(1)}, f32[80,1024]{1,0:T(8,128)S(1)}, bf16[1024,128]{1,0:T(8,128)(2,1)S(1)}, bf16[64,1024]{1,0:T(8,128)(2,1)S(1)}) custom-call(bf16[1024,128]{1,0:T(8,128)(2,1)S(1)} %shard_map.86.pair_ref, bf16[256,1024]{1,0:T(8,128)(2,1)S(1)} %get-tuple-element.73.qa_ref, ...), custom_call_target="tpu_custom_call" | custom-call | flops 5750000128 | tf_op jit(solution)/shard_map/pallas_call | solution.py:316
  21.5 0.0 collective-permute-done.6.pair_ref
  21.5 2.9 %shard_map.89 = (bf16[1024,1024]{1,0:T(8,128)(2,1)S(1)}, f32[1,1024]{1,0:T(1,128)S(1)}, f32[80,1024]{1,0:T(8,128)S(1)}, bf16[1024,128]{1,0:T(8,128)(2,1)S(1)}, bf16[64,1024]{1,0:T(8,128)(2,1)S(1)}) custom-call(bf16[1024,128]{1,0:T(8,128)(2,1)S(1)} %collective-permute-done.6.pair_ref, bf16[256,1024]{1,0:T(8,128)(2,1)S(1)} %get-tuple-element.73.qa_ref, ...), custom_call_target="tpu_custom_call" | custom-call | flops 5750000128 | tf_op jit(solution)/shard_map/pallas_call | solution.py:316
  24.5 0.0 collective-permute-done.7.refs_0_
  24.5 0.1 collective-permute-start.8
  24.6 2.9 %shard_map.91 = (bf16[1024,1024]{1,0:T(8,128)(2,1)S(1)}, f32[1,1024]{1,0:T(1,128)S(1)}, f32[80,1024]{1,0:T(8,128)S(1)}, bf16[1024,128]{1,0:T(8,128)(2,1)S(1)}, bf16[64,1024]{1,0:T(8,128)(2,1)S(1)}) custom-call(bf16[1024,128]{1,0:T(8,128)(2,1)S(1)} %shard_map.90.pair_ref, bf16[256,1024]{1,0:T(8,128)(2,1)S(1)} %get-tuple-element.73.qa_ref, ...), custom_call_target="tpu_custom_call" | custom-call | flops 5750000128 | tf_op jit(solution)/shard_map/pallas_call | solution.py:316
  27.5 0.0 collective-permute-done.8.pair_ref
  27.5 3.1 %shard_map.92 = (bf16[1024,1024]{1,0:T(8,128)(2,1)S(1)}, f32[1,1024]{1,0:T(1,128)S(1)}, f32[80,1024]{1,0:T(8,128)S(1)}, bf16[1024,128]{1,0:T(8,128)(2,1)S(1)}, bf16[64,1024]{1,0:T(8,128)(2,1)S(1)}) custom-call(bf16[1024,128]{1,0:T(8,128)(2,1)S(1)} %collective-permute-done.8.pair_ref, bf16[256,1024]{1,0:T(8,128)(2,1)S(1)} %get-tuple-element.73.qa_ref, ...), custom_call_target="tpu_custom_call" | custom-call | flops 5750000128 | tf_op jit(solution)/shard_map/pallas_call | solution.py:316
  30.7 0.2 shard_map.93
  30.8 3.1 %collective-permute-start.9 = (bf16[64,256]{1,0:T(8,128)(2,1)S(1)}, bf16[64,256]{1,0:T(8,128)(2,1)S(1)}, u32[]{:S(2)}, u32[]{:S(2)}) collective-permute-start(bf16[64,256]{1,0:T(8,128)(2,1)S(1)} %get-tuple-element.85), channel_id=1, source_target_pairs={{0,16},{2,18},{4,20},{6,22},{8,24},{10,26},{12,28},{14,30},{16,0},... | collective-permute-start | bytes 98312 | tf_op jit(solution)/shard_map/ppermute | solution.py:279
  33.9 0.4 collective-permute-start.10
  34.3 0.2 collective-permute-start.11
  34.5 2.2 %shard_map.94 = (bf16[128,1024]{1,0:T(8,128)(2,1)S(1)}, f32[64,1024]{1,0:T(8,128)S(1)}) custom-call(bf16[1024,1024]{1,0:T(8,128)(2,1)S(1)} %get-tuple-element.88.exp_ref, bf16[1024,128]{1,0:T(8,128)(2,1)S(1)} %get-tuple-element.89.v_ref, bf16[64,1024]{1,0:T(8,128)(2,1)S(1)} %get-tuple-element.90.kt_ref, bf16[64,1024]{1,0:T(8,128)(2,1)S(1)} %get-tuple-element.91.q_ref, ...), custom_call_target="tpu_custom_call" | custom-call | flops 2300000000 | tf_op jit(solution)/shard_map/pallas_call | solution.py:362
  36.7 0.0 collective-permute-done.9.refs_1_
  36.7 2.9 %collective-permute-done.10.refs_2_ = bf16[64,256]{1,0:T(8,128)(2,1)S(1)} collective-permute-done((bf16[64,256]{1,0:T(8,128)(2,1)S(1)}, bf16[64,256]{1,0:T(8,128)(2,1)S(1)}, u32[]{:S(2)}, u32[]{:S(2)}) %collective-permute-start.10) | collective-permute-done | bytes 32800 | tf_op jit(solution)/shard_map/ppermute | solution.py:279
  39.6 0.8 %shard_map.95 = (bf16[2,64,768]{2,1,0:T(8,128)(2,1)S(1)}, bf16[2,64,768]{2,1,0:T(8,128)(2,1)S(1)}) custom-call(s32[2]{0:T(128)S(1)} %copy-done.4, bf16[256,768]{1,0:T(8,128)(2,1)S(1)} %copy-done.1, bf16[64,256]{1,0:T(8,128)(2,1)S(1)} %get-tuple-element.84.refs_0_, bf16[64,256]{1,0:T(8,128)(2,1)S(1)} %collective-permute-done.9.refs_1_, ...), custom_call_target="tpu_custom_call" | custom-call | flops 805000000 | tf_op jit(solution)/shard_map/pallas_call | solution.py:336
  40.4 0.1 collective-permute-start.12
  40.5 0.5 collective-permute-start.16
  41.0 0.8 %shard_map.96._.refs_4_ = bf16[256,768]{1,0:T(8,128)(2,1)S(1)} custom-call(s32[2]{0:T(128)S(1)} %copy-done.4, bf16[4,64,768]{2,1,0:T(8,128)(2,1)S(1)} %copy-done.2, bf16[64,256]{1,0:T(8,128)(2,1)S(1)} %get-tuple-element.84.refs_0_, bf16[64,256]{1,0:T(8,128)(2,1)S(1)} %collective-permute-done.9.refs_1_, bf16[64,256]{1,0:T(8,128)(2,1)S(1)} %collective-permute-done.10.refs_2_, ...), custom_call_target="tpu_custom_call" | custom-call | flops 805000000 | tf_op jit(solution)/shard_map/pallas_call | solution.py:342
  41.9 1.6 %collective-permute-start.18 = (bf16[256,768]{1,0:T(8,128)(2,1)S(1)}, bf16[256,768]{1,0:T(8,128)(2,1)S(1)}, u32[]{:S(2)}, u32[]{:S(2)}) collective-permute-start(bf16[256,768]{1,0:T(8,128)(2,1)S(1)} %shard_map.96._.refs_4_), channel_id=1, source_target_pairs={{0,1},{1,0},{2,3},{3,2},{4,5},{5,4},{6,7},{7,6},{8,9},{9,8},{10,11... | collective-permute-start | bytes 1179656 | tf_op jit(solution)/shard_map/ppermute | solution.py:279
  43.4 0.0 collective-permute-done.12.came_ref
  43.5 1.6 %collective-permute-start.13 = (bf16[64,768]{1,0:T(8,128)(2,1)S(1)}, bf16[64,768]{1,0:T(8,128)(2,1)S(1)}, u32[]{:S(2)}, u32[]{:S(2)}) collective-permute-start(bf16[64,768]{1,0:T(8,128)(2,1)S(1)} %get-tuple-element.98), channel_id=1, source_target_pairs={{0,4},{2,6},{4,0},{6,2},{8,12},{10,14},{12,8},{14,10},{16,20},{18,... | collective-permute-start | bytes 294920 | tf_op jit(solution)/shard_map/ppermute | solution.py:279
  45.1 2.2 %shard_map.98 = (bf16[128,1024]{1,0:T(8,128)(2,1)S(1)}, f32[64,1024]{1,0:T(8,128)S(1)}) custom-call(bf16[1024,1024]{1,0:T(8,128)(2,1)S(1)} %get-tuple-element.99.exp_ref, bf16[1024,128]{1,0:T(8,128)(2,1)S(1)} %get-tuple-element.100.v_ref, bf16[64,1024]{1,0:T(8,128)(2,1)S(1)} %get-tuple-element.101.kt_ref, bf16[64,1024]{1,0:T(8,128)(2,1)S(1)} %get-tuple-element.91.q_ref, ...), custom_call_target="tpu_custom_call" | custom-call | flops 2300000000 | tf_op jit(solution)/shard_map/pallas_call | solution.py:362
  47.2 0.1 shard_map.102
  47.3 0.6 collective-permute-start.17
  47.9 0.3 collective-permute-done.13.b_ref
  48.2 1.0 %collective-permute-start.14 = (bf16[64,768]{1,0:T(8,128)(2,1)S(1)}, bf16[64,768]{1,0:T(8,128)(2,1)S(1)}, u32[]{:S(2)}, u32[]{:S(2)}) collective-permute-start(bf16[64,768]{1,0:T(8,128)(2,1)S(1)} %shard_map.99.refs_1_.a_ref), channel_id=1, source_target_pairs={{0,16},{2,18},{4,20},{6,22},{8,24},{10,26},{12,28},{14,30},{16,0},... | collective-permute-start | bytes 294920 | tf_op jit(solution)/shard_map/ppermute | solution.py:279
  49.2 2.2 %shard_map.100 = (bf16[128,1024]{1,0:T(8,128)(2,1)S(1)}, f32[64,1024]{1,0:T(8,128)S(1)}) custom-call(bf16[1024,1024]{1,0:T(8,128)(2,1)S(1)} %get-tuple-element.105.exp_ref, bf16[1024,128]{1,0:T(8,128)(2,1)S(1)} %get-tuple-element.106.v_ref, bf16[64,1024]{1,0:T(8,128)(2,1)S(1)} %get-tuple-element.107.kt_ref, bf16[64,1024]{1,0:T(8,128)(2,1)S(1)} %get-tuple-element.91.q_ref, ...), custom_call_target="tpu_custom_call" | custom-call | flops 2300000000 | tf_op jit(solution)/shard_map/pallas_call | solution.py:362
  51.3 0.1 collective-permute-start.19
  51.4 2.9 %collective-permute-done.14.b_ref = bf16[64,768]{1,0:T(8,128)(2,1)S(1)} collective-permute-done((bf16[64,768]{1,0:T(8,128)(2,1)S(1)}, bf16[64,768]{1,0:T(8,128)(2,1)S(1)}, u32[]{:S(2)}, u32[]{:S(2)}) %collective-permute-start.14) | collective-permute-done | bytes 98336 | tf_op jit(solution)/shard_map/ppermute | solution.py:279
  54.3 0.1 collective-permute-start.15
  54.4 0.7 collective-permute-done.17.refs_2_.came_ref
  55.1 2.2 %shard_map.103 = (bf16[128,1024]{1,0:T(8,128)(2,1)S(1)}, f32[64,1024]{1,0:T(8,128)S(1)}) custom-call(bf16[1024,1024]{1,0:T(8,128)(2,1)S(1)} %get-tuple-element.111.exp_ref, bf16[1024,128]{1,0:T(8,128)(2,1)S(1)} %get-tuple-element.112.v_ref, bf16[64,1024]{1,0:T(8,128)(2,1)S(1)} %get-tuple-element.113.kt_ref, bf16[64,1024]{1,0:T(8,128)(2,1)S(1)} %get-tuple-element.91.q_ref, ...), custom_call_target="tpu_custom_call" | custom-call | flops 2300000000 | tf_op jit(solution)/shard_map/pallas_call | solution.py:362
  57.3 0.1 shard_map.104.kept_ref
  57.3 0.1 shard_map.105
  57.4 2.4 %collective-permute-start.23 = (bf16[192,256]{1,0:T(8,128)(2,1)S(1)}, bf16[192,256]{1,0:T(8,128)(2,1)S(1)}, u32[]{:S(2)}, u32[]{:S(2)}) collective-permute-start(bf16[192,256]{1,0:T(8,128)(2,1)S(1)} %get-tuple-element.120), channel_id=1, source_target_pairs={{0,16},{2,18},{4,20},{6,22},{8,24},{10,26},{12,28},{14,30},{16,0},... | collective-permute-start | bytes 294920 | tf_op jit(solution)/shard_map/ppermute | solution.py:279
  59.8 1.6 %collective-permute-start.21 = (bf16[64,768]{1,0:T(8,128)(2,1)S(1)}, bf16[64,768]{1,0:T(8,128)(2,1)S(1)}, u32[]{:S(2)}, u32[]{:S(2)}) collective-permute-start(bf16[64,768]{1,0:T(8,128)(2,1)S(1)} %shard_map.106.refs_0_), channel_id=1, source_target_pairs={{0,4},{2,6},{4,0},{6,2},{8,12},{10,14},{12,8},{14,10},{16,20},{18,... | collective-permute-start | bytes 294920 | tf_op jit(solution)/shard_map/ppermute | solution.py:279
  61.4 1.6 %collective-permute-start.24 = (bf16[192,256]{1,0:T(8,128)(2,1)S(1)}, bf16[192,256]{1,0:T(8,128)(2,1)S(1)}, u32[]{:S(2)}, u32[]{:S(2)}) collective-permute-start(bf16[192,256]{1,0:T(8,128)(2,1)S(1)} %get-tuple-element.121), channel_id=1, source_target_pairs={{0,24},{2,26},{4,28},{6,30},{8,16},{10,18},{12,20},{14,22},{16,8},... | collective-permute-start | bytes 294920 | tf_op jit(solution)/shard_map/ppermute | solution.py:279
  63.1 0.0 collective-permute-start.20
  63.1 1.5 %collective-permute-done.21.refs_2_ = bf16[64,768]{1,0:T(8,128)(2,1)S(1)} collective-permute-done((bf16[64,768]{1,0:T(8,128)(2,1)S(1)}, bf16[64,768]{1,0:T(8,128)(2,1)S(1)}, u32[]{:S(2)}, u32[]{:S(2)}) %collective-permute-start.21) | collective-permute-done | bytes 98336 | tf_op jit(solution)/shard_map/ppermute | solution.py:279
  64.5 0.0 collective-permute-start.22
  64.5 1.6 %collective-permute-done.23.refs_1_ = bf16[192,256]{1,0:T(8,128)(2,1)S(1)} collective-permute-done((bf16[192,256]{1,0:T(8,128)(2,1)S(1)}, bf16[192,256]{1,0:T(8,128)(2,1)S(1)}, u32[]{:S(2)}, u32[]{:S(2)}) %collective-permute-start.23) | collective-permute-done | bytes 98336 | tf_op jit(solution)/shard_map/ppermute | solution.py:279
  66.1 1.9 %collective-permute-done.24.refs_2_ = bf16[192,256]{1,0:T(8,128)(2,1)S(1)} collective-permute-done((bf16[192,256]{1,0:T(8,128)(2,1)S(1)}, bf16[192,256]{1,0:T(8,128)(2,1)S(1)}, u32[]{:S(2)}, u32[]{:S(2)}) %collective-permute-start.24) | collective-permute-done | bytes 98336 | tf_op jit(solution)/shard_map/ppermute | solution.py:279
  68.0 0.8 %collective-permute-done.25.refs_3_ = bf16[192,256]{1,0:T(8,128)(2,1)S(1)} collective-permute-done((bf16[192,256]{1,0:T(8,128)(2,1)S(1)}, bf16[192,256]{1,0:T(8,128)(2,1)S(1)}, u32[]{:S(2)}, u32[]{:S(2)}) %collective-permute-start.25) | collective-permute-done | bytes 98336 | tf_op jit(solution)/shard_map/ppermute | solution.py:279
  68.7 1.0 %shard_map.108 = (f32[1024,128]{1,0:T(8,128)}, f32[4,64,256]{2,1,0:T(8,128)}) custom-call(bf16[192,256]{1,0:T(8,128)(2,1)S(1)} %get-tuple-element.118.refs_0_, bf16[192,256]{1,0:T(8,128)(2,1)S(1)} %collective-permute-done.23.refs_1_, bf16[192,256]{1,0:T(8,128)(2,1)S(1)} %collective-permute-done.24.refs_2_, bf16[192,256]{1,0:T(8,128)(2,1)S(1)} %collective-permute-done.25.refs_3_), custom_call_target="tpu_custom_call" | custom-call | flops 1150000000 | tf_op jit(solution)/shard_map/pallas_call | solution.py:395
  69.7 0.0 collective-permute-done.20.refs_1_
  69.7 0.0 collective-permute-done.22.refs_3_
  69.7 1.2 %shard_map.107 = (bf16[256,768]{1,0:T(8,128)(2,1)}, f32[4,64,768]{2,1,0:T(8,128)}) custom-call(bf16[64,768]{1,0:T(8,128)(2,1)S(1)} %shard_map.106.refs_0_, bf16[64,768]{1,0:T(8,128)(2,1)S(1)} %collective-permute-done.20.refs_1_, bf16[64,768]{1,0:T(8,128)(2,1)S(1)} %collective-permute-done.21.refs_2_, bf16[64,768]{1,0:T(8,128)(2,1)S(1)} %collective-permute-done.22.refs_3_, ...), custom_call_target="tpu_custom_call" | custom-call | flops 575000000 | tf_op jit(solution)/shard_map/pallas_call | solution.py:388
  (23 shorter events, 0.2 us)
Async XLA Ops:
  0.6 7.6 %copy-start.1 = (bf16[256,768]{1,0:T(8,128)(2,1)S(1)}, bf16[256,768]{1,0:T(8,128)(2,1)}, u32[]{:S(2)}) copy-start(bf16[256,768]{1,0:T(8,128)(2,1)} %go_ref.3) | copy-start | bytes 1179652
  0.6 7.6 %copy-start.2 = (bf16[4,64,768]{2,1,0:T(8,128)(2,1)S(1)}, bf16[4,64,768]{2,1,0:T(8,128)(2,1)}, u32[]{:S(2)}) copy-start(bf16[4,64,768]{2,1,0:T(8,128)(2,1)} %w_ref.3) | copy-start | bytes 1179652
  0.7 7.5 %copy-start.3 = (bf16[256,4,64]{0,2,1:T(8,128)(2,1)S(1)}, bf16[256,4,64]{0,2,1:T(8,128)(2,1)}, u32[]{:S(2)}) copy-start(bf16[256,4,64]{0,2,1:T(8,128)(2,1)} %param.5) | copy-start | bytes 393220
  0.7 7.5 %copy-start.4 = (s32[2]{0:T(128)S(1)}, s32[2]{0:T(128)}, u32[]{:S(2)}) copy-start(s32[2]{0:T(128)} %fill_ref.7) | copy-start | bytes 28
  2.6 10.7 %collective-permute-start = (bf16[256,128]{1,0:T(8,128)(2,1)}, bf16[256,128]{1,0:T(8,128)(2,1)S(1)}, u32[]{:S(2)}, u32[]{:S(2)}) collective-permute-start(bf16[256,128]{1,0:T(8,128)(2,1)} %get-tuple-element.66), channel_id=1, source_target_pairs={{0,16},{2,18},{4,20},{6,22},{8,24},{10,26},{12,28},{14,30},{16,0},... | collective-permute-start | bytes 196616 | tf_op jit(solution)/shard_map/ppermute | solution.py:279
  6.6 6.7 %collective-permute-start.1 = (bf16[256,128]{1,0:T(8,128)(2,1)}, bf16[256,128]{1,0:T(8,128)(2,1)S(1)}, u32[]{:S(2)}, u32[]{:S(2)}) collective-permute-start(bf16[256,128]{1,0:T(8,128)(2,1)} %get-tuple-element.67), channel_id=1, source_target_pairs={{0,24},{2,26},{4,28},{6,30},{8,16},{10,18},{12,20},{14,22},{16,8},... | collective-permute-start | bytes 196616 | tf_op jit(solution)/shard_map/ppermute | solution.py:279
  8.0 5.4 %collective-permute-start.2 = (bf16[256,128]{1,0:T(8,128)(2,1)}, bf16[256,128]{1,0:T(8,128)(2,1)S(1)}, u32[]{:S(2)}, u32[]{:S(2)}) collective-permute-start(bf16[256,128]{1,0:T(8,128)(2,1)} %get-tuple-element.68), channel_id=1, source_target_pairs={{0,8},{2,10},{4,12},{6,14},{8,0},{10,2},{12,4},{14,6},{16,24},{18,... | collective-permute-start | bytes 196616 | tf_op jit(solution)/shard_map/ppermute | solution.py:279
  8.2 5.1 %copy-start = (bf16[256,128]{1,0:T(8,128)(2,1)S(1)}, bf16[256,128]{1,0:T(8,128)(2,1)}, u32[]{:S(2)}) copy-start(bf16[256,128]{1,0:T(8,128)(2,1)} %get-tuple-element.65.refs_0_) | copy-start | bytes 196612
  9.1 8.1 %collective-permute-start.3 = (bf16[128,256]{1,0:T(8,128)(2,1)S(1)}, bf16[128,256]{1,0:T(8,128)(2,1)S(1)}, u32[]{:S(2)}, u32[]{:S(2)}) collective-permute-start(bf16[128,256]{1,0:T(8,128)(2,1)S(1)} %get-tuple-element.70), channel_id=1, source_target_pairs={{0,16},{2,18},{4,20},{6,22},{8,24},{10,26},{12,28},{14,30},{16,0},... | collective-permute-start | bytes 196616 | tf_op jit(solution)/shard_map/ppermute | solution.py:279
  12.0 6.2 %collective-permute-start.4 = (bf16[128,256]{1,0:T(8,128)(2,1)S(1)}, bf16[128,256]{1,0:T(8,128)(2,1)S(1)}, u32[]{:S(2)}, u32[]{:S(2)}) collective-permute-start(bf16[128,256]{1,0:T(8,128)(2,1)S(1)} %get-tuple-element.71), channel_id=1, source_target_pairs={{0,24},{2,26},{4,28},{6,30},{8,16},{10,18},{12,20},{14,22},{16,8},... | collective-permute-start | bytes 196616 | tf_op jit(solution)/shard_map/ppermute | solution.py:279
  13.3 5.1 %collective-permute-start.5 = (bf16[128,256]{1,0:T(8,128)(2,1)S(1)}, bf16[128,256]{1,0:T(8,128)(2,1)S(1)}, u32[]{:S(2)}, u32[]{:S(2)}) collective-permute-start(bf16[128,256]{1,0:T(8,128)(2,1)S(1)} %get-tuple-element.72), channel_id=1, source_target_pairs={{0,8},{2,10},{4,12},{6,14},{8,0},{10,2},{12,4},{14,6},{16,24},{18,... | collective-permute-start | bytes 196616 | tf_op jit(solution)/shard_map/ppermute | solution.py:279
  13.4 11.1 %collective-permute-start.7 = (bf16[1024,128]{1,0:T(8,128)(2,1)S(1)}, bf16[1024,128]{1,0:T(8,128)(2,1)S(1)}, u32[]{:S(2)}, u32[]{:S(2)}) collective-permute-start(bf16[1024,128]{1,0:T(8,128)(2,1)S(1)} %shard_map.86.pair_ref), channel_id=1, source_target_pairs={{0,4},{2,6},{4,0},{6,2},{8,12},{10,14},{12,8},{14,10},{16,20},{18,... | collective-permute-start | bytes 786440 | tf_op jit(solution)/shard_map/ppermute | solution.py:279
  14.9 6.5 %collective-permute-start.6 = (bf16[1024,128]{1,0:T(8,128)(2,1)S(1)}, bf16[1024,128]{1,0:T(8,128)(2,1)S(1)}, u32[]{:S(2)}, u32[]{:S(2)}) collective-permute-start(bf16[1024,128]{1,0:T(8,128)(2,1)S(1)} %shard_map.86.pair_ref), channel_id=1, source_target_pairs={{0,2},{2,0},{4,6},{6,4},{8,10},{10,8},{12,14},{14,12},{16,18},{18,... | collective-permute-start | bytes 786440 | tf_op jit(solution)/shard_map/ppermute | solution.py:279
  24.5 3.0 %collective-permute-start.8 = (bf16[1024,128]{1,0:T(8,128)(2,1)S(1)}, bf16[1024,128]{1,0:T(8,128)(2,1)S(1)}, u32[]{:S(2)}, u32[]{:S(2)}) collective-permute-start(bf16[1024,128]{1,0:T(8,128)(2,1)S(1)} %shard_map.90.pair_ref), channel_id=1, source_target_pairs={{0,2},{2,0},{4,6},{6,4},{8,10},{10,8},{12,14},{14,12},{16,18},{18,... | collective-permute-start | bytes 786440 | tf_op jit(solution)/shard_map/ppermute | solution.py:279
  30.8 5.9 %collective-permute-start.9 = (bf16[64,256]{1,0:T(8,128)(2,1)S(1)}, bf16[64,256]{1,0:T(8,128)(2,1)S(1)}, u32[]{:S(2)}, u32[]{:S(2)}) collective-permute-start(bf16[64,256]{1,0:T(8,128)(2,1)S(1)} %get-tuple-element.85), channel_id=1, source_target_pairs={{0,16},{2,18},{4,20},{6,22},{8,24},{10,26},{12,28},{14,30},{16,0},... | collective-permute-start | bytes 98312 | tf_op jit(solution)/shard_map/ppermute | solution.py:279
  33.9 5.7 %collective-permute-start.10 = (bf16[64,256]{1,0:T(8,128)(2,1)S(1)}, bf16[64,256]{1,0:T(8,128)(2,1)S(1)}, u32[]{:S(2)}, u32[]{:S(2)}) collective-permute-start(bf16[64,256]{1,0:T(8,128)(2,1)S(1)} %get-tuple-element.86), channel_id=1, source_target_pairs={{0,24},{2,26},{4,28},{6,30},{8,16},{10,18},{12,20},{14,22},{16,8},... | collective-permute-start | bytes 98312 | tf_op jit(solution)/shard_map/ppermute | solution.py:279
  34.3 5.3 %collective-permute-start.11 = (bf16[64,256]{1,0:T(8,128)(2,1)S(1)}, bf16[64,256]{1,0:T(8,128)(2,1)S(1)}, u32[]{:S(2)}, u32[]{:S(2)}) collective-permute-start(bf16[64,256]{1,0:T(8,128)(2,1)S(1)} %get-tuple-element.87), channel_id=1, source_target_pairs={{0,8},{2,10},{4,12},{6,14},{8,0},{10,2},{12,4},{14,6},{16,24},{18,... | collective-permute-start | bytes 98312 | tf_op jit(solution)/shard_map/ppermute | solution.py:279
  40.4 3.0 %collective-permute-start.12 = (bf16[2,64,768]{2,1,0:T(8,128)(2,1)S(1)}, bf16[2,64,768]{2,1,0:T(8,128)(2,1)S(1)}, u32[]{:S(2)}, u32[]{:S(2)}) collective-permute-start(bf16[2,64,768]{2,1,0:T(8,128)(2,1)S(1)} %get-tuple-element.96.refs_4_), channel_id=1, source_target_pairs={{0,2},{2,0},{4,6},{6,4},{8,10},{10,8},{12,14},{14,12},{16,18},{18,... | collective-permute-start | bytes 589832 | tf_op jit(solution)/shard_map/ppermute | solution.py:279
  40.5 6.7 %collective-permute-start.16 = (bf16[128,1024]{1,0:T(8,128)(2,1)S(1)}, bf16[128,1024]{1,0:T(8,128)(2,1)S(1)}, u32[]{:S(2)}, u32[]{:S(2)}) collective-permute-start(bf16[128,1024]{1,0:T(8,128)(2,1)S(1)} %get-tuple-element.94.refs_4_), channel_id=1, source_target_pairs={{0,2},{2,0},{4,6},{6,4},{8,10},{10,8},{12,14},{14,12},{16,18},{18,... | collective-permute-start | bytes 786440 | tf_op jit(solution)/shard_map/ppermute | solution.py:279
  41.9 12.6 %collective-permute-start.18 = (bf16[256,768]{1,0:T(8,128)(2,1)S(1)}, bf16[256,768]{1,0:T(8,128)(2,1)S(1)}, u32[]{:S(2)}, u32[]{:S(2)}) collective-permute-start(bf16[256,768]{1,0:T(8,128)(2,1)S(1)} %shard_map.96._.refs_4_), channel_id=1, source_target_pairs={{0,1},{1,0},{2,3},{3,2},{4,5},{5,4},{6,7},{7,6},{8,9},{9,8},{10,11... | collective-permute-start | bytes 1179656 | tf_op jit(solution)/shard_map/ppermute | solution.py:279
  43.5 4.7 %collective-permute-start.13 = (bf16[64,768]{1,0:T(8,128)(2,1)S(1)}, bf16[64,768]{1,0:T(8,128)(2,1)S(1)}, u32[]{:S(2)}, u32[]{:S(2)}) collective-permute-start(bf16[64,768]{1,0:T(8,128)(2,1)S(1)} %get-tuple-element.98), channel_id=1, source_target_pairs={{0,4},{2,6},{4,0},{6,2},{8,12},{10,14},{12,8},{14,10},{16,20},{18,... | collective-permute-start | bytes 294920 | tf_op jit(solution)/shard_map/ppermute | solution.py:279
  47.3 7.8 %collective-permute-start.17 = (bf16[128,1024]{1,0:T(8,128)(2,1)S(1)}, bf16[128,1024]{1,0:T(8,128)(2,1)S(1)}, u32[]{:S(2)}, u32[]{:S(2)}) collective-permute-start(bf16[128,1024]{1,0:T(8,128)(2,1)S(1)} %shard_map.102), channel_id=1, source_target_pairs={{0,4},{2,6},{4,0},{6,2},{8,12},{10,14},{12,8},{14,10},{16,20},{18,... | collective-permute-start | bytes 786440 | tf_op jit(solution)/shard_map/ppermute | solution.py:279
  48.2 6.1 %collective-permute-start.14 = (bf16[64,768]{1,0:T(8,128)(2,1)S(1)}, bf16[64,768]{1,0:T(8,128)(2,1)S(1)}, u32[]{:S(2)}, u32[]{:S(2)}) collective-permute-start(bf16[64,768]{1,0:T(8,128)(2,1)S(1)} %shard_map.99.refs_1_.a_ref), channel_id=1, source_target_pairs={{0,16},{2,18},{4,20},{6,22},{8,24},{10,26},{12,28},{14,30},{16,0},... | collective-permute-start | bytes 294920 | tf_op jit(solution)/shard_map/ppermute | solution.py:279
  51.3 5.9 %collective-permute-start.19 = (bf16[128,1024]{1,0:T(8,128)(2,1)S(1)}, bf16[128,1024]{1,0:T(8,128)(2,1)S(1)}, u32[]{:S(2)}, u32[]{:S(2)}) collective-permute-start(bf16[128,1024]{1,0:T(8,128)(2,1)S(1)} %get-tuple-element.110.refs_0_), channel_id=1, source_target_pairs={{0,2},{2,0},{4,6},{6,4},{8,10},{10,8},{12,14},{14,12},{16,18},{18,... | collective-permute-start | bytes 786440 | tf_op jit(solution)/shard_map/ppermute | solution.py:279
  54.3 5.5 %collective-permute-start.15 = (bf16[64,768]{1,0:T(8,128)(2,1)S(1)}, bf16[64,768]{1,0:T(8,128)(2,1)S(1)}, u32[]{:S(2)}, u32[]{:S(2)}) collective-permute-start(bf16[64,768]{1,0:T(8,128)(2,1)S(1)} %shard_map.101.refs_1_.a_ref), channel_id=1, source_target_pairs={{0,8},{2,10},{4,12},{6,14},{8,0},{10,2},{12,4},{14,6},{16,24},{18,... | collective-permute-start | bytes 294920 | tf_op jit(solution)/shard_map/ppermute | solution.py:279
  57.4 8.7 %collective-permute-start.23 = (bf16[192,256]{1,0:T(8,128)(2,1)S(1)}, bf16[192,256]{1,0:T(8,128)(2,1)S(1)}, u32[]{:S(2)}, u32[]{:S(2)}) collective-permute-start(bf16[192,256]{1,0:T(8,128)(2,1)S(1)} %get-tuple-element.120), channel_id=1, source_target_pairs={{0,16},{2,18},{4,20},{6,22},{8,24},{10,26},{12,28},{14,30},{16,0},... | collective-permute-start | bytes 294920 | tf_op jit(solution)/shard_map/ppermute | solution.py:279
  59.8 4.7 %collective-permute-start.21 = (bf16[64,768]{1,0:T(8,128)(2,1)S(1)}, bf16[64,768]{1,0:T(8,128)(2,1)S(1)}, u32[]{:S(2)}, u32[]{:S(2)}) collective-permute-start(bf16[64,768]{1,0:T(8,128)(2,1)S(1)} %shard_map.106.refs_0_), channel_id=1, source_target_pairs={{0,4},{2,6},{4,0},{6,2},{8,12},{10,14},{12,8},{14,10},{16,20},{18,... | collective-permute-start | bytes 294920 | tf_op jit(solution)/shard_map/ppermute | solution.py:279
  61.4 6.6 %collective-permute-start.24 = (bf16[192,256]{1,0:T(8,128)(2,1)S(1)}, bf16[192,256]{1,0:T(8,128)(2,1)S(1)}, u32[]{:S(2)}, u32[]{:S(2)}) collective-permute-start(bf16[192,256]{1,0:T(8,128)(2,1)S(1)} %get-tuple-element.121), channel_id=1, source_target_pairs={{0,24},{2,26},{4,28},{6,30},{8,16},{10,18},{12,20},{14,22},{16,8},... | collective-permute-start | bytes 294920 | tf_op jit(solution)/shard_map/ppermute | solution.py:279
  63.1 5.7 %collective-permute-start.25 = (bf16[192,256]{1,0:T(8,128)(2,1)S(1)}, bf16[192,256]{1,0:T(8,128)(2,1)S(1)}, u32[]{:S(2)}, u32[]{:S(2)}) collective-permute-start(bf16[192,256]{1,0:T(8,128)(2,1)S(1)} %get-tuple-element.122), channel_id=1, source_target_pairs={{0,8},{2,10},{4,12},{6,14},{8,0},{10,2},{12,4},{14,6},{16,24},{18,... | collective-permute-start | bytes 294920 | tf_op jit(solution)/shard_map/ppermute | solution.py:279
  63.1 6.6 %collective-permute-start.20 = (bf16[64,768]{1,0:T(8,128)(2,1)S(1)}, bf16[64,768]{1,0:T(8,128)(2,1)S(1)}, u32[]{:S(2)}, u32[]{:S(2)}) collective-permute-start(bf16[64,768]{1,0:T(8,128)(2,1)S(1)} %shard_map.106.refs_0_), channel_id=1, source_target_pairs={{0,2},{2,0},{4,6},{6,4},{8,10},{10,8},{12,14},{14,12},{16,18},{18,... | collective-permute-start | bytes 294920 | tf_op jit(solution)/shard_map/ppermute | solution.py:279
  64.5 5.2 %collective-permute-start.22 = (bf16[64,768]{1,0:T(8,128)(2,1)S(1)}, bf16[64,768]{1,0:T(8,128)(2,1)S(1)}, u32[]{:S(2)}, u32[]{:S(2)}) collective-permute-start(bf16[64,768]{1,0:T(8,128)(2,1)S(1)} %collective-permute-done.21.refs_2_), channel_id=1, source_target_pairs={{0,2},{2,0},{4,6},{6,4},{8,10},{10,8},{12,14},{14,12},{16,18},{18,... | collective-permute-start | bytes 294920 | tf_op jit(solution)/shard_map/ppermute | solution.py:279

commit v14 on v13

--- a/solution.py
+++ b/solution.py
@@ -250,7 +250,9 @@
 
 
 def unpack_kernel(slots, rows, dim, a_of, *refs):
-    pieces, (kv_out, q_out) = refs[:slots], refs[slots:]
+    pieces, (a_ref, b_ref, kv_out, q_out, sum_out, done_ref) = refs[:slots], refs[slots:]
+    sum_out[...] = (a_ref[...].astype(F32) + b_ref[...].astype(F32)).astype(BF16)
+    done_ref[...] = jnp.zeros_like(done_ref)
     wide = 2 * dim
     me = a_of()
     for slot, mask in enumerate(spread(slots)):
@@ -259,8 +261,7 @@
 
 
 def place_kernel(columns, b_of, *refs):
-    parts, (a_ref, b_ref), (sum_out, grad_out) = refs[:columns], refs[columns : columns + 2], refs[columns + 2 :]
-    sum_out[...] = (a_ref[...].astype(F32) + b_ref[...].astype(F32)).astype(BF16)
+    parts, (grad_out,) = refs[:columns], refs[columns:]
     me = b_of()
     for column in range(columns):
         grad_out[me ^ column] = parts[column][...].astype(F32)
@@ -329,7 +330,7 @@
     order = sorted(range(columns), reverse=True)
     add = call(add_kernel, [((dim, width), BF16)], n_in=2, after=1)
     add_halves = call(add_kernel, [((wide, block), BF16)], n_in=2)
-    far_masks = [seq >> level for level in range(1, slots.bit_length())]
+    z_masks = [columns << level for level in range(slots.bit_length() - 1)]
     dkv, dq, kept, summed, later = {}, None, None, {}, []
     for at, r in enumerate(order):
         if at and not halves and at == columns - 1 or halves and at == 1:
@@ -356,7 +357,7 @@
             kept = add(kept, swap(sent, 2), dkv[order[at - 1]])[0]
             later = [kept]
         if at == 3 and halves:
-            kept = add(kept, swap(kept, far_masks[0]), dkv[order[at - 1]])[0]
+            kept = add(kept, swap(kept, z_masks[0]), dkv[order[at - 1]])[0]
             later = [kept, summed[2], terms_came]
         operands = [scored[r][0], *scored[r][3:], q_all, grads, factors[r], inner] + ([] if dq is None else [dq])
         dkv[r], dq = call(
@@ -381,21 +382,20 @@
     )(*halved, dq)
     returned = exchange(pieces)
 
+    key_value_grad, query_grad, attention_out, done = call(
+        functools.partial(unpack_kernel, slots, rows, dim, a_of),
+        [((rows * heads, wide), F32), ((heads, dim, rows), F32), ((rows, width), BF16), ((8, 128), F32)],
+        n_in=slots + 2, micros=1,
+    )(*returned, terms, terms_came)
     if halves:
-        for mask in far_masks[1:]:
+        for mask in z_masks[1:]:
             kept = add(kept, swap(kept, mask), pieces[0])[0]
-        across = swap(kept, 2)
-        attention_out, weight_grad = call(
-            functools.partial(place_kernel, columns, b_of),
-            [((rows, width), BF16), ((heads, dim, width), F32)], n_in=columns + 2, micros=0.5,
-        )(kept, swap(kept, 1), across, swap(across, 1), terms, terms_came)
+        across = call(functools.partial(join_kernel, 1), [((dim, width), BF16)], after=1)(swap(kept, 2), done)[0]
+        weight_grad = call(
+            functools.partial(place_kernel, columns, b_of), [((heads, dim, width), F32)], n_in=columns, micros=0.5,
+        )(kept, swap(kept, 1), across, swap(across, 1))[0]
     else:
-        attention_out = call(add_kernel, [((rows, width), BF16)], n_in=2)(terms, terms_came)[0]
         weight_grad = lax.psum(weight_terms[0].astype(F32), "seq")
-    key_value_grad, query_grad = call(
-        functools.partial(unpack_kernel, slots, rows, dim, a_of),
-        [((rows * heads, wide), F32), ((heads, dim, rows), F32)], n_in=slots, micros=1,
-    )(*returned)
     return attention_out, jnp.transpose(query_grad, (2, 0, 1)), key_value_grad.reshape(rows, heads, wide), weight_grad
 
 

time: 71 us -> 70.4 us (level)
  starting transfers between devices: 26.2 us -> 25.1 us
    ppermute x26, starting transfers between devices: 26.2 us -> 25.1 us  [swap(): return lax.ppermute(array, axis, [(i, i ^ mask) for i in range(size)])]
  transfers between devices with their start and end apart: 26 -> 26, of which waited for: 11 -> 10; matrix products, arithmetic and copies ran while one was open for 0% -> 0% of each run, Pallas kernels for 29% -> 30%
where the time goes in v14:
time: 70.4 us; the launch traced here: 70.2 us
  Pallas kernels  27.7 us (39%)
  starting transfers between devices  25.1 us (36%)
  waiting for transfers between devices  16.4 us (23%)
  between operations  0.96 us (1%)
    ppermute x26, starting transfers between devices, swap(): return lax.ppermute(array, axis, [(i, i ^ mask) for i in range(size)])  25.1 us
    ppermute x26, waiting for transfers between devices, swap(): return lax.ppermute(array, axis, [(i, i ^ mask) for i in range(size)])  16.4 us
    pallas_call x4, Pallas kernels, shards(): call(functools.partial(score_kernel, slots, rows, dim, step), [((block, b...  11.9 us
    pallas_call x4, Pallas kernels, shards(): call(functools.partial(back_kernel, slots, rows, dim, dq is None), [((wid...  8.66 us
    pallas_call x1, Pallas kernels, shards(): call(functools.partial(pack_kv_kernel, heads, rows, dim, a_of), [((rows,...  1.9 us
  transfers between devices with their start and end apart: 26, of which 10 were waited for; matrix products, arithmetic and copies ran while one was open for 0% of the time, Pallas kernels for 30%

profile of v14, /device:TPU:0, one launch (start us, length us, event | category | flops | bytes accessed | tf_op | source)
XLA Modules:
  0.0 70.2 jit_solution(6834593931524811690)
XLA Ops:
  0.7 1.9 %shard_map.84 = (bf16[256,128]{1,0:T(8,128)(2,1)}, bf16[256,128]{1,0:T(8,128)(2,1)}, bf16[256,128]{1,0:T(8,128)(2,1)}, bf16[256,128]{1,0:T(8,128)(2,1)}) custom-call(s32[2]{0:T(128)} %fill_ref.7, bf16[1024,128]{1,0:T(8,128)(2,1)} %bitcast.5), custom_call_target="tpu_custom_call" | custom-call | flops 1724999936 | tf_op jit(solution)/shard_map/pallas_call | solution.py:286
  2.6 4.0 %collective-permute-start = (bf16[256,128]{1,0:T(8,128)(2,1)}, bf16[256,128]{1,0:T(8,128)(2,1)S(1)}, u32[]{:S(2)}, u32[]{:S(2)}) collective-permute-start(bf16[256,128]{1,0:T(8,128)(2,1)} %get-tuple-element.66), channel_id=1, source_target_pairs={{0,16},{2,18},{4,20},{6,22},{8,24},{10,26},{12,28},{14,30},{16,0},... | collective-permute-start | bytes 196616 | tf_op jit(solution)/shard_map/ppermute | solution.py:280
  6.6 1.3 %collective-permute-start.1 = (bf16[256,128]{1,0:T(8,128)(2,1)}, bf16[256,128]{1,0:T(8,128)(2,1)S(1)}, u32[]{:S(2)}, u32[]{:S(2)}) collective-permute-start(bf16[256,128]{1,0:T(8,128)(2,1)} %get-tuple-element.67), channel_id=1, source_target_pairs={{0,24},{2,26},{4,28},{6,30},{8,16},{10,18},{12,20},{14,22},{16,8},... | collective-permute-start | bytes 196616 | tf_op jit(solution)/shard_map/ppermute | solution.py:280
  8.0 0.2 collective-permute-start.2
  8.2 0.0 copy-start
  8.2 0.9 %shard_map.85 = (bf16[128,256]{1,0:T(8,128)(2,1)S(1)}, bf16[128,256]{1,0:T(8,128)(2,1)S(1)}, bf16[128,256]{1,0:T(8,128)(2,1)S(1)}, bf16[128,256]{1,0:T(8,128)(2,1)S(1)}) custom-call(s32[2]{0:T(128)S(1)} %copy-done.4, bf16[4,64,256]{2,1,0:T(8,128)(2,1)S(1)} %bitcast.4, bf16[4,64,768]{2,1,0:T(8,128)(2,1)S(1)} %copy-done.2, bf16[256,768]{1,0:T(8,128)(2,1)S(1)} %copy-done.1), custom_call_target="tpu_custom_call" | custom-call | flops 1150000000 | tf_op jit(solution)/shard_map/pallas_call | solution.py:291
  9.1 2.9 %collective-permute-start.3 = (bf16[128,256]{1,0:T(8,128)(2,1)S(1)}, bf16[128,256]{1,0:T(8,128)(2,1)S(1)}, u32[]{:S(2)}, u32[]{:S(2)}) collective-permute-start(bf16[128,256]{1,0:T(8,128)(2,1)S(1)} %get-tuple-element.70), channel_id=1, source_target_pairs={{0,16},{2,18},{4,20},{6,22},{8,24},{10,26},{12,28},{14,30},{16,0},... | collective-permute-start | bytes 196616 | tf_op jit(solution)/shard_map/ppermute | solution.py:280
  12.0 1.3 %collective-permute-start.4 = (bf16[128,256]{1,0:T(8,128)(2,1)S(1)}, bf16[128,256]{1,0:T(8,128)(2,1)S(1)}, u32[]{:S(2)}, u32[]{:S(2)}) collective-permute-start(bf16[128,256]{1,0:T(8,128)(2,1)S(1)} %get-tuple-element.71), channel_id=1, source_target_pairs={{0,24},{2,26},{4,28},{6,30},{8,16},{10,18},{12,20},{14,22},{16,8},... | collective-permute-start | bytes 196616 | tf_op jit(solution)/shard_map/ppermute | solution.py:280
  13.3 0.0 collective-permute-done.refs_1_
  13.3 0.0 collective-permute-start.5
  13.3 0.0 collective-permute-done.1.refs_2_
  13.3 0.0 collective-permute-done.2.refs_3_
  13.4 1.6 %collective-permute-start.7 = (bf16[1024,128]{1,0:T(8,128)(2,1)S(1)}, bf16[1024,128]{1,0:T(8,128)(2,1)S(1)}, u32[]{:S(2)}, u32[]{:S(2)}) collective-permute-start(bf16[1024,128]{1,0:T(8,128)(2,1)S(1)} %shard_map.86.pair_ref), channel_id=1, source_target_pairs={{0,4},{2,6},{4,0},{6,2},{8,12},{10,14},{12,8},{14,10},{16,20},{18,... | collective-permute-start | bytes 786440 | tf_op jit(solution)/shard_map/ppermute | solution.py:280
  14.9 0.0 collective-permute-start.6
  15.0 2.2 %collective-permute-done.3.refs_1_ = bf16[128,256]{1,0:T(8,128)(2,1)S(1)} collective-permute-done((bf16[128,256]{1,0:T(8,128)(2,1)S(1)}, bf16[128,256]{1,0:T(8,128)(2,1)S(1)}, u32[]{:S(2)}, u32[]{:S(2)}) %collective-permute-start.3) | collective-permute-done | bytes 65568 | tf_op jit(solution)/shard_map/ppermute | solution.py:280
  17.2 1.0 %collective-permute-done.4.refs_2_ = bf16[128,256]{1,0:T(8,128)(2,1)S(1)} collective-permute-done((bf16[128,256]{1,0:T(8,128)(2,1)S(1)}, bf16[128,256]{1,0:T(8,128)(2,1)S(1)}, u32[]{:S(2)}, u32[]{:S(2)}) %collective-permute-start.4) | collective-permute-done | bytes 65568 | tf_op jit(solution)/shard_map/ppermute | solution.py:280
  18.2 0.3 collective-permute-done.5.refs_3_
  18.4 0.1 shard_map.87
  18.6 2.9 %shard_map.88 = (bf16[1024,1024]{1,0:T(8,128)(2,1)S(1)}, f32[1,1024]{1,0:T(1,128)S(1)}, f32[80,1024]{1,0:T(8,128)S(1)}, bf16[1024,128]{1,0:T(8,128)(2,1)S(1)}, bf16[64,1024]{1,0:T(8,128)(2,1)S(1)}) custom-call(bf16[1024,128]{1,0:T(8,128)(2,1)S(1)} %shard_map.86.pair_ref, bf16[256,1024]{1,0:T(8,128)(2,1)S(1)} %get-tuple-element.73.qa_ref, ...), custom_call_target="tpu_custom_call" | custom-call | flops 5750000128 | tf_op jit(solution)/shard_map/pallas_call | solution.py:317
  21.5 0.0 collective-permute-done.6.pair_ref
  21.5 2.9 %shard_map.89 = (bf16[1024,1024]{1,0:T(8,128)(2,1)S(1)}, f32[1,1024]{1,0:T(1,128)S(1)}, f32[80,1024]{1,0:T(8,128)S(1)}, bf16[1024,128]{1,0:T(8,128)(2,1)S(1)}, bf16[64,1024]{1,0:T(8,128)(2,1)S(1)}) custom-call(bf16[1024,128]{1,0:T(8,128)(2,1)S(1)} %collective-permute-done.6.pair_ref, bf16[256,1024]{1,0:T(8,128)(2,1)S(1)} %get-tuple-element.73.qa_ref, ...), custom_call_target="tpu_custom_call" | custom-call | flops 5750000128 | tf_op jit(solution)/shard_map/pallas_call | solution.py:317
  24.5 0.0 collective-permute-done.7.refs_0_
  24.5 0.1 collective-permute-start.8
  24.6 2.9 %shard_map.91 = (bf16[1024,1024]{1,0:T(8,128)(2,1)S(1)}, f32[1,1024]{1,0:T(1,128)S(1)}, f32[80,1024]{1,0:T(8,128)S(1)}, bf16[1024,128]{1,0:T(8,128)(2,1)S(1)}, bf16[64,1024]{1,0:T(8,128)(2,1)S(1)}) custom-call(bf16[1024,128]{1,0:T(8,128)(2,1)S(1)} %shard_map.90.pair_ref, bf16[256,1024]{1,0:T(8,128)(2,1)S(1)} %get-tuple-element.73.qa_ref, ...), custom_call_target="tpu_custom_call" | custom-call | flops 5750000128 | tf_op jit(solution)/shard_map/pallas_call | solution.py:317
  27.5 0.0 collective-permute-done.8.pair_ref
  27.5 3.1 %shard_map.92 = (bf16[1024,1024]{1,0:T(8,128)(2,1)S(1)}, f32[1,1024]{1,0:T(1,128)S(1)}, f32[80,1024]{1,0:T(8,128)S(1)}, bf16[1024,128]{1,0:T(8,128)(2,1)S(1)}, bf16[64,1024]{1,0:T(8,128)(2,1)S(1)}) custom-call(bf16[1024,128]{1,0:T(8,128)(2,1)S(1)} %collective-permute-done.8.pair_ref, bf16[256,1024]{1,0:T(8,128)(2,1)S(1)} %get-tuple-element.73.qa_ref, ...), custom_call_target="tpu_custom_call" | custom-call | flops 5750000128 | tf_op jit(solution)/shard_map/pallas_call | solution.py:317
  30.7 0.2 shard_map.93
  30.8 3.1 %collective-permute-start.9 = (bf16[64,256]{1,0:T(8,128)(2,1)S(1)}, bf16[64,256]{1,0:T(8,128)(2,1)S(1)}, u32[]{:S(2)}, u32[]{:S(2)}) collective-permute-start(bf16[64,256]{1,0:T(8,128)(2,1)S(1)} %get-tuple-element.104), channel_id=1, source_target_pairs={{0,16},{2,18},{4,20},{6,22},{8,24},{10,26},{12,28},{14,30},{16,0},... | collective-permute-start | bytes 98312 | tf_op jit(solution)/shard_map/ppermute | solution.py:280
  33.9 0.4 collective-permute-start.10
  34.3 0.2 collective-permute-start.11
  34.5 2.2 %shard_map.94 = (bf16[128,1024]{1,0:T(8,128)(2,1)S(1)}, f32[64,1024]{1,0:T(8,128)S(1)}) custom-call(bf16[1024,1024]{1,0:T(8,128)(2,1)S(1)} %get-tuple-element.98.exp_ref, bf16[1024,128]{1,0:T(8,128)(2,1)S(1)} %get-tuple-element.99.v_ref, bf16[64,1024]{1,0:T(8,128)(2,1)S(1)} %get-tuple-element.100.kt_ref, bf16[64,1024]{1,0:T(8,128)(2,1)S(1)} %get-tuple-element.78.q_ref, ...), custom_call_target="tpu_custom_call" | custom-call | flops 2300000000 | tf_op jit(solution)/shard_map/pallas_call | solution.py:363
  36.7 0.0 collective-permute-done.9.refs_1_
  36.7 2.9 %collective-permute-done.10.refs_2_ = bf16[64,256]{1,0:T(8,128)(2,1)S(1)} collective-permute-done((bf16[64,256]{1,0:T(8,128)(2,1)S(1)}, bf16[64,256]{1,0:T(8,128)(2,1)S(1)}, u32[]{:S(2)}, u32[]{:S(2)}) %collective-permute-start.10) | collective-permute-done | bytes 32800 | tf_op jit(solution)/shard_map/ppermute | solution.py:280
  39.6 0.8 %shard_map.95 = (bf16[2,64,768]{2,1,0:T(8,128)(2,1)S(1)}, bf16[2,64,768]{2,1,0:T(8,128)(2,1)S(1)}) custom-call(s32[2]{0:T(128)S(1)} %copy-done.4, bf16[256,768]{1,0:T(8,128)(2,1)S(1)} %copy-done.1, bf16[64,256]{1,0:T(8,128)(2,1)S(1)} %get-tuple-element.103.refs_0_, bf16[64,256]{1,0:T(8,128)(2,1)S(1)} %collective-permute-done.9.refs_1_, ...), custom_call_target="tpu_custom_call" | custom-call | flops 805000000 | tf_op jit(solution)/shard_map/pallas_call | solution.py:337
  40.4 0.1 collective-permute-start.12
  40.5 0.5 collective-permute-start.15
  41.0 0.8 %shard_map.96._.refs_4_ = bf16[256,768]{1,0:T(8,128)(2,1)S(1)} custom-call(s32[2]{0:T(128)S(1)} %copy-done.4, bf16[4,64,768]{2,1,0:T(8,128)(2,1)S(1)} %copy-done.2, bf16[64,256]{1,0:T(8,128)(2,1)S(1)} %get-tuple-element.103.refs_0_, bf16[64,256]{1,0:T(8,128)(2,1)S(1)} %collective-permute-done.9.refs_1_, bf16[64,256]{1,0:T(8,128)(2,1)S(1)} %collective-permute-done.10.refs_2_, ...), custom_call_target="tpu_custom_call" | custom-call | flops 805000000 | tf_op jit(solution)/shard_map/pallas_call | solution.py:343
  41.9 1.6 %collective-permute-start.17 = (bf16[256,768]{1,0:T(8,128)(2,1)S(1)}, bf16[256,768]{1,0:T(8,128)(2,1)S(1)}, u32[]{:S(2)}, u32[]{:S(2)}) collective-permute-start(bf16[256,768]{1,0:T(8,128)(2,1)S(1)} %shard_map.96._.refs_4_), channel_id=1, source_target_pairs={{0,1},{1,0},{2,3},{3,2},{4,5},{5,4},{6,7},{7,6},{8,9},{9,8},{10,11... | collective-permute-start | bytes 1179656 | tf_op jit(solution)/shard_map/ppermute | solution.py:280
  43.4 0.0 collective-permute-done.12.came_ref
  43.5 1.6 %collective-permute-start.13 = (bf16[64,768]{1,0:T(8,128)(2,1)S(1)}, bf16[64,768]{1,0:T(8,128)(2,1)S(1)}, u32[]{:S(2)}, u32[]{:S(2)}) collective-permute-start(bf16[64,768]{1,0:T(8,128)(2,1)S(1)} %get-tuple-element.112), channel_id=1, source_target_pairs={{0,4},{2,6},{4,0},{6,2},{8,12},{10,14},{12,8},{14,10},{16,20},{18,... | collective-permute-start | bytes 294920 | tf_op jit(solution)/shard_map/ppermute | solution.py:280
  45.1 2.2 %shard_map.98 = (bf16[128,1024]{1,0:T(8,128)(2,1)S(1)}, f32[64,1024]{1,0:T(8,128)S(1)}) custom-call(bf16[1024,1024]{1,0:T(8,128)(2,1)S(1)} %get-tuple-element.94.exp_ref, bf16[1024,128]{1,0:T(8,128)(2,1)S(1)} %get-tuple-element.95.v_ref, bf16[64,1024]{1,0:T(8,128)(2,1)S(1)} %get-tuple-element.96.kt_ref, bf16[64,1024]{1,0:T(8,128)(2,1)S(1)} %get-tuple-element.78.q_ref, ...), custom_call_target="tpu_custom_call" | custom-call | flops 2300000000 | tf_op jit(solution)/shard_map/pallas_call | solution.py:363
  47.2 0.1 shard_map.102
  47.3 0.6 collective-permute-start.16
  47.9 0.3 collective-permute-done.13.b_ref
  48.2 0.1 collective-permute-start.14
  48.3 2.2 %shard_map.100 = (bf16[128,1024]{1,0:T(8,128)(2,1)S(1)}, f32[64,1024]{1,0:T(8,128)S(1)}) custom-call(bf16[1024,1024]{1,0:T(8,128)(2,1)S(1)} %get-tuple-element.90.exp_ref, bf16[1024,128]{1,0:T(8,128)(2,1)S(1)} %get-tuple-element.91.v_ref, bf16[64,1024]{1,0:T(8,128)(2,1)S(1)} %get-tuple-element.92.kt_ref, bf16[64,1024]{1,0:T(8,128)(2,1)S(1)} %get-tuple-element.78.q_ref, ...), custom_call_target="tpu_custom_call" | custom-call | flops 2300000000 | tf_op jit(solution)/shard_map/pallas_call | solution.py:363
  50.4 0.1 collective-permute-start.18
  50.5 2.4 %collective-permute-done.14.b_ref = bf16[64,768]{1,0:T(8,128)(2,1)S(1)} collective-permute-done((bf16[64,768]{1,0:T(8,128)(2,1)S(1)}, bf16[64,768]{1,0:T(8,128)(2,1)S(1)}, u32[]{:S(2)}, u32[]{:S(2)}) %collective-permute-start.14) | collective-permute-done | bytes 98336 | tf_op jit(solution)/shard_map/ppermute | solution.py:280
  52.9 1.0 %collective-permute-start.22 = (bf16[64,768]{1,0:T(8,128)(2,1)S(1)}, bf16[64,768]{1,0:T(8,128)(2,1)S(1)}, u32[]{:S(2)}, u32[]{:S(2)}) collective-permute-start(bf16[64,768]{1,0:T(8,128)(2,1)S(1)} %shard_map.101.refs_1_.a_ref), channel_id=1, source_target_pairs={{0,16},{2,18},{4,20},{6,22},{8,24},{10,26},{12,28},{14,30},{16,0},... | collective-permute-start | bytes 294920 | tf_op jit(solution)/shard_map/ppermute | solution.py:280
  53.9 0.0 collective-permute-done.17.refs_3_.refs_5_
  53.9 1.2 %collective-permute-done.16.refs_2_.came_ref = bf16[128,1024]{1,0:T(8,128)(2,1)S(1)} collective-permute-done((bf16[128,1024]{1,0:T(8,128)(2,1)S(1)}, bf16[128,1024]{1,0:T(8,128)(2,1)S(1)}, u32[]{:S(2)}, u32[]{:S(2)}) %collective-permute-start.16) | collective-permute-done | bytes 262176 | tf_op jit(solution)/shard_map/ppermute | solution.py:280
  55.1 2.2 %shard_map.103 = (bf16[128,1024]{1,0:T(8,128)(2,1)S(1)}, f32[64,1024]{1,0:T(8,128)S(1)}) custom-call(bf16[1024,1024]{1,0:T(8,128)(2,1)S(1)} %get-tuple-element.75.exp_ref, bf16[1024,128]{1,0:T(8,128)(2,1)S(1)} %get-tuple-element.76.v_ref, bf16[64,1024]{1,0:T(8,128)(2,1)S(1)} %get-tuple-element.77.kt_ref, bf16[64,1024]{1,0:T(8,128)(2,1)S(1)} %get-tuple-element.78.q_ref, ...), custom_call_target="tpu_custom_call" | custom-call | flops 2300000000 | tf_op jit(solution)/shard_map/pallas_call | solution.py:363
  57.3 0.1 shard_map.104.kept_ref
  57.3 0.1 shard_map.105
  57.4 1.0 %collective-permute-start.19 = (bf16[192,256]{1,0:T(8,128)(2,1)S(1)}, bf16[192,256]{1,0:T(8,128)(2,1)S(1)}, u32[]{:S(2)}, u32[]{:S(2)}) collective-permute-start(bf16[192,256]{1,0:T(8,128)(2,1)S(1)} %get-tuple-element.119), channel_id=1, source_target_pairs={{0,16},{2,18},{4,20},{6,22},{8,24},{10,26},{12,28},{14,30},{16,0},... | collective-permute-start | bytes 294920 | tf_op jit(solution)/shard_map/ppermute | solution.py:280
  58.4 1.9 %collective-permute-start.20 = (bf16[192,256]{1,0:T(8,128)(2,1)S(1)}, bf16[192,256]{1,0:T(8,128)(2,1)S(1)}, u32[]{:S(2)}, u32[]{:S(2)}) collective-permute-start(bf16[192,256]{1,0:T(8,128)(2,1)S(1)} %get-tuple-element.120), channel_id=1, source_target_pairs={{0,24},{2,26},{4,28},{6,30},{8,16},{10,18},{12,20},{14,22},{16,8},... | collective-permute-start | bytes 294920 | tf_op jit(solution)/shard_map/ppermute | solution.py:280
  60.3 0.7 collective-permute-start.21
  61.0 0.9 %collective-permute-start.24 = (bf16[64,768]{1,0:T(8,128)(2,1)S(1)}, bf16[64,768]{1,0:T(8,128)(2,1)S(1)}, u32[]{:S(2)}, u32[]{:S(2)}) collective-permute-start(bf16[64,768]{1,0:T(8,128)(2,1)S(1)} %shard_map.107.refs_0_), channel_id=1, source_target_pairs={{0,4},{2,6},{4,0},{6,2},{8,12},{10,14},{12,8},{14,10},{16,20},{18,... | collective-permute-start | bytes 294920 | tf_op jit(solution)/shard_map/ppermute | solution.py:280
  61.9 4.6 %collective-permute-done.19.refs_1_ = bf16[192,256]{1,0:T(8,128)(2,1)S(1)} collective-permute-done((bf16[192,256]{1,0:T(8,128)(2,1)S(1)}, bf16[192,256]{1,0:T(8,128)(2,1)S(1)}, u32[]{:S(2)}, u32[]{:S(2)}) %collective-permute-start.19) | collective-permute-done | bytes 98336 | tf_op jit(solution)/shard_map/ppermute | solution.py:280
  66.6 0.2 collective-permute-done.21.refs_3_
  66.8 1.1 %shard_map.106 = (f32[1024,128]{1,0:T(8,128)}, f32[4,64,256]{2,1,0:T(8,128)}, bf16[256,768]{1,0:T(8,128)(2,1)}, f32[8,128]{1,0:T(8,128)S(1)}) custom-call(bf16[192,256]{1,0:T(8,128)(2,1)S(1)} %get-tuple-element.118.refs_0_, bf16[192,256]{1,0:T(8,128)(2,1)S(1)} %collective-permute-done.19.refs_1_, bf16[192,256]{1,0:T(8,128)(2,1)S(1)} %collective-permute-done.20.refs_2_, ...), custom_call_target="tpu_custom_call" | custom-call | flops 1150000000 | tf_op jit(solution)/shard_map/pallas_call | solution.py:385
  67.9 0.1 collective-permute-start.25
  68.0 1.3 %collective-permute-done.25.refs_3_ = bf16[64,768]{1,0:T(8,128)(2,1)S(1)} collective-permute-done((bf16[64,768]{1,0:T(8,128)(2,1)S(1)}, bf16[64,768]{1,0:T(8,128)(2,1)S(1)}, u32[]{:S(2)}, u32[]{:S(2)}) %collective-permute-start.25) | collective-permute-done | bytes 98336 | tf_op jit(solution)/shard_map/ppermute | solution.py:280
  69.3 0.9 %shard_map.109 = f32[4,64,768]{2,1,0:T(8,128)} custom-call(bf16[64,768]{1,0:T(8,128)(2,1)S(1)} %shard_map.107.refs_0_, bf16[64,768]{1,0:T(8,128)(2,1)S(1)} %collective-permute-done.23.refs_1_, bf16[64,768]{1,0:T(8,128)(2,1)S(1)} %shard_map.108.refs_2_, bf16[64,768]{1,0:T(8,128)(2,1)S(1)} %collective-permute-done.25.refs_3_), custom_call_target="tpu_custom_call" | custom-call | flops 575000000 | tf_op jit(solution)/shard_map/pallas_call | solution.py:394
  (24 shorter events, 0.2 us)
Async XLA Ops:
  0.6 7.6 %copy-start.1 = (bf16[256,768]{1,0:T(8,128)(2,1)S(1)}, bf16[256,768]{1,0:T(8,128)(2,1)}, u32[]{:S(2)}) copy-start(bf16[256,768]{1,0:T(8,128)(2,1)} %go_ref.3) | copy-start | bytes 1179652
  0.6 7.6 %copy-start.2 = (bf16[4,64,768]{2,1,0:T(8,128)(2,1)S(1)}, bf16[4,64,768]{2,1,0:T(8,128)(2,1)}, u32[]{:S(2)}) copy-start(bf16[4,64,768]{2,1,0:T(8,128)(2,1)} %w_ref.3) | copy-start | bytes 1179652
  0.7 7.5 %copy-start.3 = (bf16[256,4,64]{0,2,1:T(8,128)(2,1)S(1)}, bf16[256,4,64]{0,2,1:T(8,128)(2,1)}, u32[]{:S(2)}) copy-start(bf16[256,4,64]{0,2,1:T(8,128)(2,1)} %param.5) | copy-start | bytes 393220
  0.7 7.5 %copy-start.4 = (s32[2]{0:T(128)S(1)}, s32[2]{0:T(128)}, u32[]{:S(2)}) copy-start(s32[2]{0:T(128)} %fill_ref.7) | copy-start | bytes 28
  2.6 10.7 %collective-permute-start = (bf16[256,128]{1,0:T(8,128)(2,1)}, bf16[256,128]{1,0:T(8,128)(2,1)S(1)}, u32[]{:S(2)}, u32[]{:S(2)}) collective-permute-start(bf16[256,128]{1,0:T(8,128)(2,1)} %get-tuple-element.66), channel_id=1, source_target_pairs={{0,16},{2,18},{4,20},{6,22},{8,24},{10,26},{12,28},{14,30},{16,0},... | collective-permute-start | bytes 196616 | tf_op jit(solution)/shard_map/ppermute | solution.py:280
  6.6 6.7 %collective-permute-start.1 = (bf16[256,128]{1,0:T(8,128)(2,1)}, bf16[256,128]{1,0:T(8,128)(2,1)S(1)}, u32[]{:S(2)}, u32[]{:S(2)}) collective-permute-start(bf16[256,128]{1,0:T(8,128)(2,1)} %get-tuple-element.67), channel_id=1, source_target_pairs={{0,24},{2,26},{4,28},{6,30},{8,16},{10,18},{12,20},{14,22},{16,8},... | collective-permute-start | bytes 196616 | tf_op jit(solution)/shard_map/ppermute | solution.py:280
  8.0 5.4 %collective-permute-start.2 = (bf16[256,128]{1,0:T(8,128)(2,1)}, bf16[256,128]{1,0:T(8,128)(2,1)S(1)}, u32[]{:S(2)}, u32[]{:S(2)}) collective-permute-start(bf16[256,128]{1,0:T(8,128)(2,1)} %get-tuple-element.68), channel_id=1, source_target_pairs={{0,8},{2,10},{4,12},{6,14},{8,0},{10,2},{12,4},{14,6},{16,24},{18,... | collective-permute-start | bytes 196616 | tf_op jit(solution)/shard_map/ppermute | solution.py:280
  8.2 5.1 %copy-start = (bf16[256,128]{1,0:T(8,128)(2,1)S(1)}, bf16[256,128]{1,0:T(8,128)(2,1)}, u32[]{:S(2)}) copy-start(bf16[256,128]{1,0:T(8,128)(2,1)} %get-tuple-element.65.refs_0_) | copy-start | bytes 196612
  9.1 8.1 %collective-permute-start.3 = (bf16[128,256]{1,0:T(8,128)(2,1)S(1)}, bf16[128,256]{1,0:T(8,128)(2,1)S(1)}, u32[]{:S(2)}, u32[]{:S(2)}) collective-permute-start(bf16[128,256]{1,0:T(8,128)(2,1)S(1)} %get-tuple-element.70), channel_id=1, source_target_pairs={{0,16},{2,18},{4,20},{6,22},{8,24},{10,26},{12,28},{14,30},{16,0},... | collective-permute-start | bytes 196616 | tf_op jit(solution)/shard_map/ppermute | solution.py:280
  12.0 6.2 %collective-permute-start.4 = (bf16[128,256]{1,0:T(8,128)(2,1)S(1)}, bf16[128,256]{1,0:T(8,128)(2,1)S(1)}, u32[]{:S(2)}, u32[]{:S(2)}) collective-permute-start(bf16[128,256]{1,0:T(8,128)(2,1)S(1)} %get-tuple-element.71), channel_id=1, source_target_pairs={{0,24},{2,26},{4,28},{6,30},{8,16},{10,18},{12,20},{14,22},{16,8},... | collective-permute-start | bytes 196616 | tf_op jit(solution)/shard_map/ppermute | solution.py:280
  13.3 5.1 %collective-permute-start.5 = (bf16[128,256]{1,0:T(8,128)(2,1)S(1)}, bf16[128,256]{1,0:T(8,128)(2,1)S(1)}, u32[]{:S(2)}, u32[]{:S(2)}) collective-permute-start(bf16[128,256]{1,0:T(8,128)(2,1)S(1)} %get-tuple-element.72), channel_id=1, source_target_pairs={{0,8},{2,10},{4,12},{6,14},{8,0},{10,2},{12,4},{14,6},{16,24},{18,... | collective-permute-start | bytes 196616 | tf_op jit(solution)/shard_map/ppermute | solution.py:280
  13.4 11.1 %collective-permute-start.7 = (bf16[1024,128]{1,0:T(8,128)(2,1)S(1)}, bf16[1024,128]{1,0:T(8,128)(2,1)S(1)}, u32[]{:S(2)}, u32[]{:S(2)}) collective-permute-start(bf16[1024,128]{1,0:T(8,128)(2,1)S(1)} %shard_map.86.pair_ref), channel_id=1, source_target_pairs={{0,4},{2,6},{4,0},{6,2},{8,12},{10,14},{12,8},{14,10},{16,20},{18,... | collective-permute-start | bytes 786440 | tf_op jit(solution)/shard_map/ppermute | solution.py:280
  14.9 6.5 %collective-permute-start.6 = (bf16[1024,128]{1,0:T(8,128)(2,1)S(1)}, bf16[1024,128]{1,0:T(8,128)(2,1)S(1)}, u32[]{:S(2)}, u32[]{:S(2)}) collective-permute-start(bf16[1024,128]{1,0:T(8,128)(2,1)S(1)} %shard_map.86.pair_ref), channel_id=1, source_target_pairs={{0,2},{2,0},{4,6},{6,4},{8,10},{10,8},{12,14},{14,12},{16,18},{18,... | collective-permute-start | bytes 786440 | tf_op jit(solution)/shard_map/ppermute | solution.py:280
  24.5 3.0 %collective-permute-start.8 = (bf16[1024,128]{1,0:T(8,128)(2,1)S(1)}, bf16[1024,128]{1,0:T(8,128)(2,1)S(1)}, u32[]{:S(2)}, u32[]{:S(2)}) collective-permute-start(bf16[1024,128]{1,0:T(8,128)(2,1)S(1)} %shard_map.90.pair_ref), channel_id=1, source_target_pairs={{0,2},{2,0},{4,6},{6,4},{8,10},{10,8},{12,14},{14,12},{16,18},{18,... | collective-permute-start | bytes 786440 | tf_op jit(solution)/shard_map/ppermute | solution.py:280
  30.8 5.9 %collective-permute-start.9 = (bf16[64,256]{1,0:T(8,128)(2,1)S(1)}, bf16[64,256]{1,0:T(8,128)(2,1)S(1)}, u32[]{:S(2)}, u32[]{:S(2)}) collective-permute-start(bf16[64,256]{1,0:T(8,128)(2,1)S(1)} %get-tuple-element.104), channel_id=1, source_target_pairs={{0,16},{2,18},{4,20},{6,22},{8,24},{10,26},{12,28},{14,30},{16,0},... | collective-permute-start | bytes 98312 | tf_op jit(solution)/shard_map/ppermute | solution.py:280
  33.9 5.7 %collective-permute-start.10 = (bf16[64,256]{1,0:T(8,128)(2,1)S(1)}, bf16[64,256]{1,0:T(8,128)(2,1)S(1)}, u32[]{:S(2)}, u32[]{:S(2)}) collective-permute-start(bf16[64,256]{1,0:T(8,128)(2,1)S(1)} %get-tuple-element.105), channel_id=1, source_target_pairs={{0,24},{2,26},{4,28},{6,30},{8,16},{10,18},{12,20},{14,22},{16,8},... | collective-permute-start | bytes 98312 | tf_op jit(solution)/shard_map/ppermute | solution.py:280
  34.3 5.3 %collective-permute-start.11 = (bf16[64,256]{1,0:T(8,128)(2,1)S(1)}, bf16[64,256]{1,0:T(8,128)(2,1)S(1)}, u32[]{:S(2)}, u32[]{:S(2)}) collective-permute-start(bf16[64,256]{1,0:T(8,128)(2,1)S(1)} %get-tuple-element.106), channel_id=1, source_target_pairs={{0,8},{2,10},{4,12},{6,14},{8,0},{10,2},{12,4},{14,6},{16,24},{18,... | collective-permute-start | bytes 98312 | tf_op jit(solution)/shard_map/ppermute | solution.py:280
  40.4 3.0 %collective-permute-start.12 = (bf16[2,64,768]{2,1,0:T(8,128)(2,1)S(1)}, bf16[2,64,768]{2,1,0:T(8,128)(2,1)S(1)}, u32[]{:S(2)}, u32[]{:S(2)}) collective-permute-start(bf16[2,64,768]{2,1,0:T(8,128)(2,1)S(1)} %get-tuple-element.109.refs_4_), channel_id=1, source_target_pairs={{0,2},{2,0},{4,6},{6,4},{8,10},{10,8},{12,14},{14,12},{16,18},{18,... | collective-permute-start | bytes 589832 | tf_op jit(solution)/shard_map/ppermute | solution.py:280
  40.5 6.7 %collective-permute-start.15 = (bf16[128,1024]{1,0:T(8,128)(2,1)S(1)}, bf16[128,1024]{1,0:T(8,128)(2,1)S(1)}, u32[]{:S(2)}, u32[]{:S(2)}) collective-permute-start(bf16[128,1024]{1,0:T(8,128)(2,1)S(1)} %get-tuple-element.107.refs_4_), channel_id=1, source_target_pairs={{0,2},{2,0},{4,6},{6,4},{8,10},{10,8},{12,14},{14,12},{16,18},{18,... | collective-permute-start | bytes 786440 | tf_op jit(solution)/shard_map/ppermute | solution.py:280
  41.9 12.0 %collective-permute-start.17 = (bf16[256,768]{1,0:T(8,128)(2,1)S(1)}, bf16[256,768]{1,0:T(8,128)(2,1)S(1)}, u32[]{:S(2)}, u32[]{:S(2)}) collective-permute-start(bf16[256,768]{1,0:T(8,128)(2,1)S(1)} %shard_map.96._.refs_4_), channel_id=1, source_target_pairs={{0,1},{1,0},{2,3},{3,2},{4,5},{5,4},{6,7},{7,6},{8,9},{9,8},{10,11... | collective-permute-start | bytes 1179656 | tf_op jit(solution)/shard_map/ppermute | solution.py:280
  43.5 4.7 %collective-permute-start.13 = (bf16[64,768]{1,0:T(8,128)(2,1)S(1)}, bf16[64,768]{1,0:T(8,128)(2,1)S(1)}, u32[]{:S(2)}, u32[]{:S(2)}) collective-permute-start(bf16[64,768]{1,0:T(8,128)(2,1)S(1)} %get-tuple-element.112), channel_id=1, source_target_pairs={{0,4},{2,6},{4,0},{6,2},{8,12},{10,14},{12,8},{14,10},{16,20},{18,... | collective-permute-start | bytes 294920 | tf_op jit(solution)/shard_map/ppermute | solution.py:280
  47.3 7.8 %collective-permute-start.16 = (bf16[128,1024]{1,0:T(8,128)(2,1)S(1)}, bf16[128,1024]{1,0:T(8,128)(2,1)S(1)}, u32[]{:S(2)}, u32[]{:S(2)}) collective-permute-start(bf16[128,1024]{1,0:T(8,128)(2,1)S(1)} %shard_map.102), channel_id=1, source_target_pairs={{0,4},{2,6},{4,0},{6,2},{8,12},{10,14},{12,8},{14,10},{16,20},{18,... | collective-permute-start | bytes 786440 | tf_op jit(solution)/shard_map/ppermute | solution.py:280
  48.2 4.7 %collective-permute-start.14 = (bf16[64,768]{1,0:T(8,128)(2,1)S(1)}, bf16[64,768]{1,0:T(8,128)(2,1)S(1)}, u32[]{:S(2)}, u32[]{:S(2)}) collective-permute-start(bf16[64,768]{1,0:T(8,128)(2,1)S(1)} %shard_map.99.refs_1_.a_ref), channel_id=1, source_target_pairs={{0,8},{2,10},{4,12},{6,14},{8,0},{10,2},{12,4},{14,6},{16,24},{18,... | collective-permute-start | bytes 294920 | tf_op jit(solution)/shard_map/ppermute | solution.py:280
  50.4 6.8 %collective-permute-start.18 = (bf16[128,1024]{1,0:T(8,128)(2,1)S(1)}, bf16[128,1024]{1,0:T(8,128)(2,1)S(1)}, u32[]{:S(2)}, u32[]{:S(2)}) collective-permute-start(bf16[128,1024]{1,0:T(8,128)(2,1)S(1)} %get-tuple-element.115.refs_0_), channel_id=1, source_target_pairs={{0,2},{2,0},{4,6},{6,4},{8,10},{10,8},{12,14},{14,12},{16,18},{18,... | collective-permute-start | bytes 786440 | tf_op jit(solution)/shard_map/ppermute | solution.py:280
  52.9 8.1 %collective-permute-start.22 = (bf16[64,768]{1,0:T(8,128)(2,1)S(1)}, bf16[64,768]{1,0:T(8,128)(2,1)S(1)}, u32[]{:S(2)}, u32[]{:S(2)}) collective-permute-start(bf16[64,768]{1,0:T(8,128)(2,1)S(1)} %shard_map.101.refs_1_.a_ref), channel_id=1, source_target_pairs={{0,16},{2,18},{4,20},{6,22},{8,24},{10,26},{12,28},{14,30},{16,0},... | collective-permute-start | bytes 294920 | tf_op jit(solution)/shard_map/ppermute | solution.py:280
  57.4 9.1 %collective-permute-start.19 = (bf16[192,256]{1,0:T(8,128)(2,1)S(1)}, bf16[192,256]{1,0:T(8,128)(2,1)S(1)}, u32[]{:S(2)}, u32[]{:S(2)}) collective-permute-start(bf16[192,256]{1,0:T(8,128)(2,1)S(1)} %get-tuple-element.119), channel_id=1, source_target_pairs={{0,16},{2,18},{4,20},{6,22},{8,24},{10,26},{12,28},{14,30},{16,0},... | collective-permute-start | bytes 294920 | tf_op jit(solution)/shard_map/ppermute | solution.py:280
  58.4 8.2 %collective-permute-start.20 = (bf16[192,256]{1,0:T(8,128)(2,1)S(1)}, bf16[192,256]{1,0:T(8,128)(2,1)S(1)}, u32[]{:S(2)}, u32[]{:S(2)}) collective-permute-start(bf16[192,256]{1,0:T(8,128)(2,1)S(1)} %get-tuple-element.120), channel_id=1, source_target_pairs={{0,24},{2,26},{4,28},{6,30},{8,16},{10,18},{12,20},{14,22},{16,8},... | collective-permute-start | bytes 294920 | tf_op jit(solution)/shard_map/ppermute | solution.py:280
  60.3 6.5 %collective-permute-start.21 = (bf16[192,256]{1,0:T(8,128)(2,1)S(1)}, bf16[192,256]{1,0:T(8,128)(2,1)S(1)}, u32[]{:S(2)}, u32[]{:S(2)}) collective-permute-start(bf16[192,256]{1,0:T(8,128)(2,1)S(1)} %get-tuple-element.121), channel_id=1, source_target_pairs={{0,8},{2,10},{4,12},{6,14},{8,0},{10,2},{12,4},{14,6},{16,24},{18,... | collective-permute-start | bytes 294920 | tf_op jit(solution)/shard_map/ppermute | solution.py:280
  61.0 6.9 %collective-permute-start.24 = (bf16[64,768]{1,0:T(8,128)(2,1)S(1)}, bf16[64,768]{1,0:T(8,128)(2,1)S(1)}, u32[]{:S(2)}, u32[]{:S(2)}) collective-permute-start(bf16[64,768]{1,0:T(8,128)(2,1)S(1)} %shard_map.107.refs_0_), channel_id=1, source_target_pairs={{0,4},{2,6},{4,0},{6,2},{8,12},{10,14},{12,8},{14,10},{16,20},{18,... | collective-permute-start | bytes 294920 | tf_op jit(solution)/shard_map/ppermute | solution.py:280
  61.9 6.1 %collective-permute-start.23 = (bf16[64,768]{1,0:T(8,128)(2,1)S(1)}, bf16[64,768]{1,0:T(8,128)(2,1)S(1)}, u32[]{:S(2)}, u32[]{:S(2)}) collective-permute-start(bf16[64,768]{1,0:T(8,128)(2,1)S(1)} %shard_map.107.refs_0_), channel_id=1, source_target_pairs={{0,2},{2,0},{4,6},{6,4},{8,10},{10,8},{12,14},{14,12},{16,18},{18,... | collective-permute-start | bytes 294920 | tf_op jit(solution)/shard_map/ppermute | solution.py:280
  67.9 1.4 %collective-permute-start.25 = (bf16[64,768]{1,0:T(8,128)(2,1)S(1)}, bf16[64,768]{1,0:T(8,128)(2,1)S(1)}, u32[]{:S(2)}, u32[]{:S(2)}) collective-permute-start(bf16[64,768]{1,0:T(8,128)(2,1)S(1)} %shard_map.108.refs_2_), channel_id=1, source_target_pairs={{0,2},{2,0},{4,6},{6,4},{8,10},{10,8},{12,14},{14,12},{16,18},{18,... | collective-permute-start | bytes 294920 | tf_op jit(solution)/shard_map/ppermute | solution.py:280

commit v15 on v14

--- a/solution.py
+++ b/solution.py
@@ -28,7 +28,7 @@
 
 
 def call(kernel, outs, scratch=(), n_in=1, smem_first=False, after=0, micros=0.01, limit=16):
-    specs = [SMEM if smem_first else VMEM] + [VMEM] * (n_in - 1) + [pl.BlockSpec(memory_space=pl.ANY)] * after
+    specs = ([SMEM if smem_first else VMEM] + [VMEM] * (n_in - 1))[:n_in] + [pl.BlockSpec(memory_space=pl.ANY)] * after
     return pl.pallas_call(
         kernel,
         out_shape=[jax.ShapeDtypeStruct(shape, kind) for shape, kind in outs],
@@ -204,32 +204,25 @@
     dkv_ref[0:dim, :] = grad_k.astype(BF16)
 
 
-def project_grad_kernel(slots, rows, a_of, b_of, halves, fill_ref, go_ref, *refs):
+def project_kernel(slots, rows, a_of, b_of, halves, fill_ref, go_ref, w_ref, *refs):
     att, refs = refs[:slots], refs[slots + 1 :]
+    terms_ref, held = refs[0], refs[-1]
     me = a_of()
-    held = refs[-1]
     dim = held.shape[1]
-    live = live_row(fill_ref, rows).astype(BF16)
-    grads = dot(jnp.concatenate([ref[...] * live for ref in att], axis=0), go_ref[...]).astype(BF16)
+    stacked = jnp.concatenate([ref[...].astype(F32) for ref in att], axis=0) * live_row(fill_ref, rows)
+    grads = dot(stacked.astype(BF16), go_ref[...]).astype(BF16)
     for slot, mask in enumerate(spread(slots)):
         held[me ^ mask] = grads[slot * dim : (slot + 1) * dim, :]
+    weights = jnp.concatenate([w_ref[me ^ mask] for mask in spread(slots)], axis=0)
+    terms_ref[...] = dot(stacked.T.astype(BF16), weights).astype(BF16)
     if not halves:
-        refs[0][...] = held[...]
+        refs[1][...] = held[...]
         return
     me = b_of()
-    kept_ref, sent_ref = refs[0], refs[1]
+    kept_ref, sent_ref = refs[1], refs[2]
     for pair in range(slots // 2):
         kept_ref[pair] = held[me ^ (2 * pair)]
         sent_ref[pair] = held[me ^ (2 * pair) ^ 1]
-
-
-def project_kernel(slots, rows, a_of, fill_ref, w_ref, *refs):
-    att, terms_ref = refs[:slots], refs[-1]
-    me = a_of()
-    live = live_row(fill_ref, rows)
-    rows_in = jnp.concatenate([ref[...].astype(F32) * live for ref in att], axis=0).T.astype(BF16)
-    weights = jnp.concatenate([w_ref[me ^ mask] for mask in spread(slots)], axis=0)
-    terms_ref[...] = dot(rows_in, weights).astype(BF16)
 
 
 def add_pairs_kernel(kept_ref, came_ref, _, first_ref, second_ref):
@@ -250,14 +243,17 @@
 
 
 def unpack_kernel(slots, rows, dim, a_of, *refs):
-    pieces, (a_ref, b_ref, kv_out, q_out, sum_out, done_ref) = refs[:slots], refs[slots:]
+    pieces, (a_ref, b_ref, _, kv_out, q_out, sum_out) = refs[:slots], refs[slots:]
     sum_out[...] = (a_ref[...].astype(F32) + b_ref[...].astype(F32)).astype(BF16)
-    done_ref[...] = jnp.zeros_like(done_ref)
     wide = 2 * dim
     me = a_of()
     for slot, mask in enumerate(spread(slots)):
         kv_out[pl.ds(me ^ mask, rows, stride=slots), :] = pieces[slot][0:wide, :].astype(F32).T
         q_out[me ^ mask] = pieces[slot][wide:, :].astype(F32)
+
+
+def token_kernel(*refs):
+    refs[-1][...] = jnp.zeros_like(refs[-1])
 
 
 def place_kernel(columns, b_of, *refs):
@@ -334,24 +330,20 @@
     dkv, dq, kept, summed, later = {}, None, None, {}, []
     for at, r in enumerate(order):
         if at and not halves and at == columns - 1 or halves and at == 1:
-            weight_terms = call(
-                functools.partial(project_grad_kernel, slots, rows, a_of, b_of, halves),
-                [((2, dim, width), BF16)] * 2 if halves else [((heads, dim, width), BF16)],
+            terms, *weight_terms = call(
+                functools.partial(project_kernel, slots, rows, a_of, b_of, halves),
+                [((rows, width), BF16)] + ([((2, dim, width), BF16)] * 2 if halves else [((heads, dim, width), BF16)]),
                 [pltpu.VMEM((heads, dim, width), BF16)],
-                n_in=2 + slots, smem_first=True, after=1, micros=0.7,
-            )(tile_fill, grad_output, *att_mine, dkv[order[at - 1]])
-            terms = call(
-                functools.partial(project_kernel, slots, rows, a_of), [((rows, width), BF16)],
-                n_in=2 + slots, smem_first=True, after=1, micros=0.7,
-            )(tile_fill, out_weight, *att_mine, weight_terms[-1])[0]
-            later, bit, first_terms = [terms], 1, terms
+                n_in=3 + slots, smem_first=True, after=1, micros=0.7,
+            )(tile_fill, grad_output, out_weight, *att_mine, dkv[order[at - 1]])
+            later, bit = [terms], 1
             while bit < mp // 2:
                 terms = call(add_kernel, [((rows, width), BF16)], n_in=2)(terms, swap(terms, bit, "mp", mp))[0]
                 bit *= 2
             terms_came = swap(terms, bit, "mp", mp)
             if halves:
                 kept, sent = call(add_pairs_kernel, [((dim, width), BF16)] * 2, n_in=2, after=1)(
-                    weight_terms[0], swap(weight_terms[1], 1), first_terms)
+                    weight_terms[0], swap(weight_terms[1], 1), weight_terms[0])
                 later = [kept]
         if at == 2 and halves:
             kept = add(kept, swap(sent, 2), dkv[order[at - 1]])[0]
@@ -382,20 +374,22 @@
     )(*halved, dq)
     returned = exchange(pieces)
 
-    key_value_grad, query_grad, attention_out, done = call(
-        functools.partial(unpack_kernel, slots, rows, dim, a_of),
-        [((rows * heads, wide), F32), ((heads, dim, rows), F32), ((rows, width), BF16), ((8, 128), F32)],
-        n_in=slots + 2, micros=1,
-    )(*returned, terms, terms_came)
+    arrived = call(token_kernel, [((8, 128), F32)], n_in=0, after=slots)(*returned)[0]
     if halves:
         for mask in z_masks[1:]:
             kept = add(kept, swap(kept, mask), pieces[0])[0]
-        across = call(functools.partial(join_kernel, 1), [((dim, width), BF16)], after=1)(swap(kept, 2), done)[0]
+        across = call(functools.partial(join_kernel, 1), [((dim, width), BF16)], after=1)(swap(kept, 2), arrived)[0]
         weight_grad = call(
             functools.partial(place_kernel, columns, b_of), [((heads, dim, width), F32)], n_in=columns, micros=0.5,
         )(kept, swap(kept, 1), across, swap(across, 1))[0]
+        arrived = across
     else:
         weight_grad = lax.psum(weight_terms[0].astype(F32), "seq")
+    key_value_grad, query_grad, attention_out = call(
+        functools.partial(unpack_kernel, slots, rows, dim, a_of),
+        [((rows * heads, wide), F32), ((heads, dim, rows), F32), ((rows, width), BF16)],
+        n_in=slots + 2, after=1, micros=5,
+    )(*returned, terms, terms_came, arrived)
     return attention_out, jnp.transpose(query_grad, (2, 0, 1)), key_value_grad.reshape(rows, heads, wide), weight_grad
 
 

time: 70.4 us -> 68.4 us (0.972)
  waiting for transfers between devices: 16.4 us -> 15.3 us
  Pallas kernels: 27.7 us -> 26.9 us
    ppermute x26, waiting for transfers between devices: 16.4 us -> 15.3 us  [swap(): return lax.ppermute(array, axis, [(i, i ^ mask) for i in range(size)])]
    pallas_call x2, Pallas kernels: 1.68 us -> 0.92 us  [the longest x1 0.92 us: shards(): call(functools.partial(project_kernel, slots, rows, a_of, b_of, halves),...]
  transfers between devices with their start and end apart: 26 -> 26, of which waited for: 10 -> 10; matrix products, arithmetic and copies ran while one was open for 0% -> 0% of each run, Pallas kernels for 30% -> 29%
where the time goes in v15:
time: 68.4 us; the launch traced here: 68.3 us
  Pallas kernels  26.9 us (39%)
  starting transfers between devices  25.1 us (37%)
  waiting for transfers between devices  15.3 us (22%)
  between operations  0.94 us (1%)
    ppermute x26, starting transfers between devices, swap(): return lax.ppermute(array, axis, [(i, i ^ mask) for i in range(size)])  25.1 us
    ppermute x26, waiting for transfers between devices, swap(): return lax.ppermute(array, axis, [(i, i ^ mask) for i in range(size)])  15.3 us
    pallas_call x4, Pallas kernels, shards(): call(functools.partial(score_kernel, slots, rows, dim, step), [((block, b...  11.9 us
    pallas_call x4, Pallas kernels, shards(): call(functools.partial(back_kernel, slots, rows, dim, dq is None), [((wid...  8.68 us
    pallas_call x1, Pallas kernels, shards(): call(functools.partial(pack_kv_kernel, heads, rows, dim, a_of), [((rows,...  1.9 us
  transfers between devices with their start and end apart: 26, of which 10 were waited for; matrix products, arithmetic and copies ran while one was open for 0% of the time, Pallas kernels for 29%

profile of v15, /device:TPU:0, one launch (start us, length us, event | category | flops | bytes accessed | tf_op | source)
XLA Modules:
  0.0 68.3 jit_solution(4221457052802915380)
XLA Ops:
  0.7 1.9 %shard_map.84 = (bf16[256,128]{1,0:T(8,128)(2,1)}, bf16[256,128]{1,0:T(8,128)(2,1)}, bf16[256,128]{1,0:T(8,128)(2,1)}, bf16[256,128]{1,0:T(8,128)(2,1)}) custom-call(s32[2]{0:T(128)} %fill_ref.5, bf16[1024,128]{1,0:T(8,128)(2,1)} %bitcast.5), custom_call_target="tpu_custom_call" | custom-call | flops 1724999936 | tf_op jit(solution)/shard_map/pallas_call | solution.py:282
  2.6 4.0 %collective-permute-start = (bf16[256,128]{1,0:T(8,128)(2,1)}, bf16[256,128]{1,0:T(8,128)(2,1)S(1)}, u32[]{:S(2)}, u32[]{:S(2)}) collective-permute-start(bf16[256,128]{1,0:T(8,128)(2,1)} %get-tuple-element.66), channel_id=1, source_target_pairs={{0,16},{2,18},{4,20},{6,22},{8,24},{10,26},{12,28},{14,30},{16,0},... | collective-permute-start | bytes 196616 | tf_op jit(solution)/shard_map/ppermute | solution.py:276
  6.6 1.3 %collective-permute-start.1 = (bf16[256,128]{1,0:T(8,128)(2,1)}, bf16[256,128]{1,0:T(8,128)(2,1)S(1)}, u32[]{:S(2)}, u32[]{:S(2)}) collective-permute-start(bf16[256,128]{1,0:T(8,128)(2,1)} %get-tuple-element.67), channel_id=1, source_target_pairs={{0,24},{2,26},{4,28},{6,30},{8,16},{10,18},{12,20},{14,22},{16,8},... | collective-permute-start | bytes 196616 | tf_op jit(solution)/shard_map/ppermute | solution.py:276
  8.0 0.2 collective-permute-start.2
  8.2 0.0 copy-start
  8.2 0.9 %shard_map.85 = (bf16[128,256]{1,0:T(8,128)(2,1)S(1)}, bf16[128,256]{1,0:T(8,128)(2,1)S(1)}, bf16[128,256]{1,0:T(8,128)(2,1)S(1)}, bf16[128,256]{1,0:T(8,128)(2,1)S(1)}) custom-call(s32[2]{0:T(128)S(1)} %copy-done.4, bf16[4,64,256]{2,1,0:T(8,128)(2,1)S(1)} %bitcast.4, bf16[4,64,768]{2,1,0:T(8,128)(2,1)S(1)} %copy-done.1, bf16[256,768]{1,0:T(8,128)(2,1)S(1)} %copy-done.2), custom_call_target="tpu_custom_call" | custom-call | flops 1150000000 | tf_op jit(solution)/shard_map/pallas_call | solution.py:287
  9.1 2.9 %collective-permute-start.3 = (bf16[128,256]{1,0:T(8,128)(2,1)S(1)}, bf16[128,256]{1,0:T(8,128)(2,1)S(1)}, u32[]{:S(2)}, u32[]{:S(2)}) collective-permute-start(bf16[128,256]{1,0:T(8,128)(2,1)S(1)} %get-tuple-element.70), channel_id=1, source_target_pairs={{0,16},{2,18},{4,20},{6,22},{8,24},{10,26},{12,28},{14,30},{16,0},... | collective-permute-start | bytes 196616 | tf_op jit(solution)/shard_map/ppermute | solution.py:276
  12.0 1.3 %collective-permute-start.4 = (bf16[128,256]{1,0:T(8,128)(2,1)S(1)}, bf16[128,256]{1,0:T(8,128)(2,1)S(1)}, u32[]{:S(2)}, u32[]{:S(2)}) collective-permute-start(bf16[128,256]{1,0:T(8,128)(2,1)S(1)} %get-tuple-element.71), channel_id=1, source_target_pairs={{0,24},{2,26},{4,28},{6,30},{8,16},{10,18},{12,20},{14,22},{16,8},... | collective-permute-start | bytes 196616 | tf_op jit(solution)/shard_map/ppermute | solution.py:276
  13.3 0.0 collective-permute-done.refs_1_
  13.3 0.0 collective-permute-start.5
  13.3 0.0 collective-permute-done.1.refs_2_
  13.3 0.0 collective-permute-done.2.refs_3_
  13.4 1.6 %collective-permute-start.7 = (bf16[1024,128]{1,0:T(8,128)(2,1)S(1)}, bf16[1024,128]{1,0:T(8,128)(2,1)S(1)}, u32[]{:S(2)}, u32[]{:S(2)}) collective-permute-start(bf16[1024,128]{1,0:T(8,128)(2,1)S(1)} %shard_map.86.pair_ref), channel_id=1, source_target_pairs={{0,4},{2,6},{4,0},{6,2},{8,12},{10,14},{12,8},{14,10},{16,20},{18,... | collective-permute-start | bytes 786440 | tf_op jit(solution)/shard_map/ppermute | solution.py:276
  14.9 0.0 collective-permute-start.6
  15.0 2.2 %collective-permute-done.3.refs_1_ = bf16[128,256]{1,0:T(8,128)(2,1)S(1)} collective-permute-done((bf16[128,256]{1,0:T(8,128)(2,1)S(1)}, bf16[128,256]{1,0:T(8,128)(2,1)S(1)}, u32[]{:S(2)}, u32[]{:S(2)}) %collective-permute-start.3) | collective-permute-done | bytes 65568 | tf_op jit(solution)/shard_map/ppermute | solution.py:276
  17.2 1.0 %collective-permute-done.4.refs_2_ = bf16[128,256]{1,0:T(8,128)(2,1)S(1)} collective-permute-done((bf16[128,256]{1,0:T(8,128)(2,1)S(1)}, bf16[128,256]{1,0:T(8,128)(2,1)S(1)}, u32[]{:S(2)}, u32[]{:S(2)}) %collective-permute-start.4) | collective-permute-done | bytes 65568 | tf_op jit(solution)/shard_map/ppermute | solution.py:276
  18.2 0.3 collective-permute-done.5.refs_3_
  18.4 0.1 shard_map.87
  18.5 2.9 %shard_map.88 = (bf16[1024,1024]{1,0:T(8,128)(2,1)S(1)}, f32[1,1024]{1,0:T(1,128)S(1)}, f32[80,1024]{1,0:T(8,128)S(1)}, bf16[1024,128]{1,0:T(8,128)(2,1)S(1)}, bf16[64,1024]{1,0:T(8,128)(2,1)S(1)}) custom-call(bf16[1024,128]{1,0:T(8,128)(2,1)S(1)} %shard_map.86.pair_ref, bf16[256,1024]{1,0:T(8,128)(2,1)S(1)} %get-tuple-element.73.qa_ref, ...), custom_call_target="tpu_custom_call" | custom-call | flops 5750000128 | tf_op jit(solution)/shard_map/pallas_call | solution.py:313
  21.5 0.0 collective-permute-done.6.pair_ref
  21.5 2.9 %shard_map.89 = (bf16[1024,1024]{1,0:T(8,128)(2,1)S(1)}, f32[1,1024]{1,0:T(1,128)S(1)}, f32[80,1024]{1,0:T(8,128)S(1)}, bf16[1024,128]{1,0:T(8,128)(2,1)S(1)}, bf16[64,1024]{1,0:T(8,128)(2,1)S(1)}) custom-call(bf16[1024,128]{1,0:T(8,128)(2,1)S(1)} %collective-permute-done.6.pair_ref, bf16[256,1024]{1,0:T(8,128)(2,1)S(1)} %get-tuple-element.73.qa_ref, ...), custom_call_target="tpu_custom_call" | custom-call | flops 5750000128 | tf_op jit(solution)/shard_map/pallas_call | solution.py:313
  24.4 0.0 collective-permute-done.7.refs_0_
  24.5 0.1 collective-permute-start.8
  24.6 2.9 %shard_map.91 = (bf16[1024,1024]{1,0:T(8,128)(2,1)S(1)}, f32[1,1024]{1,0:T(1,128)S(1)}, f32[80,1024]{1,0:T(8,128)S(1)}, bf16[1024,128]{1,0:T(8,128)(2,1)S(1)}, bf16[64,1024]{1,0:T(8,128)(2,1)S(1)}) custom-call(bf16[1024,128]{1,0:T(8,128)(2,1)S(1)} %shard_map.90.pair_ref, bf16[256,1024]{1,0:T(8,128)(2,1)S(1)} %get-tuple-element.73.qa_ref, ...), custom_call_target="tpu_custom_call" | custom-call | flops 5750000128 | tf_op jit(solution)/shard_map/pallas_call | solution.py:313
  27.5 0.0 collective-permute-done.8.pair_ref
  27.5 3.1 %shard_map.92 = (bf16[1024,1024]{1,0:T(8,128)(2,1)S(1)}, f32[1,1024]{1,0:T(1,128)S(1)}, f32[80,1024]{1,0:T(8,128)S(1)}, bf16[1024,128]{1,0:T(8,128)(2,1)S(1)}, bf16[64,1024]{1,0:T(8,128)(2,1)S(1)}) custom-call(bf16[1024,128]{1,0:T(8,128)(2,1)S(1)} %collective-permute-done.8.pair_ref, bf16[256,1024]{1,0:T(8,128)(2,1)S(1)} %get-tuple-element.73.qa_ref, ...), custom_call_target="tpu_custom_call" | custom-call | flops 5750000128 | tf_op jit(solution)/shard_map/pallas_call | solution.py:313
  30.6 0.2 shard_map.93
  30.8 3.1 %collective-permute-start.9 = (bf16[64,256]{1,0:T(8,128)(2,1)S(1)}, bf16[64,256]{1,0:T(8,128)(2,1)S(1)}, u32[]{:S(2)}, u32[]{:S(2)}) collective-permute-start(bf16[64,256]{1,0:T(8,128)(2,1)S(1)} %get-tuple-element.104), channel_id=1, source_target_pairs={{0,16},{2,18},{4,20},{6,22},{8,24},{10,26},{12,28},{14,30},{16,0},... | collective-permute-start | bytes 98312 | tf_op jit(solution)/shard_map/ppermute | solution.py:276
  33.9 0.4 collective-permute-start.10
  34.3 0.2 collective-permute-start.11
  34.5 2.2 %shard_map.94 = (bf16[128,1024]{1,0:T(8,128)(2,1)S(1)}, f32[64,1024]{1,0:T(8,128)S(1)}) custom-call(bf16[1024,1024]{1,0:T(8,128)(2,1)S(1)} %get-tuple-element.98.exp_ref, bf16[1024,128]{1,0:T(8,128)(2,1)S(1)} %get-tuple-element.99.v_ref, bf16[64,1024]{1,0:T(8,128)(2,1)S(1)} %get-tuple-element.100.kt_ref, bf16[64,1024]{1,0:T(8,128)(2,1)S(1)} %get-tuple-element.78.q_ref, ...), custom_call_target="tpu_custom_call" | custom-call | flops 2300000000 | tf_op jit(solution)/shard_map/pallas_call | solution.py:355
  36.7 2.9 %collective-permute-done.10.refs_2_ = bf16[64,256]{1,0:T(8,128)(2,1)S(1)} collective-permute-done((bf16[64,256]{1,0:T(8,128)(2,1)S(1)}, bf16[64,256]{1,0:T(8,128)(2,1)S(1)}, u32[]{:S(2)}, u32[]{:S(2)}) %collective-permute-start.10) | collective-permute-done | bytes 32800 | tf_op jit(solution)/shard_map/ppermute | solution.py:276
  39.6 0.9 %shard_map.95 = (bf16[256,768]{1,0:T(8,128)(2,1)S(1)}, bf16[2,64,768]{2,1,0:T(8,128)(2,1)S(1)}, bf16[2,64,768]{2,1,0:T(8,128)(2,1)S(1)}) custom-call(s32[2]{0:T(128)S(1)} %copy-done.4, bf16[256,768]{1,0:T(8,128)(2,1)S(1)} %copy-done.2, bf16[4,64,768]{2,1,0:T(8,128)(2,1)S(1)} %copy-done.1, bf16[64,256]{1,0:T(8,128)(2,1)S(1)} %get-tuple-element.103.refs_0_, ...), custom_call_target="tpu_custom_call" | custom-call | flops 805000000 | tf_op jit(solution)/shard_map/pallas_call | solution.py:333
  40.5 0.1 collective-permute-start.12
  40.6 0.5 collective-permute-start.15
  41.1 1.5 %collective-permute-start.17 = (bf16[256,768]{1,0:T(8,128)(2,1)S(1)}, bf16[256,768]{1,0:T(8,128)(2,1)S(1)}, u32[]{:S(2)}, u32[]{:S(2)}) collective-permute-start(bf16[256,768]{1,0:T(8,128)(2,1)S(1)} %get-tuple-element.116.refs_4_), channel_id=1, source_target_pairs={{0,1},{1,0},{2,3},{3,2},{4,5},{5,4},{6,7},{7,6},{8,9},{9,8},{10,11... | collective-permute-start | bytes 1179656 | tf_op jit(solution)/shard_map/ppermute | solution.py:276
  42.6 1.6 %collective-permute-start.13 = (bf16[64,768]{1,0:T(8,128)(2,1)S(1)}, bf16[64,768]{1,0:T(8,128)(2,1)S(1)}, u32[]{:S(2)}, u32[]{:S(2)}) collective-permute-start(bf16[64,768]{1,0:T(8,128)(2,1)S(1)} %get-tuple-element.112), channel_id=1, source_target_pairs={{0,4},{2,6},{4,0},{6,2},{8,12},{10,14},{12,8},{14,10},{16,20},{18,... | collective-permute-start | bytes 294920 | tf_op jit(solution)/shard_map/ppermute | solution.py:276
  44.2 2.2 %shard_map.97 = (bf16[128,1024]{1,0:T(8,128)(2,1)S(1)}, f32[64,1024]{1,0:T(8,128)S(1)}) custom-call(bf16[1024,1024]{1,0:T(8,128)(2,1)S(1)} %get-tuple-element.94.exp_ref, bf16[1024,128]{1,0:T(8,128)(2,1)S(1)} %get-tuple-element.95.v_ref, bf16[64,1024]{1,0:T(8,128)(2,1)S(1)} %get-tuple-element.96.kt_ref, bf16[64,1024]{1,0:T(8,128)(2,1)S(1)} %get-tuple-element.78.q_ref, ...), custom_call_target="tpu_custom_call" | custom-call | flops 2300000000 | tf_op jit(solution)/shard_map/pallas_call | solution.py:355
  46.4 0.1 shard_map.101
  46.5 0.6 collective-permute-start.16
  47.1 0.3 collective-permute-done.13.b_ref
  47.3 0.1 collective-permute-start.14
  47.4 2.2 %shard_map.99 = (bf16[128,1024]{1,0:T(8,128)(2,1)S(1)}, f32[64,1024]{1,0:T(8,128)S(1)}) custom-call(bf16[1024,1024]{1,0:T(8,128)(2,1)S(1)} %get-tuple-element.90.exp_ref, bf16[1024,128]{1,0:T(8,128)(2,1)S(1)} %get-tuple-element.91.v_ref, bf16[64,1024]{1,0:T(8,128)(2,1)S(1)} %get-tuple-element.92.kt_ref, bf16[64,1024]{1,0:T(8,128)(2,1)S(1)} %get-tuple-element.78.q_ref, ...), custom_call_target="tpu_custom_call" | custom-call | flops 2300000000 | tf_op jit(solution)/shard_map/pallas_call | solution.py:355
  49.6 0.1 collective-permute-start.18
  49.7 2.3 %collective-permute-done.14.b_ref = bf16[64,768]{1,0:T(8,128)(2,1)S(1)} collective-permute-done((bf16[64,768]{1,0:T(8,128)(2,1)S(1)}, bf16[64,768]{1,0:T(8,128)(2,1)S(1)}, u32[]{:S(2)}, u32[]{:S(2)}) %collective-permute-start.14) | collective-permute-done | bytes 98336 | tf_op jit(solution)/shard_map/ppermute | solution.py:276
  52.1 1.0 %collective-permute-start.22 = (bf16[64,768]{1,0:T(8,128)(2,1)S(1)}, bf16[64,768]{1,0:T(8,128)(2,1)S(1)}, u32[]{:S(2)}, u32[]{:S(2)}) collective-permute-start(bf16[64,768]{1,0:T(8,128)(2,1)S(1)} %shard_map.100.refs_1_.a_ref), channel_id=1, source_target_pairs={{0,16},{2,18},{4,20},{6,22},{8,24},{10,26},{12,28},{14,30},{16,0},... | collective-permute-start | bytes 294920 | tf_op jit(solution)/shard_map/ppermute | solution.py:276
  53.0 0.0 collective-permute-done.17.refs_3_.refs_5_
  53.0 1.2 %collective-permute-done.16.refs_2_.came_ref = bf16[128,1024]{1,0:T(8,128)(2,1)S(1)} collective-permute-done((bf16[128,1024]{1,0:T(8,128)(2,1)S(1)}, bf16[128,1024]{1,0:T(8,128)(2,1)S(1)}, u32[]{:S(2)}, u32[]{:S(2)}) %collective-permute-start.16) | collective-permute-done | bytes 262176 | tf_op jit(solution)/shard_map/ppermute | solution.py:276
  54.3 2.2 %shard_map.102 = (bf16[128,1024]{1,0:T(8,128)(2,1)S(1)}, f32[64,1024]{1,0:T(8,128)S(1)}) custom-call(bf16[1024,1024]{1,0:T(8,128)(2,1)S(1)} %get-tuple-element.75.exp_ref, bf16[1024,128]{1,0:T(8,128)(2,1)S(1)} %get-tuple-element.76.v_ref, bf16[64,1024]{1,0:T(8,128)(2,1)S(1)} %get-tuple-element.77.kt_ref, bf16[64,1024]{1,0:T(8,128)(2,1)S(1)} %get-tuple-element.78.q_ref, ...), custom_call_target="tpu_custom_call" | custom-call | flops 2300000000 | tf_op jit(solution)/shard_map/pallas_call | solution.py:355
  56.4 0.0 collective-permute-done.18.b_ref
  56.4 0.1 shard_map.103.kept_ref
  56.5 0.1 shard_map.104
  56.6 1.0 %collective-permute-start.19 = (bf16[192,256]{1,0:T(8,128)(2,1)S(1)}, bf16[192,256]{1,0:T(8,128)(2,1)S(1)}, u32[]{:S(2)}, u32[]{:S(2)}) collective-permute-start(bf16[192,256]{1,0:T(8,128)(2,1)S(1)} %get-tuple-element.120), channel_id=1, source_target_pairs={{0,16},{2,18},{4,20},{6,22},{8,24},{10,26},{12,28},{14,30},{16,0},... | collective-permute-start | bytes 294920 | tf_op jit(solution)/shard_map/ppermute | solution.py:276
  57.6 1.9 %collective-permute-start.20 = (bf16[192,256]{1,0:T(8,128)(2,1)S(1)}, bf16[192,256]{1,0:T(8,128)(2,1)S(1)}, u32[]{:S(2)}, u32[]{:S(2)}) collective-permute-start(bf16[192,256]{1,0:T(8,128)(2,1)S(1)} %get-tuple-element.121), channel_id=1, source_target_pairs={{0,24},{2,26},{4,28},{6,30},{8,16},{10,18},{12,20},{14,22},{16,8},... | collective-permute-start | bytes 294920 | tf_op jit(solution)/shard_map/ppermute | solution.py:276
  59.5 0.7 collective-permute-start.21
  60.2 0.9 %collective-permute-start.23 = (bf16[64,768]{1,0:T(8,128)(2,1)S(1)}, bf16[64,768]{1,0:T(8,128)(2,1)S(1)}, u32[]{:S(2)}, u32[]{:S(2)}) collective-permute-start(bf16[64,768]{1,0:T(8,128)(2,1)S(1)} %shard_map.105.refs_0_), channel_id=1, source_target_pairs={{0,4},{2,6},{4,0},{6,2},{8,12},{10,14},{12,8},{14,10},{16,20},{18,... | collective-permute-start | bytes 294920 | tf_op jit(solution)/shard_map/ppermute | solution.py:276
  61.1 0.0 collective-permute-start.24
  61.1 4.6 %collective-permute-done.19.refs_1_ = bf16[192,256]{1,0:T(8,128)(2,1)S(1)} collective-permute-done((bf16[192,256]{1,0:T(8,128)(2,1)S(1)}, bf16[192,256]{1,0:T(8,128)(2,1)S(1)}, u32[]{:S(2)}, u32[]{:S(2)}) %collective-permute-start.19) | collective-permute-done | bytes 98336 | tf_op jit(solution)/shard_map/ppermute | solution.py:276
  65.7 0.2 collective-permute-done.21.refs_3_
  66.0 0.1 collective-permute-start.25
  66.0 1.1 %shard_map.108 = (f32[1024,128]{1,0:T(8,128)}, f32[4,64,256]{2,1,0:T(8,128)}, bf16[256,768]{1,0:T(8,128)(2,1)}) custom-call(bf16[192,256]{1,0:T(8,128)(2,1)S(1)} %get-tuple-element.119.refs_0_, bf16[192,256]{1,0:T(8,128)(2,1)S(1)} %collective-permute-done.19.refs_1_, bf16[192,256]{1,0:T(8,128)(2,1)S(1)} %collective-permute-done.20.refs_2_, ...), custom_call_target="tpu_custom_call" | custom-call | flops 5750000128 | tf_op jit(solution)/shard_map/pallas_call | solution.py:388
  67.1 0.0 collective-permute-done.24.refs_1_
  67.1 0.2 collective-permute-done.25.refs_3_
  67.3 0.9 %shard_map.109 = f32[4,64,768]{2,1,0:T(8,128)} custom-call(bf16[64,768]{1,0:T(8,128)(2,1)S(1)} %shard_map.105.refs_0_, bf16[64,768]{1,0:T(8,128)(2,1)S(1)} %collective-permute-done.24.refs_1_, bf16[64,768]{1,0:T(8,128)(2,1)S(1)} %shard_map.107.refs_6_.refs_2_, bf16[64,768]{1,0:T(8,128)(2,1)S(1)} %collective-permute-done.25.refs_3_), custom_call_target="tpu_custom_call" | custom-call | flops 575000000 | tf_op jit(solution)/shard_map/pallas_call | solution.py:382
  (24 shorter events, 0.2 us)
Async XLA Ops:
  0.6 7.6 %copy-start.1 = (bf16[4,64,768]{2,1,0:T(8,128)(2,1)S(1)}, bf16[4,64,768]{2,1,0:T(8,128)(2,1)}, u32[]{:S(2)}) copy-start(bf16[4,64,768]{2,1,0:T(8,128)(2,1)} %w_ref.3) | copy-start | bytes 1179652
  0.6 7.6 %copy-start.2 = (bf16[256,768]{1,0:T(8,128)(2,1)S(1)}, bf16[256,768]{1,0:T(8,128)(2,1)}, u32[]{:S(2)}) copy-start(bf16[256,768]{1,0:T(8,128)(2,1)} %go_ref.3) | copy-start | bytes 1179652
  0.7 7.5 %copy-start.3 = (bf16[256,4,64]{0,2,1:T(8,128)(2,1)S(1)}, bf16[256,4,64]{0,2,1:T(8,128)(2,1)}, u32[]{:S(2)}) copy-start(bf16[256,4,64]{0,2,1:T(8,128)(2,1)} %param.5) | copy-start | bytes 393220
  0.7 7.5 %copy-start.4 = (s32[2]{0:T(128)S(1)}, s32[2]{0:T(128)}, u32[]{:S(2)}) copy-start(s32[2]{0:T(128)} %fill_ref.5) | copy-start | bytes 28
  2.6 10.7 %collective-permute-start = (bf16[256,128]{1,0:T(8,128)(2,1)}, bf16[256,128]{1,0:T(8,128)(2,1)S(1)}, u32[]{:S(2)}, u32[]{:S(2)}) collective-permute-start(bf16[256,128]{1,0:T(8,128)(2,1)} %get-tuple-element.66), channel_id=1, source_target_pairs={{0,16},{2,18},{4,20},{6,22},{8,24},{10,26},{12,28},{14,30},{16,0},... | collective-permute-start | bytes 196616 | tf_op jit(solution)/shard_map/ppermute | solution.py:276
  6.6 6.7 %collective-permute-start.1 = (bf16[256,128]{1,0:T(8,128)(2,1)}, bf16[256,128]{1,0:T(8,128)(2,1)S(1)}, u32[]{:S(2)}, u32[]{:S(2)}) collective-permute-start(bf16[256,128]{1,0:T(8,128)(2,1)} %get-tuple-element.67), channel_id=1, source_target_pairs={{0,24},{2,26},{4,28},{6,30},{8,16},{10,18},{12,20},{14,22},{16,8},... | collective-permute-start | bytes 196616 | tf_op jit(solution)/shard_map/ppermute | solution.py:276
  8.0 5.4 %collective-permute-start.2 = (bf16[256,128]{1,0:T(8,128)(2,1)}, bf16[256,128]{1,0:T(8,128)(2,1)S(1)}, u32[]{:S(2)}, u32[]{:S(2)}) collective-permute-start(bf16[256,128]{1,0:T(8,128)(2,1)} %get-tuple-element.68), channel_id=1, source_target_pairs={{0,8},{2,10},{4,12},{6,14},{8,0},{10,2},{12,4},{14,6},{16,24},{18,... | collective-permute-start | bytes 196616 | tf_op jit(solution)/shard_map/ppermute | solution.py:276
  8.2 5.1 %copy-start = (bf16[256,128]{1,0:T(8,128)(2,1)S(1)}, bf16[256,128]{1,0:T(8,128)(2,1)}, u32[]{:S(2)}) copy-start(bf16[256,128]{1,0:T(8,128)(2,1)} %get-tuple-element.65.refs_0_) | copy-start | bytes 196612
  9.1 8.1 %collective-permute-start.3 = (bf16[128,256]{1,0:T(8,128)(2,1)S(1)}, bf16[128,256]{1,0:T(8,128)(2,1)S(1)}, u32[]{:S(2)}, u32[]{:S(2)}) collective-permute-start(bf16[128,256]{1,0:T(8,128)(2,1)S(1)} %get-tuple-element.70), channel_id=1, source_target_pairs={{0,16},{2,18},{4,20},{6,22},{8,24},{10,26},{12,28},{14,30},{16,0},... | collective-permute-start | bytes 196616 | tf_op jit(solution)/shard_map/ppermute | solution.py:276
  12.0 6.2 %collective-permute-start.4 = (bf16[128,256]{1,0:T(8,128)(2,1)S(1)}, bf16[128,256]{1,0:T(8,128)(2,1)S(1)}, u32[]{:S(2)}, u32[]{:S(2)}) collective-permute-start(bf16[128,256]{1,0:T(8,128)(2,1)S(1)} %get-tuple-element.71), channel_id=1, source_target_pairs={{0,24},{2,26},{4,28},{6,30},{8,16},{10,18},{12,20},{14,22},{16,8},... | collective-permute-start | bytes 196616 | tf_op jit(solution)/shard_map/ppermute | solution.py:276
  13.3 5.1 %collective-permute-start.5 = (bf16[128,256]{1,0:T(8,128)(2,1)S(1)}, bf16[128,256]{1,0:T(8,128)(2,1)S(1)}, u32[]{:S(2)}, u32[]{:S(2)}) collective-permute-start(bf16[128,256]{1,0:T(8,128)(2,1)S(1)} %get-tuple-element.72), channel_id=1, source_target_pairs={{0,8},{2,10},{4,12},{6,14},{8,0},{10,2},{12,4},{14,6},{16,24},{18,... | collective-permute-start | bytes 196616 | tf_op jit(solution)/shard_map/ppermute | solution.py:276
  13.4 11.1 %collective-permute-start.7 = (bf16[1024,128]{1,0:T(8,128)(2,1)S(1)}, bf16[1024,128]{1,0:T(8,128)(2,1)S(1)}, u32[]{:S(2)}, u32[]{:S(2)}) collective-permute-start(bf16[1024,128]{1,0:T(8,128)(2,1)S(1)} %shard_map.86.pair_ref), channel_id=1, source_target_pairs={{0,4},{2,6},{4,0},{6,2},{8,12},{10,14},{12,8},{14,10},{16,20},{18,... | collective-permute-start | bytes 786440 | tf_op jit(solution)/shard_map/ppermute | solution.py:276
  14.9 6.5 %collective-permute-start.6 = (bf16[1024,128]{1,0:T(8,128)(2,1)S(1)}, bf16[1024,128]{1,0:T(8,128)(2,1)S(1)}, u32[]{:S(2)}, u32[]{:S(2)}) collective-permute-start(bf16[1024,128]{1,0:T(8,128)(2,1)S(1)} %shard_map.86.pair_ref), channel_id=1, source_target_pairs={{0,2},{2,0},{4,6},{6,4},{8,10},{10,8},{12,14},{14,12},{16,18},{18,... | collective-permute-start | bytes 786440 | tf_op jit(solution)/shard_map/ppermute | solution.py:276
  24.5 3.0 %collective-permute-start.8 = (bf16[1024,128]{1,0:T(8,128)(2,1)S(1)}, bf16[1024,128]{1,0:T(8,128)(2,1)S(1)}, u32[]{:S(2)}, u32[]{:S(2)}) collective-permute-start(bf16[1024,128]{1,0:T(8,128)(2,1)S(1)} %shard_map.90.pair_ref), channel_id=1, source_target_pairs={{0,2},{2,0},{4,6},{6,4},{8,10},{10,8},{12,14},{14,12},{16,18},{18,... | collective-permute-start | bytes 786440 | tf_op jit(solution)/shard_map/ppermute | solution.py:276
  30.8 5.9 %collective-permute-start.9 = (bf16[64,256]{1,0:T(8,128)(2,1)S(1)}, bf16[64,256]{1,0:T(8,128)(2,1)S(1)}, u32[]{:S(2)}, u32[]{:S(2)}) collective-permute-start(bf16[64,256]{1,0:T(8,128)(2,1)S(1)} %get-tuple-element.104), channel_id=1, source_target_pairs={{0,16},{2,18},{4,20},{6,22},{8,24},{10,26},{12,28},{14,30},{16,0},... | collective-permute-start | bytes 98312 | tf_op jit(solution)/shard_map/ppermute | solution.py:276
  33.9 5.7 %collective-permute-start.10 = (bf16[64,256]{1,0:T(8,128)(2,1)S(1)}, bf16[64,256]{1,0:T(8,128)(2,1)S(1)}, u32[]{:S(2)}, u32[]{:S(2)}) collective-permute-start(bf16[64,256]{1,0:T(8,128)(2,1)S(1)} %get-tuple-element.105), channel_id=1, source_target_pairs={{0,24},{2,26},{4,28},{6,30},{8,16},{10,18},{12,20},{14,22},{16,8},... | collective-permute-start | bytes 98312 | tf_op jit(solution)/shard_map/ppermute | solution.py:276
  34.3 5.3 %collective-permute-start.11 = (bf16[64,256]{1,0:T(8,128)(2,1)S(1)}, bf16[64,256]{1,0:T(8,128)(2,1)S(1)}, u32[]{:S(2)}, u32[]{:S(2)}) collective-permute-start(bf16[64,256]{1,0:T(8,128)(2,1)S(1)} %get-tuple-element.106), channel_id=1, source_target_pairs={{0,8},{2,10},{4,12},{6,14},{8,0},{10,2},{12,4},{14,6},{16,24},{18,... | collective-permute-start | bytes 98312 | tf_op jit(solution)/shard_map/ppermute | solution.py:276
  40.5 2.1 %collective-permute-start.12 = (bf16[2,64,768]{2,1,0:T(8,128)(2,1)S(1)}, bf16[2,64,768]{2,1,0:T(8,128)(2,1)S(1)}, u32[]{:S(2)}, u32[]{:S(2)}) collective-permute-start(bf16[2,64,768]{2,1,0:T(8,128)(2,1)S(1)} %get-tuple-element.109), channel_id=1, source_target_pairs={{0,2},{2,0},{4,6},{6,4},{8,10},{10,8},{12,14},{14,12},{16,18},{18,... | collective-permute-start | bytes 589832 | tf_op jit(solution)/shard_map/ppermute | solution.py:276
  40.6 5.8 %collective-permute-start.15 = (bf16[128,1024]{1,0:T(8,128)(2,1)S(1)}, bf16[128,1024]{1,0:T(8,128)(2,1)S(1)}, u32[]{:S(2)}, u32[]{:S(2)}) collective-permute-start(bf16[128,1024]{1,0:T(8,128)(2,1)S(1)} %get-tuple-element.107.refs_4_), channel_id=1, source_target_pairs={{0,2},{2,0},{4,6},{6,4},{8,10},{10,8},{12,14},{14,12},{16,18},{18,... | collective-permute-start | bytes 786440 | tf_op jit(solution)/shard_map/ppermute | solution.py:276
  41.1 12.0 %collective-permute-start.17 = (bf16[256,768]{1,0:T(8,128)(2,1)S(1)}, bf16[256,768]{1,0:T(8,128)(2,1)S(1)}, u32[]{:S(2)}, u32[]{:S(2)}) collective-permute-start(bf16[256,768]{1,0:T(8,128)(2,1)S(1)} %get-tuple-element.116.refs_4_), channel_id=1, source_target_pairs={{0,1},{1,0},{2,3},{3,2},{4,5},{5,4},{6,7},{7,6},{8,9},{9,8},{10,11... | collective-permute-start | bytes 1179656 | tf_op jit(solution)/shard_map/ppermute | solution.py:276
  42.6 4.7 %collective-permute-start.13 = (bf16[64,768]{1,0:T(8,128)(2,1)S(1)}, bf16[64,768]{1,0:T(8,128)(2,1)S(1)}, u32[]{:S(2)}, u32[]{:S(2)}) collective-permute-start(bf16[64,768]{1,0:T(8,128)(2,1)S(1)} %get-tuple-element.112), channel_id=1, source_target_pairs={{0,4},{2,6},{4,0},{6,2},{8,12},{10,14},{12,8},{14,10},{16,20},{18,... | collective-permute-start | bytes 294920 | tf_op jit(solution)/shard_map/ppermute | solution.py:276
  46.5 7.8 %collective-permute-start.16 = (bf16[128,1024]{1,0:T(8,128)(2,1)S(1)}, bf16[128,1024]{1,0:T(8,128)(2,1)S(1)}, u32[]{:S(2)}, u32[]{:S(2)}) collective-permute-start(bf16[128,1024]{1,0:T(8,128)(2,1)S(1)} %shard_map.101), channel_id=1, source_target_pairs={{0,4},{2,6},{4,0},{6,2},{8,12},{10,14},{12,8},{14,10},{16,20},{18,... | collective-permute-start | bytes 786440 | tf_op jit(solution)/shard_map/ppermute | solution.py:276
  47.3 4.7 %collective-permute-start.14 = (bf16[64,768]{1,0:T(8,128)(2,1)S(1)}, bf16[64,768]{1,0:T(8,128)(2,1)S(1)}, u32[]{:S(2)}, u32[]{:S(2)}) collective-permute-start(bf16[64,768]{1,0:T(8,128)(2,1)S(1)} %shard_map.98.refs_1_.a_ref), channel_id=1, source_target_pairs={{0,8},{2,10},{4,12},{6,14},{8,0},{10,2},{12,4},{14,6},{16,24},{18,... | collective-permute-start | bytes 294920 | tf_op jit(solution)/shard_map/ppermute | solution.py:276
  49.6 6.8 %collective-permute-start.18 = (bf16[128,1024]{1,0:T(8,128)(2,1)S(1)}, bf16[128,1024]{1,0:T(8,128)(2,1)S(1)}, u32[]{:S(2)}, u32[]{:S(2)}) collective-permute-start(bf16[128,1024]{1,0:T(8,128)(2,1)S(1)} %get-tuple-element.115.refs_0_), channel_id=1, source_target_pairs={{0,2},{2,0},{4,6},{6,4},{8,10},{10,8},{12,14},{14,12},{16,18},{18,... | collective-permute-start | bytes 786440 | tf_op jit(solution)/shard_map/ppermute | solution.py:276
  52.1 8.1 %collective-permute-start.22 = (bf16[64,768]{1,0:T(8,128)(2,1)S(1)}, bf16[64,768]{1,0:T(8,128)(2,1)S(1)}, u32[]{:S(2)}, u32[]{:S(2)}) collective-permute-start(bf16[64,768]{1,0:T(8,128)(2,1)S(1)} %shard_map.100.refs_1_.a_ref), channel_id=1, source_target_pairs={{0,16},{2,18},{4,20},{6,22},{8,24},{10,26},{12,28},{14,30},{16,0},... | collective-permute-start | bytes 294920 | tf_op jit(solution)/shard_map/ppermute | solution.py:276
  56.6 9.1 %collective-permute-start.19 = (bf16[192,256]{1,0:T(8,128)(2,1)S(1)}, bf16[192,256]{1,0:T(8,128)(2,1)S(1)}, u32[]{:S(2)}, u32[]{:S(2)}) collective-permute-start(bf16[192,256]{1,0:T(8,128)(2,1)S(1)} %get-tuple-element.120), channel_id=1, source_target_pairs={{0,16},{2,18},{4,20},{6,22},{8,24},{10,26},{12,28},{14,30},{16,0},... | collective-permute-start | bytes 294920 | tf_op jit(solution)/shard_map/ppermute | solution.py:276
  57.6 8.1 %collective-permute-start.20 = (bf16[192,256]{1,0:T(8,128)(2,1)S(1)}, bf16[192,256]{1,0:T(8,128)(2,1)S(1)}, u32[]{:S(2)}, u32[]{:S(2)}) collective-permute-start(bf16[192,256]{1,0:T(8,128)(2,1)S(1)} %get-tuple-element.121), channel_id=1, source_target_pairs={{0,24},{2,26},{4,28},{6,30},{8,16},{10,18},{12,20},{14,22},{16,8},... | collective-permute-start | bytes 294920 | tf_op jit(solution)/shard_map/ppermute | solution.py:276
  59.5 6.4 %collective-permute-start.21 = (bf16[192,256]{1,0:T(8,128)(2,1)S(1)}, bf16[192,256]{1,0:T(8,128)(2,1)S(1)}, u32[]{:S(2)}, u32[]{:S(2)}) collective-permute-start(bf16[192,256]{1,0:T(8,128)(2,1)S(1)} %get-tuple-element.122), channel_id=1, source_target_pairs={{0,8},{2,10},{4,12},{6,14},{8,0},{10,2},{12,4},{14,6},{16,24},{18,... | collective-permute-start | bytes 294920 | tf_op jit(solution)/shard_map/ppermute | solution.py:276
  60.2 5.7 %collective-permute-start.23 = (bf16[64,768]{1,0:T(8,128)(2,1)S(1)}, bf16[64,768]{1,0:T(8,128)(2,1)S(1)}, u32[]{:S(2)}, u32[]{:S(2)}) collective-permute-start(bf16[64,768]{1,0:T(8,128)(2,1)S(1)} %shard_map.105.refs_0_), channel_id=1, source_target_pairs={{0,4},{2,6},{4,0},{6,2},{8,12},{10,14},{12,8},{14,10},{16,20},{18,... | collective-permute-start | bytes 294920 | tf_op jit(solution)/shard_map/ppermute | solution.py:276
  61.1 6.0 %collective-permute-start.24 = (bf16[64,768]{1,0:T(8,128)(2,1)S(1)}, bf16[64,768]{1,0:T(8,128)(2,1)S(1)}, u32[]{:S(2)}, u32[]{:S(2)}) collective-permute-start(bf16[64,768]{1,0:T(8,128)(2,1)S(1)} %shard_map.105.refs_0_), channel_id=1, source_target_pairs={{0,2},{2,0},{4,6},{6,4},{8,10},{10,8},{12,14},{14,12},{16,18},{18,... | collective-permute-start | bytes 294920 | tf_op jit(solution)/shard_map/ppermute | solution.py:276
  66.0 1.4 %collective-permute-start.25 = (bf16[64,768]{1,0:T(8,128)(2,1)S(1)}, bf16[64,768]{1,0:T(8,128)(2,1)S(1)}, u32[]{:S(2)}, u32[]{:S(2)}) collective-permute-start(bf16[64,768]{1,0:T(8,128)(2,1)S(1)} %shard_map.107.refs_6_.refs_2_), channel_id=1, source_target_pairs={{0,2},{2,0},{4,6},{6,4},{8,10},{10,8},{12,14},{14,12},{16,18},{18,... | collective-permute-start | bytes 294920 | tf_op jit(solution)/shard_map/ppermute | solution.py:276

commit v16 on v15

--- a/solution.py
+++ b/solution.py
@@ -55,7 +55,7 @@
 
 
 def spread(slots):
-    return [0] + sorted(range(1, slots), key=lambda mask: (mask < slots // 2, mask))
+    return [0] + list(range(slots - 1, 0, -1))
 
 
 def pack_kv_kernel(heads, rows, dim, a_of, fill_ref, kv_ref, *refs):
@@ -177,7 +177,7 @@
 
 
 def back_kernel(slots, rows, dim, first, exp_ref, v_ref, kt_ref, q_ref, g_ref, factor_ref, inner_ref, *refs):
-    dkv_ref, dq_ref, ga_ref = refs[-3:]
+    dkv_ref, dq_ref, ga_ref, ds_ref = refs[-4:]
     block = g_ref.shape[1]
     factor = factor_ref[...]
     inner = inner_ref[...] * factor
@@ -185,23 +185,18 @@
     row = lax.broadcasted_iota(jnp.int32, (dim, block), 0)
     ga_ref[0:dim, :] = (g_ref[...].astype(F32) * factor).astype(BF16)
     ga_ref[dim:, :] = jnp.where(row == 1, -high, jnp.where(row == 2, high - inner, 0.0)).astype(BF16)
-    grad_k = grad_v = None
     ahead = dot(v_ref[...], ga_ref[:, 0:rows])
     for slot in range(slots):
         here = slice(slot * rows, (slot + 1) * rows)
         products = ahead
         if slot + 1 < slots:
             ahead = dot(v_ref[...], ga_ref[:, (slot + 1) * rows : (slot + 2) * rows])
-        exps = exp_ref[:, here]
-        grads = exps * products.astype(BF16)
-        term_v = dot_nt(ga_ref[0:dim, here], exps)
-        term_k = dot_nt(q_ref[:, here], grads)
-        grad_v = term_v if grad_v is None else grad_v + term_v
-        grad_k = term_k if grad_k is None else grad_k + term_k
+        grads = exp_ref[:, here] * products.astype(BF16)
+        ds_ref[:, here] = grads
         term = dot(kt_ref[...], grads)
         dq_ref[:, here] = term if first else refs[0][:, here] + term
-    dkv_ref[dim:, :] = grad_v.astype(BF16)
-    dkv_ref[0:dim, :] = grad_k.astype(BF16)
+    dkv_ref[dim:, :] = dot_nt(ga_ref[0:dim, :], exp_ref[...]).astype(BF16)
+    dkv_ref[0:dim, :] = dot_nt(q_ref[...], ds_ref[...]).astype(BF16)
 
 
 def project_kernel(slots, rows, a_of, b_of, halves, fill_ref, go_ref, w_ref, *refs):
@@ -354,7 +349,7 @@
         operands = [scored[r][0], *scored[r][3:], q_all, grads, factors[r], inner] + ([] if dq is None else [dq])
         dkv[r], dq = call(
             functools.partial(back_kernel, slots, rows, dim, dq is None),
-            [((wide, block), BF16), ((dim, block), F32)], [pltpu.VMEM((wide, block), BF16)],
+            [((wide, block), BF16), ((dim, block), F32)], [pltpu.VMEM((wide, block), BF16), pltpu.VMEM((block, block), BF16)],
             n_in=len(operands), after=len(later), micros=2,
         )(*operands, *later)
         later = []

time: 68.4 us -> 69.2 us (1.012)
  starting transfers between devices: 25.1 us -> 28.2 us
  waiting for transfers between devices: 15.3 us -> 12.5 us
    ppermute x26, starting transfers between devices: 25.1 us -> 28.2 us  [swap(): return lax.ppermute(array, axis, [(i, i ^ mask) for i in range(size)])]
    ppermute x26, waiting for transfers between devices: 15.3 us -> 12.5 us  [swap(): return lax.ppermute(array, axis, [(i, i ^ mask) for i in range(size)])]
  transfers between devices with their start and end apart: 26 -> 26, of which waited for: 10 -> 9; matrix products, arithmetic and copies ran while one was open for 0% -> 0% of each run, Pallas kernels for 29% -> 29%
where the time goes in v16:
time: 69.2 us; the launch traced here: 69.1 us
  starting transfers between devices  28.2 us (41%)
  Pallas kernels  27.4 us (40%)
  waiting for transfers between devices  12.5 us (18%)
  between operations  0.93 us (1%)
    ppermute x26, starting transfers between devices, swap(): return lax.ppermute(array, axis, [(i, i ^ mask) for i in range(size)])  28.2 us
    ppermute x26, waiting for transfers between devices, swap(): return lax.ppermute(array, axis, [(i, i ^ mask) for i in range(size)])  12.5 us
    pallas_call x4, Pallas kernels, shards(): call(functools.partial(score_kernel, slots, rows, dim, step), [((block, b...  11.9 us
    pallas_call x4, Pallas kernels, shards(): call(functools.partial(back_kernel, slots, rows, dim, dq is None), [((wid...  9.15 us
    pallas_call x1, Pallas kernels, shards(): call(functools.partial(pack_kv_kernel, heads, rows, dim, a_of), [((rows,...  1.9 us
  transfers between devices with their start and end apart: 26, of which 9 were waited for; matrix products, arithmetic and copies ran while one was open for 0% of the time, Pallas kernels for 29%

profile of v16, /device:TPU:0, one launch (start us, length us, event | category | flops | bytes accessed | tf_op | source)
XLA Modules:
  0.0 69.1 jit_solution(2756693053346857993)
XLA Ops:
  0.7 1.9 %shard_map.84 = (bf16[256,128]{1,0:T(8,128)(2,1)}, bf16[256,128]{1,0:T(8,128)(2,1)}, bf16[256,128]{1,0:T(8,128)(2,1)}, bf16[256,128]{1,0:T(8,128)(2,1)}) custom-call(s32[2]{0:T(128)} %fill_ref.5, bf16[1024,128]{1,0:T(8,128)(2,1)} %bitcast.5), custom_call_target="tpu_custom_call" | custom-call | flops 1724999936 | tf_op jit(solution)/shard_map/pallas_call | solution.py:277
  2.6 5.0 %collective-permute-start = (bf16[256,128]{1,0:T(8,128)(2,1)}, bf16[256,128]{1,0:T(8,128)(2,1)S(1)}, u32[]{:S(2)}, u32[]{:S(2)}) collective-permute-start(bf16[256,128]{1,0:T(8,128)(2,1)} %get-tuple-element.66), channel_id=1, source_target_pairs={{0,24},{2,26},{4,28},{6,30},{8,16},{10,18},{12,20},{14,22},{16,8},... | collective-permute-start | bytes 196616 | tf_op jit(solution)/shard_map/ppermute | solution.py:271
  7.6 0.0 collective-permute-start.1
  7.6 0.6 collective-permute-start.2
  8.2 0.0 copy-start
  8.2 0.9 %shard_map.85 = (bf16[128,256]{1,0:T(8,128)(2,1)S(1)}, bf16[128,256]{1,0:T(8,128)(2,1)S(1)}, bf16[128,256]{1,0:T(8,128)(2,1)S(1)}, bf16[128,256]{1,0:T(8,128)(2,1)S(1)}) custom-call(s32[2]{0:T(128)S(1)} %copy-done.4, bf16[4,64,256]{2,1,0:T(8,128)(2,1)S(1)} %bitcast.4, bf16[4,64,768]{2,1,0:T(8,128)(2,1)S(1)} %copy-done.1, bf16[256,768]{1,0:T(8,128)(2,1)S(1)} %copy-done.2), custom_call_target="tpu_custom_call" | custom-call | flops 1150000000 | tf_op jit(solution)/shard_map/pallas_call | solution.py:282
  9.1 3.9 %collective-permute-start.3 = (bf16[128,256]{1,0:T(8,128)(2,1)S(1)}, bf16[128,256]{1,0:T(8,128)(2,1)S(1)}, u32[]{:S(2)}, u32[]{:S(2)}) collective-permute-start(bf16[128,256]{1,0:T(8,128)(2,1)S(1)} %get-tuple-element.70), channel_id=1, source_target_pairs={{0,24},{2,26},{4,28},{6,30},{8,16},{10,18},{12,20},{14,22},{16,8},... | collective-permute-start | bytes 196616 | tf_op jit(solution)/shard_map/ppermute | solution.py:271
  13.0 0.0 collective-permute-start.4
  13.0 0.0 collective-permute-done.refs_1_
  13.0 0.6 collective-permute-start.5
  13.6 2.4 %collective-permute-done.1.refs_2_ = bf16[256,128]{1,0:T(8,128)(2,1)S(1)} collective-permute-done((bf16[256,128]{1,0:T(8,128)(2,1)}, bf16[256,128]{1,0:T(8,128)(2,1)S(1)}, u32[]{:S(2)}, u32[]{:S(2)}) %collective-permute-start.1) | collective-permute-done | bytes 65568 | tf_op jit(solution)/shard_map/ppermute | solution.py:271
  16.0 0.0 collective-permute-done.2.refs_3_
  16.0 0.4 collective-permute-start.7
  16.4 0.0 collective-permute-start.6
  16.4 0.0 collective-permute-done.3.refs_1_
  16.4 2.6 %collective-permute-done.4.refs_2_ = bf16[128,256]{1,0:T(8,128)(2,1)S(1)} collective-permute-done((bf16[128,256]{1,0:T(8,128)(2,1)S(1)}, bf16[128,256]{1,0:T(8,128)(2,1)S(1)}, u32[]{:S(2)}, u32[]{:S(2)}) %collective-permute-start.4) | collective-permute-done | bytes 65568 | tf_op jit(solution)/shard_map/ppermute | solution.py:271
  19.1 0.0 collective-permute-done.5.refs_3_
  19.1 0.1 shard_map.87
  19.2 2.9 %shard_map.88 = (bf16[1024,1024]{1,0:T(8,128)(2,1)S(1)}, f32[1,1024]{1,0:T(1,128)S(1)}, f32[80,1024]{1,0:T(8,128)S(1)}, bf16[1024,128]{1,0:T(8,128)(2,1)S(1)}, bf16[64,1024]{1,0:T(8,128)(2,1)S(1)}) custom-call(bf16[1024,128]{1,0:T(8,128)(2,1)S(1)} %shard_map.86.pair_ref, bf16[256,1024]{1,0:T(8,128)(2,1)S(1)} %get-tuple-element.73.qa_ref, ...), custom_call_target="tpu_custom_call" | custom-call | flops 5750000128 | tf_op jit(solution)/shard_map/pallas_call | solution.py:308
  22.1 0.0 collective-permute-done.6.pair_ref
  22.1 2.9 %shard_map.89 = (bf16[1024,1024]{1,0:T(8,128)(2,1)S(1)}, f32[1,1024]{1,0:T(1,128)S(1)}, f32[80,1024]{1,0:T(8,128)S(1)}, bf16[1024,128]{1,0:T(8,128)(2,1)S(1)}, bf16[64,1024]{1,0:T(8,128)(2,1)S(1)}) custom-call(bf16[1024,128]{1,0:T(8,128)(2,1)S(1)} %collective-permute-done.6.pair_ref, bf16[256,1024]{1,0:T(8,128)(2,1)S(1)} %get-tuple-element.73.qa_ref, ...), custom_call_target="tpu_custom_call" | custom-call | flops 5750000128 | tf_op jit(solution)/shard_map/pallas_call | solution.py:308
  25.1 0.0 collective-permute-done.7.refs_0_
  25.1 0.1 collective-permute-start.8
  25.2 2.9 %shard_map.91 = (bf16[1024,1024]{1,0:T(8,128)(2,1)S(1)}, f32[1,1024]{1,0:T(1,128)S(1)}, f32[80,1024]{1,0:T(8,128)S(1)}, bf16[1024,128]{1,0:T(8,128)(2,1)S(1)}, bf16[64,1024]{1,0:T(8,128)(2,1)S(1)}) custom-call(bf16[1024,128]{1,0:T(8,128)(2,1)S(1)} %shard_map.90.pair_ref, bf16[256,1024]{1,0:T(8,128)(2,1)S(1)} %get-tuple-element.73.qa_ref, ...), custom_call_target="tpu_custom_call" | custom-call | flops 5750000128 | tf_op jit(solution)/shard_map/pallas_call | solution.py:308
  28.1 0.0 collective-permute-done.8.pair_ref
  28.1 3.1 %shard_map.92 = (bf16[1024,1024]{1,0:T(8,128)(2,1)S(1)}, f32[1,1024]{1,0:T(1,128)S(1)}, f32[80,1024]{1,0:T(8,128)S(1)}, bf16[1024,128]{1,0:T(8,128)(2,1)S(1)}, bf16[64,1024]{1,0:T(8,128)(2,1)S(1)}) custom-call(bf16[1024,128]{1,0:T(8,128)(2,1)S(1)} %collective-permute-done.8.pair_ref, bf16[256,1024]{1,0:T(8,128)(2,1)S(1)} %get-tuple-element.73.qa_ref, ...), custom_call_target="tpu_custom_call" | custom-call | flops 5750000128 | tf_op jit(solution)/shard_map/pallas_call | solution.py:308
  31.2 0.2 shard_map.93
  31.4 2.7 %collective-permute-start.9 = (bf16[64,256]{1,0:T(8,128)(2,1)S(1)}, bf16[64,256]{1,0:T(8,128)(2,1)S(1)}, u32[]{:S(2)}, u32[]{:S(2)}) collective-permute-start(bf16[64,256]{1,0:T(8,128)(2,1)S(1)} %get-tuple-element.104), channel_id=1, source_target_pairs={{0,24},{2,26},{4,28},{6,30},{8,16},{10,18},{12,20},{14,22},{16,8},... | collective-permute-start | bytes 98312 | tf_op jit(solution)/shard_map/ppermute | solution.py:271
  34.1 1.7 %collective-permute-start.11 = (bf16[64,256]{1,0:T(8,128)(2,1)S(1)}, bf16[64,256]{1,0:T(8,128)(2,1)S(1)}, u32[]{:S(2)}, u32[]{:S(2)}) collective-permute-start(bf16[64,256]{1,0:T(8,128)(2,1)S(1)} %get-tuple-element.106), channel_id=1, source_target_pairs={{0,8},{2,10},{4,12},{6,14},{8,0},{10,2},{12,4},{14,6},{16,24},{18,... | collective-permute-start | bytes 98312 | tf_op jit(solution)/shard_map/ppermute | solution.py:271
  35.9 2.3 %shard_map.94 = (bf16[128,1024]{1,0:T(8,128)(2,1)S(1)}, f32[64,1024]{1,0:T(8,128)S(1)}) custom-call(bf16[1024,1024]{1,0:T(8,128)(2,1)S(1)} %get-tuple-element.98.exp_ref, bf16[1024,128]{1,0:T(8,128)(2,1)S(1)} %get-tuple-element.99.v_ref, bf16[64,1024]{1,0:T(8,128)(2,1)S(1)} %get-tuple-element.100.kt_ref, bf16[64,1024]{1,0:T(8,128)(2,1)S(1)} %get-tuple-element.78.q_ref, ...), custom_call_target="tpu_custom_call" | custom-call | flops 2300000000 | tf_op jit(solution)/shard_map/pallas_call | solution.py:350
  38.2 0.0 collective-permute-done.9.refs_1_
  38.2 0.8 %collective-permute-done.10.refs_2_ = bf16[64,256]{1,0:T(8,128)(2,1)S(1)} collective-permute-done((bf16[64,256]{1,0:T(8,128)(2,1)S(1)}, bf16[64,256]{1,0:T(8,128)(2,1)S(1)}, u32[]{:S(2)}, u32[]{:S(2)}) %collective-permute-start.10) | collective-permute-done | bytes 32800 | tf_op jit(solution)/shard_map/ppermute | solution.py:271
  38.9 0.0 collective-permute-done.11.refs_3_
  38.9 0.9 %shard_map.95 = (bf16[256,768]{1,0:T(8,128)(2,1)S(1)}, bf16[2,64,768]{2,1,0:T(8,128)(2,1)S(1)}, bf16[2,64,768]{2,1,0:T(8,128)(2,1)S(1)}) custom-call(s32[2]{0:T(128)S(1)} %copy-done.4, bf16[256,768]{1,0:T(8,128)(2,1)S(1)} %copy-done.2, bf16[4,64,768]{2,1,0:T(8,128)(2,1)S(1)} %copy-done.1, bf16[64,256]{1,0:T(8,128)(2,1)S(1)} %get-tuple-element.103.refs_0_, ...), custom_call_target="tpu_custom_call" | custom-call | flops 805000000 | tf_op jit(solution)/shard_map/pallas_call | solution.py:328
  39.9 0.1 collective-permute-start.12
  39.9 0.5 collective-permute-start.15
  40.4 1.5 %collective-permute-start.17 = (bf16[256,768]{1,0:T(8,128)(2,1)S(1)}, bf16[256,768]{1,0:T(8,128)(2,1)S(1)}, u32[]{:S(2)}, u32[]{:S(2)}) collective-permute-start(bf16[256,768]{1,0:T(8,128)(2,1)S(1)} %get-tuple-element.116.refs_4_), channel_id=1, source_target_pairs={{0,1},{1,0},{2,3},{3,2},{4,5},{5,4},{6,7},{7,6},{8,9},{9,8},{10,11... | collective-permute-start | bytes 1179656 | tf_op jit(solution)/shard_map/ppermute | solution.py:271
  42.0 1.6 %collective-permute-start.13 = (bf16[64,768]{1,0:T(8,128)(2,1)S(1)}, bf16[64,768]{1,0:T(8,128)(2,1)S(1)}, u32[]{:S(2)}, u32[]{:S(2)}) collective-permute-start(bf16[64,768]{1,0:T(8,128)(2,1)S(1)} %get-tuple-element.112), channel_id=1, source_target_pairs={{0,4},{2,6},{4,0},{6,2},{8,12},{10,14},{12,8},{14,10},{16,20},{18,... | collective-permute-start | bytes 294920 | tf_op jit(solution)/shard_map/ppermute | solution.py:271
  43.6 2.3 %shard_map.97 = (bf16[128,1024]{1,0:T(8,128)(2,1)S(1)}, f32[64,1024]{1,0:T(8,128)S(1)}) custom-call(bf16[1024,1024]{1,0:T(8,128)(2,1)S(1)} %get-tuple-element.94.exp_ref, bf16[1024,128]{1,0:T(8,128)(2,1)S(1)} %get-tuple-element.95.v_ref, bf16[64,1024]{1,0:T(8,128)(2,1)S(1)} %get-tuple-element.96.kt_ref, bf16[64,1024]{1,0:T(8,128)(2,1)S(1)} %get-tuple-element.78.q_ref, ...), custom_call_target="tpu_custom_call" | custom-call | flops 2300000000 | tf_op jit(solution)/shard_map/pallas_call | solution.py:350
  45.9 0.0 collective-permute-done.15.b_ref
  45.9 0.1 shard_map.101
  46.0 0.6 collective-permute-start.16
  46.5 0.1 collective-permute-done.13.b_ref
  46.7 0.9 %collective-permute-start.14 = (bf16[64,768]{1,0:T(8,128)(2,1)S(1)}, bf16[64,768]{1,0:T(8,128)(2,1)S(1)}, u32[]{:S(2)}, u32[]{:S(2)}) collective-permute-start(bf16[64,768]{1,0:T(8,128)(2,1)S(1)} %shard_map.98.refs_1_.a_ref), channel_id=1, source_target_pairs={{0,8},{2,10},{4,12},{6,14},{8,0},{10,2},{12,4},{14,6},{16,24},{18,... | collective-permute-start | bytes 294920 | tf_op jit(solution)/shard_map/ppermute | solution.py:271
  47.6 2.3 %shard_map.99 = (bf16[128,1024]{1,0:T(8,128)(2,1)S(1)}, f32[64,1024]{1,0:T(8,128)S(1)}) custom-call(bf16[1024,1024]{1,0:T(8,128)(2,1)S(1)} %get-tuple-element.90.exp_ref, bf16[1024,128]{1,0:T(8,128)(2,1)S(1)} %get-tuple-element.91.v_ref, bf16[64,1024]{1,0:T(8,128)(2,1)S(1)} %get-tuple-element.92.kt_ref, bf16[64,1024]{1,0:T(8,128)(2,1)S(1)} %get-tuple-element.78.q_ref, ...), custom_call_target="tpu_custom_call" | custom-call | flops 2300000000 | tf_op jit(solution)/shard_map/pallas_call | solution.py:350
  49.9 0.1 collective-permute-start.18
  50.0 1.4 %collective-permute-done.14.b_ref = bf16[64,768]{1,0:T(8,128)(2,1)S(1)} collective-permute-done((bf16[64,768]{1,0:T(8,128)(2,1)S(1)}, bf16[64,768]{1,0:T(8,128)(2,1)S(1)}, u32[]{:S(2)}, u32[]{:S(2)}) %collective-permute-start.14) | collective-permute-done | bytes 98336 | tf_op jit(solution)/shard_map/ppermute | solution.py:271
  51.4 2.1 %collective-permute-start.22 = (bf16[64,768]{1,0:T(8,128)(2,1)S(1)}, bf16[64,768]{1,0:T(8,128)(2,1)S(1)}, u32[]{:S(2)}, u32[]{:S(2)}) collective-permute-start(bf16[64,768]{1,0:T(8,128)(2,1)S(1)} %shard_map.100.refs_1_.a_ref), channel_id=1, source_target_pairs={{0,16},{2,18},{4,20},{6,22},{8,24},{10,26},{12,28},{14,30},{16,0},... | collective-permute-start | bytes 294920 | tf_op jit(solution)/shard_map/ppermute | solution.py:271
  53.5 0.2 collective-permute-done.16.refs_2_.came_ref
  53.7 2.3 %shard_map.102 = (bf16[128,1024]{1,0:T(8,128)(2,1)S(1)}, f32[64,1024]{1,0:T(8,128)S(1)}) custom-call(bf16[1024,1024]{1,0:T(8,128)(2,1)S(1)} %get-tuple-element.75.exp_ref, bf16[1024,128]{1,0:T(8,128)(2,1)S(1)} %get-tuple-element.76.v_ref, bf16[64,1024]{1,0:T(8,128)(2,1)S(1)} %get-tuple-element.77.kt_ref, bf16[64,1024]{1,0:T(8,128)(2,1)S(1)} %get-tuple-element.78.q_ref, ...), custom_call_target="tpu_custom_call" | custom-call | flops 2300000000 | tf_op jit(solution)/shard_map/pallas_call | solution.py:350
  56.1 0.1 shard_map.103.kept_ref
  56.1 0.1 shard_map.104
  56.2 2.3 %collective-permute-start.19 = (bf16[192,256]{1,0:T(8,128)(2,1)S(1)}, bf16[192,256]{1,0:T(8,128)(2,1)S(1)}, u32[]{:S(2)}, u32[]{:S(2)}) collective-permute-start(bf16[192,256]{1,0:T(8,128)(2,1)S(1)} %get-tuple-element.120), channel_id=1, source_target_pairs={{0,24},{2,26},{4,28},{6,30},{8,16},{10,18},{12,20},{14,22},{16,8},... | collective-permute-start | bytes 294920 | tf_op jit(solution)/shard_map/ppermute | solution.py:271
  58.5 0.1 collective-permute-start.20
  58.6 2.1 %collective-permute-start.21 = (bf16[192,256]{1,0:T(8,128)(2,1)S(1)}, bf16[192,256]{1,0:T(8,128)(2,1)S(1)}, u32[]{:S(2)}, u32[]{:S(2)}) collective-permute-start(bf16[192,256]{1,0:T(8,128)(2,1)S(1)} %get-tuple-element.122), channel_id=1, source_target_pairs={{0,8},{2,10},{4,12},{6,14},{8,0},{10,2},{12,4},{14,6},{16,24},{18,... | collective-permute-start | bytes 294920 | tf_op jit(solution)/shard_map/ppermute | solution.py:271
  60.7 0.0 collective-permute-done.22.b_ref
  60.7 1.3 %collective-permute-start.23 = (bf16[64,768]{1,0:T(8,128)(2,1)S(1)}, bf16[64,768]{1,0:T(8,128)(2,1)S(1)}, u32[]{:S(2)}, u32[]{:S(2)}) collective-permute-start(bf16[64,768]{1,0:T(8,128)(2,1)S(1)} %shard_map.105.refs_0_), channel_id=1, source_target_pairs={{0,4},{2,6},{4,0},{6,2},{8,12},{10,14},{12,8},{14,10},{16,20},{18,... | collective-permute-start | bytes 294920 | tf_op jit(solution)/shard_map/ppermute | solution.py:271
  62.0 1.5 %collective-permute-done.19.refs_1_ = bf16[192,256]{1,0:T(8,128)(2,1)S(1)} collective-permute-done((bf16[192,256]{1,0:T(8,128)(2,1)S(1)}, bf16[192,256]{1,0:T(8,128)(2,1)S(1)}, u32[]{:S(2)}, u32[]{:S(2)}) %collective-permute-start.19) | collective-permute-done | bytes 98336 | tf_op jit(solution)/shard_map/ppermute | solution.py:271
  63.6 3.1 %collective-permute-done.20.refs_2_ = bf16[192,256]{1,0:T(8,128)(2,1)S(1)} collective-permute-done((bf16[192,256]{1,0:T(8,128)(2,1)S(1)}, bf16[192,256]{1,0:T(8,128)(2,1)S(1)}, u32[]{:S(2)}, u32[]{:S(2)}) %collective-permute-start.20) | collective-permute-done | bytes 98336 | tf_op jit(solution)/shard_map/ppermute | solution.py:271
  66.7 0.1 collective-permute-start.25
  66.8 1.1 %shard_map.108 = (f32[1024,128]{1,0:T(8,128)}, f32[4,64,256]{2,1,0:T(8,128)}, bf16[256,768]{1,0:T(8,128)(2,1)}) custom-call(bf16[192,256]{1,0:T(8,128)(2,1)S(1)} %get-tuple-element.119.refs_0_, bf16[192,256]{1,0:T(8,128)(2,1)S(1)} %collective-permute-done.19.refs_1_, bf16[192,256]{1,0:T(8,128)(2,1)S(1)} %collective-permute-done.20.refs_2_, ...), custom_call_target="tpu_custom_call" | custom-call | flops 5750000128 | tf_op jit(solution)/shard_map/pallas_call | solution.py:383
  67.9 0.0 collective-permute-done.24.refs_1_
  67.9 0.2 collective-permute-done.25.refs_3_
  68.1 0.9 %shard_map.109 = f32[4,64,768]{2,1,0:T(8,128)} custom-call(bf16[64,768]{1,0:T(8,128)(2,1)S(1)} %shard_map.105.refs_0_, bf16[64,768]{1,0:T(8,128)(2,1)S(1)} %collective-permute-done.24.refs_1_, bf16[64,768]{1,0:T(8,128)(2,1)S(1)} %shard_map.107.refs_6_.refs_2_, bf16[64,768]{1,0:T(8,128)(2,1)S(1)} %collective-permute-done.25.refs_3_), custom_call_target="tpu_custom_call" | custom-call | flops 575000000 | tf_op jit(solution)/shard_map/pallas_call | solution.py:377
  (24 shorter events, 0.2 us)
Async XLA Ops:
  0.6 7.6 %copy-start.1 = (bf16[4,64,768]{2,1,0:T(8,128)(2,1)S(1)}, bf16[4,64,768]{2,1,0:T(8,128)(2,1)}, u32[]{:S(2)}) copy-start(bf16[4,64,768]{2,1,0:T(8,128)(2,1)} %w_ref.3) | copy-start | bytes 1179652
  0.6 7.6 %copy-start.2 = (bf16[256,768]{1,0:T(8,128)(2,1)S(1)}, bf16[256,768]{1,0:T(8,128)(2,1)}, u32[]{:S(2)}) copy-start(bf16[256,768]{1,0:T(8,128)(2,1)} %go_ref.3) | copy-start | bytes 1179652
  0.7 7.5 %copy-start.3 = (bf16[256,4,64]{0,2,1:T(8,128)(2,1)S(1)}, bf16[256,4,64]{0,2,1:T(8,128)(2,1)}, u32[]{:S(2)}) copy-start(bf16[256,4,64]{0,2,1:T(8,128)(2,1)} %param.5) | copy-start | bytes 393220
  0.7 7.5 %copy-start.4 = (s32[2]{0:T(128)S(1)}, s32[2]{0:T(128)}, u32[]{:S(2)}) copy-start(s32[2]{0:T(128)} %fill_ref.5) | copy-start | bytes 28
  2.6 10.4 %collective-permute-start = (bf16[256,128]{1,0:T(8,128)(2,1)}, bf16[256,128]{1,0:T(8,128)(2,1)S(1)}, u32[]{:S(2)}, u32[]{:S(2)}) collective-permute-start(bf16[256,128]{1,0:T(8,128)(2,1)} %get-tuple-element.66), channel_id=1, source_target_pairs={{0,24},{2,26},{4,28},{6,30},{8,16},{10,18},{12,20},{14,22},{16,8},... | collective-permute-start | bytes 196616 | tf_op jit(solution)/shard_map/ppermute | solution.py:271
  7.6 8.4 %collective-permute-start.1 = (bf16[256,128]{1,0:T(8,128)(2,1)}, bf16[256,128]{1,0:T(8,128)(2,1)S(1)}, u32[]{:S(2)}, u32[]{:S(2)}) collective-permute-start(bf16[256,128]{1,0:T(8,128)(2,1)} %get-tuple-element.67), channel_id=1, source_target_pairs={{0,16},{2,18},{4,20},{6,22},{8,24},{10,26},{12,28},{14,30},{16,0},... | collective-permute-start | bytes 196616 | tf_op jit(solution)/shard_map/ppermute | solution.py:271
  7.6 8.4 %collective-permute-start.2 = (bf16[256,128]{1,0:T(8,128)(2,1)}, bf16[256,128]{1,0:T(8,128)(2,1)S(1)}, u32[]{:S(2)}, u32[]{:S(2)}) collective-permute-start(bf16[256,128]{1,0:T(8,128)(2,1)} %get-tuple-element.68), channel_id=1, source_target_pairs={{0,8},{2,10},{4,12},{6,14},{8,0},{10,2},{12,4},{14,6},{16,24},{18,... | collective-permute-start | bytes 196616 | tf_op jit(solution)/shard_map/ppermute | solution.py:271
  8.2 7.8 %copy-start = (bf16[256,128]{1,0:T(8,128)(2,1)S(1)}, bf16[256,128]{1,0:T(8,128)(2,1)}, u32[]{:S(2)}) copy-start(bf16[256,128]{1,0:T(8,128)(2,1)} %get-tuple-element.65.refs_0_) | copy-start | bytes 196612
  9.1 7.3 %collective-permute-start.3 = (bf16[128,256]{1,0:T(8,128)(2,1)S(1)}, bf16[128,256]{1,0:T(8,128)(2,1)S(1)}, u32[]{:S(2)}, u32[]{:S(2)}) collective-permute-start(bf16[128,256]{1,0:T(8,128)(2,1)S(1)} %get-tuple-element.70), channel_id=1, source_target_pairs={{0,24},{2,26},{4,28},{6,30},{8,16},{10,18},{12,20},{14,22},{16,8},... | collective-permute-start | bytes 196616 | tf_op jit(solution)/shard_map/ppermute | solution.py:271
  13.0 6.1 %collective-permute-start.4 = (bf16[128,256]{1,0:T(8,128)(2,1)S(1)}, bf16[128,256]{1,0:T(8,128)(2,1)S(1)}, u32[]{:S(2)}, u32[]{:S(2)}) collective-permute-start(bf16[128,256]{1,0:T(8,128)(2,1)S(1)} %get-tuple-element.71), channel_id=1, source_target_pairs={{0,16},{2,18},{4,20},{6,22},{8,24},{10,26},{12,28},{14,30},{16,0},... | collective-permute-start | bytes 196616 | tf_op jit(solution)/shard_map/ppermute | solution.py:271
  13.0 6.1 %collective-permute-start.5 = (bf16[128,256]{1,0:T(8,128)(2,1)S(1)}, bf16[128,256]{1,0:T(8,128)(2,1)S(1)}, u32[]{:S(2)}, u32[]{:S(2)}) collective-permute-start(bf16[128,256]{1,0:T(8,128)(2,1)S(1)} %get-tuple-element.72), channel_id=1, source_target_pairs={{0,8},{2,10},{4,12},{6,14},{8,0},{10,2},{12,4},{14,6},{16,24},{18,... | collective-permute-start | bytes 196616 | tf_op jit(solution)/shard_map/ppermute | solution.py:271
  16.0 9.0 %collective-permute-start.7 = (bf16[1024,128]{1,0:T(8,128)(2,1)S(1)}, bf16[1024,128]{1,0:T(8,128)(2,1)S(1)}, u32[]{:S(2)}, u32[]{:S(2)}) collective-permute-start(bf16[1024,128]{1,0:T(8,128)(2,1)S(1)} %shard_map.86.pair_ref), channel_id=1, source_target_pairs={{0,4},{2,6},{4,0},{6,2},{8,12},{10,14},{12,8},{14,10},{16,20},{18,... | collective-permute-start | bytes 786440 | tf_op jit(solution)/shard_map/ppermute | solution.py:271
  16.4 5.7 %collective-permute-start.6 = (bf16[1024,128]{1,0:T(8,128)(2,1)S(1)}, bf16[1024,128]{1,0:T(8,128)(2,1)S(1)}, u32[]{:S(2)}, u32[]{:S(2)}) collective-permute-start(bf16[1024,128]{1,0:T(8,128)(2,1)S(1)} %shard_map.86.pair_ref), channel_id=1, source_target_pairs={{0,2},{2,0},{4,6},{6,4},{8,10},{10,8},{12,14},{14,12},{16,18},{18,... | collective-permute-start | bytes 786440 | tf_op jit(solution)/shard_map/ppermute | solution.py:271
  25.1 3.0 %collective-permute-start.8 = (bf16[1024,128]{1,0:T(8,128)(2,1)S(1)}, bf16[1024,128]{1,0:T(8,128)(2,1)S(1)}, u32[]{:S(2)}, u32[]{:S(2)}) collective-permute-start(bf16[1024,128]{1,0:T(8,128)(2,1)S(1)} %shard_map.90.pair_ref), channel_id=1, source_target_pairs={{0,2},{2,0},{4,6},{6,4},{8,10},{10,8},{12,14},{14,12},{16,18},{18,... | collective-permute-start | bytes 786440 | tf_op jit(solution)/shard_map/ppermute | solution.py:271
  31.4 6.7 %collective-permute-start.9 = (bf16[64,256]{1,0:T(8,128)(2,1)S(1)}, bf16[64,256]{1,0:T(8,128)(2,1)S(1)}, u32[]{:S(2)}, u32[]{:S(2)}) collective-permute-start(bf16[64,256]{1,0:T(8,128)(2,1)S(1)} %get-tuple-element.104), channel_id=1, source_target_pairs={{0,24},{2,26},{4,28},{6,30},{8,16},{10,18},{12,20},{14,22},{16,8},... | collective-permute-start | bytes 98312 | tf_op jit(solution)/shard_map/ppermute | solution.py:271
  34.1 4.8 %collective-permute-start.10 = (bf16[64,256]{1,0:T(8,128)(2,1)S(1)}, bf16[64,256]{1,0:T(8,128)(2,1)S(1)}, u32[]{:S(2)}, u32[]{:S(2)}) collective-permute-start(bf16[64,256]{1,0:T(8,128)(2,1)S(1)} %get-tuple-element.105), channel_id=1, source_target_pairs={{0,16},{2,18},{4,20},{6,22},{8,24},{10,26},{12,28},{14,30},{16,0},... | collective-permute-start | bytes 98312 | tf_op jit(solution)/shard_map/ppermute | solution.py:271
  34.1 4.8 %collective-permute-start.11 = (bf16[64,256]{1,0:T(8,128)(2,1)S(1)}, bf16[64,256]{1,0:T(8,128)(2,1)S(1)}, u32[]{:S(2)}, u32[]{:S(2)}) collective-permute-start(bf16[64,256]{1,0:T(8,128)(2,1)S(1)} %get-tuple-element.106), channel_id=1, source_target_pairs={{0,8},{2,10},{4,12},{6,14},{8,0},{10,2},{12,4},{14,6},{16,24},{18,... | collective-permute-start | bytes 98312 | tf_op jit(solution)/shard_map/ppermute | solution.py:271
  39.9 2.1 %collective-permute-start.12 = (bf16[2,64,768]{2,1,0:T(8,128)(2,1)S(1)}, bf16[2,64,768]{2,1,0:T(8,128)(2,1)S(1)}, u32[]{:S(2)}, u32[]{:S(2)}) collective-permute-start(bf16[2,64,768]{2,1,0:T(8,128)(2,1)S(1)} %get-tuple-element.109), channel_id=1, source_target_pairs={{0,2},{2,0},{4,6},{6,4},{8,10},{10,8},{12,14},{14,12},{16,18},{18,... | collective-permute-start | bytes 589832 | tf_op jit(solution)/shard_map/ppermute | solution.py:271
  39.9 5.9 %collective-permute-start.15 = (bf16[128,1024]{1,0:T(8,128)(2,1)S(1)}, bf16[128,1024]{1,0:T(8,128)(2,1)S(1)}, u32[]{:S(2)}, u32[]{:S(2)}) collective-permute-start(bf16[128,1024]{1,0:T(8,128)(2,1)S(1)} %get-tuple-element.107.refs_4_), channel_id=1, source_target_pairs={{0,2},{2,0},{4,6},{6,4},{8,10},{10,8},{12,14},{14,12},{16,18},{18,... | collective-permute-start | bytes 786440 | tf_op jit(solution)/shard_map/ppermute | solution.py:271
  40.4 13.1 %collective-permute-start.17 = (bf16[256,768]{1,0:T(8,128)(2,1)S(1)}, bf16[256,768]{1,0:T(8,128)(2,1)S(1)}, u32[]{:S(2)}, u32[]{:S(2)}) collective-permute-start(bf16[256,768]{1,0:T(8,128)(2,1)S(1)} %get-tuple-element.116.refs_4_), channel_id=1, source_target_pairs={{0,1},{1,0},{2,3},{3,2},{4,5},{5,4},{6,7},{7,6},{8,9},{9,8},{10,11... | collective-permute-start | bytes 1179656 | tf_op jit(solution)/shard_map/ppermute | solution.py:271
  42.0 4.7 %collective-permute-start.13 = (bf16[64,768]{1,0:T(8,128)(2,1)S(1)}, bf16[64,768]{1,0:T(8,128)(2,1)S(1)}, u32[]{:S(2)}, u32[]{:S(2)}) collective-permute-start(bf16[64,768]{1,0:T(8,128)(2,1)S(1)} %get-tuple-element.112), channel_id=1, source_target_pairs={{0,4},{2,6},{4,0},{6,2},{8,12},{10,14},{12,8},{14,10},{16,20},{18,... | collective-permute-start | bytes 294920 | tf_op jit(solution)/shard_map/ppermute | solution.py:271
  46.0 7.8 %collective-permute-start.16 = (bf16[128,1024]{1,0:T(8,128)(2,1)S(1)}, bf16[128,1024]{1,0:T(8,128)(2,1)S(1)}, u32[]{:S(2)}, u32[]{:S(2)}) collective-permute-start(bf16[128,1024]{1,0:T(8,128)(2,1)S(1)} %shard_map.101), channel_id=1, source_target_pairs={{0,4},{2,6},{4,0},{6,2},{8,12},{10,14},{12,8},{14,10},{16,20},{18,... | collective-permute-start | bytes 786440 | tf_op jit(solution)/shard_map/ppermute | solution.py:271
  46.7 4.7 %collective-permute-start.14 = (bf16[64,768]{1,0:T(8,128)(2,1)S(1)}, bf16[64,768]{1,0:T(8,128)(2,1)S(1)}, u32[]{:S(2)}, u32[]{:S(2)}) collective-permute-start(bf16[64,768]{1,0:T(8,128)(2,1)S(1)} %shard_map.98.refs_1_.a_ref), channel_id=1, source_target_pairs={{0,8},{2,10},{4,12},{6,14},{8,0},{10,2},{12,4},{14,6},{16,24},{18,... | collective-permute-start | bytes 294920 | tf_op jit(solution)/shard_map/ppermute | solution.py:271
  49.9 6.1 %collective-permute-start.18 = (bf16[128,1024]{1,0:T(8,128)(2,1)S(1)}, bf16[128,1024]{1,0:T(8,128)(2,1)S(1)}, u32[]{:S(2)}, u32[]{:S(2)}) collective-permute-start(bf16[128,1024]{1,0:T(8,128)(2,1)S(1)} %get-tuple-element.115.refs_0_), channel_id=1, source_target_pairs={{0,2},{2,0},{4,6},{6,4},{8,10},{10,8},{12,14},{14,12},{16,18},{18,... | collective-permute-start | bytes 786440 | tf_op jit(solution)/shard_map/ppermute | solution.py:271
  51.4 9.3 %collective-permute-start.22 = (bf16[64,768]{1,0:T(8,128)(2,1)S(1)}, bf16[64,768]{1,0:T(8,128)(2,1)S(1)}, u32[]{:S(2)}, u32[]{:S(2)}) collective-permute-start(bf16[64,768]{1,0:T(8,128)(2,1)S(1)} %shard_map.100.refs_1_.a_ref), channel_id=1, source_target_pairs={{0,16},{2,18},{4,20},{6,22},{8,24},{10,26},{12,28},{14,30},{16,0},... | collective-permute-start | bytes 294920 | tf_op jit(solution)/shard_map/ppermute | solution.py:271
  56.2 7.4 %collective-permute-start.19 = (bf16[192,256]{1,0:T(8,128)(2,1)S(1)}, bf16[192,256]{1,0:T(8,128)(2,1)S(1)}, u32[]{:S(2)}, u32[]{:S(2)}) collective-permute-start(bf16[192,256]{1,0:T(8,128)(2,1)S(1)} %get-tuple-element.120), channel_id=1, source_target_pairs={{0,24},{2,26},{4,28},{6,30},{8,16},{10,18},{12,20},{14,22},{16,8},... | collective-permute-start | bytes 294920 | tf_op jit(solution)/shard_map/ppermute | solution.py:271
  58.5 8.2 %collective-permute-start.20 = (bf16[192,256]{1,0:T(8,128)(2,1)S(1)}, bf16[192,256]{1,0:T(8,128)(2,1)S(1)}, u32[]{:S(2)}, u32[]{:S(2)}) collective-permute-start(bf16[192,256]{1,0:T(8,128)(2,1)S(1)} %get-tuple-element.121), channel_id=1, source_target_pairs={{0,16},{2,18},{4,20},{6,22},{8,24},{10,26},{12,28},{14,30},{16,0},... | collective-permute-start | bytes 294920 | tf_op jit(solution)/shard_map/ppermute | solution.py:271
  58.6 8.1 %collective-permute-start.21 = (bf16[192,256]{1,0:T(8,128)(2,1)S(1)}, bf16[192,256]{1,0:T(8,128)(2,1)S(1)}, u32[]{:S(2)}, u32[]{:S(2)}) collective-permute-start(bf16[192,256]{1,0:T(8,128)(2,1)S(1)} %get-tuple-element.122), channel_id=1, source_target_pairs={{0,8},{2,10},{4,12},{6,14},{8,0},{10,2},{12,4},{14,6},{16,24},{18,... | collective-permute-start | bytes 294920 | tf_op jit(solution)/shard_map/ppermute | solution.py:271
  60.7 6.0 %collective-permute-start.23 = (bf16[64,768]{1,0:T(8,128)(2,1)S(1)}, bf16[64,768]{1,0:T(8,128)(2,1)S(1)}, u32[]{:S(2)}, u32[]{:S(2)}) collective-permute-start(bf16[64,768]{1,0:T(8,128)(2,1)S(1)} %shard_map.105.refs_0_), channel_id=1, source_target_pairs={{0,4},{2,6},{4,0},{6,2},{8,12},{10,14},{12,8},{14,10},{16,20},{18,... | collective-permute-start | bytes 294920 | tf_op jit(solution)/shard_map/ppermute | solution.py:271
  62.0 5.9 %collective-permute-start.24 = (bf16[64,768]{1,0:T(8,128)(2,1)S(1)}, bf16[64,768]{1,0:T(8,128)(2,1)S(1)}, u32[]{:S(2)}, u32[]{:S(2)}) collective-permute-start(bf16[64,768]{1,0:T(8,128)(2,1)S(1)} %shard_map.105.refs_0_), channel_id=1, source_target_pairs={{0,2},{2,0},{4,6},{6,4},{8,10},{10,8},{12,14},{14,12},{16,18},{18,... | collective-permute-start | bytes 294920 | tf_op jit(solution)/shard_map/ppermute | solution.py:271
  66.7 1.4 %collective-permute-start.25 = (bf16[64,768]{1,0:T(8,128)(2,1)S(1)}, bf16[64,768]{1,0:T(8,128)(2,1)S(1)}, u32[]{:S(2)}, u32[]{:S(2)}) collective-permute-start(bf16[64,768]{1,0:T(8,128)(2,1)S(1)} %shard_map.107.refs_6_.refs_2_), channel_id=1, source_target_pairs={{0,2},{2,0},{4,6},{6,4},{8,10},{10,8},{12,14},{14,12},{16,18},{18,... | collective-permute-start | bytes 294920 | tf_op jit(solution)/shard_map/ppermute | solution.py:271

commit v17 on v15

--- a/solution.py
+++ b/solution.py
@@ -55,18 +55,30 @@
 
 
 def spread(slots):
-    return [0] + sorted(range(1, slots), key=lambda mask: (mask < slots // 2, mask))
-
-
-def pack_kv_kernel(heads, rows, dim, a_of, fill_ref, kv_ref, *refs):
-    outs, (held,) = refs[:heads], refs[heads:]
+    return [0] + list(range(slots - 1, 0, -1))
+
+
+def pack_kv_kernel(heads, rows, dim, a_of, fill_ref, kv_hbm, *refs):
+    outs, (kv_ref, held, made, in_sems, out_sems) = refs[:heads], refs[heads:]
+    half = rows * heads // 2
+    parts = [pl.ds(0, half), pl.ds(half, half)]
+    loads = [pltpu.make_async_copy(kv_hbm.at[part], kv_ref.at[part], in_sems.at[i]) for i, part in enumerate(parts)]
+    for load in loads:
+        load.start()
     live = live_column(fill_ref, rows)
     lane = lax.broadcasted_iota(jnp.int32, (rows, 2 * dim), 1)
     mark = jnp.where(lane == 0, DEAD * (1.0 - live), 0.0)
-    held[...] = kv_ref[...].astype(F32)
+    for load, part in zip(loads, parts):
+        load.wait()
+        held[part, :] = kv_ref[part, :].astype(F32)
     me = a_of()
-    for slot, mask in enumerate(spread(heads)):
-        outs[slot][...] = (held[pl.ds(me ^ mask, rows, stride=heads), :] * live + mark).astype(BF16)
+    stores = [pltpu.make_async_copy(made.at[slot], outs[slot], out_sems.at[slot]) for slot in range(heads)]
+    masks = spread(heads)
+    for slot in [*range(1, heads), 0]:
+        made[slot] = (held[pl.ds(me ^ masks[slot], rows, stride=heads), :] * live + mark).astype(BF16)
+        stores[slot].start()
+    for store in stores:
+        store.wait()
 
 
 def pack_qg_kernel(heads, rows, dim, a_of, fill_ref, q_ref, w_ref, go_ref, *refs):
@@ -279,10 +291,17 @@
         return [pieces[0]] + [swap(piece, mask * columns) for piece, mask in zip(pieces[1:], spread(slots)[1:])]
 
     block, wide = slots * rows, 2 * dim
-    kv_mine = exchange(call(
+    kv_mine = exchange(pl.pallas_call(
         functools.partial(pack_kv_kernel, heads, rows, dim, a_of),
-        [((rows, wide), BF16)] * slots, [pltpu.VMEM((rows * heads, wide), F32)],
-        n_in=2, smem_first=True, micros=1.5, limit=56,
+        out_shape=[jax.ShapeDtypeStruct((rows, wide), BF16)] * slots,
+        in_specs=[SMEM, pl.BlockSpec(memory_space=pl.ANY)],
+        out_specs=[pl.BlockSpec(memory_space=pl.ANY)] * slots,
+        scratch_shapes=[
+            pltpu.VMEM((rows * heads, wide), BF16), pltpu.VMEM((rows * heads, wide), F32), pltpu.VMEM((heads, rows, wide), BF16),
+            pltpu.SemaphoreType.DMA((2,)), pltpu.SemaphoreType.DMA((heads,)),
+        ],
+        compiler_params=pltpu.CompilerParams(vmem_limit_bytes=56 * MIB),
+        cost_estimate=pl.CostEstimate(flops=int(1.5 * 1.15e9), bytes_accessed=0, transcendentals=0),
     )(tile_fill, key_value.reshape(rows * heads, wide)))
     qg_send = call(
         functools.partial(pack_qg_kernel, heads, rows, dim, a_of),

time: 68.4 us -> 69.9 us (1.022)
  starting transfers between devices: 25.1 us -> 28.3 us
  waiting for transfers between devices: 15.3 us -> 12.8 us
  Pallas kernels: 26.9 us -> 27.7 us
    ppermute x26, starting transfers between devices: 25.1 us -> 28.3 us  [swap(): return lax.ppermute(array, axis, [(i, i ^ mask) for i in range(size)])]
    ppermute x26, waiting for transfers between devices: 15.3 us -> 12.8 us  [swap(): return lax.ppermute(array, axis, [(i, i ^ mask) for i in range(size)])]
    pallas_call x1, Pallas kernels: 1.9 us -> 2.64 us  [shards(): pl.pallas_call(functools.partial(pack_kv_kernel, heads, rows, dim, a_of),...]
  transfers between devices with their start and end apart: 26 -> 26, of which waited for: 10 -> 9; matrix products, arithmetic and copies ran while one was open for 0% -> 0% of each run, Pallas kernels for 29% -> 29%
where the time goes in v17:
time: 69.9 us; the launch traced here: 69.7 us
  starting transfers between devices  28.3 us (40%)
  Pallas kernels  27.7 us (40%)
  waiting for transfers between devices  12.8 us (18%)
  between operations  0.93 us (1%)
    ppermute x26, starting transfers between devices, swap(): return lax.ppermute(array, axis, [(i, i ^ mask) for i in range(size)])  28.3 us
    ppermute x26, waiting for transfers between devices, swap(): return lax.ppermute(array, axis, [(i, i ^ mask) for i in range(size)])  12.8 us
    pallas_call x4, Pallas kernels, shards(): call(functools.partial(score_kernel, slots, rows, dim, step), [((block, b...  11.9 us
    pallas_call x4, Pallas kernels, shards(): call(functools.partial(back_kernel, slots, rows, dim, dq is None), [((wid...  8.65 us
    pallas_call x1, Pallas kernels, shards(): pl.pallas_call(functools.partial(pack_kv_kernel, heads, rows, dim, a_of),...  2.64 us
  transfers between devices with their start and end apart: 26, of which 9 were waited for; matrix products, arithmetic and copies ran while one was open for 0% of the time, Pallas kernels for 29%

profile of v17, /device:TPU:0, one launch (start us, length us, event | category | flops | bytes accessed | tf_op | source)
XLA Modules:
  0.0 69.7 jit_solution(5158037830242692136)
XLA Ops:
  0.7 2.6 %shard_map.84 = (bf16[256,128]{1,0:T(8,128)(2,1)}, bf16[256,128]{1,0:T(8,128)(2,1)}, bf16[256,128]{1,0:T(8,128)(2,1)}, bf16[256,128]{1,0:T(8,128)(2,1)}) custom-call(s32[2]{0:T(128)} %fill_ref.5, bf16[1024,128]{1,0:T(8,128)(2,1)} %bitcast.5), custom_call_target="tpu_custom_call" | custom-call | flops 1724999936 | tf_op jit(solution)/shard_map/pallas_call | solution.py:294
  3.3 5.1 %collective-permute-start = (bf16[256,128]{1,0:T(8,128)(2,1)}, bf16[256,128]{1,0:T(8,128)(2,1)S(1)}, u32[]{:S(2)}, u32[]{:S(2)}) collective-permute-start(bf16[256,128]{1,0:T(8,128)(2,1)} %get-tuple-element.66), channel_id=1, source_target_pairs={{0,24},{2,26},{4,28},{6,30},{8,16},{10,18},{12,20},{14,22},{16,8},... | collective-permute-start | bytes 196616 | tf_op jit(solution)/shard_map/ppermute | solution.py:288
  8.4 0.0 collective-permute-start.1
  8.4 0.6 collective-permute-start.2
  9.1 0.0 copy-start
  9.1 0.9 %shard_map.85 = (bf16[128,256]{1,0:T(8,128)(2,1)S(1)}, bf16[128,256]{1,0:T(8,128)(2,1)S(1)}, bf16[128,256]{1,0:T(8,128)(2,1)S(1)}, bf16[128,256]{1,0:T(8,128)(2,1)S(1)}) custom-call(s32[2]{0:T(128)S(1)} %copy-done.4, bf16[4,64,256]{2,1,0:T(8,128)(2,1)S(1)} %bitcast.4, bf16[4,64,768]{2,1,0:T(8,128)(2,1)S(1)} %copy-done.1, bf16[256,768]{1,0:T(8,128)(2,1)S(1)} %copy-done.2), custom_call_target="tpu_custom_call" | custom-call | flops 1150000000 | tf_op jit(solution)/shard_map/pallas_call | solution.py:306
  10.0 3.8 %collective-permute-start.3 = (bf16[128,256]{1,0:T(8,128)(2,1)S(1)}, bf16[128,256]{1,0:T(8,128)(2,1)S(1)}, u32[]{:S(2)}, u32[]{:S(2)}) collective-permute-start(bf16[128,256]{1,0:T(8,128)(2,1)S(1)} %get-tuple-element.70), channel_id=1, source_target_pairs={{0,24},{2,26},{4,28},{6,30},{8,16},{10,18},{12,20},{14,22},{16,8},... | collective-permute-start | bytes 196616 | tf_op jit(solution)/shard_map/ppermute | solution.py:288
  13.8 0.0 collective-permute-start.4
  13.8 0.0 collective-permute-done.refs_1_
  13.8 0.6 collective-permute-start.5
  14.4 2.4 %collective-permute-done.1.refs_2_ = bf16[256,128]{1,0:T(8,128)(2,1)S(1)} collective-permute-done((bf16[256,128]{1,0:T(8,128)(2,1)}, bf16[256,128]{1,0:T(8,128)(2,1)S(1)}, u32[]{:S(2)}, u32[]{:S(2)}) %collective-permute-start.1) | collective-permute-done | bytes 65568 | tf_op jit(solution)/shard_map/ppermute | solution.py:288
  16.8 0.0 collective-permute-done.2.refs_3_
  16.8 0.4 collective-permute-start.7
  17.2 0.0 collective-permute-start.6
  17.2 0.0 collective-permute-done.3.refs_1_
  17.2 2.6 %collective-permute-done.4.refs_2_ = bf16[128,256]{1,0:T(8,128)(2,1)S(1)} collective-permute-done((bf16[128,256]{1,0:T(8,128)(2,1)S(1)}, bf16[128,256]{1,0:T(8,128)(2,1)S(1)}, u32[]{:S(2)}, u32[]{:S(2)}) %collective-permute-start.4) | collective-permute-done | bytes 65568 | tf_op jit(solution)/shard_map/ppermute | solution.py:288
  19.9 0.0 collective-permute-done.5.refs_3_
  19.9 0.1 shard_map.87
  20.0 2.9 %shard_map.88 = (bf16[1024,1024]{1,0:T(8,128)(2,1)S(1)}, f32[1,1024]{1,0:T(1,128)S(1)}, f32[80,1024]{1,0:T(8,128)S(1)}, bf16[1024,128]{1,0:T(8,128)(2,1)S(1)}, bf16[64,1024]{1,0:T(8,128)(2,1)S(1)}) custom-call(bf16[1024,128]{1,0:T(8,128)(2,1)S(1)} %shard_map.86.pair_ref, bf16[256,1024]{1,0:T(8,128)(2,1)S(1)} %get-tuple-element.73.qa_ref, ...), custom_call_target="tpu_custom_call" | custom-call | flops 5750000128 | tf_op jit(solution)/shard_map/pallas_call | solution.py:332
  22.9 0.0 collective-permute-done.6.pair_ref
  22.9 2.9 %shard_map.89 = (bf16[1024,1024]{1,0:T(8,128)(2,1)S(1)}, f32[1,1024]{1,0:T(1,128)S(1)}, f32[80,1024]{1,0:T(8,128)S(1)}, bf16[1024,128]{1,0:T(8,128)(2,1)S(1)}, bf16[64,1024]{1,0:T(8,128)(2,1)S(1)}) custom-call(bf16[1024,128]{1,0:T(8,128)(2,1)S(1)} %collective-permute-done.6.pair_ref, bf16[256,1024]{1,0:T(8,128)(2,1)S(1)} %get-tuple-element.73.qa_ref, ...), custom_call_target="tpu_custom_call" | custom-call | flops 5750000128 | tf_op jit(solution)/shard_map/pallas_call | solution.py:332
  25.9 0.0 collective-permute-done.7.refs_0_
  25.9 0.1 collective-permute-start.8
  26.0 2.9 %shard_map.91 = (bf16[1024,1024]{1,0:T(8,128)(2,1)S(1)}, f32[1,1024]{1,0:T(1,128)S(1)}, f32[80,1024]{1,0:T(8,128)S(1)}, bf16[1024,128]{1,0:T(8,128)(2,1)S(1)}, bf16[64,1024]{1,0:T(8,128)(2,1)S(1)}) custom-call(bf16[1024,128]{1,0:T(8,128)(2,1)S(1)} %shard_map.90.pair_ref, bf16[256,1024]{1,0:T(8,128)(2,1)S(1)} %get-tuple-element.73.qa_ref, ...), custom_call_target="tpu_custom_call" | custom-call | flops 5750000128 | tf_op jit(solution)/shard_map/pallas_call | solution.py:332
  28.9 0.0 collective-permute-done.8.pair_ref
  29.0 3.1 %shard_map.92 = (bf16[1024,1024]{1,0:T(8,128)(2,1)S(1)}, f32[1,1024]{1,0:T(1,128)S(1)}, f32[80,1024]{1,0:T(8,128)S(1)}, bf16[1024,128]{1,0:T(8,128)(2,1)S(1)}, bf16[64,1024]{1,0:T(8,128)(2,1)S(1)}) custom-call(bf16[1024,128]{1,0:T(8,128)(2,1)S(1)} %collective-permute-done.8.pair_ref, bf16[256,1024]{1,0:T(8,128)(2,1)S(1)} %get-tuple-element.73.qa_ref, ...), custom_call_target="tpu_custom_call" | custom-call | flops 5750000128 | tf_op jit(solution)/shard_map/pallas_call | solution.py:332
  32.1 0.2 shard_map.93
  32.2 2.8 %collective-permute-start.9 = (bf16[64,256]{1,0:T(8,128)(2,1)S(1)}, bf16[64,256]{1,0:T(8,128)(2,1)S(1)}, u32[]{:S(2)}, u32[]{:S(2)}) collective-permute-start(bf16[64,256]{1,0:T(8,128)(2,1)S(1)} %get-tuple-element.104), channel_id=1, source_target_pairs={{0,24},{2,26},{4,28},{6,30},{8,16},{10,18},{12,20},{14,22},{16,8},... | collective-permute-start | bytes 98312 | tf_op jit(solution)/shard_map/ppermute | solution.py:288
  35.0 0.0 collective-permute-start.10
  35.0 1.7 %collective-permute-start.11 = (bf16[64,256]{1,0:T(8,128)(2,1)S(1)}, bf16[64,256]{1,0:T(8,128)(2,1)S(1)}, u32[]{:S(2)}, u32[]{:S(2)}) collective-permute-start(bf16[64,256]{1,0:T(8,128)(2,1)S(1)} %get-tuple-element.106), channel_id=1, source_target_pairs={{0,8},{2,10},{4,12},{6,14},{8,0},{10,2},{12,4},{14,6},{16,24},{18,... | collective-permute-start | bytes 98312 | tf_op jit(solution)/shard_map/ppermute | solution.py:288
  36.7 2.2 %shard_map.94 = (bf16[128,1024]{1,0:T(8,128)(2,1)S(1)}, f32[64,1024]{1,0:T(8,128)S(1)}) custom-call(bf16[1024,1024]{1,0:T(8,128)(2,1)S(1)} %get-tuple-element.98.exp_ref, bf16[1024,128]{1,0:T(8,128)(2,1)S(1)} %get-tuple-element.99.v_ref, bf16[64,1024]{1,0:T(8,128)(2,1)S(1)} %get-tuple-element.100.kt_ref, bf16[64,1024]{1,0:T(8,128)(2,1)S(1)} %get-tuple-element.78.q_ref, ...), custom_call_target="tpu_custom_call" | custom-call | flops 2300000000 | tf_op jit(solution)/shard_map/pallas_call | solution.py:374
  38.9 0.0 collective-permute-done.9.refs_1_
  38.9 1.0 %collective-permute-done.10.refs_2_ = bf16[64,256]{1,0:T(8,128)(2,1)S(1)} collective-permute-done((bf16[64,256]{1,0:T(8,128)(2,1)S(1)}, bf16[64,256]{1,0:T(8,128)(2,1)S(1)}, u32[]{:S(2)}, u32[]{:S(2)}) %collective-permute-start.10) | collective-permute-done | bytes 32800 | tf_op jit(solution)/shard_map/ppermute | solution.py:288
  39.8 0.9 %shard_map.95 = (bf16[256,768]{1,0:T(8,128)(2,1)S(1)}, bf16[2,64,768]{2,1,0:T(8,128)(2,1)S(1)}, bf16[2,64,768]{2,1,0:T(8,128)(2,1)S(1)}) custom-call(s32[2]{0:T(128)S(1)} %copy-done.4, bf16[256,768]{1,0:T(8,128)(2,1)S(1)} %copy-done.2, bf16[4,64,768]{2,1,0:T(8,128)(2,1)S(1)} %copy-done.1, bf16[64,256]{1,0:T(8,128)(2,1)S(1)} %get-tuple-element.103.refs_0_, ...), custom_call_target="tpu_custom_call" | custom-call | flops 805000000 | tf_op jit(solution)/shard_map/pallas_call | solution.py:352
  40.8 0.1 collective-permute-start.12
  40.8 0.5 collective-permute-start.15
  41.3 1.5 %collective-permute-start.17 = (bf16[256,768]{1,0:T(8,128)(2,1)S(1)}, bf16[256,768]{1,0:T(8,128)(2,1)S(1)}, u32[]{:S(2)}, u32[]{:S(2)}) collective-permute-start(bf16[256,768]{1,0:T(8,128)(2,1)S(1)} %get-tuple-element.116.refs_4_), channel_id=1, source_target_pairs={{0,1},{1,0},{2,3},{3,2},{4,5},{5,4},{6,7},{7,6},{8,9},{9,8},{10,11... | collective-permute-start | bytes 1179656 | tf_op jit(solution)/shard_map/ppermute | solution.py:288
  42.9 1.6 %collective-permute-start.13 = (bf16[64,768]{1,0:T(8,128)(2,1)S(1)}, bf16[64,768]{1,0:T(8,128)(2,1)S(1)}, u32[]{:S(2)}, u32[]{:S(2)}) collective-permute-start(bf16[64,768]{1,0:T(8,128)(2,1)S(1)} %get-tuple-element.112), channel_id=1, source_target_pairs={{0,4},{2,6},{4,0},{6,2},{8,12},{10,14},{12,8},{14,10},{16,20},{18,... | collective-permute-start | bytes 294920 | tf_op jit(solution)/shard_map/ppermute | solution.py:288
  44.5 2.2 %shard_map.97 = (bf16[128,1024]{1,0:T(8,128)(2,1)S(1)}, f32[64,1024]{1,0:T(8,128)S(1)}) custom-call(bf16[1024,1024]{1,0:T(8,128)(2,1)S(1)} %get-tuple-element.94.exp_ref, bf16[1024,128]{1,0:T(8,128)(2,1)S(1)} %get-tuple-element.95.v_ref, bf16[64,1024]{1,0:T(8,128)(2,1)S(1)} %get-tuple-element.96.kt_ref, bf16[64,1024]{1,0:T(8,128)(2,1)S(1)} %get-tuple-element.78.q_ref, ...), custom_call_target="tpu_custom_call" | custom-call | flops 2300000000 | tf_op jit(solution)/shard_map/pallas_call | solution.py:374
  46.6 0.0 collective-permute-done.15.b_ref
  46.6 0.1 shard_map.101
  46.7 0.6 collective-permute-start.16
  47.3 0.3 collective-permute-done.13.b_ref
  47.6 0.8 %collective-permute-start.14 = (bf16[64,768]{1,0:T(8,128)(2,1)S(1)}, bf16[64,768]{1,0:T(8,128)(2,1)S(1)}, u32[]{:S(2)}, u32[]{:S(2)}) collective-permute-start(bf16[64,768]{1,0:T(8,128)(2,1)S(1)} %shard_map.98.refs_1_.a_ref), channel_id=1, source_target_pairs={{0,8},{2,10},{4,12},{6,14},{8,0},{10,2},{12,4},{14,6},{16,24},{18,... | collective-permute-start | bytes 294920 | tf_op jit(solution)/shard_map/ppermute | solution.py:288
  48.4 2.2 %shard_map.99 = (bf16[128,1024]{1,0:T(8,128)(2,1)S(1)}, f32[64,1024]{1,0:T(8,128)S(1)}) custom-call(bf16[1024,1024]{1,0:T(8,128)(2,1)S(1)} %get-tuple-element.90.exp_ref, bf16[1024,128]{1,0:T(8,128)(2,1)S(1)} %get-tuple-element.91.v_ref, bf16[64,1024]{1,0:T(8,128)(2,1)S(1)} %get-tuple-element.92.kt_ref, bf16[64,1024]{1,0:T(8,128)(2,1)S(1)} %get-tuple-element.78.q_ref, ...), custom_call_target="tpu_custom_call" | custom-call | flops 2300000000 | tf_op jit(solution)/shard_map/pallas_call | solution.py:374
  50.6 0.1 collective-permute-start.18
  50.7 1.6 %collective-permute-done.14.b_ref = bf16[64,768]{1,0:T(8,128)(2,1)S(1)} collective-permute-done((bf16[64,768]{1,0:T(8,128)(2,1)S(1)}, bf16[64,768]{1,0:T(8,128)(2,1)S(1)}, u32[]{:S(2)}, u32[]{:S(2)}) %collective-permute-start.14) | collective-permute-done | bytes 98336 | tf_op jit(solution)/shard_map/ppermute | solution.py:288
  52.3 2.1 %collective-permute-start.22 = (bf16[64,768]{1,0:T(8,128)(2,1)S(1)}, bf16[64,768]{1,0:T(8,128)(2,1)S(1)}, u32[]{:S(2)}, u32[]{:S(2)}) collective-permute-start(bf16[64,768]{1,0:T(8,128)(2,1)S(1)} %shard_map.100.refs_1_.a_ref), channel_id=1, source_target_pairs={{0,16},{2,18},{4,20},{6,22},{8,24},{10,26},{12,28},{14,30},{16,0},... | collective-permute-start | bytes 294920 | tf_op jit(solution)/shard_map/ppermute | solution.py:288
  54.4 0.1 collective-permute-done.16.refs_2_.came_ref
  54.5 2.2 %shard_map.102 = (bf16[128,1024]{1,0:T(8,128)(2,1)S(1)}, f32[64,1024]{1,0:T(8,128)S(1)}) custom-call(bf16[1024,1024]{1,0:T(8,128)(2,1)S(1)} %get-tuple-element.75.exp_ref, bf16[1024,128]{1,0:T(8,128)(2,1)S(1)} %get-tuple-element.76.v_ref, bf16[64,1024]{1,0:T(8,128)(2,1)S(1)} %get-tuple-element.77.kt_ref, bf16[64,1024]{1,0:T(8,128)(2,1)S(1)} %get-tuple-element.78.q_ref, ...), custom_call_target="tpu_custom_call" | custom-call | flops 2300000000 | tf_op jit(solution)/shard_map/pallas_call | solution.py:374
  56.7 0.1 shard_map.103.kept_ref
  56.8 0.1 shard_map.104
  56.9 2.2 %collective-permute-start.19 = (bf16[192,256]{1,0:T(8,128)(2,1)S(1)}, bf16[192,256]{1,0:T(8,128)(2,1)S(1)}, u32[]{:S(2)}, u32[]{:S(2)}) collective-permute-start(bf16[192,256]{1,0:T(8,128)(2,1)S(1)} %get-tuple-element.120), channel_id=1, source_target_pairs={{0,24},{2,26},{4,28},{6,30},{8,16},{10,18},{12,20},{14,22},{16,8},... | collective-permute-start | bytes 294920 | tf_op jit(solution)/shard_map/ppermute | solution.py:288
  59.0 0.1 collective-permute-start.20
  59.2 2.2 %collective-permute-start.21 = (bf16[192,256]{1,0:T(8,128)(2,1)S(1)}, bf16[192,256]{1,0:T(8,128)(2,1)S(1)}, u32[]{:S(2)}, u32[]{:S(2)}) collective-permute-start(bf16[192,256]{1,0:T(8,128)(2,1)S(1)} %get-tuple-element.122), channel_id=1, source_target_pairs={{0,8},{2,10},{4,12},{6,14},{8,0},{10,2},{12,4},{14,6},{16,24},{18,... | collective-permute-start | bytes 294920 | tf_op jit(solution)/shard_map/ppermute | solution.py:288
  61.3 1.5 %collective-permute-start.23 = (bf16[64,768]{1,0:T(8,128)(2,1)S(1)}, bf16[64,768]{1,0:T(8,128)(2,1)S(1)}, u32[]{:S(2)}, u32[]{:S(2)}) collective-permute-start(bf16[64,768]{1,0:T(8,128)(2,1)S(1)} %shard_map.105.refs_0_), channel_id=1, source_target_pairs={{0,4},{2,6},{4,0},{6,2},{8,12},{10,14},{12,8},{14,10},{16,20},{18,... | collective-permute-start | bytes 294920 | tf_op jit(solution)/shard_map/ppermute | solution.py:288
  62.8 1.4 %collective-permute-done.19.refs_1_ = bf16[192,256]{1,0:T(8,128)(2,1)S(1)} collective-permute-done((bf16[192,256]{1,0:T(8,128)(2,1)S(1)}, bf16[192,256]{1,0:T(8,128)(2,1)S(1)}, u32[]{:S(2)}, u32[]{:S(2)}) %collective-permute-start.19) | collective-permute-done | bytes 98336 | tf_op jit(solution)/shard_map/ppermute | solution.py:288
  64.2 3.2 %collective-permute-done.20.refs_2_ = bf16[192,256]{1,0:T(8,128)(2,1)S(1)} collective-permute-done((bf16[192,256]{1,0:T(8,128)(2,1)S(1)}, bf16[192,256]{1,0:T(8,128)(2,1)S(1)}, u32[]{:S(2)}, u32[]{:S(2)}) %collective-permute-start.20) | collective-permute-done | bytes 98336 | tf_op jit(solution)/shard_map/ppermute | solution.py:288
  67.4 0.0 collective-permute-done.21.refs_3_
  67.4 0.1 collective-permute-start.25
  67.5 1.1 %shard_map.108 = (f32[1024,128]{1,0:T(8,128)}, f32[4,64,256]{2,1,0:T(8,128)}, bf16[256,768]{1,0:T(8,128)(2,1)}) custom-call(bf16[192,256]{1,0:T(8,128)(2,1)S(1)} %get-tuple-element.119.refs_0_, bf16[192,256]{1,0:T(8,128)(2,1)S(1)} %collective-permute-done.19.refs_1_, bf16[192,256]{1,0:T(8,128)(2,1)S(1)} %collective-permute-done.20.refs_2_, ...), custom_call_target="tpu_custom_call" | custom-call | flops 5750000128 | tf_op jit(solution)/shard_map/pallas_call | solution.py:407
  68.6 0.0 collective-permute-done.24.refs_1_
  68.6 0.2 collective-permute-done.25.refs_3_
  68.8 0.9 %shard_map.109 = f32[4,64,768]{2,1,0:T(8,128)} custom-call(bf16[64,768]{1,0:T(8,128)(2,1)S(1)} %shard_map.105.refs_0_, bf16[64,768]{1,0:T(8,128)(2,1)S(1)} %collective-permute-done.24.refs_1_, bf16[64,768]{1,0:T(8,128)(2,1)S(1)} %shard_map.107.refs_6_.refs_2_, bf16[64,768]{1,0:T(8,128)(2,1)S(1)} %collective-permute-done.25.refs_3_), custom_call_target="tpu_custom_call" | custom-call | flops 575000000 | tf_op jit(solution)/shard_map/pallas_call | solution.py:401
  (24 shorter events, 0.2 us)
Async XLA Ops:
  0.6 8.5 %copy-start.1 = (bf16[4,64,768]{2,1,0:T(8,128)(2,1)S(1)}, bf16[4,64,768]{2,1,0:T(8,128)(2,1)}, u32[]{:S(2)}) copy-start(bf16[4,64,768]{2,1,0:T(8,128)(2,1)} %w_ref.3) | copy-start | bytes 1179652
  0.6 8.4 %copy-start.2 = (bf16[256,768]{1,0:T(8,128)(2,1)S(1)}, bf16[256,768]{1,0:T(8,128)(2,1)}, u32[]{:S(2)}) copy-start(bf16[256,768]{1,0:T(8,128)(2,1)} %go_ref.3) | copy-start | bytes 1179652
  0.7 8.4 %copy-start.3 = (bf16[256,4,64]{0,2,1:T(8,128)(2,1)S(1)}, bf16[256,4,64]{0,2,1:T(8,128)(2,1)}, u32[]{:S(2)}) copy-start(bf16[256,4,64]{0,2,1:T(8,128)(2,1)} %param.5) | copy-start | bytes 393220
  0.7 8.4 %copy-start.4 = (s32[2]{0:T(128)S(1)}, s32[2]{0:T(128)}, u32[]{:S(2)}) copy-start(s32[2]{0:T(128)} %fill_ref.5) | copy-start | bytes 28
  3.3 10.5 %collective-permute-start = (bf16[256,128]{1,0:T(8,128)(2,1)}, bf16[256,128]{1,0:T(8,128)(2,1)S(1)}, u32[]{:S(2)}, u32[]{:S(2)}) collective-permute-start(bf16[256,128]{1,0:T(8,128)(2,1)} %get-tuple-element.66), channel_id=1, source_target_pairs={{0,24},{2,26},{4,28},{6,30},{8,16},{10,18},{12,20},{14,22},{16,8},... | collective-permute-start | bytes 196616 | tf_op jit(solution)/shard_map/ppermute | solution.py:288
  8.4 8.4 %collective-permute-start.1 = (bf16[256,128]{1,0:T(8,128)(2,1)}, bf16[256,128]{1,0:T(8,128)(2,1)S(1)}, u32[]{:S(2)}, u32[]{:S(2)}) collective-permute-start(bf16[256,128]{1,0:T(8,128)(2,1)} %get-tuple-element.67), channel_id=1, source_target_pairs={{0,16},{2,18},{4,20},{6,22},{8,24},{10,26},{12,28},{14,30},{16,0},... | collective-permute-start | bytes 196616 | tf_op jit(solution)/shard_map/ppermute | solution.py:288
  8.4 8.4 %collective-permute-start.2 = (bf16[256,128]{1,0:T(8,128)(2,1)}, bf16[256,128]{1,0:T(8,128)(2,1)S(1)}, u32[]{:S(2)}, u32[]{:S(2)}) collective-permute-start(bf16[256,128]{1,0:T(8,128)(2,1)} %get-tuple-element.68), channel_id=1, source_target_pairs={{0,8},{2,10},{4,12},{6,14},{8,0},{10,2},{12,4},{14,6},{16,24},{18,... | collective-permute-start | bytes 196616 | tf_op jit(solution)/shard_map/ppermute | solution.py:288
  9.1 7.7 %copy-start = (bf16[256,128]{1,0:T(8,128)(2,1)S(1)}, bf16[256,128]{1,0:T(8,128)(2,1)}, u32[]{:S(2)}) copy-start(bf16[256,128]{1,0:T(8,128)(2,1)} %get-tuple-element.65.refs_0_) | copy-start | bytes 196612
  10.0 7.3 %collective-permute-start.3 = (bf16[128,256]{1,0:T(8,128)(2,1)S(1)}, bf16[128,256]{1,0:T(8,128)(2,1)S(1)}, u32[]{:S(2)}, u32[]{:S(2)}) collective-permute-start(bf16[128,256]{1,0:T(8,128)(2,1)S(1)} %get-tuple-element.70), channel_id=1, source_target_pairs={{0,24},{2,26},{4,28},{6,30},{8,16},{10,18},{12,20},{14,22},{16,8},... | collective-permute-start | bytes 196616 | tf_op jit(solution)/shard_map/ppermute | solution.py:288
  13.8 6.1 %collective-permute-start.4 = (bf16[128,256]{1,0:T(8,128)(2,1)S(1)}, bf16[128,256]{1,0:T(8,128)(2,1)S(1)}, u32[]{:S(2)}, u32[]{:S(2)}) collective-permute-start(bf16[128,256]{1,0:T(8,128)(2,1)S(1)} %get-tuple-element.71), channel_id=1, source_target_pairs={{0,16},{2,18},{4,20},{6,22},{8,24},{10,26},{12,28},{14,30},{16,0},... | collective-permute-start | bytes 196616 | tf_op jit(solution)/shard_map/ppermute | solution.py:288
  13.8 6.1 %collective-permute-start.5 = (bf16[128,256]{1,0:T(8,128)(2,1)S(1)}, bf16[128,256]{1,0:T(8,128)(2,1)S(1)}, u32[]{:S(2)}, u32[]{:S(2)}) collective-permute-start(bf16[128,256]{1,0:T(8,128)(2,1)S(1)} %get-tuple-element.72), channel_id=1, source_target_pairs={{0,8},{2,10},{4,12},{6,14},{8,0},{10,2},{12,4},{14,6},{16,24},{18,... | collective-permute-start | bytes 196616 | tf_op jit(solution)/shard_map/ppermute | solution.py:288
  16.8 9.0 %collective-permute-start.7 = (bf16[1024,128]{1,0:T(8,128)(2,1)S(1)}, bf16[1024,128]{1,0:T(8,128)(2,1)S(1)}, u32[]{:S(2)}, u32[]{:S(2)}) collective-permute-start(bf16[1024,128]{1,0:T(8,128)(2,1)S(1)} %shard_map.86.pair_ref), channel_id=1, source_target_pairs={{0,4},{2,6},{4,0},{6,2},{8,12},{10,14},{12,8},{14,10},{16,20},{18,... | collective-permute-start | bytes 786440 | tf_op jit(solution)/shard_map/ppermute | solution.py:288
  17.2 5.7 %collective-permute-start.6 = (bf16[1024,128]{1,0:T(8,128)(2,1)S(1)}, bf16[1024,128]{1,0:T(8,128)(2,1)S(1)}, u32[]{:S(2)}, u32[]{:S(2)}) collective-permute-start(bf16[1024,128]{1,0:T(8,128)(2,1)S(1)} %shard_map.86.pair_ref), channel_id=1, source_target_pairs={{0,2},{2,0},{4,6},{6,4},{8,10},{10,8},{12,14},{14,12},{16,18},{18,... | collective-permute-start | bytes 786440 | tf_op jit(solution)/shard_map/ppermute | solution.py:288
  25.9 3.0 %collective-permute-start.8 = (bf16[1024,128]{1,0:T(8,128)(2,1)S(1)}, bf16[1024,128]{1,0:T(8,128)(2,1)S(1)}, u32[]{:S(2)}, u32[]{:S(2)}) collective-permute-start(bf16[1024,128]{1,0:T(8,128)(2,1)S(1)} %shard_map.90.pair_ref), channel_id=1, source_target_pairs={{0,2},{2,0},{4,6},{6,4},{8,10},{10,8},{12,14},{14,12},{16,18},{18,... | collective-permute-start | bytes 786440 | tf_op jit(solution)/shard_map/ppermute | solution.py:288
  32.2 6.6 %collective-permute-start.9 = (bf16[64,256]{1,0:T(8,128)(2,1)S(1)}, bf16[64,256]{1,0:T(8,128)(2,1)S(1)}, u32[]{:S(2)}, u32[]{:S(2)}) collective-permute-start(bf16[64,256]{1,0:T(8,128)(2,1)S(1)} %get-tuple-element.104), channel_id=1, source_target_pairs={{0,24},{2,26},{4,28},{6,30},{8,16},{10,18},{12,20},{14,22},{16,8},... | collective-permute-start | bytes 98312 | tf_op jit(solution)/shard_map/ppermute | solution.py:288
  35.0 4.8 %collective-permute-start.10 = (bf16[64,256]{1,0:T(8,128)(2,1)S(1)}, bf16[64,256]{1,0:T(8,128)(2,1)S(1)}, u32[]{:S(2)}, u32[]{:S(2)}) collective-permute-start(bf16[64,256]{1,0:T(8,128)(2,1)S(1)} %get-tuple-element.105), channel_id=1, source_target_pairs={{0,16},{2,18},{4,20},{6,22},{8,24},{10,26},{12,28},{14,30},{16,0},... | collective-permute-start | bytes 98312 | tf_op jit(solution)/shard_map/ppermute | solution.py:288
  35.0 4.8 %collective-permute-start.11 = (bf16[64,256]{1,0:T(8,128)(2,1)S(1)}, bf16[64,256]{1,0:T(8,128)(2,1)S(1)}, u32[]{:S(2)}, u32[]{:S(2)}) collective-permute-start(bf16[64,256]{1,0:T(8,128)(2,1)S(1)} %get-tuple-element.106), channel_id=1, source_target_pairs={{0,8},{2,10},{4,12},{6,14},{8,0},{10,2},{12,4},{14,6},{16,24},{18,... | collective-permute-start | bytes 98312 | tf_op jit(solution)/shard_map/ppermute | solution.py:288
  40.8 2.1 %collective-permute-start.12 = (bf16[2,64,768]{2,1,0:T(8,128)(2,1)S(1)}, bf16[2,64,768]{2,1,0:T(8,128)(2,1)S(1)}, u32[]{:S(2)}, u32[]{:S(2)}) collective-permute-start(bf16[2,64,768]{2,1,0:T(8,128)(2,1)S(1)} %get-tuple-element.109), channel_id=1, source_target_pairs={{0,2},{2,0},{4,6},{6,4},{8,10},{10,8},{12,14},{14,12},{16,18},{18,... | collective-permute-start | bytes 589832 | tf_op jit(solution)/shard_map/ppermute | solution.py:288
  40.8 5.8 %collective-permute-start.15 = (bf16[128,1024]{1,0:T(8,128)(2,1)S(1)}, bf16[128,1024]{1,0:T(8,128)(2,1)S(1)}, u32[]{:S(2)}, u32[]{:S(2)}) collective-permute-start(bf16[128,1024]{1,0:T(8,128)(2,1)S(1)} %get-tuple-element.107.refs_4_), channel_id=1, source_target_pairs={{0,2},{2,0},{4,6},{6,4},{8,10},{10,8},{12,14},{14,12},{16,18},{18,... | collective-permute-start | bytes 786440 | tf_op jit(solution)/shard_map/ppermute | solution.py:288
  41.3 13.1 %collective-permute-start.17 = (bf16[256,768]{1,0:T(8,128)(2,1)S(1)}, bf16[256,768]{1,0:T(8,128)(2,1)S(1)}, u32[]{:S(2)}, u32[]{:S(2)}) collective-permute-start(bf16[256,768]{1,0:T(8,128)(2,1)S(1)} %get-tuple-element.116.refs_4_), channel_id=1, source_target_pairs={{0,1},{1,0},{2,3},{3,2},{4,5},{5,4},{6,7},{7,6},{8,9},{9,8},{10,11... | collective-permute-start | bytes 1179656 | tf_op jit(solution)/shard_map/ppermute | solution.py:288
  42.9 4.7 %collective-permute-start.13 = (bf16[64,768]{1,0:T(8,128)(2,1)S(1)}, bf16[64,768]{1,0:T(8,128)(2,1)S(1)}, u32[]{:S(2)}, u32[]{:S(2)}) collective-permute-start(bf16[64,768]{1,0:T(8,128)(2,1)S(1)} %get-tuple-element.112), channel_id=1, source_target_pairs={{0,4},{2,6},{4,0},{6,2},{8,12},{10,14},{12,8},{14,10},{16,20},{18,... | collective-permute-start | bytes 294920 | tf_op jit(solution)/shard_map/ppermute | solution.py:288
  46.7 7.8 %collective-permute-start.16 = (bf16[128,1024]{1,0:T(8,128)(2,1)S(1)}, bf16[128,1024]{1,0:T(8,128)(2,1)S(1)}, u32[]{:S(2)}, u32[]{:S(2)}) collective-permute-start(bf16[128,1024]{1,0:T(8,128)(2,1)S(1)} %shard_map.101), channel_id=1, source_target_pairs={{0,4},{2,6},{4,0},{6,2},{8,12},{10,14},{12,8},{14,10},{16,20},{18,... | collective-permute-start | bytes 786440 | tf_op jit(solution)/shard_map/ppermute | solution.py:288
  47.6 4.7 %collective-permute-start.14 = (bf16[64,768]{1,0:T(8,128)(2,1)S(1)}, bf16[64,768]{1,0:T(8,128)(2,1)S(1)}, u32[]{:S(2)}, u32[]{:S(2)}) collective-permute-start(bf16[64,768]{1,0:T(8,128)(2,1)S(1)} %shard_map.98.refs_1_.a_ref), channel_id=1, source_target_pairs={{0,8},{2,10},{4,12},{6,14},{8,0},{10,2},{12,4},{14,6},{16,24},{18,... | collective-permute-start | bytes 294920 | tf_op jit(solution)/shard_map/ppermute | solution.py:288
  50.6 6.1 %collective-permute-start.18 = (bf16[128,1024]{1,0:T(8,128)(2,1)S(1)}, bf16[128,1024]{1,0:T(8,128)(2,1)S(1)}, u32[]{:S(2)}, u32[]{:S(2)}) collective-permute-start(bf16[128,1024]{1,0:T(8,128)(2,1)S(1)} %get-tuple-element.115.refs_0_), channel_id=1, source_target_pairs={{0,2},{2,0},{4,6},{6,4},{8,10},{10,8},{12,14},{14,12},{16,18},{18,... | collective-permute-start | bytes 786440 | tf_op jit(solution)/shard_map/ppermute | solution.py:288
  52.3 9.0 %collective-permute-start.22 = (bf16[64,768]{1,0:T(8,128)(2,1)S(1)}, bf16[64,768]{1,0:T(8,128)(2,1)S(1)}, u32[]{:S(2)}, u32[]{:S(2)}) collective-permute-start(bf16[64,768]{1,0:T(8,128)(2,1)S(1)} %shard_map.100.refs_1_.a_ref), channel_id=1, source_target_pairs={{0,16},{2,18},{4,20},{6,22},{8,24},{10,26},{12,28},{14,30},{16,0},... | collective-permute-start | bytes 294920 | tf_op jit(solution)/shard_map/ppermute | solution.py:288
  56.9 7.3 %collective-permute-start.19 = (bf16[192,256]{1,0:T(8,128)(2,1)S(1)}, bf16[192,256]{1,0:T(8,128)(2,1)S(1)}, u32[]{:S(2)}, u32[]{:S(2)}) collective-permute-start(bf16[192,256]{1,0:T(8,128)(2,1)S(1)} %get-tuple-element.120), channel_id=1, source_target_pairs={{0,24},{2,26},{4,28},{6,30},{8,16},{10,18},{12,20},{14,22},{16,8},... | collective-permute-start | bytes 294920 | tf_op jit(solution)/shard_map/ppermute | solution.py:288
  59.0 8.4 %collective-permute-start.20 = (bf16[192,256]{1,0:T(8,128)(2,1)S(1)}, bf16[192,256]{1,0:T(8,128)(2,1)S(1)}, u32[]{:S(2)}, u32[]{:S(2)}) collective-permute-start(bf16[192,256]{1,0:T(8,128)(2,1)S(1)} %get-tuple-element.121), channel_id=1, source_target_pairs={{0,16},{2,18},{4,20},{6,22},{8,24},{10,26},{12,28},{14,30},{16,0},... | collective-permute-start | bytes 294920 | tf_op jit(solution)/shard_map/ppermute | solution.py:288
  59.2 8.2 %collective-permute-start.21 = (bf16[192,256]{1,0:T(8,128)(2,1)S(1)}, bf16[192,256]{1,0:T(8,128)(2,1)S(1)}, u32[]{:S(2)}, u32[]{:S(2)}) collective-permute-start(bf16[192,256]{1,0:T(8,128)(2,1)S(1)} %get-tuple-element.122), channel_id=1, source_target_pairs={{0,8},{2,10},{4,12},{6,14},{8,0},{10,2},{12,4},{14,6},{16,24},{18,... | collective-permute-start | bytes 294920 | tf_op jit(solution)/shard_map/ppermute | solution.py:288
  61.3 6.1 %collective-permute-start.23 = (bf16[64,768]{1,0:T(8,128)(2,1)S(1)}, bf16[64,768]{1,0:T(8,128)(2,1)S(1)}, u32[]{:S(2)}, u32[]{:S(2)}) collective-permute-start(bf16[64,768]{1,0:T(8,128)(2,1)S(1)} %shard_map.105.refs_0_), channel_id=1, source_target_pairs={{0,4},{2,6},{4,0},{6,2},{8,12},{10,14},{12,8},{14,10},{16,20},{18,... | collective-permute-start | bytes 294920 | tf_op jit(solution)/shard_map/ppermute | solution.py:288
  62.8 5.8 %collective-permute-start.24 = (bf16[64,768]{1,0:T(8,128)(2,1)S(1)}, bf16[64,768]{1,0:T(8,128)(2,1)S(1)}, u32[]{:S(2)}, u32[]{:S(2)}) collective-permute-start(bf16[64,768]{1,0:T(8,128)(2,1)S(1)} %shard_map.105.refs_0_), channel_id=1, source_target_pairs={{0,2},{2,0},{4,6},{6,4},{8,10},{10,8},{12,14},{14,12},{16,18},{18,... | collective-permute-start | bytes 294920 | tf_op jit(solution)/shard_map/ppermute | solution.py:288
  67.4 1.4 %collective-permute-start.25 = (bf16[64,768]{1,0:T(8,128)(2,1)S(1)}, bf16[64,768]{1,0:T(8,128)(2,1)S(1)}, u32[]{:S(2)}, u32[]{:S(2)}) collective-permute-start(bf16[64,768]{1,0:T(8,128)(2,1)S(1)} %shard_map.107.refs_6_.refs_2_), channel_id=1, source_target_pairs={{0,2},{2,0},{4,6},{6,4},{8,10},{10,8},{12,14},{14,12},{16,18},{18,... | collective-permute-start | bytes 294920 | tf_op jit(solution)/shard_map/ppermute | solution.py:288

commit v18 on v15

--- a/solution.py
+++ b/solution.py
@@ -55,7 +55,7 @@
 
 
 def spread(slots):
-    return [0] + sorted(range(1, slots), key=lambda mask: (mask < slots // 2, mask))
+    return [0] + list(range(slots - 1, 0, -1))
 
 
 def pack_kv_kernel(heads, rows, dim, a_of, fill_ref, kv_ref, *refs):
@@ -176,8 +176,9 @@
     inner_ref[...] = jnp.sum(g_ref[...].astype(F32) * attended.astype(F32), axis=0, keepdims=True)
 
 
-def back_kernel(slots, rows, dim, first, exp_ref, v_ref, kt_ref, q_ref, g_ref, factor_ref, inner_ref, *refs):
+def back_kernel(slots, rows, dim, first, low, high_key, exp_ref, v_ref, kt_ref, q_ref, g_ref, factor_ref, inner_ref, *refs):
     dkv_ref, dq_ref, ga_ref = refs[-3:]
+    part = slice(low, high_key)
     block = g_ref.shape[1]
     factor = factor_ref[...]
     inner = inner_ref[...] * factor
@@ -186,19 +187,19 @@
     ga_ref[0:dim, :] = (g_ref[...].astype(F32) * factor).astype(BF16)
     ga_ref[dim:, :] = jnp.where(row == 1, -high, jnp.where(row == 2, high - inner, 0.0)).astype(BF16)
     grad_k = grad_v = None
-    ahead = dot(v_ref[...], ga_ref[:, 0:rows])
+    ahead = dot(v_ref[part, :], ga_ref[:, 0:rows])
     for slot in range(slots):
         here = slice(slot * rows, (slot + 1) * rows)
         products = ahead
         if slot + 1 < slots:
-            ahead = dot(v_ref[...], ga_ref[:, (slot + 1) * rows : (slot + 2) * rows])
-        exps = exp_ref[:, here]
+            ahead = dot(v_ref[part, :], ga_ref[:, (slot + 1) * rows : (slot + 2) * rows])
+        exps = exp_ref[part, here]
         grads = exps * products.astype(BF16)
         term_v = dot_nt(ga_ref[0:dim, here], exps)
         term_k = dot_nt(q_ref[:, here], grads)
         grad_v = term_v if grad_v is None else grad_v + term_v
         grad_k = term_k if grad_k is None else grad_k + term_k
-        term = dot(kt_ref[...], grads)
+        term = dot(kt_ref[:, part], grads)
         dq_ref[:, here] = term if first else refs[0][:, here] + term
     dkv_ref[dim:, :] = grad_v.astype(BF16)
     dkv_ref[0:dim, :] = grad_k.astype(BF16)
@@ -236,6 +237,14 @@
         here = slice(slot * rows, (slot + 1) * rows)
         outs[slot][0:wide, :] = (kept_ref[:, here].astype(F32) + came_ref[:, here].astype(F32)).astype(BF16)
         outs[slot][wide:, :] = (dq_ref[:, here] * dim**-0.5).astype(BF16)
+
+
+def add_parts_kernel(parts, *refs):
+    start = 0
+    for part in refs[:parts]:
+        here = slice(start, start + part.shape[1])
+        refs[-1][:, here] = (part[...].astype(F32) + refs[parts][:, here].astype(F32)).astype(BF16)
+        start += part.shape[1]
 
 
 def add_kernel(a_ref, b_ref, *refs):
@@ -325,6 +334,7 @@
     halves = columns == heads == 4
     order = sorted(range(columns), reverse=True)
     add = call(add_kernel, [((dim, width), BF16)], n_in=2, after=1)
+    add_kernel_of = lambda parts: functools.partial(add_parts_kernel, parts)
     add_halves = call(add_kernel, [((wide, block), BF16)], n_in=2)
     z_masks = [columns << level for level in range(slots.bit_length() - 1)]
     dkv, dq, kept, summed, later = {}, None, None, {}, []
@@ -348,13 +358,21 @@
         if at == 2 and halves:
             kept = add(kept, swap(sent, 2), dkv[order[at - 1]])[0]
             later = [kept]
+        low = 0
         if at == 3 and halves:
-            kept = add(kept, swap(kept, z_masks[0]), dkv[order[at - 1]])[0]
+            low = block // 2
+            operands = [scored[r][0], *scored[r][3:], q_all, grads, factors[r], inner, dq]
+            lower, dq = call(
+                functools.partial(back_kernel, slots, rows, dim, False, 0, low),
+                [((wide, low), BF16), ((dim, block), F32)], [pltpu.VMEM((wide, block), BF16)],
+                n_in=len(operands), micros=2,
+            )(*operands)
+            kept = add(kept, swap(kept, z_masks[0]), lower)[0]
             later = [kept, summed[2], terms_came]
         operands = [scored[r][0], *scored[r][3:], q_all, grads, factors[r], inner] + ([] if dq is None else [dq])
         dkv[r], dq = call(
-            functools.partial(back_kernel, slots, rows, dim, dq is None),
-            [((wide, block), BF16), ((dim, block), F32)], [pltpu.VMEM((wide, block), BF16)],
+            functools.partial(back_kernel, slots, rows, dim, dq is None, low, block),
+            [((wide, block - low), BF16), ((dim, block), F32)], [pltpu.VMEM((wide, block), BF16)],
             n_in=len(operands), after=len(later), micros=2,
         )(*operands, *later)
         later = []
@@ -362,7 +380,9 @@
             summed[2] = swap(add_halves(dkv[2], swap(dkv[3], 1))[0], 2)
 
     if columns == 4:
-        halved = add_halves(dkv[0], swap(dkv[1], 1))[0], summed[2]
+        lowers = [lower] if halves else []
+        halved = call(add_kernel_of(len(lowers) + 1), [((wide, block), BF16)], n_in=len(lowers) + 2)(
+            *lowers, dkv[0], swap(dkv[1], 1))[0], summed[2]
     else:
         bit = 1
         while 2 * bit < columns:

time: 68.4 us -> 71 us (1.038)
  starting transfers between devices: 25.1 us -> 28.6 us
  waiting for transfers between devices: 15.3 us -> 14.3 us
    ppermute x26, starting transfers between devices: 25.1 us -> 28.6 us  [swap(): return lax.ppermute(array, axis, [(i, i ^ mask) for i in range(size)])]
    ppermute x26, waiting for transfers between devices: 15.3 us -> 14.3 us  [swap(): return lax.ppermute(array, axis, [(i, i ^ mask) for i in range(size)])]
    pallas_call x6 -> x7, Pallas kernels: 8.77 us -> 8.86 us  [the longest x4 7.62 us: shards(): call(functools.partial(back_kernel, slots, rows, dim, dq is None, low, bl...]
  transfers between devices with their start and end apart: 26 -> 26, of which waited for: 10 -> 10; matrix products, arithmetic and copies ran while one was open for 0% -> 0% of each run, Pallas kernels for 29% -> 28%
where the time goes in v18:
time: 71 us; the launch traced here: 70.8 us
  starting transfers between devices  28.6 us (40%)
  Pallas kernels  27 us (38%)
  waiting for transfers between devices  14.3 us (20%)
  between operations  0.92 us (1%)
    ppermute x26, starting transfers between devices, swap(): return lax.ppermute(array, axis, [(i, i ^ mask) for i in range(size)])  28.6 us
    ppermute x26, waiting for transfers between devices, swap(): return lax.ppermute(array, axis, [(i, i ^ mask) for i in range(size)])  14.3 us
    pallas_call x4, Pallas kernels, shards(): call(functools.partial(score_kernel, slots, rows, dim, step), [((block, b...  11.9 us
    pallas_call x4, Pallas kernels, shards(): call(functools.partial(back_kernel, slots, rows, dim, dq is None, low, bl...  7.62 us
    pallas_call x1, Pallas kernels, shards(): call(functools.partial(pack_kv_kernel, heads, rows, dim, a_of), [((rows,...  1.9 us
  transfers between devices with their start and end apart: 26, of which 10 were waited for; matrix products, arithmetic and copies ran while one was open for 0% of the time, Pallas kernels for 28%

profile of v18, /device:TPU:0, one launch (start us, length us, event | category | flops | bytes accessed | tf_op | source)
XLA Modules:
  0.0 70.8 jit_solution(17163681869883708158)
XLA Ops:
  0.7 1.9 %shard_map.84 = (bf16[256,128]{1,0:T(8,128)(2,1)}, bf16[256,128]{1,0:T(8,128)(2,1)}, bf16[256,128]{1,0:T(8,128)(2,1)}, bf16[256,128]{1,0:T(8,128)(2,1)}) custom-call(s32[2]{0:T(128)} %fill_ref.5, bf16[1024,128]{1,0:T(8,128)(2,1)} %bitcast.5), custom_call_target="tpu_custom_call" | custom-call | flops 1724999936 | tf_op jit(solution)/shard_map/pallas_call | solution.py:291
  2.6 5.0 %collective-permute-start = (bf16[256,128]{1,0:T(8,128)(2,1)}, bf16[256,128]{1,0:T(8,128)(2,1)S(1)}, u32[]{:S(2)}, u32[]{:S(2)}) collective-permute-start(bf16[256,128]{1,0:T(8,128)(2,1)} %get-tuple-element.68), channel_id=1, source_target_pairs={{0,24},{2,26},{4,28},{6,30},{8,16},{10,18},{12,20},{14,22},{16,8},... | collective-permute-start | bytes 196616 | tf_op jit(solution)/shard_map/ppermute | solution.py:285
  7.6 0.0 collective-permute-start.1
  7.6 0.6 collective-permute-start.2
  8.2 0.0 copy-start
  8.2 0.9 %shard_map.85 = (bf16[128,256]{1,0:T(8,128)(2,1)S(1)}, bf16[128,256]{1,0:T(8,128)(2,1)S(1)}, bf16[128,256]{1,0:T(8,128)(2,1)S(1)}, bf16[128,256]{1,0:T(8,128)(2,1)S(1)}) custom-call(s32[2]{0:T(128)S(1)} %copy-done.4, bf16[4,64,256]{2,1,0:T(8,128)(2,1)S(1)} %bitcast.4, bf16[4,64,768]{2,1,0:T(8,128)(2,1)S(1)} %copy-done.1, bf16[256,768]{1,0:T(8,128)(2,1)S(1)} %copy-done.2), custom_call_target="tpu_custom_call" | custom-call | flops 1150000000 | tf_op jit(solution)/shard_map/pallas_call | solution.py:296
  9.1 3.9 %collective-permute-start.3 = (bf16[128,256]{1,0:T(8,128)(2,1)S(1)}, bf16[128,256]{1,0:T(8,128)(2,1)S(1)}, u32[]{:S(2)}, u32[]{:S(2)}) collective-permute-start(bf16[128,256]{1,0:T(8,128)(2,1)S(1)} %get-tuple-element.72), channel_id=1, source_target_pairs={{0,24},{2,26},{4,28},{6,30},{8,16},{10,18},{12,20},{14,22},{16,8},... | collective-permute-start | bytes 196616 | tf_op jit(solution)/shard_map/ppermute | solution.py:285
  13.0 0.0 collective-permute-start.4
  13.0 0.0 collective-permute-done.refs_1_
  13.0 0.6 collective-permute-start.5
  13.6 2.4 %collective-permute-done.1.refs_2_ = bf16[256,128]{1,0:T(8,128)(2,1)S(1)} collective-permute-done((bf16[256,128]{1,0:T(8,128)(2,1)}, bf16[256,128]{1,0:T(8,128)(2,1)S(1)}, u32[]{:S(2)}, u32[]{:S(2)}) %collective-permute-start.1) | collective-permute-done | bytes 65568 | tf_op jit(solution)/shard_map/ppermute | solution.py:285
  16.0 0.4 collective-permute-start.7
  16.4 0.0 collective-permute-start.6
  16.4 0.0 collective-permute-done.3.refs_1_
  16.4 2.6 %collective-permute-done.4.refs_2_ = bf16[128,256]{1,0:T(8,128)(2,1)S(1)} collective-permute-done((bf16[128,256]{1,0:T(8,128)(2,1)S(1)}, bf16[128,256]{1,0:T(8,128)(2,1)S(1)}, u32[]{:S(2)}, u32[]{:S(2)}) %collective-permute-start.4) | collective-permute-done | bytes 65568 | tf_op jit(solution)/shard_map/ppermute | solution.py:285
  19.1 0.0 collective-permute-done.5.refs_3_
  19.1 0.1 shard_map.87
  19.2 2.9 %shard_map.88 = (bf16[1024,1024]{1,0:T(8,128)(2,1)S(1)}, f32[1,1024]{1,0:T(1,128)S(1)}, f32[80,1024]{1,0:T(8,128)S(1)}, bf16[1024,128]{1,0:T(8,128)(2,1)S(1)}, bf16[64,1024]{1,0:T(8,128)(2,1)S(1)}) custom-call(bf16[1024,128]{1,0:T(8,128)(2,1)S(1)} %shard_map.86.pair_ref, bf16[256,1024]{1,0:T(8,128)(2,1)S(1)} %get-tuple-element.75.qa_ref, ...), custom_call_target="tpu_custom_call" | custom-call | flops 5750000128 | tf_op jit(solution)/shard_map/pallas_call | solution.py:322
  22.1 2.9 %shard_map.89 = (bf16[1024,1024]{1,0:T(8,128)(2,1)S(1)}, f32[1,1024]{1,0:T(1,128)S(1)}, f32[80,1024]{1,0:T(8,128)S(1)}, bf16[1024,128]{1,0:T(8,128)(2,1)S(1)}, bf16[64,1024]{1,0:T(8,128)(2,1)S(1)}) custom-call(bf16[1024,128]{1,0:T(8,128)(2,1)S(1)} %collective-permute-done.6.pair_ref, bf16[256,1024]{1,0:T(8,128)(2,1)S(1)} %get-tuple-element.75.qa_ref, ...), custom_call_target="tpu_custom_call" | custom-call | flops 5750000128 | tf_op jit(solution)/shard_map/pallas_call | solution.py:322
  25.0 0.0 collective-permute-done.7.refs_0_
  25.1 0.1 collective-permute-start.8
  25.2 2.9 %shard_map.91 = (bf16[1024,1024]{1,0:T(8,128)(2,1)S(1)}, f32[1,1024]{1,0:T(1,128)S(1)}, f32[80,1024]{1,0:T(8,128)S(1)}, bf16[1024,128]{1,0:T(8,128)(2,1)S(1)}, bf16[64,1024]{1,0:T(8,128)(2,1)S(1)}) custom-call(bf16[1024,128]{1,0:T(8,128)(2,1)S(1)} %shard_map.90.pair_ref, bf16[256,1024]{1,0:T(8,128)(2,1)S(1)} %get-tuple-element.75.qa_ref, ...), custom_call_target="tpu_custom_call" | custom-call | flops 5750000128 | tf_op jit(solution)/shard_map/pallas_call | solution.py:322
  28.1 3.1 %shard_map.92 = (bf16[1024,1024]{1,0:T(8,128)(2,1)S(1)}, f32[1,1024]{1,0:T(1,128)S(1)}, f32[80,1024]{1,0:T(8,128)S(1)}, bf16[1024,128]{1,0:T(8,128)(2,1)S(1)}, bf16[64,1024]{1,0:T(8,128)(2,1)S(1)}) custom-call(bf16[1024,128]{1,0:T(8,128)(2,1)S(1)} %collective-permute-done.8.pair_ref, bf16[256,1024]{1,0:T(8,128)(2,1)S(1)} %get-tuple-element.75.qa_ref, ...), custom_call_target="tpu_custom_call" | custom-call | flops 5750000128 | tf_op jit(solution)/shard_map/pallas_call | solution.py:322
  31.2 0.2 shard_map.93
  31.4 2.7 %collective-permute-start.9 = (bf16[64,256]{1,0:T(8,128)(2,1)S(1)}, bf16[64,256]{1,0:T(8,128)(2,1)S(1)}, u32[]{:S(2)}, u32[]{:S(2)}) collective-permute-start(bf16[64,256]{1,0:T(8,128)(2,1)S(1)} %get-tuple-element.106), channel_id=1, source_target_pairs={{0,24},{2,26},{4,28},{6,30},{8,16},{10,18},{12,20},{14,22},{16,8},... | collective-permute-start | bytes 98312 | tf_op jit(solution)/shard_map/ppermute | solution.py:285
  34.1 0.0 collective-permute-start.10
  34.1 1.7 %collective-permute-start.11 = (bf16[64,256]{1,0:T(8,128)(2,1)S(1)}, bf16[64,256]{1,0:T(8,128)(2,1)S(1)}, u32[]{:S(2)}, u32[]{:S(2)}) collective-permute-start(bf16[64,256]{1,0:T(8,128)(2,1)S(1)} %get-tuple-element.108), channel_id=1, source_target_pairs={{0,8},{2,10},{4,12},{6,14},{8,0},{10,2},{12,4},{14,6},{16,24},{18,... | collective-permute-start | bytes 98312 | tf_op jit(solution)/shard_map/ppermute | solution.py:285
  35.9 2.2 %shard_map.94 = (bf16[128,1024]{1,0:T(8,128)(2,1)S(1)}, f32[64,1024]{1,0:T(8,128)S(1)}) custom-call(bf16[1024,1024]{1,0:T(8,128)(2,1)S(1)} %get-tuple-element.100.exp_ref, bf16[1024,128]{1,0:T(8,128)(2,1)S(1)} %get-tuple-element.101.v_ref, bf16[64,1024]{1,0:T(8,128)(2,1)S(1)} %get-tuple-element.102.kt_ref, bf16[64,1024]{1,0:T(8,128)(2,1)S(1)} %get-tuple-element.80.q_ref, ...), custom_call_target="tpu_custom_call" | custom-call | flops 2300000000 | tf_op jit(solution)/shard_map/pallas_call | solution.py:373
  38.0 0.9 %collective-permute-done.10.refs_2_ = bf16[64,256]{1,0:T(8,128)(2,1)S(1)} collective-permute-done((bf16[64,256]{1,0:T(8,128)(2,1)S(1)}, bf16[64,256]{1,0:T(8,128)(2,1)S(1)}, u32[]{:S(2)}, u32[]{:S(2)}) %collective-permute-start.10) | collective-permute-done | bytes 32800 | tf_op jit(solution)/shard_map/ppermute | solution.py:285
  38.9 0.9 %shard_map.95 = (bf16[256,768]{1,0:T(8,128)(2,1)S(1)}, bf16[2,64,768]{2,1,0:T(8,128)(2,1)S(1)}, bf16[2,64,768]{2,1,0:T(8,128)(2,1)S(1)}) custom-call(s32[2]{0:T(128)S(1)} %copy-done.4, bf16[256,768]{1,0:T(8,128)(2,1)S(1)} %copy-done.2, bf16[4,64,768]{2,1,0:T(8,128)(2,1)S(1)} %copy-done.1, bf16[64,256]{1,0:T(8,128)(2,1)S(1)} %get-tuple-element.105.refs_0_, ...), custom_call_target="tpu_custom_call" | custom-call | flops 805000000 | tf_op jit(solution)/shard_map/pallas_call | solution.py:343
  39.9 0.1 collective-permute-start.12
  39.9 0.5 collective-permute-start.15
  40.4 1.5 %collective-permute-start.17 = (bf16[256,768]{1,0:T(8,128)(2,1)S(1)}, bf16[256,768]{1,0:T(8,128)(2,1)S(1)}, u32[]{:S(2)}, u32[]{:S(2)}) collective-permute-start(bf16[256,768]{1,0:T(8,128)(2,1)S(1)} %get-tuple-element.119.refs_4_), channel_id=1, source_target_pairs={{0,1},{1,0},{2,3},{3,2},{4,5},{5,4},{6,7},{7,6},{8,9},{9,8},{10,11... | collective-permute-start | bytes 1179656 | tf_op jit(solution)/shard_map/ppermute | solution.py:285
  42.0 1.6 %collective-permute-start.13 = (bf16[64,768]{1,0:T(8,128)(2,1)S(1)}, bf16[64,768]{1,0:T(8,128)(2,1)S(1)}, u32[]{:S(2)}, u32[]{:S(2)}) collective-permute-start(bf16[64,768]{1,0:T(8,128)(2,1)S(1)} %get-tuple-element.114), channel_id=1, source_target_pairs={{0,4},{2,6},{4,0},{6,2},{8,12},{10,14},{12,8},{14,10},{16,20},{18,... | collective-permute-start | bytes 294920 | tf_op jit(solution)/shard_map/ppermute | solution.py:285
  43.6 2.1 %shard_map.97 = (bf16[128,1024]{1,0:T(8,128)(2,1)S(1)}, f32[64,1024]{1,0:T(8,128)S(1)}) custom-call(bf16[1024,1024]{1,0:T(8,128)(2,1)S(1)} %get-tuple-element.96.exp_ref, bf16[1024,128]{1,0:T(8,128)(2,1)S(1)} %get-tuple-element.97.v_ref, bf16[64,1024]{1,0:T(8,128)(2,1)S(1)} %get-tuple-element.98.kt_ref, bf16[64,1024]{1,0:T(8,128)(2,1)S(1)} %get-tuple-element.80.q_ref, ...), custom_call_target="tpu_custom_call" | custom-call | flops 2300000000 | tf_op jit(solution)/shard_map/pallas_call | solution.py:373
  45.7 0.0 collective-permute-done.15.b_ref
  45.7 0.1 shard_map.102
  45.8 0.6 collective-permute-start.16
  46.4 0.3 collective-permute-done.13.b_ref
  46.7 0.9 %collective-permute-start.14 = (bf16[64,768]{1,0:T(8,128)(2,1)S(1)}, bf16[64,768]{1,0:T(8,128)(2,1)S(1)}, u32[]{:S(2)}, u32[]{:S(2)}) collective-permute-start(bf16[64,768]{1,0:T(8,128)(2,1)S(1)} %shard_map.98.refs_1_.a_ref), channel_id=1, source_target_pairs={{0,8},{2,10},{4,12},{6,14},{8,0},{10,2},{12,4},{14,6},{16,24},{18,... | collective-permute-start | bytes 294920 | tf_op jit(solution)/shard_map/ppermute | solution.py:285
  47.6 2.2 %shard_map.99 = (bf16[128,1024]{1,0:T(8,128)(2,1)S(1)}, f32[64,1024]{1,0:T(8,128)S(1)}) custom-call(bf16[1024,1024]{1,0:T(8,128)(2,1)S(1)} %get-tuple-element.92.exp_ref, bf16[1024,128]{1,0:T(8,128)(2,1)S(1)} %get-tuple-element.93.v_ref, bf16[64,1024]{1,0:T(8,128)(2,1)S(1)} %get-tuple-element.94.kt_ref, bf16[64,1024]{1,0:T(8,128)(2,1)S(1)} %get-tuple-element.80.q_ref, ...), custom_call_target="tpu_custom_call" | custom-call | flops 2300000000 | tf_op jit(solution)/shard_map/pallas_call | solution.py:373
  49.8 0.1 collective-permute-start.18
  49.8 1.1 %shard_map.100 = (bf16[128,512]{1,0:T(8,128)(2,1)S(1)}, f32[64,1024]{1,0:T(8,128)S(1)}) custom-call(bf16[1024,1024]{1,0:T(8,128)(2,1)S(1)} %get-tuple-element.77.exp_ref, bf16[1024,128]{1,0:T(8,128)(2,1)S(1)} %get-tuple-element.78.v_ref, bf16[64,1024]{1,0:T(8,128)(2,1)S(1)} %get-tuple-element.79.kt_ref, bf16[64,1024]{1,0:T(8,128)(2,1)S(1)} %get-tuple-element.80.q_ref, ...), custom_call_target="tpu_custom_call" | custom-call | flops 2300000000 | tf_op jit(solution)/shard_map/pallas_call | solution.py:365
  51.0 0.4 collective-permute-done.14.b_ref
  51.4 2.1 %collective-permute-start.22 = (bf16[64,768]{1,0:T(8,128)(2,1)S(1)}, bf16[64,768]{1,0:T(8,128)(2,1)S(1)}, u32[]{:S(2)}, u32[]{:S(2)}) collective-permute-start(bf16[64,768]{1,0:T(8,128)(2,1)S(1)} %shard_map.101.refs_1_.a_ref), channel_id=1, source_target_pairs={{0,16},{2,18},{4,20},{6,22},{8,24},{10,26},{12,28},{14,30},{16,0},... | collective-permute-start | bytes 294920 | tf_op jit(solution)/shard_map/ppermute | solution.py:285
  53.5 0.1 collective-permute-done.16.refs_2_.came_ref
  53.6 1.2 %shard_map.103 = (bf16[128,512]{1,0:T(8,128)(2,1)S(1)}, f32[64,1024]{1,0:T(8,128)S(1)}) custom-call(bf16[1024,1024]{1,0:T(8,128)(2,1)S(1)} %get-tuple-element.77.exp_ref, bf16[1024,128]{1,0:T(8,128)(2,1)S(1)} %get-tuple-element.78.v_ref, bf16[64,1024]{1,0:T(8,128)(2,1)S(1)} %get-tuple-element.79.kt_ref, bf16[64,1024]{1,0:T(8,128)(2,1)S(1)} %get-tuple-element.80.q_ref, ...), custom_call_target="tpu_custom_call" | custom-call | flops 2300000000 | tf_op jit(solution)/shard_map/pallas_call | solution.py:373
  54.8 0.1 shard_map.104.kept_ref
  54.9 0.1 shard_map.105
  54.9 2.3 %collective-permute-start.19 = (bf16[192,256]{1,0:T(8,128)(2,1)S(1)}, bf16[192,256]{1,0:T(8,128)(2,1)S(1)}, u32[]{:S(2)}, u32[]{:S(2)}) collective-permute-start(bf16[192,256]{1,0:T(8,128)(2,1)S(1)} %get-tuple-element.124), channel_id=1, source_target_pairs={{0,24},{2,26},{4,28},{6,30},{8,16},{10,18},{12,20},{14,22},{16,8},... | collective-permute-start | bytes 294920 | tf_op jit(solution)/shard_map/ppermute | solution.py:285
  57.2 0.1 collective-permute-start.20
  57.3 2.1 %collective-permute-start.21 = (bf16[192,256]{1,0:T(8,128)(2,1)S(1)}, bf16[192,256]{1,0:T(8,128)(2,1)S(1)}, u32[]{:S(2)}, u32[]{:S(2)}) collective-permute-start(bf16[192,256]{1,0:T(8,128)(2,1)S(1)} %get-tuple-element.126), channel_id=1, source_target_pairs={{0,8},{2,10},{4,12},{6,14},{8,0},{10,2},{12,4},{14,6},{16,24},{18,... | collective-permute-start | bytes 294920 | tf_op jit(solution)/shard_map/ppermute | solution.py:285
  59.4 4.4 %collective-permute-done.22.b_ref = bf16[64,768]{1,0:T(8,128)(2,1)S(1)} collective-permute-done((bf16[64,768]{1,0:T(8,128)(2,1)S(1)}, bf16[64,768]{1,0:T(8,128)(2,1)S(1)}, u32[]{:S(2)}, u32[]{:S(2)}) %collective-permute-start.22) | collective-permute-done | bytes 98336 | tf_op jit(solution)/shard_map/ppermute | solution.py:285
  63.8 1.7 %collective-permute-start.23 = (bf16[64,768]{1,0:T(8,128)(2,1)S(1)}, bf16[64,768]{1,0:T(8,128)(2,1)S(1)}, u32[]{:S(2)}, u32[]{:S(2)}) collective-permute-start(bf16[64,768]{1,0:T(8,128)(2,1)S(1)} %shard_map.106.refs_0_), channel_id=1, source_target_pairs={{0,4},{2,6},{4,0},{6,2},{8,12},{10,14},{12,8},{14,10},{16,20},{18,... | collective-permute-start | bytes 294920 | tf_op jit(solution)/shard_map/ppermute | solution.py:285
  65.5 0.0 collective-permute-start.24
  65.6 0.0 collective-permute-done.19.refs_1_
  65.6 2.2 %collective-permute-done.20.refs_2_ = bf16[192,256]{1,0:T(8,128)(2,1)S(1)} collective-permute-done((bf16[192,256]{1,0:T(8,128)(2,1)S(1)}, bf16[192,256]{1,0:T(8,128)(2,1)S(1)}, u32[]{:S(2)}, u32[]{:S(2)}) %collective-permute-start.20) | collective-permute-done | bytes 98336 | tf_op jit(solution)/shard_map/ppermute | solution.py:285
  67.7 0.0 collective-permute-done.21.refs_3_
  67.7 0.8 %collective-permute-done.23.refs_0_ = bf16[64,768]{1,0:T(8,128)(2,1)S(1)} collective-permute-done((bf16[64,768]{1,0:T(8,128)(2,1)S(1)}, bf16[64,768]{1,0:T(8,128)(2,1)S(1)}, u32[]{:S(2)}, u32[]{:S(2)}) %collective-permute-start.23) | collective-permute-done | bytes 98336 | tf_op jit(solution)/shard_map/ppermute | solution.py:285
  68.5 0.1 collective-permute-start.25
  68.6 1.1 %shard_map.109 = (f32[1024,128]{1,0:T(8,128)}, f32[4,64,256]{2,1,0:T(8,128)}, bf16[256,768]{1,0:T(8,128)(2,1)}) custom-call(bf16[192,256]{1,0:T(8,128)(2,1)S(1)} %get-tuple-element.123.refs_0_, bf16[192,256]{1,0:T(8,128)(2,1)S(1)} %collective-permute-done.19.refs_1_, bf16[192,256]{1,0:T(8,128)(2,1)S(1)} %collective-permute-done.20.refs_2_, ...), custom_call_target="tpu_custom_call" | custom-call | flops 5750000128 | tf_op jit(solution)/shard_map/pallas_call | solution.py:408
  69.7 0.0 collective-permute-done.24.refs_1_
  69.7 0.2 collective-permute-done.25.refs_3_
  69.9 0.9 %shard_map.110 = f32[4,64,768]{2,1,0:T(8,128)} custom-call(bf16[64,768]{1,0:T(8,128)(2,1)S(1)} %shard_map.106.refs_0_, bf16[64,768]{1,0:T(8,128)(2,1)S(1)} %collective-permute-done.24.refs_1_, bf16[64,768]{1,0:T(8,128)(2,1)S(1)} %shard_map.108.refs_6_.refs_2_, bf16[64,768]{1,0:T(8,128)(2,1)S(1)} %collective-permute-done.25.refs_3_), custom_call_target="tpu_custom_call" | custom-call | flops 575000000 | tf_op jit(solution)/shard_map/pallas_call | solution.py:402
  (25 shorter events, 0.2 us)
Async XLA Ops:
  0.6 7.6 %copy-start.1 = (bf16[4,64,768]{2,1,0:T(8,128)(2,1)S(1)}, bf16[4,64,768]{2,1,0:T(8,128)(2,1)}, u32[]{:S(2)}) copy-start(bf16[4,64,768]{2,1,0:T(8,128)(2,1)} %w_ref.3) | copy-start | bytes 1179652
  0.6 7.6 %copy-start.2 = (bf16[256,768]{1,0:T(8,128)(2,1)S(1)}, bf16[256,768]{1,0:T(8,128)(2,1)}, u32[]{:S(2)}) copy-start(bf16[256,768]{1,0:T(8,128)(2,1)} %go_ref.3) | copy-start | bytes 1179652
  0.7 7.5 %copy-start.3 = (bf16[256,4,64]{0,2,1:T(8,128)(2,1)S(1)}, bf16[256,4,64]{0,2,1:T(8,128)(2,1)}, u32[]{:S(2)}) copy-start(bf16[256,4,64]{0,2,1:T(8,128)(2,1)} %param.5) | copy-start | bytes 393220
  0.7 7.5 %copy-start.4 = (s32[2]{0:T(128)S(1)}, s32[2]{0:T(128)}, u32[]{:S(2)}) copy-start(s32[2]{0:T(128)} %fill_ref.5) | copy-start | bytes 28
  2.6 10.4 %collective-permute-start = (bf16[256,128]{1,0:T(8,128)(2,1)}, bf16[256,128]{1,0:T(8,128)(2,1)S(1)}, u32[]{:S(2)}, u32[]{:S(2)}) collective-permute-start(bf16[256,128]{1,0:T(8,128)(2,1)} %get-tuple-element.68), channel_id=1, source_target_pairs={{0,24},{2,26},{4,28},{6,30},{8,16},{10,18},{12,20},{14,22},{16,8},... | collective-permute-start | bytes 196616 | tf_op jit(solution)/shard_map/ppermute | solution.py:285
  7.6 8.4 %collective-permute-start.1 = (bf16[256,128]{1,0:T(8,128)(2,1)}, bf16[256,128]{1,0:T(8,128)(2,1)S(1)}, u32[]{:S(2)}, u32[]{:S(2)}) collective-permute-start(bf16[256,128]{1,0:T(8,128)(2,1)} %get-tuple-element.69), channel_id=1, source_target_pairs={{0,16},{2,18},{4,20},{6,22},{8,24},{10,26},{12,28},{14,30},{16,0},... | collective-permute-start | bytes 196616 | tf_op jit(solution)/shard_map/ppermute | solution.py:285
  7.6 8.4 %collective-permute-start.2 = (bf16[256,128]{1,0:T(8,128)(2,1)}, bf16[256,128]{1,0:T(8,128)(2,1)S(1)}, u32[]{:S(2)}, u32[]{:S(2)}) collective-permute-start(bf16[256,128]{1,0:T(8,128)(2,1)} %get-tuple-element.70), channel_id=1, source_target_pairs={{0,8},{2,10},{4,12},{6,14},{8,0},{10,2},{12,4},{14,6},{16,24},{18,... | collective-permute-start | bytes 196616 | tf_op jit(solution)/shard_map/ppermute | solution.py:285
  8.2 7.8 %copy-start = (bf16[256,128]{1,0:T(8,128)(2,1)S(1)}, bf16[256,128]{1,0:T(8,128)(2,1)}, u32[]{:S(2)}) copy-start(bf16[256,128]{1,0:T(8,128)(2,1)} %get-tuple-element.67.refs_0_) | copy-start | bytes 196612
  9.1 7.3 %collective-permute-start.3 = (bf16[128,256]{1,0:T(8,128)(2,1)S(1)}, bf16[128,256]{1,0:T(8,128)(2,1)S(1)}, u32[]{:S(2)}, u32[]{:S(2)}) collective-permute-start(bf16[128,256]{1,0:T(8,128)(2,1)S(1)} %get-tuple-element.72), channel_id=1, source_target_pairs={{0,24},{2,26},{4,28},{6,30},{8,16},{10,18},{12,20},{14,22},{16,8},... | collective-permute-start | bytes 196616 | tf_op jit(solution)/shard_map/ppermute | solution.py:285
  13.0 6.1 %collective-permute-start.4 = (bf16[128,256]{1,0:T(8,128)(2,1)S(1)}, bf16[128,256]{1,0:T(8,128)(2,1)S(1)}, u32[]{:S(2)}, u32[]{:S(2)}) collective-permute-start(bf16[128,256]{1,0:T(8,128)(2,1)S(1)} %get-tuple-element.73), channel_id=1, source_target_pairs={{0,16},{2,18},{4,20},{6,22},{8,24},{10,26},{12,28},{14,30},{16,0},... | collective-permute-start | bytes 196616 | tf_op jit(solution)/shard_map/ppermute | solution.py:285
  13.0 6.1 %collective-permute-start.5 = (bf16[128,256]{1,0:T(8,128)(2,1)S(1)}, bf16[128,256]{1,0:T(8,128)(2,1)S(1)}, u32[]{:S(2)}, u32[]{:S(2)}) collective-permute-start(bf16[128,256]{1,0:T(8,128)(2,1)S(1)} %get-tuple-element.74), channel_id=1, source_target_pairs={{0,8},{2,10},{4,12},{6,14},{8,0},{10,2},{12,4},{14,6},{16,24},{18,... | collective-permute-start | bytes 196616 | tf_op jit(solution)/shard_map/ppermute | solution.py:285
  16.0 9.0 %collective-permute-start.7 = (bf16[1024,128]{1,0:T(8,128)(2,1)S(1)}, bf16[1024,128]{1,0:T(8,128)(2,1)S(1)}, u32[]{:S(2)}, u32[]{:S(2)}) collective-permute-start(bf16[1024,128]{1,0:T(8,128)(2,1)S(1)} %shard_map.86.pair_ref), channel_id=1, source_target_pairs={{0,4},{2,6},{4,0},{6,2},{8,12},{10,14},{12,8},{14,10},{16,20},{18,... | collective-permute-start | bytes 786440 | tf_op jit(solution)/shard_map/ppermute | solution.py:285
  16.4 5.7 %collective-permute-start.6 = (bf16[1024,128]{1,0:T(8,128)(2,1)S(1)}, bf16[1024,128]{1,0:T(8,128)(2,1)S(1)}, u32[]{:S(2)}, u32[]{:S(2)}) collective-permute-start(bf16[1024,128]{1,0:T(8,128)(2,1)S(1)} %shard_map.86.pair_ref), channel_id=1, source_target_pairs={{0,2},{2,0},{4,6},{6,4},{8,10},{10,8},{12,14},{14,12},{16,18},{18,... | collective-permute-start | bytes 786440 | tf_op jit(solution)/shard_map/ppermute | solution.py:285
  25.1 3.0 %collective-permute-start.8 = (bf16[1024,128]{1,0:T(8,128)(2,1)S(1)}, bf16[1024,128]{1,0:T(8,128)(2,1)S(1)}, u32[]{:S(2)}, u32[]{:S(2)}) collective-permute-start(bf16[1024,128]{1,0:T(8,128)(2,1)S(1)} %shard_map.90.pair_ref), channel_id=1, source_target_pairs={{0,2},{2,0},{4,6},{6,4},{8,10},{10,8},{12,14},{14,12},{16,18},{18,... | collective-permute-start | bytes 786440 | tf_op jit(solution)/shard_map/ppermute | solution.py:285
  31.4 6.6 %collective-permute-start.9 = (bf16[64,256]{1,0:T(8,128)(2,1)S(1)}, bf16[64,256]{1,0:T(8,128)(2,1)S(1)}, u32[]{:S(2)}, u32[]{:S(2)}) collective-permute-start(bf16[64,256]{1,0:T(8,128)(2,1)S(1)} %get-tuple-element.106), channel_id=1, source_target_pairs={{0,24},{2,26},{4,28},{6,30},{8,16},{10,18},{12,20},{14,22},{16,8},... | collective-permute-start | bytes 98312 | tf_op jit(solution)/shard_map/ppermute | solution.py:285
  34.1 4.8 %collective-permute-start.10 = (bf16[64,256]{1,0:T(8,128)(2,1)S(1)}, bf16[64,256]{1,0:T(8,128)(2,1)S(1)}, u32[]{:S(2)}, u32[]{:S(2)}) collective-permute-start(bf16[64,256]{1,0:T(8,128)(2,1)S(1)} %get-tuple-element.107), channel_id=1, source_target_pairs={{0,16},{2,18},{4,20},{6,22},{8,24},{10,26},{12,28},{14,30},{16,0},... | collective-permute-start | bytes 98312 | tf_op jit(solution)/shard_map/ppermute | solution.py:285
  34.1 4.8 %collective-permute-start.11 = (bf16[64,256]{1,0:T(8,128)(2,1)S(1)}, bf16[64,256]{1,0:T(8,128)(2,1)S(1)}, u32[]{:S(2)}, u32[]{:S(2)}) collective-permute-start(bf16[64,256]{1,0:T(8,128)(2,1)S(1)} %get-tuple-element.108), channel_id=1, source_target_pairs={{0,8},{2,10},{4,12},{6,14},{8,0},{10,2},{12,4},{14,6},{16,24},{18,... | collective-permute-start | bytes 98312 | tf_op jit(solution)/shard_map/ppermute | solution.py:285
  39.9 2.1 %collective-permute-start.12 = (bf16[2,64,768]{2,1,0:T(8,128)(2,1)S(1)}, bf16[2,64,768]{2,1,0:T(8,128)(2,1)S(1)}, u32[]{:S(2)}, u32[]{:S(2)}) collective-permute-start(bf16[2,64,768]{2,1,0:T(8,128)(2,1)S(1)} %get-tuple-element.111), channel_id=1, source_target_pairs={{0,2},{2,0},{4,6},{6,4},{8,10},{10,8},{12,14},{14,12},{16,18},{18,... | collective-permute-start | bytes 589832 | tf_op jit(solution)/shard_map/ppermute | solution.py:285
  39.9 5.8 %collective-permute-start.15 = (bf16[128,1024]{1,0:T(8,128)(2,1)S(1)}, bf16[128,1024]{1,0:T(8,128)(2,1)S(1)}, u32[]{:S(2)}, u32[]{:S(2)}) collective-permute-start(bf16[128,1024]{1,0:T(8,128)(2,1)S(1)} %get-tuple-element.109.refs_4_), channel_id=1, source_target_pairs={{0,2},{2,0},{4,6},{6,4},{8,10},{10,8},{12,14},{14,12},{16,18},{18,... | collective-permute-start | bytes 786440 | tf_op jit(solution)/shard_map/ppermute | solution.py:285
  40.4 13.1 %collective-permute-start.17 = (bf16[256,768]{1,0:T(8,128)(2,1)S(1)}, bf16[256,768]{1,0:T(8,128)(2,1)S(1)}, u32[]{:S(2)}, u32[]{:S(2)}) collective-permute-start(bf16[256,768]{1,0:T(8,128)(2,1)S(1)} %get-tuple-element.119.refs_4_), channel_id=1, source_target_pairs={{0,1},{1,0},{2,3},{3,2},{4,5},{5,4},{6,7},{7,6},{8,9},{9,8},{10,11... | collective-permute-start | bytes 1179656 | tf_op jit(solution)/shard_map/ppermute | solution.py:285
  42.0 4.7 %collective-permute-start.13 = (bf16[64,768]{1,0:T(8,128)(2,1)S(1)}, bf16[64,768]{1,0:T(8,128)(2,1)S(1)}, u32[]{:S(2)}, u32[]{:S(2)}) collective-permute-start(bf16[64,768]{1,0:T(8,128)(2,1)S(1)} %get-tuple-element.114), channel_id=1, source_target_pairs={{0,4},{2,6},{4,0},{6,2},{8,12},{10,14},{12,8},{14,10},{16,20},{18,... | collective-permute-start | bytes 294920 | tf_op jit(solution)/shard_map/ppermute | solution.py:285
  45.8 7.8 %collective-permute-start.16 = (bf16[128,1024]{1,0:T(8,128)(2,1)S(1)}, bf16[128,1024]{1,0:T(8,128)(2,1)S(1)}, u32[]{:S(2)}, u32[]{:S(2)}) collective-permute-start(bf16[128,1024]{1,0:T(8,128)(2,1)S(1)} %shard_map.102), channel_id=1, source_target_pairs={{0,4},{2,6},{4,0},{6,2},{8,12},{10,14},{12,8},{14,10},{16,20},{18,... | collective-permute-start | bytes 786440 | tf_op jit(solution)/shard_map/ppermute | solution.py:285
  46.7 4.7 %collective-permute-start.14 = (bf16[64,768]{1,0:T(8,128)(2,1)S(1)}, bf16[64,768]{1,0:T(8,128)(2,1)S(1)}, u32[]{:S(2)}, u32[]{:S(2)}) collective-permute-start(bf16[64,768]{1,0:T(8,128)(2,1)S(1)} %shard_map.98.refs_1_.a_ref), channel_id=1, source_target_pairs={{0,8},{2,10},{4,12},{6,14},{8,0},{10,2},{12,4},{14,6},{16,24},{18,... | collective-permute-start | bytes 294920 | tf_op jit(solution)/shard_map/ppermute | solution.py:285
  49.8 5.0 %collective-permute-start.18 = (bf16[128,1024]{1,0:T(8,128)(2,1)S(1)}, bf16[128,1024]{1,0:T(8,128)(2,1)S(1)}, u32[]{:S(2)}, u32[]{:S(2)}) collective-permute-start(bf16[128,1024]{1,0:T(8,128)(2,1)S(1)} %get-tuple-element.121), channel_id=1, source_target_pairs={{0,2},{2,0},{4,6},{6,4},{8,10},{10,8},{12,14},{14,12},{16,18},{18,... | collective-permute-start | bytes 786440 | tf_op jit(solution)/shard_map/ppermute | solution.py:285
  51.4 12.4 %collective-permute-start.22 = (bf16[64,768]{1,0:T(8,128)(2,1)S(1)}, bf16[64,768]{1,0:T(8,128)(2,1)S(1)}, u32[]{:S(2)}, u32[]{:S(2)}) collective-permute-start(bf16[64,768]{1,0:T(8,128)(2,1)S(1)} %shard_map.101.refs_1_.a_ref), channel_id=1, source_target_pairs={{0,16},{2,18},{4,20},{6,22},{8,24},{10,26},{12,28},{14,30},{16,0},... | collective-permute-start | bytes 294920 | tf_op jit(solution)/shard_map/ppermute | solution.py:285
  54.9 10.6 %collective-permute-start.19 = (bf16[192,256]{1,0:T(8,128)(2,1)S(1)}, bf16[192,256]{1,0:T(8,128)(2,1)S(1)}, u32[]{:S(2)}, u32[]{:S(2)}) collective-permute-start(bf16[192,256]{1,0:T(8,128)(2,1)S(1)} %get-tuple-element.124), channel_id=1, source_target_pairs={{0,24},{2,26},{4,28},{6,30},{8,16},{10,18},{12,20},{14,22},{16,8},... | collective-permute-start | bytes 294920 | tf_op jit(solution)/shard_map/ppermute | solution.py:285
  57.2 10.5 %collective-permute-start.20 = (bf16[192,256]{1,0:T(8,128)(2,1)S(1)}, bf16[192,256]{1,0:T(8,128)(2,1)S(1)}, u32[]{:S(2)}, u32[]{:S(2)}) collective-permute-start(bf16[192,256]{1,0:T(8,128)(2,1)S(1)} %get-tuple-element.125), channel_id=1, source_target_pairs={{0,16},{2,18},{4,20},{6,22},{8,24},{10,26},{12,28},{14,30},{16,0},... | collective-permute-start | bytes 294920 | tf_op jit(solution)/shard_map/ppermute | solution.py:285
  57.3 10.4 %collective-permute-start.21 = (bf16[192,256]{1,0:T(8,128)(2,1)S(1)}, bf16[192,256]{1,0:T(8,128)(2,1)S(1)}, u32[]{:S(2)}, u32[]{:S(2)}) collective-permute-start(bf16[192,256]{1,0:T(8,128)(2,1)S(1)} %get-tuple-element.126), channel_id=1, source_target_pairs={{0,8},{2,10},{4,12},{6,14},{8,0},{10,2},{12,4},{14,6},{16,24},{18,... | collective-permute-start | bytes 294920 | tf_op jit(solution)/shard_map/ppermute | solution.py:285
  63.8 4.7 %collective-permute-start.23 = (bf16[64,768]{1,0:T(8,128)(2,1)S(1)}, bf16[64,768]{1,0:T(8,128)(2,1)S(1)}, u32[]{:S(2)}, u32[]{:S(2)}) collective-permute-start(bf16[64,768]{1,0:T(8,128)(2,1)S(1)} %shard_map.106.refs_0_), channel_id=1, source_target_pairs={{0,4},{2,6},{4,0},{6,2},{8,12},{10,14},{12,8},{14,10},{16,20},{18,... | collective-permute-start | bytes 294920 | tf_op jit(solution)/shard_map/ppermute | solution.py:285
  65.5 4.1 %collective-permute-start.24 = (bf16[64,768]{1,0:T(8,128)(2,1)S(1)}, bf16[64,768]{1,0:T(8,128)(2,1)S(1)}, u32[]{:S(2)}, u32[]{:S(2)}) collective-permute-start(bf16[64,768]{1,0:T(8,128)(2,1)S(1)} %shard_map.106.refs_0_), channel_id=1, source_target_pairs={{0,2},{2,0},{4,6},{6,4},{8,10},{10,8},{12,14},{14,12},{16,18},{18,... | collective-permute-start | bytes 294920 | tf_op jit(solution)/shard_map/ppermute | solution.py:285
  68.5 1.4 %collective-permute-start.25 = (bf16[64,768]{1,0:T(8,128)(2,1)S(1)}, bf16[64,768]{1,0:T(8,128)(2,1)S(1)}, u32[]{:S(2)}, u32[]{:S(2)}) collective-permute-start(bf16[64,768]{1,0:T(8,128)(2,1)S(1)} %shard_map.108.refs_6_.refs_2_), channel_id=1, source_target_pairs={{0,2},{2,0},{4,6},{6,4},{8,10},{10,8},{12,14},{14,12},{16,18},{18,... | collective-permute-start | bytes 294920 | tf_op jit(solution)/shard_map/ppermute | solution.py:285

commit v19 on v15

--- a/solution.py
+++ b/solution.py
@@ -55,7 +55,7 @@
 
 
 def spread(slots):
-    return [0] + sorted(range(1, slots), key=lambda mask: (mask < slots // 2, mask))
+    return [0] + list(range(slots - 1, 0, -1))
 
 
 def pack_kv_kernel(heads, rows, dim, a_of, fill_ref, kv_ref, *refs):

time: 68.4 us -> 69.1 us (1.010)
  starting transfers between devices: 25.1 us -> 28.3 us
  waiting for transfers between devices: 15.3 us -> 12.7 us
    ppermute x26, starting transfers between devices: 25.1 us -> 28.3 us  [swap(): return lax.ppermute(array, axis, [(i, i ^ mask) for i in range(size)])]
    ppermute x26, waiting for transfers between devices: 15.3 us -> 12.7 us  [swap(): return lax.ppermute(array, axis, [(i, i ^ mask) for i in range(size)])]
  transfers between devices with their start and end apart: 26 -> 26, of which waited for: 10 -> 9; matrix products, arithmetic and copies ran while one was open for 0% -> 0% of each run, Pallas kernels for 29% -> 29%
where the time goes in v19:
time: 69.1 us; the launch traced here: 68.9 us
  starting transfers between devices  28.3 us (41%)
  Pallas kernels  26.9 us (39%)
  waiting for transfers between devices  12.7 us (18%)
  between operations  0.92 us (1%)
    ppermute x26, starting transfers between devices, swap(): return lax.ppermute(array, axis, [(i, i ^ mask) for i in range(size)])  28.3 us
    ppermute x26, waiting for transfers between devices, swap(): return lax.ppermute(array, axis, [(i, i ^ mask) for i in range(size)])  12.7 us
    pallas_call x4, Pallas kernels, shards(): call(functools.partial(score_kernel, slots, rows, dim, step), [((block, b...  11.9 us
    pallas_call x4, Pallas kernels, shards(): call(functools.partial(back_kernel, slots, rows, dim, dq is None), [((wid...  8.65 us
    pallas_call x1, Pallas kernels, shards(): call(functools.partial(pack_kv_kernel, heads, rows, dim, a_of), [((rows,...  1.9 us
  transfers between devices with their start and end apart: 26, of which 9 were waited for; matrix products, arithmetic and copies ran while one was open for 0% of the time, Pallas kernels for 29%

profile of v19, /device:TPU:0, one launch (start us, length us, event | category | flops | bytes accessed | tf_op | source)
XLA Modules:
  0.0 68.9 jit_solution(15095558841672138129)
XLA Ops:
  0.7 1.9 %shard_map.84 = (bf16[256,128]{1,0:T(8,128)(2,1)}, bf16[256,128]{1,0:T(8,128)(2,1)}, bf16[256,128]{1,0:T(8,128)(2,1)}, bf16[256,128]{1,0:T(8,128)(2,1)}) custom-call(s32[2]{0:T(128)} %fill_ref.5, bf16[1024,128]{1,0:T(8,128)(2,1)} %bitcast.5), custom_call_target="tpu_custom_call" | custom-call | flops 1724999936 | tf_op jit(solution)/shard_map/pallas_call | solution.py:282
  2.6 5.0 %collective-permute-start = (bf16[256,128]{1,0:T(8,128)(2,1)}, bf16[256,128]{1,0:T(8,128)(2,1)S(1)}, u32[]{:S(2)}, u32[]{:S(2)}) collective-permute-start(bf16[256,128]{1,0:T(8,128)(2,1)} %get-tuple-element.66), channel_id=1, source_target_pairs={{0,24},{2,26},{4,28},{6,30},{8,16},{10,18},{12,20},{14,22},{16,8},... | collective-permute-start | bytes 196616 | tf_op jit(solution)/shard_map/ppermute | solution.py:276
  7.6 0.0 collective-permute-start.1
  7.6 0.6 collective-permute-start.2
  8.2 0.0 copy-start
  8.2 0.9 %shard_map.85 = (bf16[128,256]{1,0:T(8,128)(2,1)S(1)}, bf16[128,256]{1,0:T(8,128)(2,1)S(1)}, bf16[128,256]{1,0:T(8,128)(2,1)S(1)}, bf16[128,256]{1,0:T(8,128)(2,1)S(1)}) custom-call(s32[2]{0:T(128)S(1)} %copy-done.4, bf16[4,64,256]{2,1,0:T(8,128)(2,1)S(1)} %bitcast.4, bf16[4,64,768]{2,1,0:T(8,128)(2,1)S(1)} %copy-done.1, bf16[256,768]{1,0:T(8,128)(2,1)S(1)} %copy-done.2), custom_call_target="tpu_custom_call" | custom-call | flops 1150000000 | tf_op jit(solution)/shard_map/pallas_call | solution.py:287
  9.1 3.9 %collective-permute-start.3 = (bf16[128,256]{1,0:T(8,128)(2,1)S(1)}, bf16[128,256]{1,0:T(8,128)(2,1)S(1)}, u32[]{:S(2)}, u32[]{:S(2)}) collective-permute-start(bf16[128,256]{1,0:T(8,128)(2,1)S(1)} %get-tuple-element.70), channel_id=1, source_target_pairs={{0,24},{2,26},{4,28},{6,30},{8,16},{10,18},{12,20},{14,22},{16,8},... | collective-permute-start | bytes 196616 | tf_op jit(solution)/shard_map/ppermute | solution.py:276
  13.0 0.0 collective-permute-start.4
  13.0 0.0 collective-permute-done.refs_1_
  13.0 0.6 collective-permute-start.5
  13.6 2.4 %collective-permute-done.1.refs_2_ = bf16[256,128]{1,0:T(8,128)(2,1)S(1)} collective-permute-done((bf16[256,128]{1,0:T(8,128)(2,1)}, bf16[256,128]{1,0:T(8,128)(2,1)S(1)}, u32[]{:S(2)}, u32[]{:S(2)}) %collective-permute-start.1) | collective-permute-done | bytes 65568 | tf_op jit(solution)/shard_map/ppermute | solution.py:276
  16.0 0.0 collective-permute-done.2.refs_3_
  16.0 0.4 collective-permute-start.7
  16.4 0.0 collective-permute-start.6
  16.4 0.0 collective-permute-done.3.refs_1_
  16.4 2.6 %collective-permute-done.4.refs_2_ = bf16[128,256]{1,0:T(8,128)(2,1)S(1)} collective-permute-done((bf16[128,256]{1,0:T(8,128)(2,1)S(1)}, bf16[128,256]{1,0:T(8,128)(2,1)S(1)}, u32[]{:S(2)}, u32[]{:S(2)}) %collective-permute-start.4) | collective-permute-done | bytes 65568 | tf_op jit(solution)/shard_map/ppermute | solution.py:276
  19.1 0.0 collective-permute-done.5.refs_3_
  19.1 0.1 shard_map.87
  19.2 2.9 %shard_map.88 = (bf16[1024,1024]{1,0:T(8,128)(2,1)S(1)}, f32[1,1024]{1,0:T(1,128)S(1)}, f32[80,1024]{1,0:T(8,128)S(1)}, bf16[1024,128]{1,0:T(8,128)(2,1)S(1)}, bf16[64,1024]{1,0:T(8,128)(2,1)S(1)}) custom-call(bf16[1024,128]{1,0:T(8,128)(2,1)S(1)} %shard_map.86.pair_ref, bf16[256,1024]{1,0:T(8,128)(2,1)S(1)} %get-tuple-element.73.qa_ref, ...), custom_call_target="tpu_custom_call" | custom-call | flops 5750000128 | tf_op jit(solution)/shard_map/pallas_call | solution.py:313
  22.1 0.0 collective-permute-done.6.pair_ref
  22.1 2.9 %shard_map.89 = (bf16[1024,1024]{1,0:T(8,128)(2,1)S(1)}, f32[1,1024]{1,0:T(1,128)S(1)}, f32[80,1024]{1,0:T(8,128)S(1)}, bf16[1024,128]{1,0:T(8,128)(2,1)S(1)}, bf16[64,1024]{1,0:T(8,128)(2,1)S(1)}) custom-call(bf16[1024,128]{1,0:T(8,128)(2,1)S(1)} %collective-permute-done.6.pair_ref, bf16[256,1024]{1,0:T(8,128)(2,1)S(1)} %get-tuple-element.73.qa_ref, ...), custom_call_target="tpu_custom_call" | custom-call | flops 5750000128 | tf_op jit(solution)/shard_map/pallas_call | solution.py:313
  25.1 0.0 collective-permute-done.7.refs_0_
  25.1 0.1 collective-permute-start.8
  25.2 2.9 %shard_map.91 = (bf16[1024,1024]{1,0:T(8,128)(2,1)S(1)}, f32[1,1024]{1,0:T(1,128)S(1)}, f32[80,1024]{1,0:T(8,128)S(1)}, bf16[1024,128]{1,0:T(8,128)(2,1)S(1)}, bf16[64,1024]{1,0:T(8,128)(2,1)S(1)}) custom-call(bf16[1024,128]{1,0:T(8,128)(2,1)S(1)} %shard_map.90.pair_ref, bf16[256,1024]{1,0:T(8,128)(2,1)S(1)} %get-tuple-element.73.qa_ref, ...), custom_call_target="tpu_custom_call" | custom-call | flops 5750000128 | tf_op jit(solution)/shard_map/pallas_call | solution.py:313
  28.1 0.0 collective-permute-done.8.pair_ref
  28.1 3.1 %shard_map.92 = (bf16[1024,1024]{1,0:T(8,128)(2,1)S(1)}, f32[1,1024]{1,0:T(1,128)S(1)}, f32[80,1024]{1,0:T(8,128)S(1)}, bf16[1024,128]{1,0:T(8,128)(2,1)S(1)}, bf16[64,1024]{1,0:T(8,128)(2,1)S(1)}) custom-call(bf16[1024,128]{1,0:T(8,128)(2,1)S(1)} %collective-permute-done.8.pair_ref, bf16[256,1024]{1,0:T(8,128)(2,1)S(1)} %get-tuple-element.73.qa_ref, ...), custom_call_target="tpu_custom_call" | custom-call | flops 5750000128 | tf_op jit(solution)/shard_map/pallas_call | solution.py:313
  31.2 0.2 shard_map.93
  31.4 2.7 %collective-permute-start.9 = (bf16[64,256]{1,0:T(8,128)(2,1)S(1)}, bf16[64,256]{1,0:T(8,128)(2,1)S(1)}, u32[]{:S(2)}, u32[]{:S(2)}) collective-permute-start(bf16[64,256]{1,0:T(8,128)(2,1)S(1)} %get-tuple-element.104), channel_id=1, source_target_pairs={{0,24},{2,26},{4,28},{6,30},{8,16},{10,18},{12,20},{14,22},{16,8},... | collective-permute-start | bytes 98312 | tf_op jit(solution)/shard_map/ppermute | solution.py:276
  34.1 0.0 collective-permute-start.10
  34.1 1.7 %collective-permute-start.11 = (bf16[64,256]{1,0:T(8,128)(2,1)S(1)}, bf16[64,256]{1,0:T(8,128)(2,1)S(1)}, u32[]{:S(2)}, u32[]{:S(2)}) collective-permute-start(bf16[64,256]{1,0:T(8,128)(2,1)S(1)} %get-tuple-element.106), channel_id=1, source_target_pairs={{0,8},{2,10},{4,12},{6,14},{8,0},{10,2},{12,4},{14,6},{16,24},{18,... | collective-permute-start | bytes 98312 | tf_op jit(solution)/shard_map/ppermute | solution.py:276
  35.9 2.2 %shard_map.94 = (bf16[128,1024]{1,0:T(8,128)(2,1)S(1)}, f32[64,1024]{1,0:T(8,128)S(1)}) custom-call(bf16[1024,1024]{1,0:T(8,128)(2,1)S(1)} %get-tuple-element.98.exp_ref, bf16[1024,128]{1,0:T(8,128)(2,1)S(1)} %get-tuple-element.99.v_ref, bf16[64,1024]{1,0:T(8,128)(2,1)S(1)} %get-tuple-element.100.kt_ref, bf16[64,1024]{1,0:T(8,128)(2,1)S(1)} %get-tuple-element.78.q_ref, ...), custom_call_target="tpu_custom_call" | custom-call | flops 2300000000 | tf_op jit(solution)/shard_map/pallas_call | solution.py:355
  38.0 0.9 %collective-permute-done.10.refs_2_ = bf16[64,256]{1,0:T(8,128)(2,1)S(1)} collective-permute-done((bf16[64,256]{1,0:T(8,128)(2,1)S(1)}, bf16[64,256]{1,0:T(8,128)(2,1)S(1)}, u32[]{:S(2)}, u32[]{:S(2)}) %collective-permute-start.10) | collective-permute-done | bytes 32800 | tf_op jit(solution)/shard_map/ppermute | solution.py:276
  38.9 0.0 collective-permute-done.11.refs_3_
  38.9 0.9 %shard_map.95 = (bf16[256,768]{1,0:T(8,128)(2,1)S(1)}, bf16[2,64,768]{2,1,0:T(8,128)(2,1)S(1)}, bf16[2,64,768]{2,1,0:T(8,128)(2,1)S(1)}) custom-call(s32[2]{0:T(128)S(1)} %copy-done.4, bf16[256,768]{1,0:T(8,128)(2,1)S(1)} %copy-done.2, bf16[4,64,768]{2,1,0:T(8,128)(2,1)S(1)} %copy-done.1, bf16[64,256]{1,0:T(8,128)(2,1)S(1)} %get-tuple-element.103.refs_0_, ...), custom_call_target="tpu_custom_call" | custom-call | flops 805000000 | tf_op jit(solution)/shard_map/pallas_call | solution.py:333
  39.9 0.1 collective-permute-start.12
  39.9 0.5 collective-permute-start.15
  40.4 1.5 %collective-permute-start.17 = (bf16[256,768]{1,0:T(8,128)(2,1)S(1)}, bf16[256,768]{1,0:T(8,128)(2,1)S(1)}, u32[]{:S(2)}, u32[]{:S(2)}) collective-permute-start(bf16[256,768]{1,0:T(8,128)(2,1)S(1)} %get-tuple-element.116.refs_4_), channel_id=1, source_target_pairs={{0,1},{1,0},{2,3},{3,2},{4,5},{5,4},{6,7},{7,6},{8,9},{9,8},{10,11... | collective-permute-start | bytes 1179656 | tf_op jit(solution)/shard_map/ppermute | solution.py:276
  42.0 1.6 %collective-permute-start.13 = (bf16[64,768]{1,0:T(8,128)(2,1)S(1)}, bf16[64,768]{1,0:T(8,128)(2,1)S(1)}, u32[]{:S(2)}, u32[]{:S(2)}) collective-permute-start(bf16[64,768]{1,0:T(8,128)(2,1)S(1)} %get-tuple-element.112), channel_id=1, source_target_pairs={{0,4},{2,6},{4,0},{6,2},{8,12},{10,14},{12,8},{14,10},{16,20},{18,... | collective-permute-start | bytes 294920 | tf_op jit(solution)/shard_map/ppermute | solution.py:276
  43.6 2.2 %shard_map.97 = (bf16[128,1024]{1,0:T(8,128)(2,1)S(1)}, f32[64,1024]{1,0:T(8,128)S(1)}) custom-call(bf16[1024,1024]{1,0:T(8,128)(2,1)S(1)} %get-tuple-element.94.exp_ref, bf16[1024,128]{1,0:T(8,128)(2,1)S(1)} %get-tuple-element.95.v_ref, bf16[64,1024]{1,0:T(8,128)(2,1)S(1)} %get-tuple-element.96.kt_ref, bf16[64,1024]{1,0:T(8,128)(2,1)S(1)} %get-tuple-element.78.q_ref, ...), custom_call_target="tpu_custom_call" | custom-call | flops 2300000000 | tf_op jit(solution)/shard_map/pallas_call | solution.py:355
  45.7 0.0 collective-permute-done.15.b_ref
  45.8 0.1 shard_map.101
  45.8 0.6 collective-permute-start.16
  46.4 0.3 collective-permute-done.13.b_ref
  46.7 0.9 %collective-permute-start.14 = (bf16[64,768]{1,0:T(8,128)(2,1)S(1)}, bf16[64,768]{1,0:T(8,128)(2,1)S(1)}, u32[]{:S(2)}, u32[]{:S(2)}) collective-permute-start(bf16[64,768]{1,0:T(8,128)(2,1)S(1)} %shard_map.98.refs_1_.a_ref), channel_id=1, source_target_pairs={{0,8},{2,10},{4,12},{6,14},{8,0},{10,2},{12,4},{14,6},{16,24},{18,... | collective-permute-start | bytes 294920 | tf_op jit(solution)/shard_map/ppermute | solution.py:276
  47.6 2.2 %shard_map.99 = (bf16[128,1024]{1,0:T(8,128)(2,1)S(1)}, f32[64,1024]{1,0:T(8,128)S(1)}) custom-call(bf16[1024,1024]{1,0:T(8,128)(2,1)S(1)} %get-tuple-element.90.exp_ref, bf16[1024,128]{1,0:T(8,128)(2,1)S(1)} %get-tuple-element.91.v_ref, bf16[64,1024]{1,0:T(8,128)(2,1)S(1)} %get-tuple-element.92.kt_ref, bf16[64,1024]{1,0:T(8,128)(2,1)S(1)} %get-tuple-element.78.q_ref, ...), custom_call_target="tpu_custom_call" | custom-call | flops 2300000000 | tf_op jit(solution)/shard_map/pallas_call | solution.py:355
  49.8 0.1 collective-permute-start.18
  49.9 1.5 %collective-permute-done.14.b_ref = bf16[64,768]{1,0:T(8,128)(2,1)S(1)} collective-permute-done((bf16[64,768]{1,0:T(8,128)(2,1)S(1)}, bf16[64,768]{1,0:T(8,128)(2,1)S(1)}, u32[]{:S(2)}, u32[]{:S(2)}) %collective-permute-start.14) | collective-permute-done | bytes 98336 | tf_op jit(solution)/shard_map/ppermute | solution.py:276
  51.4 2.1 %collective-permute-start.22 = (bf16[64,768]{1,0:T(8,128)(2,1)S(1)}, bf16[64,768]{1,0:T(8,128)(2,1)S(1)}, u32[]{:S(2)}, u32[]{:S(2)}) collective-permute-start(bf16[64,768]{1,0:T(8,128)(2,1)S(1)} %shard_map.100.refs_1_.a_ref), channel_id=1, source_target_pairs={{0,16},{2,18},{4,20},{6,22},{8,24},{10,26},{12,28},{14,30},{16,0},... | collective-permute-start | bytes 294920 | tf_op jit(solution)/shard_map/ppermute | solution.py:276
  53.5 0.1 collective-permute-done.16.refs_2_.came_ref
  53.6 2.2 %shard_map.102 = (bf16[128,1024]{1,0:T(8,128)(2,1)S(1)}, f32[64,1024]{1,0:T(8,128)S(1)}) custom-call(bf16[1024,1024]{1,0:T(8,128)(2,1)S(1)} %get-tuple-element.75.exp_ref, bf16[1024,128]{1,0:T(8,128)(2,1)S(1)} %get-tuple-element.76.v_ref, bf16[64,1024]{1,0:T(8,128)(2,1)S(1)} %get-tuple-element.77.kt_ref, bf16[64,1024]{1,0:T(8,128)(2,1)S(1)} %get-tuple-element.78.q_ref, ...), custom_call_target="tpu_custom_call" | custom-call | flops 2300000000 | tf_op jit(solution)/shard_map/pallas_call | solution.py:355
  55.8 0.1 shard_map.103.kept_ref
  55.9 0.1 shard_map.104
  56.0 2.3 %collective-permute-start.19 = (bf16[192,256]{1,0:T(8,128)(2,1)S(1)}, bf16[192,256]{1,0:T(8,128)(2,1)S(1)}, u32[]{:S(2)}, u32[]{:S(2)}) collective-permute-start(bf16[192,256]{1,0:T(8,128)(2,1)S(1)} %get-tuple-element.120), channel_id=1, source_target_pairs={{0,24},{2,26},{4,28},{6,30},{8,16},{10,18},{12,20},{14,22},{16,8},... | collective-permute-start | bytes 294920 | tf_op jit(solution)/shard_map/ppermute | solution.py:276
  58.2 0.1 collective-permute-start.20
  58.3 2.1 %collective-permute-start.21 = (bf16[192,256]{1,0:T(8,128)(2,1)S(1)}, bf16[192,256]{1,0:T(8,128)(2,1)S(1)}, u32[]{:S(2)}, u32[]{:S(2)}) collective-permute-start(bf16[192,256]{1,0:T(8,128)(2,1)S(1)} %get-tuple-element.122), channel_id=1, source_target_pairs={{0,8},{2,10},{4,12},{6,14},{8,0},{10,2},{12,4},{14,6},{16,24},{18,... | collective-permute-start | bytes 294920 | tf_op jit(solution)/shard_map/ppermute | solution.py:276
  60.5 1.5 %collective-permute-start.23 = (bf16[64,768]{1,0:T(8,128)(2,1)S(1)}, bf16[64,768]{1,0:T(8,128)(2,1)S(1)}, u32[]{:S(2)}, u32[]{:S(2)}) collective-permute-start(bf16[64,768]{1,0:T(8,128)(2,1)S(1)} %shard_map.105.refs_0_), channel_id=1, source_target_pairs={{0,4},{2,6},{4,0},{6,2},{8,12},{10,14},{12,8},{14,10},{16,20},{18,... | collective-permute-start | bytes 294920 | tf_op jit(solution)/shard_map/ppermute | solution.py:276
  61.9 1.4 %collective-permute-done.19.refs_1_ = bf16[192,256]{1,0:T(8,128)(2,1)S(1)} collective-permute-done((bf16[192,256]{1,0:T(8,128)(2,1)S(1)}, bf16[192,256]{1,0:T(8,128)(2,1)S(1)}, u32[]{:S(2)}, u32[]{:S(2)}) %collective-permute-start.19) | collective-permute-done | bytes 98336 | tf_op jit(solution)/shard_map/ppermute | solution.py:276
  63.3 3.2 %collective-permute-done.20.refs_2_ = bf16[192,256]{1,0:T(8,128)(2,1)S(1)} collective-permute-done((bf16[192,256]{1,0:T(8,128)(2,1)S(1)}, bf16[192,256]{1,0:T(8,128)(2,1)S(1)}, u32[]{:S(2)}, u32[]{:S(2)}) %collective-permute-start.20) | collective-permute-done | bytes 98336 | tf_op jit(solution)/shard_map/ppermute | solution.py:276
  66.6 0.0 collective-permute-done.23.refs_0_
  66.6 0.1 collective-permute-start.25
  66.7 1.1 %shard_map.108 = (f32[1024,128]{1,0:T(8,128)}, f32[4,64,256]{2,1,0:T(8,128)}, bf16[256,768]{1,0:T(8,128)(2,1)}) custom-call(bf16[192,256]{1,0:T(8,128)(2,1)S(1)} %get-tuple-element.119.refs_0_, bf16[192,256]{1,0:T(8,128)(2,1)S(1)} %collective-permute-done.19.refs_1_, bf16[192,256]{1,0:T(8,128)(2,1)S(1)} %collective-permute-done.20.refs_2_, ...), custom_call_target="tpu_custom_call" | custom-call | flops 5750000128 | tf_op jit(solution)/shard_map/pallas_call | solution.py:388
  67.8 0.0 collective-permute-done.24.refs_1_
  67.8 0.2 collective-permute-done.25.refs_3_
  68.0 0.9 %shard_map.109 = f32[4,64,768]{2,1,0:T(8,128)} custom-call(bf16[64,768]{1,0:T(8,128)(2,1)S(1)} %shard_map.105.refs_0_, bf16[64,768]{1,0:T(8,128)(2,1)S(1)} %collective-permute-done.24.refs_1_, bf16[64,768]{1,0:T(8,128)(2,1)S(1)} %shard_map.107.refs_6_.refs_2_, bf16[64,768]{1,0:T(8,128)(2,1)S(1)} %collective-permute-done.25.refs_3_), custom_call_target="tpu_custom_call" | custom-call | flops 575000000 | tf_op jit(solution)/shard_map/pallas_call | solution.py:382
  (24 shorter events, 0.2 us)
Async XLA Ops:
  0.6 7.6 %copy-start.1 = (bf16[4,64,768]{2,1,0:T(8,128)(2,1)S(1)}, bf16[4,64,768]{2,1,0:T(8,128)(2,1)}, u32[]{:S(2)}) copy-start(bf16[4,64,768]{2,1,0:T(8,128)(2,1)} %w_ref.3) | copy-start | bytes 1179652
  0.6 7.6 %copy-start.2 = (bf16[256,768]{1,0:T(8,128)(2,1)S(1)}, bf16[256,768]{1,0:T(8,128)(2,1)}, u32[]{:S(2)}) copy-start(bf16[256,768]{1,0:T(8,128)(2,1)} %go_ref.3) | copy-start | bytes 1179652
  0.7 7.5 %copy-start.3 = (bf16[256,4,64]{0,2,1:T(8,128)(2,1)S(1)}, bf16[256,4,64]{0,2,1:T(8,128)(2,1)}, u32[]{:S(2)}) copy-start(bf16[256,4,64]{0,2,1:T(8,128)(2,1)} %param.5) | copy-start | bytes 393220
  0.7 7.5 %copy-start.4 = (s32[2]{0:T(128)S(1)}, s32[2]{0:T(128)}, u32[]{:S(2)}) copy-start(s32[2]{0:T(128)} %fill_ref.5) | copy-start | bytes 28
  2.6 10.4 %collective-permute-start = (bf16[256,128]{1,0:T(8,128)(2,1)}, bf16[256,128]{1,0:T(8,128)(2,1)S(1)}, u32[]{:S(2)}, u32[]{:S(2)}) collective-permute-start(bf16[256,128]{1,0:T(8,128)(2,1)} %get-tuple-element.66), channel_id=1, source_target_pairs={{0,24},{2,26},{4,28},{6,30},{8,16},{10,18},{12,20},{14,22},{16,8},... | collective-permute-start | bytes 196616 | tf_op jit(solution)/shard_map/ppermute | solution.py:276
  7.6 8.4 %collective-permute-start.1 = (bf16[256,128]{1,0:T(8,128)(2,1)}, bf16[256,128]{1,0:T(8,128)(2,1)S(1)}, u32[]{:S(2)}, u32[]{:S(2)}) collective-permute-start(bf16[256,128]{1,0:T(8,128)(2,1)} %get-tuple-element.67), channel_id=1, source_target_pairs={{0,16},{2,18},{4,20},{6,22},{8,24},{10,26},{12,28},{14,30},{16,0},... | collective-permute-start | bytes 196616 | tf_op jit(solution)/shard_map/ppermute | solution.py:276
  7.6 8.4 %collective-permute-start.2 = (bf16[256,128]{1,0:T(8,128)(2,1)}, bf16[256,128]{1,0:T(8,128)(2,1)S(1)}, u32[]{:S(2)}, u32[]{:S(2)}) collective-permute-start(bf16[256,128]{1,0:T(8,128)(2,1)} %get-tuple-element.68), channel_id=1, source_target_pairs={{0,8},{2,10},{4,12},{6,14},{8,0},{10,2},{12,4},{14,6},{16,24},{18,... | collective-permute-start | bytes 196616 | tf_op jit(solution)/shard_map/ppermute | solution.py:276
  8.2 7.8 %copy-start = (bf16[256,128]{1,0:T(8,128)(2,1)S(1)}, bf16[256,128]{1,0:T(8,128)(2,1)}, u32[]{:S(2)}) copy-start(bf16[256,128]{1,0:T(8,128)(2,1)} %get-tuple-element.65.refs_0_) | copy-start | bytes 196612
  9.1 7.3 %collective-permute-start.3 = (bf16[128,256]{1,0:T(8,128)(2,1)S(1)}, bf16[128,256]{1,0:T(8,128)(2,1)S(1)}, u32[]{:S(2)}, u32[]{:S(2)}) collective-permute-start(bf16[128,256]{1,0:T(8,128)(2,1)S(1)} %get-tuple-element.70), channel_id=1, source_target_pairs={{0,24},{2,26},{4,28},{6,30},{8,16},{10,18},{12,20},{14,22},{16,8},... | collective-permute-start | bytes 196616 | tf_op jit(solution)/shard_map/ppermute | solution.py:276
  13.0 6.1 %collective-permute-start.4 = (bf16[128,256]{1,0:T(8,128)(2,1)S(1)}, bf16[128,256]{1,0:T(8,128)(2,1)S(1)}, u32[]{:S(2)}, u32[]{:S(2)}) collective-permute-start(bf16[128,256]{1,0:T(8,128)(2,1)S(1)} %get-tuple-element.71), channel_id=1, source_target_pairs={{0,16},{2,18},{4,20},{6,22},{8,24},{10,26},{12,28},{14,30},{16,0},... | collective-permute-start | bytes 196616 | tf_op jit(solution)/shard_map/ppermute | solution.py:276
  13.0 6.1 %collective-permute-start.5 = (bf16[128,256]{1,0:T(8,128)(2,1)S(1)}, bf16[128,256]{1,0:T(8,128)(2,1)S(1)}, u32[]{:S(2)}, u32[]{:S(2)}) collective-permute-start(bf16[128,256]{1,0:T(8,128)(2,1)S(1)} %get-tuple-element.72), channel_id=1, source_target_pairs={{0,8},{2,10},{4,12},{6,14},{8,0},{10,2},{12,4},{14,6},{16,24},{18,... | collective-permute-start | bytes 196616 | tf_op jit(solution)/shard_map/ppermute | solution.py:276
  16.0 9.0 %collective-permute-start.7 = (bf16[1024,128]{1,0:T(8,128)(2,1)S(1)}, bf16[1024,128]{1,0:T(8,128)(2,1)S(1)}, u32[]{:S(2)}, u32[]{:S(2)}) collective-permute-start(bf16[1024,128]{1,0:T(8,128)(2,1)S(1)} %shard_map.86.pair_ref), channel_id=1, source_target_pairs={{0,4},{2,6},{4,0},{6,2},{8,12},{10,14},{12,8},{14,10},{16,20},{18,... | collective-permute-start | bytes 786440 | tf_op jit(solution)/shard_map/ppermute | solution.py:276
  16.4 5.7 %collective-permute-start.6 = (bf16[1024,128]{1,0:T(8,128)(2,1)S(1)}, bf16[1024,128]{1,0:T(8,128)(2,1)S(1)}, u32[]{:S(2)}, u32[]{:S(2)}) collective-permute-start(bf16[1024,128]{1,0:T(8,128)(2,1)S(1)} %shard_map.86.pair_ref), channel_id=1, source_target_pairs={{0,2},{2,0},{4,6},{6,4},{8,10},{10,8},{12,14},{14,12},{16,18},{18,... | collective-permute-start | bytes 786440 | tf_op jit(solution)/shard_map/ppermute | solution.py:276
  25.1 3.0 %collective-permute-start.8 = (bf16[1024,128]{1,0:T(8,128)(2,1)S(1)}, bf16[1024,128]{1,0:T(8,128)(2,1)S(1)}, u32[]{:S(2)}, u32[]{:S(2)}) collective-permute-start(bf16[1024,128]{1,0:T(8,128)(2,1)S(1)} %shard_map.90.pair_ref), channel_id=1, source_target_pairs={{0,2},{2,0},{4,6},{6,4},{8,10},{10,8},{12,14},{14,12},{16,18},{18,... | collective-permute-start | bytes 786440 | tf_op jit(solution)/shard_map/ppermute | solution.py:276
  31.4 6.6 %collective-permute-start.9 = (bf16[64,256]{1,0:T(8,128)(2,1)S(1)}, bf16[64,256]{1,0:T(8,128)(2,1)S(1)}, u32[]{:S(2)}, u32[]{:S(2)}) collective-permute-start(bf16[64,256]{1,0:T(8,128)(2,1)S(1)} %get-tuple-element.104), channel_id=1, source_target_pairs={{0,24},{2,26},{4,28},{6,30},{8,16},{10,18},{12,20},{14,22},{16,8},... | collective-permute-start | bytes 98312 | tf_op jit(solution)/shard_map/ppermute | solution.py:276
  34.1 4.8 %collective-permute-start.10 = (bf16[64,256]{1,0:T(8,128)(2,1)S(1)}, bf16[64,256]{1,0:T(8,128)(2,1)S(1)}, u32[]{:S(2)}, u32[]{:S(2)}) collective-permute-start(bf16[64,256]{1,0:T(8,128)(2,1)S(1)} %get-tuple-element.105), channel_id=1, source_target_pairs={{0,16},{2,18},{4,20},{6,22},{8,24},{10,26},{12,28},{14,30},{16,0},... | collective-permute-start | bytes 98312 | tf_op jit(solution)/shard_map/ppermute | solution.py:276
  34.1 4.8 %collective-permute-start.11 = (bf16[64,256]{1,0:T(8,128)(2,1)S(1)}, bf16[64,256]{1,0:T(8,128)(2,1)S(1)}, u32[]{:S(2)}, u32[]{:S(2)}) collective-permute-start(bf16[64,256]{1,0:T(8,128)(2,1)S(1)} %get-tuple-element.106), channel_id=1, source_target_pairs={{0,8},{2,10},{4,12},{6,14},{8,0},{10,2},{12,4},{14,6},{16,24},{18,... | collective-permute-start | bytes 98312 | tf_op jit(solution)/shard_map/ppermute | solution.py:276
  39.9 2.1 %collective-permute-start.12 = (bf16[2,64,768]{2,1,0:T(8,128)(2,1)S(1)}, bf16[2,64,768]{2,1,0:T(8,128)(2,1)S(1)}, u32[]{:S(2)}, u32[]{:S(2)}) collective-permute-start(bf16[2,64,768]{2,1,0:T(8,128)(2,1)S(1)} %get-tuple-element.109), channel_id=1, source_target_pairs={{0,2},{2,0},{4,6},{6,4},{8,10},{10,8},{12,14},{14,12},{16,18},{18,... | collective-permute-start | bytes 589832 | tf_op jit(solution)/shard_map/ppermute | solution.py:276
  39.9 5.8 %collective-permute-start.15 = (bf16[128,1024]{1,0:T(8,128)(2,1)S(1)}, bf16[128,1024]{1,0:T(8,128)(2,1)S(1)}, u32[]{:S(2)}, u32[]{:S(2)}) collective-permute-start(bf16[128,1024]{1,0:T(8,128)(2,1)S(1)} %get-tuple-element.107.refs_4_), channel_id=1, source_target_pairs={{0,2},{2,0},{4,6},{6,4},{8,10},{10,8},{12,14},{14,12},{16,18},{18,... | collective-permute-start | bytes 786440 | tf_op jit(solution)/shard_map/ppermute | solution.py:276
  40.4 13.1 %collective-permute-start.17 = (bf16[256,768]{1,0:T(8,128)(2,1)S(1)}, bf16[256,768]{1,0:T(8,128)(2,1)S(1)}, u32[]{:S(2)}, u32[]{:S(2)}) collective-permute-start(bf16[256,768]{1,0:T(8,128)(2,1)S(1)} %get-tuple-element.116.refs_4_), channel_id=1, source_target_pairs={{0,1},{1,0},{2,3},{3,2},{4,5},{5,4},{6,7},{7,6},{8,9},{9,8},{10,11... | collective-permute-start | bytes 1179656 | tf_op jit(solution)/shard_map/ppermute | solution.py:276
  42.0 4.7 %collective-permute-start.13 = (bf16[64,768]{1,0:T(8,128)(2,1)S(1)}, bf16[64,768]{1,0:T(8,128)(2,1)S(1)}, u32[]{:S(2)}, u32[]{:S(2)}) collective-permute-start(bf16[64,768]{1,0:T(8,128)(2,1)S(1)} %get-tuple-element.112), channel_id=1, source_target_pairs={{0,4},{2,6},{4,0},{6,2},{8,12},{10,14},{12,8},{14,10},{16,20},{18,... | collective-permute-start | bytes 294920 | tf_op jit(solution)/shard_map/ppermute | solution.py:276
  45.8 7.8 %collective-permute-start.16 = (bf16[128,1024]{1,0:T(8,128)(2,1)S(1)}, bf16[128,1024]{1,0:T(8,128)(2,1)S(1)}, u32[]{:S(2)}, u32[]{:S(2)}) collective-permute-start(bf16[128,1024]{1,0:T(8,128)(2,1)S(1)} %shard_map.101), channel_id=1, source_target_pairs={{0,4},{2,6},{4,0},{6,2},{8,12},{10,14},{12,8},{14,10},{16,20},{18,... | collective-permute-start | bytes 786440 | tf_op jit(solution)/shard_map/ppermute | solution.py:276
  46.7 4.7 %collective-permute-start.14 = (bf16[64,768]{1,0:T(8,128)(2,1)S(1)}, bf16[64,768]{1,0:T(8,128)(2,1)S(1)}, u32[]{:S(2)}, u32[]{:S(2)}) collective-permute-start(bf16[64,768]{1,0:T(8,128)(2,1)S(1)} %shard_map.98.refs_1_.a_ref), channel_id=1, source_target_pairs={{0,8},{2,10},{4,12},{6,14},{8,0},{10,2},{12,4},{14,6},{16,24},{18,... | collective-permute-start | bytes 294920 | tf_op jit(solution)/shard_map/ppermute | solution.py:276
  49.8 6.0 %collective-permute-start.18 = (bf16[128,1024]{1,0:T(8,128)(2,1)S(1)}, bf16[128,1024]{1,0:T(8,128)(2,1)S(1)}, u32[]{:S(2)}, u32[]{:S(2)}) collective-permute-start(bf16[128,1024]{1,0:T(8,128)(2,1)S(1)} %get-tuple-element.115.refs_0_), channel_id=1, source_target_pairs={{0,2},{2,0},{4,6},{6,4},{8,10},{10,8},{12,14},{14,12},{16,18},{18,... | collective-permute-start | bytes 786440 | tf_op jit(solution)/shard_map/ppermute | solution.py:276
  51.4 9.0 %collective-permute-start.22 = (bf16[64,768]{1,0:T(8,128)(2,1)S(1)}, bf16[64,768]{1,0:T(8,128)(2,1)S(1)}, u32[]{:S(2)}, u32[]{:S(2)}) collective-permute-start(bf16[64,768]{1,0:T(8,128)(2,1)S(1)} %shard_map.100.refs_1_.a_ref), channel_id=1, source_target_pairs={{0,16},{2,18},{4,20},{6,22},{8,24},{10,26},{12,28},{14,30},{16,0},... | collective-permute-start | bytes 294920 | tf_op jit(solution)/shard_map/ppermute | solution.py:276
  56.0 7.4 %collective-permute-start.19 = (bf16[192,256]{1,0:T(8,128)(2,1)S(1)}, bf16[192,256]{1,0:T(8,128)(2,1)S(1)}, u32[]{:S(2)}, u32[]{:S(2)}) collective-permute-start(bf16[192,256]{1,0:T(8,128)(2,1)S(1)} %get-tuple-element.120), channel_id=1, source_target_pairs={{0,24},{2,26},{4,28},{6,30},{8,16},{10,18},{12,20},{14,22},{16,8},... | collective-permute-start | bytes 294920 | tf_op jit(solution)/shard_map/ppermute | solution.py:276
  58.2 8.4 %collective-permute-start.20 = (bf16[192,256]{1,0:T(8,128)(2,1)S(1)}, bf16[192,256]{1,0:T(8,128)(2,1)S(1)}, u32[]{:S(2)}, u32[]{:S(2)}) collective-permute-start(bf16[192,256]{1,0:T(8,128)(2,1)S(1)} %get-tuple-element.121), channel_id=1, source_target_pairs={{0,16},{2,18},{4,20},{6,22},{8,24},{10,26},{12,28},{14,30},{16,0},... | collective-permute-start | bytes 294920 | tf_op jit(solution)/shard_map/ppermute | solution.py:276
  58.3 8.2 %collective-permute-start.21 = (bf16[192,256]{1,0:T(8,128)(2,1)S(1)}, bf16[192,256]{1,0:T(8,128)(2,1)S(1)}, u32[]{:S(2)}, u32[]{:S(2)}) collective-permute-start(bf16[192,256]{1,0:T(8,128)(2,1)S(1)} %get-tuple-element.122), channel_id=1, source_target_pairs={{0,8},{2,10},{4,12},{6,14},{8,0},{10,2},{12,4},{14,6},{16,24},{18,... | collective-permute-start | bytes 294920 | tf_op jit(solution)/shard_map/ppermute | solution.py:276
  60.5 6.1 %collective-permute-start.23 = (bf16[64,768]{1,0:T(8,128)(2,1)S(1)}, bf16[64,768]{1,0:T(8,128)(2,1)S(1)}, u32[]{:S(2)}, u32[]{:S(2)}) collective-permute-start(bf16[64,768]{1,0:T(8,128)(2,1)S(1)} %shard_map.105.refs_0_), channel_id=1, source_target_pairs={{0,4},{2,6},{4,0},{6,2},{8,12},{10,14},{12,8},{14,10},{16,20},{18,... | collective-permute-start | bytes 294920 | tf_op jit(solution)/shard_map/ppermute | solution.py:276
  61.9 5.9 %collective-permute-start.24 = (bf16[64,768]{1,0:T(8,128)(2,1)S(1)}, bf16[64,768]{1,0:T(8,128)(2,1)S(1)}, u32[]{:S(2)}, u32[]{:S(2)}) collective-permute-start(bf16[64,768]{1,0:T(8,128)(2,1)S(1)} %shard_map.105.refs_0_), channel_id=1, source_target_pairs={{0,2},{2,0},{4,6},{6,4},{8,10},{10,8},{12,14},{14,12},{16,18},{18,... | collective-permute-start | bytes 294920 | tf_op jit(solution)/shard_map/ppermute | solution.py:276
  66.6 1.4 %collective-permute-start.25 = (bf16[64,768]{1,0:T(8,128)(2,1)S(1)}, bf16[64,768]{1,0:T(8,128)(2,1)S(1)}, u32[]{:S(2)}, u32[]{:S(2)}) collective-permute-start(bf16[64,768]{1,0:T(8,128)(2,1)S(1)} %shard_map.107.refs_6_.refs_2_), channel_id=1, source_target_pairs={{0,2},{2,0},{4,6},{6,4},{8,10},{10,8},{12,14},{14,12},{16,18},{18,... | collective-permute-start | bytes 294920 | tf_op jit(solution)/shard_map/ppermute | solution.py:276

commit v20 on v19

--- a/solution.py
+++ b/solution.py
@@ -242,12 +242,12 @@
     refs[-1][...] = (a_ref[...].astype(F32) + b_ref[...].astype(F32)).astype(refs[-1].dtype)
 
 
-def unpack_kernel(slots, rows, dim, a_of, *refs):
+def unpack_kernel(slots, rows, dim, a_of, order, *refs):
     pieces, (a_ref, b_ref, _, kv_out, q_out, sum_out) = refs[:slots], refs[slots:]
     sum_out[...] = (a_ref[...].astype(F32) + b_ref[...].astype(F32)).astype(BF16)
     wide = 2 * dim
     me = a_of()
-    for slot, mask in enumerate(spread(slots)):
+    for slot, mask in enumerate(order):
         kv_out[pl.ds(me ^ mask, rows, stride=slots), :] = pieces[slot][0:wide, :].astype(F32).T
         q_out[me ^ mask] = pieces[slot][wide:, :].astype(F32)
 
@@ -374,6 +374,9 @@
     )(*halved, dq)
     returned = exchange(pieces)
 
+    masks = spread(slots)
+    order = [0] + sorted(masks[1:], key=lambda mask: (mask < slots // 2, mask))
+    returned = [returned[masks.index(mask)] for mask in order]
     arrived = call(token_kernel, [((8, 128), F32)], n_in=0, after=slots)(*returned)[0]
     if halves:
         for mask in z_masks[1:]:
@@ -386,7 +389,7 @@
     else:
         weight_grad = lax.psum(weight_terms[0].astype(F32), "seq")
     key_value_grad, query_grad, attention_out = call(
-        functools.partial(unpack_kernel, slots, rows, dim, a_of),
+        functools.partial(unpack_kernel, slots, rows, dim, a_of, order),
         [((rows * heads, wide), F32), ((heads, dim, rows), F32), ((rows, width), BF16)],
         n_in=slots + 2, after=1, micros=5,
     )(*returned, terms, terms_came, arrived)

time: 69.1 us -> 68.4 us (0.990)
  starting transfers between devices: 28.3 us -> 27.4 us
    ppermute x26, starting transfers between devices: 28.3 us -> 27.4 us  [swap(): return lax.ppermute(array, axis, [(i, i ^ mask) for i in range(size)])]
where the time goes in v20:
time: 68.4 us; the launch traced here: 68.2 us
  starting transfers between devices  27.4 us (40%)
  Pallas kernels  26.9 us (39%)
  waiting for transfers between devices  12.9 us (19%)
  between operations  0.92 us (1%)
    ppermute x26, starting transfers between devices, swap(): return lax.ppermute(array, axis, [(i, i ^ mask) for i in range(size)])  27.4 us
    ppermute x26, waiting for transfers between devices, swap(): return lax.ppermute(array, axis, [(i, i ^ mask) for i in range(size)])  12.9 us
    pallas_call x4, Pallas kernels, shards(): call(functools.partial(score_kernel, slots, rows, dim, step), [((block, b...  11.9 us
    pallas_call x4, Pallas kernels, shards(): call(functools.partial(back_kernel, slots, rows, dim, dq is None), [((wid...  8.65 us
    pallas_call x1, Pallas kernels, shards(): call(functools.partial(pack_kv_kernel, heads, rows, dim, a_of), [((rows,...  1.9 us
  transfers between devices with their start and end apart: 26, of which 9 were waited for; matrix products, arithmetic and copies ran while one was open for 0% of the time, Pallas kernels for 29%

profile of v20, /device:TPU:0, one launch (start us, length us, event | category | flops | bytes accessed | tf_op | source)
XLA Modules:
  0.0 68.2 jit_solution(7385045794185477795)
XLA Ops:
  0.7 1.9 %shard_map.84 = (bf16[256,128]{1,0:T(8,128)(2,1)}, bf16[256,128]{1,0:T(8,128)(2,1)}, bf16[256,128]{1,0:T(8,128)(2,1)}, bf16[256,128]{1,0:T(8,128)(2,1)}) custom-call(s32[2]{0:T(128)} %fill_ref.5, bf16[1024,128]{1,0:T(8,128)(2,1)} %bitcast.5), custom_call_target="tpu_custom_call" | custom-call | flops 1724999936 | tf_op jit(solution)/shard_map/pallas_call | solution.py:282
  2.6 5.0 %collective-permute-start = (bf16[256,128]{1,0:T(8,128)(2,1)}, bf16[256,128]{1,0:T(8,128)(2,1)S(1)}, u32[]{:S(2)}, u32[]{:S(2)}) collective-permute-start(bf16[256,128]{1,0:T(8,128)(2,1)} %get-tuple-element.66), channel_id=1, source_target_pairs={{0,24},{2,26},{4,28},{6,30},{8,16},{10,18},{12,20},{14,22},{16,8},... | collective-permute-start | bytes 196616 | tf_op jit(solution)/shard_map/ppermute | solution.py:276
  7.6 0.0 collective-permute-start.1
  7.6 0.6 collective-permute-start.2
  8.2 0.0 copy-start
  8.2 0.9 %shard_map.85 = (bf16[128,256]{1,0:T(8,128)(2,1)S(1)}, bf16[128,256]{1,0:T(8,128)(2,1)S(1)}, bf16[128,256]{1,0:T(8,128)(2,1)S(1)}, bf16[128,256]{1,0:T(8,128)(2,1)S(1)}) custom-call(s32[2]{0:T(128)S(1)} %copy-done.4, bf16[4,64,256]{2,1,0:T(8,128)(2,1)S(1)} %bitcast.4, bf16[4,64,768]{2,1,0:T(8,128)(2,1)S(1)} %copy-done.1, bf16[256,768]{1,0:T(8,128)(2,1)S(1)} %copy-done.2), custom_call_target="tpu_custom_call" | custom-call | flops 1150000000 | tf_op jit(solution)/shard_map/pallas_call | solution.py:287
  9.1 3.9 %collective-permute-start.3 = (bf16[128,256]{1,0:T(8,128)(2,1)S(1)}, bf16[128,256]{1,0:T(8,128)(2,1)S(1)}, u32[]{:S(2)}, u32[]{:S(2)}) collective-permute-start(bf16[128,256]{1,0:T(8,128)(2,1)S(1)} %get-tuple-element.70), channel_id=1, source_target_pairs={{0,24},{2,26},{4,28},{6,30},{8,16},{10,18},{12,20},{14,22},{16,8},... | collective-permute-start | bytes 196616 | tf_op jit(solution)/shard_map/ppermute | solution.py:276
  13.0 0.0 collective-permute-start.4
  13.0 0.0 collective-permute-done.refs_1_
  13.0 0.6 collective-permute-start.5
  13.6 2.4 %collective-permute-done.1.refs_2_ = bf16[256,128]{1,0:T(8,128)(2,1)S(1)} collective-permute-done((bf16[256,128]{1,0:T(8,128)(2,1)}, bf16[256,128]{1,0:T(8,128)(2,1)S(1)}, u32[]{:S(2)}, u32[]{:S(2)}) %collective-permute-start.1) | collective-permute-done | bytes 65568 | tf_op jit(solution)/shard_map/ppermute | solution.py:276
  16.0 0.0 collective-permute-done.2.refs_3_
  16.0 0.4 collective-permute-start.7
  16.4 0.0 collective-permute-start.6
  16.4 0.0 collective-permute-done.3.refs_1_
  16.4 2.6 %collective-permute-done.4.refs_2_ = bf16[128,256]{1,0:T(8,128)(2,1)S(1)} collective-permute-done((bf16[128,256]{1,0:T(8,128)(2,1)S(1)}, bf16[128,256]{1,0:T(8,128)(2,1)S(1)}, u32[]{:S(2)}, u32[]{:S(2)}) %collective-permute-start.4) | collective-permute-done | bytes 65568 | tf_op jit(solution)/shard_map/ppermute | solution.py:276
  19.1 0.0 collective-permute-done.5.refs_3_
  19.1 0.1 shard_map.87
  19.2 2.9 %shard_map.88 = (bf16[1024,1024]{1,0:T(8,128)(2,1)S(1)}, f32[1,1024]{1,0:T(1,128)S(1)}, f32[80,1024]{1,0:T(8,128)S(1)}, bf16[1024,128]{1,0:T(8,128)(2,1)S(1)}, bf16[64,1024]{1,0:T(8,128)(2,1)S(1)}) custom-call(bf16[1024,128]{1,0:T(8,128)(2,1)S(1)} %shard_map.86.pair_ref, bf16[256,1024]{1,0:T(8,128)(2,1)S(1)} %get-tuple-element.73.qa_ref, ...), custom_call_target="tpu_custom_call" | custom-call | flops 5750000128 | tf_op jit(solution)/shard_map/pallas_call | solution.py:313
  22.1 0.0 collective-permute-done.6.pair_ref
  22.1 2.9 %shard_map.89 = (bf16[1024,1024]{1,0:T(8,128)(2,1)S(1)}, f32[1,1024]{1,0:T(1,128)S(1)}, f32[80,1024]{1,0:T(8,128)S(1)}, bf16[1024,128]{1,0:T(8,128)(2,1)S(1)}, bf16[64,1024]{1,0:T(8,128)(2,1)S(1)}) custom-call(bf16[1024,128]{1,0:T(8,128)(2,1)S(1)} %collective-permute-done.6.pair_ref, bf16[256,1024]{1,0:T(8,128)(2,1)S(1)} %get-tuple-element.73.qa_ref, ...), custom_call_target="tpu_custom_call" | custom-call | flops 5750000128 | tf_op jit(solution)/shard_map/pallas_call | solution.py:313
  25.1 0.0 collective-permute-done.7.refs_0_
  25.1 0.1 collective-permute-start.8
  25.2 2.9 %shard_map.91 = (bf16[1024,1024]{1,0:T(8,128)(2,1)S(1)}, f32[1,1024]{1,0:T(1,128)S(1)}, f32[80,1024]{1,0:T(8,128)S(1)}, bf16[1024,128]{1,0:T(8,128)(2,1)S(1)}, bf16[64,1024]{1,0:T(8,128)(2,1)S(1)}) custom-call(bf16[1024,128]{1,0:T(8,128)(2,1)S(1)} %shard_map.90.pair_ref, bf16[256,1024]{1,0:T(8,128)(2,1)S(1)} %get-tuple-element.73.qa_ref, ...), custom_call_target="tpu_custom_call" | custom-call | flops 5750000128 | tf_op jit(solution)/shard_map/pallas_call | solution.py:313
  28.1 0.0 collective-permute-done.8.pair_ref
  28.1 3.1 %shard_map.92 = (bf16[1024,1024]{1,0:T(8,128)(2,1)S(1)}, f32[1,1024]{1,0:T(1,128)S(1)}, f32[80,1024]{1,0:T(8,128)S(1)}, bf16[1024,128]{1,0:T(8,128)(2,1)S(1)}, bf16[64,1024]{1,0:T(8,128)(2,1)S(1)}) custom-call(bf16[1024,128]{1,0:T(8,128)(2,1)S(1)} %collective-permute-done.8.pair_ref, bf16[256,1024]{1,0:T(8,128)(2,1)S(1)} %get-tuple-element.73.qa_ref, ...), custom_call_target="tpu_custom_call" | custom-call | flops 5750000128 | tf_op jit(solution)/shard_map/pallas_call | solution.py:313
  31.2 0.2 shard_map.93
  31.4 2.7 %collective-permute-start.9 = (bf16[64,256]{1,0:T(8,128)(2,1)S(1)}, bf16[64,256]{1,0:T(8,128)(2,1)S(1)}, u32[]{:S(2)}, u32[]{:S(2)}) collective-permute-start(bf16[64,256]{1,0:T(8,128)(2,1)S(1)} %get-tuple-element.104), channel_id=1, source_target_pairs={{0,24},{2,26},{4,28},{6,30},{8,16},{10,18},{12,20},{14,22},{16,8},... | collective-permute-start | bytes 98312 | tf_op jit(solution)/shard_map/ppermute | solution.py:276
  34.1 1.7 %collective-permute-start.11 = (bf16[64,256]{1,0:T(8,128)(2,1)S(1)}, bf16[64,256]{1,0:T(8,128)(2,1)S(1)}, u32[]{:S(2)}, u32[]{:S(2)}) collective-permute-start(bf16[64,256]{1,0:T(8,128)(2,1)S(1)} %get-tuple-element.106), channel_id=1, source_target_pairs={{0,8},{2,10},{4,12},{6,14},{8,0},{10,2},{12,4},{14,6},{16,24},{18,... | collective-permute-start | bytes 98312 | tf_op jit(solution)/shard_map/ppermute | solution.py:276
  35.9 2.2 %shard_map.94 = (bf16[128,1024]{1,0:T(8,128)(2,1)S(1)}, f32[64,1024]{1,0:T(8,128)S(1)}) custom-call(bf16[1024,1024]{1,0:T(8,128)(2,1)S(1)} %get-tuple-element.98.exp_ref, bf16[1024,128]{1,0:T(8,128)(2,1)S(1)} %get-tuple-element.99.v_ref, bf16[64,1024]{1,0:T(8,128)(2,1)S(1)} %get-tuple-element.100.kt_ref, bf16[64,1024]{1,0:T(8,128)(2,1)S(1)} %get-tuple-element.78.q_ref, ...), custom_call_target="tpu_custom_call" | custom-call | flops 2300000000 | tf_op jit(solution)/shard_map/pallas_call | solution.py:355
  38.0 0.9 %collective-permute-done.10.refs_2_ = bf16[64,256]{1,0:T(8,128)(2,1)S(1)} collective-permute-done((bf16[64,256]{1,0:T(8,128)(2,1)S(1)}, bf16[64,256]{1,0:T(8,128)(2,1)S(1)}, u32[]{:S(2)}, u32[]{:S(2)}) %collective-permute-start.10) | collective-permute-done | bytes 32800 | tf_op jit(solution)/shard_map/ppermute | solution.py:276
  38.9 0.0 collective-permute-done.11.refs_3_
  38.9 0.9 %shard_map.95 = (bf16[256,768]{1,0:T(8,128)(2,1)S(1)}, bf16[2,64,768]{2,1,0:T(8,128)(2,1)S(1)}, bf16[2,64,768]{2,1,0:T(8,128)(2,1)S(1)}) custom-call(s32[2]{0:T(128)S(1)} %copy-done.4, bf16[256,768]{1,0:T(8,128)(2,1)S(1)} %copy-done.2, bf16[4,64,768]{2,1,0:T(8,128)(2,1)S(1)} %copy-done.1, bf16[64,256]{1,0:T(8,128)(2,1)S(1)} %get-tuple-element.103.refs_0_, ...), custom_call_target="tpu_custom_call" | custom-call | flops 805000000 | tf_op jit(solution)/shard_map/pallas_call | solution.py:333
  39.9 0.1 collective-permute-start.12
  39.9 0.5 collective-permute-start.15
  40.4 1.5 %collective-permute-start.17 = (bf16[256,768]{1,0:T(8,128)(2,1)S(1)}, bf16[256,768]{1,0:T(8,128)(2,1)S(1)}, u32[]{:S(2)}, u32[]{:S(2)}) collective-permute-start(bf16[256,768]{1,0:T(8,128)(2,1)S(1)} %get-tuple-element.116.refs_4_), channel_id=1, source_target_pairs={{0,1},{1,0},{2,3},{3,2},{4,5},{5,4},{6,7},{7,6},{8,9},{9,8},{10,11... | collective-permute-start | bytes 1179656 | tf_op jit(solution)/shard_map/ppermute | solution.py:276
  42.0 1.6 %collective-permute-start.13 = (bf16[64,768]{1,0:T(8,128)(2,1)S(1)}, bf16[64,768]{1,0:T(8,128)(2,1)S(1)}, u32[]{:S(2)}, u32[]{:S(2)}) collective-permute-start(bf16[64,768]{1,0:T(8,128)(2,1)S(1)} %get-tuple-element.112), channel_id=1, source_target_pairs={{0,4},{2,6},{4,0},{6,2},{8,12},{10,14},{12,8},{14,10},{16,20},{18,... | collective-permute-start | bytes 294920 | tf_op jit(solution)/shard_map/ppermute | solution.py:276
  43.6 2.2 %shard_map.97 = (bf16[128,1024]{1,0:T(8,128)(2,1)S(1)}, f32[64,1024]{1,0:T(8,128)S(1)}) custom-call(bf16[1024,1024]{1,0:T(8,128)(2,1)S(1)} %get-tuple-element.94.exp_ref, bf16[1024,128]{1,0:T(8,128)(2,1)S(1)} %get-tuple-element.95.v_ref, bf16[64,1024]{1,0:T(8,128)(2,1)S(1)} %get-tuple-element.96.kt_ref, bf16[64,1024]{1,0:T(8,128)(2,1)S(1)} %get-tuple-element.78.q_ref, ...), custom_call_target="tpu_custom_call" | custom-call | flops 2300000000 | tf_op jit(solution)/shard_map/pallas_call | solution.py:355
  45.7 0.0 collective-permute-done.15.b_ref
  45.8 0.1 shard_map.101
  45.8 0.6 collective-permute-start.16
  46.4 0.3 collective-permute-done.13.b_ref
  46.7 0.9 %collective-permute-start.14 = (bf16[64,768]{1,0:T(8,128)(2,1)S(1)}, bf16[64,768]{1,0:T(8,128)(2,1)S(1)}, u32[]{:S(2)}, u32[]{:S(2)}) collective-permute-start(bf16[64,768]{1,0:T(8,128)(2,1)S(1)} %shard_map.98.refs_1_.a_ref), channel_id=1, source_target_pairs={{0,8},{2,10},{4,12},{6,14},{8,0},{10,2},{12,4},{14,6},{16,24},{18,... | collective-permute-start | bytes 294920 | tf_op jit(solution)/shard_map/ppermute | solution.py:276
  47.6 2.2 %shard_map.99 = (bf16[128,1024]{1,0:T(8,128)(2,1)S(1)}, f32[64,1024]{1,0:T(8,128)S(1)}) custom-call(bf16[1024,1024]{1,0:T(8,128)(2,1)S(1)} %get-tuple-element.90.exp_ref, bf16[1024,128]{1,0:T(8,128)(2,1)S(1)} %get-tuple-element.91.v_ref, bf16[64,1024]{1,0:T(8,128)(2,1)S(1)} %get-tuple-element.92.kt_ref, bf16[64,1024]{1,0:T(8,128)(2,1)S(1)} %get-tuple-element.78.q_ref, ...), custom_call_target="tpu_custom_call" | custom-call | flops 2300000000 | tf_op jit(solution)/shard_map/pallas_call | solution.py:355
  49.8 0.1 collective-permute-start.18
  49.9 1.5 %collective-permute-done.14.b_ref = bf16[64,768]{1,0:T(8,128)(2,1)S(1)} collective-permute-done((bf16[64,768]{1,0:T(8,128)(2,1)S(1)}, bf16[64,768]{1,0:T(8,128)(2,1)S(1)}, u32[]{:S(2)}, u32[]{:S(2)}) %collective-permute-start.14) | collective-permute-done | bytes 98336 | tf_op jit(solution)/shard_map/ppermute | solution.py:276
  51.4 2.1 %collective-permute-start.22 = (bf16[64,768]{1,0:T(8,128)(2,1)S(1)}, bf16[64,768]{1,0:T(8,128)(2,1)S(1)}, u32[]{:S(2)}, u32[]{:S(2)}) collective-permute-start(bf16[64,768]{1,0:T(8,128)(2,1)S(1)} %shard_map.100.refs_1_.a_ref), channel_id=1, source_target_pairs={{0,16},{2,18},{4,20},{6,22},{8,24},{10,26},{12,28},{14,30},{16,0},... | collective-permute-start | bytes 294920 | tf_op jit(solution)/shard_map/ppermute | solution.py:276
  53.5 0.1 collective-permute-done.16.refs_2_.came_ref
  53.6 2.2 %shard_map.102 = (bf16[128,1024]{1,0:T(8,128)(2,1)S(1)}, f32[64,1024]{1,0:T(8,128)S(1)}) custom-call(bf16[1024,1024]{1,0:T(8,128)(2,1)S(1)} %get-tuple-element.75.exp_ref, bf16[1024,128]{1,0:T(8,128)(2,1)S(1)} %get-tuple-element.76.v_ref, bf16[64,1024]{1,0:T(8,128)(2,1)S(1)} %get-tuple-element.77.kt_ref, bf16[64,1024]{1,0:T(8,128)(2,1)S(1)} %get-tuple-element.78.q_ref, ...), custom_call_target="tpu_custom_call" | custom-call | flops 2300000000 | tf_op jit(solution)/shard_map/pallas_call | solution.py:355
  55.8 0.1 shard_map.103.kept_ref
  55.9 0.1 shard_map.104
  56.0 2.1 %collective-permute-start.19 = (bf16[192,256]{1,0:T(8,128)(2,1)S(1)}, bf16[192,256]{1,0:T(8,128)(2,1)S(1)}, u32[]{:S(2)}, u32[]{:S(2)}) collective-permute-start(bf16[192,256]{1,0:T(8,128)(2,1)S(1)} %get-tuple-element.120), channel_id=1, source_target_pairs={{0,16},{2,18},{4,20},{6,22},{8,24},{10,26},{12,28},{14,30},{16,0},... | collective-permute-start | bytes 294920 | tf_op jit(solution)/shard_map/ppermute | solution.py:276
  58.1 1.2 %collective-permute-start.20 = (bf16[192,256]{1,0:T(8,128)(2,1)S(1)}, bf16[192,256]{1,0:T(8,128)(2,1)S(1)}, u32[]{:S(2)}, u32[]{:S(2)}) collective-permute-start(bf16[192,256]{1,0:T(8,128)(2,1)S(1)} %get-tuple-element.121), channel_id=1, source_target_pairs={{0,24},{2,26},{4,28},{6,30},{8,16},{10,18},{12,20},{14,22},{16,8},... | collective-permute-start | bytes 294920 | tf_op jit(solution)/shard_map/ppermute | solution.py:276
  59.2 0.3 collective-permute-start.21
  59.5 0.0 collective-permute-done.22.b_ref
  59.6 1.5 %collective-permute-start.23 = (bf16[64,768]{1,0:T(8,128)(2,1)S(1)}, bf16[64,768]{1,0:T(8,128)(2,1)S(1)}, u32[]{:S(2)}, u32[]{:S(2)}) collective-permute-start(bf16[64,768]{1,0:T(8,128)(2,1)S(1)} %shard_map.105.refs_0_), channel_id=1, source_target_pairs={{0,4},{2,6},{4,0},{6,2},{8,12},{10,14},{12,8},{14,10},{16,20},{18,... | collective-permute-start | bytes 294920 | tf_op jit(solution)/shard_map/ppermute | solution.py:276
  61.0 0.0 collective-permute-start.24
  61.0 4.5 %collective-permute-done.19.refs_1_ = bf16[192,256]{1,0:T(8,128)(2,1)S(1)} collective-permute-done((bf16[192,256]{1,0:T(8,128)(2,1)S(1)}, bf16[192,256]{1,0:T(8,128)(2,1)S(1)}, u32[]{:S(2)}, u32[]{:S(2)}) %collective-permute-start.19) | collective-permute-done | bytes 98336 | tf_op jit(solution)/shard_map/ppermute | solution.py:276
  65.6 0.3 collective-permute-done.21.refs_3_
  65.9 0.1 collective-permute-start.25
  66.0 1.1 %shard_map.108 = (f32[1024,128]{1,0:T(8,128)}, f32[4,64,256]{2,1,0:T(8,128)}, bf16[256,768]{1,0:T(8,128)(2,1)}) custom-call(bf16[192,256]{1,0:T(8,128)(2,1)S(1)} %get-tuple-element.119.refs_0_, bf16[192,256]{1,0:T(8,128)(2,1)S(1)} %collective-permute-done.19.refs_1_, bf16[192,256]{1,0:T(8,128)(2,1)S(1)} %collective-permute-done.20.refs_2_, ...), custom_call_target="tpu_custom_call" | custom-call | flops 5750000128 | tf_op jit(solution)/shard_map/pallas_call | solution.py:391
  67.1 0.0 collective-permute-done.24.refs_1_
  67.1 0.2 collective-permute-done.25.refs_3_
  67.3 0.9 %shard_map.109 = f32[4,64,768]{2,1,0:T(8,128)} custom-call(bf16[64,768]{1,0:T(8,128)(2,1)S(1)} %shard_map.105.refs_0_, bf16[64,768]{1,0:T(8,128)(2,1)S(1)} %collective-permute-done.24.refs_1_, bf16[64,768]{1,0:T(8,128)(2,1)S(1)} %shard_map.107.refs_6_.refs_2_, bf16[64,768]{1,0:T(8,128)(2,1)S(1)} %collective-permute-done.25.refs_3_), custom_call_target="tpu_custom_call" | custom-call | flops 575000000 | tf_op jit(solution)/shard_map/pallas_call | solution.py:385
  (24 shorter events, 0.2 us)
Async XLA Ops:
  0.6 7.6 %copy-start.1 = (bf16[4,64,768]{2,1,0:T(8,128)(2,1)S(1)}, bf16[4,64,768]{2,1,0:T(8,128)(2,1)}, u32[]{:S(2)}) copy-start(bf16[4,64,768]{2,1,0:T(8,128)(2,1)} %w_ref.3) | copy-start | bytes 1179652
  0.6 7.6 %copy-start.2 = (bf16[256,768]{1,0:T(8,128)(2,1)S(1)}, bf16[256,768]{1,0:T(8,128)(2,1)}, u32[]{:S(2)}) copy-start(bf16[256,768]{1,0:T(8,128)(2,1)} %go_ref.3) | copy-start | bytes 1179652
  0.7 7.5 %copy-start.3 = (bf16[256,4,64]{0,2,1:T(8,128)(2,1)S(1)}, bf16[256,4,64]{0,2,1:T(8,128)(2,1)}, u32[]{:S(2)}) copy-start(bf16[256,4,64]{0,2,1:T(8,128)(2,1)} %param.5) | copy-start | bytes 393220
  0.7 7.5 %copy-start.4 = (s32[2]{0:T(128)S(1)}, s32[2]{0:T(128)}, u32[]{:S(2)}) copy-start(s32[2]{0:T(128)} %fill_ref.5) | copy-start | bytes 28
  2.6 10.4 %collective-permute-start = (bf16[256,128]{1,0:T(8,128)(2,1)}, bf16[256,128]{1,0:T(8,128)(2,1)S(1)}, u32[]{:S(2)}, u32[]{:S(2)}) collective-permute-start(bf16[256,128]{1,0:T(8,128)(2,1)} %get-tuple-element.66), channel_id=1, source_target_pairs={{0,24},{2,26},{4,28},{6,30},{8,16},{10,18},{12,20},{14,22},{16,8},... | collective-permute-start | bytes 196616 | tf_op jit(solution)/shard_map/ppermute | solution.py:276
  7.6 8.4 %collective-permute-start.1 = (bf16[256,128]{1,0:T(8,128)(2,1)}, bf16[256,128]{1,0:T(8,128)(2,1)S(1)}, u32[]{:S(2)}, u32[]{:S(2)}) collective-permute-start(bf16[256,128]{1,0:T(8,128)(2,1)} %get-tuple-element.67), channel_id=1, source_target_pairs={{0,16},{2,18},{4,20},{6,22},{8,24},{10,26},{12,28},{14,30},{16,0},... | collective-permute-start | bytes 196616 | tf_op jit(solution)/shard_map/ppermute | solution.py:276
  7.6 8.4 %collective-permute-start.2 = (bf16[256,128]{1,0:T(8,128)(2,1)}, bf16[256,128]{1,0:T(8,128)(2,1)S(1)}, u32[]{:S(2)}, u32[]{:S(2)}) collective-permute-start(bf16[256,128]{1,0:T(8,128)(2,1)} %get-tuple-element.68), channel_id=1, source_target_pairs={{0,8},{2,10},{4,12},{6,14},{8,0},{10,2},{12,4},{14,6},{16,24},{18,... | collective-permute-start | bytes 196616 | tf_op jit(solution)/shard_map/ppermute | solution.py:276
  8.2 7.8 %copy-start = (bf16[256,128]{1,0:T(8,128)(2,1)S(1)}, bf16[256,128]{1,0:T(8,128)(2,1)}, u32[]{:S(2)}) copy-start(bf16[256,128]{1,0:T(8,128)(2,1)} %get-tuple-element.65.refs_0_) | copy-start | bytes 196612
  9.1 7.3 %collective-permute-start.3 = (bf16[128,256]{1,0:T(8,128)(2,1)S(1)}, bf16[128,256]{1,0:T(8,128)(2,1)S(1)}, u32[]{:S(2)}, u32[]{:S(2)}) collective-permute-start(bf16[128,256]{1,0:T(8,128)(2,1)S(1)} %get-tuple-element.70), channel_id=1, source_target_pairs={{0,24},{2,26},{4,28},{6,30},{8,16},{10,18},{12,20},{14,22},{16,8},... | collective-permute-start | bytes 196616 | tf_op jit(solution)/shard_map/ppermute | solution.py:276
  13.0 6.1 %collective-permute-start.4 = (bf16[128,256]{1,0:T(8,128)(2,1)S(1)}, bf16[128,256]{1,0:T(8,128)(2,1)S(1)}, u32[]{:S(2)}, u32[]{:S(2)}) collective-permute-start(bf16[128,256]{1,0:T(8,128)(2,1)S(1)} %get-tuple-element.71), channel_id=1, source_target_pairs={{0,16},{2,18},{4,20},{6,22},{8,24},{10,26},{12,28},{14,30},{16,0},... | collective-permute-start | bytes 196616 | tf_op jit(solution)/shard_map/ppermute | solution.py:276
  13.0 6.1 %collective-permute-start.5 = (bf16[128,256]{1,0:T(8,128)(2,1)S(1)}, bf16[128,256]{1,0:T(8,128)(2,1)S(1)}, u32[]{:S(2)}, u32[]{:S(2)}) collective-permute-start(bf16[128,256]{1,0:T(8,128)(2,1)S(1)} %get-tuple-element.72), channel_id=1, source_target_pairs={{0,8},{2,10},{4,12},{6,14},{8,0},{10,2},{12,4},{14,6},{16,24},{18,... | collective-permute-start | bytes 196616 | tf_op jit(solution)/shard_map/ppermute | solution.py:276
  16.0 9.0 %collective-permute-start.7 = (bf16[1024,128]{1,0:T(8,128)(2,1)S(1)}, bf16[1024,128]{1,0:T(8,128)(2,1)S(1)}, u32[]{:S(2)}, u32[]{:S(2)}) collective-permute-start(bf16[1024,128]{1,0:T(8,128)(2,1)S(1)} %shard_map.86.pair_ref), channel_id=1, source_target_pairs={{0,4},{2,6},{4,0},{6,2},{8,12},{10,14},{12,8},{14,10},{16,20},{18,... | collective-permute-start | bytes 786440 | tf_op jit(solution)/shard_map/ppermute | solution.py:276
  16.4 5.7 %collective-permute-start.6 = (bf16[1024,128]{1,0:T(8,128)(2,1)S(1)}, bf16[1024,128]{1,0:T(8,128)(2,1)S(1)}, u32[]{:S(2)}, u32[]{:S(2)}) collective-permute-start(bf16[1024,128]{1,0:T(8,128)(2,1)S(1)} %shard_map.86.pair_ref), channel_id=1, source_target_pairs={{0,2},{2,0},{4,6},{6,4},{8,10},{10,8},{12,14},{14,12},{16,18},{18,... | collective-permute-start | bytes 786440 | tf_op jit(solution)/shard_map/ppermute | solution.py:276
  25.1 3.0 %collective-permute-start.8 = (bf16[1024,128]{1,0:T(8,128)(2,1)S(1)}, bf16[1024,128]{1,0:T(8,128)(2,1)S(1)}, u32[]{:S(2)}, u32[]{:S(2)}) collective-permute-start(bf16[1024,128]{1,0:T(8,128)(2,1)S(1)} %shard_map.90.pair_ref), channel_id=1, source_target_pairs={{0,2},{2,0},{4,6},{6,4},{8,10},{10,8},{12,14},{14,12},{16,18},{18,... | collective-permute-start | bytes 786440 | tf_op jit(solution)/shard_map/ppermute | solution.py:276
  31.4 6.6 %collective-permute-start.9 = (bf16[64,256]{1,0:T(8,128)(2,1)S(1)}, bf16[64,256]{1,0:T(8,128)(2,1)S(1)}, u32[]{:S(2)}, u32[]{:S(2)}) collective-permute-start(bf16[64,256]{1,0:T(8,128)(2,1)S(1)} %get-tuple-element.104), channel_id=1, source_target_pairs={{0,24},{2,26},{4,28},{6,30},{8,16},{10,18},{12,20},{14,22},{16,8},... | collective-permute-start | bytes 98312 | tf_op jit(solution)/shard_map/ppermute | solution.py:276
  34.1 4.8 %collective-permute-start.10 = (bf16[64,256]{1,0:T(8,128)(2,1)S(1)}, bf16[64,256]{1,0:T(8,128)(2,1)S(1)}, u32[]{:S(2)}, u32[]{:S(2)}) collective-permute-start(bf16[64,256]{1,0:T(8,128)(2,1)S(1)} %get-tuple-element.105), channel_id=1, source_target_pairs={{0,16},{2,18},{4,20},{6,22},{8,24},{10,26},{12,28},{14,30},{16,0},... | collective-permute-start | bytes 98312 | tf_op jit(solution)/shard_map/ppermute | solution.py:276
  34.1 4.8 %collective-permute-start.11 = (bf16[64,256]{1,0:T(8,128)(2,1)S(1)}, bf16[64,256]{1,0:T(8,128)(2,1)S(1)}, u32[]{:S(2)}, u32[]{:S(2)}) collective-permute-start(bf16[64,256]{1,0:T(8,128)(2,1)S(1)} %get-tuple-element.106), channel_id=1, source_target_pairs={{0,8},{2,10},{4,12},{6,14},{8,0},{10,2},{12,4},{14,6},{16,24},{18,... | collective-permute-start | bytes 98312 | tf_op jit(solution)/shard_map/ppermute | solution.py:276
  39.9 2.1 %collective-permute-start.12 = (bf16[2,64,768]{2,1,0:T(8,128)(2,1)S(1)}, bf16[2,64,768]{2,1,0:T(8,128)(2,1)S(1)}, u32[]{:S(2)}, u32[]{:S(2)}) collective-permute-start(bf16[2,64,768]{2,1,0:T(8,128)(2,1)S(1)} %get-tuple-element.109), channel_id=1, source_target_pairs={{0,2},{2,0},{4,6},{6,4},{8,10},{10,8},{12,14},{14,12},{16,18},{18,... | collective-permute-start | bytes 589832 | tf_op jit(solution)/shard_map/ppermute | solution.py:276
  39.9 5.8 %collective-permute-start.15 = (bf16[128,1024]{1,0:T(8,128)(2,1)S(1)}, bf16[128,1024]{1,0:T(8,128)(2,1)S(1)}, u32[]{:S(2)}, u32[]{:S(2)}) collective-permute-start(bf16[128,1024]{1,0:T(8,128)(2,1)S(1)} %get-tuple-element.107.refs_4_), channel_id=1, source_target_pairs={{0,2},{2,0},{4,6},{6,4},{8,10},{10,8},{12,14},{14,12},{16,18},{18,... | collective-permute-start | bytes 786440 | tf_op jit(solution)/shard_map/ppermute | solution.py:276
  40.4 13.1 %collective-permute-start.17 = (bf16[256,768]{1,0:T(8,128)(2,1)S(1)}, bf16[256,768]{1,0:T(8,128)(2,1)S(1)}, u32[]{:S(2)}, u32[]{:S(2)}) collective-permute-start(bf16[256,768]{1,0:T(8,128)(2,1)S(1)} %get-tuple-element.116.refs_4_), channel_id=1, source_target_pairs={{0,1},{1,0},{2,3},{3,2},{4,5},{5,4},{6,7},{7,6},{8,9},{9,8},{10,11... | collective-permute-start | bytes 1179656 | tf_op jit(solution)/shard_map/ppermute | solution.py:276
  42.0 4.7 %collective-permute-start.13 = (bf16[64,768]{1,0:T(8,128)(2,1)S(1)}, bf16[64,768]{1,0:T(8,128)(2,1)S(1)}, u32[]{:S(2)}, u32[]{:S(2)}) collective-permute-start(bf16[64,768]{1,0:T(8,128)(2,1)S(1)} %get-tuple-element.112), channel_id=1, source_target_pairs={{0,4},{2,6},{4,0},{6,2},{8,12},{10,14},{12,8},{14,10},{16,20},{18,... | collective-permute-start | bytes 294920 | tf_op jit(solution)/shard_map/ppermute | solution.py:276
  45.8 7.8 %collective-permute-start.16 = (bf16[128,1024]{1,0:T(8,128)(2,1)S(1)}, bf16[128,1024]{1,0:T(8,128)(2,1)S(1)}, u32[]{:S(2)}, u32[]{:S(2)}) collective-permute-start(bf16[128,1024]{1,0:T(8,128)(2,1)S(1)} %shard_map.101), channel_id=1, source_target_pairs={{0,4},{2,6},{4,0},{6,2},{8,12},{10,14},{12,8},{14,10},{16,20},{18,... | collective-permute-start | bytes 786440 | tf_op jit(solution)/shard_map/ppermute | solution.py:276
  46.7 4.7 %collective-permute-start.14 = (bf16[64,768]{1,0:T(8,128)(2,1)S(1)}, bf16[64,768]{1,0:T(8,128)(2,1)S(1)}, u32[]{:S(2)}, u32[]{:S(2)}) collective-permute-start(bf16[64,768]{1,0:T(8,128)(2,1)S(1)} %shard_map.98.refs_1_.a_ref), channel_id=1, source_target_pairs={{0,8},{2,10},{4,12},{6,14},{8,0},{10,2},{12,4},{14,6},{16,24},{18,... | collective-permute-start | bytes 294920 | tf_op jit(solution)/shard_map/ppermute | solution.py:276
  49.8 6.0 %collective-permute-start.18 = (bf16[128,1024]{1,0:T(8,128)(2,1)S(1)}, bf16[128,1024]{1,0:T(8,128)(2,1)S(1)}, u32[]{:S(2)}, u32[]{:S(2)}) collective-permute-start(bf16[128,1024]{1,0:T(8,128)(2,1)S(1)} %get-tuple-element.115.refs_0_), channel_id=1, source_target_pairs={{0,2},{2,0},{4,6},{6,4},{8,10},{10,8},{12,14},{14,12},{16,18},{18,... | collective-permute-start | bytes 786440 | tf_op jit(solution)/shard_map/ppermute | solution.py:276
  51.4 8.1 %collective-permute-start.22 = (bf16[64,768]{1,0:T(8,128)(2,1)S(1)}, bf16[64,768]{1,0:T(8,128)(2,1)S(1)}, u32[]{:S(2)}, u32[]{:S(2)}) collective-permute-start(bf16[64,768]{1,0:T(8,128)(2,1)S(1)} %shard_map.100.refs_1_.a_ref), channel_id=1, source_target_pairs={{0,16},{2,18},{4,20},{6,22},{8,24},{10,26},{12,28},{14,30},{16,0},... | collective-permute-start | bytes 294920 | tf_op jit(solution)/shard_map/ppermute | solution.py:276
  56.0 9.6 %collective-permute-start.19 = (bf16[192,256]{1,0:T(8,128)(2,1)S(1)}, bf16[192,256]{1,0:T(8,128)(2,1)S(1)}, u32[]{:S(2)}, u32[]{:S(2)}) collective-permute-start(bf16[192,256]{1,0:T(8,128)(2,1)S(1)} %get-tuple-element.120), channel_id=1, source_target_pairs={{0,16},{2,18},{4,20},{6,22},{8,24},{10,26},{12,28},{14,30},{16,0},... | collective-permute-start | bytes 294920 | tf_op jit(solution)/shard_map/ppermute | solution.py:276
  58.1 7.5 %collective-permute-start.20 = (bf16[192,256]{1,0:T(8,128)(2,1)S(1)}, bf16[192,256]{1,0:T(8,128)(2,1)S(1)}, u32[]{:S(2)}, u32[]{:S(2)}) collective-permute-start(bf16[192,256]{1,0:T(8,128)(2,1)S(1)} %get-tuple-element.121), channel_id=1, source_target_pairs={{0,24},{2,26},{4,28},{6,30},{8,16},{10,18},{12,20},{14,22},{16,8},... | collective-permute-start | bytes 294920 | tf_op jit(solution)/shard_map/ppermute | solution.py:276
  59.2 6.6 %collective-permute-start.21 = (bf16[192,256]{1,0:T(8,128)(2,1)S(1)}, bf16[192,256]{1,0:T(8,128)(2,1)S(1)}, u32[]{:S(2)}, u32[]{:S(2)}) collective-permute-start(bf16[192,256]{1,0:T(8,128)(2,1)S(1)} %get-tuple-element.122), channel_id=1, source_target_pairs={{0,8},{2,10},{4,12},{6,14},{8,0},{10,2},{12,4},{14,6},{16,24},{18,... | collective-permute-start | bytes 294920 | tf_op jit(solution)/shard_map/ppermute | solution.py:276
  59.6 6.3 %collective-permute-start.23 = (bf16[64,768]{1,0:T(8,128)(2,1)S(1)}, bf16[64,768]{1,0:T(8,128)(2,1)S(1)}, u32[]{:S(2)}, u32[]{:S(2)}) collective-permute-start(bf16[64,768]{1,0:T(8,128)(2,1)S(1)} %shard_map.105.refs_0_), channel_id=1, source_target_pairs={{0,4},{2,6},{4,0},{6,2},{8,12},{10,14},{12,8},{14,10},{16,20},{18,... | collective-permute-start | bytes 294920 | tf_op jit(solution)/shard_map/ppermute | solution.py:276
  61.0 6.1 %collective-permute-start.24 = (bf16[64,768]{1,0:T(8,128)(2,1)S(1)}, bf16[64,768]{1,0:T(8,128)(2,1)S(1)}, u32[]{:S(2)}, u32[]{:S(2)}) collective-permute-start(bf16[64,768]{1,0:T(8,128)(2,1)S(1)} %shard_map.105.refs_0_), channel_id=1, source_target_pairs={{0,2},{2,0},{4,6},{6,4},{8,10},{10,8},{12,14},{14,12},{16,18},{18,... | collective-permute-start | bytes 294920 | tf_op jit(solution)/shard_map/ppermute | solution.py:276
  65.9 1.4 %collective-permute-start.25 = (bf16[64,768]{1,0:T(8,128)(2,1)S(1)}, bf16[64,768]{1,0:T(8,128)(2,1)S(1)}, u32[]{:S(2)}, u32[]{:S(2)}) collective-permute-start(bf16[64,768]{1,0:T(8,128)(2,1)S(1)} %shard_map.107.refs_6_.refs_2_), channel_id=1, source_target_pairs={{0,2},{2,0},{4,6},{6,4},{8,10},{10,8},{12,14},{14,12},{16,18},{18,... | collective-permute-start | bytes 294920 | tf_op jit(solution)/shard_map/ppermute | solution.py:276

commit v21 on v20

--- a/solution.py
+++ b/solution.py
@@ -88,17 +88,17 @@
         out_ref[index * rows : (index + 1) * rows, :] = refs[index][...]
 
 
-def join_q_kernel(slots, rows, dim, *refs):
+def join_q_kernel(slots, rows, dim, places, *refs):
     pieces, (qa_ref, q_ref, g_ref, norm_ref) = refs[:slots], refs[slots:]
     wide = 2 * dim
     row = lax.broadcasted_iota(jnp.int32, (dim, slots * rows), 0)
     qa_ref[wide : wide + dim, :] = jnp.zeros((dim, slots * rows), BF16)
     qa_ref[wide + dim :, :] = jnp.where(row == 0, 1.0, 0.0).astype(BF16)
-    for slot in range(slots):
+    for piece, slot in zip(pieces, places):
         here = slice(slot * rows, (slot + 1) * rows)
-        queries = pieces[slot][0:dim, :]
+        queries = piece[0:dim, :]
         q_ref[:, here] = queries
-        g_ref[:, here] = pieces[slot][dim:, :]
+        g_ref[:, here] = piece[dim:, :]
         scaled = queries.astype(F32) * LOG2_E
         high = scaled.astype(BF16)
         qa_ref[0:dim, here] = high
@@ -294,10 +294,11 @@
         functools.partial(join_kernel, slots), [((block, wide), BF16)], n_in=slots, after=1,
     )(*kv_mine, qg_send[0])[0]
 
+    places = [0] + sorted(range(1, slots), key=lambda slot: (spread(slots)[slot] < slots // 2, spread(slots)[slot]))
     qa, q_all, grads, q_norm = call(
-        functools.partial(join_q_kernel, slots, rows, dim),
+        functools.partial(join_q_kernel, slots, rows, dim, places),
         [((2 * wide, block), BF16), ((dim, block), BF16), ((dim, block), BF16), ((1, block), F32)], n_in=slots,
-    )(*qg_mine)
+    )(*[qg_mine[slot] for slot in places])
     step = min(block, 512)
     scored, blocks = {}, {0: own}
     bit = columns // 2

time: 68.4 us -> 67.8 us (level)
  waiting for transfers between devices: 12.9 us -> 11.8 us
    ppermute x26, waiting for transfers between devices: 12.9 us -> 11.8 us  [swap(): return lax.ppermute(array, axis, [(i, i ^ mask) for i in range(size)])]
  transfers between devices with their start and end apart: 26 -> 26, of which waited for: 9 -> 10; matrix products, arithmetic and copies ran while one was open for 0% -> 0% of each run, Pallas kernels for 29% -> 29%
where the time goes in v21:
time: 67.8 us; the launch traced here: 67.6 us
  starting transfers between devices  27.9 us (41%)
  Pallas kernels  26.9 us (40%)
  waiting for transfers between devices  11.8 us (17%)
  between operations  0.92 us (1%)
    ppermute x26, starting transfers between devices, swap(): return lax.ppermute(array, axis, [(i, i ^ mask) for i in range(size)])  27.9 us
    pallas_call x4, Pallas kernels, shards(): call(functools.partial(score_kernel, slots, rows, dim, step), [((block, b...  11.9 us
    ppermute x26, waiting for transfers between devices, swap(): return lax.ppermute(array, axis, [(i, i ^ mask) for i in range(size)])  11.8 us
    pallas_call x4, Pallas kernels, shards(): call(functools.partial(back_kernel, slots, rows, dim, dq is None), [((wid...  8.66 us
    pallas_call x1, Pallas kernels, shards(): call(functools.partial(pack_kv_kernel, heads, rows, dim, a_of), [((rows,...  1.9 us
  transfers between devices with their start and end apart: 26, of which 10 were waited for; matrix products, arithmetic and copies ran while one was open for 0% of the time, Pallas kernels for 29%

profile of v21, /device:TPU:0, one launch (start us, length us, event | category | flops | bytes accessed | tf_op | source)
XLA Modules:
  0.0 67.6 jit_solution(17240041939931210726)
XLA Ops:
  0.7 1.9 %shard_map.84 = (bf16[256,128]{1,0:T(8,128)(2,1)}, bf16[256,128]{1,0:T(8,128)(2,1)}, bf16[256,128]{1,0:T(8,128)(2,1)}, bf16[256,128]{1,0:T(8,128)(2,1)}) custom-call(s32[2]{0:T(128)} %fill_ref.5, bf16[1024,128]{1,0:T(8,128)(2,1)} %bitcast.5), custom_call_target="tpu_custom_call" | custom-call | flops 1724999936 | tf_op jit(solution)/shard_map/pallas_call | solution.py:282
  2.6 5.0 %collective-permute-start = (bf16[256,128]{1,0:T(8,128)(2,1)}, bf16[256,128]{1,0:T(8,128)(2,1)S(1)}, u32[]{:S(2)}, u32[]{:S(2)}) collective-permute-start(bf16[256,128]{1,0:T(8,128)(2,1)} %get-tuple-element.66), channel_id=1, source_target_pairs={{0,24},{2,26},{4,28},{6,30},{8,16},{10,18},{12,20},{14,22},{16,8},... | collective-permute-start | bytes 196616 | tf_op jit(solution)/shard_map/ppermute | solution.py:276
  7.6 0.0 collective-permute-start.1
  7.6 0.6 collective-permute-start.2
  8.2 0.0 copy-start
  8.2 0.9 %shard_map.85 = (bf16[128,256]{1,0:T(8,128)(2,1)S(1)}, bf16[128,256]{1,0:T(8,128)(2,1)S(1)}, bf16[128,256]{1,0:T(8,128)(2,1)S(1)}, bf16[128,256]{1,0:T(8,128)(2,1)S(1)}) custom-call(s32[2]{0:T(128)S(1)} %copy-done.4, bf16[4,64,256]{2,1,0:T(8,128)(2,1)S(1)} %bitcast.4, bf16[4,64,768]{2,1,0:T(8,128)(2,1)S(1)} %copy-done.1, bf16[256,768]{1,0:T(8,128)(2,1)S(1)} %copy-done.2), custom_call_target="tpu_custom_call" | custom-call | flops 1150000000 | tf_op jit(solution)/shard_map/pallas_call | solution.py:287
  9.1 2.4 %collective-permute-start.3 = (bf16[128,256]{1,0:T(8,128)(2,1)S(1)}, bf16[128,256]{1,0:T(8,128)(2,1)S(1)}, u32[]{:S(2)}, u32[]{:S(2)}) collective-permute-start(bf16[128,256]{1,0:T(8,128)(2,1)S(1)} %get-tuple-element.70), channel_id=1, source_target_pairs={{0,16},{2,18},{4,20},{6,22},{8,24},{10,26},{12,28},{14,30},{16,0},... | collective-permute-start | bytes 196616 | tf_op jit(solution)/shard_map/ppermute | solution.py:276
  11.5 1.5 %collective-permute-start.4 = (bf16[128,256]{1,0:T(8,128)(2,1)S(1)}, bf16[128,256]{1,0:T(8,128)(2,1)S(1)}, u32[]{:S(2)}, u32[]{:S(2)}) collective-permute-start(bf16[128,256]{1,0:T(8,128)(2,1)S(1)} %get-tuple-element.71), channel_id=1, source_target_pairs={{0,24},{2,26},{4,28},{6,30},{8,16},{10,18},{12,20},{14,22},{16,8},... | collective-permute-start | bytes 196616 | tf_op jit(solution)/shard_map/ppermute | solution.py:276
  13.1 0.5 collective-permute-start.5
  13.5 1.1 %collective-permute-done.1.refs_2_ = bf16[256,128]{1,0:T(8,128)(2,1)S(1)} collective-permute-done((bf16[256,128]{1,0:T(8,128)(2,1)}, bf16[256,128]{1,0:T(8,128)(2,1)S(1)}, u32[]{:S(2)}, u32[]{:S(2)}) %collective-permute-start.1) | collective-permute-done | bytes 65568 | tf_op jit(solution)/shard_map/ppermute | solution.py:276
  14.6 1.4 %collective-permute-start.7 = (bf16[1024,128]{1,0:T(8,128)(2,1)S(1)}, bf16[1024,128]{1,0:T(8,128)(2,1)S(1)}, u32[]{:S(2)}, u32[]{:S(2)}) collective-permute-start(bf16[1024,128]{1,0:T(8,128)(2,1)S(1)} %shard_map.86.pair_ref), channel_id=1, source_target_pairs={{0,4},{2,6},{4,0},{6,2},{8,12},{10,14},{12,8},{14,10},{16,20},{18,... | collective-permute-start | bytes 786440 | tf_op jit(solution)/shard_map/ppermute | solution.py:276
  16.0 0.0 collective-permute-start.6
  16.0 2.1 %collective-permute-done.3.refs_1_ = bf16[128,256]{1,0:T(8,128)(2,1)S(1)} collective-permute-done((bf16[128,256]{1,0:T(8,128)(2,1)S(1)}, bf16[128,256]{1,0:T(8,128)(2,1)S(1)}, u32[]{:S(2)}, u32[]{:S(2)}) %collective-permute-start.3) | collective-permute-done | bytes 65568 | tf_op jit(solution)/shard_map/ppermute | solution.py:276
  18.1 0.0 collective-permute-done.4.refs_2_
  18.1 0.3 collective-permute-done.5.refs_3_
  18.4 0.1 shard_map.87
  18.5 2.9 %shard_map.88 = (bf16[1024,1024]{1,0:T(8,128)(2,1)S(1)}, f32[1,1024]{1,0:T(1,128)S(1)}, f32[80,1024]{1,0:T(8,128)S(1)}, bf16[1024,128]{1,0:T(8,128)(2,1)S(1)}, bf16[64,1024]{1,0:T(8,128)(2,1)S(1)}) custom-call(bf16[1024,128]{1,0:T(8,128)(2,1)S(1)} %shard_map.86.pair_ref, bf16[256,1024]{1,0:T(8,128)(2,1)S(1)} %get-tuple-element.73.qa_ref, ...), custom_call_target="tpu_custom_call" | custom-call | flops 5750000128 | tf_op jit(solution)/shard_map/pallas_call | solution.py:314
  21.5 0.0 collective-permute-done.6.pair_ref
  21.5 2.9 %shard_map.89 = (bf16[1024,1024]{1,0:T(8,128)(2,1)S(1)}, f32[1,1024]{1,0:T(1,128)S(1)}, f32[80,1024]{1,0:T(8,128)S(1)}, bf16[1024,128]{1,0:T(8,128)(2,1)S(1)}, bf16[64,1024]{1,0:T(8,128)(2,1)S(1)}) custom-call(bf16[1024,128]{1,0:T(8,128)(2,1)S(1)} %collective-permute-done.6.pair_ref, bf16[256,1024]{1,0:T(8,128)(2,1)S(1)} %get-tuple-element.73.qa_ref, ...), custom_call_target="tpu_custom_call" | custom-call | flops 5750000128 | tf_op jit(solution)/shard_map/pallas_call | solution.py:314
  24.4 0.0 collective-permute-done.7.refs_0_
  24.4 0.1 collective-permute-start.8
  24.5 2.9 %shard_map.91 = (bf16[1024,1024]{1,0:T(8,128)(2,1)S(1)}, f32[1,1024]{1,0:T(1,128)S(1)}, f32[80,1024]{1,0:T(8,128)S(1)}, bf16[1024,128]{1,0:T(8,128)(2,1)S(1)}, bf16[64,1024]{1,0:T(8,128)(2,1)S(1)}) custom-call(bf16[1024,128]{1,0:T(8,128)(2,1)S(1)} %shard_map.90.pair_ref, bf16[256,1024]{1,0:T(8,128)(2,1)S(1)} %get-tuple-element.73.qa_ref, ...), custom_call_target="tpu_custom_call" | custom-call | flops 5750000128 | tf_op jit(solution)/shard_map/pallas_call | solution.py:314
  27.5 0.0 collective-permute-done.8.pair_ref
  27.5 3.1 %shard_map.92 = (bf16[1024,1024]{1,0:T(8,128)(2,1)S(1)}, f32[1,1024]{1,0:T(1,128)S(1)}, f32[80,1024]{1,0:T(8,128)S(1)}, bf16[1024,128]{1,0:T(8,128)(2,1)S(1)}, bf16[64,1024]{1,0:T(8,128)(2,1)S(1)}) custom-call(bf16[1024,128]{1,0:T(8,128)(2,1)S(1)} %collective-permute-done.8.pair_ref, bf16[256,1024]{1,0:T(8,128)(2,1)S(1)} %get-tuple-element.73.qa_ref, ...), custom_call_target="tpu_custom_call" | custom-call | flops 5750000128 | tf_op jit(solution)/shard_map/pallas_call | solution.py:314
  30.6 0.2 shard_map.93
  30.8 2.6 %collective-permute-start.9 = (bf16[64,256]{1,0:T(8,128)(2,1)S(1)}, bf16[64,256]{1,0:T(8,128)(2,1)S(1)}, u32[]{:S(2)}, u32[]{:S(2)}) collective-permute-start(bf16[64,256]{1,0:T(8,128)(2,1)S(1)} %get-tuple-element.104), channel_id=1, source_target_pairs={{0,24},{2,26},{4,28},{6,30},{8,16},{10,18},{12,20},{14,22},{16,8},... | collective-permute-start | bytes 98312 | tf_op jit(solution)/shard_map/ppermute | solution.py:276
  33.4 0.1 collective-permute-start.10
  33.5 1.7 %collective-permute-start.11 = (bf16[64,256]{1,0:T(8,128)(2,1)S(1)}, bf16[64,256]{1,0:T(8,128)(2,1)S(1)}, u32[]{:S(2)}, u32[]{:S(2)}) collective-permute-start(bf16[64,256]{1,0:T(8,128)(2,1)S(1)} %get-tuple-element.106), channel_id=1, source_target_pairs={{0,8},{2,10},{4,12},{6,14},{8,0},{10,2},{12,4},{14,6},{16,24},{18,... | collective-permute-start | bytes 98312 | tf_op jit(solution)/shard_map/ppermute | solution.py:276
  35.2 2.2 %shard_map.94 = (bf16[128,1024]{1,0:T(8,128)(2,1)S(1)}, f32[64,1024]{1,0:T(8,128)S(1)}) custom-call(bf16[1024,1024]{1,0:T(8,128)(2,1)S(1)} %get-tuple-element.98.exp_ref, bf16[1024,128]{1,0:T(8,128)(2,1)S(1)} %get-tuple-element.99.v_ref, bf16[64,1024]{1,0:T(8,128)(2,1)S(1)} %get-tuple-element.100.kt_ref, bf16[64,1024]{1,0:T(8,128)(2,1)S(1)} %get-tuple-element.78.q_ref, ...), custom_call_target="tpu_custom_call" | custom-call | flops 2300000000 | tf_op jit(solution)/shard_map/pallas_call | solution.py:356
  37.4 0.0 collective-permute-done.9.refs_1_
  37.4 1.0 %collective-permute-done.10.refs_2_ = bf16[64,256]{1,0:T(8,128)(2,1)S(1)} collective-permute-done((bf16[64,256]{1,0:T(8,128)(2,1)S(1)}, bf16[64,256]{1,0:T(8,128)(2,1)S(1)}, u32[]{:S(2)}, u32[]{:S(2)}) %collective-permute-start.10) | collective-permute-done | bytes 32800 | tf_op jit(solution)/shard_map/ppermute | solution.py:276
  38.4 0.0 collective-permute-done.11.refs_3_
  38.4 0.9 %shard_map.95 = (bf16[256,768]{1,0:T(8,128)(2,1)S(1)}, bf16[2,64,768]{2,1,0:T(8,128)(2,1)S(1)}, bf16[2,64,768]{2,1,0:T(8,128)(2,1)S(1)}) custom-call(s32[2]{0:T(128)S(1)} %copy-done.4, bf16[256,768]{1,0:T(8,128)(2,1)S(1)} %copy-done.2, bf16[4,64,768]{2,1,0:T(8,128)(2,1)S(1)} %copy-done.1, bf16[64,256]{1,0:T(8,128)(2,1)S(1)} %get-tuple-element.103.refs_0_, ...), custom_call_target="tpu_custom_call" | custom-call | flops 805000000 | tf_op jit(solution)/shard_map/pallas_call | solution.py:334
  39.3 0.1 collective-permute-start.12
  39.4 0.5 collective-permute-start.15
  39.9 1.5 %collective-permute-start.17 = (bf16[256,768]{1,0:T(8,128)(2,1)S(1)}, bf16[256,768]{1,0:T(8,128)(2,1)S(1)}, u32[]{:S(2)}, u32[]{:S(2)}) collective-permute-start(bf16[256,768]{1,0:T(8,128)(2,1)S(1)} %get-tuple-element.116.refs_4_), channel_id=1, source_target_pairs={{0,1},{1,0},{2,3},{3,2},{4,5},{5,4},{6,7},{7,6},{8,9},{9,8},{10,11... | collective-permute-start | bytes 1179656 | tf_op jit(solution)/shard_map/ppermute | solution.py:276
  41.4 0.0 collective-permute-done.12.came_ref
  41.4 1.6 %collective-permute-start.13 = (bf16[64,768]{1,0:T(8,128)(2,1)S(1)}, bf16[64,768]{1,0:T(8,128)(2,1)S(1)}, u32[]{:S(2)}, u32[]{:S(2)}) collective-permute-start(bf16[64,768]{1,0:T(8,128)(2,1)S(1)} %get-tuple-element.112), channel_id=1, source_target_pairs={{0,4},{2,6},{4,0},{6,2},{8,12},{10,14},{12,8},{14,10},{16,20},{18,... | collective-permute-start | bytes 294920 | tf_op jit(solution)/shard_map/ppermute | solution.py:276
  43.0 2.2 %shard_map.97 = (bf16[128,1024]{1,0:T(8,128)(2,1)S(1)}, f32[64,1024]{1,0:T(8,128)S(1)}) custom-call(bf16[1024,1024]{1,0:T(8,128)(2,1)S(1)} %get-tuple-element.94.exp_ref, bf16[1024,128]{1,0:T(8,128)(2,1)S(1)} %get-tuple-element.95.v_ref, bf16[64,1024]{1,0:T(8,128)(2,1)S(1)} %get-tuple-element.96.kt_ref, bf16[64,1024]{1,0:T(8,128)(2,1)S(1)} %get-tuple-element.78.q_ref, ...), custom_call_target="tpu_custom_call" | custom-call | flops 2300000000 | tf_op jit(solution)/shard_map/pallas_call | solution.py:356
  45.2 0.0 collective-permute-done.15.b_ref
  45.2 0.1 shard_map.101
  45.3 0.6 collective-permute-start.16
  45.9 0.3 collective-permute-done.13.b_ref
  46.1 0.8 %collective-permute-start.14 = (bf16[64,768]{1,0:T(8,128)(2,1)S(1)}, bf16[64,768]{1,0:T(8,128)(2,1)S(1)}, u32[]{:S(2)}, u32[]{:S(2)}) collective-permute-start(bf16[64,768]{1,0:T(8,128)(2,1)S(1)} %shard_map.98.refs_1_.a_ref), channel_id=1, source_target_pairs={{0,8},{2,10},{4,12},{6,14},{8,0},{10,2},{12,4},{14,6},{16,24},{18,... | collective-permute-start | bytes 294920 | tf_op jit(solution)/shard_map/ppermute | solution.py:276
  46.9 2.2 %shard_map.99 = (bf16[128,1024]{1,0:T(8,128)(2,1)S(1)}, f32[64,1024]{1,0:T(8,128)S(1)}) custom-call(bf16[1024,1024]{1,0:T(8,128)(2,1)S(1)} %get-tuple-element.90.exp_ref, bf16[1024,128]{1,0:T(8,128)(2,1)S(1)} %get-tuple-element.91.v_ref, bf16[64,1024]{1,0:T(8,128)(2,1)S(1)} %get-tuple-element.92.kt_ref, bf16[64,1024]{1,0:T(8,128)(2,1)S(1)} %get-tuple-element.78.q_ref, ...), custom_call_target="tpu_custom_call" | custom-call | flops 2300000000 | tf_op jit(solution)/shard_map/pallas_call | solution.py:356
  49.1 0.1 collective-permute-start.18
  49.1 1.7 %collective-permute-done.14.b_ref = bf16[64,768]{1,0:T(8,128)(2,1)S(1)} collective-permute-done((bf16[64,768]{1,0:T(8,128)(2,1)S(1)}, bf16[64,768]{1,0:T(8,128)(2,1)S(1)}, u32[]{:S(2)}, u32[]{:S(2)}) %collective-permute-start.14) | collective-permute-done | bytes 98336 | tf_op jit(solution)/shard_map/ppermute | solution.py:276
  50.9 1.9 %collective-permute-start.22 = (bf16[64,768]{1,0:T(8,128)(2,1)S(1)}, bf16[64,768]{1,0:T(8,128)(2,1)S(1)}, u32[]{:S(2)}, u32[]{:S(2)}) collective-permute-start(bf16[64,768]{1,0:T(8,128)(2,1)S(1)} %shard_map.100.refs_1_.a_ref), channel_id=1, source_target_pairs={{0,16},{2,18},{4,20},{6,22},{8,24},{10,26},{12,28},{14,30},{16,0},... | collective-permute-start | bytes 294920 | tf_op jit(solution)/shard_map/ppermute | solution.py:276
  52.8 0.3 collective-permute-done.16.refs_2_.came_ref
  53.1 2.2 %shard_map.102 = (bf16[128,1024]{1,0:T(8,128)(2,1)S(1)}, f32[64,1024]{1,0:T(8,128)S(1)}) custom-call(bf16[1024,1024]{1,0:T(8,128)(2,1)S(1)} %get-tuple-element.75.exp_ref, bf16[1024,128]{1,0:T(8,128)(2,1)S(1)} %get-tuple-element.76.v_ref, bf16[64,1024]{1,0:T(8,128)(2,1)S(1)} %get-tuple-element.77.kt_ref, bf16[64,1024]{1,0:T(8,128)(2,1)S(1)} %get-tuple-element.78.q_ref, ...), custom_call_target="tpu_custom_call" | custom-call | flops 2300000000 | tf_op jit(solution)/shard_map/pallas_call | solution.py:356
  55.3 0.1 shard_map.103.kept_ref
  55.3 0.1 shard_map.104
  55.4 1.9 %collective-permute-start.19 = (bf16[192,256]{1,0:T(8,128)(2,1)S(1)}, bf16[192,256]{1,0:T(8,128)(2,1)S(1)}, u32[]{:S(2)}, u32[]{:S(2)}) collective-permute-start(bf16[192,256]{1,0:T(8,128)(2,1)S(1)} %get-tuple-element.120), channel_id=1, source_target_pairs={{0,16},{2,18},{4,20},{6,22},{8,24},{10,26},{12,28},{14,30},{16,0},... | collective-permute-start | bytes 294920 | tf_op jit(solution)/shard_map/ppermute | solution.py:276
  57.4 1.2 %collective-permute-start.20 = (bf16[192,256]{1,0:T(8,128)(2,1)S(1)}, bf16[192,256]{1,0:T(8,128)(2,1)S(1)}, u32[]{:S(2)}, u32[]{:S(2)}) collective-permute-start(bf16[192,256]{1,0:T(8,128)(2,1)S(1)} %get-tuple-element.121), channel_id=1, source_target_pairs={{0,24},{2,26},{4,28},{6,30},{8,16},{10,18},{12,20},{14,22},{16,8},... | collective-permute-start | bytes 294920 | tf_op jit(solution)/shard_map/ppermute | solution.py:276
  58.5 0.4 collective-permute-start.21
  59.0 0.0 collective-permute-done.22.b_ref
  59.0 1.3 %collective-permute-start.23 = (bf16[64,768]{1,0:T(8,128)(2,1)S(1)}, bf16[64,768]{1,0:T(8,128)(2,1)S(1)}, u32[]{:S(2)}, u32[]{:S(2)}) collective-permute-start(bf16[64,768]{1,0:T(8,128)(2,1)S(1)} %shard_map.105.refs_0_), channel_id=1, source_target_pairs={{0,4},{2,6},{4,0},{6,2},{8,12},{10,14},{12,8},{14,10},{16,20},{18,... | collective-permute-start | bytes 294920 | tf_op jit(solution)/shard_map/ppermute | solution.py:276
  60.3 0.0 collective-permute-start.24
  60.3 4.6 %collective-permute-done.19.refs_1_ = bf16[192,256]{1,0:T(8,128)(2,1)S(1)} collective-permute-done((bf16[192,256]{1,0:T(8,128)(2,1)S(1)}, bf16[192,256]{1,0:T(8,128)(2,1)S(1)}, u32[]{:S(2)}, u32[]{:S(2)}) %collective-permute-start.19) | collective-permute-done | bytes 98336 | tf_op jit(solution)/shard_map/ppermute | solution.py:276
  65.0 0.3 collective-permute-done.21.refs_3_
  65.3 0.1 collective-permute-start.25
  65.4 1.1 %shard_map.108 = (f32[1024,128]{1,0:T(8,128)}, f32[4,64,256]{2,1,0:T(8,128)}, bf16[256,768]{1,0:T(8,128)(2,1)}) custom-call(bf16[192,256]{1,0:T(8,128)(2,1)S(1)} %get-tuple-element.119.refs_0_, bf16[192,256]{1,0:T(8,128)(2,1)S(1)} %collective-permute-done.19.refs_1_, bf16[192,256]{1,0:T(8,128)(2,1)S(1)} %collective-permute-done.20.refs_2_, ...), custom_call_target="tpu_custom_call" | custom-call | flops 5750000128 | tf_op jit(solution)/shard_map/pallas_call | solution.py:392
  66.5 0.2 collective-permute-done.25.refs_3_
  66.7 0.9 %shard_map.109 = f32[4,64,768]{2,1,0:T(8,128)} custom-call(bf16[64,768]{1,0:T(8,128)(2,1)S(1)} %shard_map.105.refs_0_, bf16[64,768]{1,0:T(8,128)(2,1)S(1)} %collective-permute-done.24.refs_1_, bf16[64,768]{1,0:T(8,128)(2,1)S(1)} %shard_map.107.refs_6_.refs_2_, bf16[64,768]{1,0:T(8,128)(2,1)S(1)} %collective-permute-done.25.refs_3_), custom_call_target="tpu_custom_call" | custom-call | flops 575000000 | tf_op jit(solution)/shard_map/pallas_call | solution.py:386
  (24 shorter events, 0.2 us)
Async XLA Ops:
  0.6 7.6 %copy-start.1 = (bf16[4,64,768]{2,1,0:T(8,128)(2,1)S(1)}, bf16[4,64,768]{2,1,0:T(8,128)(2,1)}, u32[]{:S(2)}) copy-start(bf16[4,64,768]{2,1,0:T(8,128)(2,1)} %w_ref.3) | copy-start | bytes 1179652
  0.6 7.6 %copy-start.2 = (bf16[256,768]{1,0:T(8,128)(2,1)S(1)}, bf16[256,768]{1,0:T(8,128)(2,1)}, u32[]{:S(2)}) copy-start(bf16[256,768]{1,0:T(8,128)(2,1)} %go_ref.3) | copy-start | bytes 1179652
  0.7 7.5 %copy-start.3 = (bf16[256,4,64]{0,2,1:T(8,128)(2,1)S(1)}, bf16[256,4,64]{0,2,1:T(8,128)(2,1)}, u32[]{:S(2)}) copy-start(bf16[256,4,64]{0,2,1:T(8,128)(2,1)} %param.5) | copy-start | bytes 393220
  0.7 7.5 %copy-start.4 = (s32[2]{0:T(128)S(1)}, s32[2]{0:T(128)}, u32[]{:S(2)}) copy-start(s32[2]{0:T(128)} %fill_ref.5) | copy-start | bytes 28
  2.6 10.5 %collective-permute-start = (bf16[256,128]{1,0:T(8,128)(2,1)}, bf16[256,128]{1,0:T(8,128)(2,1)S(1)}, u32[]{:S(2)}, u32[]{:S(2)}) collective-permute-start(bf16[256,128]{1,0:T(8,128)(2,1)} %get-tuple-element.66), channel_id=1, source_target_pairs={{0,24},{2,26},{4,28},{6,30},{8,16},{10,18},{12,20},{14,22},{16,8},... | collective-permute-start | bytes 196616 | tf_op jit(solution)/shard_map/ppermute | solution.py:276
  7.6 7.0 %collective-permute-start.1 = (bf16[256,128]{1,0:T(8,128)(2,1)}, bf16[256,128]{1,0:T(8,128)(2,1)S(1)}, u32[]{:S(2)}, u32[]{:S(2)}) collective-permute-start(bf16[256,128]{1,0:T(8,128)(2,1)} %get-tuple-element.67), channel_id=1, source_target_pairs={{0,16},{2,18},{4,20},{6,22},{8,24},{10,26},{12,28},{14,30},{16,0},... | collective-permute-start | bytes 196616 | tf_op jit(solution)/shard_map/ppermute | solution.py:276
  7.6 7.0 %collective-permute-start.2 = (bf16[256,128]{1,0:T(8,128)(2,1)}, bf16[256,128]{1,0:T(8,128)(2,1)S(1)}, u32[]{:S(2)}, u32[]{:S(2)}) collective-permute-start(bf16[256,128]{1,0:T(8,128)(2,1)} %get-tuple-element.68), channel_id=1, source_target_pairs={{0,8},{2,10},{4,12},{6,14},{8,0},{10,2},{12,4},{14,6},{16,24},{18,... | collective-permute-start | bytes 196616 | tf_op jit(solution)/shard_map/ppermute | solution.py:276
  8.2 6.4 %copy-start = (bf16[256,128]{1,0:T(8,128)(2,1)S(1)}, bf16[256,128]{1,0:T(8,128)(2,1)}, u32[]{:S(2)}) copy-start(bf16[256,128]{1,0:T(8,128)(2,1)} %get-tuple-element.65.refs_0_) | copy-start | bytes 196612
  9.1 9.0 %collective-permute-start.3 = (bf16[128,256]{1,0:T(8,128)(2,1)S(1)}, bf16[128,256]{1,0:T(8,128)(2,1)S(1)}, u32[]{:S(2)}, u32[]{:S(2)}) collective-permute-start(bf16[128,256]{1,0:T(8,128)(2,1)S(1)} %get-tuple-element.70), channel_id=1, source_target_pairs={{0,16},{2,18},{4,20},{6,22},{8,24},{10,26},{12,28},{14,30},{16,0},... | collective-permute-start | bytes 196616 | tf_op jit(solution)/shard_map/ppermute | solution.py:276
  11.5 6.6 %collective-permute-start.4 = (bf16[128,256]{1,0:T(8,128)(2,1)S(1)}, bf16[128,256]{1,0:T(8,128)(2,1)S(1)}, u32[]{:S(2)}, u32[]{:S(2)}) collective-permute-start(bf16[128,256]{1,0:T(8,128)(2,1)S(1)} %get-tuple-element.71), channel_id=1, source_target_pairs={{0,24},{2,26},{4,28},{6,30},{8,16},{10,18},{12,20},{14,22},{16,8},... | collective-permute-start | bytes 196616 | tf_op jit(solution)/shard_map/ppermute | solution.py:276
  13.1 5.4 %collective-permute-start.5 = (bf16[128,256]{1,0:T(8,128)(2,1)S(1)}, bf16[128,256]{1,0:T(8,128)(2,1)S(1)}, u32[]{:S(2)}, u32[]{:S(2)}) collective-permute-start(bf16[128,256]{1,0:T(8,128)(2,1)S(1)} %get-tuple-element.72), channel_id=1, source_target_pairs={{0,8},{2,10},{4,12},{6,14},{8,0},{10,2},{12,4},{14,6},{16,24},{18,... | collective-permute-start | bytes 196616 | tf_op jit(solution)/shard_map/ppermute | solution.py:276
  14.6 9.8 %collective-permute-start.7 = (bf16[1024,128]{1,0:T(8,128)(2,1)S(1)}, bf16[1024,128]{1,0:T(8,128)(2,1)S(1)}, u32[]{:S(2)}, u32[]{:S(2)}) collective-permute-start(bf16[1024,128]{1,0:T(8,128)(2,1)S(1)} %shard_map.86.pair_ref), channel_id=1, source_target_pairs={{0,4},{2,6},{4,0},{6,2},{8,12},{10,14},{12,8},{14,10},{16,20},{18,... | collective-permute-start | bytes 786440 | tf_op jit(solution)/shard_map/ppermute | solution.py:276
  16.0 5.5 %collective-permute-start.6 = (bf16[1024,128]{1,0:T(8,128)(2,1)S(1)}, bf16[1024,128]{1,0:T(8,128)(2,1)S(1)}, u32[]{:S(2)}, u32[]{:S(2)}) collective-permute-start(bf16[1024,128]{1,0:T(8,128)(2,1)S(1)} %shard_map.86.pair_ref), channel_id=1, source_target_pairs={{0,2},{2,0},{4,6},{6,4},{8,10},{10,8},{12,14},{14,12},{16,18},{18,... | collective-permute-start | bytes 786440 | tf_op jit(solution)/shard_map/ppermute | solution.py:276
  24.4 3.0 %collective-permute-start.8 = (bf16[1024,128]{1,0:T(8,128)(2,1)S(1)}, bf16[1024,128]{1,0:T(8,128)(2,1)S(1)}, u32[]{:S(2)}, u32[]{:S(2)}) collective-permute-start(bf16[1024,128]{1,0:T(8,128)(2,1)S(1)} %shard_map.90.pair_ref), channel_id=1, source_target_pairs={{0,2},{2,0},{4,6},{6,4},{8,10},{10,8},{12,14},{14,12},{16,18},{18,... | collective-permute-start | bytes 786440 | tf_op jit(solution)/shard_map/ppermute | solution.py:276
  30.8 6.6 %collective-permute-start.9 = (bf16[64,256]{1,0:T(8,128)(2,1)S(1)}, bf16[64,256]{1,0:T(8,128)(2,1)S(1)}, u32[]{:S(2)}, u32[]{:S(2)}) collective-permute-start(bf16[64,256]{1,0:T(8,128)(2,1)S(1)} %get-tuple-element.104), channel_id=1, source_target_pairs={{0,24},{2,26},{4,28},{6,30},{8,16},{10,18},{12,20},{14,22},{16,8},... | collective-permute-start | bytes 98312 | tf_op jit(solution)/shard_map/ppermute | solution.py:276
  33.4 5.0 %collective-permute-start.10 = (bf16[64,256]{1,0:T(8,128)(2,1)S(1)}, bf16[64,256]{1,0:T(8,128)(2,1)S(1)}, u32[]{:S(2)}, u32[]{:S(2)}) collective-permute-start(bf16[64,256]{1,0:T(8,128)(2,1)S(1)} %get-tuple-element.105), channel_id=1, source_target_pairs={{0,16},{2,18},{4,20},{6,22},{8,24},{10,26},{12,28},{14,30},{16,0},... | collective-permute-start | bytes 98312 | tf_op jit(solution)/shard_map/ppermute | solution.py:276
  33.5 4.9 %collective-permute-start.11 = (bf16[64,256]{1,0:T(8,128)(2,1)S(1)}, bf16[64,256]{1,0:T(8,128)(2,1)S(1)}, u32[]{:S(2)}, u32[]{:S(2)}) collective-permute-start(bf16[64,256]{1,0:T(8,128)(2,1)S(1)} %get-tuple-element.106), channel_id=1, source_target_pairs={{0,8},{2,10},{4,12},{6,14},{8,0},{10,2},{12,4},{14,6},{16,24},{18,... | collective-permute-start | bytes 98312 | tf_op jit(solution)/shard_map/ppermute | solution.py:276
  39.3 2.1 %collective-permute-start.12 = (bf16[2,64,768]{2,1,0:T(8,128)(2,1)S(1)}, bf16[2,64,768]{2,1,0:T(8,128)(2,1)S(1)}, u32[]{:S(2)}, u32[]{:S(2)}) collective-permute-start(bf16[2,64,768]{2,1,0:T(8,128)(2,1)S(1)} %get-tuple-element.109), channel_id=1, source_target_pairs={{0,2},{2,0},{4,6},{6,4},{8,10},{10,8},{12,14},{14,12},{16,18},{18,... | collective-permute-start | bytes 589832 | tf_op jit(solution)/shard_map/ppermute | solution.py:276
  39.4 5.8 %collective-permute-start.15 = (bf16[128,1024]{1,0:T(8,128)(2,1)S(1)}, bf16[128,1024]{1,0:T(8,128)(2,1)S(1)}, u32[]{:S(2)}, u32[]{:S(2)}) collective-permute-start(bf16[128,1024]{1,0:T(8,128)(2,1)S(1)} %get-tuple-element.107.refs_4_), channel_id=1, source_target_pairs={{0,2},{2,0},{4,6},{6,4},{8,10},{10,8},{12,14},{14,12},{16,18},{18,... | collective-permute-start | bytes 786440 | tf_op jit(solution)/shard_map/ppermute | solution.py:276
  39.9 12.9 %collective-permute-start.17 = (bf16[256,768]{1,0:T(8,128)(2,1)S(1)}, bf16[256,768]{1,0:T(8,128)(2,1)S(1)}, u32[]{:S(2)}, u32[]{:S(2)}) collective-permute-start(bf16[256,768]{1,0:T(8,128)(2,1)S(1)} %get-tuple-element.116.refs_4_), channel_id=1, source_target_pairs={{0,1},{1,0},{2,3},{3,2},{4,5},{5,4},{6,7},{7,6},{8,9},{9,8},{10,11... | collective-permute-start | bytes 1179656 | tf_op jit(solution)/shard_map/ppermute | solution.py:276
  41.4 4.7 %collective-permute-start.13 = (bf16[64,768]{1,0:T(8,128)(2,1)S(1)}, bf16[64,768]{1,0:T(8,128)(2,1)S(1)}, u32[]{:S(2)}, u32[]{:S(2)}) collective-permute-start(bf16[64,768]{1,0:T(8,128)(2,1)S(1)} %get-tuple-element.112), channel_id=1, source_target_pairs={{0,4},{2,6},{4,0},{6,2},{8,12},{10,14},{12,8},{14,10},{16,20},{18,... | collective-permute-start | bytes 294920 | tf_op jit(solution)/shard_map/ppermute | solution.py:276
  45.3 7.8 %collective-permute-start.16 = (bf16[128,1024]{1,0:T(8,128)(2,1)S(1)}, bf16[128,1024]{1,0:T(8,128)(2,1)S(1)}, u32[]{:S(2)}, u32[]{:S(2)}) collective-permute-start(bf16[128,1024]{1,0:T(8,128)(2,1)S(1)} %shard_map.101), channel_id=1, source_target_pairs={{0,4},{2,6},{4,0},{6,2},{8,12},{10,14},{12,8},{14,10},{16,20},{18,... | collective-permute-start | bytes 786440 | tf_op jit(solution)/shard_map/ppermute | solution.py:276
  46.1 4.7 %collective-permute-start.14 = (bf16[64,768]{1,0:T(8,128)(2,1)S(1)}, bf16[64,768]{1,0:T(8,128)(2,1)S(1)}, u32[]{:S(2)}, u32[]{:S(2)}) collective-permute-start(bf16[64,768]{1,0:T(8,128)(2,1)S(1)} %shard_map.98.refs_1_.a_ref), channel_id=1, source_target_pairs={{0,8},{2,10},{4,12},{6,14},{8,0},{10,2},{12,4},{14,6},{16,24},{18,... | collective-permute-start | bytes 294920 | tf_op jit(solution)/shard_map/ppermute | solution.py:276
  49.1 6.2 %collective-permute-start.18 = (bf16[128,1024]{1,0:T(8,128)(2,1)S(1)}, bf16[128,1024]{1,0:T(8,128)(2,1)S(1)}, u32[]{:S(2)}, u32[]{:S(2)}) collective-permute-start(bf16[128,1024]{1,0:T(8,128)(2,1)S(1)} %get-tuple-element.115.refs_0_), channel_id=1, source_target_pairs={{0,2},{2,0},{4,6},{6,4},{8,10},{10,8},{12,14},{14,12},{16,18},{18,... | collective-permute-start | bytes 786440 | tf_op jit(solution)/shard_map/ppermute | solution.py:276
  50.9 8.1 %collective-permute-start.22 = (bf16[64,768]{1,0:T(8,128)(2,1)S(1)}, bf16[64,768]{1,0:T(8,128)(2,1)S(1)}, u32[]{:S(2)}, u32[]{:S(2)}) collective-permute-start(bf16[64,768]{1,0:T(8,128)(2,1)S(1)} %shard_map.100.refs_1_.a_ref), channel_id=1, source_target_pairs={{0,16},{2,18},{4,20},{6,22},{8,24},{10,26},{12,28},{14,30},{16,0},... | collective-permute-start | bytes 294920 | tf_op jit(solution)/shard_map/ppermute | solution.py:276
  55.4 9.6 %collective-permute-start.19 = (bf16[192,256]{1,0:T(8,128)(2,1)S(1)}, bf16[192,256]{1,0:T(8,128)(2,1)S(1)}, u32[]{:S(2)}, u32[]{:S(2)}) collective-permute-start(bf16[192,256]{1,0:T(8,128)(2,1)S(1)} %get-tuple-element.120), channel_id=1, source_target_pairs={{0,16},{2,18},{4,20},{6,22},{8,24},{10,26},{12,28},{14,30},{16,0},... | collective-permute-start | bytes 294920 | tf_op jit(solution)/shard_map/ppermute | solution.py:276
  57.4 7.6 %collective-permute-start.20 = (bf16[192,256]{1,0:T(8,128)(2,1)S(1)}, bf16[192,256]{1,0:T(8,128)(2,1)S(1)}, u32[]{:S(2)}, u32[]{:S(2)}) collective-permute-start(bf16[192,256]{1,0:T(8,128)(2,1)S(1)} %get-tuple-element.121), channel_id=1, source_target_pairs={{0,24},{2,26},{4,28},{6,30},{8,16},{10,18},{12,20},{14,22},{16,8},... | collective-permute-start | bytes 294920 | tf_op jit(solution)/shard_map/ppermute | solution.py:276
  58.5 6.7 %collective-permute-start.21 = (bf16[192,256]{1,0:T(8,128)(2,1)S(1)}, bf16[192,256]{1,0:T(8,128)(2,1)S(1)}, u32[]{:S(2)}, u32[]{:S(2)}) collective-permute-start(bf16[192,256]{1,0:T(8,128)(2,1)S(1)} %get-tuple-element.122), channel_id=1, source_target_pairs={{0,8},{2,10},{4,12},{6,14},{8,0},{10,2},{12,4},{14,6},{16,24},{18,... | collective-permute-start | bytes 294920 | tf_op jit(solution)/shard_map/ppermute | solution.py:276
  59.0 6.3 %collective-permute-start.23 = (bf16[64,768]{1,0:T(8,128)(2,1)S(1)}, bf16[64,768]{1,0:T(8,128)(2,1)S(1)}, u32[]{:S(2)}, u32[]{:S(2)}) collective-permute-start(bf16[64,768]{1,0:T(8,128)(2,1)S(1)} %shard_map.105.refs_0_), channel_id=1, source_target_pairs={{0,4},{2,6},{4,0},{6,2},{8,12},{10,14},{12,8},{14,10},{16,20},{18,... | collective-permute-start | bytes 294920 | tf_op jit(solution)/shard_map/ppermute | solution.py:276
  60.3 6.1 %collective-permute-start.24 = (bf16[64,768]{1,0:T(8,128)(2,1)S(1)}, bf16[64,768]{1,0:T(8,128)(2,1)S(1)}, u32[]{:S(2)}, u32[]{:S(2)}) collective-permute-start(bf16[64,768]{1,0:T(8,128)(2,1)S(1)} %shard_map.105.refs_0_), channel_id=1, source_target_pairs={{0,2},{2,0},{4,6},{6,4},{8,10},{10,8},{12,14},{14,12},{16,18},{18,... | collective-permute-start | bytes 294920 | tf_op jit(solution)/shard_map/ppermute | solution.py:276
  65.3 1.4 %collective-permute-start.25 = (bf16[64,768]{1,0:T(8,128)(2,1)S(1)}, bf16[64,768]{1,0:T(8,128)(2,1)S(1)}, u32[]{:S(2)}, u32[]{:S(2)}) collective-permute-start(bf16[64,768]{1,0:T(8,128)(2,1)S(1)} %shard_map.107.refs_6_.refs_2_), channel_id=1, source_target_pairs={{0,2},{2,0},{4,6},{6,4},{8,10},{10,8},{12,14},{14,12},{16,18},{18,... | collective-permute-start | bytes 294920 | tf_op jit(solution)/shard_map/ppermute | solution.py:276
